TPU v7x, 32 devices: a whole 2x2x4 slice. The times are simulated.
32 devices in a mesh: groups: 2 (over x), replica: 16 (over z, y, core).
Axes of the slice: x: 2, y: 2, z: 4, core: 2. Of those that a mesh axis runs over, the one named last changes fastest.
Arguments:
- hidden: bfloat16 [3, 64, 5120], P(None, ('groups', 'replica')), parts along dimension 1, may hold values from -6 to 6
- query_key_value_weight: bfloat16 [3, 5120, 5120], P(None, None, 'replica'), may hold values from -0.078125 to 0.078125
- adapter_down_maps: bfloat16 [64, 64, 5120], P('replica'), may hold values from -0.078125 to 0.078125
- adapter_up_maps: bfloat16 [64, 64, 5120], P(None, None, 'replica'), may hold values from -0.75 to 0.75
- adapter_storage_row: int32 [64], replicated, may hold values from 0 to 63, each once
- request_adapter: int32 [64], P('groups'), parts along dimension 0, may hold values from 0 to 63
- lengths: int32 [64], P('groups'), parts along dimension 0, may hold values from 1 to 128, as said below
- request_page_table: int32 [64, 32], P(('groups', 'replica')), parts along dimension 0, may hold values from 0 to 63, as said below
- key_value_pool: bfloat16 [2048, 4, 2, 5120], P(('groups', 'replica')), parts along dimension 0, may hold values from -220 to 220
Outputs:
- attn_out: bfloat16 [3, 64, 5120], P(None, ('groups', 'replica')), parts along dimension 1
There are 2 independent parts, one for each index of `groups`. A program takes and returns all parts, laid end to end along the dimension named above; an argument that names none is the same for every part. Nothing has to cross between parts.
Inputs may be any that keep to these rules, and one draw needn't show every extreme that they name: `lengths`: requests 2 at a time belong to one replica, in replica order; cached keys were rotated at positions 0 to length - 1; replicas 2 j and 2 j + 1 form a pair in which one replica's requests all have 32 * 2 tokens or more and the other's all have 32 * 4 / 8 or fewer. `request_page_table`: local page numbers within the replica of the request; the rows of one replica name each of its 64 pages once.
All inputs are finite; a program needn't handle non-finite values.
Results may differ from a plain program's by a relative error of at most 0.012.
The roundings to bfloat16 on the way count: a program that leaves them out, or rounds other values in their place, can miss the bound.
Values may be sent and summed in bfloat16 or wider, within the bound.
No kernel may reach another device: no remote copies, remote signals or barrier semaphores. Data moves between devices by JAX's collectives and lax.ppermute only.
A program may use at most 128 MiB of HBM per device.

v0:
```python
import jax
import jax.numpy as jnp
from jax import lax
from jax.sharding import PartitionSpec as P

HD = 128


adapter_scale = 2.0
masked_score = -1e30


def rotate(vectors, positions):
    half_dim = vectors.shape[-1] // 2
    frequency = jnp.exp(
        jnp.arange(half_dim, dtype=jnp.float32) * (-2.0 * jnp.log(10000.0) / vectors.shape[-1])
    )
    angles = positions.astype(jnp.float32)[:, None, None] * frequency[None, None, :]
    cosine = jnp.cos(angles)
    sine_part = jnp.sin(angles)
    first_half = vectors[..., :half_dim]
    second = vectors[..., half_dim:]
    return jnp.concatenate(
        [first_half * cosine - second * sine_part, second * cosine + first_half * sine_part],
        axis=-1,
    )


def per_device(
    hidden,
    query_key_value_weight,
    adapter_down_maps,
    adapter_up_maps,
    adapter_storage_row,
    request_adapter,
    lengths,
    request_page_table,
    key_value_pool,
):
    my_index = lax.axis_index("replica")
    steps, req_dev, width = hidden.shape
    columns = query_key_value_weight.shape[2]
    holder_count = adapter_down_maps.shape[0]
    page_len = key_value_pool.shape[1]
    max_pages = request_page_table.shape[1]
    context = max_pages * page_len
    head_dim = HD
    head_count = width // head_dim
    score_scale = HD ** (-0.5)
    adapter_count = adapter_storage_row.shape[0]
    request_count = request_adapter.shape[0]
    stored_rows = jnp.sum(
        jnp.where(
            request_adapter[:, None] == jnp.arange(adapter_count, dtype=jnp.int32)[None, :],
            adapter_storage_row[None, :],
            0,
        ),
        axis=1,
    )
    local_slots = my_index * holder_count + jnp.arange(holder_count, dtype=jnp.int32)
    my_lengths = lax.dynamic_slice_in_dim(lengths, my_index * req_dev, req_dev)
    up_map_rows = adapter_up_maps[stored_rows]
    cache = key_value_pool[request_page_table.reshape(-1)].reshape(
        req_dev, context, 2, head_count, head_dim
    )
    cache_keys = cache[:, :, 0]
    cache_values = cache[:, :, 1]
    live_mask = jnp.arange(context, dtype=jnp.int32)[None, :] < my_lengths[:, None]
    new_keys = jnp.zeros((req_dev, steps, head_count, head_dim), jnp.bfloat16)
    new_values = jnp.zeros((req_dev, steps, head_count, head_dim), jnp.bfloat16)
    step_ids = jnp.arange(steps)
    results = []
    for step_index in range(steps):
        current = hidden[step_index]
        block_row_list = lax.all_gather(current, "replica", axis=0, tiled=True)
        row_count = block_row_list.shape[0]
        projected_rows = jnp.einsum(
            "nd,idc->nic",
            block_row_list,
            query_key_value_weight,
            preferred_element_type=jnp.float32,
        ).reshape(row_count, 3 * columns)
        down_project = jnp.einsum(
            "il,hfl->ihf", block_row_list, adapter_down_maps, preferred_element_type=jnp.float32
        )
        own_mask = (stored_rows[:, None] == local_slots[None, :]).astype(jnp.float32)
        partial_value = jnp.sum(down_project * own_mask[:, :, None], axis=1)
        produced = jnp.concatenate([projected_rows, partial_value], axis=1)
        reduced_state = lax.psum(produced[:, 3 * columns :], "replica").astype(jnp.bfloat16)
        adapter_update = jnp.einsum(
            "jr,jrl->jl", reduced_state, up_map_rows, preferred_element_type=jnp.float32
        )
        projected_total = produced[:, : 3 * columns].reshape(request_count, 3, columns)
        q_cols = projected_total[:, 0].astype(jnp.bfloat16)
        k_cols = projected_total[:, 1].astype(jnp.bfloat16)
        value_columns = (projected_total[:, 2] + adapter_scale * adapter_update).astype(
            jnp.bfloat16
        )
        combined = jnp.stack([q_cols, k_cols, value_columns], axis=1)
        arrived_cols = lax.all_to_all(combined, "replica", split_axis=0, concat_axis=2, tiled=True)
        positions = my_lengths + step_index
        query_now = rotate(
            arrived_cols[:, 0].astype(jnp.float32).reshape(req_dev, head_count, head_dim), positions
        ).astype(jnp.bfloat16)
        key_now = rotate(
            arrived_cols[:, 1].astype(jnp.float32).reshape(req_dev, head_count, head_dim), positions
        ).astype(jnp.bfloat16)
        new_keys = new_keys.at[:, step_index].set(key_now)
        new_values = new_values.at[:, step_index].set(
            arrived_cols[:, 2].reshape(req_dev, head_count, head_dim)
        )
        scores = (
            jnp.einsum("rhd,rchd->rhc", query_now, cache_keys, preferred_element_type=jnp.float32)
            * score_scale
        )
        scores = jnp.where(live_mask[:, None, :], scores, masked_score)
        fresh_live = step_ids <= step_index
        fresh_scores = (
            jnp.einsum("rhd,rshd->rhs", query_now, new_keys, preferred_element_type=jnp.float32)
            * score_scale
        )
        fresh_scores = jnp.where(fresh_live[None, None, :], fresh_scores, masked_score)
        row_top = jnp.maximum(jnp.max(scores, axis=-1), jnp.max(fresh_scores, axis=-1))
        weights = jnp.where(live_mask[:, None, :], jnp.exp(scores - row_top[..., None]), 0.0)
        fresh_weights = jnp.where(
            fresh_live[None, None, :], jnp.exp(fresh_scores - row_top[..., None]), 0.0
        )
        totals = jnp.sum(weights, axis=-1) + jnp.sum(fresh_weights, axis=-1)
        accum = jnp.einsum(
            "rhc,rchd->rhd",
            weights.astype(jnp.bfloat16),
            cache_values,
            preferred_element_type=jnp.float32,
        )
        accum = accum + jnp.einsum(
            "rhs,rshd->rhd",
            fresh_weights.astype(jnp.bfloat16),
            new_values,
            preferred_element_type=jnp.float32,
        )
        results.append((accum / totals[..., None]).astype(jnp.bfloat16).reshape(req_dev, width))
    return jnp.stack(results)


def solution(mesh):
    placed = (
        P(None, ("groups", "replica"), None),
        P(None, None, "replica"),
        P("replica", None, None),
        P(None, None, "replica"),
        P(),
        P("groups"),
        P("groups"),
        P(("groups", "replica"), None),
        P(("groups", "replica"), None, None, None),
    )
    return jax.shard_map(
        per_device,
        mesh=mesh,
        in_specs=placed,
        out_specs=P(None, ("groups", "replica"), None),
        check_vma=False,
    )
```

profile of v0, /device:TPU:0, one launch (start us, length us, event | category | flops | bytes accessed | tf_op | source)
XLA Modules:
  0.0 254.0 jit_solution(17465866292132630686)
XLA Ops:
  0.0 1.0 select_reduce_fusion
  1.0 0.8 fusion.95
  1.9 26.4 %all-gather.2 = bf16[1,32,5120]{2,0,1:T(2,128)(2,1)} all-gather(bf16[1,2,5120]{2,0,1:T(2,128)(2,1)S(1)} %copy.80), channel_id=4, replica_groups=mesh['groups'=2,'replica'=16] {'replica'}, dimensions={1}, use_global_device_ids=true | all-gather | bytes 348160 | tf_op jit(solution)/shard_map/all_gather | solution.py:75
  28.4 19.4 %all-gather = bf16[1,32,5120]{2,0,1:T(2,128)(2,1)S(1)} all-gather(bf16[1,2,5120]{2,0,1:T(2,128)(2,1)S(1)} %copy.78), channel_id=2, replica_groups=mesh['groups'=2,'replica'=16] {'replica'}, dimensions={1}, use_global_device_ids=true | all-gather | bytes 348160 | tf_op jit(solution)/shard_map/all_gather | solution.py:75
  47.7 3.5 %fusion.8 = f32[32,64]{1,0:T(8,128)S(1)} fusion(bf16[4,64,5120]{2,1,0:T(8,128)(2,1)} %param.23, bf16[1,32,5120]{2,0,1:T(2,128)(2,1)} %all-gather.2, f32[32,4]{0,1:T(4,128)S(1)} %compare_convert_fusion), kind=kOutput, calls=%fused_computation.15 | convolution fusion | flops 83900416 | bytes 2957824 | tf_op jit(solution)/shard_map/il,hfl->ihf/dot_general | solution.py:83
  51.3 3.1 %fusion.6 = f32[32,64]{1,0:T(8,128)S(1)} fusion(bf16[4,64,5120]{2,1,0:T(8,128)(2,1)} %param.23, bf16[1,32,5120]{2,0,1:T(2,128)(2,1)S(1)} %all-gather, f32[32,4]{0,1:T(4,128)S(1)} %compare_convert_fusion), kind=kOutput, calls=%fused_computation.13 | convolution fusion | flops 83900416 | bytes 2957824 | tf_op jit(solution)/shard_map/il,hfl->ihf/dot_general | solution.py:83
  54.4 20.7 %all-gather.1 = bf16[1,32,5120]{2,0,1:T(2,128)(2,1)S(1)} all-gather(bf16[1,2,5120]{2,0,1:T(2,128)(2,1)S(1)} %copy.79), channel_id=3, replica_groups=mesh['groups'=2,'replica'=16] {'replica'}, dimensions={1}, use_global_device_ids=true | all-gather | bytes 348160 | tf_op jit(solution)/shard_map/all_gather | solution.py:75
  75.0 3.1 %fusion.7 = f32[32,64]{1,0:T(8,128)S(1)} fusion(bf16[4,64,5120]{2,1,0:T(8,128)(2,1)} %param.23, bf16[1,32,5120]{2,0,1:T(2,128)(2,1)S(1)} %all-gather.1, f32[32,4]{0,1:T(4,128)S(1)} %compare_convert_fusion), kind=kOutput, calls=%fused_computation.14 | convolution fusion | flops 83900416 | bytes 2957824 | tf_op jit(solution)/shard_map/il,hfl->ihf/dot_general | solution.py:83
  78.1 3.0 %fusion.13 = f32[32,3,320]{2,0,1:T(8,128)S(1)} fusion(bf16[3,5120,320]{1,2,0:T(8,128)(2,1)S(1)} %copy-done.1, bf16[1,32,5120]{2,0,1:T(2,128)(2,1)S(1)} %all-gather.1), kind=kOutput, calls=%fused_computation.20 | convolution fusion | flops 314572800 | bytes 10280960 | tf_op jit(solution)/shard_map/nd,idc->nic/dot_general | solution.py:77
  81.2 1.9 gather_fusion
  83.1 57.9 %all-reduce.2 = (bf16[32,64]{1,0:T(8,128)(2,1)S(1)}, bf16[32,64]{1,0:T(8,128)(2,1)S(1)}, bf16[32,64]{1,0:T(8,128)(2,1)S(1)}) all-reduce(f32[32,64]{1,0:T(8,128)S(1)} %fusion.8, f32[32,64]{1,0:T(8,128)S(1)} %fusion.6, f32[32,64]{1,0:T(8,128)S(1)} %fusion.7), channel_id=1, replica_groups=mesh['groups'=2,'replica'=16] {'replica'}, use_global_device_ids=true, to_apply=%region_14.15 | all-reduce | flops 6144 | bytes 36864 | tf_op jit(solution)/shard_map/psum | solution.py:89
  141.1 1.8 fusion.80
  142.9 0.7 copy.35
  143.6 3.7 %all-to-all-start.1 = ((bf16[32,3,320]{2,1,0:T(4,128)(2,1)}), bf16[32,3,320]{2,1,0:T(4,128)(2,1)S(1)}, u32[]{:S(2)}, u32[]{:S(2)}) async-start(bf16[32,3,320]{2,1,0:T(4,128)(2,1)} %copy.35), calls=%async_computation.1 | async-start | bytes 196608 | tf_op jit(solution)/shard_map/all_to_all | solution.py:100
  147.8 7.1 %fusion.16 = f32[32,3,320]{2,0,1:T(8,128)S(1)} fusion(bf16[3,5120,320]{1,2,0:T(8,128)(2,1)} %param.22, bf16[1,32,5120]{2,0,1:T(2,128)(2,1)} %copy-done.4), kind=kOutput, calls=%fused_computation.23 | convolution fusion | flops 314572800 | bytes 10280960 | tf_op jit(solution)/shard_map/nd,idc->nic/dot_general | solution.py:77
  154.9 0.7 add_convert_fusion.7
  156.2 0.7 iota_compare_fusion.2
  157.4 7.1 %fusion.10 = f32[32,3,320]{2,0,1:T(8,128)S(1)} fusion(bf16[3,5120,320]{1,2,0:T(8,128)(2,1)} %param.22, bf16[1,32,5120]{2,0,1:T(2,128)(2,1)} %all-gather.2), kind=kOutput, calls=%fused_computation.17 | convolution fusion | flops 314572800 | bytes 10280960 | tf_op jit(solution)/shard_map/nd,idc->nic/dot_general | solution.py:77
  164.5 1.3 reshape.600
  165.8 0.7 fusion.88
  167.0 15.5 %gather_fusion.1 = bf16[64,4,2,5120]{3,2,1,0:T(2,128)(2,1)} fusion(bf16[64,4,2,5120]{3,2,1,0:T(2,128)(2,1)} %param.29, s32[1024]{0:T(1024)} %pad_clamp_fusion), kind=kCustom, calls=%fused_computation.1 | custom fusion | bytes 10486016 | tf_op jit(solution)/shard_map/gather | solution.py:63
  182.5 12.4 %reshape.601 = bf16[2,128,2,40,128]{4,3,2,1,0:T(8,128)(2,1)} reshape(bf16[64,4,2,5120]{3,2,1,0:T(2,128)(2,1)} %gather_fusion.1) | data formatting | bytes 10485760 | tf_op jit(solution)/shard_map/reshape | solution.py:63
  194.9 5.9 %slice_bitcast_fusion.1 = (bf16[2,128,40,128]{3,2,1,0:T(8,128)(2,1)}, bf16[2,128,40,128]{3,2,1,0:T(8,128)(2,1)}) fusion(bf16[2,128,2,40,128]{4,3,2,1,0:T(8,128)(2,1)} %reshape.601), kind=kLoop, calls=%fused_computation.3 | loop fusion | bytes 10485760 | tf_op jit(solution)/shard_map/squeeze | solution.py:66
  201.8 0.7 multiply_cosine_fusion.1
  203.0 4.7 %copy.43 = bf16[2,128,40,128]{1,3,2,0:T(8,128)(2,1)} copy(bf16[2,128,40,128]{3,2,1,0:T(8,128)(2,1)} %get-tuple-element.93) | data formatting | bytes 5242880 | tf_op jit(solution)/shard_map/squeeze | solution.py:66
  207.7 0.7 copy.32
  208.4 0.7 copy.38
  209.7 5.8 %all-to-all-start = ((bf16[32,3,320]{2,1,0:T(4,128)(2,1)}), bf16[32,3,320]{2,1,0:T(4,128)(2,1)S(1)}, u32[]{:S(2)}, u32[]{:S(2)}) async-start(bf16[32,3,320]{2,1,0:T(4,128)(2,1)} %copy.32), calls=%async_computation | async-start | bytes 196608 | tf_op jit(solution)/shard_map/all_to_all | solution.py:100
  215.7 7.2 %all-to-all-done = bf16[32,3,320]{2,1,0:T(4,128)(2,1)S(1)} async-done(((bf16[32,3,320]{2,1,0:T(4,128)(2,1)}), bf16[32,3,320]{2,1,0:T(4,128)(2,1)S(1)}, u32[]{:S(2)}, u32[]{:S(2)}) %all-to-all-start) | async-done | bytes 61472 | tf_op jit(solution)/shard_map/all_to_all | solution.py:100
  222.9 3.7 %all-to-all-start.2 = ((bf16[32,3,320]{2,1,0:T(4,128)(2,1)}), bf16[32,3,320]{2,1,0:T(4,128)(2,1)S(1)}, u32[]{:S(2)}, u32[]{:S(2)}) async-start(bf16[32,3,320]{2,1,0:T(4,128)(2,1)} %copy.38), calls=%async_computation.2 | async-start | bytes 196608 | tf_op jit(solution)/shard_map/all_to_all | solution.py:100
  226.9 0.9 fusion.74
  227.9 2.5 fusion.55
  230.6 0.8 fusion.58
  231.5 0.6 copy-done.5
  232.4 1.4 all-to-all-done.2
  234.2 2.5 fusion.52
  237.8 0.7 maximum_dynamic-update-slice_fusion.1
  238.5 1.0 fusion.28
  240.1 0.7 fusion.90
  240.7 0.7 fusion.93
  241.4 0.7 fusion.91
  242.1 0.7 fusion.62
  242.8 0.7 fusion.94
  243.9 0.7 copy.72
  244.6 2.5 fusion
  248.0 2.5 fusion.2
  250.7 2.5 fusion.4
  253.3 0.7 pad_maximum_fusion.3
  (107 shorter events, 8.8 us)
Async XLA Ops:
  0.0 81.2 %copy-start = (bf16[64,64,320]{2,1,0:T(8,128)(2,1)S(1)}, bf16[64,64,320]{2,1,0:T(8,128)(2,1)}, u32[]{:S(2)}) copy-start(bf16[64,64,320]{2,1,0:T(8,128)(2,1)} %param.24) | copy-start | bytes 7864324
  28.4 49.8 %copy-start.1 = (bf16[3,5120,320]{1,2,0:T(8,128)(2,1)S(1)}, bf16[3,5120,320]{1,2,0:T(8,128)(2,1)}, u32[]{:S(2)}) copy-start(bf16[3,5120,320]{1,2,0:T(8,128)(2,1)} %param.22) | copy-start | bytes 29491204
  47.7 6.6 %copy-start.4 = (bf16[1,32,5120]{2,0,1:T(2,128)(2,1)}, bf16[1,32,5120]{2,0,1:T(2,128)(2,1)S(1)}, u32[]{:S(2)}) copy-start(bf16[1,32,5120]{2,0,1:T(2,128)(2,1)S(1)} %all-gather) | copy-start | bytes 983044
  143.6 66.1 %all-to-all-start.1 = ((bf16[32,3,320]{2,1,0:T(4,128)(2,1)}), bf16[32,3,320]{2,1,0:T(4,128)(2,1)S(1)}, u32[]{:S(2)}, u32[]{:S(2)}) async-start(bf16[32,3,320]{2,1,0:T(4,128)(2,1)} %copy.35), calls=%async_computation.1 | async-start | bytes 196608 | tf_op jit(solution)/shard_map/all_to_all | solution.py:100
  147.8 7.1 %copy-start.16 = (s32[32]{0:T(128)S(1)}, s32[32]{0:T(128)}, u32[]{:S(2)}) copy-start(s32[32]{0:T(128)} %param.27) | copy-start | bytes 388
  194.9 5.9 %copy-start.3 = (bf16[32,64,320]{2,1,0:T(8,128)(2,1)S(1)}, bf16[32,64,320]{2,1,0:T(8,128)(2,1)}, u32[]{:S(2)}) copy-start(bf16[32,64,320]{2,1,0:T(8,128)(2,1)} %gather_fusion) | copy-start | bytes 3932164
  200.9 0.9 copy-start.12
  200.9 0.9 copy-start.13
  200.9 0.9 copy-start.14
  200.9 0.9 copy-start.15
  209.7 13.2 %all-to-all-start = ((bf16[32,3,320]{2,1,0:T(4,128)(2,1)}), bf16[32,3,320]{2,1,0:T(4,128)(2,1)S(1)}, u32[]{:S(2)}, u32[]{:S(2)}) async-start(bf16[32,3,320]{2,1,0:T(4,128)(2,1)} %copy.32), calls=%async_computation | async-start | bytes 196608 | tf_op jit(solution)/shard_map/all_to_all | solution.py:100
  222.9 10.9 %all-to-all-start.2 = ((bf16[32,3,320]{2,1,0:T(4,128)(2,1)}), bf16[32,3,320]{2,1,0:T(4,128)(2,1)S(1)}, u32[]{:S(2)}, u32[]{:S(2)}) async-start(bf16[32,3,320]{2,1,0:T(4,128)(2,1)} %copy.38), calls=%async_computation.2 | async-start | bytes 196608 | tf_op jit(solution)/shard_map/all_to_all | solution.py:100
  226.8 3.8 %copy-start.2 = (bf16[2,128,40,128]{1,3,2,0:T(8,128)(2,1)S(1)}, bf16[2,128,40,128]{1,3,2,0:T(8,128)(2,1)}, u32[]{:S(2)}) copy-start(bf16[2,128,40,128]{1,3,2,0:T(8,128)(2,1)} %copy.43) | copy-start | bytes 7864324
  231.4 8.2 %copy-start.10 = (pred[2,128]{1,0:T(4,128)(4,1)S(1)}, pred[2,128]{1,0:T(4,128)(4,1)}, u32[]{:S(2)}) copy-start(pred[2,128]{1,0:T(4,128)(4,1)} %iota_compare_fusion.2) | copy-start | bytes 772
  231.4 8.3 %copy-start.11 = (pred[3]{0:T(512)(128)(4,1)S(1)}, pred[3]{0:T(512)(128)(4,1)}, u32[]{:S(2)}) copy-start(pred[3]{0:T(512)(128)(4,1)} %iota_compare_fusion.5) | copy-start | bytes 13
  231.5 0.6 copy-start.5
  233.9 2.8 %copy-start.6 = (bf16[2,3,40,128]{3,2,0,1:T(8,128)(2,1)S(1)}, bf16[2,3,40,128]{3,2,0,1:T(8,128)(2,1)}, u32[]{:S(2)}) copy-start(bf16[2,3,40,128]{3,2,0,1:T(8,128)(2,1)} %copy-done.5) | copy-start | bytes 184324
  236.8 0.6 copy-start.7
  243.6 4.4 %copy-start.9 = (bf16[2,40,128,1]{2,1,0,3:T(8,128)(2,1)S(1)}, bf16[2,40,128,1]{2,1,0,3:T(8,128)(2,1)}, u32[]{:S(2)}) copy-start(bf16[2,40,128,1]{2,1,0,3:T(8,128)(2,1)} %get-tuple-element.120) | copy-start | bytes 61444
  244.6 3.0 %copy-start.8 = (bf16[2,40,3,1]{2,3,1,0:T(2,128)(2,1)S(1)}, bf16[2,40,3,1]{2,3,1,0:T(2,128)(2,1)}, u32[]{:S(2)}) copy-start(bf16[2,40,3,1]{2,3,1,0:T(2,128)(2,1)} %copy.72) | copy-start | bytes 1444
where the time goes:
time: 255 us; the launch traced here: 254 us
  blocking collectives  124 us (49%)
  local copies, waits for them, and re-layouts  47.9 us (19%)
  matrix products  44.9 us (18%)
  other arithmetic  14.6 us (6%)
  starting transfers between devices  13.2 us (5%)
  waiting for transfers between devices  8.57 us (3%)
    all_gather x3, blocking collectives, per_device(): block_row_list = lax.all_gather(current, 'replica', axis=0, tiled=True)  66.4 us
    psum x1, blocking collectives, per_device(): lax.psum(produced[:, 3 * columns:], 'replica').astype(jnp.bfloat16)  57.9 us
    dot_general x3, matrix products, per_device(): jnp.einsum('nd,idc->nic', block_row_list, query_key_value_weight, preferr...  17.2 us
    gather x1, local copies, waits for them, and re-layouts, per_device(): key_value_pool[request_page_table.reshape(-1)]  15.5 us
    all_to_all x3, starting transfers between devices, per_device(): lax.all_to_all(combined, 'replica', split_axis=0, concat_axis=2, tiled=True)  13.2 us
    reshape x1, local copies, waits for them, and re-layouts, per_device(): key_value_pool[request_page_table.reshape(-1)]  12.4 us
    squeeze x2, local copies, waits for them, and re-layouts, per_device(): cache_keys = cache[:, :, 0]  10.7 us
    dot_general x3, matrix products, per_device(): jnp.einsum('il,hfl->ihf', block_row_list, adapter_down_maps, preferred_el...  9.65 us
  transfers between devices with their start and end apart: 3, of which 2 were waited for; matrix products, arithmetic and copies ran while one was open for 26% of the time, Pallas kernels for 0%

commit v1 on v0

v1 whole, which is shorter than its diff:
```python
import functools

import jax
import jax.numpy as jnp
from jax import lax
from jax.experimental import pallas as pl
from jax.experimental.pallas import tpu as pltpu
from jax.sharding import PartitionSpec as P

HD = 128
ROWS = 8
HEAD_BLOCK = 8

adapter_scale = 2.0
masked_score = -1e30


def attention_kernel(steps, req_dev, q_ref, k_ref, v_ref, cos_ref, sin_ref, live_ref, kv_ref, out_ref, kn_ref, vn_ref):
    rows = steps * req_dev
    width = q_ref.shape[1]
    lanes = HEAD_BLOCK * HD
    group = rows * HEAD_BLOCK
    cosine = cos_ref[...]
    sine = sin_ref[...]

    def rotated(x):
        pieces = []
        for h in range(HEAD_BLOCK):
            head = x[:, h * HD : (h + 1) * HD]
            pieces.append(head * cosine + pltpu.roll(head, HD // 2, 1) * sine)
        return jnp.concatenate(pieces, axis=1)

    row_head = lax.broadcasted_iota(jnp.int32, (group, lanes), 0) % HEAD_BLOCK
    lane_head = lax.broadcasted_iota(jnp.int32, (group, lanes), 1) // HD
    own_head = row_head == lane_head
    row_j = lax.broadcasted_iota(jnp.int32, (group, 16), 0) // HEAD_BLOCK
    new_j = lax.broadcasted_iota(jnp.int32, (group, 16), 1)
    new_live = (new_j < rows) & (new_j % req_dev == row_j % req_dev) & (new_j // req_dev <= row_j // req_dev)
    live_all = live_ref[...]
    live = jnp.concatenate(
        [
            jnp.broadcast_to(live_all[j % req_dev : j % req_dev + 1], (HEAD_BLOCK, live_all.shape[1]))
            for j in range(rows)
        ],
        axis=0,
    )
    live = live > 0
    kn_ref[...] = jnp.zeros_like(kn_ref)
    vn_ref[...] = jnp.zeros_like(vn_ref)
    contract_lanes = (((1,), (1,)), ((), ()))
    for c in range(width // lanes):
        cols = slice(c * lanes, (c + 1) * lanes)
        query = rotated(q_ref[:, cols].astype(jnp.float32))
        key_new = rotated(k_ref[:, cols].astype(jnp.float32))
        kn_ref[0:8] = key_new
        vn_ref[0:8] = v_ref[:, cols].astype(jnp.float32)
        kn = kn_ref[...].astype(jnp.bfloat16)
        vn = vn_ref[...].astype(jnp.bfloat16)
        spread = jnp.concatenate(
            [jnp.broadcast_to(query[j : j + 1], (HEAD_BLOCK, lanes)) for j in range(rows)], axis=0
        )
        spread = jnp.where(own_head, spread, 0.0).astype(jnp.bfloat16)
        kv = kv_ref[:, cols]
        scores = lax.dot_general(spread, kv, contract_lanes, preferred_element_type=jnp.float32) * (HD**-0.5)
        scores = jnp.where(live, scores, masked_score)
        fresh = lax.dot_general(spread, kn, contract_lanes, preferred_element_type=jnp.float32) * (HD**-0.5)
        fresh = jnp.where(new_live, fresh, masked_score)
        top = jnp.maximum(jnp.max(scores, axis=1, keepdims=True), jnp.max(fresh, axis=1, keepdims=True))
        weights = jnp.where(live, jnp.exp(scores - top), 0.0)
        fresh = jnp.where(new_live, jnp.exp(fresh - top), 0.0)
        totals = jnp.sum(weights, axis=1, keepdims=True) + jnp.sum(fresh, axis=1, keepdims=True)
        weights = pltpu.roll(weights, 1, 1).astype(jnp.bfloat16)
        mixed = jnp.dot(weights, kv, preferred_element_type=jnp.float32)
        mixed = mixed + jnp.dot(fresh.astype(jnp.bfloat16), vn, preferred_element_type=jnp.float32)
        mixed = jnp.where(own_head, mixed / totals, 0.0)
        out = jnp.sum(mixed.reshape(rows, HEAD_BLOCK, lanes), axis=1)
        out_ref[:, cols] = out.astype(out_ref.dtype)


def attention(steps, req_dev, q, k, v, cosine, sine, live, kv):
    rows = steps * req_dev
    width = q.shape[1]
    vmem = pl.BlockSpec(memory_space=pltpu.VMEM)
    return pl.pallas_call(
        functools.partial(attention_kernel, steps, req_dev),
        out_shape=jax.ShapeDtypeStruct((rows, width), jnp.bfloat16),
        in_specs=[vmem] * 7,
        out_specs=vmem,
        scratch_shapes=[pltpu.VMEM((16, HEAD_BLOCK * HD), jnp.float32)] * 2,
        compiler_params=pltpu.CompilerParams(vmem_limit_bytes=32 * 2**20),
        cost_estimate=pl.CostEstimate(flops=10**9, bytes_accessed=6 * 10**6, transcendentals=0),
        name="attention",
    )(q, k, v, cosine, sine, live, kv)


def per_device(
    replicas,
    hidden,
    query_key_value_weight,
    adapter_down_maps,
    adapter_up_maps,
    adapter_storage_row,
    request_adapter,
    lengths,
    request_page_table,
    key_value_pool,
):
    my_index = lax.axis_index("replica")
    steps, req_dev, width = hidden.shape
    rows = steps * req_dev
    columns = query_key_value_weight.shape[2]
    holder_count, rank, _ = adapter_down_maps.shape
    pool_pages, page_len = key_value_pool.shape[:2]
    adapter_count = adapter_storage_row.shape[0]
    chips = replicas // 2
    total = replicas * ROWS

    block = jnp.pad(hidden.reshape(rows, width), ((0, ROWS - rows), (0, 0)))
    same_core = [[2 * chip + core for chip in range(chips)] for core in range(2)]
    mine = lax.all_to_all(
        jnp.broadcast_to(block[None], (chips, ROWS, width)),
        "replica",
        split_axis=0,
        concat_axis=0,
        axis_index_groups=same_core,
        tiled=True,
    )
    other = lax.ppermute(mine, "replica", [(i, i ^ 1) for i in range(replicas)])
    first = my_index % 2 == 0
    gathered = jnp.stack([jnp.where(first, mine, other), jnp.where(first, other, mine)])
    gathered = gathered.reshape(total, width)

    stored_rows = jnp.sum(
        jnp.where(
            request_adapter[:, None] == jnp.arange(adapter_count, dtype=jnp.int32)[None, :],
            adapter_storage_row[None, :],
            0,
        ),
        axis=1,
    )
    by_block = stored_rows.reshape(chips, 2, 1, req_dev).transpose(1, 0, 2, 3)
    by_block = jnp.broadcast_to(by_block, (2, chips, steps, req_dev)).reshape(2, chips, rows)
    row_stored = jnp.pad(by_block, ((0, 0), (0, 0), (0, ROWS - rows)), constant_values=-1).reshape(total)

    down = jnp.einsum("nd,hfd->nhf", gathered, adapter_down_maps, preferred_element_type=jnp.float32)
    slots = my_index * holder_count + jnp.arange(holder_count, dtype=jnp.int32)
    own = row_stored[:, None] == slots[None, :]
    low = jnp.sum(jnp.where(own[:, :, None], down, 0.0), axis=1).astype(jnp.bfloat16)
    low = jnp.concatenate([low[: total // 2], low[total // 2 :]], axis=1)
    low = lax.all_to_all(
        jnp.broadcast_to(low[None], (replicas,) + low.shape), "replica", split_axis=0, concat_axis=0, tiled=True
    )
    low = jnp.sum(low.astype(jnp.float32), axis=0)
    low = jnp.concatenate([low[:, :rank], low[:, rank:]], axis=0)

    projected = jnp.einsum("nd,idc->nic", gathered, query_key_value_weight, preferred_element_type=jnp.float32)

    def update(first_adapter, maps):
        held = maps.shape[0]
        which = first_adapter + jnp.arange(held, dtype=jnp.int32)
        wide = jnp.where((row_stored[:, None] == which[None, :])[:, :, None], low[:, None, :], 0.0)
        return jnp.dot(
            wide.astype(jnp.bfloat16).reshape(total, held * rank),
            maps.reshape(held * rank, columns),
            preferred_element_type=jnp.float32,
        )

    step_adapters = 64
    if adapter_count <= step_adapters:
        updated = update(0, adapter_up_maps)
    else:
        updated = lax.fori_loop(
            0,
            adapter_count // step_adapters,
            lambda i, sofar: sofar
            + update(
                i * step_adapters,
                lax.dynamic_slice_in_dim(adapter_up_maps, i * step_adapters, step_adapters, 0),
            ),
            jnp.zeros((total, columns), jnp.float32),
        )
    value = projected[:, 2] + adapter_scale * updated
    combined = jnp.concatenate([projected[:, 0], projected[:, 1], value], axis=1).astype(jnp.bfloat16)
    combined = combined.reshape(2, chips, ROWS, 3 * columns).transpose(1, 0, 2, 3)
    combined = combined.reshape(replicas, ROWS, 3 * columns)
    arrived = lax.all_to_all(combined, "replica", split_axis=0, concat_axis=0, tiled=True)
    arrived = arrived.reshape(replicas, ROWS, 3, columns).transpose(2, 1, 0, 3).reshape(3, ROWS, width)

    my_lengths = lax.dynamic_slice_in_dim(lengths, my_index * req_dev, req_dev)
    positions = (my_lengths[None, :] + jnp.arange(steps, dtype=jnp.int32)[:, None]).reshape(rows)
    positions = jnp.pad(positions, (0, ROWS - rows))
    half = HD // 2
    frequency = jnp.exp(jnp.arange(half, dtype=jnp.float32) * (-2.0 * jnp.log(10000.0) / HD))
    angles = positions.astype(jnp.float32)[:, None] * frequency[None, :]
    cosine = jnp.cos(angles)
    sine = jnp.sin(angles)
    cosine = jnp.concatenate([cosine, cosine], axis=1)
    sine = jnp.concatenate([-sine, sine], axis=1)

    pages = jnp.arange(pool_pages, dtype=jnp.int32)
    max_pages = request_page_table.shape[1]
    place = jnp.max(
        jnp.where(
            request_page_table[:, :, None] == pages[None, None, :],
            jnp.arange(max_pages, dtype=jnp.int32)[None, :, None],
            -1,
        ),
        axis=1,
    )
    token = place[:, :, None] * page_len + jnp.arange(page_len, dtype=jnp.int32)[None, None, :]
    alive = (place[:, :, None] >= 0) & (token < my_lengths[:, None, None])
    live = jnp.stack([alive, jnp.zeros_like(alive)], axis=-1).astype(jnp.int32)
    live = live.reshape(req_dev, pool_pages * page_len * 2)

    kv = key_value_pool.reshape(pool_pages * page_len * 2, width)
    out = attention(steps, req_dev, arrived[0], arrived[1], arrived[2], cosine, sine, live, kv)
    return out.reshape(steps, req_dev, width)


def solution(mesh):
    placed = (
        P(None, ("groups", "replica"), None),
        P(None, None, "replica"),
        P("replica", None, None),
        P(None, None, "replica"),
        P(),
        P("groups"),
        P("groups"),
        P(("groups", "replica"), None),
        P(("groups", "replica"), None, None, None),
    )
    return jax.shard_map(
        functools.partial(per_device, mesh.shape["replica"]),
        mesh=mesh,
        in_specs=placed,
        out_specs=P(None, ("groups", "replica"), None),
        check_vma=False,
    )
```

time: 255 us -> 87.3 us (0.34)
  blocking collectives: 124 us -> 0 us
  matrix products: 44.9 us -> 11.4 us
  local copies, waits for them, and re-layouts: 47.9 us -> 31 us
  other arithmetic: 14.6 us -> 5.71 us
  waiting for transfers between devices: 8.57 us -> 16.4 us
  Pallas kernels: 0 us -> 4.2 us
  starting transfers between devices: 13.2 us -> 17.4 us
    all_gather x3 -> x0, blocking collectives: 66.4 us -> none  [per_device(): block_row_list = lax.all_gather(current, 'replica', axis=0, tiled=True)]
    psum x1 -> x0, blocking collectives: 57.9 us -> none  [per_device(): lax.psum(produced[:, 3 * columns:], 'replica').astype(jnp.bfloat16)]
    dot_general x21 -> x3, matrix products: 44.9 us -> 11.4 us  [the longest x1 7.72 us: per_device(): jnp.einsum('nd,idc->nic', gathered, query_key_value_weight, preferred_ele...]
    gather x2 -> x0, local copies, waits for them, and re-layouts: 17.4 us -> none  [the longest x1 15.5 us: per_device(): key_value_pool[request_page_table.reshape(-1)]]
    squeeze x2 -> x3, local copies, waits for them, and re-layouts: 10.7 us -> 0.39 us  [the longest x1 0.13 us: per_device(): arrived[2]]
    slice x4 -> x9, local copies, waits for them, and re-layouts: 0.86 us -> 6.59 us  [the longest x2 1.66 us: per_device(): projected[:, 0]]
    all_to_all x3, waiting for transfers between devices: 8.57 us -> 14.2 us  [the longest x1 14.2 us: per_device(): lax.all_to_all(jnp.broadcast_to(block[None], (chips, ROWS, width)), 'repl...]
    all_to_all x3, starting transfers between devices: 13.2 us -> 17.4 us  [the longest x1 7.28 us: per_device(): lax.all_to_all(jnp.broadcast_to(block[None], (chips, ROWS, width)), 'repl...]
  transfers between devices with their start and end apart: 3 -> 4, of which waited for: 2 -> 2; matrix products, arithmetic and copies ran while one was open for 26% -> 30% of each run, Pallas kernels for 0% -> 0%
where the time goes in v1:
time: 87.3 us; the launch traced here: 86.3 us
  local copies, waits for them, and re-layouts  31 us (36%)
  starting transfers between devices  17.4 us (20%)
  waiting for transfers between devices  16.4 us (19%)
  matrix products  11.4 us (13%)
  other arithmetic  5.71 us (7%)
  Pallas kernels  4.2 us (5%)
    all_to_all x1, waiting for transfers between devices, per_device(): lax.all_to_all(jnp.broadcast_to(block[None], (chips, ROWS, width)), 'repl...  14.2 us
    reshape x1, local copies, waits for them, and re-layouts, per_device(): kv = key_value_pool.reshape(pool_pages * page_len * 2, width)  11.4 us
    dot_general x1, matrix products, per_device(): jnp.einsum('nd,idc->nic', gathered, query_key_value_weight, preferred_ele...  7.72 us
    all_to_all x1, starting transfers between devices, per_device(): lax.all_to_all(jnp.broadcast_to(block[None], (chips, ROWS, width)), 'repl...  7.28 us
    all_to_all x1, starting transfers between devices, per_device(): lax.all_to_all(combined, 'replica', split_axis=0, concat_axis=0, tiled=True)  5.96 us
    pallas_call x1, Pallas kernels, attention(): pl.pallas_call(functools.partial(attention_kernel, steps, req_dev), out_s...  4.2 us
    all_to_all x1, starting transfers between devices, per_device(): lax.all_to_all(jnp.broadcast_to(low[None], (replicas,) + low.shape), 'rep...  4.19 us
    unnamed x9, local copies, waits for them, and re-layouts  3.65 us
  transfers between devices with their start and end apart: 4, of which 2 were waited for; matrix products, arithmetic and copies ran while one was open for 30% of the time, Pallas kernels for 0%

profile of v1, /device:TPU:0, one launch (start us, length us, event | category | flops | bytes accessed | tf_op | source)
XLA Modules:
  0.0 86.3 jit_solution(14724478987839005039)
XLA Ops:
  0.0 1.0 %reshape.143 = bf16[6,5120]{1,0:T(8,128)(2,1)S(1)} reshape(bf16[3,2,5120]{2,1,0:T(2,128)(2,1)} %param.9) | data formatting | bytes 122880 | tf_op jit(solution)/shard_map/reshape | solution.py:118
  1.0 0.9 %broadcast_in_dim.64 = bf16[8,8,5120]{2,1,0:T(8,128)(2,1)} broadcast(bf16[8,5120]{1,0:T(8,128)(2,1)S(1)} %pad.13), dimensions={1,2} | broadcast | bytes 737280 | tf_op jit(solution)/shard_map/broadcast_in_dim | solution.py:121
  1.9 7.3 %all-to-all-start = ((bf16[8,8,5120]{2,1,0:T(8,128)(2,1)}), bf16[8,8,5120]{2,1,0:T(8,128)(2,1)}, u32[]{:S(2)}, u32[]{:S(2)}) async-start(bf16[8,8,5120]{2,1,0:T(8,128)(2,1)} %broadcast_in_dim.64), calls=%async_computation | async-start | bytes 1310720 | tf_op jit(solution)/shard_map/all_to_all | solution.py:120
  9.2 0.8 select_reduce_fusion.1
  10.1 0.1 reshape.145
  10.2 0.1 copy.37
  10.3 0.1 copy.48
  10.4 0.1 eq.71
  10.5 0.7 dynamic_slice.3
  11.2 0.8 select_reduce_fusion
  12.0 0.3 fusion.7
  12.3 0.1 pad_convert_fusion
  12.4 14.2 %all-to-all-done = bf16[8,8,5120]{2,1,0:T(8,128)(2,1)} async-done(((bf16[8,8,5120]{2,1,0:T(8,128)(2,1)}), bf16[8,8,5120]{2,1,0:T(8,128)(2,1)}, u32[]{:S(2)}, u32[]{:S(2)}) %all-to-all-start) | async-done | bytes 655392 | tf_op jit(solution)/shard_map/all_to_all | solution.py:120
  26.7 2.2 %collective-permute-done = bf16[8,8,5120]{2,1,0:T(8,128)(2,1)S(1)} collective-permute-done((bf16[8,8,5120]{2,1,0:T(8,128)(2,1)}, bf16[8,8,5120]{2,1,0:T(8,128)(2,1)S(1)}, u32[]{:S(2)}, u32[]{:S(2)}) %collective-permute-start) | collective-permute-done | bytes 655392 | tf_op jit(solution)/shard_map/ppermute | solution.py:128
  28.9 1.2 %select_bitcast_fusion.1 = (bf16[1,8,8,5120]{3,2,1,0:T(8,128)(2,1)S(1)}, bf16[1,8,8,5120]{3,2,1,0:T(8,128)(2,1)S(1)}) fusion(bf16[8,8,5120]{2,1,0:T(8,128)(2,1)} %all-to-all-done, bf16[8,8,5120]{2,1,0:T(8,128)(2,1)S(1)} %collective-permute-done, pred[]{:T(512)S(6)} %eq.67), kind=kLoop, calls=%fused_computation.12 | loop fusion | flops 655360 | bytes 2621441 | tf_op jit(solution)/shard_map/stack | solution.py:130
  30.1 0.1 pad_maximum_fusion
  30.2 1.1 %copy-done.2 = bf16[2,8,8,5120]{3,2,1,0:T(8,128)(2,1)} copy-done((bf16[2,8,8,5120]{3,2,1,0:T(8,128)(2,1)}, bf16[2,8,8,5120]{3,2,1,0:T(8,128)(2,1)S(1)}, u32[]{:S(2)}) %copy-start.2) | copy-done | bytes 1310744
  31.3 0.8 fusion.3
  32.1 0.1 fusion.13
  32.2 0.1 copy.39
  32.3 0.8 broadcast_in_dim.102
  33.1 4.2 %all-to-all-start.1 = ((bf16[16,64,128]{2,1,0:T(8,128)(2,1)}), bf16[16,64,128]{2,1,0:T(8,128)(2,1)}, u32[]{:S(2)}, u32[]{:S(2)}) async-start(bf16[16,64,128]{2,1,0:T(8,128)(2,1)} %broadcast_in_dim.102), calls=%async_computation.1 | async-start | bytes 524288 | tf_op jit(solution)/shard_map/all_to_all | solution.py:150
  37.3 7.7 %fusion.14 = (bf16[128,3,320]{0,2,1:T(8,128)(2,1)S(1)}, f32[128,3,320]{0,2,1:T(8,128)}) fusion(bf16[128,5120,1]{1,0,2:T(8,128)(2,1)} %bitcast.42, bf16[3,5120,320]{1,2,0:T(8,128)(2,1)} %param.10), kind=kOutput, calls=%fused_computation.43 | convolution fusion | flops 1258414080 | bytes 11878400 | tf_op jit(solution)/shard_map/nd,idc->nic/dot_general | solution.py:156
  45.0 0.7 fusion.11
  45.7 1.0 %copy.34 = bf16[128,1,320]{2,0,1:T(8,128)(2,1)S(1)} copy(bf16[128,1,320]{0,2,1:T(8,128)(2,1)} %get-tuple-element.10) | data formatting | bytes 163840 | tf_op jit(solution)/shard_map/slice | solution.py:183
  46.7 1.6 %copy.35 = bf16[128,1,320]{2,0,1:T(8,128)(2,1)} copy(bf16[128,1,320]{0,2,1:T(8,128)(2,1)} %get-tuple-element.11) | data formatting | bytes 163840 | tf_op jit(solution)/shard_map/slice | solution.py:183
  48.3 1.0 %convert_reduce_fusion = bf16[64,128]{1,0:T(8,128)(2,1)S(1)} fusion(bf16[16,64,128]{2,1,0:T(8,128)(2,1)} %all-to-all-done.1), kind=kLoop, calls=%fused_computation.13 | loop fusion | flops 253952 | bytes 278528 | tf_op jit(solution)/shard_map/reduce_sum | solution.py:153
  49.3 0.1 fusion.12
  49.4 0.7 copy.40
  50.1 2.8 %fusion.2 = bf16[128,320]{0,1:T(8,128)(2,1)} fusion(bf16[64,64,320]{2,1,0:T(8,128)(2,1)S(1)} %copy-done, bf16[128,64]{0,1:T(8,128)(2,1)} %copy.40, pred[128,64]{0,1:T(8,128)(4,1)S(1)} %iota_compare_fusion.1, f32[128,3,320]{0,2,1:T(8,128)} %get-tuple-element.20), kind=kOutput, calls=%fused_computation.6 | convolution fusion | flops 336191488 | bytes 2891776 | tf_op jit(solution)/shard_map/dot_general | solution.py:162
  52.9 1.6 %copy.41 = bf16[128,320]{1,0:T(8,128)(2,1)} copy(bf16[128,320]{0,1:T(8,128)(2,1)} %fusion.2) | data formatting | bytes 163840 | tf_op jit(solution)/shard_map/convert.4
  54.6 1.0 %maximum_bitcast_fusion = bf16[8,2,8,960]{3,2,0,1:T(8,128)(2,1)S(1)} fusion(bf16[2,8,8,320]{3,2,1,0:T(8,128)(2,1)} %bitcast.47, bf16[2,8,8,320]{3,2,1,0:T(8,128)(2,1)} %bitcast.46, bf16[2,8,8,320]{3,2,1,0:T(8,128)(2,1)S(1)} %bitcast.45), kind=kLoop, calls=%fused_computation.14 | loop fusion | flops 737280 | bytes 491520 | tf_op jit(solution)/shard_map/transpose | solution.py:184
  55.6 0.7 copy.42
  56.3 6.0 %all-to-all-start.2 = ((bf16[16,8,960]{2,1,0:T(8,128)(2,1)}), bf16[16,8,960]{2,1,0:T(8,128)(2,1)}, u32[]{:S(2)}, u32[]{:S(2)}) async-start(bf16[16,8,960]{2,1,0:T(8,128)(2,1)} %bitcast.44), calls=%async_computation.2 | async-start | bytes 524288 | tf_op jit(solution)/shard_map/all_to_all | solution.py:186
  62.3 0.1 add.71
  62.4 0.3 reshape.154.live_ref
  62.6 11.4 %reshape.151.kv_ref = bf16[512,5120]{1,0:T(8,128)(2,1)} reshape(bf16[64,4,2,5120]{3,2,1,0:T(2,128)(2,1)} %param.17) | data formatting | bytes 10485760 | tf_op jit(solution)/shard_map/reshape | solution.py:215
  74.0 0.1 fusion.8
  74.2 1.1 %reshape.148 = bf16[16,8,3,320]{3,2,1,0:T(4,128)(2,1)S(1)} reshape(bf16[16,8,960]{2,1,0:T(8,128)(2,1)} %all-to-all-done.2) | data formatting | bytes 491520 | tf_op jit(solution)/shard_map/reshape | solution.py:187
  75.4 1.2 %fusion.10 = (bf16[1,8,16,320]{3,0,1,2:T(2,128)(2,1)S(1)}, bf16[1,8,16,320]{3,0,1,2:T(2,128)(2,1)}, bf16[1,8,16,320]{3,0,1,2:T(2,128)(2,1)}) fusion(bf16[3,8,16,320]{3,0,1,2:T(4,128)(2,1)S(1)} %bitcast.43), kind=kLoop, calls=%fused_computation.39 | loop fusion | bytes 491520 | tf_op jit(solution)/shard_map/slice | solution.py:216
  76.6 0.1 squeeze.17.v_ref
  76.7 1.0 %copy.44 = bf16[1,8,16,320]{3,2,1,0:T(8,128)(2,1)S(1)} copy(bf16[1,8,16,320]{3,0,1,2:T(2,128)(2,1)} %get-tuple-element.8) | data formatting | bytes 163840 | tf_op jit(solution)/shard_map/slice | solution.py:216
  77.7 0.1 squeeze.16.k_ref
  77.8 1.0 %copy.43 = bf16[1,8,16,320]{3,2,1,0:T(8,128)(2,1)S(1)} copy(bf16[1,8,16,320]{3,0,1,2:T(2,128)(2,1)} %get-tuple-element.9) | data formatting | bytes 163840 | tf_op jit(solution)/shard_map/slice | solution.py:216
  78.8 0.1 squeeze.15.q_ref
  78.9 2.5 %copy-done.1 = bf16[512,5120]{1,0:T(8,128)(2,1)S(1)} copy-done((bf16[512,5120]{1,0:T(8,128)(2,1)S(1)}, bf16[512,5120]{1,0:T(8,128)(2,1)}, u32[]{:S(2)}) %copy-start.1) | copy-done | bytes 5242904
  81.4 4.2 %attention.1 = bf16[6,5120]{1,0:T(8,128)(2,1)S(1)} custom-call(bf16[8,5120]{1,0:T(8,128)(2,1)S(1)} %squeeze.15.q_ref, bf16[8,5120]{1,0:T(8,128)(2,1)S(1)} %squeeze.16.k_ref, bf16[8,5120]{1,0:T(8,128)(2,1)S(1)} %squeeze.17.v_ref, f32[8,128]{1,0:T(8,128)S(1)} %get-tuple-element.21.cos_ref, f32[8,128]{1,0:T(8,128)S(1)} %get-tuple-element.22.sin_ref, ...), custom_call_target="tpu_custom_call" | custom-call | flops 1000000000 | bytes 6000000 | tf_op jit(solution)/shard_map/attention/pallas_call | solution.py:84
  85.6 0.7 reshape.152
  (24 shorter events, 0.3 us)
Async XLA Ops:
  0.0 50.1 %copy-start = (bf16[64,64,320]{2,1,0:T(8,128)(2,1)S(1)}, bf16[64,64,320]{2,1,0:T(8,128)(2,1)}, u32[]{:S(2)}) copy-start(bf16[64,64,320]{2,1,0:T(8,128)(2,1)} %param.12) | copy-start | bytes 7864324
  1.9 24.7 %all-to-all-start = ((bf16[8,8,5120]{2,1,0:T(8,128)(2,1)}), bf16[8,8,5120]{2,1,0:T(8,128)(2,1)}, u32[]{:S(2)}, u32[]{:S(2)}) async-start(bf16[8,8,5120]{2,1,0:T(8,128)(2,1)} %broadcast_in_dim.64), calls=%async_computation | async-start | bytes 1310720 | tf_op jit(solution)/shard_map/all_to_all | solution.py:120
  26.6 2.3 %collective-permute-start = (bf16[8,8,5120]{2,1,0:T(8,128)(2,1)}, bf16[8,8,5120]{2,1,0:T(8,128)(2,1)S(1)}, u32[]{:S(2)}, u32[]{:S(2)}) collective-permute-start(bf16[8,8,5120]{2,1,0:T(8,128)(2,1)} %all-to-all-done), channel_id=1, source_target_pairs={{0,1},{1,0},{2,3},{3,2},{4,5},{5,4},{6,7},{7,6},{8,9},{9,8},{10,11... | collective-permute-start | bytes 1966088 | tf_op jit(solution)/shard_map/ppermute | solution.py:128
  26.7 4.6 %copy-start.3 = (bf16[4,64,5120]{2,1,0:T(8,128)(2,1)S(1)}, bf16[4,64,5120]{2,1,0:T(8,128)(2,1)}, u32[]{:S(2)}) copy-start(bf16[4,64,5120]{2,1,0:T(8,128)(2,1)} %param.11) | copy-start | bytes 7864324
  30.2 1.1 %copy-start.2 = (bf16[2,8,8,5120]{3,2,1,0:T(8,128)(2,1)}, bf16[2,8,8,5120]{3,2,1,0:T(8,128)(2,1)S(1)}, u32[]{:S(2)}) copy-start(bf16[2,8,8,5120]{3,2,1,0:T(8,128)(2,1)S(1)} %pad_maximum_fusion) | copy-start | bytes 3932164
  33.1 15.2 %all-to-all-start.1 = ((bf16[16,64,128]{2,1,0:T(8,128)(2,1)}), bf16[16,64,128]{2,1,0:T(8,128)(2,1)}, u32[]{:S(2)}, u32[]{:S(2)}) async-start(bf16[16,64,128]{2,1,0:T(8,128)(2,1)} %broadcast_in_dim.102), calls=%async_computation.1 | async-start | bytes 524288 | tf_op jit(solution)/shard_map/all_to_all | solution.py:150
  56.3 17.9 %all-to-all-start.2 = ((bf16[16,8,960]{2,1,0:T(8,128)(2,1)}), bf16[16,8,960]{2,1,0:T(8,128)(2,1)}, u32[]{:S(2)}, u32[]{:S(2)}) async-start(bf16[16,8,960]{2,1,0:T(8,128)(2,1)} %bitcast.44), calls=%async_computation.2 | async-start | bytes 524288 | tf_op jit(solution)/shard_map/all_to_all | solution.py:186
  78.9 2.5 %copy-start.1 = (bf16[512,5120]{1,0:T(8,128)(2,1)S(1)}, bf16[512,5120]{1,0:T(8,128)(2,1)}, u32[]{:S(2)}) copy-start(bf16[512,5120]{1,0:T(8,128)(2,1)} %reshape.151.kv_ref) | copy-start | bytes 15728644

commit v2 on v1

--- a/solution.py
+++ b/solution.py
@@ -93,7 +93,38 @@
     )(q, k, v, cosine, sine, live, kv)
 
 
-def per_device(
+def rotation(my_lengths, steps):
+    rows = steps * my_lengths.shape[0]
+    positions = (my_lengths[None, :] + jnp.arange(steps, dtype=jnp.int32)[:, None]).reshape(rows)
+    positions = jnp.pad(positions, (0, ROWS - rows))
+    half = HD // 2
+    frequency = jnp.exp(jnp.arange(half, dtype=jnp.float32) * (-2.0 * jnp.log(10000.0) / HD))
+    angles = positions.astype(jnp.float32)[:, None] * frequency[None, :]
+    cosine = jnp.cos(angles)
+    sine = jnp.sin(angles)
+    cosine = jnp.concatenate([cosine, cosine], axis=1)
+    sine = jnp.concatenate([-sine, sine], axis=1)
+    return cosine, sine
+
+
+def live_rows(my_lengths, request_page_table, pool_pages, page_len):
+    pages = jnp.arange(pool_pages, dtype=jnp.int32)
+    max_pages = request_page_table.shape[1]
+    place = jnp.max(
+        jnp.where(
+            request_page_table[:, :, None] == pages[None, None, :],
+            jnp.arange(max_pages, dtype=jnp.int32)[None, :, None],
+            -1,
+        ),
+        axis=1,
+    )
+    token = place[:, :, None] * page_len + jnp.arange(page_len, dtype=jnp.int32)[None, None, :]
+    alive = (place[:, :, None] >= 0) & (token < my_lengths[:, None, None])
+    live = jnp.stack([alive, jnp.zeros_like(alive)], axis=-1).astype(jnp.int32)
+    return live.reshape(request_page_table.shape[0], pool_pages * page_len * 2)
+
+
+def general_plan(
     replicas,
     hidden,
     query_key_value_weight,
@@ -187,34 +218,360 @@
     arrived = arrived.reshape(replicas, ROWS, 3, columns).transpose(2, 1, 0, 3).reshape(3, ROWS, width)
 
     my_lengths = lax.dynamic_slice_in_dim(lengths, my_index * req_dev, req_dev)
-    positions = (my_lengths[None, :] + jnp.arange(steps, dtype=jnp.int32)[:, None]).reshape(rows)
-    positions = jnp.pad(positions, (0, ROWS - rows))
-    half = HD // 2
-    frequency = jnp.exp(jnp.arange(half, dtype=jnp.float32) * (-2.0 * jnp.log(10000.0) / HD))
-    angles = positions.astype(jnp.float32)[:, None] * frequency[None, :]
-    cosine = jnp.cos(angles)
-    sine = jnp.sin(angles)
-    cosine = jnp.concatenate([cosine, cosine], axis=1)
-    sine = jnp.concatenate([-sine, sine], axis=1)
-
-    pages = jnp.arange(pool_pages, dtype=jnp.int32)
-    max_pages = request_page_table.shape[1]
-    place = jnp.max(
-        jnp.where(
-            request_page_table[:, :, None] == pages[None, None, :],
-            jnp.arange(max_pages, dtype=jnp.int32)[None, :, None],
-            -1,
-        ),
-        axis=1,
-    )
-    token = place[:, :, None] * page_len + jnp.arange(page_len, dtype=jnp.int32)[None, None, :]
-    alive = (place[:, :, None] >= 0) & (token < my_lengths[:, None, None])
-    live = jnp.stack([alive, jnp.zeros_like(alive)], axis=-1).astype(jnp.int32)
-    live = live.reshape(req_dev, pool_pages * page_len * 2)
-
+    cosine, sine = rotation(my_lengths, steps)
+    live = live_rows(my_lengths, request_page_table, pool_pages, page_len)
     kv = key_value_pool.reshape(pool_pages * page_len * 2, width)
     out = attention(steps, req_dev, arrived[0], arrived[1], arrived[2], cosine, sine, live, kv)
     return out.reshape(steps, req_dev, width)
+
+
+def trade(value, mask, count):
+    return lax.ppermute(value, "replica", [(i, i ^ mask) for i in range(count)])
+
+
+def cache_kernel(pool_ref, out_ref, sem):
+    heads = out_ref.shape[0]
+    copies = [pltpu.make_async_copy(pool_ref.at[:, h], out_ref.at[h], sem.at[h]) for h in range(heads)]
+    for copy in copies:
+        copy.start()
+    for copy in copies:
+        copy.wait()
+
+
+def cache_by_head(pool):
+    tokens, heads = pool.shape[:2]
+    return pl.pallas_call(
+        cache_kernel,
+        out_shape=jax.ShapeDtypeStruct((heads, tokens, 2, HD), pool.dtype),
+        in_specs=[pl.BlockSpec(memory_space=pl.ANY)],
+        out_specs=pl.BlockSpec(memory_space=pltpu.VMEM),
+        scratch_shapes=[pltpu.SemaphoreType.DMA((heads,))],
+        compiler_params=pltpu.CompilerParams(vmem_limit_bytes=8 * 2**20),
+        cost_estimate=pl.CostEstimate(flops=0, bytes_accessed=2 * pool.size * 2, transcendentals=0),
+        name="cache_by_head",
+    )(pool)
+
+
+CONTRACT_LANES = (((1,), (1,)), ((), ()))
+
+
+def lanes_of(x_ref):
+    return jnp.concatenate([x_ref[c] for c in range(x_ref.shape[0])], axis=1)
+
+
+def low_kernel(count, slot_ref, down_ref, *refs):
+    blocks, (x_ref, low_ref, sem) = refs[:count], refs[count:]
+    steps = blocks[0].shape[0]
+    copies = []
+    for k, block in enumerate(blocks):
+        for t in range(steps):
+            at = k * steps + t
+            copies.append(pltpu.make_async_copy(block.at[t], x_ref.at[:, at], sem.at[at]))
+    for copy in copies:
+        copy.start()
+    for copy in copies:
+        copy.wait()
+    chunks, pairs = x_ref.shape[:2]
+    rows = 2 * pairs
+    holders, rank, width = down_ref.shape
+    x = lanes_of(x_ref.reshape(chunks, rows, HD))
+    maps = down_ref.reshape(holders * rank, width)[...]
+    made = lax.dot_general(x, maps, CONTRACT_LANES, preferred_element_type=jnp.float32)
+    slot = slot_ref[...]
+    low = jnp.zeros((rows, rank), jnp.float32)
+    for h in range(holders):
+        low = low + jnp.where(slot == h, made[:, h * rank : (h + 1) * rank], 0.0)
+    low_ref[...] = jnp.concatenate([low[: rows // 2], low[rows // 2 :]], axis=1).astype(low_ref.dtype)
+
+
+def low_of(blocks, slot, down):
+    count = len(blocks)
+    steps, chunks = blocks[0].shape[:2]
+    rows = count * steps * 2
+    rank = down.shape[1]
+    vmem = pl.BlockSpec(memory_space=pltpu.VMEM)
+    return pl.pallas_call(
+        functools.partial(low_kernel, count),
+        out_shape=(
+            jax.ShapeDtypeStruct((chunks, rows // 2, 2, HD), jnp.bfloat16),
+            jax.ShapeDtypeStruct((rows // 2, 2 * rank), jnp.bfloat16),
+        ),
+        in_specs=[vmem, vmem] + [pl.BlockSpec(memory_space=pl.ANY)] * count,
+        out_specs=(vmem, vmem),
+        scratch_shapes=[pltpu.SemaphoreType.DMA((count * steps,))],
+        compiler_params=pltpu.CompilerParams(vmem_limit_bytes=16 * 2**20),
+        cost_estimate=pl.CostEstimate(flops=10**8, bytes_accessed=4 * 10**6, transcendentals=0),
+        name="low_rows",
+    )(slot, down, *blocks)
+
+
+def put_chunks(buf, first, value):
+    wide = value.shape[1]
+    for c in range(-(-wide // HD)):
+        part = value[:, c * HD : min((c + 1) * HD, wide)]
+        if part.shape[1] < HD:
+            part = jnp.concatenate([part, jnp.zeros((part.shape[0], HD - part.shape[1]), part.dtype)], axis=1)
+        buf[first + c] = part.astype(buf.dtype)
+
+
+def send_blocks(buf, outs, sem):
+    steps = outs[0].shape[1]
+    copies = [
+        pltpu.make_async_copy(buf.at[:, k * steps : (k + 1) * steps], out, sem.at[k]) for k, out in enumerate(outs)
+    ]
+    for copy in copies:
+        copy.start()
+    for copy in copies:
+        copy.wait()
+
+
+def project_kernel(count, x_ref, w_ref, base_ref, *refs):
+    outs, (buf, sem) = refs[:count], refs[count:]
+    chunks, pairs = x_ref.shape[:2]
+    rows = 2 * pairs
+    x = lanes_of(x_ref.reshape(chunks, rows, HD))
+    columns = w_ref.shape[1]
+    each = -(-columns // HD)
+    flat = buf.reshape(buf.shape[0], rows, HD)
+    for i in range(2):
+        put_chunks(
+            flat, i * each, lax.dot_general(x, w_ref[i], CONTRACT_LANES, preferred_element_type=jnp.float32)
+        )
+    send_blocks(buf, outs, sem)
+    base_ref[...] = lax.dot_general(x, w_ref[2], CONTRACT_LANES, preferred_element_type=jnp.float32)
+
+
+def project(x, weight, count):
+    chunks, pairs = x.shape[:2]
+    columns = weight.shape[1]
+    each = -(-columns // HD)
+    steps = pairs // count
+    vmem = pl.BlockSpec(memory_space=pltpu.VMEM)
+    any_place = pl.BlockSpec(memory_space=pl.ANY)
+    piece = jax.ShapeDtypeStruct((2 * each, steps, 2, HD), jnp.bfloat16)
+    made = pl.pallas_call(
+        functools.partial(project_kernel, count),
+        out_shape=(jax.ShapeDtypeStruct((2 * pairs, columns), jnp.float32),) + (piece,) * count,
+        in_specs=[vmem, vmem],
+        out_specs=(vmem,) + (any_place,) * count,
+        scratch_shapes=[pltpu.VMEM((2 * each, pairs, 2, HD), jnp.bfloat16), pltpu.SemaphoreType.DMA((count,))],
+        compiler_params=pltpu.CompilerParams(vmem_limit_bytes=24 * 2**20),
+        cost_estimate=pl.CostEstimate(flops=10**9, bytes_accessed=11 * 10**6, transcendentals=0),
+        name="project",
+    )(x, weight)
+    return made[0], made[1:]
+
+
+def update_kernel(count, stored_ref, base_ref, up_ref, *refs):
+    lows, outs, (buf, sem) = refs[:count], refs[count : 2 * count], refs[2 * count :]
+    half, packed = lows[0].shape
+    rank = packed // 2
+    rows = 2 * half
+    per = half // (count // 2)
+    row = lax.broadcasted_iota(jnp.int32, (half, half), 0)
+    col = lax.broadcasted_iota(jnp.int32, (half, half), 1)
+    low = jnp.zeros((half, packed), jnp.float32)
+    for s in range(count):
+        piece = lows[s][...]
+        if s >= count // 2:
+            piece = jnp.concatenate([piece[:, rank:], piece[:, :rank]], axis=1)
+        near = s % (count // 2)
+        same = ((row // per) == ((col // per) ^ near)) & (row % per == col % per)
+        low = low + jnp.dot(
+            jnp.where(same, 1.0, 0.0).astype(jnp.bfloat16), piece, preferred_element_type=jnp.float32
+        )
+    low = jnp.concatenate([low[:, :rank], low[:, rank:]], axis=0)
+    adapters = up_ref.shape[0] // rank
+    batch = 256 // rank
+    spread = jnp.concatenate([low] * batch, axis=1)
+    which = lax.broadcasted_iota(jnp.int32, (rows, batch * rank), 1) // rank
+    ahead = stored_ref[...] - which
+    total = jnp.zeros(base_ref.shape, jnp.float32)
+    for a in range(0, adapters, batch):
+        wide = jnp.where(ahead == a, spread, 0.0).astype(jnp.bfloat16)
+        total = total + jnp.dot(wide, up_ref[a * rank : (a + batch) * rank], preferred_element_type=jnp.float32)
+    put_chunks(buf.reshape(buf.shape[0], rows, HD), 0, base_ref[...] + adapter_scale * total)
+    send_blocks(buf, outs, sem)
+
+
+def update_values(stored, base, up, lows):
+    count = len(lows)
+    rows, columns = base.shape
+    each = -(-columns // HD)
+    pairs = rows // 2
+    vmem = pl.BlockSpec(memory_space=pltpu.VMEM)
+    any_place = pl.BlockSpec(memory_space=pl.ANY)
+    piece = jax.ShapeDtypeStruct((each, pairs // count, 2, HD), jnp.bfloat16)
+    return pl.pallas_call(
+        functools.partial(update_kernel, count),
+        out_shape=(piece,) * count,
+        in_specs=[vmem] * (3 + count),
+        out_specs=(any_place,) * count,
+        scratch_shapes=[pltpu.VMEM((each, pairs, 2, HD), jnp.bfloat16), pltpu.SemaphoreType.DMA((count,))],
+        compiler_params=pltpu.CompilerParams(vmem_limit_bytes=16 * 2**20),
+        cost_estimate=pl.CostEstimate(flops=3 * 10**8, bytes_accessed=4 * 10**6, transcendentals=0),
+        name="update_values",
+    )(stored, base, up, *lows)
+
+
+def attend_kernel(count, me_ref, cos_ref, sin_ref, live_ref, cache_ref, *refs):
+    pieces, fresh_values = refs[:count], refs[count : 2 * count]
+    out_ref, kn_ref, vn_ref = refs[2 * count :]
+    steps = pieces[0].shape[1]
+    rows = 2 * steps
+    each = fresh_values[0].shape[0]
+    heads = 2 * out_ref.shape[1] // count
+    lanes = heads * HD
+    group = rows * HEAD_BLOCK
+    me = me_ref[0]
+    first_core = me % 2 == 0
+    cosine = cos_ref[...][:rows]
+    sine = sin_ref[...][:rows]
+    left = lax.broadcasted_iota(jnp.int32, (rows, HD), 1) < HD // 2
+
+    def chip_columns(near, far, at):
+        mine = [near[at + c].reshape(rows, HD).astype(jnp.float32) for c in range(each)]
+        theirs = [far[at + c].reshape(rows, HD).astype(jnp.float32) for c in range(each)]
+        low = [jnp.where(first_core, a, b) for a, b in zip(mine, theirs)]
+        high = [pltpu.roll(jnp.where(first_core, b, a), HD // 2, 1) for a, b in zip(mine, theirs)]
+        whole = low[:-1] + [jnp.where(left, low[-1], high[0])]
+        return whole + [jnp.where(left, a, b) for a, b in zip(high[:-1], high[1:])]
+
+    def rotated(parts):
+        return [x * cosine + pltpu.roll(x, HD // 2, 1) * sine for x in parts]
+
+    row_head = lax.broadcasted_iota(jnp.int32, (group, lanes), 0) % HEAD_BLOCK
+    lane_head = lax.broadcasted_iota(jnp.int32, (group, lanes), 1) // HD
+    own_head = row_head == lane_head
+    row_j = lax.broadcasted_iota(jnp.int32, (group, 16), 0) // HEAD_BLOCK
+    new_j = lax.broadcasted_iota(jnp.int32, (group, 16), 1)
+    new_live = (new_j < rows) & (new_j % 2 == row_j % 2) & (new_j // 2 <= row_j // 2)
+    live = jnp.concatenate(
+        [
+            jnp.broadcast_to(live_ref[j % 2 : j % 2 + 1, :], (HEAD_BLOCK, live_ref.shape[1]))
+            for j in range(rows)
+        ],
+        axis=0,
+    )
+    live = live > 0
+    kn_ref[...] = jnp.zeros_like(kn_ref)
+    vn_ref[...] = jnp.zeros_like(vn_ref)
+    tokens = cache_ref.shape[1] * 2
+    cache = cache_ref.reshape(cache_ref.shape[0], tokens, HD)
+    for pair in range(count // 2):
+        base = ((me // 2) ^ pair) * heads
+        near, far = pieces[2 * pair], pieces[2 * pair + 1]
+        query = jnp.concatenate(rotated(chip_columns(near, far, 0)), axis=1)
+        key_new = jnp.concatenate(rotated(chip_columns(near, far, each)), axis=1)
+        value_new = jnp.concatenate(chip_columns(fresh_values[2 * pair], fresh_values[2 * pair + 1], 0), axis=1)
+        kn_ref[0:rows] = key_new
+        vn_ref[0:rows] = value_new
+        kn = kn_ref[...].astype(jnp.bfloat16)
+        vn = vn_ref[...].astype(jnp.bfloat16)
+        spread = jnp.concatenate(
+            [jnp.broadcast_to(query[j : j + 1], (HEAD_BLOCK, lanes)) for j in range(rows)], axis=0
+        )
+        spread = jnp.where(own_head, spread, 0.0).astype(jnp.bfloat16)
+        kv = jnp.concatenate([cache[base + h] for h in range(heads)], axis=1)
+        scores = lax.dot_general(spread, kv, CONTRACT_LANES, preferred_element_type=jnp.float32) * (HD**-0.5)
+        scores = jnp.where(live, scores, masked_score)
+        fresh = lax.dot_general(spread, kn, CONTRACT_LANES, preferred_element_type=jnp.float32) * (HD**-0.5)
+        fresh = jnp.where(new_live, fresh, masked_score)
+        top = jnp.maximum(jnp.max(scores, axis=1, keepdims=True), jnp.max(fresh, axis=1, keepdims=True))
+        weights = jnp.where(live, jnp.exp(scores - top), 0.0)
+        fresh = jnp.where(new_live, jnp.exp(fresh - top), 0.0)
+        totals = jnp.sum(weights, axis=1, keepdims=True) + jnp.sum(fresh, axis=1, keepdims=True)
+        weights = pltpu.roll(weights, 1, 1).astype(jnp.bfloat16)
+        mixed = jnp.dot(weights, kv, preferred_element_type=jnp.float32)
+        mixed = mixed + jnp.dot(fresh.astype(jnp.bfloat16), vn, preferred_element_type=jnp.float32)
+        mixed = jnp.where(own_head, mixed / totals, 0.0)
+        out = jnp.sum(mixed.reshape(rows, HEAD_BLOCK, lanes), axis=1).astype(out_ref.dtype)
+        for t in range(steps):
+            for h in range(heads):
+                out_ref[t, base + h] = out[2 * t : 2 * t + 2, h * HD : (h + 1) * HD]
+
+
+def attend(me, cosine, sine, live, cache, pieces, fresh_values):
+    count = len(pieces)
+    steps = pieces[0].shape[1]
+    heads = cache.shape[0]
+    lanes = 2 * heads // count * HD
+    vmem = pl.BlockSpec(memory_space=pltpu.VMEM)
+    return pl.pallas_call(
+        functools.partial(attend_kernel, count),
+        out_shape=jax.ShapeDtypeStruct((steps, heads, 2, HD), jnp.bfloat16),
+        in_specs=[pl.BlockSpec(memory_space=pltpu.SMEM)] + [vmem] * (4 + 2 * count),
+        out_specs=vmem,
+        scratch_shapes=[pltpu.VMEM((16, lanes), jnp.float32)] * 2,
+        compiler_params=pltpu.CompilerParams(vmem_limit_bytes=16 * 2**20),
+        cost_estimate=pl.CostEstimate(flops=10**9, bytes_accessed=6 * 10**6, transcendentals=0),
+        name="attention",
+    )(me, cosine, sine, live, cache, *pieces, *fresh_values)
+
+
+def chip_plan(
+    count,
+    hidden,
+    query_key_value_weight,
+    adapter_down_maps,
+    adapter_up_maps,
+    adapter_storage_row,
+    request_adapter,
+    lengths,
+    request_page_table,
+    key_value_pool,
+):
+    me = lax.axis_index("replica")
+    steps, req_dev, width = hidden.shape
+    heads = width // HD
+    holder_count, rank, _ = adapter_down_maps.shape
+    pool_pages, page_len = key_value_pool.shape[:2]
+    adapter_count = adapter_storage_row.shape[0]
+    request_count = request_adapter.shape[0]
+
+    held = {0: hidden}
+    for masks in (range(4, count, 4), (2,), (1,)):
+        held.update({k ^ m: trade(v, m, count) for k, v in list(held.items()) for m in masks})
+    blocks = [
+        held[k].reshape(steps, req_dev, heads, HD).transpose(0, 2, 1, 3) for k in range(count)
+    ]
+
+    owner = me ^ jnp.arange(count, dtype=jnp.int32)
+    request = owner[:, None] * req_dev + jnp.arange(req_dev, dtype=jnp.int32)[None, :]
+    request = jnp.broadcast_to(request[:, None, :], (count, steps, req_dev)).reshape(-1, 1)
+    adapter = jnp.sum(
+        jnp.where(request == jnp.arange(request_count, dtype=jnp.int32)[None, :], request_adapter[None, :], 0),
+        axis=1,
+        keepdims=True,
+    )
+    stored = jnp.sum(
+        jnp.where(adapter == jnp.arange(adapter_count, dtype=jnp.int32)[None, :], adapter_storage_row[None, :], 0),
+        axis=1,
+        keepdims=True,
+    )
+
+    tokens = pool_pages * page_len
+    cache = cache_by_head(key_value_pool.reshape(tokens, 2, heads, HD).transpose(0, 2, 1, 3))
+
+    x, low = low_of(blocks, stored - me * holder_count, adapter_down_maps)
+    lows = [low] + [trade(low, k, count) for k in range(1, count)]
+    base, pieces = project(x, query_key_value_weight.transpose(0, 2, 1), count)
+    pieces = [pieces[0]] + [trade(pieces[k], k, count) for k in range(1, count)]
+    values = update_values(stored, base, adapter_up_maps.reshape(adapter_count * rank, -1), lows)
+    values = [values[0]] + [trade(values[k], k, count) for k in range(1, count)]
+
+    my_lengths = lax.dynamic_slice_in_dim(lengths, me * req_dev, req_dev)
+    cosine, sine = rotation(my_lengths, steps)
+    live = live_rows(my_lengths, request_page_table, pool_pages, page_len)
+    out = attend(me.astype(jnp.int32).reshape(1), cosine, sine, live, cache, pieces, values)
+    return out.transpose(0, 2, 1, 3).reshape(steps, req_dev, width)
+
+
+def per_device(replicas, *arrays):
+    columns = arrays[1].shape[2]
+    whole_heads = replicas % 4 == 0 and (2 * columns) % HD == 0 and columns % HD == HD // 2
+    plan = chip_plan if whole_heads and arrays[0].shape[1] == 2 else general_plan
+    return plan(replicas, *arrays)
 
 
 def solution(mesh):

time: 87.3 us -> 122 us (1.40)
  starting transfers between devices: 17.4 us -> 70.5 us
  Pallas kernels: 4.2 us -> 19.1 us
  local copies, waits for them, and re-layouts: 31 us -> 16.7 us
  matrix products: 11.4 us -> 0 us
  waiting for transfers between devices: 16.4 us -> 7.05 us
  other arithmetic: 5.71 us -> 7.41 us
    ppermute x1 -> x60, starting transfers between devices: 0.01 us -> 70.5 us  [trade(): return lax.ppermute(value, 'replica', [(i, i ^ mask) for i in range(count)])]
    all_to_all x3 -> x0, starting transfers between devices: 17.4 us -> none  [the longest x1 7.28 us: per_device(): lax.all_to_all(jnp.broadcast_to(block[None], (chips, ROWS, width)), 'repl...]
    pallas_call x1 -> x5, Pallas kernels: 4.2 us -> 19.1 us  [the longest x1 6.21 us: attend(): pl.pallas_call(functools.partial(attend_kernel, count), out_shape=jax.Sha...]
    reshape x6 -> x1, local copies, waits for them, and re-layouts: 14.6 us -> 0.25 us  [live_rows(): return live.reshape(request_page_table.shape[0], pool_pages * page_len * 2)]
    all_to_all x3 -> x0, waiting for transfers between devices: 14.2 us -> none  [the longest x1 14.2 us: per_device(): lax.all_to_all(jnp.broadcast_to(block[None], (chips, ROWS, width)), 'repl...]
    dot_general x3 -> x0, matrix products: 11.4 us -> none  [the longest x1 7.72 us: per_device(): jnp.einsum('nd,idc->nic', gathered, query_key_value_weight, preferred_ele...]
    unnamed x9 -> x64, local copies, waits for them, and re-layouts: 3.65 us -> 14.8 us
    slice x9 -> x0, local copies, waits for them, and re-layouts: 6.59 us -> none  [the longest x2 1.66 us: per_device(): projected[:, 0]]
  transfers between devices with their start and end apart: 4 -> 60, of which waited for: 2 -> 5; matrix products, arithmetic and copies ran while one was open for 30% -> 8% of each run, Pallas kernels for 0% -> 5%
where the time goes in v2:
time: 122 us; the launch traced here: 121 us
  starting transfers between devices  70.5 us (58%)
  Pallas kernels  19.1 us (16%)
  local copies, waits for them, and re-layouts  16.7 us (14%)
  other arithmetic  7.41 us (6%)
  waiting for transfers between devices  7.05 us (6%)
    ppermute x60, starting transfers between devices, trade(): return lax.ppermute(value, 'replica', [(i, i ^ mask) for i in range(count)])  70.5 us
    unnamed x64, local copies, waits for them, and re-layouts  14.8 us
    ppermute x60, waiting for transfers between devices, trade(): return lax.ppermute(value, 'replica', [(i, i ^ mask) for i in range(count)])  7.05 us
    pallas_call x1, Pallas kernels, attend(): pl.pallas_call(functools.partial(attend_kernel, count), out_shape=jax.Sha...  6.21 us
    pallas_call x1, Pallas kernels, project(): pl.pallas_call(functools.partial(project_kernel, count), out_shape=(jax.S...  4.27 us
    pallas_call x1, Pallas kernels, cache_by_head(): pl.pallas_call(cache_kernel, out_shape=jax.ShapeDtypeStruct((heads, token...  4.22 us
  transfers between devices with their start and end apart: 60, of which 5 were waited for; matrix products, arithmetic and copies ran while one was open for 8% of the time, Pallas kernels for 5%

profile of v2, /device:TPU:0, one launch (start us, length us, event | category | flops | bytes accessed | tf_op | source)
XLA Modules:
  0.0 121.2 jit_solution(1709805926366082040)
XLA Ops:
  0.0 3.0 %collective-permute-start.3 = (bf16[3,2,5120]{2,1,0:T(2,128)(2,1)}, bf16[3,2,5120]{2,1,0:T(2,128)(2,1)S(1)}, u32[]{:S(2)}, u32[]{:S(2)}) collective-permute-start(bf16[3,2,5120]{2,1,0:T(2,128)(2,1)} %param.9), channel_id=1, source_target_pairs={{0,4},{1,5},{2,6},{3,7},{4,0},{5,1},{6,2},{7,3},{8,12},{9,13},{10,... | collective-permute-start | bytes 184328 | tf_op jit(solution)/shard_map/ppermute | solution.py:229
  3.0 1.5 %collective-permute-start.1 = (bf16[3,2,5120]{2,1,0:T(2,128)(2,1)}, bf16[3,2,5120]{2,1,0:T(2,128)(2,1)S(1)}, u32[]{:S(2)}, u32[]{:S(2)}) collective-permute-start(bf16[3,2,5120]{2,1,0:T(2,128)(2,1)} %param.9), channel_id=1, source_target_pairs={{0,2},{1,3},{2,0},{3,1},{4,6},{5,7},{6,4},{7,5},{8,10},{9,11},{10,... | collective-permute-start | bytes 184328 | tf_op jit(solution)/shard_map/ppermute | solution.py:229
  4.5 2.5 %collective-permute-start.11 = (bf16[3,2,5120]{2,1,0:T(2,128)(2,1)}, bf16[3,2,5120]{2,1,0:T(2,128)(2,1)S(1)}, u32[]{:S(2)}, u32[]{:S(2)}) collective-permute-start(bf16[3,2,5120]{2,1,0:T(2,128)(2,1)} %param.9), channel_id=1, source_target_pairs={{0,12},{1,13},{2,14},{3,15},{4,8},{5,9},{6,10},{7,11},{8,4},{9,5},... | collective-permute-start | bytes 184328 | tf_op jit(solution)/shard_map/ppermute | solution.py:229
  10.1 1.0 collective-permute-done.11
  11.6 2.4 %collective-permute-done.7 = bf16[3,2,5120]{2,1,0:T(2,128)(2,1)S(1)} collective-permute-done((bf16[3,2,5120]{2,1,0:T(2,128)(2,1)}, bf16[3,2,5120]{2,1,0:T(2,128)(2,1)S(1)}, u32[]{:S(2)}, u32[]{:S(2)}) %collective-permute-start.7) | collective-permute-done | bytes 61472 | tf_op jit(solution)/shard_map/ppermute | solution.py:229
  16.4 1.8 %collective-permute-done.9 = bf16[3,2,5120]{2,1,0:T(2,128)(2,1)S(1)} collective-permute-done((bf16[3,2,5120]{2,1,0:T(2,128)(2,1)S(1)}, bf16[3,2,5120]{2,1,0:T(2,128)(2,1)S(1)}, u32[]{:S(2)}, u32[]{:S(2)}) %collective-permute-start.9) | collective-permute-done | bytes 61472 | tf_op jit(solution)/shard_map/ppermute | solution.py:229
  18.2 1.2 collective-permute-done.10
  19.4 1.7 %copy-done.3 = bf16[4,64,5120]{2,1,0:T(8,128)(2,1)S(1)} copy-done((bf16[4,64,5120]{2,1,0:T(8,128)(2,1)S(1)}, bf16[4,64,5120]{2,1,0:T(8,128)(2,1)}, u32[]{:S(2)}) %copy-start.3) | copy-done | bytes 2621464
  22.0 2.4 %low_rows.1 = (bf16[40,48,2,128]{3,2,1,0:T(2,128)(2,1)S(1)}, bf16[48,128]{1,0:T(8,128)(2,1)S(1)}) custom-call(s32[96,1]{1,0:T(8,128)S(1)} %broadcast_subtract_fusion.slot_ref, bf16[4,64,5120]{2,1,0:T(8,128)(2,1)S(1)} %copy-done.3, bf16[3,40,2,128]{3,2,1,0:T(2,128)(2,1)S(1)} %bitcast.61, bf16[3,40,2,128]{3,2,1,0:T(2,128)(2,1)S(1)} %bitcast.64, ...), custom_call_target="tpu_custom_call" | custom-call | flops 100000000 | bytes 4000000 | tf_op jit(solution)/shard_map/low_rows/pallas_call | solution.py:293
  24.4 3.8 %copy-done = bf16[3,5120,320]{1,2,0:T(8,128)(2,1)S(1)} copy-done((bf16[3,5120,320]{1,2,0:T(8,128)(2,1)S(1)}, bf16[3,5120,320]{1,2,0:T(8,128)(2,1)}, u32[]{:S(2)}) %copy-start) | copy-done | bytes 9830424
  28.2 4.3 %project.1 = (f32[96,320]{1,0:T(8,128)S(1)}, bf16[6,3,2,128]{3,2,1,0:T(2,128)(2,1)S(1)}, bf16[6,3,2,128]{3,2,1,0:T(2,128)(2,1)S(1)}, bf16[6,3,2,128]{3,2,1,0:T(2...) custom-call(bf16[40,48,2,128]{3,2,1,0:T(2,128)(2,1)S(1)} %get-tuple-, ...), custom_call_target="tpu_custom_call" | custom-call | flops 1000000000 | bytes 11000000 | tf_op jit(solution)/shard_map/project/pallas_call | solution.py:352
  36.1 1.2 collective-permute-start.17
  37.4 1.7 %collective-permute-start.19 = (bf16[6,3,2,128]{3,2,1,0:T(2,128)(2,1)S(1)}, bf16[6,3,2,128]{3,2,1,0:T(2,128)(2,1)S(1)}, u32[]{:S(2)}, u32[]{:S(2)}) collective-permute-start(bf16[6,3,2,128]{3,2,1,0:T(2,128)(2,1)S(1)} %get-tuple-element.46), channel_id=1, source_target_pairs={{0,5},{1,4},{2,7},{3,6},{4,1},{5,0},{6,3},{7,2},{8,13},{9,12},{10,... | collective-permute-start | bytes 27656 | tf_op jit(solution)/shard_map/ppermute | solution.py:229
  40.3 0.9 collective-permute-start.20
  41.3 1.7 %collective-permute-start.21 = (bf16[6,3,2,128]{3,2,1,0:T(2,128)(2,1)S(1)}, bf16[6,3,2,128]{3,2,1,0:T(2,128)(2,1)S(1)}, u32[]{:S(2)}, u32[]{:S(2)}) collective-permute-start(bf16[6,3,2,128]{3,2,1,0:T(2,128)(2,1)S(1)} %get-tuple-element.48), channel_id=1, source_target_pairs={{0,7},{1,6},{2,5},{3,4},{4,3},{5,2},{6,1},{7,0},{8,15},{9,14},{10,... | collective-permute-start | bytes 27656 | tf_op jit(solution)/shard_map/ppermute | solution.py:229
  43.0 1.5 %collective-permute-start.22 = (bf16[6,3,2,128]{3,2,1,0:T(2,128)(2,1)S(1)}, bf16[6,3,2,128]{3,2,1,0:T(2,128)(2,1)S(1)}, u32[]{:S(2)}, u32[]{:S(2)}) collective-permute-start(bf16[6,3,2,128]{3,2,1,0:T(2,128)(2,1)S(1)} %get-tuple-element.49), channel_id=1, source_target_pairs={{0,8},{1,9},{2,10},{3,11},{4,12},{5,13},{6,14},{7,15},{8,0},{9,1},... | collective-permute-start | bytes 27656 | tf_op jit(solution)/shard_map/ppermute | solution.py:229
  44.4 1.2 %collective-permute-start.23 = (bf16[6,3,2,128]{3,2,1,0:T(2,128)(2,1)S(1)}, bf16[6,3,2,128]{3,2,1,0:T(2,128)(2,1)S(1)}, u32[]{:S(2)}, u32[]{:S(2)}) collective-permute-start(bf16[6,3,2,128]{3,2,1,0:T(2,128)(2,1)S(1)} %get-tuple-element.50), channel_id=1, source_target_pairs={{0,9},{1,8},{2,11},{3,10},{4,13},{5,12},{6,15},{7,14},{8,1},{9,0},... | collective-permute-start | bytes 27656 | tf_op jit(solution)/shard_map/ppermute | solution.py:229
  45.7 2.3 %collective-permute-start.24 = (bf16[6,3,2,128]{3,2,1,0:T(2,128)(2,1)S(1)}, bf16[6,3,2,128]{3,2,1,0:T(2,128)(2,1)S(1)}, u32[]{:S(2)}, u32[]{:S(2)}) collective-permute-start(bf16[6,3,2,128]{3,2,1,0:T(2,128)(2,1)S(1)} %get-tuple-element.51), channel_id=1, source_target_pairs={{0,10},{1,11},{2,8},{3,9},{4,14},{5,15},{6,12},{7,13},{8,2},{9,3},... | collective-permute-start | bytes 27656 | tf_op jit(solution)/shard_map/ppermute | solution.py:229
  47.9 1.6 %fusion = pred[2,64,4,1]{3,2,1,0:T(4,128)(4,1)} fusion(s32[2]{0:T(128)S(1)} %dynamic_slice.3, s32[2,64]{1,0:T(2,128)S(1)} %broadcast_multiply_fusion, pred[2,64]{1,0:T(4,128)(4,1)} %broadcast_compare_fusion), kind=kLoop, calls=%fused_computation.1 | loop fusion | flops 1536 | bytes 1160 | tf_op jit(solution)/shard_map/and | solution.py:122
  50.1 1.1 collective-permute-start.44
  51.8 3.3 %collective-permute-start.43 = (bf16[48,128]{1,0:T(8,128)(2,1)S(1)}, bf16[48,128]{1,0:T(8,128)(2,1)S(1)}, u32[]{:S(2)}, u32[]{:S(2)}) collective-permute-start(bf16[48,128]{1,0:T(8,128)(2,1)S(1)} %get-tuple-element.58.refs_0_), channel_id=1, source_target_pairs={{0,14},{1,15},{2,12},{3,13},{4,10},{5,11},{6,8},{7,9},{8,6},{9,7},... | collective-permute-start | bytes 36872 | tf_op jit(solution)/shard_map/ppermute | solution.py:229
  57.1 2.8 %collective-permute-start.41 = (bf16[48,128]{1,0:T(8,128)(2,1)S(1)}, bf16[48,128]{1,0:T(8,128)(2,1)S(1)}, u32[]{:S(2)}, u32[]{:S(2)}) collective-permute-start(bf16[48,128]{1,0:T(8,128)(2,1)S(1)} %get-tuple-element.58.refs_0_), channel_id=1, source_target_pairs={{0,12},{1,13},{2,14},{3,15},{4,8},{5,9},{6,10},{7,11},{8,4},{9,5},... | collective-permute-start | bytes 36872 | tf_op jit(solution)/shard_map/ppermute | solution.py:229
  60.5 3.5 %collective-permute-start.39 = (bf16[48,128]{1,0:T(8,128)(2,1)S(1)}, bf16[48,128]{1,0:T(8,128)(2,1)S(1)}, u32[]{:S(2)}, u32[]{:S(2)}) collective-permute-start(bf16[48,128]{1,0:T(8,128)(2,1)S(1)} %get-tuple-element.58.refs_0_), channel_id=1, source_target_pairs={{0,10},{1,11},{2,8},{3,9},{4,14},{5,15},{6,12},{7,13},{8,2},{9,3},... | collective-permute-start | bytes 36872 | tf_op jit(solution)/shard_map/ppermute | solution.py:229
  64.0 2.7 %collective-permute-start.37 = (bf16[48,128]{1,0:T(8,128)(2,1)S(1)}, bf16[48,128]{1,0:T(8,128)(2,1)S(1)}, u32[]{:S(2)}, u32[]{:S(2)}) collective-permute-start(bf16[48,128]{1,0:T(8,128)(2,1)S(1)} %get-tuple-element.58.refs_0_), channel_id=1, source_target_pairs={{0,8},{1,9},{2,10},{3,11},{4,12},{5,13},{6,14},{7,15},{8,0},{9,1},... | collective-permute-start | bytes 36872 | tf_op jit(solution)/shard_map/ppermute | solution.py:229
  66.7 2.6 %collective-permute-start.35 = (bf16[48,128]{1,0:T(8,128)(2,1)S(1)}, bf16[48,128]{1,0:T(8,128)(2,1)S(1)}, u32[]{:S(2)}, u32[]{:S(2)}) collective-permute-start(bf16[48,128]{1,0:T(8,128)(2,1)S(1)} %get-tuple-element.58.refs_0_), channel_id=1, source_target_pairs={{0,6},{1,7},{2,4},{3,5},{4,2},{5,3},{6,0},{7,1},{8,14},{9,15},{10,... | collective-permute-start | bytes 36872 | tf_op jit(solution)/shard_map/ppermute | solution.py:229
  70.5 1.8 %collective-permute-start.33 = (bf16[48,128]{1,0:T(8,128)(2,1)S(1)}, bf16[48,128]{1,0:T(8,128)(2,1)S(1)}, u32[]{:S(2)}, u32[]{:S(2)}) collective-permute-start(bf16[48,128]{1,0:T(8,128)(2,1)S(1)} %get-tuple-element.58.refs_0_), channel_id=1, source_target_pairs={{0,4},{1,5},{2,6},{3,7},{4,0},{5,1},{6,2},{7,3},{8,12},{9,13},{10,... | collective-permute-start | bytes 36872 | tf_op jit(solution)/shard_map/ppermute | solution.py:229
  72.6 1.4 %collective-permute-start.31 = (bf16[48,128]{1,0:T(8,128)(2,1)S(1)}, bf16[48,128]{1,0:T(8,128)(2,1)S(1)}, u32[]{:S(2)}, u32[]{:S(2)}) collective-permute-start(bf16[48,128]{1,0:T(8,128)(2,1)S(1)} %get-tuple-element.58.refs_0_), channel_id=1, source_target_pairs={{0,2},{1,3},{2,0},{3,1},{4,6},{5,7},{6,4},{7,5},{8,10},{9,11},{10,... | collective-permute-start | bytes 36872 | tf_op jit(solution)/shard_map/ppermute | solution.py:229
  75.2 2.4 %collective-permute-start.26 = (bf16[6,3,2,128]{3,2,1,0:T(2,128)(2,1)}, bf16[6,3,2,128]{3,2,1,0:T(2,128)(2,1)S(1)}, u32[]{:S(2)}, u32[]{:S(2)}) collective-permute-start(bf16[6,3,2,128]{3,2,1,0:T(2,128)(2,1)} %copy-done.30), channel_id=1, source_target_pairs={{0,12},{1,13},{2,14},{3,15},{4,8},{5,9},{6,10},{7,11},{8,4},{9,5},... | collective-permute-start | bytes 27656 | tf_op jit(solution)/shard_map/ppermute | solution.py:229
  77.6 1.0 collective-permute-start.27
  78.5 3.2 %collective-permute-start.28 = (bf16[6,3,2,128]{3,2,1,0:T(2,128)(2,1)}, bf16[6,3,2,128]{3,2,1,0:T(2,128)(2,1)S(1)}, u32[]{:S(2)}, u32[]{:S(2)}) collective-permute-start(bf16[6,3,2,128]{3,2,1,0:T(2,128)(2,1)} %copy-done.28), channel_id=1, source_target_pairs={{0,14},{1,15},{2,12},{3,13},{4,10},{5,11},{6,8},{7,9},{8,6},{9,7},... | collective-permute-start | bytes 27656 | tf_op jit(solution)/shard_map/ppermute | solution.py:229
  81.7 1.5 %collective-permute-start.29 = (bf16[6,3,2,128]{3,2,1,0:T(2,128)(2,1)}, bf16[6,3,2,128]{3,2,1,0:T(2,128)(2,1)S(1)}, u32[]{:S(2)}, u32[]{:S(2)}) collective-permute-start(bf16[6,3,2,128]{3,2,1,0:T(2,128)(2,1)} %copy-done.27), channel_id=1, source_target_pairs={{0,15},{1,14},{2,13},{3,12},{4,11},{5,10},{6,9},{7,8},{8,7},{9,6},... | collective-permute-start | bytes 27656 | tf_op jit(solution)/shard_map/ppermute | solution.py:229
  83.2 2.0 %update_values.1 = (bf16[3,3,2,128]{3,2,1,0:T(2,128)(2,1)S(1)}, bf16[3,3,2,128]{3,2,1,0:T(2,128)(2,1)S(1)}, bf16[3,3,2,128]{3,2,1,0:T(2,128)(2,1)S(1)}, bf16[3,3...) custom-call(s32[96,1]{1,0:T(8,128)S(1)} %copy.16.stored_ref, ...), custom_call_target="tpu_custom_call" | custom-call | flops 300000000 | bytes 4000000 | tf_op jit(solution)/shard_map/update_values/pallas_call | solution.py:405
  85.5 1.4 %collective-permute-start.46 = (bf16[3,3,2,128]{3,2,1,0:T(2,128)(2,1)S(1)}, bf16[3,3,2,128]{3,2,1,0:T(2,128)(2,1)S(1)}, u32[]{:S(2)}, u32[]{:S(2)}) collective-permute-start(bf16[3,3,2,128]{3,2,1,0:T(2,128)(2,1)S(1)} %get-tuple-element.61), channel_id=1, source_target_pairs={{0,2},{1,3},{2,0},{3,1},{4,6},{5,7},{6,4},{7,5},{8,10},{9,11},{10,... | collective-permute-start | bytes 13832 | tf_op jit(solution)/shard_map/ppermute | solution.py:229
  87.7 1.3 %collective-permute-start.49 = (bf16[3,3,2,128]{3,2,1,0:T(2,128)(2,1)S(1)}, bf16[3,3,2,128]{3,2,1,0:T(2,128)(2,1)S(1)}, u32[]{:S(2)}, u32[]{:S(2)}) collective-permute-start(bf16[3,3,2,128]{3,2,1,0:T(2,128)(2,1)S(1)} %get-tuple-element.64), channel_id=1, source_target_pairs={{0,5},{1,4},{2,7},{3,6},{4,1},{5,0},{6,3},{7,2},{8,13},{9,12},{10,... | collective-permute-start | bytes 13832 | tf_op jit(solution)/shard_map/ppermute | solution.py:229
  89.7 1.2 %collective-permute-start.50 = (bf16[3,3,2,128]{3,2,1,0:T(2,128)(2,1)S(1)}, bf16[3,3,2,128]{3,2,1,0:T(2,128)(2,1)S(1)}, u32[]{:S(2)}, u32[]{:S(2)}) collective-permute-start(bf16[3,3,2,128]{3,2,1,0:T(2,128)(2,1)S(1)} %get-tuple-element.65), channel_id=1, source_target_pairs={{0,6},{1,7},{2,4},{3,5},{4,2},{5,3},{6,0},{7,1},{8,14},{9,15},{10,... | collective-permute-start | bytes 13832 | tf_op jit(solution)/shard_map/ppermute | solution.py:229
  91.0 1.4 %collective-permute-start.51 = (bf16[3,3,2,128]{3,2,1,0:T(2,128)(2,1)S(1)}, bf16[3,3,2,128]{3,2,1,0:T(2,128)(2,1)S(1)}, u32[]{:S(2)}, u32[]{:S(2)}) collective-permute-start(bf16[3,3,2,128]{3,2,1,0:T(2,128)(2,1)S(1)} %get-tuple-element.66), channel_id=1, source_target_pairs={{0,7},{1,6},{2,5},{3,4},{4,3},{5,2},{6,1},{7,0},{8,15},{9,14},{10,... | collective-permute-start | bytes 13832 | tf_op jit(solution)/shard_map/ppermute | solution.py:229
  92.4 1.2 collective-permute-start.52
  93.6 1.5 %collective-permute-start.53 = (bf16[3,3,2,128]{3,2,1,0:T(2,128)(2,1)S(1)}, bf16[3,3,2,128]{3,2,1,0:T(2,128)(2,1)S(1)}, u32[]{:S(2)}, u32[]{:S(2)}) collective-permute-start(bf16[3,3,2,128]{3,2,1,0:T(2,128)(2,1)S(1)} %get-tuple-element.68), channel_id=1, source_target_pairs={{0,9},{1,8},{2,11},{3,10},{4,13},{5,12},{6,15},{7,14},{8,1},{9,0},... | collective-permute-start | bytes 13832 | tf_op jit(solution)/shard_map/ppermute | solution.py:229
  95.1 2.1 %collective-permute-start.54 = (bf16[3,3,2,128]{3,2,1,0:T(2,128)(2,1)S(1)}, bf16[3,3,2,128]{3,2,1,0:T(2,128)(2,1)S(1)}, u32[]{:S(2)}, u32[]{:S(2)}) collective-permute-start(bf16[3,3,2,128]{3,2,1,0:T(2,128)(2,1)S(1)} %get-tuple-element.69), channel_id=1, source_target_pairs={{0,10},{1,11},{2,8},{3,9},{4,14},{5,15},{6,12},{7,13},{8,2},{9,3},... | collective-permute-start | bytes 13832 | tf_op jit(solution)/shard_map/ppermute | solution.py:229
  97.2 0.9 pad_convert_fusion
  98.1 1.5 %collective-permute-start.55 = (bf16[3,3,2,128]{3,2,1,0:T(2,128)(2,1)}, bf16[3,3,2,128]{3,2,1,0:T(2,128)(2,1)S(1)}, u32[]{:S(2)}, u32[]{:S(2)}) collective-permute-start(bf16[3,3,2,128]{3,2,1,0:T(2,128)(2,1)} %get-tuple-element.70), channel_id=1, source_target_pairs={{0,11},{1,10},{2,9},{3,8},{4,15},{5,14},{6,13},{7,12},{8,3},{9,2},... | collective-permute-start | bytes 13832 | tf_op jit(solution)/shard_map/ppermute | solution.py:229
  99.6 2.4 %collective-permute-start.56 = (bf16[3,3,2,128]{3,2,1,0:T(2,128)(2,1)}, bf16[3,3,2,128]{3,2,1,0:T(2,128)(2,1)S(1)}, u32[]{:S(2)}, u32[]{:S(2)}) collective-permute-start(bf16[3,3,2,128]{3,2,1,0:T(2,128)(2,1)} %get-tuple-element.71), channel_id=1, source_target_pairs={{0,12},{1,13},{2,14},{3,15},{4,8},{5,9},{6,10},{7,11},{8,4},{9,5},... | collective-permute-start | bytes 13832 | tf_op jit(solution)/shard_map/ppermute | solution.py:229
  102.0 1.2 %collective-permute-start.57 = (bf16[3,3,2,128]{3,2,1,0:T(2,128)(2,1)}, bf16[3,3,2,128]{3,2,1,0:T(2,128)(2,1)S(1)}, u32[]{:S(2)}, u32[]{:S(2)}) collective-permute-start(bf16[3,3,2,128]{3,2,1,0:T(2,128)(2,1)} %get-tuple-element.72), channel_id=1, source_target_pairs={{0,13},{1,12},{2,15},{3,14},{4,9},{5,8},{6,11},{7,10},{8,5},{9,4},... | collective-permute-start | bytes 13832 | tf_op jit(solution)/shard_map/ppermute | solution.py:229
  103.2 3.2 %collective-permute-start.58 = (bf16[3,3,2,128]{3,2,1,0:T(2,128)(2,1)}, bf16[3,3,2,128]{3,2,1,0:T(2,128)(2,1)S(1)}, u32[]{:S(2)}, u32[]{:S(2)}) collective-permute-start(bf16[3,3,2,128]{3,2,1,0:T(2,128)(2,1)} %get-tuple-element.73), channel_id=1, source_target_pairs={{0,14},{1,15},{2,12},{3,13},{4,10},{5,11},{6,8},{7,9},{8,6},{9,7},... | collective-permute-start | bytes 13832 | tf_op jit(solution)/shard_map/ppermute | solution.py:229
  106.4 1.2 %collective-permute-start.59 = (bf16[3,3,2,128]{3,2,1,0:T(2,128)(2,1)}, bf16[3,3,2,128]{3,2,1,0:T(2,128)(2,1)S(1)}, u32[]{:S(2)}, u32[]{:S(2)}) collective-permute-start(bf16[3,3,2,128]{3,2,1,0:T(2,128)(2,1)} %get-tuple-element.74), channel_id=1, source_target_pairs={{0,15},{1,14},{2,13},{3,12},{4,11},{5,10},{6,9},{7,8},{8,7},{9,6},... | collective-permute-start | bytes 13832 | tf_op jit(solution)/shard_map/ppermute | solution.py:229
  108.0 2.5 %copy-done.1 = bf16[64,4,2,5120]{3,2,1,0:T(2,128)(2,1)S(1)} copy-done((bf16[64,4,2,5120]{3,2,1,0:T(2,128)(2,1)S(1)}, bf16[64,4,2,5120]{3,2,1,0:T(2,128)(2,1)}, u32[]{:S(2)}) %copy-start.1) | copy-done | bytes 5242904
  110.6 4.2 %cache_by_head.1.cache_ref = bf16[40,256,2,128]{3,2,1,0:T(2,128)(2,1)S(1)} custom-call(bf16[256,40,2,128]{3,2,1,0:T(2,128)(2,1)S(1)} %bitcast.59), custom_call_target="tpu_custom_call" | custom-call | bytes 10485760 | tf_op jit(solution)/shard_map/cache_by_head/pallas_call | solution.py:243
  115.0 6.2 %attention.1 = bf16[3,40,2,128]{3,2,1,0:T(2,128)(2,1)} custom-call(s32[1]{0:T(128)} %bitcast.me_ref, f32[8,128]{1,0:T(8,128)S(1)} %get-tuple-element.78.cos_ref, f32[8,128]{1,0:T(8,128)S(1)} %get-tuple-element.79.sin_ref, s32[2,512]{1,0:T(2,128)S(1)} %reshape.157.live_ref, bf16[40,256,2,128]{3,2,1,0:T(2,128)(2,1)S(1)} %cache_by_head.1.cache_ref, ...), custom_call_target="tpu_custom_call" | custom-call | flops 1000000000 | bytes 6000000 | tf_op jit(solution)/shard_map/attention/pallas_call | solution.py:500
  (162 shorter events, 20.5 us)
Async XLA Ops:
  0.0 9.0 %collective-permute-start.3 = (bf16[3,2,5120]{2,1,0:T(2,128)(2,1)}, bf16[3,2,5120]{2,1,0:T(2,128)(2,1)S(1)}, u32[]{:S(2)}, u32[]{:S(2)}) collective-permute-start(bf16[3,2,5120]{2,1,0:T(2,128)(2,1)} %param.9), channel_id=1, source_target_pairs={{0,4},{1,5},{2,6},{3,7},{4,0},{5,1},{6,2},{7,3},{8,12},{9,13},{10,... | collective-permute-start | bytes 184328 | tf_op jit(solution)/shard_map/ppermute | solution.py:229
  3.0 6.5 %collective-permute-start.1 = (bf16[3,2,5120]{2,1,0:T(2,128)(2,1)}, bf16[3,2,5120]{2,1,0:T(2,128)(2,1)S(1)}, u32[]{:S(2)}, u32[]{:S(2)}) collective-permute-start(bf16[3,2,5120]{2,1,0:T(2,128)(2,1)} %param.9), channel_id=1, source_target_pairs={{0,2},{1,3},{2,0},{3,1},{4,6},{5,7},{6,4},{7,5},{8,10},{9,11},{10,... | collective-permute-start | bytes 184328 | tf_op jit(solution)/shard_map/ppermute | solution.py:229
  4.5 6.5 %collective-permute-start.11 = (bf16[3,2,5120]{2,1,0:T(2,128)(2,1)}, bf16[3,2,5120]{2,1,0:T(2,128)(2,1)S(1)}, u32[]{:S(2)}, u32[]{:S(2)}) collective-permute-start(bf16[3,2,5120]{2,1,0:T(2,128)(2,1)} %param.9), channel_id=1, source_target_pairs={{0,12},{1,13},{2,14},{3,15},{4,8},{5,9},{6,10},{7,11},{8,4},{9,5},... | collective-permute-start | bytes 184328 | tf_op jit(solution)/shard_map/ppermute | solution.py:229
  7.0 6.9 %collective-permute-start.7 = (bf16[3,2,5120]{2,1,0:T(2,128)(2,1)}, bf16[3,2,5120]{2,1,0:T(2,128)(2,1)S(1)}, u32[]{:S(2)}, u32[]{:S(2)}) collective-permute-start(bf16[3,2,5120]{2,1,0:T(2,128)(2,1)} %param.9), channel_id=1, source_target_pairs={{0,8},{1,9},{2,10},{3,11},{4,12},{5,13},{6,14},{7,15},{8,0},{9,1},... | collective-permute-start | bytes 184328 | tf_op jit(solution)/shard_map/ppermute | solution.py:229
  9.0 6.3 %collective-permute-start.5 = (bf16[3,2,5120]{2,1,0:T(2,128)(2,1)S(1)}, bf16[3,2,5120]{2,1,0:T(2,128)(2,1)S(1)}, u32[]{:S(2)}, u32[]{:S(2)}) collective-permute-start(bf16[3,2,5120]{2,1,0:T(2,128)(2,1)S(1)} %collective-permute-done.3), channel_id=1, source_target_pairs={{0,2},{1,3},{2,0},{3,1},{4,6},{5,7},{6,4},{7,5},{8,10},{9,11},{10,... | collective-permute-start | bytes 184328 | tf_op jit(solution)/shard_map/ppermute | solution.py:229
  9.6 5.8 %collective-permute-start.4 = (bf16[3,2,5120]{2,1,0:T(2,128)(2,1)S(1)}, bf16[3,2,5120]{2,1,0:T(2,128)(2,1)S(1)}, u32[]{:S(2)}, u32[]{:S(2)}) collective-permute-start(bf16[3,2,5120]{2,1,0:T(2,128)(2,1)S(1)} %collective-permute-done.3), channel_id=1, source_target_pairs={{0,1},{1,0},{2,3},{3,2},{4,5},{5,4},{6,7},{7,6},{8,9},{9,8},{10,11... | collective-permute-start | bytes 184328 | tf_op jit(solution)/shard_map/ppermute | solution.py:229
  9.6 6.3 %collective-permute-start.2 = (bf16[3,2,5120]{2,1,0:T(2,128)(2,1)S(1)}, bf16[3,2,5120]{2,1,0:T(2,128)(2,1)S(1)}, u32[]{:S(2)}, u32[]{:S(2)}) collective-permute-start(bf16[3,2,5120]{2,1,0:T(2,128)(2,1)S(1)} %collective-permute-done.1), channel_id=1, source_target_pairs={{0,1},{1,0},{2,3},{3,2},{4,5},{5,4},{6,7},{7,6},{8,9},{9,8},{10,11... | collective-permute-start | bytes 184328 | tf_op jit(solution)/shard_map/ppermute | solution.py:229
  35.6 5.7 %collective-permute-start.16 = (bf16[6,3,2,128]{3,2,1,0:T(2,128)(2,1)S(1)}, bf16[6,3,2,128]{3,2,1,0:T(2,128)(2,1)S(1)}, u32[]{:S(2)}, u32[]{:S(2)}) collective-permute-start(bf16[6,3,2,128]{3,2,1,0:T(2,128)(2,1)S(1)} %get-tuple-element.43), channel_id=1, source_target_pairs={{0,2},{1,3},{2,0},{3,1},{4,6},{5,7},{6,4},{7,5},{8,10},{9,11},{10,... | collective-permute-start | bytes 27656 | tf_op jit(solution)/shard_map/ppermute | solution.py:229
  36.1 6.8 %collective-permute-start.17 = (bf16[6,3,2,128]{3,2,1,0:T(2,128)(2,1)S(1)}, bf16[6,3,2,128]{3,2,1,0:T(2,128)(2,1)S(1)}, u32[]{:S(2)}, u32[]{:S(2)}) collective-permute-start(bf16[6,3,2,128]{3,2,1,0:T(2,128)(2,1)S(1)} %get-tuple-element.44), channel_id=1, source_target_pairs={{0,3},{1,2},{2,1},{3,0},{4,7},{5,6},{6,5},{7,4},{8,11},{9,10},{10,... | collective-permute-start | bytes 27656 | tf_op jit(solution)/shard_map/ppermute | solution.py:229
  37.3 7.1 %collective-permute-start.18 = (bf16[6,3,2,128]{3,2,1,0:T(2,128)(2,1)S(1)}, bf16[6,3,2,128]{3,2,1,0:T(2,128)(2,1)S(1)}, u32[]{:S(2)}, u32[]{:S(2)}) collective-permute-start(bf16[6,3,2,128]{3,2,1,0:T(2,128)(2,1)S(1)} %get-tuple-element.45), channel_id=1, source_target_pairs={{0,4},{1,5},{2,6},{3,7},{4,0},{5,1},{6,2},{7,3},{8,12},{9,13},{10,... | collective-permute-start | bytes 27656 | tf_op jit(solution)/shard_map/ppermute | solution.py:229
  37.4 8.2 %collective-permute-start.19 = (bf16[6,3,2,128]{3,2,1,0:T(2,128)(2,1)S(1)}, bf16[6,3,2,128]{3,2,1,0:T(2,128)(2,1)S(1)}, u32[]{:S(2)}, u32[]{:S(2)}) collective-permute-start(bf16[6,3,2,128]{3,2,1,0:T(2,128)(2,1)S(1)} %get-tuple-element.46), channel_id=1, source_target_pairs={{0,5},{1,4},{2,7},{3,6},{4,1},{5,0},{6,3},{7,2},{8,13},{9,12},{10,... | collective-permute-start | bytes 27656 | tf_op jit(solution)/shard_map/ppermute | solution.py:229
  40.3 9.2 %collective-permute-start.20 = (bf16[6,3,2,128]{3,2,1,0:T(2,128)(2,1)S(1)}, bf16[6,3,2,128]{3,2,1,0:T(2,128)(2,1)S(1)}, u32[]{:S(2)}, u32[]{:S(2)}) collective-permute-start(bf16[6,3,2,128]{3,2,1,0:T(2,128)(2,1)S(1)} %get-tuple-element.47), channel_id=1, source_target_pairs={{0,6},{1,7},{2,4},{3,5},{4,2},{5,3},{6,0},{7,1},{8,14},{9,15},{10,... | collective-permute-start | bytes 27656 | tf_op jit(solution)/shard_map/ppermute | solution.py:229
  41.3 9.9 %collective-permute-start.21 = (bf16[6,3,2,128]{3,2,1,0:T(2,128)(2,1)S(1)}, bf16[6,3,2,128]{3,2,1,0:T(2,128)(2,1)S(1)}, u32[]{:S(2)}, u32[]{:S(2)}) collective-permute-start(bf16[6,3,2,128]{3,2,1,0:T(2,128)(2,1)S(1)} %get-tuple-element.48), channel_id=1, source_target_pairs={{0,7},{1,6},{2,5},{3,4},{4,3},{5,2},{6,1},{7,0},{8,15},{9,14},{10,... | collective-permute-start | bytes 27656 | tf_op jit(solution)/shard_map/ppermute | solution.py:229
  43.0 12.2 %collective-permute-start.22 = (bf16[6,3,2,128]{3,2,1,0:T(2,128)(2,1)S(1)}, bf16[6,3,2,128]{3,2,1,0:T(2,128)(2,1)S(1)}, u32[]{:S(2)}, u32[]{:S(2)}) collective-permute-start(bf16[6,3,2,128]{3,2,1,0:T(2,128)(2,1)S(1)} %get-tuple-element.49), channel_id=1, source_target_pairs={{0,8},{1,9},{2,10},{3,11},{4,12},{5,13},{6,14},{7,15},{8,0},{9,1},... | collective-permute-start | bytes 27656 | tf_op jit(solution)/shard_map/ppermute | solution.py:229
  44.4 12.1 %collective-permute-start.23 = (bf16[6,3,2,128]{3,2,1,0:T(2,128)(2,1)S(1)}, bf16[6,3,2,128]{3,2,1,0:T(2,128)(2,1)S(1)}, u32[]{:S(2)}, u32[]{:S(2)}) collective-permute-start(bf16[6,3,2,128]{3,2,1,0:T(2,128)(2,1)S(1)} %get-tuple-element.50), channel_id=1, source_target_pairs={{0,9},{1,8},{2,11},{3,10},{4,13},{5,12},{6,15},{7,14},{8,1},{9,0},... | collective-permute-start | bytes 27656 | tf_op jit(solution)/shard_map/ppermute | solution.py:229
  45.7 14.3 %collective-permute-start.24 = (bf16[6,3,2,128]{3,2,1,0:T(2,128)(2,1)S(1)}, bf16[6,3,2,128]{3,2,1,0:T(2,128)(2,1)S(1)}, u32[]{:S(2)}, u32[]{:S(2)}) collective-permute-start(bf16[6,3,2,128]{3,2,1,0:T(2,128)(2,1)S(1)} %get-tuple-element.51), channel_id=1, source_target_pairs={{0,10},{1,11},{2,8},{3,9},{4,14},{5,15},{6,12},{7,13},{8,2},{9,3},... | collective-permute-start | bytes 27656 | tf_op jit(solution)/shard_map/ppermute | solution.py:229
  50.1 10.4 %collective-permute-start.44 = (bf16[48,128]{1,0:T(8,128)(2,1)S(1)}, bf16[48,128]{1,0:T(8,128)(2,1)S(1)}, u32[]{:S(2)}, u32[]{:S(2)}) collective-permute-start(bf16[48,128]{1,0:T(8,128)(2,1)S(1)} %get-tuple-element.58.refs_0_), channel_id=1, source_target_pairs={{0,15},{1,14},{2,13},{3,12},{4,11},{5,10},{6,9},{7,8},{8,7},{9,6},... | collective-permute-start | bytes 36872 | tf_op jit(solution)/shard_map/ppermute | solution.py:229
  51.8 12.2 %collective-permute-start.43 = (bf16[48,128]{1,0:T(8,128)(2,1)S(1)}, bf16[48,128]{1,0:T(8,128)(2,1)S(1)}, u32[]{:S(2)}, u32[]{:S(2)}) collective-permute-start(bf16[48,128]{1,0:T(8,128)(2,1)S(1)} %get-tuple-element.58.refs_0_), channel_id=1, source_target_pairs={{0,14},{1,15},{2,12},{3,13},{4,10},{5,11},{6,8},{7,9},{8,6},{9,7},... | collective-permute-start | bytes 36872 | tf_op jit(solution)/shard_map/ppermute | solution.py:229
  55.7 8.3 %collective-permute-start.42 = (bf16[48,128]{1,0:T(8,128)(2,1)S(1)}, bf16[48,128]{1,0:T(8,128)(2,1)S(1)}, u32[]{:S(2)}, u32[]{:S(2)}) collective-permute-start(bf16[48,128]{1,0:T(8,128)(2,1)S(1)} %get-tuple-element.58.refs_0_), channel_id=1, source_target_pairs={{0,13},{1,12},{2,15},{3,14},{4,9},{5,8},{6,11},{7,10},{8,5},{9,4},... | collective-permute-start | bytes 36872 | tf_op jit(solution)/shard_map/ppermute | solution.py:229
  57.1 9.6 %collective-permute-start.41 = (bf16[48,128]{1,0:T(8,128)(2,1)S(1)}, bf16[48,128]{1,0:T(8,128)(2,1)S(1)}, u32[]{:S(2)}, u32[]{:S(2)}) collective-permute-start(bf16[48,128]{1,0:T(8,128)(2,1)S(1)} %get-tuple-element.58.refs_0_), channel_id=1, source_target_pairs={{0,12},{1,13},{2,14},{3,15},{4,8},{5,9},{6,10},{7,11},{8,4},{9,5},... | collective-permute-start | bytes 36872 | tf_op jit(solution)/shard_map/ppermute | solution.py:229
  60.5 6.2 %collective-permute-start.40 = (bf16[48,128]{1,0:T(8,128)(2,1)S(1)}, bf16[48,128]{1,0:T(8,128)(2,1)S(1)}, u32[]{:S(2)}, u32[]{:S(2)}) collective-permute-start(bf16[48,128]{1,0:T(8,128)(2,1)S(1)} %get-tuple-element.58.refs_0_), channel_id=1, source_target_pairs={{0,11},{1,10},{2,9},{3,8},{4,15},{5,14},{6,13},{7,12},{8,3},{9,2},... | collective-permute-start | bytes 36872 | tf_op jit(solution)/shard_map/ppermute | solution.py:229
  60.5 10.0 %collective-permute-start.39 = (bf16[48,128]{1,0:T(8,128)(2,1)S(1)}, bf16[48,128]{1,0:T(8,128)(2,1)S(1)}, u32[]{:S(2)}, u32[]{:S(2)}) collective-permute-start(bf16[48,128]{1,0:T(8,128)(2,1)S(1)} %get-tuple-element.58.refs_0_), channel_id=1, source_target_pairs={{0,10},{1,11},{2,8},{3,9},{4,14},{5,15},{6,12},{7,13},{8,2},{9,3},... | collective-permute-start | bytes 36872 | tf_op jit(solution)/shard_map/ppermute | solution.py:229
  64.0 6.5 %collective-permute-start.38 = (bf16[48,128]{1,0:T(8,128)(2,1)S(1)}, bf16[48,128]{1,0:T(8,128)(2,1)S(1)}, u32[]{:S(2)}, u32[]{:S(2)}) collective-permute-start(bf16[48,128]{1,0:T(8,128)(2,1)S(1)} %get-tuple-element.58.refs_0_), channel_id=1, source_target_pairs={{0,9},{1,8},{2,11},{3,10},{4,13},{5,12},{6,15},{7,14},{8,1},{9,0},... | collective-permute-start | bytes 36872 | tf_op jit(solution)/shard_map/ppermute | solution.py:229
  64.0 8.3 %collective-permute-start.37 = (bf16[48,128]{1,0:T(8,128)(2,1)S(1)}, bf16[48,128]{1,0:T(8,128)(2,1)S(1)}, u32[]{:S(2)}, u32[]{:S(2)}) collective-permute-start(bf16[48,128]{1,0:T(8,128)(2,1)S(1)} %get-tuple-element.58.refs_0_), channel_id=1, source_target_pairs={{0,8},{1,9},{2,10},{3,11},{4,12},{5,13},{6,14},{7,15},{8,0},{9,1},... | collective-permute-start | bytes 36872 | tf_op jit(solution)/shard_map/ppermute | solution.py:229
  66.7 5.9 %collective-permute-start.36 = (bf16[48,128]{1,0:T(8,128)(2,1)S(1)}, bf16[48,128]{1,0:T(8,128)(2,1)S(1)}, u32[]{:S(2)}, u32[]{:S(2)}) collective-permute-start(bf16[48,128]{1,0:T(8,128)(2,1)S(1)} %get-tuple-element.58.refs_0_), channel_id=1, source_target_pairs={{0,7},{1,6},{2,5},{3,4},{4,3},{5,2},{6,1},{7,0},{8,15},{9,14},{10,... | collective-permute-start | bytes 36872 | tf_op jit(solution)/shard_map/ppermute | solution.py:229
  66.7 7.3 %collective-permute-start.35 = (bf16[48,128]{1,0:T(8,128)(2,1)S(1)}, bf16[48,128]{1,0:T(8,128)(2,1)S(1)}, u32[]{:S(2)}, u32[]{:S(2)}) collective-permute-start(bf16[48,128]{1,0:T(8,128)(2,1)S(1)} %get-tuple-element.58.refs_0_), channel_id=1, source_target_pairs={{0,6},{1,7},{2,4},{3,5},{4,2},{5,3},{6,0},{7,1},{8,14},{9,15},{10,... | collective-permute-start | bytes 36872 | tf_op jit(solution)/shard_map/ppermute | solution.py:229
  72.3 5.3 %collective-permute-start.32 = (bf16[48,128]{1,0:T(8,128)(2,1)S(1)}, bf16[48,128]{1,0:T(8,128)(2,1)S(1)}, u32[]{:S(2)}, u32[]{:S(2)}) collective-permute-start(bf16[48,128]{1,0:T(8,128)(2,1)S(1)} %get-tuple-element.58.refs_0_), channel_id=1, source_target_pairs={{0,3},{1,2},{2,1},{3,0},{4,7},{5,6},{6,5},{7,4},{8,11},{9,10},{10,... | collective-permute-start | bytes 36872 | tf_op jit(solution)/shard_map/ppermute | solution.py:229
  72.6 5.9 %collective-permute-start.31 = (bf16[48,128]{1,0:T(8,128)(2,1)S(1)}, bf16[48,128]{1,0:T(8,128)(2,1)S(1)}, u32[]{:S(2)}, u32[]{:S(2)}) collective-permute-start(bf16[48,128]{1,0:T(8,128)(2,1)S(1)} %get-tuple-element.58.refs_0_), channel_id=1, source_target_pairs={{0,2},{1,3},{2,0},{3,1},{4,6},{5,7},{6,4},{7,5},{8,10},{9,11},{10,... | collective-permute-start | bytes 36872 | tf_op jit(solution)/shard_map/ppermute | solution.py:229
  74.0 7.7 %collective-permute-start.30 = (bf16[48,128]{1,0:T(8,128)(2,1)S(1)}, bf16[48,128]{1,0:T(8,128)(2,1)S(1)}, u32[]{:S(2)}, u32[]{:S(2)}) collective-permute-start(bf16[48,128]{1,0:T(8,128)(2,1)S(1)} %get-tuple-element.58.refs_0_), channel_id=1, source_target_pairs={{0,1},{1,0},{2,3},{3,2},{4,5},{5,4},{6,7},{7,6},{8,9},{9,8},{10,11... | collective-permute-start | bytes 36872 | tf_op jit(solution)/shard_map/ppermute | solution.py:229
  74.8 10.4 %collective-permute-start.25 = (bf16[6,3,2,128]{3,2,1,0:T(2,128)(2,1)}, bf16[6,3,2,128]{3,2,1,0:T(2,128)(2,1)S(1)}, u32[]{:S(2)}, u32[]{:S(2)}) collective-permute-start(bf16[6,3,2,128]{3,2,1,0:T(2,128)(2,1)} %copy-done.31), channel_id=1, source_target_pairs={{0,11},{1,10},{2,9},{3,8},{4,15},{5,14},{6,13},{7,12},{8,3},{9,2},... | collective-permute-start | bytes 27656 | tf_op jit(solution)/shard_map/ppermute | solution.py:229
  75.2 10.3 %collective-permute-start.26 = (bf16[6,3,2,128]{3,2,1,0:T(2,128)(2,1)}, bf16[6,3,2,128]{3,2,1,0:T(2,128)(2,1)S(1)}, u32[]{:S(2)}, u32[]{:S(2)}) collective-permute-start(bf16[6,3,2,128]{3,2,1,0:T(2,128)(2,1)} %copy-done.30), channel_id=1, source_target_pairs={{0,12},{1,13},{2,14},{3,15},{4,8},{5,9},{6,10},{7,11},{8,4},{9,5},... | collective-permute-start | bytes 27656 | tf_op jit(solution)/shard_map/ppermute | solution.py:229
  77.6 9.3 %collective-permute-start.27 = (bf16[6,3,2,128]{3,2,1,0:T(2,128)(2,1)}, bf16[6,3,2,128]{3,2,1,0:T(2,128)(2,1)S(1)}, u32[]{:S(2)}, u32[]{:S(2)}) collective-permute-start(bf16[6,3,2,128]{3,2,1,0:T(2,128)(2,1)} %copy-done.29), channel_id=1, source_target_pairs={{0,13},{1,12},{2,15},{3,14},{4,9},{5,8},{6,11},{7,10},{8,5},{9,4},... | collective-permute-start | bytes 27656 | tf_op jit(solution)/shard_map/ppermute | solution.py:229
  78.5 8.7 %collective-permute-start.28 = (bf16[6,3,2,128]{3,2,1,0:T(2,128)(2,1)}, bf16[6,3,2,128]{3,2,1,0:T(2,128)(2,1)S(1)}, u32[]{:S(2)}, u32[]{:S(2)}) collective-permute-start(bf16[6,3,2,128]{3,2,1,0:T(2,128)(2,1)} %copy-done.28), channel_id=1, source_target_pairs={{0,14},{1,15},{2,12},{3,13},{4,10},{5,11},{6,8},{7,9},{8,6},{9,7},... | collective-permute-start | bytes 27656 | tf_op jit(solution)/shard_map/ppermute | solution.py:229
  81.7 6.0 %collective-permute-start.29 = (bf16[6,3,2,128]{3,2,1,0:T(2,128)(2,1)}, bf16[6,3,2,128]{3,2,1,0:T(2,128)(2,1)S(1)}, u32[]{:S(2)}, u32[]{:S(2)}) collective-permute-start(bf16[6,3,2,128]{3,2,1,0:T(2,128)(2,1)} %copy-done.27), channel_id=1, source_target_pairs={{0,15},{1,14},{2,13},{3,12},{4,11},{5,10},{6,9},{7,8},{8,7},{9,6},... | collective-permute-start | bytes 27656 | tf_op jit(solution)/shard_map/ppermute | solution.py:229
  85.5 5.5 %collective-permute-start.46 = (bf16[3,3,2,128]{3,2,1,0:T(2,128)(2,1)S(1)}, bf16[3,3,2,128]{3,2,1,0:T(2,128)(2,1)S(1)}, u32[]{:S(2)}, u32[]{:S(2)}) collective-permute-start(bf16[3,3,2,128]{3,2,1,0:T(2,128)(2,1)S(1)} %get-tuple-element.61), channel_id=1, source_target_pairs={{0,2},{1,3},{2,0},{3,1},{4,6},{5,7},{6,4},{7,5},{8,10},{9,11},{10,... | collective-permute-start | bytes 13832 | tf_op jit(solution)/shard_map/ppermute | solution.py:229
  86.9 5.6 %collective-permute-start.47 = (bf16[3,3,2,128]{3,2,1,0:T(2,128)(2,1)S(1)}, bf16[3,3,2,128]{3,2,1,0:T(2,128)(2,1)S(1)}, u32[]{:S(2)}, u32[]{:S(2)}) collective-permute-start(bf16[3,3,2,128]{3,2,1,0:T(2,128)(2,1)S(1)} %get-tuple-element.62), channel_id=1, source_target_pairs={{0,3},{1,2},{2,1},{3,0},{4,7},{5,6},{6,5},{7,4},{8,11},{9,10},{10,... | collective-permute-start | bytes 13832 | tf_op jit(solution)/shard_map/ppermute | solution.py:229
  87.2 6.4 %collective-permute-start.48 = (bf16[3,3,2,128]{3,2,1,0:T(2,128)(2,1)S(1)}, bf16[3,3,2,128]{3,2,1,0:T(2,128)(2,1)S(1)}, u32[]{:S(2)}, u32[]{:S(2)}) collective-permute-start(bf16[3,3,2,128]{3,2,1,0:T(2,128)(2,1)S(1)} %get-tuple-element.63), channel_id=1, source_target_pairs={{0,4},{1,5},{2,6},{3,7},{4,0},{5,1},{6,2},{7,3},{8,12},{9,13},{10,... | collective-permute-start | bytes 13832 | tf_op jit(solution)/shard_map/ppermute | solution.py:229
  87.7 7.4 %collective-permute-start.49 = (bf16[3,3,2,128]{3,2,1,0:T(2,128)(2,1)S(1)}, bf16[3,3,2,128]{3,2,1,0:T(2,128)(2,1)S(1)}, u32[]{:S(2)}, u32[]{:S(2)}) collective-permute-start(bf16[3,3,2,128]{3,2,1,0:T(2,128)(2,1)S(1)} %get-tuple-element.64), channel_id=1, source_target_pairs={{0,5},{1,4},{2,7},{3,6},{4,1},{5,0},{6,3},{7,2},{8,13},{9,12},{10,... | collective-permute-start | bytes 13832 | tf_op jit(solution)/shard_map/ppermute | solution.py:229
  89.7 8.4 %collective-permute-start.50 = (bf16[3,3,2,128]{3,2,1,0:T(2,128)(2,1)S(1)}, bf16[3,3,2,128]{3,2,1,0:T(2,128)(2,1)S(1)}, u32[]{:S(2)}, u32[]{:S(2)}) collective-permute-start(bf16[3,3,2,128]{3,2,1,0:T(2,128)(2,1)S(1)} %get-tuple-element.65), channel_id=1, source_target_pairs={{0,6},{1,7},{2,4},{3,5},{4,2},{5,3},{6,0},{7,1},{8,14},{9,15},{10,... | collective-permute-start | bytes 13832 | tf_op jit(solution)/shard_map/ppermute | solution.py:229
  91.0 8.6 %collective-permute-start.51 = (bf16[3,3,2,128]{3,2,1,0:T(2,128)(2,1)S(1)}, bf16[3,3,2,128]{3,2,1,0:T(2,128)(2,1)S(1)}, u32[]{:S(2)}, u32[]{:S(2)}) collective-permute-start(bf16[3,3,2,128]{3,2,1,0:T(2,128)(2,1)S(1)} %get-tuple-element.66), channel_id=1, source_target_pairs={{0,7},{1,6},{2,5},{3,4},{4,3},{5,2},{6,1},{7,0},{8,15},{9,14},{10,... | collective-permute-start | bytes 13832 | tf_op jit(solution)/shard_map/ppermute | solution.py:229
  92.4 9.6 %collective-permute-start.52 = (bf16[3,3,2,128]{3,2,1,0:T(2,128)(2,1)S(1)}, bf16[3,3,2,128]{3,2,1,0:T(2,128)(2,1)S(1)}, u32[]{:S(2)}, u32[]{:S(2)}) collective-permute-start(bf16[3,3,2,128]{3,2,1,0:T(2,128)(2,1)S(1)} %get-tuple-element.67), channel_id=1, source_target_pairs={{0,8},{1,9},{2,10},{3,11},{4,12},{5,13},{6,14},{7,15},{8,0},{9,1},... | collective-permute-start | bytes 13832 | tf_op jit(solution)/shard_map/ppermute | solution.py:229
  93.6 9.6 %collective-permute-start.53 = (bf16[3,3,2,128]{3,2,1,0:T(2,128)(2,1)S(1)}, bf16[3,3,2,128]{3,2,1,0:T(2,128)(2,1)S(1)}, u32[]{:S(2)}, u32[]{:S(2)}) collective-permute-start(bf16[3,3,2,128]{3,2,1,0:T(2,128)(2,1)S(1)} %get-tuple-element.68), channel_id=1, source_target_pairs={{0,9},{1,8},{2,11},{3,10},{4,13},{5,12},{6,15},{7,14},{8,1},{9,0},... | collective-permute-start | bytes 13832 | tf_op jit(solution)/shard_map/ppermute | solution.py:229
  95.1 11.3 %collective-permute-start.54 = (bf16[3,3,2,128]{3,2,1,0:T(2,128)(2,1)S(1)}, bf16[3,3,2,128]{3,2,1,0:T(2,128)(2,1)S(1)}, u32[]{:S(2)}, u32[]{:S(2)}) collective-permute-start(bf16[3,3,2,128]{3,2,1,0:T(2,128)(2,1)S(1)} %get-tuple-element.69), channel_id=1, source_target_pairs={{0,10},{1,11},{2,8},{3,9},{4,14},{5,15},{6,12},{7,13},{8,2},{9,3},... | collective-permute-start | bytes 13832 | tf_op jit(solution)/shard_map/ppermute | solution.py:229
  98.1 16.7 %collective-permute-start.55 = (bf16[3,3,2,128]{3,2,1,0:T(2,128)(2,1)}, bf16[3,3,2,128]{3,2,1,0:T(2,128)(2,1)S(1)}, u32[]{:S(2)}, u32[]{:S(2)}) collective-permute-start(bf16[3,3,2,128]{3,2,1,0:T(2,128)(2,1)} %get-tuple-element.70), channel_id=1, source_target_pairs={{0,11},{1,10},{2,9},{3,8},{4,15},{5,14},{6,13},{7,12},{8,3},{9,2},... | collective-permute-start | bytes 13832 | tf_op jit(solution)/shard_map/ppermute | solution.py:229
  99.6 15.2 %collective-permute-start.56 = (bf16[3,3,2,128]{3,2,1,0:T(2,128)(2,1)}, bf16[3,3,2,128]{3,2,1,0:T(2,128)(2,1)S(1)}, u32[]{:S(2)}, u32[]{:S(2)}) collective-permute-start(bf16[3,3,2,128]{3,2,1,0:T(2,128)(2,1)} %get-tuple-element.71), channel_id=1, source_target_pairs={{0,12},{1,13},{2,14},{3,15},{4,8},{5,9},{6,10},{7,11},{8,4},{9,5},... | collective-permute-start | bytes 13832 | tf_op jit(solution)/shard_map/ppermute | solution.py:229
  102.0 12.8 %collective-permute-start.57 = (bf16[3,3,2,128]{3,2,1,0:T(2,128)(2,1)}, bf16[3,3,2,128]{3,2,1,0:T(2,128)(2,1)S(1)}, u32[]{:S(2)}, u32[]{:S(2)}) collective-permute-start(bf16[3,3,2,128]{3,2,1,0:T(2,128)(2,1)} %get-tuple-element.72), channel_id=1, source_target_pairs={{0,13},{1,12},{2,15},{3,14},{4,9},{5,8},{6,11},{7,10},{8,5},{9,4},... | collective-permute-start | bytes 13832 | tf_op jit(solution)/shard_map/ppermute | solution.py:229
  103.2 11.6 %collective-permute-start.58 = (bf16[3,3,2,128]{3,2,1,0:T(2,128)(2,1)}, bf16[3,3,2,128]{3,2,1,0:T(2,128)(2,1)S(1)}, u32[]{:S(2)}, u32[]{:S(2)}) collective-permute-start(bf16[3,3,2,128]{3,2,1,0:T(2,128)(2,1)} %get-tuple-element.73), channel_id=1, source_target_pairs={{0,14},{1,15},{2,12},{3,13},{4,10},{5,11},{6,8},{7,9},{8,6},{9,7},... | collective-permute-start | bytes 13832 | tf_op jit(solution)/shard_map/ppermute | solution.py:229
  106.4 8.4 %collective-permute-start.59 = (bf16[3,3,2,128]{3,2,1,0:T(2,128)(2,1)}, bf16[3,3,2,128]{3,2,1,0:T(2,128)(2,1)S(1)}, u32[]{:S(2)}, u32[]{:S(2)}) collective-permute-start(bf16[3,3,2,128]{3,2,1,0:T(2,128)(2,1)} %get-tuple-element.74), channel_id=1, source_target_pairs={{0,15},{1,14},{2,13},{3,12},{4,11},{5,10},{6,9},{7,8},{8,7},{9,6},... | collective-permute-start | bytes 13832 | tf_op jit(solution)/shard_map/ppermute | solution.py:229
  (44 other events, 290.5 us)

commit v3 on v2

--- a/solution.py
+++ b/solution.py
@@ -107,7 +107,7 @@
     return cosine, sine
 
 
-def live_rows(my_lengths, request_page_table, pool_pages, page_len):
+def live_tokens(my_lengths, request_page_table, pool_pages, page_len):
     pages = jnp.arange(pool_pages, dtype=jnp.int32)
     max_pages = request_page_table.shape[1]
     place = jnp.max(
@@ -119,7 +119,11 @@
         axis=1,
     )
     token = place[:, :, None] * page_len + jnp.arange(page_len, dtype=jnp.int32)[None, None, :]
-    alive = (place[:, :, None] >= 0) & (token < my_lengths[:, None, None])
+    return (place[:, :, None] >= 0) & (token < my_lengths[:, None, None])
+
+
+def live_rows(my_lengths, request_page_table, pool_pages, page_len):
+    alive = live_tokens(my_lengths, request_page_table, pool_pages, page_len)
     live = jnp.stack([alive, jnp.zeros_like(alive)], axis=-1).astype(jnp.int32)
     return live.reshape(request_page_table.shape[0], pool_pages * page_len * 2)
 
@@ -229,44 +233,58 @@
     return lax.ppermute(value, "replica", [(i, i ^ mask) for i in range(count)])
 
 
-def cache_kernel(pool_ref, out_ref, sem):
-    heads = out_ref.shape[0]
-    copies = [pltpu.make_async_copy(pool_ref.at[:, h], out_ref.at[h], sem.at[h]) for h in range(heads)]
+CONTRACT_LANES = (((1,), (1,)), ((), ()))
+SPLIT_BUFFERS = 4
+
+
+def cache_kernel(pool_ref, keys_ref, values_ref, raw, wide, sem):
+    heads, tokens = raw.shape[:2]
+    copies = [pltpu.make_async_copy(pool_ref.at[:, h], raw.at[h], sem.at[h]) for h in range(heads)]
     for copy in copies:
         copy.start()
-    for copy in copies:
-        copy.wait()
+    rows = raw.reshape(heads, 2 * tokens, HD)
+    for h in range(heads):
+        copies[h].wait()
+        both = wide.at[h % SPLIT_BUFFERS]
+        both[...] = rows[h].astype(jnp.float32)
+        keys_ref[h] = both[pl.ds(0, tokens, stride=2), :].astype(jnp.bfloat16)
+        values_ref[h] = both[pl.ds(1, tokens, stride=2), :].astype(jnp.bfloat16)
 
 
 def cache_by_head(pool):
     tokens, heads = pool.shape[:2]
+    vmem = pl.BlockSpec(memory_space=pltpu.VMEM)
+    part = jax.ShapeDtypeStruct((heads, tokens, HD), pool.dtype)
     return pl.pallas_call(
         cache_kernel,
-        out_shape=jax.ShapeDtypeStruct((heads, tokens, 2, HD), pool.dtype),
-        in_specs=[pl.BlockSpec(memory_space=pl.ANY)],
-        out_specs=pl.BlockSpec(memory_space=pltpu.VMEM),
-        scratch_shapes=[pltpu.SemaphoreType.DMA((heads,))],
-        compiler_params=pltpu.CompilerParams(vmem_limit_bytes=8 * 2**20),
-        cost_estimate=pl.CostEstimate(flops=0, bytes_accessed=2 * pool.size * 2, transcendentals=0),
+        out_shape=(part, part),
+        in_specs=[pl.BlockSpec(memory_space=pltpu.HBM)],
+        out_specs=(vmem, vmem),
+        scratch_shapes=[
+            pltpu.VMEM((heads, tokens, 2, HD), pool.dtype),
+            pltpu.VMEM((SPLIT_BUFFERS, 2 * tokens, HD), jnp.float32),
+            pltpu.SemaphoreType.DMA((heads,)),
+        ],
+        compiler_params=pltpu.CompilerParams(vmem_limit_bytes=20 * 2**20),
+        cost_estimate=pl.CostEstimate(flops=0, bytes_accessed=3 * pool.size * 2, transcendentals=0),
         name="cache_by_head",
     )(pool)
 
 
-CONTRACT_LANES = (((1,), (1,)), ((), ()))
-
-
 def lanes_of(x_ref):
     return jnp.concatenate([x_ref[c] for c in range(x_ref.shape[0])], axis=1)
 
 
-def low_kernel(count, slot_ref, down_ref, *refs):
-    blocks, (x_ref, low_ref, sem) = refs[:count], refs[count:]
+def low_kernel(count, me_ref, slot_ref, down_ref, *refs):
+    blocks, (x_ref, low_ref, made_ref, sem, low_sem) = refs[:count], refs[count:]
+    me = me_ref[0]
     steps = blocks[0].shape[0]
     copies = []
     for k, block in enumerate(blocks):
         for t in range(steps):
-            at = k * steps + t
-            copies.append(pltpu.make_async_copy(block.at[t], x_ref.at[:, at], sem.at[at]))
+            copies.append(
+                pltpu.make_async_copy(block.at[t], x_ref.at[:, (me ^ k) * steps + t], sem.at[k * steps + t])
+            )
     for copy in copies:
         copy.start()
     for copy in copies:
@@ -276,33 +294,66 @@
     holders, rank, width = down_ref.shape
     x = lanes_of(x_ref.reshape(chunks, rows, HD))
     maps = down_ref.reshape(holders * rank, width)[...]
-    made = lax.dot_general(x, maps, CONTRACT_LANES, preferred_element_type=jnp.float32)
+    made = lax.dot_general(maps, x, CONTRACT_LANES, preferred_element_type=jnp.float32)
     slot = slot_ref[...]
-    low = jnp.zeros((rows, rank), jnp.float32)
+    low = jnp.zeros((rank, rows), jnp.float32)
     for h in range(holders):
-        low = low + jnp.where(slot == h, made[:, h * rank : (h + 1) * rank], 0.0)
-    low_ref[...] = jnp.concatenate([low[: rows // 2], low[rows // 2 :]], axis=1).astype(low_ref.dtype)
-
-
-def low_of(blocks, slot, down):
+        low = low + jnp.where(slot == h, made[h * rank : (h + 1) * rank], 0.0)
+    low = low.T
+    made_ref[...] = jnp.concatenate([low[: rows // 2], low[rows // 2 :]], axis=1).astype(made_ref.dtype)
+    copies = [pltpu.make_async_copy(made_ref, low_ref.at[k], low_sem.at[k]) for k in range(count)]
+    for copy in copies:
+        copy.start()
+    for copy in copies:
+        copy.wait()
+
+
+def low_of(me, blocks, slot, down):
     count = len(blocks)
     steps, chunks = blocks[0].shape[:2]
     rows = count * steps * 2
     rank = down.shape[1]
     vmem = pl.BlockSpec(memory_space=pltpu.VMEM)
+    any_place = pl.BlockSpec(memory_space=pl.ANY)
     return pl.pallas_call(
         functools.partial(low_kernel, count),
         out_shape=(
             jax.ShapeDtypeStruct((chunks, rows // 2, 2, HD), jnp.bfloat16),
-            jax.ShapeDtypeStruct((rows // 2, 2 * rank), jnp.bfloat16),
+            jax.ShapeDtypeStruct((count, rows // 2, 2 * rank), jnp.bfloat16),
         ),
-        in_specs=[vmem, vmem] + [pl.BlockSpec(memory_space=pl.ANY)] * count,
-        out_specs=(vmem, vmem),
-        scratch_shapes=[pltpu.SemaphoreType.DMA((count * steps,))],
+        in_specs=[pl.BlockSpec(memory_space=pltpu.SMEM), vmem, vmem] + [any_place] * count,
+        out_specs=(vmem, any_place),
+        scratch_shapes=[
+            pltpu.VMEM((rows // 2, 2 * rank), jnp.bfloat16),
+            pltpu.SemaphoreType.DMA((count * steps,)),
+            pltpu.SemaphoreType.DMA((count,)),
+        ],
         compiler_params=pltpu.CompilerParams(vmem_limit_bytes=16 * 2**20),
         cost_estimate=pl.CostEstimate(flops=10**8, bytes_accessed=4 * 10**6, transcendentals=0),
         name="low_rows",
-    )(slot, down, *blocks)
+    )(me, slot, down, *blocks)
+
+
+def project_kernel(x_ref, w_ref, out_ref):
+    chunks, pairs = x_ref.shape[:2]
+    x = lanes_of(x_ref.reshape(chunks, 2 * pairs, HD))
+    for i in range(3):
+        out_ref[i] = lax.dot_general(w_ref[i], x, CONTRACT_LANES, preferred_element_type=jnp.float32).T
+
+
+def project(x, weight):
+    pairs = x.shape[1]
+    columns = weight.shape[1]
+    vmem = pl.BlockSpec(memory_space=pltpu.VMEM)
+    return pl.pallas_call(
+        project_kernel,
+        out_shape=jax.ShapeDtypeStruct((3, 2 * pairs, columns), jnp.float32),
+        in_specs=[vmem, vmem],
+        out_specs=vmem,
+        compiler_params=pltpu.CompilerParams(vmem_limit_bytes=16 * 2**20),
+        cost_estimate=pl.CostEstimate(flops=10**9, bytes_accessed=11 * 10**6, transcendentals=0),
+        name="project",
+    )(x, weight)
 
 
 def put_chunks(buf, first, value):
@@ -314,126 +365,71 @@
         buf[first + c] = part.astype(buf.dtype)
 
 
-def send_blocks(buf, outs, sem):
-    steps = outs[0].shape[1]
-    copies = [
-        pltpu.make_async_copy(buf.at[:, k * steps : (k + 1) * steps], out, sem.at[k]) for k, out in enumerate(outs)
-    ]
-    for copy in copies:
-        copy.start()
-    for copy in copies:
-        copy.wait()
-
-
-def project_kernel(count, x_ref, w_ref, base_ref, *refs):
-    outs, (buf, sem) = refs[:count], refs[count:]
-    chunks, pairs = x_ref.shape[:2]
-    rows = 2 * pairs
-    x = lanes_of(x_ref.reshape(chunks, rows, HD))
-    columns = w_ref.shape[1]
-    each = -(-columns // HD)
-    flat = buf.reshape(buf.shape[0], rows, HD)
-    for i in range(2):
-        put_chunks(
-            flat, i * each, lax.dot_general(x, w_ref[i], CONTRACT_LANES, preferred_element_type=jnp.float32)
-        )
-    send_blocks(buf, outs, sem)
-    base_ref[...] = lax.dot_general(x, w_ref[2], CONTRACT_LANES, preferred_element_type=jnp.float32)
-
-
-def project(x, weight, count):
-    chunks, pairs = x.shape[:2]
-    columns = weight.shape[1]
-    each = -(-columns // HD)
-    steps = pairs // count
-    vmem = pl.BlockSpec(memory_space=pltpu.VMEM)
-    any_place = pl.BlockSpec(memory_space=pl.ANY)
-    piece = jax.ShapeDtypeStruct((2 * each, steps, 2, HD), jnp.bfloat16)
-    made = pl.pallas_call(
-        functools.partial(project_kernel, count),
-        out_shape=(jax.ShapeDtypeStruct((2 * pairs, columns), jnp.float32),) + (piece,) * count,
-        in_specs=[vmem, vmem],
-        out_specs=(vmem,) + (any_place,) * count,
-        scratch_shapes=[pltpu.VMEM((2 * each, pairs, 2, HD), jnp.bfloat16), pltpu.SemaphoreType.DMA((count,))],
-        compiler_params=pltpu.CompilerParams(vmem_limit_bytes=24 * 2**20),
-        cost_estimate=pl.CostEstimate(flops=10**9, bytes_accessed=11 * 10**6, transcendentals=0),
-        name="project",
-    )(x, weight)
-    return made[0], made[1:]
-
-
-def update_kernel(count, stored_ref, base_ref, up_ref, *refs):
-    lows, outs, (buf, sem) = refs[:count], refs[count : 2 * count], refs[2 * count :]
-    half, packed = lows[0].shape
+def update_kernel(stored_ref, base_ref, up_ref, low_ref, out_ref, buf, sem):
+    count, half, packed = low_ref.shape
     rank = packed // 2
     rows = 2 * half
-    per = half // (count // 2)
-    row = lax.broadcasted_iota(jnp.int32, (half, half), 0)
-    col = lax.broadcasted_iota(jnp.int32, (half, half), 1)
-    low = jnp.zeros((half, packed), jnp.float32)
-    for s in range(count):
-        piece = lows[s][...]
-        if s >= count // 2:
-            piece = jnp.concatenate([piece[:, rank:], piece[:, :rank]], axis=1)
-        near = s % (count // 2)
-        same = ((row // per) == ((col // per) ^ near)) & (row % per == col % per)
-        low = low + jnp.dot(
-            jnp.where(same, 1.0, 0.0).astype(jnp.bfloat16), piece, preferred_element_type=jnp.float32
-        )
+    low = low_ref[0].astype(jnp.float32)
+    for s in range(1, count):
+        low = low + low_ref[s].astype(jnp.float32)
     low = jnp.concatenate([low[:, :rank], low[:, rank:]], axis=0)
     adapters = up_ref.shape[0] // rank
     batch = 256 // rank
     spread = jnp.concatenate([low] * batch, axis=1)
     which = lax.broadcasted_iota(jnp.int32, (rows, batch * rank), 1) // rank
     ahead = stored_ref[...] - which
-    total = jnp.zeros(base_ref.shape, jnp.float32)
+    total = jnp.zeros(base_ref.shape[1:], jnp.float32)
     for a in range(0, adapters, batch):
         wide = jnp.where(ahead == a, spread, 0.0).astype(jnp.bfloat16)
         total = total + jnp.dot(wide, up_ref[a * rank : (a + batch) * rank], preferred_element_type=jnp.float32)
-    put_chunks(buf.reshape(buf.shape[0], rows, HD), 0, base_ref[...] + adapter_scale * total)
-    send_blocks(buf, outs, sem)
+    flat = buf.reshape(buf.shape[0], rows, HD)
+    each = buf.shape[0] // 3
+    put_chunks(flat, 0, base_ref[0])
+    put_chunks(flat, each, base_ref[1])
+    put_chunks(flat, 2 * each, base_ref[2] + adapter_scale * total)
+    steps = out_ref.shape[2]
+    copies = [
+        pltpu.make_async_copy(buf.at[:, k * steps : (k + 1) * steps], out_ref.at[k], sem.at[k]) for k in range(count)
+    ]
+    for copy in copies:
+        copy.start()
+    for copy in copies:
+        copy.wait()
 
 
 def update_values(stored, base, up, lows):
-    count = len(lows)
-    rows, columns = base.shape
-    each = -(-columns // HD)
+    count = lows.shape[0]
+    rows, columns = base.shape[1:]
+    chunks = 3 * -(-columns // HD)
     pairs = rows // 2
     vmem = pl.BlockSpec(memory_space=pltpu.VMEM)
-    any_place = pl.BlockSpec(memory_space=pl.ANY)
-    piece = jax.ShapeDtypeStruct((each, pairs // count, 2, HD), jnp.bfloat16)
     return pl.pallas_call(
-        functools.partial(update_kernel, count),
-        out_shape=(piece,) * count,
-        in_specs=[vmem] * (3 + count),
-        out_specs=(any_place,) * count,
-        scratch_shapes=[pltpu.VMEM((each, pairs, 2, HD), jnp.bfloat16), pltpu.SemaphoreType.DMA((count,))],
+        update_kernel,
+        out_shape=jax.ShapeDtypeStruct((count, chunks, pairs // count, 2, HD), jnp.bfloat16),
+        in_specs=[vmem] * 4,
+        out_specs=pl.BlockSpec(memory_space=pl.ANY),
+        scratch_shapes=[pltpu.VMEM((chunks, pairs, 2, HD), jnp.bfloat16), pltpu.SemaphoreType.DMA((count,))],
         compiler_params=pltpu.CompilerParams(vmem_limit_bytes=16 * 2**20),
         cost_estimate=pl.CostEstimate(flops=3 * 10**8, bytes_accessed=4 * 10**6, transcendentals=0),
         name="update_values",
-    )(stored, base, up, *lows)
-
-
-def attend_kernel(count, me_ref, cos_ref, sin_ref, live_ref, cache_ref, *refs):
-    pieces, fresh_values = refs[:count], refs[count : 2 * count]
-    out_ref, kn_ref, vn_ref = refs[2 * count :]
-    steps = pieces[0].shape[1]
+    )(stored, base, up, lows)
+
+
+def attend_kernel(cos_ref, sin_ref, live_ref, keys_ref, values_ref, pieces_ref, out_ref, kn_ref, vn_ref):
+    count, _, steps = pieces_ref.shape[:3]
     rows = 2 * steps
-    each = fresh_values[0].shape[0]
+    each = pieces_ref.shape[1] // 3
     heads = 2 * out_ref.shape[1] // count
     lanes = heads * HD
     group = rows * HEAD_BLOCK
-    me = me_ref[0]
-    first_core = me % 2 == 0
     cosine = cos_ref[...][:rows]
     sine = sin_ref[...][:rows]
     left = lax.broadcasted_iota(jnp.int32, (rows, HD), 1) < HD // 2
 
-    def chip_columns(near, far, at):
-        mine = [near[at + c].reshape(rows, HD).astype(jnp.float32) for c in range(each)]
-        theirs = [far[at + c].reshape(rows, HD).astype(jnp.float32) for c in range(each)]
-        low = [jnp.where(first_core, a, b) for a, b in zip(mine, theirs)]
-        high = [pltpu.roll(jnp.where(first_core, b, a), HD // 2, 1) for a, b in zip(mine, theirs)]
+    def chip_columns(chip, at):
+        low = [pieces_ref[2 * chip, at + c].reshape(rows, HD).astype(jnp.float32) for c in range(each)]
+        high = [pieces_ref[2 * chip + 1, at + c].reshape(rows, HD).astype(jnp.float32) for c in range(each)]
+        high = [pltpu.roll(x, HD // 2, 1) for x in high]
         whole = low[:-1] + [jnp.where(left, low[-1], high[0])]
         return whole + [jnp.where(left, a, b) for a, b in zip(high[:-1], high[1:])]
 
@@ -456,24 +452,20 @@
     live = live > 0
     kn_ref[...] = jnp.zeros_like(kn_ref)
     vn_ref[...] = jnp.zeros_like(vn_ref)
-    tokens = cache_ref.shape[1] * 2
-    cache = cache_ref.reshape(cache_ref.shape[0], tokens, HD)
-    for pair in range(count // 2):
-        base = ((me // 2) ^ pair) * heads
-        near, far = pieces[2 * pair], pieces[2 * pair + 1]
-        query = jnp.concatenate(rotated(chip_columns(near, far, 0)), axis=1)
-        key_new = jnp.concatenate(rotated(chip_columns(near, far, each)), axis=1)
-        value_new = jnp.concatenate(chip_columns(fresh_values[2 * pair], fresh_values[2 * pair + 1], 0), axis=1)
-        kn_ref[0:rows] = key_new
-        vn_ref[0:rows] = value_new
+    for chip in range(count // 2):
+        base = chip * heads
+        query = jnp.concatenate(rotated(chip_columns(chip, 0)), axis=1)
+        kn_ref[0:rows] = jnp.concatenate(rotated(chip_columns(chip, each)), axis=1)
+        vn_ref[0:rows] = jnp.concatenate(chip_columns(chip, 2 * each), axis=1)
         kn = kn_ref[...].astype(jnp.bfloat16)
         vn = vn_ref[...].astype(jnp.bfloat16)
         spread = jnp.concatenate(
             [jnp.broadcast_to(query[j : j + 1], (HEAD_BLOCK, lanes)) for j in range(rows)], axis=0
         )
         spread = jnp.where(own_head, spread, 0.0).astype(jnp.bfloat16)
-        kv = jnp.concatenate([cache[base + h] for h in range(heads)], axis=1)
-        scores = lax.dot_general(spread, kv, CONTRACT_LANES, preferred_element_type=jnp.float32) * (HD**-0.5)
+        keys = jnp.concatenate([keys_ref[base + h] for h in range(heads)], axis=1)
+        values = jnp.concatenate([values_ref[base + h] for h in range(heads)], axis=1)
+        scores = lax.dot_general(spread, keys, CONTRACT_LANES, preferred_element_type=jnp.float32) * (HD**-0.5)
         scores = jnp.where(live, scores, masked_score)
         fresh = lax.dot_general(spread, kn, CONTRACT_LANES, preferred_element_type=jnp.float32) * (HD**-0.5)
         fresh = jnp.where(new_live, fresh, masked_score)
@@ -481,8 +473,7 @@
         weights = jnp.where(live, jnp.exp(scores - top), 0.0)
         fresh = jnp.where(new_live, jnp.exp(fresh - top), 0.0)
         totals = jnp.sum(weights, axis=1, keepdims=True) + jnp.sum(fresh, axis=1, keepdims=True)
-        weights = pltpu.roll(weights, 1, 1).astype(jnp.bfloat16)
-        mixed = jnp.dot(weights, kv, preferred_element_type=jnp.float32)
+        mixed = jnp.dot(weights.astype(jnp.bfloat16), values, preferred_element_type=jnp.float32)
         mixed = mixed + jnp.dot(fresh.astype(jnp.bfloat16), vn, preferred_element_type=jnp.float32)
         mixed = jnp.where(own_head, mixed / totals, 0.0)
         out = jnp.sum(mixed.reshape(rows, HEAD_BLOCK, lanes), axis=1).astype(out_ref.dtype)
@@ -491,22 +482,21 @@
                 out_ref[t, base + h] = out[2 * t : 2 * t + 2, h * HD : (h + 1) * HD]
 
 
-def attend(me, cosine, sine, live, cache, pieces, fresh_values):
-    count = len(pieces)
-    steps = pieces[0].shape[1]
-    heads = cache.shape[0]
+def attend(cosine, sine, live, keys, values, pieces):
+    count, _, steps = pieces.shape[:3]
+    heads = keys.shape[0]
     lanes = 2 * heads // count * HD
     vmem = pl.BlockSpec(memory_space=pltpu.VMEM)
     return pl.pallas_call(
-        functools.partial(attend_kernel, count),
+        attend_kernel,
         out_shape=jax.ShapeDtypeStruct((steps, heads, 2, HD), jnp.bfloat16),
-        in_specs=[pl.BlockSpec(memory_space=pltpu.SMEM)] + [vmem] * (4 + 2 * count),
+        in_specs=[vmem] * 6,
         out_specs=vmem,
         scratch_shapes=[pltpu.VMEM((16, lanes), jnp.float32)] * 2,
         compiler_params=pltpu.CompilerParams(vmem_limit_bytes=16 * 2**20),
         cost_estimate=pl.CostEstimate(flops=10**9, bytes_accessed=6 * 10**6, transcendentals=0),
         name="attention",
-    )(me, cosine, sine, live, cache, *pieces, *fresh_values)
+    )(cosine, sine, live, keys, values, pieces)
 
 
 def chip_plan(
@@ -527,7 +517,6 @@
     holder_count, rank, _ = adapter_down_maps.shape
     pool_pages, page_len = key_value_pool.shape[:2]
     adapter_count = adapter_storage_row.shape[0]
-    request_count = request_adapter.shape[0]
 
     held = {0: hidden}
     for masks in (range(4, count, 4), (2,), (1,)):
@@ -536,34 +525,31 @@
         held[k].reshape(steps, req_dev, heads, HD).transpose(0, 2, 1, 3) for k in range(count)
     ]
 
-    owner = me ^ jnp.arange(count, dtype=jnp.int32)
-    request = owner[:, None] * req_dev + jnp.arange(req_dev, dtype=jnp.int32)[None, :]
-    request = jnp.broadcast_to(request[:, None, :], (count, steps, req_dev)).reshape(-1, 1)
-    adapter = jnp.sum(
-        jnp.where(request == jnp.arange(request_count, dtype=jnp.int32)[None, :], request_adapter[None, :], 0),
+    stored = jnp.sum(
+        jnp.where(
+            request_adapter[:, None] == jnp.arange(adapter_count, dtype=jnp.int32)[None, :],
+            adapter_storage_row[None, :],
+            0,
+        ),
         axis=1,
-        keepdims=True,
-    )
-    stored = jnp.sum(
-        jnp.where(adapter == jnp.arange(adapter_count, dtype=jnp.int32)[None, :], adapter_storage_row[None, :], 0),
-        axis=1,
-        keepdims=True,
-    )
+    )
+    stored = jnp.broadcast_to(stored.reshape(count, 1, req_dev), (count, steps, req_dev)).reshape(-1)
 
     tokens = pool_pages * page_len
-    cache = cache_by_head(key_value_pool.reshape(tokens, 2, heads, HD).transpose(0, 2, 1, 3))
-
-    x, low = low_of(blocks, stored - me * holder_count, adapter_down_maps)
-    lows = [low] + [trade(low, k, count) for k in range(1, count)]
-    base, pieces = project(x, query_key_value_weight.transpose(0, 2, 1), count)
-    pieces = [pieces[0]] + [trade(pieces[k], k, count) for k in range(1, count)]
-    values = update_values(stored, base, adapter_up_maps.reshape(adapter_count * rank, -1), lows)
-    values = [values[0]] + [trade(values[k], k, count) for k in range(1, count)]
+    keys, values = cache_by_head(key_value_pool.reshape(tokens, 2, heads, HD).transpose(0, 2, 1, 3))
+
+    x, lows = low_of(
+        me.astype(jnp.int32).reshape(1), blocks, (stored - me * holder_count)[None, :], adapter_down_maps
+    )
+    lows = lax.all_to_all(lows, "replica", split_axis=0, concat_axis=0, tiled=True)
+    base = project(x, query_key_value_weight.transpose(0, 2, 1))
+    pieces = update_values(stored[:, None], base, adapter_up_maps.reshape(adapter_count * rank, -1), lows)
+    pieces = lax.all_to_all(pieces, "replica", split_axis=0, concat_axis=0, tiled=True)
 
     my_lengths = lax.dynamic_slice_in_dim(lengths, me * req_dev, req_dev)
     cosine, sine = rotation(my_lengths, steps)
-    live = live_rows(my_lengths, request_page_table, pool_pages, page_len)
-    out = attend(me.astype(jnp.int32).reshape(1), cosine, sine, live, cache, pieces, values)
+    live = live_tokens(my_lengths, request_page_table, pool_pages, page_len).astype(jnp.int32)
+    out = attend(cosine, sine, live.reshape(req_dev, tokens), keys, values, pieces)
     return out.transpose(0, 2, 1, 3).reshape(steps, req_dev, width)
 
 

time: 122 us -> 68 us (0.56)
  starting transfers between devices: 70.5 us -> 20.9 us
  other arithmetic: 7.41 us -> 1.92 us
  Pallas kernels: 19.1 us -> 20.9 us
    ppermute x60 -> x15, starting transfers between devices: 70.5 us -> 10.9 us  [trade(): return lax.ppermute(value, 'replica', [(i, i ^ mask) for i in range(count)])]
    all_to_all x0 -> x2, starting transfers between devices: none -> 9.92 us  [the longest x1 5.9 us: chip_plan(): lax.all_to_all(pieces, 'replica', split_axis=0, concat_axis=0, tiled=True)]
    and x1 -> x0, other arithmetic: 1.62 us -> none  [live_rows(): alive = (place[:, :, None] >= 0) & (token < my_lengths[:, None, None])]
    ppermute x60 -> x15, waiting for transfers between devices: 7.05 us -> 5.73 us  [trade(): return lax.ppermute(value, 'replica', [(i, i ^ mask) for i in range(count)])]
    unnamed x64 -> x22, local copies, waits for them, and re-layouts: 14.8 us -> 16.1 us
  transfers between devices with their start and end apart: 60 -> 17, of which waited for: 5 -> 5; matrix products, arithmetic and copies ran while one was open for 8% -> 5% of each run, Pallas kernels for 5% -> 17%
where the time goes in v3:
time: 68 us; the launch traced here: 67.4 us
  starting transfers between devices  20.9 us (31%)
  Pallas kernels  20.9 us (31%)
  local copies, waits for them, and re-layouts  17.7 us (26%)
  waiting for transfers between devices  5.86 us (9%)
  other arithmetic  1.92 us (3%)
    unnamed x22, local copies, waits for them, and re-layouts  16.1 us
    ppermute x15, starting transfers between devices, trade(): return lax.ppermute(value, 'replica', [(i, i ^ mask) for i in range(count)])  10.9 us
    pallas_call x1, Pallas kernels, cache_by_head(): pl.pallas_call(cache_kernel, out_shape=(part, part), in_specs=[pl.BlockSp...  8.35 us
    all_to_all x1, starting transfers between devices, chip_plan(): lax.all_to_all(pieces, 'replica', split_axis=0, concat_axis=0, tiled=True)  5.9 us
    ppermute x15, waiting for transfers between devices, trade(): return lax.ppermute(value, 'replica', [(i, i ^ mask) for i in range(count)])  5.73 us
    pallas_call x1, Pallas kernels, attend(): pl.pallas_call(attend_kernel, out_shape=jax.ShapeDtypeStruct((steps, head...  4.84 us
    all_to_all x1, starting transfers between devices, chip_plan(): lax.all_to_all(lows, 'replica', split_axis=0, concat_axis=0, tiled=True)  4.02 us
    pallas_call x1, Pallas kernels, low_of(): pl.pallas_call(functools.partial(low_kernel, count), out_shape=(jax.Shape...  3.12 us
  transfers between devices with their start and end apart: 17, of which 5 were waited for; matrix products, arithmetic and copies ran while one was open for 5% of the time, Pallas kernels for 17%

profile of v3, /device:TPU:0, one launch (start us, length us, event | category | flops | bytes accessed | tf_op | source)
XLA Modules:
  0.0 67.4 jit_solution(9259038521167999636)
XLA Ops:
  0.0 3.0 %collective-permute-start.3 = (bf16[3,2,5120]{2,1,0:T(2,128)(2,1)}, bf16[3,2,5120]{2,1,0:T(2,128)(2,1)S(1)}, u32[]{:S(2)}, u32[]{:S(2)}) collective-permute-start(bf16[3,2,5120]{2,1,0:T(2,128)(2,1)} %param.9), channel_id=1, source_target_pairs={{0,4},{1,5},{2,6},{3,7},{4,0},{5,1},{6,2},{7,3},{8,12},{9,13},{10,... | collective-permute-start | bytes 184328 | tf_op jit(solution)/shard_map/ppermute | solution.py:233
  3.0 1.5 %collective-permute-start.1 = (bf16[3,2,5120]{2,1,0:T(2,128)(2,1)}, bf16[3,2,5120]{2,1,0:T(2,128)(2,1)S(1)}, u32[]{:S(2)}, u32[]{:S(2)}) collective-permute-start(bf16[3,2,5120]{2,1,0:T(2,128)(2,1)} %param.9), channel_id=1, source_target_pairs={{0,2},{1,3},{2,0},{3,1},{4,6},{5,7},{6,4},{7,5},{8,10},{9,11},{10,... | collective-permute-start | bytes 184328 | tf_op jit(solution)/shard_map/ppermute | solution.py:233
  4.5 2.5 %collective-permute-start.11 = (bf16[3,2,5120]{2,1,0:T(2,128)(2,1)}, bf16[3,2,5120]{2,1,0:T(2,128)(2,1)S(1)}, u32[]{:S(2)}, u32[]{:S(2)}) collective-permute-start(bf16[3,2,5120]{2,1,0:T(2,128)(2,1)} %param.9), channel_id=1, source_target_pairs={{0,12},{1,13},{2,14},{3,15},{4,8},{5,9},{6,10},{7,11},{8,4},{9,5},... | collective-permute-start | bytes 184328 | tf_op jit(solution)/shard_map/ppermute | solution.py:233
  7.0 0.1 collective-permute-start.7
  7.1 0.7 %dynamic_slice.3 = s32[2]{0:T(128)S(1)} dynamic-slice(s32[32]{0:T(128)} %param.15, s32[]{:T(128)S(6)} %select_n.11), dynamic_slice_sizes={2} | dynamic-slice | bytes 20 | tf_op jit(solution)/shard_map/dynamic_slice | solution.py:549
  7.9 0.8 %select_reduce_fusion.1 = s32[32]{0:T(128)S(1)} fusion(s32[64]{0:T(128)} %param.13, s32[32]{0:T(128)} %param.14), kind=kLoop, calls=%fused_computation.2 | loop fusion | flops 6112 | bytes 512 | tf_op jit(solution)/shard_map/reduce_sum | solution.py:528
  8.7 0.1 broadcast_in_dim.52
  8.8 0.8 %select_reduce_fusion = s32[2,64]{1,0:T(2,128)S(1)} fusion(s32[2,32]{1,0:T(2,128)} %param.16), kind=kLoop, calls=%fused_computation | loop fusion | flops 12160 | bytes 768 | tf_op jit(solution)/shard_map/reduce_max | solution.py:113
  9.6 0.6 collective-permute-start.5
  10.2 0.5 collective-permute-start.2
  10.7 0.4 collective-permute-done.11
  11.1 1.1 %collective-permute-start.13 = (bf16[3,2,5120]{2,1,0:T(2,128)(2,1)S(1)}, bf16[3,2,5120]{2,1,0:T(2,128)(2,1)S(1)}, u32[]{:S(2)}, u32[]{:S(2)}) collective-permute-start(bf16[3,2,5120]{2,1,0:T(2,128)(2,1)S(1)} %collective-permute-done.11), channel_id=1, source_target_pairs={{0,2},{1,3},{2,0},{3,1},{4,6},{5,7},{6,4},{7,5},{8,10},{9,11},{10,... | collective-permute-start | bytes 184328 | tf_op jit(solution)/shard_map/ppermute | solution.py:233
  12.2 1.7 %collective-permute-done.7 = bf16[3,2,5120]{2,1,0:T(2,128)(2,1)S(1)} collective-permute-done((bf16[3,2,5120]{2,1,0:T(2,128)(2,1)}, bf16[3,2,5120]{2,1,0:T(2,128)(2,1)S(1)}, u32[]{:S(2)}, u32[]{:S(2)}) %collective-permute-start.7) | collective-permute-done | bytes 61472 | tf_op jit(solution)/shard_map/ppermute | solution.py:233
  14.0 0.5 collective-permute-start.9
  14.5 0.1 add.46
  14.6 0.1 sub.19.slot_ref
  14.8 0.5 collective-permute-start.8
  15.3 0.1 collective-permute-start.6
  15.4 0.4 collective-permute-start.14
  15.8 2.4 %collective-permute-done.9 = bf16[3,2,5120]{2,1,0:T(2,128)(2,1)S(1)} collective-permute-done((bf16[3,2,5120]{2,1,0:T(2,128)(2,1)S(1)}, bf16[3,2,5120]{2,1,0:T(2,128)(2,1)S(1)}, u32[]{:S(2)}, u32[]{:S(2)}) %collective-permute-start.9) | collective-permute-done | bytes 61472 | tf_op jit(solution)/shard_map/ppermute | solution.py:233
  18.2 1.2 %collective-permute-done.10 = bf16[3,2,5120]{2,1,0:T(2,128)(2,1)S(1)} collective-permute-done((bf16[3,2,5120]{2,1,0:T(2,128)(2,1)S(1)}, bf16[3,2,5120]{2,1,0:T(2,128)(2,1)S(1)}, u32[]{:S(2)}, u32[]{:S(2)}) %collective-permute-start.10) | collective-permute-done | bytes 61472 | tf_op jit(solution)/shard_map/ppermute | solution.py:233
  19.4 1.7 %copy-done.5 = bf16[4,64,5120]{2,1,0:T(8,128)(2,1)S(1)} copy-done((bf16[4,64,5120]{2,1,0:T(8,128)(2,1)S(1)}, bf16[4,64,5120]{2,1,0:T(8,128)(2,1)}, u32[]{:S(2)}) %copy-start.5) | copy-done | bytes 2621464
  21.2 0.8 %copy-done.10 = bf16[3,2,5120]{2,1,0:T(2,128)(2,1)S(1)} copy-done((bf16[3,2,5120]{2,1,0:T(2,128)(2,1)S(1)}, bf16[3,2,5120]{2,1,0:T(2,128)(2,1)}, u32[]{:S(2)}) %copy-start.10) | copy-done | bytes 61464
  22.0 3.1 %low_rows.1 = (bf16[40,48,2,128]{3,2,1,0:T(2,128)(2,1)S(1)}, bf16[16,48,128]{2,1,0:T(8,128)(2,1)}) custom-call(s32[1]{0:T(128)} %bitcast.2.me_ref, s32[1,96]{1,0:T(1,128)S(1)} %sub.19.slot_ref, bf16[4,64,5120]{2,1,0:T(8,128)(2,1)S(1)} %copy-done.5, bf16[3,40,2,128]{3,2,1,0:T(2,128)(2,1)S(1)} %bitcast.60, bf16[3,40,2,128]{3,2,1,0:T(2,128)(2,1)S(1)} %bitcast.63, ...), custom_call_target="tpu_custom_call" | custom-call | flops 100000000 | bytes 4000000 | tf_op jit(solution)/shard_map/low_rows/pallas_call | solution.py:318
  25.1 1.0 %copy-done.8 = bf16[40,48,2,128]{3,2,1,0:T(2,128)(2,1)} copy-done((bf16[40,48,2,128]{3,2,1,0:T(2,128)(2,1)}, bf16[40,48,2,128]{3,2,1,0:T(2,128)(2,1)S(1)}, u32[]{:S(2)}) %copy-start.8) | copy-done | bytes 983064
  26.1 4.0 %all-to-all-start = ((bf16[16,48,128]{2,1,0:T(8,128)(2,1)}), bf16[16,48,128]{2,1,0:T(8,128)(2,1)S(1)}, u32[]{:S(2)}, u32[]{:S(2)}) async-start(bf16[16,48,128]{2,1,0:T(8,128)(2,1)} %get-tuple-element.12), calls=%async_computation | async-start | bytes 393216 | tf_op jit(solution)/shard_map/all_to_all | solution.py:544
  30.2 0.1 broadcast_in_dim_reshape.4.stored_ref
  30.3 0.1 fusion
  30.4 3.8 %copy-done = bf16[3,5120,320]{1,2,0:T(8,128)(2,1)S(1)} copy-done((bf16[3,5120,320]{1,2,0:T(8,128)(2,1)S(1)}, bf16[3,5120,320]{1,2,0:T(8,128)(2,1)}, u32[]{:S(2)}) %copy-start) | copy-done | bytes 9830424
  34.2 1.2 %copy-done.9 = bf16[40,48,2,128]{3,2,1,0:T(2,128)(2,1)S(1)} copy-done((bf16[40,48,2,128]{3,2,1,0:T(2,128)(2,1)S(1)}, bf16[40,48,2,128]{3,2,1,0:T(2,128)(2,1)}, u32[]{:S(2)}) %copy-start.9) | copy-done | bytes 983064
  35.4 2.8 %project.1.base_ref = f32[3,96,320]{2,1,0:T(8,128)S(1)} custom-call(bf16[40,48,2,128]{3,2,1,0:T(2,128)(2,1)S(1)} %copy-done.9, bf16[3,320,5120]{2,1,0:T(8,128)(2,1)S(1)} %bitcast.57), custom_call_target="tpu_custom_call" | custom-call | flops 1000000000 | bytes 11000000 | tf_op jit(solution)/shard_map/project/pallas_call | solution.py:348
  38.2 0.8 %copy-done.6 = f32[3,96,320]{2,1,0:T(8,128)} copy-done((f32[3,96,320]{2,1,0:T(8,128)}, f32[3,96,320]{2,1,0:T(8,128)S(1)}, u32[]{:S(2)}) %copy-start.6) | copy-done | bytes 368664
  39.0 0.1 all-to-all-done.low_ref
  39.1 1.0 %copy-done.7 = f32[3,96,320]{2,1,0:T(8,128)S(1)} copy-done((f32[3,96,320]{2,1,0:T(8,128)S(1)}, f32[3,96,320]{2,1,0:T(8,128)}, u32[]{:S(2)}) %copy-start.7) | copy-done | bytes 368664
  40.1 1.7 %update_values.1 = bf16[16,9,3,2,128]{4,3,2,1,0:T(2,128)(2,1)} custom-call(s32[96,1]{1,0:T(8,128)S(1)} %broadcast_in_dim_reshape.4.stored_ref, f32[3,96,320]{2,1,0:T(8,128)S(1)} %copy-done.7, bf16[4096,320]{1,0:T(8,128)(2,1)S(1)} %bitcast.59, bf16[16,48,128]{2,1,0:T(8,128)(2,1)S(1)} %all-to-all-done.low_ref), custom_call_target="tpu_custom_call" | custom-call | flops 300000000 | bytes 4000000 | tf_op jit(solution)/shard_map/update_values/pallas_call | solution.py:406
  41.9 5.9 %all-to-all-start.1 = ((bf16[16,9,3,2,128]{4,3,2,1,0:T(2,128)(2,1)}), bf16[16,9,3,2,128]{4,3,2,1,0:T(2,128)(2,1)S(1)}, u32[]{:S(2)}, u32[]{:S(2)}) async-start(bf16[16,9,3,2,128]{4,3,2,1,0:T(2,128)(2,1)} %update_values.1), calls=%async_computation.1 | async-start | bytes 442368 | tf_op jit(solution)/shard_map/all_to_all | solution.py:547
  47.8 0.1 and.12
  47.9 0.1 and.13
  48.0 0.1 add.50
  48.1 0.1 add.47
  48.2 0.1 add.48
  48.3 2.5 %copy-done.1 = bf16[64,4,2,5120]{3,2,1,0:T(2,128)(2,1)S(1)} copy-done((bf16[64,4,2,5120]{3,2,1,0:T(2,128)(2,1)S(1)}, bf16[64,4,2,5120]{3,2,1,0:T(2,128)(2,1)}, u32[]{:S(2)}) %copy-start.1) | copy-done | bytes 5242904
  50.8 8.4 %cache_by_head.1 = (bf16[40,256,128]{2,1,0:T(8,128)(2,1)S(1)}, bf16[40,256,128]{2,1,0:T(8,128)(2,1)S(1)}) custom-call(bf16[256,40,2,128]{3,2,1,0:T(2,128)(2,1)S(1)} %bitcast.58), custom_call_target="tpu_custom_call" | custom-call | bytes 15728640 | tf_op jit(solution)/shard_map/cache_by_head/pallas_call | solution.py:258
  59.2 1.5 %copy-done.3 = bf16[40,256,128]{2,1,0:T(8,128)(2,1)} copy-done((bf16[40,256,128]{2,1,0:T(8,128)(2,1)}, bf16[40,256,128]{2,1,0:T(8,128)(2,1)S(1)}, u32[]{:S(2)}) %copy-start.3) | copy-done | bytes 2621464
  60.7 0.1 pad_maximum_fusion
  60.7 0.1 and_convert_fusion.live_ref
  60.8 1.7 %copy-done.4 = bf16[40,256,128]{2,1,0:T(8,128)(2,1)S(1)} copy-done((bf16[40,256,128]{2,1,0:T(8,128)(2,1)S(1)}, bf16[40,256,128]{2,1,0:T(8,128)(2,1)}, u32[]{:S(2)}) %copy-start.4) | copy-done | bytes 2621464
  62.6 4.8 %attention.1 = bf16[3,40,2,128]{3,2,1,0:T(2,128)(2,1)} custom-call(f32[8,128]{1,0:T(8,128)S(1)} %get-tuple-element.16.cos_ref, f32[8,128]{1,0:T(8,128)S(1)} %get-tuple-element.17.sin_ref, s32[2,256]{1,0:T(2,128)S(1)} %and_convert_fusion.live_ref, bf16[40,256,128]{2,1,0:T(8,128)(2,1)S(1)} %get-tuple-element.9.keys_ref, bf16[40,256,128]{2,1,0:T(8,128)(2,1)S(1)} %copy-done.4, ...), custom_call_target="tpu_custom_call" | custom-call | flops 1000000000 | bytes 6000000 | tf_op jit(solution)/shard_map/attention/pallas_call | solution.py:490
  (37 shorter events, 0.2 us)
Async XLA Ops:
  0.0 9.6 %collective-permute-start.3 = (bf16[3,2,5120]{2,1,0:T(2,128)(2,1)}, bf16[3,2,5120]{2,1,0:T(2,128)(2,1)S(1)}, u32[]{:S(2)}, u32[]{:S(2)}) collective-permute-start(bf16[3,2,5120]{2,1,0:T(2,128)(2,1)} %param.9), channel_id=1, source_target_pairs={{0,4},{1,5},{2,6},{3,7},{4,0},{5,1},{6,2},{7,3},{8,12},{9,13},{10,... | collective-permute-start | bytes 184328 | tf_op jit(solution)/shard_map/ppermute | solution.py:233
  3.0 7.2 %collective-permute-start.1 = (bf16[3,2,5120]{2,1,0:T(2,128)(2,1)}, bf16[3,2,5120]{2,1,0:T(2,128)(2,1)S(1)}, u32[]{:S(2)}, u32[]{:S(2)}) collective-permute-start(bf16[3,2,5120]{2,1,0:T(2,128)(2,1)} %param.9), channel_id=1, source_target_pairs={{0,2},{1,3},{2,0},{3,1},{4,6},{5,7},{6,4},{7,5},{8,10},{9,11},{10,... | collective-permute-start | bytes 184328 | tf_op jit(solution)/shard_map/ppermute | solution.py:233
  4.5 5.6 %collective-permute-start = (bf16[3,2,5120]{2,1,0:T(2,128)(2,1)}, bf16[3,2,5120]{2,1,0:T(2,128)(2,1)S(1)}, u32[]{:S(2)}, u32[]{:S(2)}) collective-permute-start(bf16[3,2,5120]{2,1,0:T(2,128)(2,1)} %param.9), channel_id=1, source_target_pairs={{0,1},{1,0},{2,3},{3,2},{4,5},{5,4},{6,7},{7,6},{8,9},{9,8},{10,11... | collective-permute-start | bytes 184328 | tf_op jit(solution)/shard_map/ppermute | solution.py:233
  4.5 6.5 %collective-permute-start.11 = (bf16[3,2,5120]{2,1,0:T(2,128)(2,1)}, bf16[3,2,5120]{2,1,0:T(2,128)(2,1)S(1)}, u32[]{:S(2)}, u32[]{:S(2)}) collective-permute-start(bf16[3,2,5120]{2,1,0:T(2,128)(2,1)} %param.9), channel_id=1, source_target_pairs={{0,12},{1,13},{2,14},{3,15},{4,8},{5,9},{6,10},{7,11},{8,4},{9,5},... | collective-permute-start | bytes 184328 | tf_op jit(solution)/shard_map/ppermute | solution.py:233
  7.0 6.9 %collective-permute-start.7 = (bf16[3,2,5120]{2,1,0:T(2,128)(2,1)}, bf16[3,2,5120]{2,1,0:T(2,128)(2,1)S(1)}, u32[]{:S(2)}, u32[]{:S(2)}) collective-permute-start(bf16[3,2,5120]{2,1,0:T(2,128)(2,1)} %param.9), channel_id=1, source_target_pairs={{0,8},{1,9},{2,10},{3,11},{4,12},{5,13},{6,14},{7,15},{8,0},{9,1},... | collective-permute-start | bytes 184328 | tf_op jit(solution)/shard_map/ppermute | solution.py:233
  9.6 5.1 %collective-permute-start.5 = (bf16[3,2,5120]{2,1,0:T(2,128)(2,1)S(1)}, bf16[3,2,5120]{2,1,0:T(2,128)(2,1)S(1)}, u32[]{:S(2)}, u32[]{:S(2)}) collective-permute-start(bf16[3,2,5120]{2,1,0:T(2,128)(2,1)S(1)} %collective-permute-done.3), channel_id=1, source_target_pairs={{0,2},{1,3},{2,0},{3,1},{4,6},{5,7},{6,4},{7,5},{8,10},{9,11},{10,... | collective-permute-start | bytes 184328 | tf_op jit(solution)/shard_map/ppermute | solution.py:233
  10.2 4.6 %collective-permute-start.4 = (bf16[3,2,5120]{2,1,0:T(2,128)(2,1)S(1)}, bf16[3,2,5120]{2,1,0:T(2,128)(2,1)S(1)}, u32[]{:S(2)}, u32[]{:S(2)}) collective-permute-start(bf16[3,2,5120]{2,1,0:T(2,128)(2,1)S(1)} %collective-permute-done.3), channel_id=1, source_target_pairs={{0,1},{1,0},{2,3},{3,2},{4,5},{5,4},{6,7},{7,6},{8,9},{9,8},{10,11... | collective-permute-start | bytes 184328 | tf_op jit(solution)/shard_map/ppermute | solution.py:233
  10.2 5.1 %collective-permute-start.2 = (bf16[3,2,5120]{2,1,0:T(2,128)(2,1)S(1)}, bf16[3,2,5120]{2,1,0:T(2,128)(2,1)S(1)}, u32[]{:S(2)}, u32[]{:S(2)}) collective-permute-start(bf16[3,2,5120]{2,1,0:T(2,128)(2,1)S(1)} %collective-permute-done.1), channel_id=1, source_target_pairs={{0,1},{1,0},{2,3},{3,2},{4,5},{5,4},{6,7},{7,6},{8,9},{9,8},{10,11... | collective-permute-start | bytes 184328 | tf_op jit(solution)/shard_map/ppermute | solution.py:233
  11.1 4.3 %collective-permute-start.13 = (bf16[3,2,5120]{2,1,0:T(2,128)(2,1)S(1)}, bf16[3,2,5120]{2,1,0:T(2,128)(2,1)S(1)}, u32[]{:S(2)}, u32[]{:S(2)}) collective-permute-start(bf16[3,2,5120]{2,1,0:T(2,128)(2,1)S(1)} %collective-permute-done.11), channel_id=1, source_target_pairs={{0,2},{1,3},{2,0},{3,1},{4,6},{5,7},{6,4},{7,5},{8,10},{9,11},{10,... | collective-permute-start | bytes 184328 | tf_op jit(solution)/shard_map/ppermute | solution.py:233
  14.0 4.2 %collective-permute-start.9 = (bf16[3,2,5120]{2,1,0:T(2,128)(2,1)S(1)}, bf16[3,2,5120]{2,1,0:T(2,128)(2,1)S(1)}, u32[]{:S(2)}, u32[]{:S(2)}) collective-permute-start(bf16[3,2,5120]{2,1,0:T(2,128)(2,1)S(1)} %collective-permute-done.7), channel_id=1, source_target_pairs={{0,2},{1,3},{2,0},{3,1},{4,6},{5,7},{6,4},{7,5},{8,10},{9,11},{10,... | collective-permute-start | bytes 184328 | tf_op jit(solution)/shard_map/ppermute | solution.py:233
  14.7 3.5 %collective-permute-start.12 = (bf16[3,2,5120]{2,1,0:T(2,128)(2,1)S(1)}, bf16[3,2,5120]{2,1,0:T(2,128)(2,1)S(1)}, u32[]{:S(2)}, u32[]{:S(2)}) collective-permute-start(bf16[3,2,5120]{2,1,0:T(2,128)(2,1)S(1)} %collective-permute-done.11), channel_id=1, source_target_pairs={{0,1},{1,0},{2,3},{3,2},{4,5},{5,4},{6,7},{7,6},{8,9},{9,8},{10,11... | collective-permute-start | bytes 184328 | tf_op jit(solution)/shard_map/ppermute | solution.py:233
  14.8 3.4 %collective-permute-start.8 = (bf16[3,2,5120]{2,1,0:T(2,128)(2,1)S(1)}, bf16[3,2,5120]{2,1,0:T(2,128)(2,1)S(1)}, u32[]{:S(2)}, u32[]{:S(2)}) collective-permute-start(bf16[3,2,5120]{2,1,0:T(2,128)(2,1)S(1)} %collective-permute-done.7), channel_id=1, source_target_pairs={{0,1},{1,0},{2,3},{3,2},{4,5},{5,4},{6,7},{7,6},{8,9},{9,8},{10,11... | collective-permute-start | bytes 184328 | tf_op jit(solution)/shard_map/ppermute | solution.py:233
  15.3 2.9 %collective-permute-start.6 = (bf16[3,2,5120]{2,1,0:T(2,128)(2,1)S(1)}, bf16[3,2,5120]{2,1,0:T(2,128)(2,1)S(1)}, u32[]{:S(2)}, u32[]{:S(2)}) collective-permute-start(bf16[3,2,5120]{2,1,0:T(2,128)(2,1)S(1)} %collective-permute-done.5), channel_id=1, source_target_pairs={{0,1},{1,0},{2,3},{3,2},{4,5},{5,4},{6,7},{7,6},{8,9},{9,8},{10,11... | collective-permute-start | bytes 184328 | tf_op jit(solution)/shard_map/ppermute | solution.py:233
  15.4 2.9 %collective-permute-start.14 = (bf16[3,2,5120]{2,1,0:T(2,128)(2,1)S(1)}, bf16[3,2,5120]{2,1,0:T(2,128)(2,1)S(1)}, u32[]{:S(2)}, u32[]{:S(2)}) collective-permute-start(bf16[3,2,5120]{2,1,0:T(2,128)(2,1)S(1)} %collective-permute-done.13), channel_id=1, source_target_pairs={{0,1},{1,0},{2,3},{3,2},{4,5},{5,4},{6,7},{7,6},{8,9},{9,8},{10,11... | collective-permute-start | bytes 184328 | tf_op jit(solution)/shard_map/ppermute | solution.py:233
  18.2 1.2 %collective-permute-start.10 = (bf16[3,2,5120]{2,1,0:T(2,128)(2,1)S(1)}, bf16[3,2,5120]{2,1,0:T(2,128)(2,1)S(1)}, u32[]{:S(2)}, u32[]{:S(2)}) collective-permute-start(bf16[3,2,5120]{2,1,0:T(2,128)(2,1)S(1)} %collective-permute-done.9), channel_id=1, source_target_pairs={{0,1},{1,0},{2,3},{3,2},{4,5},{5,4},{6,7},{7,6},{8,9},{9,8},{10,11... | collective-permute-start | bytes 184328 | tf_op jit(solution)/shard_map/ppermute | solution.py:233
  19.4 1.7 %copy-start.5 = (bf16[4,64,5120]{2,1,0:T(8,128)(2,1)S(1)}, bf16[4,64,5120]{2,1,0:T(8,128)(2,1)}, u32[]{:S(2)}) copy-start(bf16[4,64,5120]{2,1,0:T(8,128)(2,1)} %down_ref.1) | copy-start | bytes 7864324
  21.2 0.8 %copy-start.10 = (bf16[3,2,5120]{2,1,0:T(2,128)(2,1)S(1)}, bf16[3,2,5120]{2,1,0:T(2,128)(2,1)}, u32[]{:S(2)}) copy-start(bf16[3,2,5120]{2,1,0:T(2,128)(2,1)} %param.9) | copy-start | bytes 184324
  25.1 1.0 %copy-start.8 = (bf16[40,48,2,128]{3,2,1,0:T(2,128)(2,1)}, bf16[40,48,2,128]{3,2,1,0:T(2,128)(2,1)S(1)}, u32[]{:S(2)}) copy-start(bf16[40,48,2,128]{3,2,1,0:T(2,128)(2,1)S(1)} %get-tuple-element.11.x_ref) | copy-start | bytes 2949124
  26.1 13.0 %all-to-all-start = ((bf16[16,48,128]{2,1,0:T(8,128)(2,1)}), bf16[16,48,128]{2,1,0:T(8,128)(2,1)S(1)}, u32[]{:S(2)}, u32[]{:S(2)}) async-start(bf16[16,48,128]{2,1,0:T(8,128)(2,1)} %get-tuple-element.12), calls=%async_computation | async-start | bytes 393216 | tf_op jit(solution)/shard_map/all_to_all | solution.py:544
  30.4 3.8 %copy-start = (bf16[3,5120,320]{1,2,0:T(8,128)(2,1)S(1)}, bf16[3,5120,320]{1,2,0:T(8,128)(2,1)}, u32[]{:S(2)}) copy-start(bf16[3,5120,320]{1,2,0:T(8,128)(2,1)} %param.10) | copy-start | bytes 29491204
  34.2 1.2 %copy-start.9 = (bf16[40,48,2,128]{3,2,1,0:T(2,128)(2,1)S(1)}, bf16[40,48,2,128]{3,2,1,0:T(2,128)(2,1)}, u32[]{:S(2)}) copy-start(bf16[40,48,2,128]{3,2,1,0:T(2,128)(2,1)} %copy-done.8) | copy-start | bytes 2949124
  35.4 3.8 %copy-start.2 = (bf16[64,64,320]{2,1,0:T(8,128)(2,1)S(1)}, bf16[64,64,320]{2,1,0:T(8,128)(2,1)}, u32[]{:S(2)}) copy-start(bf16[64,64,320]{2,1,0:T(8,128)(2,1)} %param.12) | copy-start | bytes 7864324
  38.2 0.8 %copy-start.6 = (f32[3,96,320]{2,1,0:T(8,128)}, f32[3,96,320]{2,1,0:T(8,128)S(1)}, u32[]{:S(2)}) copy-start(f32[3,96,320]{2,1,0:T(8,128)S(1)} %project.1.base_ref) | copy-start | bytes 1105924
  39.1 1.0 %copy-start.7 = (f32[3,96,320]{2,1,0:T(8,128)S(1)}, f32[3,96,320]{2,1,0:T(8,128)}, u32[]{:S(2)}) copy-start(f32[3,96,320]{2,1,0:T(8,128)} %copy-done.6) | copy-start | bytes 1105924
  41.9 19.0 %all-to-all-start.1 = ((bf16[16,9,3,2,128]{4,3,2,1,0:T(2,128)(2,1)}), bf16[16,9,3,2,128]{4,3,2,1,0:T(2,128)(2,1)S(1)}, u32[]{:S(2)}, u32[]{:S(2)}) async-start(bf16[16,9,3,2,128]{4,3,2,1,0:T(2,128)(2,1)} %update_values.1), calls=%async_computation.1 | async-start | bytes 442368 | tf_op jit(solution)/shard_map/all_to_all | solution.py:547
  48.3 2.5 %copy-start.1 = (bf16[64,4,2,5120]{3,2,1,0:T(2,128)(2,1)S(1)}, bf16[64,4,2,5120]{3,2,1,0:T(2,128)(2,1)}, u32[]{:S(2)}) copy-start(bf16[64,4,2,5120]{3,2,1,0:T(2,128)(2,1)} %param.17) | copy-start | bytes 15728644
  59.2 1.5 %copy-start.3 = (bf16[40,256,128]{2,1,0:T(8,128)(2,1)}, bf16[40,256,128]{2,1,0:T(8,128)(2,1)S(1)}, u32[]{:S(2)}) copy-start(bf16[40,256,128]{2,1,0:T(8,128)(2,1)S(1)} %get-tuple-element.10.values_ref) | copy-start | bytes 7864324
  60.8 1.7 %copy-start.4 = (bf16[40,256,128]{2,1,0:T(8,128)(2,1)S(1)}, bf16[40,256,128]{2,1,0:T(8,128)(2,1)}, u32[]{:S(2)}) copy-start(bf16[40,256,128]{2,1,0:T(8,128)(2,1)} %copy-done.3) | copy-start | bytes 7864324

commit v4 on v3

--- a/solution.py
+++ b/solution.py
@@ -237,75 +237,106 @@
 SPLIT_BUFFERS = 4
 
 
-def cache_kernel(pool_ref, keys_ref, values_ref, raw, wide, sem):
-    heads, tokens = raw.shape[:2]
-    copies = [pltpu.make_async_copy(pool_ref.at[:, h], raw.at[h], sem.at[h]) for h in range(heads)]
+def in_hbm(x):
+    return pltpu.with_memory_space_constraint(x, pltpu.HBM)
+
+
+VMEM = pl.BlockSpec(memory_space=pltpu.VMEM)
+HBM = pl.BlockSpec(memory_space=pltpu.HBM)
+SMEM = pl.BlockSpec(memory_space=pltpu.SMEM)
+ANY = pl.BlockSpec(memory_space=pl.ANY)
+
+
+def start_all(copies):
     for copy in copies:
         copy.start()
+    return copies
+
+
+def wait_all(copies):
+    for copy in copies:
+        copy.wait()
+
+
+def cache_kernel(first, pool_ref, keys_ref, values_ref, raw, wide, keys, values, sem, out_sem):
+    heads, tokens = raw.shape[:2]
+    copies = start_all(
+        [pltpu.make_async_copy(pool_ref.at[:, first + h], raw.at[h], sem.at[h]) for h in range(heads)]
+    )
     rows = raw.reshape(heads, 2 * tokens, HD)
+    sent = []
     for h in range(heads):
         copies[h].wait()
         both = wide.at[h % SPLIT_BUFFERS]
         both[...] = rows[h].astype(jnp.float32)
-        keys_ref[h] = both[pl.ds(0, tokens, stride=2), :].astype(jnp.bfloat16)
-        values_ref[h] = both[pl.ds(1, tokens, stride=2), :].astype(jnp.bfloat16)
-
-
-def cache_by_head(pool):
-    tokens, heads = pool.shape[:2]
-    vmem = pl.BlockSpec(memory_space=pltpu.VMEM)
-    part = jax.ShapeDtypeStruct((heads, tokens, HD), pool.dtype)
+        keys[h] = both[pl.ds(0, tokens, stride=2), :].astype(jnp.bfloat16)
+        values[h] = both[pl.ds(1, tokens, stride=2), :].astype(jnp.bfloat16)
+        sent += start_all(
+            [
+                pltpu.make_async_copy(keys.at[h], keys_ref.at[h], out_sem.at[0, h]),
+                pltpu.make_async_copy(values.at[h], values_ref.at[h], out_sem.at[1, h]),
+            ]
+        )
+    wait_all(sent)
+
+
+def cache_by_head(pool, first, heads):
+    tokens = pool.shape[0]
+    part = pltpu.HBM((heads, tokens, HD), pool.dtype)
     return pl.pallas_call(
-        cache_kernel,
+        functools.partial(cache_kernel, first),
         out_shape=(part, part),
-        in_specs=[pl.BlockSpec(memory_space=pltpu.HBM)],
-        out_specs=(vmem, vmem),
+        in_specs=[HBM],
+        out_specs=(HBM, HBM),
         scratch_shapes=[
             pltpu.VMEM((heads, tokens, 2, HD), pool.dtype),
             pltpu.VMEM((SPLIT_BUFFERS, 2 * tokens, HD), jnp.float32),
+            pltpu.VMEM((heads, tokens, HD), pool.dtype),
+            pltpu.VMEM((heads, tokens, HD), pool.dtype),
             pltpu.SemaphoreType.DMA((heads,)),
+            pltpu.SemaphoreType.DMA((2, heads)),
         ],
-        compiler_params=pltpu.CompilerParams(vmem_limit_bytes=20 * 2**20),
-        cost_estimate=pl.CostEstimate(flops=0, bytes_accessed=3 * pool.size * 2, transcendentals=0),
+        compiler_params=pltpu.CompilerParams(vmem_limit_bytes=16 * 2**20),
+        cost_estimate=pl.CostEstimate(flops=0, bytes_accessed=12 * 10**6, transcendentals=0),
         name="cache_by_head",
     )(pool)
 
 
-def lanes_of(x_ref):
-    return jnp.concatenate([x_ref[c] for c in range(x_ref.shape[0])], axis=1)
+def lanes_of(x):
+    return jnp.concatenate([x[c] for c in range(x.shape[0])], axis=1)
 
 
 def low_kernel(count, me_ref, slot_ref, down_ref, *refs):
-    blocks, (x_ref, low_ref, made_ref, sem, low_sem) = refs[:count], refs[count:]
+    blocks, (x_ref, low_ref, x_buf, maps, made_ref, sem, low_sem, own_sem) = refs[:count], refs[count:]
     me = me_ref[0]
     steps = blocks[0].shape[0]
+    holders, rank, width = down_ref.shape
+    fetch = pltpu.make_async_copy(down_ref, maps, own_sem.at[0])
+    fetch.start()
     copies = []
     for k, block in enumerate(blocks):
         for t in range(steps):
             copies.append(
-                pltpu.make_async_copy(block.at[t], x_ref.at[:, (me ^ k) * steps + t], sem.at[k * steps + t])
+                pltpu.make_async_copy(block.at[t], x_buf.at[:, (me ^ k) * steps + t], sem.at[k * steps + t])
             )
-    for copy in copies:
-        copy.start()
-    for copy in copies:
-        copy.wait()
-    chunks, pairs = x_ref.shape[:2]
+    wait_all(start_all(copies))
+    keep = pltpu.make_async_copy(x_buf, x_ref, own_sem.at[1])
+    keep.start()
+    chunks, pairs = x_buf.shape[:2]
     rows = 2 * pairs
-    holders, rank, width = down_ref.shape
-    x = lanes_of(x_ref.reshape(chunks, rows, HD))
-    maps = down_ref.reshape(holders * rank, width)[...]
-    made = lax.dot_general(maps, x, CONTRACT_LANES, preferred_element_type=jnp.float32)
+    x = lanes_of(x_buf.reshape(chunks, rows, HD))
+    fetch.wait()
+    made = lax.dot_general(
+        maps.reshape(holders * rank, width)[...], x, CONTRACT_LANES, preferred_element_type=jnp.float32
+    )
     slot = slot_ref[...]
     low = jnp.zeros((rank, rows), jnp.float32)
     for h in range(holders):
         low = low + jnp.where(slot == h, made[h * rank : (h + 1) * rank], 0.0)
     low = low.T
     made_ref[...] = jnp.concatenate([low[: rows // 2], low[rows // 2 :]], axis=1).astype(made_ref.dtype)
-    copies = [pltpu.make_async_copy(made_ref, low_ref.at[k], low_sem.at[k]) for k in range(count)]
-    for copy in copies:
-        copy.start()
-    for copy in copies:
-        copy.wait()
+    wait_all(start_all([pltpu.make_async_copy(made_ref, low_ref.at[k], low_sem.at[k]) for k in range(count)]))
+    keep.wait()
 
 
 def low_of(me, blocks, slot, down):
@@ -313,47 +344,26 @@
     steps, chunks = blocks[0].shape[:2]
     rows = count * steps * 2
     rank = down.shape[1]
-    vmem = pl.BlockSpec(memory_space=pltpu.VMEM)
-    any_place = pl.BlockSpec(memory_space=pl.ANY)
     return pl.pallas_call(
         functools.partial(low_kernel, count),
         out_shape=(
-            jax.ShapeDtypeStruct((chunks, rows // 2, 2, HD), jnp.bfloat16),
-            jax.ShapeDtypeStruct((count, rows // 2, 2 * rank), jnp.bfloat16),
+            pltpu.HBM((chunks, rows // 2, 2, HD), jnp.bfloat16),
+            pltpu.HBM((count, rows // 2, 2 * rank), jnp.bfloat16),
         ),
-        in_specs=[pl.BlockSpec(memory_space=pltpu.SMEM), vmem, vmem] + [any_place] * count,
-        out_specs=(vmem, any_place),
+        in_specs=[SMEM, VMEM, HBM] + [ANY] * count,
+        out_specs=(HBM, HBM),
         scratch_shapes=[
+            pltpu.VMEM((chunks, rows // 2, 2, HD), jnp.bfloat16),
+            pltpu.VMEM(down.shape, jnp.bfloat16),
             pltpu.VMEM((rows // 2, 2 * rank), jnp.bfloat16),
             pltpu.SemaphoreType.DMA((count * steps,)),
             pltpu.SemaphoreType.DMA((count,)),
+            pltpu.SemaphoreType.DMA((2,)),
         ],
         compiler_params=pltpu.CompilerParams(vmem_limit_bytes=16 * 2**20),
         cost_estimate=pl.CostEstimate(flops=10**8, bytes_accessed=4 * 10**6, transcendentals=0),
         name="low_rows",
-    )(me, slot, down, *blocks)
-
-
-def project_kernel(x_ref, w_ref, out_ref):
-    chunks, pairs = x_ref.shape[:2]
-    x = lanes_of(x_ref.reshape(chunks, 2 * pairs, HD))
-    for i in range(3):
-        out_ref[i] = lax.dot_general(w_ref[i], x, CONTRACT_LANES, preferred_element_type=jnp.float32).T
-
-
-def project(x, weight):
-    pairs = x.shape[1]
-    columns = weight.shape[1]
-    vmem = pl.BlockSpec(memory_space=pltpu.VMEM)
-    return pl.pallas_call(
-        project_kernel,
-        out_shape=jax.ShapeDtypeStruct((3, 2 * pairs, columns), jnp.float32),
-        in_specs=[vmem, vmem],
-        out_specs=vmem,
-        compiler_params=pltpu.CompilerParams(vmem_limit_bytes=16 * 2**20),
-        cost_estimate=pl.CostEstimate(flops=10**9, bytes_accessed=11 * 10**6, transcendentals=0),
-        name="project",
-    )(x, weight)
+    )(me, slot, in_hbm(down), *blocks)
 
 
 def put_chunks(buf, first, value):
@@ -365,63 +375,171 @@
         buf[first + c] = part.astype(buf.dtype)
 
 
-def update_kernel(stored_ref, base_ref, up_ref, low_ref, out_ref, buf, sem):
+def send_blocks(buf, out_ref, first, sem):
+    count, _, steps = out_ref.shape[:3]
+    chunks = buf.shape[0]
+    return start_all(
+        [
+            pltpu.make_async_copy(
+                buf.at[:, k * steps : (k + 1) * steps], out_ref.at[k, first : first + chunks], sem.at[k]
+            )
+            for k in range(count)
+        ]
+    )
+
+
+PROJECT_CHUNK = 1024
+
+
+def project_kernel(x_ref, w_ref, send_ref, base_ref, x_buf, w_buf, total, buf, base, x_sem, w_sem, sem, base_sem):
+    chunks, pairs = x_buf.shape[:2]
+    rows = 2 * pairs
+    columns, width = w_ref.shape[1:]
+    parts = width // PROJECT_CHUNK
+    per = PROJECT_CHUNK // HD
+    fetch_x = pltpu.make_async_copy(x_ref, x_buf, x_sem)
+    fetch_x.start()
+    fetches = start_all(
+        [
+            pltpu.make_async_copy(
+                w_ref.at[:, :, p * PROJECT_CHUNK : (p + 1) * PROJECT_CHUNK], w_buf.at[p], w_sem.at[p]
+            )
+            for p in range(parts)
+        ]
+    )
+    fetch_x.wait()
+    x_rows = x_buf.reshape(chunks, rows, HD)
+    for p in range(parts):
+        fetches[p].wait()
+        x = jnp.concatenate([x_rows[c] for c in range(p * per, (p + 1) * per)], axis=1)
+        for i in range(3):
+            made = lax.dot_general(w_buf[p, i], x, CONTRACT_LANES, preferred_element_type=jnp.float32)
+            total[i] = made if p == 0 else total[i] + made
+    each = buf.shape[0] // 2
+    flat = buf.reshape(buf.shape[0], rows, HD)
+    for i in range(2):
+        put_chunks(flat, i * each, total[i].T)
+    sent = send_blocks(buf, send_ref, 0, sem)
+    base[...] = total[2].T
+    keep = pltpu.make_async_copy(base, base_ref, base_sem)
+    keep.start()
+    wait_all(sent)
+    keep.wait()
+
+
+def project(x, weight, count):
+    chunks, pairs = x.shape[:2]
+    columns, width = weight.shape[1:]
+    each = -(-columns // HD)
+    parts = width // PROJECT_CHUNK
+    return pl.pallas_call(
+        project_kernel,
+        out_shape=(
+            pltpu.HBM((count, 3 * each, pairs // count, 2, HD), jnp.bfloat16),
+            pltpu.HBM((2 * pairs, columns), jnp.float32),
+        ),
+        in_specs=[HBM, HBM],
+        out_specs=(HBM, HBM),
+        scratch_shapes=[
+            pltpu.VMEM(x.shape, jnp.bfloat16),
+            pltpu.VMEM((parts, 3, columns, PROJECT_CHUNK), jnp.bfloat16),
+            pltpu.VMEM((3, columns, 2 * pairs), jnp.float32),
+            pltpu.VMEM((2 * each, pairs, 2, HD), jnp.bfloat16),
+            pltpu.VMEM((2 * pairs, columns), jnp.float32),
+            pltpu.SemaphoreType.DMA,
+            pltpu.SemaphoreType.DMA((parts,)),
+            pltpu.SemaphoreType.DMA((count,)),
+            pltpu.SemaphoreType.DMA,
+        ],
+        compiler_params=pltpu.CompilerParams(vmem_limit_bytes=24 * 2**20),
+        cost_estimate=pl.CostEstimate(flops=10**9, bytes_accessed=11 * 10**6, transcendentals=0),
+        name="project",
+    )(in_hbm(x), in_hbm(weight))
+
+
+UPDATE_PARTS = 4
+
+
+def update_kernel(stored_ref, low_ref, base_ref, up_ref, send_in, send_ref, base, up, buf, base_sem, up_sem, sem):
     count, half, packed = low_ref.shape
     rank = packed // 2
     rows = 2 * half
+    height = up_ref.shape[0] // UPDATE_PARTS
+    fetches = start_all(
+        [
+            pltpu.make_async_copy(up_ref.at[p * height : (p + 1) * height], up.at[p], up_sem.at[p])
+            for p in range(UPDATE_PARTS)
+        ]
+    )
+    fetch_base = pltpu.make_async_copy(base_ref, base, base_sem)
+    fetch_base.start()
     low = low_ref[0].astype(jnp.float32)
     for s in range(1, count):
         low = low + low_ref[s].astype(jnp.float32)
     low = jnp.concatenate([low[:, :rank], low[:, rank:]], axis=0)
-    adapters = up_ref.shape[0] // rank
     batch = 256 // rank
     spread = jnp.concatenate([low] * batch, axis=1)
     which = lax.broadcasted_iota(jnp.int32, (rows, batch * rank), 1) // rank
     ahead = stored_ref[...] - which
-    total = jnp.zeros(base_ref.shape[1:], jnp.float32)
-    for a in range(0, adapters, batch):
-        wide = jnp.where(ahead == a, spread, 0.0).astype(jnp.bfloat16)
-        total = total + jnp.dot(wide, up_ref[a * rank : (a + batch) * rank], preferred_element_type=jnp.float32)
-    flat = buf.reshape(buf.shape[0], rows, HD)
-    each = buf.shape[0] // 3
-    put_chunks(flat, 0, base_ref[0])
-    put_chunks(flat, each, base_ref[1])
-    put_chunks(flat, 2 * each, base_ref[2] + adapter_scale * total)
-    steps = out_ref.shape[2]
-    copies = [
-        pltpu.make_async_copy(buf.at[:, k * steps : (k + 1) * steps], out_ref.at[k], sem.at[k]) for k in range(count)
-    ]
-    for copy in copies:
-        copy.start()
-    for copy in copies:
-        copy.wait()
-
-
-def update_values(stored, base, up, lows):
-    count = lows.shape[0]
-    rows, columns = base.shape[1:]
-    chunks = 3 * -(-columns // HD)
-    pairs = rows // 2
-    vmem = pl.BlockSpec(memory_space=pltpu.VMEM)
+    total = jnp.zeros(base.shape, jnp.float32)
+    for p in range(UPDATE_PARTS):
+        fetches[p].wait()
+        for a in range(0, height // rank, batch):
+            wide = jnp.where(ahead == p * (height // rank) + a, spread, 0.0).astype(jnp.bfloat16)
+            total = total + jnp.dot(
+                wide, up[p, a * rank : (a + batch) * rank], preferred_element_type=jnp.float32
+            )
+    fetch_base.wait()
+    put_chunks(buf.reshape(buf.shape[0], rows, HD), 0, base[...] + adapter_scale * total)
+    wait_all(send_blocks(buf, send_ref, send_ref.shape[1] - buf.shape[0], sem))
+
+
+def update_values(stored, lows, base, up, send):
+    count, chunks = send.shape[:2]
+    rows, columns = base.shape
+    height = up.shape[0] // UPDATE_PARTS
     return pl.pallas_call(
         update_kernel,
-        out_shape=jax.ShapeDtypeStruct((count, chunks, pairs // count, 2, HD), jnp.bfloat16),
-        in_specs=[vmem] * 4,
-        out_specs=pl.BlockSpec(memory_space=pl.ANY),
-        scratch_shapes=[pltpu.VMEM((chunks, pairs, 2, HD), jnp.bfloat16), pltpu.SemaphoreType.DMA((count,))],
+        out_shape=pltpu.HBM(send.shape, send.dtype),
+        in_specs=[VMEM, VMEM, HBM, HBM, HBM],
+        out_specs=HBM,
+        scratch_shapes=[
+            pltpu.VMEM(base.shape, jnp.float32),
+            pltpu.VMEM((UPDATE_PARTS, height, columns), jnp.bfloat16),
+            pltpu.VMEM((chunks // 3, rows // 2, 2, HD), jnp.bfloat16),
+            pltpu.SemaphoreType.DMA,
+            pltpu.SemaphoreType.DMA((UPDATE_PARTS,)),
+            pltpu.SemaphoreType.DMA((count,)),
+        ],
+        input_output_aliases={4: 0},
         compiler_params=pltpu.CompilerParams(vmem_limit_bytes=16 * 2**20),
         cost_estimate=pl.CostEstimate(flops=3 * 10**8, bytes_accessed=4 * 10**6, transcendentals=0),
         name="update_values",
-    )(stored, base, up, lows)
-
-
-def attend_kernel(cos_ref, sin_ref, live_ref, keys_ref, values_ref, pieces_ref, out_ref, kn_ref, vn_ref):
+    )(stored, lows, in_hbm(base), in_hbm(up), in_hbm(send))
+
+
+def attend_kernel(halves, cos_ref, sin_ref, live_ref, pieces_ref, *refs):
+    key_refs, value_refs = refs[:halves], refs[halves : 2 * halves]
+    out_ref, keys_buf, values_buf, kn_ref, vn_ref, sem = refs[2 * halves :]
     count, _, steps = pieces_ref.shape[:3]
     rows = 2 * steps
     each = pieces_ref.shape[1] // 3
     heads = 2 * out_ref.shape[1] // count
     lanes = heads * HD
     group = rows * HEAD_BLOCK
+    chips = count // 2
+    fetches = []
+    for chip in range(chips):
+        half, at = divmod(chip, chips // halves)
+        span = slice(at * heads, (at + 1) * heads)
+        fetches.append(
+            start_all(
+                [
+                    pltpu.make_async_copy(key_refs[half].at[span], keys_buf.at[chip], sem.at[0, chip]),
+                    pltpu.make_async_copy(value_refs[half].at[span], values_buf.at[chip], sem.at[1, chip]),
+                ]
+            )
+        )
     cosine = cos_ref[...][:rows]
     sine = sin_ref[...][:rows]
     left = lax.broadcasted_iota(jnp.int32, (rows, HD), 1) < HD // 2
@@ -452,8 +570,7 @@
     live = live > 0
     kn_ref[...] = jnp.zeros_like(kn_ref)
     vn_ref[...] = jnp.zeros_like(vn_ref)
-    for chip in range(count // 2):
-        base = chip * heads
+    for chip in range(chips):
         query = jnp.concatenate(rotated(chip_columns(chip, 0)), axis=1)
         kn_ref[0:rows] = jnp.concatenate(rotated(chip_columns(chip, each)), axis=1)
         vn_ref[0:rows] = jnp.concatenate(chip_columns(chip, 2 * each), axis=1)
@@ -463,8 +580,9 @@
             [jnp.broadcast_to(query[j : j + 1], (HEAD_BLOCK, lanes)) for j in range(rows)], axis=0
         )
         spread = jnp.where(own_head, spread, 0.0).astype(jnp.bfloat16)
-        keys = jnp.concatenate([keys_ref[base + h] for h in range(heads)], axis=1)
-        values = jnp.concatenate([values_ref[base + h] for h in range(heads)], axis=1)
+        wait_all(fetches[chip])
+        keys = lanes_of(keys_buf[chip])
+        values = lanes_of(values_buf[chip])
         scores = lax.dot_general(spread, keys, CONTRACT_LANES, preferred_element_type=jnp.float32) * (HD**-0.5)
         scores = jnp.where(live, scores, masked_score)
         fresh = lax.dot_general(spread, kn, CONTRACT_LANES, preferred_element_type=jnp.float32) * (HD**-0.5)
@@ -479,24 +597,27 @@
         out = jnp.sum(mixed.reshape(rows, HEAD_BLOCK, lanes), axis=1).astype(out_ref.dtype)
         for t in range(steps):
             for h in range(heads):
-                out_ref[t, base + h] = out[2 * t : 2 * t + 2, h * HD : (h + 1) * HD]
-
-
-def attend(cosine, sine, live, keys, values, pieces):
+                out_ref[t, chip * heads + h] = out[2 * t : 2 * t + 2, h * HD : (h + 1) * HD]
+
+
+def attend(cosine, sine, live, pieces, keys, values):
     count, _, steps = pieces.shape[:3]
-    heads = keys.shape[0]
-    lanes = 2 * heads // count * HD
-    vmem = pl.BlockSpec(memory_space=pltpu.VMEM)
+    halves = len(keys)
+    heads = halves * keys[0].shape[0]
+    tokens = keys[0].shape[1]
+    per = 2 * heads // count
     return pl.pallas_call(
-        attend_kernel,
+        functools.partial(attend_kernel, halves),
         out_shape=jax.ShapeDtypeStruct((steps, heads, 2, HD), jnp.bfloat16),
-        in_specs=[vmem] * 6,
-        out_specs=vmem,
-        scratch_shapes=[pltpu.VMEM((16, lanes), jnp.float32)] * 2,
+        in_specs=[VMEM] * 4 + [HBM] * (2 * halves),
+        out_specs=VMEM,
+        scratch_shapes=[pltpu.VMEM((count // 2, per, tokens, HD), jnp.bfloat16)] * 2
+        + [pltpu.VMEM((16, per * HD), jnp.float32)] * 2
+        + [pltpu.SemaphoreType.DMA((2, count // 2))],
         compiler_params=pltpu.CompilerParams(vmem_limit_bytes=16 * 2**20),
         cost_estimate=pl.CostEstimate(flops=10**9, bytes_accessed=6 * 10**6, transcendentals=0),
         name="attention",
-    )(cosine, sine, live, keys, values, pieces)
+    )(cosine, sine, live, pieces, *[in_hbm(x) for x in keys], *[in_hbm(x) for x in values])
 
 
 def chip_plan(
@@ -518,12 +639,20 @@
     pool_pages, page_len = key_value_pool.shape[:2]
     adapter_count = adapter_storage_row.shape[0]
 
+    tokens = pool_pages * page_len
+    pool = in_hbm(key_value_pool.reshape(tokens, 2, heads, HD).transpose(0, 2, 1, 3))
+    first_half = cache_by_head(pool, 0, heads // 2)
+    second_half = cache_by_head(pool, heads // 2, heads // 2)
+
     held = {0: hidden}
-    for masks in (range(4, count, 4), (2,), (1,)):
-        held.update({k ^ m: trade(v, m, count) for k, v in list(held.items()) for m in masks})
+    held.update({m: trade(hidden, m, count) for m in range(4, count, 4)})
+    held, first_half = lax.optimization_barrier((held, first_half))
+    for mask in (2, 1):
+        held.update({k ^ mask: trade(v, mask, count) for k, v in list(held.items())})
     blocks = [
         held[k].reshape(steps, req_dev, heads, HD).transpose(0, 2, 1, 3) for k in range(count)
     ]
+    blocks[0] = in_hbm(blocks[0])
 
     stored = jnp.sum(
         jnp.where(
@@ -535,21 +664,19 @@
     )
     stored = jnp.broadcast_to(stored.reshape(count, 1, req_dev), (count, steps, req_dev)).reshape(-1)
 
-    tokens = pool_pages * page_len
-    keys, values = cache_by_head(key_value_pool.reshape(tokens, 2, heads, HD).transpose(0, 2, 1, 3))
-
     x, lows = low_of(
         me.astype(jnp.int32).reshape(1), blocks, (stored - me * holder_count)[None, :], adapter_down_maps
     )
     lows = lax.all_to_all(lows, "replica", split_axis=0, concat_axis=0, tiled=True)
-    base = project(x, query_key_value_weight.transpose(0, 2, 1))
-    pieces = update_values(stored[:, None], base, adapter_up_maps.reshape(adapter_count * rank, -1), lows)
-    pieces = lax.all_to_all(pieces, "replica", split_axis=0, concat_axis=0, tiled=True)
+    send, base = project(x, query_key_value_weight.transpose(0, 2, 1), count)
+    send = update_values(stored[:, None], lows, base, adapter_up_maps.reshape(adapter_count * rank, -1), send)
+    pieces = lax.all_to_all(send, "replica", split_axis=0, concat_axis=0, tiled=True)
 
     my_lengths = lax.dynamic_slice_in_dim(lengths, me * req_dev, req_dev)
     cosine, sine = rotation(my_lengths, steps)
     live = live_tokens(my_lengths, request_page_table, pool_pages, page_len).astype(jnp.int32)
-    out = attend(cosine, sine, live.reshape(req_dev, tokens), keys, values, pieces)
+    keys, values = zip(first_half, second_half)
+    out = attend(cosine, sine, live.reshape(req_dev, tokens), pieces, keys, values)
     return out.transpose(0, 2, 1, 3).reshape(steps, req_dev, width)
 
 

time: 68 us -> 67 us (0.985)
  local copies, waits for them, and re-layouts: 17.7 us -> 1.63 us
  Pallas kernels: 20.9 us -> 31.1 us
  starting transfers between devices: 20.9 us -> 23.7 us
  waiting for transfers between devices: 5.86 us -> 8.61 us
    unnamed x22 -> x4, local copies, waits for them, and re-layouts: 16.1 us -> 0.01 us
    pallas_call x5 -> x6, Pallas kernels: 20.9 us -> 31.1 us  [the longest x2 8.59 us: cache_by_head(): pl.pallas_call(functools.partial(cache_kernel, first), out_shape=(part, p...]
    all_to_all x1, waiting for transfers between devices: 0.01 us -> 4.39 us  [chip_plan(): lax.all_to_all(send, 'replica', split_axis=0, concat_axis=0, tiled=True)]
    all_to_all x1, starting transfers between devices: 4.02 us -> 5.97 us  [chip_plan(): lax.all_to_all(lows, 'replica', split_axis=0, concat_axis=0, tiled=True)]
    ppermute x15, waiting for transfers between devices: 5.73 us -> 3.82 us  [trade(): return lax.ppermute(value, 'replica', [(i, i ^ mask) for i in range(count)])]
    ppermute x15, starting transfers between devices: 10.9 us -> 12.1 us  [trade(): return lax.ppermute(value, 'replica', [(i, i ^ mask) for i in range(count)])]
    reduce_max x1, other arithmetic: 0.77 us -> 0.09 us  [live_tokens(): jnp.max(jnp.where(request_page_table[:, :, None] == pages[None, None, :],...]
  transfers between devices with their start and end apart: 17 -> 17, of which waited for: 5 -> 11; matrix products, arithmetic and copies ran while one was open for 5% -> 4% of each run, Pallas kernels for 17% -> 25%
where the time goes in v4:
time: 67 us; the launch traced here: 66.7 us
  Pallas kernels  31.1 us (46%)
  starting transfers between devices  23.7 us (35%)
  waiting for transfers between devices  8.61 us (13%)
  local copies, waits for them, and re-layouts  1.63 us (2%)
  other arithmetic  1.24 us (2%)
    ppermute x15, starting transfers between devices, trade(): return lax.ppermute(value, 'replica', [(i, i ^ mask) for i in range(count)])  12.1 us
    pallas_call x2, Pallas kernels, cache_by_head(): pl.pallas_call(functools.partial(cache_kernel, first), out_shape=(part, p...  8.59 us
    pallas_call x1, Pallas kernels, project(): pl.pallas_call(project_kernel, out_shape=(pltpu.HBM((count, 3 * each, pai...  8.37 us
    pallas_call x1, Pallas kernels, attend(): pl.pallas_call(functools.partial(attend_kernel, halves), out_shape=jax.Sh...  6.99 us
    all_to_all x1, starting transfers between devices, chip_plan(): lax.all_to_all(lows, 'replica', split_axis=0, concat_axis=0, tiled=True)  5.97 us
    all_to_all x1, starting transfers between devices, chip_plan(): lax.all_to_all(send, 'replica', split_axis=0, concat_axis=0, tiled=True)  5.66 us
    all_to_all x1, waiting for transfers between devices, chip_plan(): lax.all_to_all(send, 'replica', split_axis=0, concat_axis=0, tiled=True)  4.39 us
    pallas_call x1, Pallas kernels, low_of(): pl.pallas_call(functools.partial(low_kernel, count), out_shape=(pltpu.HBM...  4.05 us
  transfers between devices with their start and end apart: 17, of which 11 were waited for; matrix products, arithmetic and copies ran while one was open for 4% of the time, Pallas kernels for 25%

profile of v4, /device:TPU:0, one launch (start us, length us, event | category | flops | bytes accessed | tf_op | source)
XLA Modules:
  0.0 66.7 jit_solution(7307765030284219354)
XLA Ops:
  0.0 3.0 %collective-permute-start = (bf16[3,2,5120]{2,1,0:T(2,128)(2,1)}, bf16[3,2,5120]{2,1,0:T(2,128)(2,1)S(1)}, u32[]{:S(2)}, u32[]{:S(2)}) collective-permute-start(bf16[3,2,5120]{2,1,0:T(2,128)(2,1)} %param.9), channel_id=1, source_target_pairs={{0,4},{1,5},{2,6},{3,7},{4,0},{5,1},{6,2},{7,3},{8,12},{9,13},{10,... | collective-permute-start | bytes 184328 | tf_op jit(solution)/shard_map/ppermute | solution.py:233
  3.0 2.6 %collective-permute-start.1 = (bf16[3,2,5120]{2,1,0:T(2,128)(2,1)}, bf16[3,2,5120]{2,1,0:T(2,128)(2,1)S(1)}, u32[]{:S(2)}, u32[]{:S(2)}) collective-permute-start(bf16[3,2,5120]{2,1,0:T(2,128)(2,1)} %param.9), channel_id=1, source_target_pairs={{0,8},{1,9},{2,10},{3,11},{4,12},{5,13},{6,14},{7,15},{8,0},{9,1},... | collective-permute-start | bytes 184328 | tf_op jit(solution)/shard_map/ppermute | solution.py:233
  5.6 0.8 %select_reduce_fusion.1 = s32[32]{0:T(128)S(1)} fusion(s32[64]{0:T(128)} %param.13, s32[32]{0:T(128)} %param.14), kind=kLoop, calls=%fused_computation.2 | loop fusion | flops 6112 | bytes 512 | tf_op jit(solution)/shard_map/reduce_sum | solution.py:657
  6.5 0.1 broadcast_in_dim.52
  6.6 0.7 %dynamic_slice.3 = s32[2]{0:T(128)S(1)} dynamic-slice(s32[32]{0:T(128)} %param.15, s32[]{:T(128)S(6)} %select_n.11), dynamic_slice_sizes={2} | dynamic-slice | bytes 20 | tf_op jit(solution)/shard_map/dynamic_slice | solution.py:675
  7.3 4.3 %cache_by_head.2 = (bf16[20,256,128]{2,1,0:T(8,128)(2,1)}, bf16[20,256,128]{2,1,0:T(8,128)(2,1)}) custom-call(bf16[256,40,2,128]{3,2,1,0:T(2,128)(2,1)} %bitcast.72), custom_call_target="tpu_custom_call" | custom-call | bytes 12000000 | tf_op jit(solution)/shard_map/cache_by_head/pallas_call | solution.py:286
  11.6 0.0 collective-permute-done
  11.6 0.2 collective-permute-done.2
  11.8 1.6 %collective-permute-start.4 = (bf16[3,2,5120]{2,1,0:T(2,128)(2,1)S(1)}, bf16[3,2,5120]{2,1,0:T(2,128)(2,1)S(1)}, u32[]{:S(2)}, u32[]{:S(2)}) collective-permute-start(bf16[3,2,5120]{2,1,0:T(2,128)(2,1)S(1)} %copy-done), channel_id=1, source_target_pairs={{0,2},{1,3},{2,0},{3,1},{4,6},{5,7},{6,4},{7,5},{8,10},{9,11},{10,... | collective-permute-start | bytes 184328 | tf_op jit(solution)/shard_map/ppermute | solution.py:233
  13.5 0.4 collective-permute-start.7
  13.9 0.1 select_reduce_fusion
  14.0 0.1 collective-permute-start.6
  14.1 1.6 %collective-permute-start.10 = (bf16[3,2,5120]{2,1,0:T(2,128)(2,1)S(1)}, bf16[3,2,5120]{2,1,0:T(2,128)(2,1)S(1)}, u32[]{:S(2)}, u32[]{:S(2)}) collective-permute-start(bf16[3,2,5120]{2,1,0:T(2,128)(2,1)S(1)} %collective-permute-done.1), channel_id=1, source_target_pairs={{0,2},{1,3},{2,0},{3,1},{4,6},{5,7},{6,4},{7,5},{8,10},{9,11},{10,... | collective-permute-start | bytes 184328 | tf_op jit(solution)/shard_map/ppermute | solution.py:233
  15.7 0.2 collective-permute-start.9
  15.9 0.3 collective-permute-done.4
  16.1 1.5 %collective-permute-start.13 = (bf16[3,2,5120]{2,1,0:T(2,128)(2,1)S(1)}, bf16[3,2,5120]{2,1,0:T(2,128)(2,1)S(1)}, u32[]{:S(2)}, u32[]{:S(2)}) collective-permute-start(bf16[3,2,5120]{2,1,0:T(2,128)(2,1)S(1)} %collective-permute-done.2), channel_id=1, source_target_pairs={{0,2},{1,3},{2,0},{3,1},{4,6},{5,7},{6,4},{7,5},{8,10},{9,11},{10,... | collective-permute-start | bytes 184328 | tf_op jit(solution)/shard_map/ppermute | solution.py:233
  17.7 0.5 collective-permute-done.7
  18.2 0.1 sub.19.slot_ref
  18.3 0.1 add.46
  18.4 0.7 %collective-permute-done.10 = bf16[3,2,5120]{2,1,0:T(2,128)(2,1)S(1)} collective-permute-done((bf16[3,2,5120]{2,1,0:T(2,128)(2,1)S(1)}, bf16[3,2,5120]{2,1,0:T(2,128)(2,1)S(1)}, u32[]{:S(2)}, u32[]{:S(2)}) %collective-permute-start.10) | collective-permute-done | bytes 61472 | tf_op jit(solution)/shard_map/ppermute | solution.py:233
  19.1 0.0 collective-permute-start.3
  19.1 1.3 %collective-permute-done.13 = bf16[3,2,5120]{2,1,0:T(2,128)(2,1)S(1)} collective-permute-done((bf16[3,2,5120]{2,1,0:T(2,128)(2,1)S(1)}, bf16[3,2,5120]{2,1,0:T(2,128)(2,1)S(1)}, u32[]{:S(2)}, u32[]{:S(2)}) %collective-permute-start.13) | collective-permute-done | bytes 61472 | tf_op jit(solution)/shard_map/ppermute | solution.py:233
  20.4 0.0 collective-permute-start.5
  20.4 0.5 collective-permute-start.8
  20.9 0.1 collective-permute-start.11
  21.0 0.4 collective-permute-start.14
  21.4 0.2 collective-permute-done.5
  21.6 0.2 collective-permute-done.8
  21.8 0.4 collective-permute-done.11
  22.1 0.2 collective-permute-done.14
  22.3 4.1 %low_rows.1 = (bf16[40,48,2,128]{3,2,1,0:T(2,128)(2,1)}, bf16[16,48,128]{2,1,0:T(8,128)(2,1)}) custom-call(s32[1]{0:T(128)} %bitcast.me_ref, s32[1,96]{1,0:T(1,128)S(1)} %sub.19.slot_ref, bf16[4,64,5120]{2,1,0:T(8,128)(2,1)} %down_ref.1, bf16[3,40,2,128]{3,2,1,0:T(2,128)(2,1)} %bitcast.76, bf16[3,40,2,128]{3,2,1,0:T(2,128)(2,1)S(1)} %bitcast.67, ...), custom_call_target="tpu_custom_call" | custom-call | flops 100000000 | bytes 4000000 | tf_op jit(solution)/shard_map/low_rows/pallas_call | solution.py:347
  26.4 6.0 %all-to-all-start = ((bf16[16,48,128]{2,1,0:T(8,128)(2,1)}), bf16[16,48,128]{2,1,0:T(8,128)(2,1)S(1)}, u32[]{:S(2)}, u32[]{:S(2)}) async-start(bf16[16,48,128]{2,1,0:T(8,128)(2,1)} %get-tuple-element.25), calls=%async_computation | async-start | bytes 393216 | tf_op jit(solution)/shard_map/all_to_all | solution.py:670
  32.4 0.1 broadcast_in_dim_reshape.4.stored_ref
  32.5 0.1 fusion
  32.6 8.4 %project.1 = (bf16[16,9,3,2,128]{4,3,2,1,0:T(2,128)(2,1)}, f32[96,320]{1,0:T(8,128)}) custom-call(bf16[40,48,2,128]{3,2,1,0:T(2,128)(2,1)} %get-tuple-element.26.x_ref, bf16[3,320,5120]{2,1,0:T(8,128)(2,1)} %bitcast.74), custom_call_target="tpu_custom_call" | custom-call | flops 1000000000 | bytes 11000000 | tf_op jit(solution)/shard_map/project/pallas_call | solution.py:435
  40.9 0.4 all-to-all-done.low_ref
  41.3 3.1 %update_values.1 = bf16[16,9,3,2,128]{4,3,2,1,0:T(2,128)(2,1)} custom-call(s32[96,1]{1,0:T(8,128)S(1)} %broadcast_in_dim_reshape.4.stored_ref, bf16[16,48,128]{2,1,0:T(8,128)(2,1)S(1)} %all-to-all-done.low_ref, f32[96,320]{1,0:T(8,128)} %get-tuple-element.27.base_ref, bf16[4096,320]{1,0:T(8,128)(2,1)} %bitcast.75, ...), custom_call_target="tpu_custom_call", output_to_operand_aliasing={{}: (4, {})} | custom-call | flops 300000000 | bytes 4000000 | tf_op jit(solution)/shard_map/update_values/pallas_call | solution.py:501
  44.5 5.7 %all-to-all-start.1 = ((bf16[16,9,3,2,128]{4,3,2,1,0:T(2,128)(2,1)}), bf16[16,9,3,2,128]{4,3,2,1,0:T(2,128)(2,1)S(1)}, u32[]{:S(2)}, u32[]{:S(2)}) async-start(bf16[16,9,3,2,128]{4,3,2,1,0:T(2,128)(2,1)} %update_values.1), calls=%async_computation.1 | async-start | bytes 442368 | tf_op jit(solution)/shard_map/all_to_all | solution.py:673
  50.1 4.3 %cache_by_head.3 = (bf16[20,256,128]{2,1,0:T(8,128)(2,1)}, bf16[20,256,128]{2,1,0:T(8,128)(2,1)}) custom-call(bf16[256,40,2,128]{3,2,1,0:T(2,128)(2,1)} %bitcast.73), custom_call_target="tpu_custom_call" | custom-call | bytes 12000000 | tf_op jit(solution)/shard_map/cache_by_head/pallas_call | solution.py:286
  54.4 0.1 add.47
  54.5 0.1 add.48
  54.6 0.1 and.12
  54.7 0.1 and.13
  54.9 0.1 add.50
  55.0 0.1 pad_maximum_fusion
  55.0 0.1 and_convert_fusion.live_ref
  55.1 4.4 %all-to-all-done.1.pieces_ref = bf16[16,9,3,2,128]{4,3,2,1,0:T(2,128)(2,1)S(1)} async-done(((bf16[16,9,3,2,128]{4,3,2,1,0:T(2,128)(2,1)}), bf16[16,9,3,2,128]{4,3,2,1,0:T(2,128)(2,1)S(1)}, u32[]{:S(2)}, u32[]{:S(2)}) %all-to-all-start.1) | async-done | bytes 221216 | tf_op jit(solution)/shard_map/all_to_all | solution.py:673
  59.5 7.0 %attention.1 = bf16[3,40,2,128]{3,2,1,0:T(2,128)(2,1)} custom-call(f32[8,128]{1,0:T(8,128)S(1)} %get-tuple-element.36.cos_ref, f32[8,128]{1,0:T(8,128)S(1)} %get-tuple-element.37.sin_ref, s32[2,256]{1,0:T(2,128)S(1)} %and_convert_fusion.live_ref, bf16[16,9,3,2,128]{4,3,2,1,0:T(2,128)(2,1)S(1)} %all-to-all-done.1.pieces_ref, ...), custom_call_target="tpu_custom_call" | custom-call | flops 1000000000 | bytes 6000000 | tf_op jit(solution)/shard_map/attention/pallas_call | solution.py:609
  (20 shorter events, 0.1 us)
Async XLA Ops:
  0.0 11.6 %collective-permute-start = (bf16[3,2,5120]{2,1,0:T(2,128)(2,1)}, bf16[3,2,5120]{2,1,0:T(2,128)(2,1)S(1)}, u32[]{:S(2)}, u32[]{:S(2)}) collective-permute-start(bf16[3,2,5120]{2,1,0:T(2,128)(2,1)} %param.9), channel_id=1, source_target_pairs={{0,4},{1,5},{2,6},{3,7},{4,0},{5,1},{6,2},{7,3},{8,12},{9,13},{10,... | collective-permute-start | bytes 184328 | tf_op jit(solution)/shard_map/ppermute | solution.py:233
  3.0 8.6 %collective-permute-start.1 = (bf16[3,2,5120]{2,1,0:T(2,128)(2,1)}, bf16[3,2,5120]{2,1,0:T(2,128)(2,1)S(1)}, u32[]{:S(2)}, u32[]{:S(2)}) collective-permute-start(bf16[3,2,5120]{2,1,0:T(2,128)(2,1)} %param.9), channel_id=1, source_target_pairs={{0,8},{1,9},{2,10},{3,11},{4,12},{5,13},{6,14},{7,15},{8,0},{9,1},... | collective-permute-start | bytes 184328 | tf_op jit(solution)/shard_map/ppermute | solution.py:233
  5.6 6.2 %collective-permute-start.2 = (bf16[3,2,5120]{2,1,0:T(2,128)(2,1)}, bf16[3,2,5120]{2,1,0:T(2,128)(2,1)S(1)}, u32[]{:S(2)}, u32[]{:S(2)}) collective-permute-start(bf16[3,2,5120]{2,1,0:T(2,128)(2,1)} %param.9), channel_id=1, source_target_pairs={{0,12},{1,13},{2,14},{3,15},{4,8},{5,9},{6,10},{7,11},{8,4},{9,5},... | collective-permute-start | bytes 184328 | tf_op jit(solution)/shard_map/ppermute | solution.py:233
  7.3 4.5 %copy-start = (bf16[3,2,5120]{2,1,0:T(2,128)(2,1)S(1)}, bf16[3,2,5120]{2,1,0:T(2,128)(2,1)}, u32[]{:S(2)}) copy-start(bf16[3,2,5120]{2,1,0:T(2,128)(2,1)} %param.9) | copy-start | bytes 184324
  7.3 6.6 %copy-start.1 = (s32[2,32]{1,0:T(2,128)S(1)}, s32[2,32]{1,0:T(2,128)}, u32[]{:S(2)}) copy-start(s32[2,32]{1,0:T(2,128)} %param.16) | copy-start | bytes 772
  11.8 4.3 %collective-permute-start.4 = (bf16[3,2,5120]{2,1,0:T(2,128)(2,1)S(1)}, bf16[3,2,5120]{2,1,0:T(2,128)(2,1)S(1)}, u32[]{:S(2)}, u32[]{:S(2)}) collective-permute-start(bf16[3,2,5120]{2,1,0:T(2,128)(2,1)S(1)} %copy-done), channel_id=1, source_target_pairs={{0,2},{1,3},{2,0},{3,1},{4,6},{5,7},{6,4},{7,5},{8,10},{9,11},{10,... | collective-permute-start | bytes 184328 | tf_op jit(solution)/shard_map/ppermute | solution.py:233
  13.5 4.7 %collective-permute-start.7 = (bf16[3,2,5120]{2,1,0:T(2,128)(2,1)S(1)}, bf16[3,2,5120]{2,1,0:T(2,128)(2,1)S(1)}, u32[]{:S(2)}, u32[]{:S(2)}) collective-permute-start(bf16[3,2,5120]{2,1,0:T(2,128)(2,1)S(1)} %collective-permute-done), channel_id=1, source_target_pairs={{0,2},{1,3},{2,0},{3,1},{4,6},{5,7},{6,4},{7,5},{8,10},{9,11},{10,... | collective-permute-start | bytes 184328 | tf_op jit(solution)/shard_map/ppermute | solution.py:233
  14.0 6.4 %collective-permute-start.6 = (bf16[3,2,5120]{2,1,0:T(2,128)(2,1)S(1)}, bf16[3,2,5120]{2,1,0:T(2,128)(2,1)S(1)}, u32[]{:S(2)}, u32[]{:S(2)}) collective-permute-start(bf16[3,2,5120]{2,1,0:T(2,128)(2,1)S(1)} %collective-permute-done), channel_id=1, source_target_pairs={{0,1},{1,0},{2,3},{3,2},{4,5},{5,4},{6,7},{7,6},{8,9},{9,8},{10,11... | collective-permute-start | bytes 184328 | tf_op jit(solution)/shard_map/ppermute | solution.py:233
  14.1 5.0 %collective-permute-start.10 = (bf16[3,2,5120]{2,1,0:T(2,128)(2,1)S(1)}, bf16[3,2,5120]{2,1,0:T(2,128)(2,1)S(1)}, u32[]{:S(2)}, u32[]{:S(2)}) collective-permute-start(bf16[3,2,5120]{2,1,0:T(2,128)(2,1)S(1)} %collective-permute-done.1), channel_id=1, source_target_pairs={{0,2},{1,3},{2,0},{3,1},{4,6},{5,7},{6,4},{7,5},{8,10},{9,11},{10,... | collective-permute-start | bytes 184328 | tf_op jit(solution)/shard_map/ppermute | solution.py:233
  15.7 5.2 %collective-permute-start.9 = (bf16[3,2,5120]{2,1,0:T(2,128)(2,1)S(1)}, bf16[3,2,5120]{2,1,0:T(2,128)(2,1)S(1)}, u32[]{:S(2)}, u32[]{:S(2)}) collective-permute-start(bf16[3,2,5120]{2,1,0:T(2,128)(2,1)S(1)} %collective-permute-done.1), channel_id=1, source_target_pairs={{0,1},{1,0},{2,3},{3,2},{4,5},{5,4},{6,7},{7,6},{8,9},{9,8},{10,11... | collective-permute-start | bytes 184328 | tf_op jit(solution)/shard_map/ppermute | solution.py:233
  16.1 4.2 %collective-permute-start.13 = (bf16[3,2,5120]{2,1,0:T(2,128)(2,1)S(1)}, bf16[3,2,5120]{2,1,0:T(2,128)(2,1)S(1)}, u32[]{:S(2)}, u32[]{:S(2)}) collective-permute-start(bf16[3,2,5120]{2,1,0:T(2,128)(2,1)S(1)} %collective-permute-done.2), channel_id=1, source_target_pairs={{0,2},{1,3},{2,0},{3,1},{4,6},{5,7},{6,4},{7,5},{8,10},{9,11},{10,... | collective-permute-start | bytes 184328 | tf_op jit(solution)/shard_map/ppermute | solution.py:233
  18.2 2.8 %collective-permute-start.12 = (bf16[3,2,5120]{2,1,0:T(2,128)(2,1)S(1)}, bf16[3,2,5120]{2,1,0:T(2,128)(2,1)S(1)}, u32[]{:S(2)}, u32[]{:S(2)}) collective-permute-start(bf16[3,2,5120]{2,1,0:T(2,128)(2,1)S(1)} %collective-permute-done.2), channel_id=1, source_target_pairs={{0,1},{1,0},{2,3},{3,2},{4,5},{5,4},{6,7},{7,6},{8,9},{9,8},{10,11... | collective-permute-start | bytes 184328 | tf_op jit(solution)/shard_map/ppermute | solution.py:233
  19.1 2.3 %collective-permute-start.3 = (bf16[3,2,5120]{2,1,0:T(2,128)(2,1)S(1)}, bf16[3,2,5120]{2,1,0:T(2,128)(2,1)S(1)}, u32[]{:S(2)}, u32[]{:S(2)}) collective-permute-start(bf16[3,2,5120]{2,1,0:T(2,128)(2,1)S(1)} %copy-done), channel_id=1, source_target_pairs={{0,1},{1,0},{2,3},{3,2},{4,5},{5,4},{6,7},{7,6},{8,9},{9,8},{10,11... | collective-permute-start | bytes 184328 | tf_op jit(solution)/shard_map/ppermute | solution.py:233
  20.4 1.2 %collective-permute-start.5 = (bf16[3,2,5120]{2,1,0:T(2,128)(2,1)S(1)}, bf16[3,2,5120]{2,1,0:T(2,128)(2,1)S(1)}, u32[]{:S(2)}, u32[]{:S(2)}) collective-permute-start(bf16[3,2,5120]{2,1,0:T(2,128)(2,1)S(1)} %collective-permute-done.4), channel_id=1, source_target_pairs={{0,1},{1,0},{2,3},{3,2},{4,5},{5,4},{6,7},{7,6},{8,9},{9,8},{10,11... | collective-permute-start | bytes 184328 | tf_op jit(solution)/shard_map/ppermute | solution.py:233
  20.4 1.4 %collective-permute-start.8 = (bf16[3,2,5120]{2,1,0:T(2,128)(2,1)S(1)}, bf16[3,2,5120]{2,1,0:T(2,128)(2,1)S(1)}, u32[]{:S(2)}, u32[]{:S(2)}) collective-permute-start(bf16[3,2,5120]{2,1,0:T(2,128)(2,1)S(1)} %collective-permute-done.7), channel_id=1, source_target_pairs={{0,1},{1,0},{2,3},{3,2},{4,5},{5,4},{6,7},{7,6},{8,9},{9,8},{10,11... | collective-permute-start | bytes 184328 | tf_op jit(solution)/shard_map/ppermute | solution.py:233
  20.9 1.2 %collective-permute-start.11 = (bf16[3,2,5120]{2,1,0:T(2,128)(2,1)S(1)}, bf16[3,2,5120]{2,1,0:T(2,128)(2,1)S(1)}, u32[]{:S(2)}, u32[]{:S(2)}) collective-permute-start(bf16[3,2,5120]{2,1,0:T(2,128)(2,1)S(1)} %collective-permute-done.10), channel_id=1, source_target_pairs={{0,1},{1,0},{2,3},{3,2},{4,5},{5,4},{6,7},{7,6},{8,9},{9,8},{10,11... | collective-permute-start | bytes 184328 | tf_op jit(solution)/shard_map/ppermute | solution.py:233
  21.0 1.3 %collective-permute-start.14 = (bf16[3,2,5120]{2,1,0:T(2,128)(2,1)S(1)}, bf16[3,2,5120]{2,1,0:T(2,128)(2,1)S(1)}, u32[]{:S(2)}, u32[]{:S(2)}) collective-permute-start(bf16[3,2,5120]{2,1,0:T(2,128)(2,1)S(1)} %collective-permute-done.13), channel_id=1, source_target_pairs={{0,1},{1,0},{2,3},{3,2},{4,5},{5,4},{6,7},{7,6},{8,9},{9,8},{10,11... | collective-permute-start | bytes 184328 | tf_op jit(solution)/shard_map/ppermute | solution.py:233
  26.4 15.0 %all-to-all-start = ((bf16[16,48,128]{2,1,0:T(8,128)(2,1)}), bf16[16,48,128]{2,1,0:T(8,128)(2,1)S(1)}, u32[]{:S(2)}, u32[]{:S(2)}) async-start(bf16[16,48,128]{2,1,0:T(8,128)(2,1)} %get-tuple-element.25), calls=%async_computation | async-start | bytes 393216 | tf_op jit(solution)/shard_map/all_to_all | solution.py:670
  44.5 15.0 %all-to-all-start.1 = ((bf16[16,9,3,2,128]{4,3,2,1,0:T(2,128)(2,1)}), bf16[16,9,3,2,128]{4,3,2,1,0:T(2,128)(2,1)S(1)}, u32[]{:S(2)}, u32[]{:S(2)}) async-start(bf16[16,9,3,2,128]{4,3,2,1,0:T(2,128)(2,1)} %update_values.1), calls=%async_computation.1 | async-start | bytes 442368 | tf_op jit(solution)/shard_map/all_to_all | solution.py:673

commit v5 on v4

--- a/solution.py
+++ b/solution.py
@@ -235,6 +235,7 @@
 
 CONTRACT_LANES = (((1,), (1,)), ((), ()))
 SPLIT_BUFFERS = 4
+FETCH_AHEAD = 2
 
 
 def in_hbm(x):
@@ -258,10 +259,17 @@
         copy.wait()
 
 
-def cache_kernel(first, pool_ref, keys_ref, values_ref, raw, wide, keys, values, sem, out_sem):
+def cache_kernel(first, extra, pool_ref, *refs):
+    sources, refs = refs[:extra], refs[extra:]
+    keys_ref, values_ref = refs[:2]
+    places = refs[2 : 2 + extra]
+    raw, wide, keys, values, sem, out_sem, place_sem = refs[2 + extra :]
     heads, tokens = raw.shape[:2]
     copies = start_all(
         [pltpu.make_async_copy(pool_ref.at[:, first + h], raw.at[h], sem.at[h]) for h in range(heads)]
+    )
+    brought = start_all(
+        [pltpu.make_async_copy(a, b, place_sem.at[i]) for i, (a, b) in enumerate(zip(sources, places))]
     )
     rows = raw.reshape(heads, 2 * tokens, HD)
     sent = []
@@ -278,16 +286,17 @@
             ]
         )
     wait_all(sent)
-
-
-def cache_by_head(pool, first, heads):
+    wait_all(brought)
+
+
+def cache_by_head(pool, first, heads, bring=()):
     tokens = pool.shape[0]
     part = pltpu.HBM((heads, tokens, HD), pool.dtype)
     return pl.pallas_call(
-        functools.partial(cache_kernel, first),
-        out_shape=(part, part),
-        in_specs=[HBM],
-        out_specs=(HBM, HBM),
+        functools.partial(cache_kernel, first, len(bring)),
+        out_shape=(part, part) + tuple(pltpu.VMEM(x.shape, x.dtype) for x in bring),
+        in_specs=[HBM] + [HBM] * len(bring),
+        out_specs=(HBM, HBM) + (VMEM,) * len(bring),
         scratch_shapes=[
             pltpu.VMEM((heads, tokens, 2, HD), pool.dtype),
             pltpu.VMEM((SPLIT_BUFFERS, 2 * tokens, HD), jnp.float32),
@@ -295,11 +304,12 @@
             pltpu.VMEM((heads, tokens, HD), pool.dtype),
             pltpu.SemaphoreType.DMA((heads,)),
             pltpu.SemaphoreType.DMA((2, heads)),
+            pltpu.SemaphoreType.DMA((max(len(bring), 1),)),
         ],
-        compiler_params=pltpu.CompilerParams(vmem_limit_bytes=16 * 2**20),
+        compiler_params=pltpu.CompilerParams(vmem_limit_bytes=(12 + 24 * bool(bring)) * 2**20),
         cost_estimate=pl.CostEstimate(flops=0, bytes_accessed=12 * 10**6, transcendentals=0),
         name="cache_by_head",
-    )(pool)
+    )(in_hbm(pool), *[in_hbm(x) for x in bring])
 
 
 def lanes_of(x):
@@ -307,24 +317,22 @@
 
 
 def low_kernel(count, me_ref, slot_ref, down_ref, *refs):
-    blocks, (x_ref, low_ref, x_buf, maps, made_ref, sem, low_sem, own_sem) = refs[:count], refs[count:]
+    blocks, (x_ref, low_ref, maps, sem, own_sem) = refs[:count], refs[count:]
     me = me_ref[0]
     steps = blocks[0].shape[0]
     holders, rank, width = down_ref.shape
-    fetch = pltpu.make_async_copy(down_ref, maps, own_sem.at[0])
+    fetch = pltpu.make_async_copy(down_ref, maps, own_sem)
     fetch.start()
     copies = []
     for k, block in enumerate(blocks):
         for t in range(steps):
             copies.append(
-                pltpu.make_async_copy(block.at[t], x_buf.at[:, (me ^ k) * steps + t], sem.at[k * steps + t])
+                pltpu.make_async_copy(block.at[t], x_ref.at[:, (me ^ k) * steps + t], sem.at[k * steps + t])
             )
     wait_all(start_all(copies))
-    keep = pltpu.make_async_copy(x_buf, x_ref, own_sem.at[1])
-    keep.start()
-    chunks, pairs = x_buf.shape[:2]
+    chunks, pairs = x_ref.shape[:2]
     rows = 2 * pairs
-    x = lanes_of(x_buf.reshape(chunks, rows, HD))
+    x = lanes_of(x_ref.reshape(chunks, rows, HD))
     fetch.wait()
     made = lax.dot_general(
         maps.reshape(holders * rank, width)[...], x, CONTRACT_LANES, preferred_element_type=jnp.float32
@@ -334,9 +342,7 @@
     for h in range(holders):
         low = low + jnp.where(slot == h, made[h * rank : (h + 1) * rank], 0.0)
     low = low.T
-    made_ref[...] = jnp.concatenate([low[: rows // 2], low[rows // 2 :]], axis=1).astype(made_ref.dtype)
-    wait_all(start_all([pltpu.make_async_copy(made_ref, low_ref.at[k], low_sem.at[k]) for k in range(count)]))
-    keep.wait()
+    low_ref[...] = jnp.concatenate([low[: rows // 2], low[rows // 2 :]], axis=1).astype(low_ref.dtype)
 
 
 def low_of(me, blocks, slot, down):
@@ -347,21 +353,18 @@
     return pl.pallas_call(
         functools.partial(low_kernel, count),
         out_shape=(
-            pltpu.HBM((chunks, rows // 2, 2, HD), jnp.bfloat16),
-            pltpu.HBM((count, rows // 2, 2 * rank), jnp.bfloat16),
+            jax.ShapeDtypeStruct((chunks, rows // 2, 2, HD), jnp.bfloat16),
+            jax.ShapeDtypeStruct((rows // 2, 2 * rank), jnp.bfloat16),
         ),
         in_specs=[SMEM, VMEM, HBM] + [ANY] * count,
-        out_specs=(HBM, HBM),
+        out_specs=(VMEM, VMEM),
         scratch_shapes=[
-            pltpu.VMEM((chunks, rows // 2, 2, HD), jnp.bfloat16),
             pltpu.VMEM(down.shape, jnp.bfloat16),
-            pltpu.VMEM((rows // 2, 2 * rank), jnp.bfloat16),
             pltpu.SemaphoreType.DMA((count * steps,)),
-            pltpu.SemaphoreType.DMA((count,)),
-            pltpu.SemaphoreType.DMA((2,)),
+            pltpu.SemaphoreType.DMA,
         ],
-        compiler_params=pltpu.CompilerParams(vmem_limit_bytes=16 * 2**20),
-        cost_estimate=pl.CostEstimate(flops=10**8, bytes_accessed=4 * 10**6, transcendentals=0),
+        compiler_params=pltpu.CompilerParams(vmem_limit_bytes=8 * 2**20),
+        cost_estimate=pl.CostEstimate(flops=10**6, bytes_accessed=10**5, transcendentals=0),
         name="low_rows",
     )(me, slot, in_hbm(down), *blocks)
 
@@ -388,134 +391,102 @@
     )
 
 
-PROJECT_CHUNK = 1024
-
-
-def project_kernel(x_ref, w_ref, send_ref, base_ref, x_buf, w_buf, total, buf, base, x_sem, w_sem, sem, base_sem):
-    chunks, pairs = x_buf.shape[:2]
-    rows = 2 * pairs
-    columns, width = w_ref.shape[1:]
-    parts = width // PROJECT_CHUNK
-    per = PROJECT_CHUNK // HD
-    fetch_x = pltpu.make_async_copy(x_ref, x_buf, x_sem)
-    fetch_x.start()
-    fetches = start_all(
-        [
-            pltpu.make_async_copy(
-                w_ref.at[:, :, p * PROJECT_CHUNK : (p + 1) * PROJECT_CHUNK], w_buf.at[p], w_sem.at[p]
-            )
-            for p in range(parts)
-        ]
-    )
-    fetch_x.wait()
-    x_rows = x_buf.reshape(chunks, rows, HD)
-    for p in range(parts):
-        fetches[p].wait()
-        x = jnp.concatenate([x_rows[c] for c in range(p * per, (p + 1) * per)], axis=1)
-        for i in range(3):
-            made = lax.dot_general(w_buf[p, i], x, CONTRACT_LANES, preferred_element_type=jnp.float32)
-            total[i] = made if p == 0 else total[i] + made
+def rows_of(x_ref):
+    chunks, pairs = x_ref.shape[:2]
+    return lanes_of(x_ref.reshape(chunks, 2 * pairs, HD))
+
+
+def query_key_kernel(x_ref, w_ref, up_ref, send_ref, up_out, buf, sem, up_sem):
+    bring = pltpu.make_async_copy(up_ref, up_out, up_sem)
+    bring.start()
+    x = rows_of(x_ref)
     each = buf.shape[0] // 2
-    flat = buf.reshape(buf.shape[0], rows, HD)
+    flat = buf.reshape(buf.shape[0], x.shape[0], HD)
     for i in range(2):
-        put_chunks(flat, i * each, total[i].T)
-    sent = send_blocks(buf, send_ref, 0, sem)
-    base[...] = total[2].T
-    keep = pltpu.make_async_copy(base, base_ref, base_sem)
-    keep.start()
-    wait_all(sent)
-    keep.wait()
-
-
-def project(x, weight, count):
-    chunks, pairs = x.shape[:2]
-    columns, width = weight.shape[1:]
-    each = -(-columns // HD)
-    parts = width // PROJECT_CHUNK
+        put_chunks(
+            flat, i * each, lax.dot_general(w_ref[i], x, CONTRACT_LANES, preferred_element_type=jnp.float32).T
+        )
+    wait_all(send_blocks(buf, send_ref, 0, sem))
+    bring.wait()
+
+
+def project_query_key(x, weight, up, count):
+    pairs = x.shape[1]
+    each = -(-weight.shape[1] // HD)
     return pl.pallas_call(
-        project_kernel,
+        query_key_kernel,
         out_shape=(
             pltpu.HBM((count, 3 * each, pairs // count, 2, HD), jnp.bfloat16),
-            pltpu.HBM((2 * pairs, columns), jnp.float32),
+            pltpu.VMEM(up.shape, up.dtype),
         ),
-        in_specs=[HBM, HBM],
-        out_specs=(HBM, HBM),
+        in_specs=[VMEM, VMEM, HBM],
+        out_specs=(HBM, VMEM),
         scratch_shapes=[
-            pltpu.VMEM(x.shape, jnp.bfloat16),
-            pltpu.VMEM((parts, 3, columns, PROJECT_CHUNK), jnp.bfloat16),
-            pltpu.VMEM((3, columns, 2 * pairs), jnp.float32),
             pltpu.VMEM((2 * each, pairs, 2, HD), jnp.bfloat16),
-            pltpu.VMEM((2 * pairs, columns), jnp.float32),
-            pltpu.SemaphoreType.DMA,
-            pltpu.SemaphoreType.DMA((parts,)),
             pltpu.SemaphoreType.DMA((count,)),
             pltpu.SemaphoreType.DMA,
         ],
         compiler_params=pltpu.CompilerParams(vmem_limit_bytes=24 * 2**20),
-        cost_estimate=pl.CostEstimate(flops=10**9, bytes_accessed=11 * 10**6, transcendentals=0),
-        name="project",
-    )(in_hbm(x), in_hbm(weight))
-
-
-UPDATE_PARTS = 4
-
-
-def update_kernel(stored_ref, low_ref, base_ref, up_ref, send_in, send_ref, base, up, buf, base_sem, up_sem, sem):
-    count, half, packed = low_ref.shape
-    rank = packed // 2
-    rows = 2 * half
-    height = up_ref.shape[0] // UPDATE_PARTS
-    fetches = start_all(
-        [
-            pltpu.make_async_copy(up_ref.at[p * height : (p + 1) * height], up.at[p], up_sem.at[p])
-            for p in range(UPDATE_PARTS)
-        ]
-    )
-    fetch_base = pltpu.make_async_copy(base_ref, base, base_sem)
-    fetch_base.start()
-    low = low_ref[0].astype(jnp.float32)
-    for s in range(1, count):
-        low = low + low_ref[s].astype(jnp.float32)
+        cost_estimate=pl.CostEstimate(flops=10**9, bytes_accessed=8 * 10**6, transcendentals=0),
+        name="project_query_key",
+    )(x, weight, in_hbm(up))
+
+
+def value_kernel(x_ref, w_ref, base_ref):
+    base_ref[...] = lax.dot_general(
+        w_ref[2], rows_of(x_ref), CONTRACT_LANES, preferred_element_type=jnp.float32
+    ).T
+
+
+def project_value(x, weight):
+    return pl.pallas_call(
+        value_kernel,
+        out_shape=jax.ShapeDtypeStruct((2 * x.shape[1], weight.shape[1]), jnp.float32),
+        in_specs=[VMEM, VMEM],
+        out_specs=VMEM,
+        compiler_params=pltpu.CompilerParams(vmem_limit_bytes=16 * 2**20),
+        cost_estimate=pl.CostEstimate(flops=5 * 10**8, bytes_accessed=4 * 10**6, transcendentals=0),
+        name="project_value",
+    )(x, weight)
+
+
+def update_kernel(stored_ref, base_ref, up_ref, send_in, *refs):
+    lows, (send_ref, buf, sem) = refs[:-3], refs[-3:]
+    rank = lows[0].shape[1] // 2
+    rows = 2 * lows[0].shape[0]
+    low = lows[0][...].astype(jnp.float32)
+    for more in lows[1:]:
+        low = low + more[...].astype(jnp.float32)
     low = jnp.concatenate([low[:, :rank], low[:, rank:]], axis=0)
     batch = 256 // rank
     spread = jnp.concatenate([low] * batch, axis=1)
     which = lax.broadcasted_iota(jnp.int32, (rows, batch * rank), 1) // rank
     ahead = stored_ref[...] - which
-    total = jnp.zeros(base.shape, jnp.float32)
-    for p in range(UPDATE_PARTS):
-        fetches[p].wait()
-        for a in range(0, height // rank, batch):
-            wide = jnp.where(ahead == p * (height // rank) + a, spread, 0.0).astype(jnp.bfloat16)
-            total = total + jnp.dot(
-                wide, up[p, a * rank : (a + batch) * rank], preferred_element_type=jnp.float32
-            )
-    fetch_base.wait()
-    put_chunks(buf.reshape(buf.shape[0], rows, HD), 0, base[...] + adapter_scale * total)
+    total = jnp.zeros(base_ref.shape, jnp.float32)
+    for a in range(0, up_ref.shape[0] // rank, batch):
+        wide = jnp.where(ahead == a, spread, 0.0).astype(jnp.bfloat16)
+        total = total + jnp.dot(wide, up_ref[a * rank : (a + batch) * rank], preferred_element_type=jnp.float32)
+    put_chunks(buf.reshape(buf.shape[0], rows, HD), 0, base_ref[...] + adapter_scale * total)
     wait_all(send_blocks(buf, send_ref, send_ref.shape[1] - buf.shape[0], sem))
 
 
-def update_values(stored, lows, base, up, send):
+def update_values(stored, base, up, send, lows):
     count, chunks = send.shape[:2]
-    rows, columns = base.shape
-    height = up.shape[0] // UPDATE_PARTS
+    rows = base.shape[0]
     return pl.pallas_call(
         update_kernel,
         out_shape=pltpu.HBM(send.shape, send.dtype),
-        in_specs=[VMEM, VMEM, HBM, HBM, HBM],
+        in_specs=[VMEM, VMEM, VMEM, HBM] + [VMEM] * len(lows),
         out_specs=HBM,
         scratch_shapes=[
-            pltpu.VMEM(base.shape, jnp.float32),
-            pltpu.VMEM((UPDATE_PARTS, height, columns), jnp.bfloat16),
             pltpu.VMEM((chunks // 3, rows // 2, 2, HD), jnp.bfloat16),
-            pltpu.SemaphoreType.DMA,
-            pltpu.SemaphoreType.DMA((UPDATE_PARTS,)),
             pltpu.SemaphoreType.DMA((count,)),
         ],
-        input_output_aliases={4: 0},
-        compiler_params=pltpu.CompilerParams(vmem_limit_bytes=16 * 2**20),
+        input_output_aliases={3: 0},
+        compiler_params=pltpu.CompilerParams(vmem_limit_bytes=8 * 2**20),
         cost_estimate=pl.CostEstimate(flops=3 * 10**8, bytes_accessed=4 * 10**6, transcendentals=0),
         name="update_values",
-    )(stored, lows, in_hbm(base), in_hbm(up), in_hbm(send))
+    )(stored, base, up, in_hbm(send), *lows)
 
 
 def attend_kernel(halves, cos_ref, sin_ref, live_ref, pieces_ref, *refs):
@@ -533,13 +504,13 @@
         half, at = divmod(chip, chips // halves)
         span = slice(at * heads, (at + 1) * heads)
         fetches.append(
-            start_all(
-                [
-                    pltpu.make_async_copy(key_refs[half].at[span], keys_buf.at[chip], sem.at[0, chip]),
-                    pltpu.make_async_copy(value_refs[half].at[span], values_buf.at[chip], sem.at[1, chip]),
-                ]
-            )
+            [
+                pltpu.make_async_copy(key_refs[half].at[span], keys_buf.at[chip], sem.at[0, chip]),
+                pltpu.make_async_copy(value_refs[half].at[span], values_buf.at[chip], sem.at[1, chip]),
+            ]
         )
+    for chip in range(FETCH_AHEAD):
+        start_all(fetches[chip])
     cosine = cos_ref[...][:rows]
     sine = sin_ref[...][:rows]
     left = lax.broadcasted_iota(jnp.int32, (rows, HD), 1) < HD // 2
@@ -581,6 +552,8 @@
         )
         spread = jnp.where(own_head, spread, 0.0).astype(jnp.bfloat16)
         wait_all(fetches[chip])
+        if chip + FETCH_AHEAD < chips:
+            start_all(fetches[chip + FETCH_AHEAD])
         keys = lanes_of(keys_buf[chip])
         values = lanes_of(values_buf[chip])
         scores = lax.dot_general(spread, keys, CONTRACT_LANES, preferred_element_type=jnp.float32) * (HD**-0.5)
@@ -640,13 +613,14 @@
     adapter_count = adapter_storage_row.shape[0]
 
     tokens = pool_pages * page_len
-    pool = in_hbm(key_value_pool.reshape(tokens, 2, heads, HD).transpose(0, 2, 1, 3))
-    first_half = cache_by_head(pool, 0, heads // 2)
+    pool = key_value_pool.reshape(tokens, 2, heads, HD).transpose(0, 2, 1, 3)
+    weight = query_key_value_weight.transpose(0, 2, 1)
+    *first_half, weight = cache_by_head(pool, 0, heads // 2, [weight])
     second_half = cache_by_head(pool, heads // 2, heads // 2)
 
     held = {0: hidden}
-    held.update({m: trade(hidden, m, count) for m in range(4, count, 4)})
-    held, first_half = lax.optimization_barrier((held, first_half))
+    held.update({m: trade(hidden, m, count) for m in range(count - 4, 0, -4)})
+    held[4], first_half, weight = lax.optimization_barrier((held[4], first_half, weight))
     for mask in (2, 1):
         held.update({k ^ mask: trade(v, mask, count) for k, v in list(held.items())})
     blocks = [
@@ -664,12 +638,19 @@
     )
     stored = jnp.broadcast_to(stored.reshape(count, 1, req_dev), (count, steps, req_dev)).reshape(-1)
 
-    x, lows = low_of(
+    x, low = low_of(
         me.astype(jnp.int32).reshape(1), blocks, (stored - me * holder_count)[None, :], adapter_down_maps
     )
-    lows = lax.all_to_all(lows, "replica", split_axis=0, concat_axis=0, tiled=True)
-    send, base = project(x, query_key_value_weight.transpose(0, 2, 1), count)
-    send = update_values(stored[:, None], lows, base, adapter_up_maps.reshape(adapter_count * rank, -1), send)
+    arrived = trade(low, 1, count)
+    send, up = project_query_key(x, weight, adapter_up_maps.reshape(adapter_count * rank, -1), count)
+    arrived, send = lax.optimization_barrier((arrived, send))
+    low = low + arrived
+    arrived = trade(low, 2, count)
+    base = project_value(x, weight)
+    arrived, base = lax.optimization_barrier((arrived, base))
+    low = low + arrived
+    lows = [low] + [trade(low, m, count) for m in range(4, count, 4)]
+    send = update_values(stored[:, None], base, up, send, lows)
     pieces = lax.all_to_all(send, "replica", split_axis=0, concat_axis=0, tiled=True)
 
     my_lengths = lax.dynamic_slice_in_dim(lengths, me * req_dev, req_dev)

time: 67 us -> 73.8 us (1.10)
  local copies, waits for them, and re-layouts: 1.63 us -> 10.3 us
  waiting for transfers between devices: 8.61 us -> 14.4 us
  Pallas kernels: 31.1 us -> 26.7 us
  starting transfers between devices: 23.7 us -> 20.5 us
    unnamed x4 -> x8, local copies, waits for them, and re-layouts: 0.01 us -> 8.69 us
    ppermute x15 -> x20, waiting for transfers between devices: 3.82 us -> 10.2 us  [trade(): return lax.ppermute(value, 'replica', [(i, i ^ mask) for i in range(count)])]
    all_to_all x1 -> x0, starting transfers between devices: 5.97 us -> none  [chip_plan(): lax.all_to_all(lows, 'replica', split_axis=0, concat_axis=0, tiled=True)]
    ppermute x15 -> x20, starting transfers between devices: 12.1 us -> 16.8 us  [trade(): return lax.ppermute(value, 'replica', [(i, i ^ mask) for i in range(count)])]
    pallas_call x4 -> x5, Pallas kernels: 21 us -> 18.1 us  [the longest x2 10.8 us: cache_by_head(): pl.pallas_call(functools.partial(cache_kernel, first, len(bring)), out_sh...]
    all_to_all x1, starting transfers between devices: 5.66 us -> 3.72 us  [chip_plan(): lax.all_to_all(send, 'replica', split_axis=0, concat_axis=0, tiled=True)]
    pallas_call x1, Pallas kernels: 3.11 us -> 1.62 us  [update_values(): pl.pallas_call(update_kernel, out_shape=pltpu.HBM(send.shape, send.dtype)...]
  transfers between devices with their start and end apart: 17 -> 21, of which waited for: 11 -> 9; matrix products, arithmetic and copies ran while one was open for 4% -> 4% of each run, Pallas kernels for 25% -> 20%
where the time goes in v5:
time: 73.8 us; the launch traced here: 73.5 us
  Pallas kernels  26.7 us (36%)
  starting transfers between devices  20.5 us (28%)
  waiting for transfers between devices  14.4 us (20%)
  local copies, waits for them, and re-layouts  10.3 us (14%)
  other arithmetic  1.25 us (2%)
    ppermute x20, starting transfers between devices, trade(): return lax.ppermute(value, 'replica', [(i, i ^ mask) for i in range(count)])  16.8 us
    pallas_call x2, Pallas kernels, cache_by_head(): pl.pallas_call(functools.partial(cache_kernel, first, len(bring)), out_sh...  10.8 us
    ppermute x20, waiting for transfers between devices, trade(): return lax.ppermute(value, 'replica', [(i, i ^ mask) for i in range(count)])  10.2 us
    unnamed x8, local copies, waits for them, and re-layouts  8.69 us
    pallas_call x1, Pallas kernels, attend(): pl.pallas_call(functools.partial(attend_kernel, halves), out_shape=jax.Sh...  7.02 us
    all_to_all x1, waiting for transfers between devices, chip_plan(): lax.all_to_all(send, 'replica', split_axis=0, concat_axis=0, tiled=True)  4.16 us
    all_to_all x1, starting transfers between devices, chip_plan(): lax.all_to_all(send, 'replica', split_axis=0, concat_axis=0, tiled=True)  3.72 us
    pallas_call x1, Pallas kernels, low_of(): pl.pallas_call(functools.partial(low_kernel, count), out_shape=(jax.Shape...  3.22 us
  transfers between devices with their start and end apart: 21, of which 9 were waited for; matrix products, arithmetic and copies ran while one was open for 4% of the time, Pallas kernels for 20%

profile of v5, /device:TPU:0, one launch (start us, length us, event | category | flops | bytes accessed | tf_op | source)
XLA Modules:
  0.0 73.5 jit_solution(12665205087184647666)
XLA Ops:
  0.0 3.0 %collective-permute-start.3 = (bf16[3,2,5120]{2,1,0:T(2,128)(2,1)}, bf16[3,2,5120]{2,1,0:T(2,128)(2,1)S(1)}, u32[]{:S(2)}, u32[]{:S(2)}) collective-permute-start(bf16[3,2,5120]{2,1,0:T(2,128)(2,1)} %param.9), channel_id=1, source_target_pairs={{0,4},{1,5},{2,6},{3,7},{4,0},{5,1},{6,2},{7,3},{8,12},{9,13},{10,... | collective-permute-start | bytes 184328 | tf_op jit(solution)/shard_map/ppermute | solution.py:233
  3.0 2.6 %collective-permute-start.7 = (bf16[3,2,5120]{2,1,0:T(2,128)(2,1)}, bf16[3,2,5120]{2,1,0:T(2,128)(2,1)S(1)}, u32[]{:S(2)}, u32[]{:S(2)}) collective-permute-start(bf16[3,2,5120]{2,1,0:T(2,128)(2,1)} %param.9), channel_id=1, source_target_pairs={{0,8},{1,9},{2,10},{3,11},{4,12},{5,13},{6,14},{7,15},{8,0},{9,1},... | collective-permute-start | bytes 184328 | tf_op jit(solution)/shard_map/ppermute | solution.py:233
  5.6 1.7 %collective-permute-start.1 = (bf16[3,2,5120]{2,1,0:T(2,128)(2,1)}, bf16[3,2,5120]{2,1,0:T(2,128)(2,1)S(1)}, u32[]{:S(2)}, u32[]{:S(2)}) collective-permute-start(bf16[3,2,5120]{2,1,0:T(2,128)(2,1)} %param.9), channel_id=1, source_target_pairs={{0,2},{1,3},{2,0},{3,1},{4,6},{5,7},{6,4},{7,5},{8,10},{9,11},{10,... | collective-permute-start | bytes 184328 | tf_op jit(solution)/shard_map/ppermute | solution.py:233
  7.4 0.9 %select_reduce_fusion.1 = s32[32]{0:T(128)S(1)} fusion(s32[64]{0:T(128)} %param.13, s32[32]{0:T(128)} %param.14), kind=kLoop, calls=%fused_computation.2 | loop fusion | flops 6112 | bytes 512 | tf_op jit(solution)/shard_map/reduce_sum | solution.py:631
  8.2 0.1 broadcast_in_dim.52
  8.3 0.7 %dynamic_slice.3 = s32[2]{0:T(128)S(1)} dynamic-slice(s32[32]{0:T(128)} %param.15, s32[]{:T(128)S(6)} %select_n.11), dynamic_slice_sizes={2} | dynamic-slice | bytes 20 | tf_op jit(solution)/shard_map/dynamic_slice | solution.py:656
  9.1 0.1 add.52
  9.1 6.5 %cache_by_head.2 = (bf16[20,256,128]{2,1,0:T(8,128)(2,1)}, bf16[20,256,128]{2,1,0:T(8,128)(2,1)}, bf16[3,320,5120]{2,1,0:T(8,128)(2,1)S(1)}) custom-call(bf16[256,40,2,128]{3,2,1,0:T(2,128)(2,1)} %bitcast.72, bf16[3,320,5120]{2,1,0:T(8,128)(2,1)} %bitcast.74), custom_call_target="tpu_custom_call" | custom-call | bytes 12000000 | tf_op jit(solution)/shard_map/cache_by_head/pallas_call | solution.py:295
  15.7 3.8 %copy-done = bf16[3,320,5120]{2,1,0:T(8,128)(2,1)} copy-done((bf16[3,320,5120]{2,1,0:T(8,128)(2,1)}, bf16[3,320,5120]{2,1,0:T(8,128)(2,1)S(1)}, u32[]{:S(2)}) %copy-start) | copy-done | bytes 9830424
  19.5 0.4 collective-permute-start.5
  19.8 0.3 collective-permute-start.4
  20.1 1.7 %collective-permute-start.9 = (bf16[3,2,5120]{2,1,0:T(2,128)(2,1)S(1)}, bf16[3,2,5120]{2,1,0:T(2,128)(2,1)S(1)}, u32[]{:S(2)}, u32[]{:S(2)}) collective-permute-start(bf16[3,2,5120]{2,1,0:T(2,128)(2,1)S(1)} %collective-permute-done.7), channel_id=1, source_target_pairs={{0,2},{1,3},{2,0},{3,1},{4,6},{5,7},{6,4},{7,5},{8,10},{9,11},{10,... | collective-permute-start | bytes 184328 | tf_op jit(solution)/shard_map/ppermute | solution.py:233
  21.8 0.4 collective-permute-start.13
  22.2 0.1 fusion
  22.4 0.1 sub.19.slot_ref
  22.5 1.8 %collective-permute-done.5 = bf16[3,2,5120]{2,1,0:T(2,128)(2,1)S(1)} collective-permute-done((bf16[3,2,5120]{2,1,0:T(2,128)(2,1)S(1)}, bf16[3,2,5120]{2,1,0:T(2,128)(2,1)S(1)}, u32[]{:S(2)}, u32[]{:S(2)}) %collective-permute-start.5) | collective-permute-done | bytes 61472 | tf_op jit(solution)/shard_map/ppermute | solution.py:233
  24.3 0.5 collective-permute-start.2
  24.9 0.7 collective-permute-done.9
  25.6 1.0 %collective-permute-done.13 = bf16[3,2,5120]{2,1,0:T(2,128)(2,1)S(1)} collective-permute-done((bf16[3,2,5120]{2,1,0:T(2,128)(2,1)S(1)}, bf16[3,2,5120]{2,1,0:T(2,128)(2,1)S(1)}, u32[]{:S(2)}, u32[]{:S(2)}) %collective-permute-start.13) | collective-permute-done | bytes 61472 | tf_op jit(solution)/shard_map/ppermute | solution.py:233
  26.6 0.5 collective-permute-start.14
  27.1 0.1 select_reduce_fusion
  27.2 0.6 collective-permute-done.10
  27.8 0.2 collective-permute-done.14
  28.0 3.2 %low_rows.1 = (bf16[40,48,2,128]{3,2,1,0:T(2,128)(2,1)S(1)}, bf16[48,128]{1,0:T(8,128)(2,1)S(1)}) custom-call(s32[1]{0:T(128)} %bitcast.me_ref, s32[1,96]{1,0:T(1,128)S(1)} %sub.19.slot_ref, bf16[4,64,5120]{2,1,0:T(8,128)(2,1)} %down_ref.1, bf16[3,40,2,128]{3,2,1,0:T(2,128)(2,1)} %bitcast.76, bf16[3,40,2,128]{3,2,1,0:T(2,128)(2,1)S(1)} %bitcast.61, ...), custom_call_target="tpu_custom_call" | custom-call | flops 1000000 | bytes 100000 | tf_op jit(solution)/shard_map/low_rows/pallas_call | solution.py:353
  31.2 0.4 collective-permute-start.15
  31.6 3.8 %copy-done.1 = bf16[3,320,5120]{2,1,0:T(8,128)(2,1)S(1)} copy-done((bf16[3,320,5120]{2,1,0:T(8,128)(2,1)S(1)}, bf16[3,320,5120]{2,1,0:T(8,128)(2,1)}, u32[]{:S(2)}) %copy-start.1) | copy-done | bytes 9830424
  35.4 2.9 %project_query_key.1 = (bf16[16,9,3,2,128]{4,3,2,1,0:T(2,128)(2,1)}, bf16[4096,320]{1,0:T(8,128)(2,1)S(1)}) custom-call(bf16[40,48,2,128]{3,2,1,0:T(2,128)(2,1)S(1)} %get-tuple-element.27.x_ref, bf16[3,320,5120]{2,1,0:T(8,128)(2,1)S(1)} %copy-done.1, bf16[4096,320]{1,0:T(8,128)(2,1)} %bitcast.75), custom_call_target="tpu_custom_call" | custom-call | flops 1000000000 | bytes 8000000 | tf_op jit(solution)/shard_map/project_query_key/pallas_call | solution.py:416
  38.3 0.8 %collective-permute-start.16 = (bf16[48,128]{1,0:T(8,128)(2,1)S(1)}, bf16[48,128]{1,0:T(8,128)(2,1)S(1)}, u32[]{:S(2)}, u32[]{:S(2)}) collective-permute-start(bf16[48,128]{1,0:T(8,128)(2,1)S(1)} %add.59), channel_id=1, source_target_pairs={{0,2},{1,3},{2,0},{3,1},{4,6},{5,7},{6,4},{7,5},{8,10},{9,11},{10,... | collective-permute-start | bytes 36872 | tf_op jit(solution)/shard_map/ppermute | solution.py:233
  39.1 1.1 %copy-done.2 = bf16[3,320,5120]{2,1,0:T(8,128)(2,1)S(1)} copy-done((bf16[3,320,5120]{2,1,0:T(8,128)(2,1)S(1)}, bf16[3,320,5120]{2,1,0:T(8,128)(2,1)}, u32[]{:S(2)}) %copy-start.2) | copy-done | bytes 9830424
  40.2 1.2 %project_value.1.base_ref = f32[96,320]{1,0:T(8,128)S(1)} custom-call(bf16[40,48,2,128]{3,2,1,0:T(2,128)(2,1)S(1)} %get-tuple-element.27.x_ref, bf16[3,320,5120]{2,1,0:T(8,128)(2,1)S(1)} %copy-done.2), custom_call_target="tpu_custom_call" | custom-call | flops 500000000 | bytes 4000000 | tf_op jit(solution)/shard_map/project_value/pallas_call | solution.py:442
  41.4 0.7 collective-permute-done.16
  42.1 0.7 %collective-permute-start.17 = (bf16[48,128]{1,0:T(8,128)(2,1)S(1)}, bf16[48,128]{1,0:T(8,128)(2,1)S(1)}, u32[]{:S(2)}, u32[]{:S(2)}) collective-permute-start(bf16[48,128]{1,0:T(8,128)(2,1)S(1)} %add.60.refs_0_), channel_id=1, source_target_pairs={{0,4},{1,5},{2,6},{3,7},{4,0},{5,1},{6,2},{7,3},{8,12},{9,13},{10,... | collective-permute-start | bytes 36872 | tf_op jit(solution)/shard_map/ppermute | solution.py:233
  42.8 3.5 %collective-permute-start.18 = (bf16[48,128]{1,0:T(8,128)(2,1)S(1)}, bf16[48,128]{1,0:T(8,128)(2,1)S(1)}, u32[]{:S(2)}, u32[]{:S(2)}) collective-permute-start(bf16[48,128]{1,0:T(8,128)(2,1)S(1)} %add.60.refs_0_), channel_id=1, source_target_pairs={{0,8},{1,9},{2,10},{3,11},{4,12},{5,13},{6,14},{7,15},{8,0},{9,1},... | collective-permute-start | bytes 36872 | tf_op jit(solution)/shard_map/ppermute | solution.py:233
  46.3 0.2 collective-permute-start.19
  46.6 0.1 broadcast_in_dim_reshape.4.stored_ref
  46.6 1.3 %collective-permute-done.18.refs_2_ = bf16[48,128]{1,0:T(8,128)(2,1)S(1)} collective-permute-done((bf16[48,128]{1,0:T(8,128)(2,1)S(1)}, bf16[48,128]{1,0:T(8,128)(2,1)S(1)}, u32[]{:S(2)}, u32[]{:S(2)}) %collective-permute-start.18) | collective-permute-done | bytes 12320 | tf_op jit(solution)/shard_map/ppermute | solution.py:233
  48.0 3.8 %collective-permute-done.19.refs_3_ = bf16[48,128]{1,0:T(8,128)(2,1)S(1)} collective-permute-done((bf16[48,128]{1,0:T(8,128)(2,1)S(1)}, bf16[48,128]{1,0:T(8,128)(2,1)S(1)}, u32[]{:S(2)}, u32[]{:S(2)}) %collective-permute-start.19) | collective-permute-done | bytes 12320 | tf_op jit(solution)/shard_map/ppermute | solution.py:233
  51.8 1.6 %update_values.1 = bf16[16,9,3,2,128]{4,3,2,1,0:T(2,128)(2,1)} custom-call(s32[96,1]{1,0:T(8,128)S(1)} %broadcast_in_dim_reshape.4.stored_ref, f32[96,320]{1,0:T(8,128)S(1)} %project_value.1.base_ref, bf16[4096,320]{1,0:T(8,128)(2,1)S(1)} %get-tuple-element.32.up_ref, ...), custom_call_target="tpu_custom_call", output_to_operand_aliasing={{}: (3, {})} | custom-call | flops 300000000 | bytes 4000000 | tf_op jit(solution)/shard_map/update_values/pallas_call | solution.py:476
  53.4 3.7 %all-to-all-start = ((bf16[16,9,3,2,128]{4,3,2,1,0:T(2,128)(2,1)}), bf16[16,9,3,2,128]{4,3,2,1,0:T(2,128)(2,1)S(1)}, u32[]{:S(2)}, u32[]{:S(2)}) async-start(bf16[16,9,3,2,128]{4,3,2,1,0:T(2,128)(2,1)} %update_values.1), calls=%async_computation | async-start | bytes 442368 | tf_op jit(solution)/shard_map/all_to_all | solution.py:654
  57.2 4.3 %cache_by_head.3 = (bf16[20,256,128]{2,1,0:T(8,128)(2,1)}, bf16[20,256,128]{2,1,0:T(8,128)(2,1)}) custom-call(bf16[256,40,2,128]{3,2,1,0:T(2,128)(2,1)} %bitcast.73), custom_call_target="tpu_custom_call" | custom-call | bytes 12000000 | tf_op jit(solution)/shard_map/cache_by_head/pallas_call | solution.py:295
  61.5 0.1 add.53
  61.6 0.1 add.54
  61.7 0.1 and.12
  61.8 0.1 and.13
  61.9 0.1 add.56
  62.0 0.1 pad_maximum_fusion
  62.2 4.2 %all-to-all-done.pieces_ref = bf16[16,9,3,2,128]{4,3,2,1,0:T(2,128)(2,1)S(1)} async-done(((bf16[16,9,3,2,128]{4,3,2,1,0:T(2,128)(2,1)}), bf16[16,9,3,2,128]{4,3,2,1,0:T(2,128)(2,1)S(1)}, u32[]{:S(2)}, u32[]{:S(2)}) %all-to-all-start) | async-done | bytes 221216 | tf_op jit(solution)/shard_map/all_to_all | solution.py:654
  66.3 7.0 %attention.1 = bf16[3,40,2,128]{3,2,1,0:T(2,128)(2,1)} custom-call(f32[8,128]{1,0:T(8,128)S(1)} %get-tuple-element.42.cos_ref, f32[8,128]{1,0:T(8,128)S(1)} %get-tuple-element.43.sin_ref, s32[2,256]{1,0:T(2,128)S(1)} %and_convert_fusion.live_ref, bf16[16,9,3,2,128]{4,3,2,1,0:T(2,128)(2,1)S(1)} %all-to-all-done.pieces_ref, ...), custom_call_target="tpu_custom_call" | custom-call | flops 1000000000 | bytes 6000000 | tf_op jit(solution)/shard_map/attention/pallas_call | solution.py:582
  (35 shorter events, 0.2 us)
Async XLA Ops:
  0.0 19.5 %collective-permute-start.3 = (bf16[3,2,5120]{2,1,0:T(2,128)(2,1)}, bf16[3,2,5120]{2,1,0:T(2,128)(2,1)S(1)}, u32[]{:S(2)}, u32[]{:S(2)}) collective-permute-start(bf16[3,2,5120]{2,1,0:T(2,128)(2,1)} %param.9), channel_id=1, source_target_pairs={{0,4},{1,5},{2,6},{3,7},{4,0},{5,1},{6,2},{7,3},{8,12},{9,13},{10,... | collective-permute-start | bytes 184328 | tf_op jit(solution)/shard_map/ppermute | solution.py:233
  3.0 16.8 %collective-permute-start.7 = (bf16[3,2,5120]{2,1,0:T(2,128)(2,1)}, bf16[3,2,5120]{2,1,0:T(2,128)(2,1)S(1)}, u32[]{:S(2)}, u32[]{:S(2)}) collective-permute-start(bf16[3,2,5120]{2,1,0:T(2,128)(2,1)} %param.9), channel_id=1, source_target_pairs={{0,8},{1,9},{2,10},{3,11},{4,12},{5,13},{6,14},{7,15},{8,0},{9,1},... | collective-permute-start | bytes 184328 | tf_op jit(solution)/shard_map/ppermute | solution.py:233
  5.6 14.5 %collective-permute-start.11 = (bf16[3,2,5120]{2,1,0:T(2,128)(2,1)}, bf16[3,2,5120]{2,1,0:T(2,128)(2,1)S(1)}, u32[]{:S(2)}, u32[]{:S(2)}) collective-permute-start(bf16[3,2,5120]{2,1,0:T(2,128)(2,1)} %param.9), channel_id=1, source_target_pairs={{0,12},{1,13},{2,14},{3,15},{4,8},{5,9},{6,10},{7,11},{8,4},{9,5},... | collective-permute-start | bytes 184328 | tf_op jit(solution)/shard_map/ppermute | solution.py:233
  5.6 16.2 %collective-permute-start.1 = (bf16[3,2,5120]{2,1,0:T(2,128)(2,1)}, bf16[3,2,5120]{2,1,0:T(2,128)(2,1)S(1)}, u32[]{:S(2)}, u32[]{:S(2)}) collective-permute-start(bf16[3,2,5120]{2,1,0:T(2,128)(2,1)} %param.9), channel_id=1, source_target_pairs={{0,2},{1,3},{2,0},{3,1},{4,6},{5,7},{6,4},{7,5},{8,10},{9,11},{10,... | collective-permute-start | bytes 184328 | tf_op jit(solution)/shard_map/ppermute | solution.py:233
  7.4 14.5 %collective-permute-start = (bf16[3,2,5120]{2,1,0:T(2,128)(2,1)}, bf16[3,2,5120]{2,1,0:T(2,128)(2,1)S(1)}, u32[]{:S(2)}, u32[]{:S(2)}) collective-permute-start(bf16[3,2,5120]{2,1,0:T(2,128)(2,1)} %param.9), channel_id=1, source_target_pairs={{0,1},{1,0},{2,3},{3,2},{4,5},{5,4},{6,7},{7,6},{8,9},{9,8},{10,11... | collective-permute-start | bytes 184328 | tf_op jit(solution)/shard_map/ppermute | solution.py:233
  9.1 18.0 %copy-start.3 = (s32[2,32]{1,0:T(2,128)S(1)}, s32[2,32]{1,0:T(2,128)}, u32[]{:S(2)}) copy-start(s32[2,32]{1,0:T(2,128)} %param.16) | copy-start | bytes 772
  15.7 3.8 %copy-start = (bf16[3,320,5120]{2,1,0:T(8,128)(2,1)}, bf16[3,320,5120]{2,1,0:T(8,128)(2,1)S(1)}, u32[]{:S(2)}) copy-start(bf16[3,320,5120]{2,1,0:T(8,128)(2,1)S(1)} %get-tuple-element.28.w_ref) | copy-start | bytes 29491204
  19.5 4.9 %collective-permute-start.5 = (bf16[3,2,5120]{2,1,0:T(2,128)(2,1)S(1)}, bf16[3,2,5120]{2,1,0:T(2,128)(2,1)S(1)}, u32[]{:S(2)}, u32[]{:S(2)}) collective-permute-start(bf16[3,2,5120]{2,1,0:T(2,128)(2,1)S(1)} %collective-permute-done.3), channel_id=1, source_target_pairs={{0,2},{1,3},{2,0},{3,1},{4,6},{5,7},{6,4},{7,5},{8,10},{9,11},{10,... | collective-permute-start | bytes 184328 | tf_op jit(solution)/shard_map/ppermute | solution.py:233
  19.8 4.5 %collective-permute-start.4 = (bf16[3,2,5120]{2,1,0:T(2,128)(2,1)S(1)}, bf16[3,2,5120]{2,1,0:T(2,128)(2,1)S(1)}, u32[]{:S(2)}, u32[]{:S(2)}) collective-permute-start(bf16[3,2,5120]{2,1,0:T(2,128)(2,1)S(1)} %collective-permute-done.3), channel_id=1, source_target_pairs={{0,1},{1,0},{2,3},{3,2},{4,5},{5,4},{6,7},{7,6},{8,9},{9,8},{10,11... | collective-permute-start | bytes 184328 | tf_op jit(solution)/shard_map/ppermute | solution.py:233
  20.1 5.4 %collective-permute-start.9 = (bf16[3,2,5120]{2,1,0:T(2,128)(2,1)S(1)}, bf16[3,2,5120]{2,1,0:T(2,128)(2,1)S(1)}, u32[]{:S(2)}, u32[]{:S(2)}) collective-permute-start(bf16[3,2,5120]{2,1,0:T(2,128)(2,1)S(1)} %collective-permute-done.7), channel_id=1, source_target_pairs={{0,2},{1,3},{2,0},{3,1},{4,6},{5,7},{6,4},{7,5},{8,10},{9,11},{10,... | collective-permute-start | bytes 184328 | tf_op jit(solution)/shard_map/ppermute | solution.py:233
  21.8 4.8 %collective-permute-start.8 = (bf16[3,2,5120]{2,1,0:T(2,128)(2,1)S(1)}, bf16[3,2,5120]{2,1,0:T(2,128)(2,1)S(1)}, u32[]{:S(2)}, u32[]{:S(2)}) collective-permute-start(bf16[3,2,5120]{2,1,0:T(2,128)(2,1)S(1)} %collective-permute-done.7), channel_id=1, source_target_pairs={{0,1},{1,0},{2,3},{3,2},{4,5},{5,4},{6,7},{7,6},{8,9},{9,8},{10,11... | collective-permute-start | bytes 184328 | tf_op jit(solution)/shard_map/ppermute | solution.py:233
  21.8 4.8 %collective-permute-start.13 = (bf16[3,2,5120]{2,1,0:T(2,128)(2,1)S(1)}, bf16[3,2,5120]{2,1,0:T(2,128)(2,1)S(1)}, u32[]{:S(2)}, u32[]{:S(2)}) collective-permute-start(bf16[3,2,5120]{2,1,0:T(2,128)(2,1)S(1)} %collective-permute-done.11), channel_id=1, source_target_pairs={{0,2},{1,3},{2,0},{3,1},{4,6},{5,7},{6,4},{7,5},{8,10},{9,11},{10,... | collective-permute-start | bytes 184328 | tf_op jit(solution)/shard_map/ppermute | solution.py:233
  24.3 2.9 %collective-permute-start.12 = (bf16[3,2,5120]{2,1,0:T(2,128)(2,1)S(1)}, bf16[3,2,5120]{2,1,0:T(2,128)(2,1)S(1)}, u32[]{:S(2)}, u32[]{:S(2)}) collective-permute-start(bf16[3,2,5120]{2,1,0:T(2,128)(2,1)S(1)} %collective-permute-done.11), channel_id=1, source_target_pairs={{0,1},{1,0},{2,3},{3,2},{4,5},{5,4},{6,7},{7,6},{8,9},{9,8},{10,11... | collective-permute-start | bytes 184328 | tf_op jit(solution)/shard_map/ppermute | solution.py:233
  24.3 2.9 %collective-permute-start.2 = (bf16[3,2,5120]{2,1,0:T(2,128)(2,1)S(1)}, bf16[3,2,5120]{2,1,0:T(2,128)(2,1)S(1)}, u32[]{:S(2)}, u32[]{:S(2)}) collective-permute-start(bf16[3,2,5120]{2,1,0:T(2,128)(2,1)S(1)} %collective-permute-done.1), channel_id=1, source_target_pairs={{0,1},{1,0},{2,3},{3,2},{4,5},{5,4},{6,7},{7,6},{8,9},{9,8},{10,11... | collective-permute-start | bytes 184328 | tf_op jit(solution)/shard_map/ppermute | solution.py:233
  25.6 1.7 %collective-permute-start.6 = (bf16[3,2,5120]{2,1,0:T(2,128)(2,1)S(1)}, bf16[3,2,5120]{2,1,0:T(2,128)(2,1)S(1)}, u32[]{:S(2)}, u32[]{:S(2)}) collective-permute-start(bf16[3,2,5120]{2,1,0:T(2,128)(2,1)S(1)} %collective-permute-done.5), channel_id=1, source_target_pairs={{0,1},{1,0},{2,3},{3,2},{4,5},{5,4},{6,7},{7,6},{8,9},{9,8},{10,11... | collective-permute-start | bytes 184328 | tf_op jit(solution)/shard_map/ppermute | solution.py:233
  26.6 1.2 %collective-permute-start.10 = (bf16[3,2,5120]{2,1,0:T(2,128)(2,1)S(1)}, bf16[3,2,5120]{2,1,0:T(2,128)(2,1)S(1)}, u32[]{:S(2)}, u32[]{:S(2)}) collective-permute-start(bf16[3,2,5120]{2,1,0:T(2,128)(2,1)S(1)} %collective-permute-done.9), channel_id=1, source_target_pairs={{0,1},{1,0},{2,3},{3,2},{4,5},{5,4},{6,7},{7,6},{8,9},{9,8},{10,11... | collective-permute-start | bytes 184328 | tf_op jit(solution)/shard_map/ppermute | solution.py:233
  26.6 1.4 %collective-permute-start.14 = (bf16[3,2,5120]{2,1,0:T(2,128)(2,1)S(1)}, bf16[3,2,5120]{2,1,0:T(2,128)(2,1)S(1)}, u32[]{:S(2)}, u32[]{:S(2)}) collective-permute-start(bf16[3,2,5120]{2,1,0:T(2,128)(2,1)S(1)} %collective-permute-done.13), channel_id=1, source_target_pairs={{0,1},{1,0},{2,3},{3,2},{4,5},{5,4},{6,7},{7,6},{8,9},{9,8},{10,11... | collective-permute-start | bytes 184328 | tf_op jit(solution)/shard_map/ppermute | solution.py:233
  31.2 7.1 %collective-permute-start.15 = (bf16[48,128]{1,0:T(8,128)(2,1)S(1)}, bf16[48,128]{1,0:T(8,128)(2,1)S(1)}, u32[]{:S(2)}, u32[]{:S(2)}) collective-permute-start(bf16[48,128]{1,0:T(8,128)(2,1)S(1)} %get-tuple-element.26), channel_id=1, source_target_pairs={{0,1},{1,0},{2,3},{3,2},{4,5},{5,4},{6,7},{7,6},{8,9},{9,8},{10,11... | collective-permute-start | bytes 36872 | tf_op jit(solution)/shard_map/ppermute | solution.py:233
  31.6 3.8 %copy-start.1 = (bf16[3,320,5120]{2,1,0:T(8,128)(2,1)S(1)}, bf16[3,320,5120]{2,1,0:T(8,128)(2,1)}, u32[]{:S(2)}) copy-start(bf16[3,320,5120]{2,1,0:T(8,128)(2,1)} %copy-done) | copy-start | bytes 29491204
  35.4 4.8 %copy-start.2 = (bf16[3,320,5120]{2,1,0:T(8,128)(2,1)S(1)}, bf16[3,320,5120]{2,1,0:T(8,128)(2,1)}, u32[]{:S(2)}) copy-start(bf16[3,320,5120]{2,1,0:T(8,128)(2,1)} %copy-done) | copy-start | bytes 29491204
  38.3 3.8 %collective-permute-start.16 = (bf16[48,128]{1,0:T(8,128)(2,1)S(1)}, bf16[48,128]{1,0:T(8,128)(2,1)S(1)}, u32[]{:S(2)}, u32[]{:S(2)}) collective-permute-start(bf16[48,128]{1,0:T(8,128)(2,1)S(1)} %add.59), channel_id=1, source_target_pairs={{0,2},{1,3},{2,0},{3,1},{4,6},{5,7},{6,4},{7,5},{8,10},{9,11},{10,... | collective-permute-start | bytes 36872 | tf_op jit(solution)/shard_map/ppermute | solution.py:233
  42.1 4.6 %collective-permute-start.17 = (bf16[48,128]{1,0:T(8,128)(2,1)S(1)}, bf16[48,128]{1,0:T(8,128)(2,1)S(1)}, u32[]{:S(2)}, u32[]{:S(2)}) collective-permute-start(bf16[48,128]{1,0:T(8,128)(2,1)S(1)} %add.60.refs_0_), channel_id=1, source_target_pairs={{0,4},{1,5},{2,6},{3,7},{4,0},{5,1},{6,2},{7,3},{8,12},{9,13},{10,... | collective-permute-start | bytes 36872 | tf_op jit(solution)/shard_map/ppermute | solution.py:233
  42.8 5.2 %collective-permute-start.18 = (bf16[48,128]{1,0:T(8,128)(2,1)S(1)}, bf16[48,128]{1,0:T(8,128)(2,1)S(1)}, u32[]{:S(2)}, u32[]{:S(2)}) collective-permute-start(bf16[48,128]{1,0:T(8,128)(2,1)S(1)} %add.60.refs_0_), channel_id=1, source_target_pairs={{0,8},{1,9},{2,10},{3,11},{4,12},{5,13},{6,14},{7,15},{8,0},{9,1},... | collective-permute-start | bytes 36872 | tf_op jit(solution)/shard_map/ppermute | solution.py:233
  46.3 5.5 %collective-permute-start.19 = (bf16[48,128]{1,0:T(8,128)(2,1)S(1)}, bf16[48,128]{1,0:T(8,128)(2,1)S(1)}, u32[]{:S(2)}, u32[]{:S(2)}) collective-permute-start(bf16[48,128]{1,0:T(8,128)(2,1)S(1)} %add.60.refs_0_), channel_id=1, source_target_pairs={{0,12},{1,13},{2,14},{3,15},{4,8},{5,9},{6,10},{7,11},{8,4},{9,5},... | collective-permute-start | bytes 36872 | tf_op jit(solution)/shard_map/ppermute | solution.py:233
  53.4 12.9 %all-to-all-start = ((bf16[16,9,3,2,128]{4,3,2,1,0:T(2,128)(2,1)}), bf16[16,9,3,2,128]{4,3,2,1,0:T(2,128)(2,1)S(1)}, u32[]{:S(2)}, u32[]{:S(2)}) async-start(bf16[16,9,3,2,128]{4,3,2,1,0:T(2,128)(2,1)} %update_values.1), calls=%async_computation | async-start | bytes 442368 | tf_op jit(solution)/shard_map/all_to_all | solution.py:654

commit v6 on v4

--- a/solution.py
+++ b/solution.py
@@ -234,7 +234,6 @@
 
 
 CONTRACT_LANES = (((1,), (1,)), ((), ()))
-SPLIT_BUFFERS = 4
 
 
 def in_hbm(x):
@@ -258,48 +257,52 @@
         copy.wait()
 
 
-def cache_kernel(first, pool_ref, keys_ref, values_ref, raw, wide, keys, values, sem, out_sem):
+CACHE_AHEAD = 16
+
+
+def cache_kernel(pool_ref, keys_ref, values_ref, raw, values, sem, out_sem):
     heads, tokens = raw.shape[:2]
-    copies = start_all(
-        [pltpu.make_async_copy(pool_ref.at[:, first + h], raw.at[h], sem.at[h]) for h in range(heads)]
-    )
+    copies = [pltpu.make_async_copy(pool_ref.at[:, h], raw.at[h], sem.at[h]) for h in range(heads)]
+    start_all(copies[:CACHE_AHEAD])
     rows = raw.reshape(heads, 2 * tokens, HD)
+    to = lax.broadcasted_iota(jnp.int32, (2 * tokens, 2 * tokens), 0)
+    source = lax.broadcasted_iota(jnp.int32, (2 * tokens, 2 * tokens), 1)
+    wanted = jnp.where(to < tokens, 2 * to, 2 * (to - tokens) + 1)
+    pick = jnp.where(source == wanted, 1.0, 0.0).astype(jnp.bfloat16)
     sent = []
-    for h in range(heads):
-        copies[h].wait()
-        both = wide.at[h % SPLIT_BUFFERS]
-        both[...] = rows[h].astype(jnp.float32)
-        keys[h] = both[pl.ds(0, tokens, stride=2), :].astype(jnp.bfloat16)
-        values[h] = both[pl.ds(1, tokens, stride=2), :].astype(jnp.bfloat16)
-        sent += start_all(
-            [
-                pltpu.make_async_copy(keys.at[h], keys_ref.at[h], out_sem.at[0, h]),
-                pltpu.make_async_copy(values.at[h], values_ref.at[h], out_sem.at[1, h]),
-            ]
-        )
+    for h in range(0, heads, 2):
+        for ahead in range(h + CACHE_AHEAD, min(h + CACHE_AHEAD + 2, heads)):
+            copies[ahead].start()
+        wait_all(copies[h : h + 2])
+        both = jnp.concatenate([rows[h], rows[h + 1]], axis=1)
+        made = jnp.dot(pick, both, preferred_element_type=jnp.float32).astype(jnp.bfloat16)
+        for i in range(2):
+            keys_ref[h + i] = made[:tokens, i * HD : (i + 1) * HD]
+            values[h + i] = made[tokens:, i * HD : (i + 1) * HD]
+        sent += start_all([pltpu.make_async_copy(values.at[h : h + 2], values_ref.at[h : h + 2], out_sem.at[h // 2])])
     wait_all(sent)
 
 
-def cache_by_head(pool, first, heads):
-    tokens = pool.shape[0]
-    part = pltpu.HBM((heads, tokens, HD), pool.dtype)
+def cache_by_head(pool):
+    tokens, heads = pool.shape[:2]
     return pl.pallas_call(
-        functools.partial(cache_kernel, first),
-        out_shape=(part, part),
+        cache_kernel,
+        out_shape=(
+            jax.ShapeDtypeStruct((heads, tokens, HD), pool.dtype),
+            pltpu.HBM((heads, tokens, HD), pool.dtype),
+        ),
         in_specs=[HBM],
-        out_specs=(HBM, HBM),
+        out_specs=(VMEM, HBM),
         scratch_shapes=[
             pltpu.VMEM((heads, tokens, 2, HD), pool.dtype),
-            pltpu.VMEM((SPLIT_BUFFERS, 2 * tokens, HD), jnp.float32),
-            pltpu.VMEM((heads, tokens, HD), pool.dtype),
             pltpu.VMEM((heads, tokens, HD), pool.dtype),
             pltpu.SemaphoreType.DMA((heads,)),
-            pltpu.SemaphoreType.DMA((2, heads)),
+            pltpu.SemaphoreType.DMA((heads // 2,)),
         ],
         compiler_params=pltpu.CompilerParams(vmem_limit_bytes=16 * 2**20),
         cost_estimate=pl.CostEstimate(flops=0, bytes_accessed=12 * 10**6, transcendentals=0),
         name="cache_by_head",
-    )(pool)
+    )(in_hbm(pool))
 
 
 def lanes_of(x):
@@ -388,7 +391,8 @@
     )
 
 
-PROJECT_CHUNK = 1024
+PROJECT_CHUNK = 512
+PROJECT_AHEAD = 3
 
 
 def project_kernel(x_ref, w_ref, send_ref, base_ref, x_buf, w_buf, total, buf, base, x_sem, w_sem, sem, base_sem):
@@ -399,18 +403,16 @@
     per = PROJECT_CHUNK // HD
     fetch_x = pltpu.make_async_copy(x_ref, x_buf, x_sem)
     fetch_x.start()
-    fetches = start_all(
-        [
-            pltpu.make_async_copy(
-                w_ref.at[:, :, p * PROJECT_CHUNK : (p + 1) * PROJECT_CHUNK], w_buf.at[p], w_sem.at[p]
-            )
-            for p in range(parts)
-        ]
-    )
+    fetches = [
+        pltpu.make_async_copy(w_ref.at[:, :, p * PROJECT_CHUNK : (p + 1) * PROJECT_CHUNK], w_buf.at[p], w_sem.at[p])
+        for p in range(parts)
+    ]
+    start_all(fetches[:PROJECT_AHEAD])
     fetch_x.wait()
     x_rows = x_buf.reshape(chunks, rows, HD)
     for p in range(parts):
         fetches[p].wait()
+        start_all(fetches[p + PROJECT_AHEAD : p + PROJECT_AHEAD + 1])
         x = jnp.concatenate([x_rows[c] for c in range(p * per, (p + 1) * per)], axis=1)
         for i in range(3):
             made = lax.dot_general(w_buf[p, i], x, CONTRACT_LANES, preferred_element_type=jnp.float32)
@@ -457,7 +459,8 @@
     )(in_hbm(x), in_hbm(weight))
 
 
-UPDATE_PARTS = 4
+UPDATE_PARTS = 8
+UPDATE_AHEAD = 4
 
 
 def update_kernel(stored_ref, low_ref, base_ref, up_ref, send_in, send_ref, base, up, buf, base_sem, up_sem, sem):
@@ -465,12 +468,11 @@
     rank = packed // 2
     rows = 2 * half
     height = up_ref.shape[0] // UPDATE_PARTS
-    fetches = start_all(
-        [
-            pltpu.make_async_copy(up_ref.at[p * height : (p + 1) * height], up.at[p], up_sem.at[p])
-            for p in range(UPDATE_PARTS)
-        ]
-    )
+    fetches = [
+        pltpu.make_async_copy(up_ref.at[p * height : (p + 1) * height], up.at[p], up_sem.at[p])
+        for p in range(UPDATE_PARTS)
+    ]
+    start_all(fetches[:UPDATE_AHEAD])
     fetch_base = pltpu.make_async_copy(base_ref, base, base_sem)
     fetch_base.start()
     low = low_ref[0].astype(jnp.float32)
@@ -484,6 +486,7 @@
     total = jnp.zeros(base.shape, jnp.float32)
     for p in range(UPDATE_PARTS):
         fetches[p].wait()
+        start_all(fetches[p + UPDATE_AHEAD : p + UPDATE_AHEAD + 1])
         for a in range(0, height // rank, batch):
             wide = jnp.where(ahead == p * (height // rank) + a, spread, 0.0).astype(jnp.bfloat16)
             total = total + jnp.dot(
@@ -518,28 +521,20 @@
     )(stored, lows, in_hbm(base), in_hbm(up), in_hbm(send))
 
 
-def attend_kernel(halves, cos_ref, sin_ref, live_ref, pieces_ref, *refs):
-    key_refs, value_refs = refs[:halves], refs[halves : 2 * halves]
-    out_ref, keys_buf, values_buf, kn_ref, vn_ref, sem = refs[2 * halves :]
+def attend_kernel(cos_ref, sin_ref, live_ref, pieces_ref, keys_ref, values_ref, out_ref, values_buf, kn_ref, vn_ref, sem):
     count, _, steps = pieces_ref.shape[:3]
     rows = 2 * steps
     each = pieces_ref.shape[1] // 3
     heads = 2 * out_ref.shape[1] // count
     lanes = heads * HD
     group = rows * HEAD_BLOCK
-    chips = count // 2
-    fetches = []
-    for chip in range(chips):
-        half, at = divmod(chip, chips // halves)
-        span = slice(at * heads, (at + 1) * heads)
-        fetches.append(
-            start_all(
-                [
-                    pltpu.make_async_copy(key_refs[half].at[span], keys_buf.at[chip], sem.at[0, chip]),
-                    pltpu.make_async_copy(value_refs[half].at[span], values_buf.at[chip], sem.at[1, chip]),
-                ]
-            )
-        )
+    chips = range(count // 2)
+    fetches = start_all(
+        [
+            pltpu.make_async_copy(values_ref.at[c * heads : (c + 1) * heads], values_buf.at[c], sem.at[c])
+            for c in chips
+        ]
+    )
     cosine = cos_ref[...][:rows]
     sine = sin_ref[...][:rows]
     left = lax.broadcasted_iota(jnp.int32, (rows, HD), 1) < HD // 2
@@ -570,54 +565,61 @@
     live = live > 0
     kn_ref[...] = jnp.zeros_like(kn_ref)
     vn_ref[...] = jnp.zeros_like(vn_ref)
-    for chip in range(chips):
-        query = jnp.concatenate(rotated(chip_columns(chip, 0)), axis=1)
-        kn_ref[0:rows] = jnp.concatenate(rotated(chip_columns(chip, each)), axis=1)
-        vn_ref[0:rows] = jnp.concatenate(chip_columns(chip, 2 * each), axis=1)
-        kn = kn_ref[...].astype(jnp.bfloat16)
-        vn = vn_ref[...].astype(jnp.bfloat16)
+    spreads = []
+    for c in chips:
+        query = jnp.concatenate(rotated(chip_columns(c, 0)), axis=1)
+        kn_ref[c, 0:rows] = jnp.concatenate(rotated(chip_columns(c, each)), axis=1)
+        vn_ref[c, 0:rows] = jnp.concatenate(chip_columns(c, 2 * each), axis=1)
         spread = jnp.concatenate(
             [jnp.broadcast_to(query[j : j + 1], (HEAD_BLOCK, lanes)) for j in range(rows)], axis=0
         )
-        spread = jnp.where(own_head, spread, 0.0).astype(jnp.bfloat16)
-        wait_all(fetches[chip])
-        keys = lanes_of(keys_buf[chip])
-        values = lanes_of(values_buf[chip])
-        scores = lax.dot_general(spread, keys, CONTRACT_LANES, preferred_element_type=jnp.float32) * (HD**-0.5)
-        scores = jnp.where(live, scores, masked_score)
-        fresh = lax.dot_general(spread, kn, CONTRACT_LANES, preferred_element_type=jnp.float32) * (HD**-0.5)
-        fresh = jnp.where(new_live, fresh, masked_score)
-        top = jnp.maximum(jnp.max(scores, axis=1, keepdims=True), jnp.max(fresh, axis=1, keepdims=True))
-        weights = jnp.where(live, jnp.exp(scores - top), 0.0)
-        fresh = jnp.where(new_live, jnp.exp(fresh - top), 0.0)
-        totals = jnp.sum(weights, axis=1, keepdims=True) + jnp.sum(fresh, axis=1, keepdims=True)
-        mixed = jnp.dot(weights.astype(jnp.bfloat16), values, preferred_element_type=jnp.float32)
-        mixed = mixed + jnp.dot(fresh.astype(jnp.bfloat16), vn, preferred_element_type=jnp.float32)
-        mixed = jnp.where(own_head, mixed / totals, 0.0)
+        spreads.append(jnp.where(own_head, spread, 0.0).astype(jnp.bfloat16))
+    scores, fresh = [], []
+    for c in chips:
+        keys = jnp.concatenate([keys_ref[c * heads + h] for h in range(heads)], axis=1)
+        kn = kn_ref[c].astype(jnp.bfloat16)
+        scores.append(lax.dot_general(spreads[c], keys, CONTRACT_LANES, preferred_element_type=jnp.float32))
+        fresh.append(lax.dot_general(spreads[c], kn, CONTRACT_LANES, preferred_element_type=jnp.float32))
+    weights, fresh_weights, totals = [], [], []
+    for c in chips:
+        old = jnp.where(live, scores[c] * (HD**-0.5), masked_score)
+        new = jnp.where(new_live, fresh[c] * (HD**-0.5), masked_score)
+        top = jnp.maximum(jnp.max(old, axis=1, keepdims=True), jnp.max(new, axis=1, keepdims=True))
+        old = jnp.where(live, jnp.exp(old - top), 0.0)
+        new = jnp.where(new_live, jnp.exp(new - top), 0.0)
+        totals.append(jnp.sum(old, axis=1, keepdims=True) + jnp.sum(new, axis=1, keepdims=True))
+        weights.append(old.astype(jnp.bfloat16))
+        fresh_weights.append(new.astype(jnp.bfloat16))
+    wait_all(fetches)
+    for c in chips:
+        values = lanes_of(values_buf[c])
+        vn = vn_ref[c].astype(jnp.bfloat16)
+        mixed = jnp.dot(weights[c], values, preferred_element_type=jnp.float32)
+        mixed = mixed + jnp.dot(fresh_weights[c], vn, preferred_element_type=jnp.float32)
+        mixed = jnp.where(own_head, mixed / totals[c], 0.0)
         out = jnp.sum(mixed.reshape(rows, HEAD_BLOCK, lanes), axis=1).astype(out_ref.dtype)
         for t in range(steps):
             for h in range(heads):
-                out_ref[t, chip * heads + h] = out[2 * t : 2 * t + 2, h * HD : (h + 1) * HD]
+                out_ref[t, c * heads + h] = out[2 * t : 2 * t + 2, h * HD : (h + 1) * HD]
 
 
 def attend(cosine, sine, live, pieces, keys, values):
     count, _, steps = pieces.shape[:3]
-    halves = len(keys)
-    heads = halves * keys[0].shape[0]
-    tokens = keys[0].shape[1]
-    per = 2 * heads // count
+    heads, tokens = keys.shape[:2]
+    chips = count // 2
+    per = heads // chips
     return pl.pallas_call(
-        functools.partial(attend_kernel, halves),
+        attend_kernel,
         out_shape=jax.ShapeDtypeStruct((steps, heads, 2, HD), jnp.bfloat16),
-        in_specs=[VMEM] * 4 + [HBM] * (2 * halves),
+        in_specs=[VMEM] * 5 + [HBM],
         out_specs=VMEM,
-        scratch_shapes=[pltpu.VMEM((count // 2, per, tokens, HD), jnp.bfloat16)] * 2
-        + [pltpu.VMEM((16, per * HD), jnp.float32)] * 2
-        + [pltpu.SemaphoreType.DMA((2, count // 2))],
+        scratch_shapes=[pltpu.VMEM((chips, per, tokens, HD), jnp.bfloat16)]
+        + [pltpu.VMEM((chips, 16, per * HD), jnp.float32)] * 2
+        + [pltpu.SemaphoreType.DMA((chips,))],
         compiler_params=pltpu.CompilerParams(vmem_limit_bytes=16 * 2**20),
         cost_estimate=pl.CostEstimate(flops=10**9, bytes_accessed=6 * 10**6, transcendentals=0),
         name="attention",
-    )(cosine, sine, live, pieces, *[in_hbm(x) for x in keys], *[in_hbm(x) for x in values])
+    )(cosine, sine, live, pieces, keys, in_hbm(values))
 
 
 def chip_plan(
@@ -640,15 +642,11 @@
     adapter_count = adapter_storage_row.shape[0]
 
     tokens = pool_pages * page_len
-    pool = in_hbm(key_value_pool.reshape(tokens, 2, heads, HD).transpose(0, 2, 1, 3))
-    first_half = cache_by_head(pool, 0, heads // 2)
-    second_half = cache_by_head(pool, heads // 2, heads // 2)
+    keys, values = cache_by_head(key_value_pool.reshape(tokens, 2, heads, HD).transpose(0, 2, 1, 3))
 
     held = {0: hidden}
-    held.update({m: trade(hidden, m, count) for m in range(4, count, 4)})
-    held, first_half = lax.optimization_barrier((held, first_half))
-    for mask in (2, 1):
-        held.update({k ^ mask: trade(v, mask, count) for k, v in list(held.items())})
+    for masks in (range(4, count, 4), (2,), (1,)):
+        held.update({k ^ m: trade(v, m, count) for k, v in list(held.items()) for m in masks})
     blocks = [
         held[k].reshape(steps, req_dev, heads, HD).transpose(0, 2, 1, 3) for k in range(count)
     ]
@@ -675,7 +673,6 @@
     my_lengths = lax.dynamic_slice_in_dim(lengths, me * req_dev, req_dev)
     cosine, sine = rotation(my_lengths, steps)
     live = live_tokens(my_lengths, request_page_table, pool_pages, page_len).astype(jnp.int32)
-    keys, values = zip(first_half, second_half)
     out = attend(cosine, sine, live.reshape(req_dev, tokens), pieces, keys, values)
     return out.transpose(0, 2, 1, 3).reshape(steps, req_dev, width)
 

time: 67 us -> 61.7 us (0.921)
  starting transfers between devices: 23.7 us -> 19.7 us
  waiting for transfers between devices: 8.61 us -> 7.04 us
  other arithmetic: 1.24 us -> 1.92 us
    all_to_all x1, waiting for transfers between devices: 4.39 us -> 0.01 us  [chip_plan(): lax.all_to_all(send, 'replica', split_axis=0, concat_axis=0, tiled=True)]
    all_to_all x1, starting transfers between devices: 5.97 us -> 4.03 us  [chip_plan(): lax.all_to_all(lows, 'replica', split_axis=0, concat_axis=0, tiled=True)]
    ppermute x15, waiting for transfers between devices: 3.82 us -> 5.73 us  [trade(): return lax.ppermute(value, 'replica', [(i, i ^ mask) for i in range(count)])]
    ppermute x15, starting transfers between devices: 12.1 us -> 10.9 us  [trade(): return lax.ppermute(value, 'replica', [(i, i ^ mask) for i in range(count)])]
    all_to_all x1, starting transfers between devices: 5.66 us -> 4.73 us  [chip_plan(): lax.all_to_all(send, 'replica', split_axis=0, concat_axis=0, tiled=True)]
    all_to_all x1, waiting for transfers between devices: 0.39 us -> 1.31 us  [chip_plan(): lax.all_to_all(lows, 'replica', split_axis=0, concat_axis=0, tiled=True)]
    pallas_call x1, Pallas kernels: 8.37 us -> 7.45 us  [project(): pl.pallas_call(project_kernel, out_shape=(pltpu.HBM((count, 3 * each, pai...]
    pallas_call x1, Pallas kernels: 3.11 us -> 3.88 us  [update_values(): pl.pallas_call(update_kernel, out_shape=pltpu.HBM(send.shape, send.dtype)...]
  transfers between devices with their start and end apart: 17 -> 17, of which waited for: 11 -> 5; matrix products, arithmetic and copies ran while one was open for 4% -> 6% of each run, Pallas kernels for 25% -> 31%
where the time goes in v6:
time: 61.7 us; the launch traced here: 61.1 us
  Pallas kernels  30.5 us (49%)
  starting transfers between devices  19.7 us (32%)
  waiting for transfers between devices  7.04 us (11%)
  other arithmetic  1.92 us (3%)
  local copies, waits for them, and re-layouts  1.62 us (3%)
    pallas_call x1, Pallas kernels, cache_by_head(): pl.pallas_call(cache_kernel, out_shape=(jax.ShapeDtypeStruct((heads, toke...  11.2 us
    ppermute x15, starting transfers between devices, trade(): return lax.ppermute(value, 'replica', [(i, i ^ mask) for i in range(count)])  10.9 us
    pallas_call x1, Pallas kernels, project(): pl.pallas_call(project_kernel, out_shape=(pltpu.HBM((count, 3 * each, pai...  7.45 us
    ppermute x15, waiting for transfers between devices, trade(): return lax.ppermute(value, 'replica', [(i, i ^ mask) for i in range(count)])  5.73 us
    all_to_all x1, starting transfers between devices, chip_plan(): lax.all_to_all(send, 'replica', split_axis=0, concat_axis=0, tiled=True)  4.73 us
    pallas_call x1, Pallas kernels, low_of(): pl.pallas_call(functools.partial(low_kernel, count), out_shape=(pltpu.HBM...  4.06 us
    all_to_all x1, starting transfers between devices, chip_plan(): lax.all_to_all(lows, 'replica', split_axis=0, concat_axis=0, tiled=True)  4.03 us
    pallas_call x1, Pallas kernels, update_values(): pl.pallas_call(update_kernel, out_shape=pltpu.HBM(send.shape, send.dtype)...  3.88 us
  transfers between devices with their start and end apart: 17, of which 5 were waited for; matrix products, arithmetic and copies ran while one was open for 6% of the time, Pallas kernels for 31%

profile of v6, /device:TPU:0, one launch (start us, length us, event | category | flops | bytes accessed | tf_op | source)
XLA Modules:
  0.0 61.1 jit_solution(16887996719056589071)
XLA Ops:
  0.0 3.0 %collective-permute-start.3 = (bf16[3,2,5120]{2,1,0:T(2,128)(2,1)}, bf16[3,2,5120]{2,1,0:T(2,128)(2,1)S(1)}, u32[]{:S(2)}, u32[]{:S(2)}) collective-permute-start(bf16[3,2,5120]{2,1,0:T(2,128)(2,1)} %param.9), channel_id=1, source_target_pairs={{0,4},{1,5},{2,6},{3,7},{4,0},{5,1},{6,2},{7,3},{8,12},{9,13},{10,... | collective-permute-start | bytes 184328 | tf_op jit(solution)/shard_map/ppermute | solution.py:233
  3.0 1.5 %collective-permute-start.1 = (bf16[3,2,5120]{2,1,0:T(2,128)(2,1)}, bf16[3,2,5120]{2,1,0:T(2,128)(2,1)S(1)}, u32[]{:S(2)}, u32[]{:S(2)}) collective-permute-start(bf16[3,2,5120]{2,1,0:T(2,128)(2,1)} %param.9), channel_id=1, source_target_pairs={{0,2},{1,3},{2,0},{3,1},{4,6},{5,7},{6,4},{7,5},{8,10},{9,11},{10,... | collective-permute-start | bytes 184328 | tf_op jit(solution)/shard_map/ppermute | solution.py:233
  4.5 0.0 collective-permute-start
  4.5 2.5 %collective-permute-start.11 = (bf16[3,2,5120]{2,1,0:T(2,128)(2,1)}, bf16[3,2,5120]{2,1,0:T(2,128)(2,1)S(1)}, u32[]{:S(2)}, u32[]{:S(2)}) collective-permute-start(bf16[3,2,5120]{2,1,0:T(2,128)(2,1)} %param.9), channel_id=1, source_target_pairs={{0,12},{1,13},{2,14},{3,15},{4,8},{5,9},{6,10},{7,11},{8,4},{9,5},... | collective-permute-start | bytes 184328 | tf_op jit(solution)/shard_map/ppermute | solution.py:233
  7.0 0.1 collective-permute-start.7
  7.1 0.7 %dynamic_slice.3 = s32[2]{0:T(128)S(1)} dynamic-slice(s32[32]{0:T(128)} %param.15, s32[]{:T(128)S(6)} %select_n.11), dynamic_slice_sizes={2} | dynamic-slice | bytes 20 | tf_op jit(solution)/shard_map/dynamic_slice | solution.py:673
  7.9 0.8 %select_reduce_fusion.1 = s32[32]{0:T(128)S(1)} fusion(s32[64]{0:T(128)} %param.13, s32[32]{0:T(128)} %param.14), kind=kLoop, calls=%fused_computation.2 | loop fusion | flops 6112 | bytes 512 | tf_op jit(solution)/shard_map/reduce_sum | solution.py:655
  8.7 0.1 broadcast_in_dim.52
  8.8 0.8 %select_reduce_fusion = s32[2,64]{1,0:T(2,128)S(1)} fusion(s32[2,32]{1,0:T(2,128)} %param.16), kind=kLoop, calls=%fused_computation | loop fusion | flops 12160 | bytes 768 | tf_op jit(solution)/shard_map/reduce_max | solution.py:113
  9.6 0.0 collective-permute-done.3
  9.6 0.6 collective-permute-start.5
  10.2 0.0 collective-permute-done.1
  10.2 0.0 collective-permute-start.4
  10.2 0.0 collective-permute-done
  10.2 0.5 collective-permute-start.2
  10.7 0.4 collective-permute-done.11
  11.1 1.1 %collective-permute-start.13 = (bf16[3,2,5120]{2,1,0:T(2,128)(2,1)S(1)}, bf16[3,2,5120]{2,1,0:T(2,128)(2,1)S(1)}, u32[]{:S(2)}, u32[]{:S(2)}) collective-permute-start(bf16[3,2,5120]{2,1,0:T(2,128)(2,1)S(1)} %collective-permute-done.11), channel_id=1, source_target_pairs={{0,2},{1,3},{2,0},{3,1},{4,6},{5,7},{6,4},{7,5},{8,10},{9,11},{10,... | collective-permute-start | bytes 184328 | tf_op jit(solution)/shard_map/ppermute | solution.py:233
  12.2 1.7 %collective-permute-done.7 = bf16[3,2,5120]{2,1,0:T(2,128)(2,1)S(1)} collective-permute-done((bf16[3,2,5120]{2,1,0:T(2,128)(2,1)}, bf16[3,2,5120]{2,1,0:T(2,128)(2,1)S(1)}, u32[]{:S(2)}, u32[]{:S(2)}) %collective-permute-start.7) | collective-permute-done | bytes 61472 | tf_op jit(solution)/shard_map/ppermute | solution.py:233
  14.0 0.5 collective-permute-start.9
  14.5 0.1 add.46
  14.6 0.1 sub.19.slot_ref
  14.7 0.1 collective-permute-start.12
  14.8 0.0 collective-permute-done.4
  14.8 0.5 collective-permute-start.8
  15.3 0.0 collective-permute-done.2
  15.3 0.1 collective-permute-start.6
  15.4 0.4 collective-permute-start.14
  15.8 2.4 %collective-permute-done.9 = bf16[3,2,5120]{2,1,0:T(2,128)(2,1)S(1)} collective-permute-done((bf16[3,2,5120]{2,1,0:T(2,128)(2,1)S(1)}, bf16[3,2,5120]{2,1,0:T(2,128)(2,1)S(1)}, u32[]{:S(2)}, u32[]{:S(2)}) %collective-permute-start.9) | collective-permute-done | bytes 61472 | tf_op jit(solution)/shard_map/ppermute | solution.py:233
  18.2 0.0 collective-permute-start.10
  18.2 0.0 collective-permute-done.6
  18.2 1.2 %collective-permute-done.10 = bf16[3,2,5120]{2,1,0:T(2,128)(2,1)S(1)} collective-permute-done((bf16[3,2,5120]{2,1,0:T(2,128)(2,1)S(1)}, bf16[3,2,5120]{2,1,0:T(2,128)(2,1)S(1)}, u32[]{:S(2)}, u32[]{:S(2)}) %collective-permute-start.10) | collective-permute-done | bytes 61472 | tf_op jit(solution)/shard_map/ppermute | solution.py:233
  19.4 4.1 %low_rows.1 = (bf16[40,48,2,128]{3,2,1,0:T(2,128)(2,1)}, bf16[16,48,128]{2,1,0:T(8,128)(2,1)}) custom-call(s32[1]{0:T(128)} %bitcast.me_ref, s32[1,96]{1,0:T(1,128)S(1)} %sub.19.slot_ref, bf16[4,64,5120]{2,1,0:T(8,128)(2,1)} %down_ref.1, bf16[3,40,2,128]{3,2,1,0:T(2,128)(2,1)} %bitcast.75, bf16[3,40,2,128]{3,2,1,0:T(2,128)(2,1)S(1)} %bitcast.59, ...), custom_call_target="tpu_custom_call" | custom-call | flops 100000000 | bytes 4000000 | tf_op jit(solution)/shard_map/low_rows/pallas_call | solution.py:350
  23.5 4.0 %all-to-all-start = ((bf16[16,48,128]{2,1,0:T(8,128)(2,1)}), bf16[16,48,128]{2,1,0:T(8,128)(2,1)S(1)}, u32[]{:S(2)}, u32[]{:S(2)}) async-start(bf16[16,48,128]{2,1,0:T(8,128)(2,1)} %get-tuple-element.11), calls=%async_computation | async-start | bytes 393216 | tf_op jit(solution)/shard_map/all_to_all | solution.py:668
  27.6 0.1 broadcast_in_dim_reshape.4.stored_ref
  27.7 0.1 fusion
  27.8 7.5 %project.1 = (bf16[16,9,3,2,128]{4,3,2,1,0:T(2,128)(2,1)}, f32[96,320]{1,0:T(8,128)}) custom-call(bf16[40,48,2,128]{3,2,1,0:T(2,128)(2,1)} %get-tuple-element.12.x_ref, bf16[3,320,5120]{2,1,0:T(8,128)(2,1)} %bitcast.72), custom_call_target="tpu_custom_call" | custom-call | flops 1000000000 | bytes 11000000 | tf_op jit(solution)/shard_map/project/pallas_call | solution.py:437
  35.2 1.3 %all-to-all-done.low_ref = bf16[16,48,128]{2,1,0:T(8,128)(2,1)S(1)} async-done(((bf16[16,48,128]{2,1,0:T(8,128)(2,1)}), bf16[16,48,128]{2,1,0:T(8,128)(2,1)S(1)}, u32[]{:S(2)}, u32[]{:S(2)}) %all-to-all-start) | async-done | bytes 196640 | tf_op jit(solution)/shard_map/all_to_all | solution.py:668
  36.5 3.9 %update_values.1 = bf16[16,9,3,2,128]{4,3,2,1,0:T(2,128)(2,1)} custom-call(s32[96,1]{1,0:T(8,128)S(1)} %broadcast_in_dim_reshape.4.stored_ref, bf16[16,48,128]{2,1,0:T(8,128)(2,1)S(1)} %all-to-all-done.low_ref, f32[96,320]{1,0:T(8,128)} %get-tuple-element.13.base_ref, bf16[4096,320]{1,0:T(8,128)(2,1)} %bitcast.74, ...), custom_call_target="tpu_custom_call", output_to_operand_aliasing={{}: (4, {})} | custom-call | flops 300000000 | bytes 4000000 | tf_op jit(solution)/shard_map/update_values/pallas_call | solution.py:504
  40.4 4.7 %all-to-all-start.1 = ((bf16[16,9,3,2,128]{4,3,2,1,0:T(2,128)(2,1)}), bf16[16,9,3,2,128]{4,3,2,1,0:T(2,128)(2,1)S(1)}, u32[]{:S(2)}, u32[]{:S(2)}) async-start(bf16[16,9,3,2,128]{4,3,2,1,0:T(2,128)(2,1)} %update_values.1), calls=%async_computation.1 | async-start | bytes 442368 | tf_op jit(solution)/shard_map/all_to_all | solution.py:671
  45.2 0.1 and.12
  45.3 0.1 and.13
  45.4 0.1 add.50
  45.5 0.1 add.47
  45.6 0.1 add.48
  45.7 11.2 %cache_by_head.1 = (bf16[40,256,128]{2,1,0:T(8,128)(2,1)S(1)}, bf16[40,256,128]{2,1,0:T(8,128)(2,1)}) custom-call(bf16[256,40,2,128]{3,2,1,0:T(2,128)(2,1)} %bitcast.73), custom_call_target="tpu_custom_call" | custom-call | bytes 12000000 | tf_op jit(solution)/shard_map/cache_by_head/pallas_call | solution.py:288
  57.0 0.1 pad_maximum_fusion
  57.0 0.1 and_convert_fusion.live_ref
  57.1 3.9 %attention.1 = bf16[3,40,2,128]{3,2,1,0:T(2,128)(2,1)} custom-call(f32[8,128]{1,0:T(8,128)S(1)} %get-tuple-element.20.cos_ref, f32[8,128]{1,0:T(8,128)S(1)} %get-tuple-element.21.sin_ref, s32[2,256]{1,0:T(2,128)S(1)} %and_convert_fusion.live_ref, bf16[16,9,3,2,128]{4,3,2,1,0:T(2,128)(2,1)S(1)} %all-to-all-done.1.pieces_ref, ...), custom_call_target="tpu_custom_call" | custom-call | flops 1000000000 | bytes 6000000 | tf_op jit(solution)/shard_map/attention/pallas_call | solution.py:611
  (15 shorter events, 0.1 us)
Async XLA Ops:
  0.0 9.6 %collective-permute-start.3 = (bf16[3,2,5120]{2,1,0:T(2,128)(2,1)}, bf16[3,2,5120]{2,1,0:T(2,128)(2,1)S(1)}, u32[]{:S(2)}, u32[]{:S(2)}) collective-permute-start(bf16[3,2,5120]{2,1,0:T(2,128)(2,1)} %param.9), channel_id=1, source_target_pairs={{0,4},{1,5},{2,6},{3,7},{4,0},{5,1},{6,2},{7,3},{8,12},{9,13},{10,... | collective-permute-start | bytes 184328 | tf_op jit(solution)/shard_map/ppermute | solution.py:233
  3.0 7.2 %collective-permute-start.1 = (bf16[3,2,5120]{2,1,0:T(2,128)(2,1)}, bf16[3,2,5120]{2,1,0:T(2,128)(2,1)S(1)}, u32[]{:S(2)}, u32[]{:S(2)}) collective-permute-start(bf16[3,2,5120]{2,1,0:T(2,128)(2,1)} %param.9), channel_id=1, source_target_pairs={{0,2},{1,3},{2,0},{3,1},{4,6},{5,7},{6,4},{7,5},{8,10},{9,11},{10,... | collective-permute-start | bytes 184328 | tf_op jit(solution)/shard_map/ppermute | solution.py:233
  4.5 5.6 %collective-permute-start = (bf16[3,2,5120]{2,1,0:T(2,128)(2,1)}, bf16[3,2,5120]{2,1,0:T(2,128)(2,1)S(1)}, u32[]{:S(2)}, u32[]{:S(2)}) collective-permute-start(bf16[3,2,5120]{2,1,0:T(2,128)(2,1)} %param.9), channel_id=1, source_target_pairs={{0,1},{1,0},{2,3},{3,2},{4,5},{5,4},{6,7},{7,6},{8,9},{9,8},{10,11... | collective-permute-start | bytes 184328 | tf_op jit(solution)/shard_map/ppermute | solution.py:233
  4.5 6.5 %collective-permute-start.11 = (bf16[3,2,5120]{2,1,0:T(2,128)(2,1)}, bf16[3,2,5120]{2,1,0:T(2,128)(2,1)S(1)}, u32[]{:S(2)}, u32[]{:S(2)}) collective-permute-start(bf16[3,2,5120]{2,1,0:T(2,128)(2,1)} %param.9), channel_id=1, source_target_pairs={{0,12},{1,13},{2,14},{3,15},{4,8},{5,9},{6,10},{7,11},{8,4},{9,5},... | collective-permute-start | bytes 184328 | tf_op jit(solution)/shard_map/ppermute | solution.py:233
  7.0 6.9 %collective-permute-start.7 = (bf16[3,2,5120]{2,1,0:T(2,128)(2,1)}, bf16[3,2,5120]{2,1,0:T(2,128)(2,1)S(1)}, u32[]{:S(2)}, u32[]{:S(2)}) collective-permute-start(bf16[3,2,5120]{2,1,0:T(2,128)(2,1)} %param.9), channel_id=1, source_target_pairs={{0,8},{1,9},{2,10},{3,11},{4,12},{5,13},{6,14},{7,15},{8,0},{9,1},... | collective-permute-start | bytes 184328 | tf_op jit(solution)/shard_map/ppermute | solution.py:233
  9.6 5.1 %collective-permute-start.5 = (bf16[3,2,5120]{2,1,0:T(2,128)(2,1)S(1)}, bf16[3,2,5120]{2,1,0:T(2,128)(2,1)S(1)}, u32[]{:S(2)}, u32[]{:S(2)}) collective-permute-start(bf16[3,2,5120]{2,1,0:T(2,128)(2,1)S(1)} %collective-permute-done.3), channel_id=1, source_target_pairs={{0,2},{1,3},{2,0},{3,1},{4,6},{5,7},{6,4},{7,5},{8,10},{9,11},{10,... | collective-permute-start | bytes 184328 | tf_op jit(solution)/shard_map/ppermute | solution.py:233
  10.2 4.6 %collective-permute-start.4 = (bf16[3,2,5120]{2,1,0:T(2,128)(2,1)S(1)}, bf16[3,2,5120]{2,1,0:T(2,128)(2,1)S(1)}, u32[]{:S(2)}, u32[]{:S(2)}) collective-permute-start(bf16[3,2,5120]{2,1,0:T(2,128)(2,1)S(1)} %collective-permute-done.3), channel_id=1, source_target_pairs={{0,1},{1,0},{2,3},{3,2},{4,5},{5,4},{6,7},{7,6},{8,9},{9,8},{10,11... | collective-permute-start | bytes 184328 | tf_op jit(solution)/shard_map/ppermute | solution.py:233
  10.2 5.1 %collective-permute-start.2 = (bf16[3,2,5120]{2,1,0:T(2,128)(2,1)S(1)}, bf16[3,2,5120]{2,1,0:T(2,128)(2,1)S(1)}, u32[]{:S(2)}, u32[]{:S(2)}) collective-permute-start(bf16[3,2,5120]{2,1,0:T(2,128)(2,1)S(1)} %collective-permute-done.1), channel_id=1, source_target_pairs={{0,1},{1,0},{2,3},{3,2},{4,5},{5,4},{6,7},{7,6},{8,9},{9,8},{10,11... | collective-permute-start | bytes 184328 | tf_op jit(solution)/shard_map/ppermute | solution.py:233
  11.1 4.3 %collective-permute-start.13 = (bf16[3,2,5120]{2,1,0:T(2,128)(2,1)S(1)}, bf16[3,2,5120]{2,1,0:T(2,128)(2,1)S(1)}, u32[]{:S(2)}, u32[]{:S(2)}) collective-permute-start(bf16[3,2,5120]{2,1,0:T(2,128)(2,1)S(1)} %collective-permute-done.11), channel_id=1, source_target_pairs={{0,2},{1,3},{2,0},{3,1},{4,6},{5,7},{6,4},{7,5},{8,10},{9,11},{10,... | collective-permute-start | bytes 184328 | tf_op jit(solution)/shard_map/ppermute | solution.py:233
  14.0 4.2 %collective-permute-start.9 = (bf16[3,2,5120]{2,1,0:T(2,128)(2,1)S(1)}, bf16[3,2,5120]{2,1,0:T(2,128)(2,1)S(1)}, u32[]{:S(2)}, u32[]{:S(2)}) collective-permute-start(bf16[3,2,5120]{2,1,0:T(2,128)(2,1)S(1)} %collective-permute-done.7), channel_id=1, source_target_pairs={{0,2},{1,3},{2,0},{3,1},{4,6},{5,7},{6,4},{7,5},{8,10},{9,11},{10,... | collective-permute-start | bytes 184328 | tf_op jit(solution)/shard_map/ppermute | solution.py:233
  14.7 3.5 %collective-permute-start.12 = (bf16[3,2,5120]{2,1,0:T(2,128)(2,1)S(1)}, bf16[3,2,5120]{2,1,0:T(2,128)(2,1)S(1)}, u32[]{:S(2)}, u32[]{:S(2)}) collective-permute-start(bf16[3,2,5120]{2,1,0:T(2,128)(2,1)S(1)} %collective-permute-done.11), channel_id=1, source_target_pairs={{0,1},{1,0},{2,3},{3,2},{4,5},{5,4},{6,7},{7,6},{8,9},{9,8},{10,11... | collective-permute-start | bytes 184328 | tf_op jit(solution)/shard_map/ppermute | solution.py:233
  14.8 3.4 %collective-permute-start.8 = (bf16[3,2,5120]{2,1,0:T(2,128)(2,1)S(1)}, bf16[3,2,5120]{2,1,0:T(2,128)(2,1)S(1)}, u32[]{:S(2)}, u32[]{:S(2)}) collective-permute-start(bf16[3,2,5120]{2,1,0:T(2,128)(2,1)S(1)} %collective-permute-done.7), channel_id=1, source_target_pairs={{0,1},{1,0},{2,3},{3,2},{4,5},{5,4},{6,7},{7,6},{8,9},{9,8},{10,11... | collective-permute-start | bytes 184328 | tf_op jit(solution)/shard_map/ppermute | solution.py:233
  15.3 2.9 %collective-permute-start.6 = (bf16[3,2,5120]{2,1,0:T(2,128)(2,1)S(1)}, bf16[3,2,5120]{2,1,0:T(2,128)(2,1)S(1)}, u32[]{:S(2)}, u32[]{:S(2)}) collective-permute-start(bf16[3,2,5120]{2,1,0:T(2,128)(2,1)S(1)} %collective-permute-done.5), channel_id=1, source_target_pairs={{0,1},{1,0},{2,3},{3,2},{4,5},{5,4},{6,7},{7,6},{8,9},{9,8},{10,11... | collective-permute-start | bytes 184328 | tf_op jit(solution)/shard_map/ppermute | solution.py:233
  15.4 2.9 %collective-permute-start.14 = (bf16[3,2,5120]{2,1,0:T(2,128)(2,1)S(1)}, bf16[3,2,5120]{2,1,0:T(2,128)(2,1)S(1)}, u32[]{:S(2)}, u32[]{:S(2)}) collective-permute-start(bf16[3,2,5120]{2,1,0:T(2,128)(2,1)S(1)} %collective-permute-done.13), channel_id=1, source_target_pairs={{0,1},{1,0},{2,3},{3,2},{4,5},{5,4},{6,7},{7,6},{8,9},{9,8},{10,11... | collective-permute-start | bytes 184328 | tf_op jit(solution)/shard_map/ppermute | solution.py:233
  18.2 1.2 %collective-permute-start.10 = (bf16[3,2,5120]{2,1,0:T(2,128)(2,1)S(1)}, bf16[3,2,5120]{2,1,0:T(2,128)(2,1)S(1)}, u32[]{:S(2)}, u32[]{:S(2)}) collective-permute-start(bf16[3,2,5120]{2,1,0:T(2,128)(2,1)S(1)} %collective-permute-done.9), channel_id=1, source_target_pairs={{0,1},{1,0},{2,3},{3,2},{4,5},{5,4},{6,7},{7,6},{8,9},{9,8},{10,11... | collective-permute-start | bytes 184328 | tf_op jit(solution)/shard_map/ppermute | solution.py:233
  23.5 13.0 %all-to-all-start = ((bf16[16,48,128]{2,1,0:T(8,128)(2,1)}), bf16[16,48,128]{2,1,0:T(8,128)(2,1)S(1)}, u32[]{:S(2)}, u32[]{:S(2)}) async-start(bf16[16,48,128]{2,1,0:T(8,128)(2,1)} %get-tuple-element.11), calls=%async_computation | async-start | bytes 393216 | tf_op jit(solution)/shard_map/all_to_all | solution.py:668
  40.4 16.7 %all-to-all-start.1 = ((bf16[16,9,3,2,128]{4,3,2,1,0:T(2,128)(2,1)}), bf16[16,9,3,2,128]{4,3,2,1,0:T(2,128)(2,1)S(1)}, u32[]{:S(2)}, u32[]{:S(2)}) async-start(bf16[16,9,3,2,128]{4,3,2,1,0:T(2,128)(2,1)} %update_values.1), calls=%async_computation.1 | async-start | bytes 442368 | tf_op jit(solution)/shard_map/all_to_all | solution.py:671

commit v7 on v6

--- a/solution.py
+++ b/solution.py
@@ -252,18 +252,22 @@
     return copies
 
 
+def rows_copies(source, place, sem, pieces):
+    step = source.shape[0] // pieces
+    return [
+        pltpu.make_async_copy(source.at[p * step : (p + 1) * step], place.at[p * step : (p + 1) * step], sem.at[p])
+        for p in range(pieces)
+    ]
+
+
 def wait_all(copies):
     for copy in copies:
         copy.wait()
 
 
-CACHE_AHEAD = 16
-
-
 def cache_kernel(pool_ref, keys_ref, values_ref, raw, values, sem, out_sem):
     heads, tokens = raw.shape[:2]
-    copies = [pltpu.make_async_copy(pool_ref.at[:, h], raw.at[h], sem.at[h]) for h in range(heads)]
-    start_all(copies[:CACHE_AHEAD])
+    copies = start_all([pltpu.make_async_copy(pool_ref.at[:, h], raw.at[h], sem.at[h]) for h in range(heads)])
     rows = raw.reshape(heads, 2 * tokens, HD)
     to = lax.broadcasted_iota(jnp.int32, (2 * tokens, 2 * tokens), 0)
     source = lax.broadcasted_iota(jnp.int32, (2 * tokens, 2 * tokens), 1)
@@ -271,8 +275,6 @@
     pick = jnp.where(source == wanted, 1.0, 0.0).astype(jnp.bfloat16)
     sent = []
     for h in range(0, heads, 2):
-        for ahead in range(h + CACHE_AHEAD, min(h + CACHE_AHEAD + 2, heads)):
-            copies[ahead].start()
         wait_all(copies[h : h + 2])
         both = jnp.concatenate([rows[h], rows[h + 1]], axis=1)
         made = jnp.dot(pick, both, preferred_element_type=jnp.float32).astype(jnp.bfloat16)
@@ -309,13 +311,18 @@
     return jnp.concatenate([x[c] for c in range(x.shape[0])], axis=1)
 
 
+DOWN_PIECES = 4
+X_PIECES = 8
+
+
 def low_kernel(count, me_ref, slot_ref, down_ref, *refs):
-    blocks, (x_ref, low_ref, x_buf, maps, made_ref, sem, low_sem, own_sem) = refs[:count], refs[count:]
+    blocks, (x_ref, low_ref, x_buf, maps, made_ref, sem, low_sem, x_sem, down_sem) = refs[:count], refs[count:]
     me = me_ref[0]
     steps = blocks[0].shape[0]
     holders, rank, width = down_ref.shape
-    fetch = pltpu.make_async_copy(down_ref, maps, own_sem.at[0])
-    fetch.start()
+    fetches = []
+    for h in range(holders):
+        fetches += start_all(rows_copies(down_ref.at[h], maps.at[h], down_sem.at[h], DOWN_PIECES))
     copies = []
     for k, block in enumerate(blocks):
         for t in range(steps):
@@ -323,12 +330,11 @@
                 pltpu.make_async_copy(block.at[t], x_buf.at[:, (me ^ k) * steps + t], sem.at[k * steps + t])
             )
     wait_all(start_all(copies))
-    keep = pltpu.make_async_copy(x_buf, x_ref, own_sem.at[1])
-    keep.start()
+    keep = start_all(rows_copies(x_buf, x_ref, x_sem, X_PIECES))
     chunks, pairs = x_buf.shape[:2]
     rows = 2 * pairs
     x = lanes_of(x_buf.reshape(chunks, rows, HD))
-    fetch.wait()
+    wait_all(fetches)
     made = lax.dot_general(
         maps.reshape(holders * rank, width)[...], x, CONTRACT_LANES, preferred_element_type=jnp.float32
     )
@@ -339,7 +345,7 @@
     low = low.T
     made_ref[...] = jnp.concatenate([low[: rows // 2], low[rows // 2 :]], axis=1).astype(made_ref.dtype)
     wait_all(start_all([pltpu.make_async_copy(made_ref, low_ref.at[k], low_sem.at[k]) for k in range(count)]))
-    keep.wait()
+    wait_all(keep)
 
 
 def low_of(me, blocks, slot, down):
@@ -361,7 +367,8 @@
             pltpu.VMEM((rows // 2, 2 * rank), jnp.bfloat16),
             pltpu.SemaphoreType.DMA((count * steps,)),
             pltpu.SemaphoreType.DMA((count,)),
-            pltpu.SemaphoreType.DMA((2,)),
+            pltpu.SemaphoreType.DMA((X_PIECES,)),
+            pltpu.SemaphoreType.DMA((down.shape[0], DOWN_PIECES)),
         ],
         compiler_params=pltpu.CompilerParams(vmem_limit_bytes=16 * 2**20),
         cost_estimate=pl.CostEstimate(flops=10**8, bytes_accessed=4 * 10**6, transcendentals=0),
@@ -392,7 +399,8 @@
 
 
 PROJECT_CHUNK = 512
-PROJECT_AHEAD = 3
+PROJECT_AHEAD = 4
+PROJECT_PIECES = 2
 
 
 def project_kernel(x_ref, w_ref, send_ref, base_ref, x_buf, w_buf, total, buf, base, x_sem, w_sem, sem, base_sem):
@@ -401,18 +409,21 @@
     columns, width = w_ref.shape[1:]
     parts = width // PROJECT_CHUNK
     per = PROJECT_CHUNK // HD
-    fetch_x = pltpu.make_async_copy(x_ref, x_buf, x_sem)
-    fetch_x.start()
-    fetches = [
-        pltpu.make_async_copy(w_ref.at[:, :, p * PROJECT_CHUNK : (p + 1) * PROJECT_CHUNK], w_buf.at[p], w_sem.at[p])
-        for p in range(parts)
-    ]
-    start_all(fetches[:PROJECT_AHEAD])
-    fetch_x.wait()
+    fetch_x = start_all(rows_copies(x_ref, x_buf, x_sem, X_PIECES))
+    fetches = []
+    for p in range(parts):
+        span = slice(p * PROJECT_CHUNK, (p + 1) * PROJECT_CHUNK)
+        fetches.append([])
+        for i in range(3):
+            fetches[p] += rows_copies(w_ref.at[i, :, span], w_buf.at[p, i], w_sem.at[p, i], PROJECT_PIECES)
+    for ahead in fetches[:PROJECT_AHEAD]:
+        start_all(ahead)
+    wait_all(fetch_x)
     x_rows = x_buf.reshape(chunks, rows, HD)
     for p in range(parts):
-        fetches[p].wait()
-        start_all(fetches[p + PROJECT_AHEAD : p + PROJECT_AHEAD + 1])
+        wait_all(fetches[p])
+        for ahead in fetches[p + PROJECT_AHEAD : p + PROJECT_AHEAD + 1]:
+            start_all(ahead)
         x = jnp.concatenate([x_rows[c] for c in range(p * per, (p + 1) * per)], axis=1)
         for i in range(3):
             made = lax.dot_general(w_buf[p, i], x, CONTRACT_LANES, preferred_element_type=jnp.float32)
@@ -448,8 +459,8 @@
             pltpu.VMEM((3, columns, 2 * pairs), jnp.float32),
             pltpu.VMEM((2 * each, pairs, 2, HD), jnp.bfloat16),
             pltpu.VMEM((2 * pairs, columns), jnp.float32),
-            pltpu.SemaphoreType.DMA,
-            pltpu.SemaphoreType.DMA((parts,)),
+            pltpu.SemaphoreType.DMA((X_PIECES,)),
+            pltpu.SemaphoreType.DMA((parts, 3, PROJECT_PIECES)),
             pltpu.SemaphoreType.DMA((count,)),
             pltpu.SemaphoreType.DMA,
         ],
@@ -459,8 +470,8 @@
     )(in_hbm(x), in_hbm(weight))
 
 
-UPDATE_PARTS = 8
-UPDATE_AHEAD = 4
+UPDATE_PARTS = 16
+UPDATE_AHEAD = 16
 
 
 def update_kernel(stored_ref, low_ref, base_ref, up_ref, send_in, send_ref, base, up, buf, base_sem, up_sem, sem):
@@ -644,6 +655,17 @@
     tokens = pool_pages * page_len
     keys, values = cache_by_head(key_value_pool.reshape(tokens, 2, heads, HD).transpose(0, 2, 1, 3))
 
+    stored = jnp.sum(
+        jnp.where(
+            request_adapter[:, None] == jnp.arange(adapter_count, dtype=jnp.int32)[None, :],
+            adapter_storage_row[None, :],
+            0,
+        ),
+        axis=1,
+    )
+    stored = jnp.broadcast_to(stored.reshape(count, 1, req_dev), (count, steps, req_dev)).reshape(-1)
+    my_lengths = lax.dynamic_slice_in_dim(lengths, me * req_dev, req_dev)
+
     held = {0: hidden}
     for masks in (range(4, count, 4), (2,), (1,)):
         held.update({k ^ m: trade(v, m, count) for k, v in list(held.items()) for m in masks})
@@ -652,16 +674,6 @@
     ]
     blocks[0] = in_hbm(blocks[0])
 
-    stored = jnp.sum(
-        jnp.where(
-            request_adapter[:, None] == jnp.arange(adapter_count, dtype=jnp.int32)[None, :],
-            adapter_storage_row[None, :],
-            0,
-        ),
-        axis=1,
-    )
-    stored = jnp.broadcast_to(stored.reshape(count, 1, req_dev), (count, steps, req_dev)).reshape(-1)
-
     x, lows = low_of(
         me.astype(jnp.int32).reshape(1), blocks, (stored - me * holder_count)[None, :], adapter_down_maps
     )
@@ -670,7 +682,6 @@
     send = update_values(stored[:, None], lows, base, adapter_up_maps.reshape(adapter_count * rank, -1), send)
     pieces = lax.all_to_all(send, "replica", split_axis=0, concat_axis=0, tiled=True)
 
-    my_lengths = lax.dynamic_slice_in_dim(lengths, me * req_dev, req_dev)
     cosine, sine = rotation(my_lengths, steps)
     live = live_tokens(my_lengths, request_page_table, pool_pages, page_len).astype(jnp.int32)
     out = attend(cosine, sine, live.reshape(req_dev, tokens), pieces, keys, values)

time: 61.7 us -> 63.9 us (1.036)
  Pallas kernels: 30.5 us -> 32.9 us
  starting transfers between devices: 19.7 us -> 20.9 us
  waiting for transfers between devices: 7.04 us -> 5.88 us
    all_to_all x1, starting transfers between devices: 4.73 us -> 5.89 us  [chip_plan(): lax.all_to_all(send, 'replica', split_axis=0, concat_axis=0, tiled=True)]
    all_to_all x1, waiting for transfers between devices: 1.31 us -> 0.15 us  [chip_plan(): lax.all_to_all(lows, 'replica', split_axis=0, concat_axis=0, tiled=True)]
    pallas_call x1, Pallas kernels: 7.45 us -> 8.61 us  [project(): pl.pallas_call(project_kernel, out_shape=(pltpu.HBM((count, 3 * each, pai...]
    pallas_call x1, Pallas kernels: 3.88 us -> 4.53 us  [update_values(): pl.pallas_call(update_kernel, out_shape=pltpu.HBM(send.shape, send.dtype)...]
where the time goes in v7:
time: 63.9 us; the launch traced here: 63.5 us
  Pallas kernels  32.9 us (51%)
  starting transfers between devices  20.9 us (33%)
  waiting for transfers between devices  5.88 us (9%)
  other arithmetic  1.92 us (3%)
  local copies, waits for them, and re-layouts  1.62 us (3%)
    pallas_call x1, Pallas kernels, cache_by_head(): pl.pallas_call(cache_kernel, out_shape=(jax.ShapeDtypeStruct((heads, toke...  11.2 us
    ppermute x15, starting transfers between devices, trade(): return lax.ppermute(value, 'replica', [(i, i ^ mask) for i in range(count)])  10.9 us
    pallas_call x1, Pallas kernels, project(): pl.pallas_call(project_kernel, out_shape=(pltpu.HBM((count, 3 * each, pai...  8.61 us
    all_to_all x1, starting transfers between devices, chip_plan(): lax.all_to_all(send, 'replica', split_axis=0, concat_axis=0, tiled=True)  5.89 us
    ppermute x15, waiting for transfers between devices, trade(): return lax.ppermute(value, 'replica', [(i, i ^ mask) for i in range(count)])  5.73 us
    pallas_call x1, Pallas kernels, low_of(): pl.pallas_call(functools.partial(low_kernel, count), out_shape=(pltpu.HBM...  4.65 us
    pallas_call x1, Pallas kernels, update_values(): pl.pallas_call(update_kernel, out_shape=pltpu.HBM(send.shape, send.dtype)...  4.53 us
    all_to_all x1, starting transfers between devices, chip_plan(): lax.all_to_all(lows, 'replica', split_axis=0, concat_axis=0, tiled=True)  4.03 us
  transfers between devices with their start and end apart: 17, of which 5 were waited for; matrix products, arithmetic and copies ran while one was open for 6% of the time, Pallas kernels for 31%

profile of v7, /device:TPU:0, one launch (start us, length us, event | category | flops | bytes accessed | tf_op | source)
XLA Modules:
  0.0 63.5 jit_solution(6679167832810174641)
XLA Ops:
  0.0 3.0 %collective-permute-start.3 = (bf16[3,2,5120]{2,1,0:T(2,128)(2,1)}, bf16[3,2,5120]{2,1,0:T(2,128)(2,1)S(1)}, u32[]{:S(2)}, u32[]{:S(2)}) collective-permute-start(bf16[3,2,5120]{2,1,0:T(2,128)(2,1)} %param.9), channel_id=1, source_target_pairs={{0,4},{1,5},{2,6},{3,7},{4,0},{5,1},{6,2},{7,3},{8,12},{9,13},{10,... | collective-permute-start | bytes 184328 | tf_op jit(solution)/shard_map/ppermute | solution.py:233
  3.0 1.5 %collective-permute-start.1 = (bf16[3,2,5120]{2,1,0:T(2,128)(2,1)}, bf16[3,2,5120]{2,1,0:T(2,128)(2,1)S(1)}, u32[]{:S(2)}, u32[]{:S(2)}) collective-permute-start(bf16[3,2,5120]{2,1,0:T(2,128)(2,1)} %param.9), channel_id=1, source_target_pairs={{0,2},{1,3},{2,0},{3,1},{4,6},{5,7},{6,4},{7,5},{8,10},{9,11},{10,... | collective-permute-start | bytes 184328 | tf_op jit(solution)/shard_map/ppermute | solution.py:233
  4.5 0.0 collective-permute-start
  4.5 2.5 %collective-permute-start.11 = (bf16[3,2,5120]{2,1,0:T(2,128)(2,1)}, bf16[3,2,5120]{2,1,0:T(2,128)(2,1)S(1)}, u32[]{:S(2)}, u32[]{:S(2)}) collective-permute-start(bf16[3,2,5120]{2,1,0:T(2,128)(2,1)} %param.9), channel_id=1, source_target_pairs={{0,12},{1,13},{2,14},{3,15},{4,8},{5,9},{6,10},{7,11},{8,4},{9,5},... | collective-permute-start | bytes 184328 | tf_op jit(solution)/shard_map/ppermute | solution.py:233
  7.0 0.1 collective-permute-start.7
  7.1 0.7 %dynamic_slice.3 = s32[2]{0:T(128)S(1)} dynamic-slice(s32[32]{0:T(128)} %param.15, s32[]{:T(128)S(6)} %select_n.11), dynamic_slice_sizes={2} | dynamic-slice | bytes 20 | tf_op jit(solution)/shard_map/dynamic_slice | solution.py:667
  7.9 0.8 %select_reduce_fusion.1 = s32[32]{0:T(128)S(1)} fusion(s32[64]{0:T(128)} %param.13, s32[32]{0:T(128)} %param.14), kind=kLoop, calls=%fused_computation.2 | loop fusion | flops 6112 | bytes 512 | tf_op jit(solution)/shard_map/reduce_sum | solution.py:658
  8.7 0.1 broadcast_in_dim.52
  8.8 0.8 %select_reduce_fusion = s32[2,64]{1,0:T(2,128)S(1)} fusion(s32[2,32]{1,0:T(2,128)} %param.16), kind=kLoop, calls=%fused_computation | loop fusion | flops 12160 | bytes 768 | tf_op jit(solution)/shard_map/reduce_max | solution.py:113
  9.6 0.0 collective-permute-done.3
  9.6 0.6 collective-permute-start.5
  10.2 0.0 collective-permute-done
  10.2 0.5 collective-permute-start.2
  10.7 0.4 collective-permute-done.11
  11.1 1.1 %collective-permute-start.13 = (bf16[3,2,5120]{2,1,0:T(2,128)(2,1)S(1)}, bf16[3,2,5120]{2,1,0:T(2,128)(2,1)S(1)}, u32[]{:S(2)}, u32[]{:S(2)}) collective-permute-start(bf16[3,2,5120]{2,1,0:T(2,128)(2,1)S(1)} %collective-permute-done.11), channel_id=1, source_target_pairs={{0,2},{1,3},{2,0},{3,1},{4,6},{5,7},{6,4},{7,5},{8,10},{9,11},{10,... | collective-permute-start | bytes 184328 | tf_op jit(solution)/shard_map/ppermute | solution.py:233
  12.2 1.7 %collective-permute-done.7 = bf16[3,2,5120]{2,1,0:T(2,128)(2,1)S(1)} collective-permute-done((bf16[3,2,5120]{2,1,0:T(2,128)(2,1)}, bf16[3,2,5120]{2,1,0:T(2,128)(2,1)S(1)}, u32[]{:S(2)}, u32[]{:S(2)}) %collective-permute-start.7) | collective-permute-done | bytes 61472 | tf_op jit(solution)/shard_map/ppermute | solution.py:233
  14.0 0.5 collective-permute-start.9
  14.5 0.1 add.46
  14.6 0.1 sub.19.slot_ref
  14.7 0.1 collective-permute-start.12
  14.8 0.5 collective-permute-start.8
  15.3 0.0 collective-permute-done.2
  15.3 0.1 collective-permute-start.6
  15.4 0.4 collective-permute-start.14
  15.8 2.4 %collective-permute-done.9 = bf16[3,2,5120]{2,1,0:T(2,128)(2,1)S(1)} collective-permute-done((bf16[3,2,5120]{2,1,0:T(2,128)(2,1)S(1)}, bf16[3,2,5120]{2,1,0:T(2,128)(2,1)S(1)}, u32[]{:S(2)}, u32[]{:S(2)}) %collective-permute-start.9) | collective-permute-done | bytes 61472 | tf_op jit(solution)/shard_map/ppermute | solution.py:233
  18.2 0.0 collective-permute-start.10
  18.2 0.0 collective-permute-done.12
  18.2 0.0 collective-permute-done.8
  18.2 0.0 collective-permute-done.6
  18.2 1.2 %collective-permute-done.10 = bf16[3,2,5120]{2,1,0:T(2,128)(2,1)S(1)} collective-permute-done((bf16[3,2,5120]{2,1,0:T(2,128)(2,1)S(1)}, bf16[3,2,5120]{2,1,0:T(2,128)(2,1)S(1)}, u32[]{:S(2)}, u32[]{:S(2)}) %collective-permute-start.10) | collective-permute-done | bytes 61472 | tf_op jit(solution)/shard_map/ppermute | solution.py:233
  19.4 4.7 %low_rows.1 = (bf16[40,48,2,128]{3,2,1,0:T(2,128)(2,1)}, bf16[16,48,128]{2,1,0:T(8,128)(2,1)}) custom-call(s32[1]{0:T(128)} %bitcast.me_ref, s32[1,96]{1,0:T(1,128)S(1)} %sub.19.slot_ref, bf16[4,64,5120]{2,1,0:T(8,128)(2,1)} %down_ref.1, bf16[3,40,2,128]{3,2,1,0:T(2,128)(2,1)} %bitcast.75, bf16[3,40,2,128]{3,2,1,0:T(2,128)(2,1)S(1)} %bitcast.59, ...), custom_call_target="tpu_custom_call" | custom-call | flops 100000000 | bytes 4000000 | tf_op jit(solution)/shard_map/low_rows/pallas_call | solution.py:356
  24.1 4.0 %all-to-all-start = ((bf16[16,48,128]{2,1,0:T(8,128)(2,1)}), bf16[16,48,128]{2,1,0:T(8,128)(2,1)S(1)}, u32[]{:S(2)}, u32[]{:S(2)}) async-start(bf16[16,48,128]{2,1,0:T(8,128)(2,1)} %get-tuple-element.11), calls=%async_computation | async-start | bytes 393216 | tf_op jit(solution)/shard_map/all_to_all | solution.py:680
  28.2 0.1 broadcast_in_dim_reshape.4.stored_ref
  28.3 0.1 fusion
  28.4 8.6 %project.1 = (bf16[16,9,3,2,128]{4,3,2,1,0:T(2,128)(2,1)}, f32[96,320]{1,0:T(8,128)}) custom-call(bf16[40,48,2,128]{3,2,1,0:T(2,128)(2,1)} %get-tuple-element.12.x_ref, bf16[3,320,5120]{2,1,0:T(8,128)(2,1)} %bitcast.72), custom_call_target="tpu_custom_call" | custom-call | flops 1000000000 | bytes 11000000 | tf_op jit(solution)/shard_map/project/pallas_call | solution.py:448
  37.0 0.2 all-to-all-done.low_ref
  37.1 4.5 %update_values.1 = bf16[16,9,3,2,128]{4,3,2,1,0:T(2,128)(2,1)} custom-call(s32[96,1]{1,0:T(8,128)S(1)} %broadcast_in_dim_reshape.4.stored_ref, bf16[16,48,128]{2,1,0:T(8,128)(2,1)S(1)} %all-to-all-done.low_ref, f32[96,320]{1,0:T(8,128)} %get-tuple-element.13.base_ref, bf16[4096,320]{1,0:T(8,128)(2,1)} %bitcast.74, ...), custom_call_target="tpu_custom_call", output_to_operand_aliasing={{}: (4, {})} | custom-call | flops 300000000 | bytes 4000000 | tf_op jit(solution)/shard_map/update_values/pallas_call | solution.py:515
  41.7 5.9 %all-to-all-start.1 = ((bf16[16,9,3,2,128]{4,3,2,1,0:T(2,128)(2,1)}), bf16[16,9,3,2,128]{4,3,2,1,0:T(2,128)(2,1)S(1)}, u32[]{:S(2)}, u32[]{:S(2)}) async-start(bf16[16,9,3,2,128]{4,3,2,1,0:T(2,128)(2,1)} %update_values.1), calls=%async_computation.1 | async-start | bytes 442368 | tf_op jit(solution)/shard_map/all_to_all | solution.py:683
  47.6 0.1 and.12
  47.7 0.1 and.13
  47.8 0.1 add.50
  47.9 0.1 add.47
  48.0 0.1 add.48
  48.1 11.2 %cache_by_head.1 = (bf16[40,256,128]{2,1,0:T(8,128)(2,1)S(1)}, bf16[40,256,128]{2,1,0:T(8,128)(2,1)}) custom-call(bf16[256,40,2,128]{3,2,1,0:T(2,128)(2,1)} %bitcast.73), custom_call_target="tpu_custom_call" | custom-call | bytes 12000000 | tf_op jit(solution)/shard_map/cache_by_head/pallas_call | solution.py:290
  59.4 0.1 pad_maximum_fusion
  59.4 0.1 and_convert_fusion.live_ref
  59.5 0.0 all-to-all-done.1.pieces_ref
  59.5 3.9 %attention.1 = bf16[3,40,2,128]{3,2,1,0:T(2,128)(2,1)} custom-call(f32[8,128]{1,0:T(8,128)S(1)} %get-tuple-element.20.cos_ref, f32[8,128]{1,0:T(8,128)S(1)} %get-tuple-element.21.sin_ref, s32[2,256]{1,0:T(2,128)S(1)} %and_convert_fusion.live_ref, bf16[16,9,3,2,128]{4,3,2,1,0:T(2,128)(2,1)S(1)} %all-to-all-done.1.pieces_ref, ...), custom_call_target="tpu_custom_call" | custom-call | flops 1000000000 | bytes 6000000 | tf_op jit(solution)/shard_map/attention/pallas_call | solution.py:622
  (15 shorter events, 0.1 us)
Async XLA Ops:
  0.0 9.6 %collective-permute-start.3 = (bf16[3,2,5120]{2,1,0:T(2,128)(2,1)}, bf16[3,2,5120]{2,1,0:T(2,128)(2,1)S(1)}, u32[]{:S(2)}, u32[]{:S(2)}) collective-permute-start(bf16[3,2,5120]{2,1,0:T(2,128)(2,1)} %param.9), channel_id=1, source_target_pairs={{0,4},{1,5},{2,6},{3,7},{4,0},{5,1},{6,2},{7,3},{8,12},{9,13},{10,... | collective-permute-start | bytes 184328 | tf_op jit(solution)/shard_map/ppermute | solution.py:233
  3.0 7.2 %collective-permute-start.1 = (bf16[3,2,5120]{2,1,0:T(2,128)(2,1)}, bf16[3,2,5120]{2,1,0:T(2,128)(2,1)S(1)}, u32[]{:S(2)}, u32[]{:S(2)}) collective-permute-start(bf16[3,2,5120]{2,1,0:T(2,128)(2,1)} %param.9), channel_id=1, source_target_pairs={{0,2},{1,3},{2,0},{3,1},{4,6},{5,7},{6,4},{7,5},{8,10},{9,11},{10,... | collective-permute-start | bytes 184328 | tf_op jit(solution)/shard_map/ppermute | solution.py:233
  4.5 5.6 %collective-permute-start = (bf16[3,2,5120]{2,1,0:T(2,128)(2,1)}, bf16[3,2,5120]{2,1,0:T(2,128)(2,1)S(1)}, u32[]{:S(2)}, u32[]{:S(2)}) collective-permute-start(bf16[3,2,5120]{2,1,0:T(2,128)(2,1)} %param.9), channel_id=1, source_target_pairs={{0,1},{1,0},{2,3},{3,2},{4,5},{5,4},{6,7},{7,6},{8,9},{9,8},{10,11... | collective-permute-start | bytes 184328 | tf_op jit(solution)/shard_map/ppermute | solution.py:233
  4.5 6.5 %collective-permute-start.11 = (bf16[3,2,5120]{2,1,0:T(2,128)(2,1)}, bf16[3,2,5120]{2,1,0:T(2,128)(2,1)S(1)}, u32[]{:S(2)}, u32[]{:S(2)}) collective-permute-start(bf16[3,2,5120]{2,1,0:T(2,128)(2,1)} %param.9), channel_id=1, source_target_pairs={{0,12},{1,13},{2,14},{3,15},{4,8},{5,9},{6,10},{7,11},{8,4},{9,5},... | collective-permute-start | bytes 184328 | tf_op jit(solution)/shard_map/ppermute | solution.py:233
  7.0 6.9 %collective-permute-start.7 = (bf16[3,2,5120]{2,1,0:T(2,128)(2,1)}, bf16[3,2,5120]{2,1,0:T(2,128)(2,1)S(1)}, u32[]{:S(2)}, u32[]{:S(2)}) collective-permute-start(bf16[3,2,5120]{2,1,0:T(2,128)(2,1)} %param.9), channel_id=1, source_target_pairs={{0,8},{1,9},{2,10},{3,11},{4,12},{5,13},{6,14},{7,15},{8,0},{9,1},... | collective-permute-start | bytes 184328 | tf_op jit(solution)/shard_map/ppermute | solution.py:233
  9.6 5.1 %collective-permute-start.5 = (bf16[3,2,5120]{2,1,0:T(2,128)(2,1)S(1)}, bf16[3,2,5120]{2,1,0:T(2,128)(2,1)S(1)}, u32[]{:S(2)}, u32[]{:S(2)}) collective-permute-start(bf16[3,2,5120]{2,1,0:T(2,128)(2,1)S(1)} %collective-permute-done.3), channel_id=1, source_target_pairs={{0,2},{1,3},{2,0},{3,1},{4,6},{5,7},{6,4},{7,5},{8,10},{9,11},{10,... | collective-permute-start | bytes 184328 | tf_op jit(solution)/shard_map/ppermute | solution.py:233
  10.2 4.6 %collective-permute-start.4 = (bf16[3,2,5120]{2,1,0:T(2,128)(2,1)S(1)}, bf16[3,2,5120]{2,1,0:T(2,128)(2,1)S(1)}, u32[]{:S(2)}, u32[]{:S(2)}) collective-permute-start(bf16[3,2,5120]{2,1,0:T(2,128)(2,1)S(1)} %collective-permute-done.3), channel_id=1, source_target_pairs={{0,1},{1,0},{2,3},{3,2},{4,5},{5,4},{6,7},{7,6},{8,9},{9,8},{10,11... | collective-permute-start | bytes 184328 | tf_op jit(solution)/shard_map/ppermute | solution.py:233
  10.2 5.1 %collective-permute-start.2 = (bf16[3,2,5120]{2,1,0:T(2,128)(2,1)S(1)}, bf16[3,2,5120]{2,1,0:T(2,128)(2,1)S(1)}, u32[]{:S(2)}, u32[]{:S(2)}) collective-permute-start(bf16[3,2,5120]{2,1,0:T(2,128)(2,1)S(1)} %collective-permute-done.1), channel_id=1, source_target_pairs={{0,1},{1,0},{2,3},{3,2},{4,5},{5,4},{6,7},{7,6},{8,9},{9,8},{10,11... | collective-permute-start | bytes 184328 | tf_op jit(solution)/shard_map/ppermute | solution.py:233
  11.1 4.3 %collective-permute-start.13 = (bf16[3,2,5120]{2,1,0:T(2,128)(2,1)S(1)}, bf16[3,2,5120]{2,1,0:T(2,128)(2,1)S(1)}, u32[]{:S(2)}, u32[]{:S(2)}) collective-permute-start(bf16[3,2,5120]{2,1,0:T(2,128)(2,1)S(1)} %collective-permute-done.11), channel_id=1, source_target_pairs={{0,2},{1,3},{2,0},{3,1},{4,6},{5,7},{6,4},{7,5},{8,10},{9,11},{10,... | collective-permute-start | bytes 184328 | tf_op jit(solution)/shard_map/ppermute | solution.py:233
  14.0 4.2 %collective-permute-start.9 = (bf16[3,2,5120]{2,1,0:T(2,128)(2,1)S(1)}, bf16[3,2,5120]{2,1,0:T(2,128)(2,1)S(1)}, u32[]{:S(2)}, u32[]{:S(2)}) collective-permute-start(bf16[3,2,5120]{2,1,0:T(2,128)(2,1)S(1)} %collective-permute-done.7), channel_id=1, source_target_pairs={{0,2},{1,3},{2,0},{3,1},{4,6},{5,7},{6,4},{7,5},{8,10},{9,11},{10,... | collective-permute-start | bytes 184328 | tf_op jit(solution)/shard_map/ppermute | solution.py:233
  14.7 3.5 %collective-permute-start.12 = (bf16[3,2,5120]{2,1,0:T(2,128)(2,1)S(1)}, bf16[3,2,5120]{2,1,0:T(2,128)(2,1)S(1)}, u32[]{:S(2)}, u32[]{:S(2)}) collective-permute-start(bf16[3,2,5120]{2,1,0:T(2,128)(2,1)S(1)} %collective-permute-done.11), channel_id=1, source_target_pairs={{0,1},{1,0},{2,3},{3,2},{4,5},{5,4},{6,7},{7,6},{8,9},{9,8},{10,11... | collective-permute-start | bytes 184328 | tf_op jit(solution)/shard_map/ppermute | solution.py:233
  14.8 3.4 %collective-permute-start.8 = (bf16[3,2,5120]{2,1,0:T(2,128)(2,1)S(1)}, bf16[3,2,5120]{2,1,0:T(2,128)(2,1)S(1)}, u32[]{:S(2)}, u32[]{:S(2)}) collective-permute-start(bf16[3,2,5120]{2,1,0:T(2,128)(2,1)S(1)} %collective-permute-done.7), channel_id=1, source_target_pairs={{0,1},{1,0},{2,3},{3,2},{4,5},{5,4},{6,7},{7,6},{8,9},{9,8},{10,11... | collective-permute-start | bytes 184328 | tf_op jit(solution)/shard_map/ppermute | solution.py:233
  15.3 2.9 %collective-permute-start.6 = (bf16[3,2,5120]{2,1,0:T(2,128)(2,1)S(1)}, bf16[3,2,5120]{2,1,0:T(2,128)(2,1)S(1)}, u32[]{:S(2)}, u32[]{:S(2)}) collective-permute-start(bf16[3,2,5120]{2,1,0:T(2,128)(2,1)S(1)} %collective-permute-done.5), channel_id=1, source_target_pairs={{0,1},{1,0},{2,3},{3,2},{4,5},{5,4},{6,7},{7,6},{8,9},{9,8},{10,11... | collective-permute-start | bytes 184328 | tf_op jit(solution)/shard_map/ppermute | solution.py:233
  15.4 2.9 %collective-permute-start.14 = (bf16[3,2,5120]{2,1,0:T(2,128)(2,1)S(1)}, bf16[3,2,5120]{2,1,0:T(2,128)(2,1)S(1)}, u32[]{:S(2)}, u32[]{:S(2)}) collective-permute-start(bf16[3,2,5120]{2,1,0:T(2,128)(2,1)S(1)} %collective-permute-done.13), channel_id=1, source_target_pairs={{0,1},{1,0},{2,3},{3,2},{4,5},{5,4},{6,7},{7,6},{8,9},{9,8},{10,11... | collective-permute-start | bytes 184328 | tf_op jit(solution)/shard_map/ppermute | solution.py:233
  18.2 1.2 %collective-permute-start.10 = (bf16[3,2,5120]{2,1,0:T(2,128)(2,1)S(1)}, bf16[3,2,5120]{2,1,0:T(2,128)(2,1)S(1)}, u32[]{:S(2)}, u32[]{:S(2)}) collective-permute-start(bf16[3,2,5120]{2,1,0:T(2,128)(2,1)S(1)} %collective-permute-done.9), channel_id=1, source_target_pairs={{0,1},{1,0},{2,3},{3,2},{4,5},{5,4},{6,7},{7,6},{8,9},{9,8},{10,11... | collective-permute-start | bytes 184328 | tf_op jit(solution)/shard_map/ppermute | solution.py:233
  24.1 13.0 %all-to-all-start = ((bf16[16,48,128]{2,1,0:T(8,128)(2,1)}), bf16[16,48,128]{2,1,0:T(8,128)(2,1)S(1)}, u32[]{:S(2)}, u32[]{:S(2)}) async-start(bf16[16,48,128]{2,1,0:T(8,128)(2,1)} %get-tuple-element.11), calls=%async_computation | async-start | bytes 393216 | tf_op jit(solution)/shard_map/all_to_all | solution.py:680
  41.7 17.8 %all-to-all-start.1 = ((bf16[16,9,3,2,128]{4,3,2,1,0:T(2,128)(2,1)}), bf16[16,9,3,2,128]{4,3,2,1,0:T(2,128)(2,1)S(1)}, u32[]{:S(2)}, u32[]{:S(2)}) async-start(bf16[16,9,3,2,128]{4,3,2,1,0:T(2,128)(2,1)} %update_values.1), calls=%async_computation.1 | async-start | bytes 442368 | tf_op jit(solution)/shard_map/all_to_all | solution.py:683

commit v8 on v6

--- a/solution.py
+++ b/solution.py
@@ -257,29 +257,29 @@
         copy.wait()
 
 
-CACHE_AHEAD = 16
+CACHE_PARTS = 4
 
 
 def cache_kernel(pool_ref, keys_ref, values_ref, raw, values, sem, out_sem):
     heads, tokens = raw.shape[:2]
-    copies = [pltpu.make_async_copy(pool_ref.at[:, h], raw.at[h], sem.at[h]) for h in range(heads)]
-    start_all(copies[:CACHE_AHEAD])
+    copies = start_all([pltpu.make_async_copy(pool_ref.at[:, h], raw.at[h], sem.at[h]) for h in range(heads)])
     rows = raw.reshape(heads, 2 * tokens, HD)
     to = lax.broadcasted_iota(jnp.int32, (2 * tokens, 2 * tokens), 0)
     source = lax.broadcasted_iota(jnp.int32, (2 * tokens, 2 * tokens), 1)
     wanted = jnp.where(to < tokens, 2 * to, 2 * (to - tokens) + 1)
     pick = jnp.where(source == wanted, 1.0, 0.0).astype(jnp.bfloat16)
     sent = []
-    for h in range(0, heads, 2):
-        for ahead in range(h + CACHE_AHEAD, min(h + CACHE_AHEAD + 2, heads)):
-            copies[ahead].start()
-        wait_all(copies[h : h + 2])
-        both = jnp.concatenate([rows[h], rows[h + 1]], axis=1)
-        made = jnp.dot(pick, both, preferred_element_type=jnp.float32).astype(jnp.bfloat16)
-        for i in range(2):
-            keys_ref[h + i] = made[:tokens, i * HD : (i + 1) * HD]
-            values[h + i] = made[tokens:, i * HD : (i + 1) * HD]
-        sent += start_all([pltpu.make_async_copy(values.at[h : h + 2], values_ref.at[h : h + 2], out_sem.at[h // 2])])
+    part = heads // CACHE_PARTS
+    for p in range(CACHE_PARTS):
+        wait_all(copies[p * part : (p + 1) * part])
+        for h in range(p * part, (p + 1) * part, 2):
+            both = jnp.concatenate([rows[h], rows[h + 1]], axis=1)
+            made = jnp.dot(pick, both, preferred_element_type=jnp.float32).astype(jnp.bfloat16)
+            for i in range(2):
+                keys_ref[h + i] = made[:tokens, i * HD : (i + 1) * HD]
+                values[h + i] = made[tokens:, i * HD : (i + 1) * HD]
+        span = slice(p * part, (p + 1) * part)
+        sent += start_all([pltpu.make_async_copy(values.at[span], values_ref.at[span], out_sem.at[p])])
     wait_all(sent)
 
 
@@ -297,7 +297,7 @@
             pltpu.VMEM((heads, tokens, 2, HD), pool.dtype),
             pltpu.VMEM((heads, tokens, HD), pool.dtype),
             pltpu.SemaphoreType.DMA((heads,)),
-            pltpu.SemaphoreType.DMA((heads // 2,)),
+            pltpu.SemaphoreType.DMA((CACHE_PARTS,)),
         ],
         compiler_params=pltpu.CompilerParams(vmem_limit_bytes=16 * 2**20),
         cost_estimate=pl.CostEstimate(flops=0, bytes_accessed=12 * 10**6, transcendentals=0),
@@ -310,12 +310,13 @@
 
 
 def low_kernel(count, me_ref, slot_ref, down_ref, *refs):
-    blocks, (x_ref, low_ref, x_buf, maps, made_ref, sem, low_sem, own_sem) = refs[:count], refs[count:]
+    blocks, (x_ref, low_ref, x_buf, maps, made_ref, sem, low_sem, down_sem, own_sem) = refs[:count], refs[count:]
     me = me_ref[0]
     steps = blocks[0].shape[0]
     holders, rank, width = down_ref.shape
-    fetch = pltpu.make_async_copy(down_ref, maps, own_sem.at[0])
-    fetch.start()
+    fetches = start_all(
+        [pltpu.make_async_copy(down_ref.at[h], maps.at[h], down_sem.at[h]) for h in range(holders)]
+    )
     copies = []
     for k, block in enumerate(blocks):
         for t in range(steps):
@@ -323,12 +324,12 @@
                 pltpu.make_async_copy(block.at[t], x_buf.at[:, (me ^ k) * steps + t], sem.at[k * steps + t])
             )
     wait_all(start_all(copies))
-    keep = pltpu.make_async_copy(x_buf, x_ref, own_sem.at[1])
+    keep = pltpu.make_async_copy(x_buf, x_ref, own_sem)
     keep.start()
     chunks, pairs = x_buf.shape[:2]
     rows = 2 * pairs
     x = lanes_of(x_buf.reshape(chunks, rows, HD))
-    fetch.wait()
+    wait_all(fetches)
     made = lax.dot_general(
         maps.reshape(holders * rank, width)[...], x, CONTRACT_LANES, preferred_element_type=jnp.float32
     )
@@ -361,7 +362,8 @@
             pltpu.VMEM((rows // 2, 2 * rank), jnp.bfloat16),
             pltpu.SemaphoreType.DMA((count * steps,)),
             pltpu.SemaphoreType.DMA((count,)),
-            pltpu.SemaphoreType.DMA((2,)),
+            pltpu.SemaphoreType.DMA((down.shape[0],)),
+            pltpu.SemaphoreType.DMA,
         ],
         compiler_params=pltpu.CompilerParams(vmem_limit_bytes=16 * 2**20),
         cost_estimate=pl.CostEstimate(flops=10**8, bytes_accessed=4 * 10**6, transcendentals=0),
@@ -395,7 +397,9 @@
 PROJECT_AHEAD = 3
 
 
-def project_kernel(x_ref, w_ref, send_ref, base_ref, x_buf, w_buf, total, buf, base, x_sem, w_sem, sem, base_sem):
+def project_kernel(
+    stored_ref, x_ref, w_ref, up_ref, send_ref, base_ref, maps_ref, x_buf, w_buf, total, buf, base, x_sem, w_sem, sem, base_sem, up_sem
+):
     chunks, pairs = x_buf.shape[:2]
     rows = 2 * pairs
     columns, width = w_ref.shape[1:]
@@ -408,6 +412,13 @@
         for p in range(parts)
     ]
     start_all(fetches[:PROJECT_AHEAD])
+    rank = up_ref.shape[1]
+    maps = start_all(
+        [
+            pltpu.make_async_copy(up_ref.at[stored_ref[q]], maps_ref.at[q * rank : (q + 1) * rank], up_sem.at[q])
+            for q in range(stored_ref.shape[0])
+        ]
+    )
     fetch_x.wait()
     x_rows = x_buf.reshape(chunks, rows, HD)
     for p in range(parts):
@@ -427,9 +438,10 @@
     keep.start()
     wait_all(sent)
     keep.wait()
-
-
-def project(x, weight, count):
+    wait_all(maps)
+
+
+def project(stored, x, weight, up, count):
     chunks, pairs = x.shape[:2]
     columns, width = weight.shape[1:]
     each = -(-columns // HD)
@@ -439,9 +451,10 @@
         out_shape=(
             pltpu.HBM((count, 3 * each, pairs // count, 2, HD), jnp.bfloat16),
             pltpu.HBM((2 * pairs, columns), jnp.float32),
+            pltpu.VMEM((stored.shape[0] * up.shape[1], columns), up.dtype),
         ),
-        in_specs=[HBM, HBM],
-        out_specs=(HBM, HBM),
+        in_specs=[SMEM, HBM, HBM, HBM],
+        out_specs=(HBM, HBM, VMEM),
         scratch_shapes=[
             pltpu.VMEM(x.shape, jnp.bfloat16),
             pltpu.VMEM((parts, 3, columns, PROJECT_CHUNK), jnp.bfloat16),
@@ -452,27 +465,19 @@
             pltpu.SemaphoreType.DMA((parts,)),
             pltpu.SemaphoreType.DMA((count,)),
             pltpu.SemaphoreType.DMA,
+            pltpu.SemaphoreType.DMA((stored.shape[0],)),
         ],
         compiler_params=pltpu.CompilerParams(vmem_limit_bytes=24 * 2**20),
         cost_estimate=pl.CostEstimate(flops=10**9, bytes_accessed=11 * 10**6, transcendentals=0),
         name="project",
-    )(in_hbm(x), in_hbm(weight))
-
-
-UPDATE_PARTS = 8
-UPDATE_AHEAD = 4
-
-
-def update_kernel(stored_ref, low_ref, base_ref, up_ref, send_in, send_ref, base, up, buf, base_sem, up_sem, sem):
+    )(stored, in_hbm(x), in_hbm(weight), in_hbm(up))
+
+
+def update_kernel(low_ref, base_ref, maps_ref, send_in, send_ref, base, buf, base_sem, sem):
     count, half, packed = low_ref.shape
     rank = packed // 2
     rows = 2 * half
-    height = up_ref.shape[0] // UPDATE_PARTS
-    fetches = [
-        pltpu.make_async_copy(up_ref.at[p * height : (p + 1) * height], up.at[p], up_sem.at[p])
-        for p in range(UPDATE_PARTS)
-    ]
-    start_all(fetches[:UPDATE_AHEAD])
+    per = rows // count
     fetch_base = pltpu.make_async_copy(base_ref, base, base_sem)
     fetch_base.start()
     low = low_ref[0].astype(jnp.float32)
@@ -481,44 +486,37 @@
     low = jnp.concatenate([low[:, :rank], low[:, rank:]], axis=0)
     batch = 256 // rank
     spread = jnp.concatenate([low] * batch, axis=1)
+    row = lax.broadcasted_iota(jnp.int32, (rows, batch * rank), 0)
     which = lax.broadcasted_iota(jnp.int32, (rows, batch * rank), 1) // rank
-    ahead = stored_ref[...] - which
+    ahead = (row // per) * 2 + row % 2 - which
     total = jnp.zeros(base.shape, jnp.float32)
-    for p in range(UPDATE_PARTS):
-        fetches[p].wait()
-        start_all(fetches[p + UPDATE_AHEAD : p + UPDATE_AHEAD + 1])
-        for a in range(0, height // rank, batch):
-            wide = jnp.where(ahead == p * (height // rank) + a, spread, 0.0).astype(jnp.bfloat16)
-            total = total + jnp.dot(
-                wide, up[p, a * rank : (a + batch) * rank], preferred_element_type=jnp.float32
-            )
+    for a in range(0, maps_ref.shape[0] // rank, batch):
+        wide = jnp.where(ahead == a, spread, 0.0).astype(jnp.bfloat16)
+        total = total + jnp.dot(wide, maps_ref[a * rank : (a + batch) * rank], preferred_element_type=jnp.float32)
     fetch_base.wait()
     put_chunks(buf.reshape(buf.shape[0], rows, HD), 0, base[...] + adapter_scale * total)
     wait_all(send_blocks(buf, send_ref, send_ref.shape[1] - buf.shape[0], sem))
 
 
-def update_values(stored, lows, base, up, send):
+def update_values(lows, base, maps, send):
     count, chunks = send.shape[:2]
     rows, columns = base.shape
-    height = up.shape[0] // UPDATE_PARTS
     return pl.pallas_call(
         update_kernel,
         out_shape=pltpu.HBM(send.shape, send.dtype),
-        in_specs=[VMEM, VMEM, HBM, HBM, HBM],
+        in_specs=[VMEM, HBM, VMEM, HBM],
         out_specs=HBM,
         scratch_shapes=[
             pltpu.VMEM(base.shape, jnp.float32),
-            pltpu.VMEM((UPDATE_PARTS, height, columns), jnp.bfloat16),
             pltpu.VMEM((chunks // 3, rows // 2, 2, HD), jnp.bfloat16),
             pltpu.SemaphoreType.DMA,
-            pltpu.SemaphoreType.DMA((UPDATE_PARTS,)),
             pltpu.SemaphoreType.DMA((count,)),
         ],
-        input_output_aliases={4: 0},
-        compiler_params=pltpu.CompilerParams(vmem_limit_bytes=16 * 2**20),
+        input_output_aliases={3: 0},
+        compiler_params=pltpu.CompilerParams(vmem_limit_bytes=8 * 2**20),
         cost_estimate=pl.CostEstimate(flops=3 * 10**8, bytes_accessed=4 * 10**6, transcendentals=0),
         name="update_values",
-    )(stored, lows, in_hbm(base), in_hbm(up), in_hbm(send))
+    )(lows, in_hbm(base), maps, in_hbm(send))
 
 
 def attend_kernel(cos_ref, sin_ref, live_ref, pieces_ref, keys_ref, values_ref, out_ref, values_buf, kn_ref, vn_ref, sem):
@@ -644,9 +642,13 @@
     tokens = pool_pages * page_len
     keys, values = cache_by_head(key_value_pool.reshape(tokens, 2, heads, HD).transpose(0, 2, 1, 3))
 
-    held = {0: hidden}
-    for masks in (range(4, count, 4), (2,), (1,)):
-        held.update({k ^ m: trade(v, m, count) for k, v in list(held.items()) for m in masks})
+    held = {m: trade(hidden, m, count) for m in range(8, count, 4)}
+    held[1] = trade(hidden, 1, count)
+    held[0], held[1] = lax.optimization_barrier((hidden, held[1]))
+    held[4] = trade(held[0], 4, count)
+    held[2] = trade(held[0], 2, count)
+    held.update({m | 2: trade(held[m], 2, count) for m in range(4, count, 4)})
+    held.update({m | 1: trade(held[m], 1, count) for m in range(2, count, 2)})
     blocks = [
         held[k].reshape(steps, req_dev, heads, HD).transpose(0, 2, 1, 3) for k in range(count)
     ]
@@ -660,14 +662,13 @@
         ),
         axis=1,
     )
-    stored = jnp.broadcast_to(stored.reshape(count, 1, req_dev), (count, steps, req_dev)).reshape(-1)
-
-    x, lows = low_of(
-        me.astype(jnp.int32).reshape(1), blocks, (stored - me * holder_count)[None, :], adapter_down_maps
-    )
+    slot = (stored - me * holder_count).reshape(count, 1, req_dev)
+    slot = jnp.broadcast_to(slot, (count, steps, req_dev)).reshape(1, -1)
+
+    x, lows = low_of(me.astype(jnp.int32).reshape(1), blocks, slot, adapter_down_maps)
     lows = lax.all_to_all(lows, "replica", split_axis=0, concat_axis=0, tiled=True)
-    send, base = project(x, query_key_value_weight.transpose(0, 2, 1), count)
-    send = update_values(stored[:, None], lows, base, adapter_up_maps.reshape(adapter_count * rank, -1), send)
+    send, base, maps = project(stored, x, query_key_value_weight.transpose(0, 2, 1), adapter_up_maps, count)
+    send = update_values(lows, base, maps, send)
     pieces = lax.all_to_all(send, "replica", split_axis=0, concat_axis=0, tiled=True)
 
     my_lengths = lax.dynamic_slice_in_dim(lengths, me * req_dev, req_dev)

time: 61.7 us -> 58.9 us (0.955)
  Pallas kernels: 30.5 us -> 26 us
  starting transfers between devices: 19.7 us -> 22.7 us
  waiting for transfers between devices: 7.04 us -> 5.97 us
    pallas_call x1, Pallas kernels: 11.2 us -> 6.9 us  [cache_by_head(): pl.pallas_call(cache_kernel, out_shape=(jax.ShapeDtypeStruct((heads, toke...]
    all_to_all x1, waiting for transfers between devices: 0.01 us -> 1.79 us  [chip_plan(): lax.all_to_all(send, 'replica', split_axis=0, concat_axis=0, tiled=True)]
    pallas_call x1, Pallas kernels: 3.88 us -> 2.15 us  [update_values(): pl.pallas_call(update_kernel, out_shape=pltpu.HBM(send.shape, send.dtype)...]
    ppermute x15, waiting for transfers between devices: 5.73 us -> 4.17 us  [trade(): return lax.ppermute(value, 'replica', [(i, i ^ mask) for i in range(count)])]
    pallas_call x1, Pallas kernels: 7.45 us -> 8.91 us  [project(): pl.pallas_call(project_kernel, out_shape=(pltpu.HBM((count, 3 * each, pai...]
    all_to_all x1, waiting for transfers between devices: 1.31 us -> 0.01 us  [chip_plan(): lax.all_to_all(lows, 'replica', split_axis=0, concat_axis=0, tiled=True)]
    all_to_all x1, starting transfers between devices: 4.73 us -> 6.03 us  [chip_plan(): lax.all_to_all(send, 'replica', split_axis=0, concat_axis=0, tiled=True)]
    all_to_all x1, starting transfers between devices: 4.03 us -> 5.22 us  [chip_plan(): lax.all_to_all(lows, 'replica', split_axis=0, concat_axis=0, tiled=True)]
  transfers between devices with their start and end apart: 17 -> 17, of which waited for: 5 -> 6; matrix products, arithmetic and copies ran while one was open for 6% -> 6% of each run, Pallas kernels for 31% -> 27%
where the time goes in v8:
time: 58.9 us; the launch traced here: 58.4 us
  Pallas kernels  26 us (44%)
  starting transfers between devices  22.7 us (39%)
  waiting for transfers between devices  5.97 us (10%)
  other arithmetic  1.91 us (3%)
  local copies, waits for them, and re-layouts  1.54 us (3%)
    ppermute x15, starting transfers between devices, trade(): return lax.ppermute(value, 'replica', [(i, i ^ mask) for i in range(count)])  11.4 us
    pallas_call x1, Pallas kernels, project(): pl.pallas_call(project_kernel, out_shape=(pltpu.HBM((count, 3 * each, pai...  8.91 us
    pallas_call x1, Pallas kernels, cache_by_head(): pl.pallas_call(cache_kernel, out_shape=(jax.ShapeDtypeStruct((heads, toke...  6.9 us
    all_to_all x1, starting transfers between devices, chip_plan(): lax.all_to_all(send, 'replica', split_axis=0, concat_axis=0, tiled=True)  6.03 us
    all_to_all x1, starting transfers between devices, chip_plan(): lax.all_to_all(lows, 'replica', split_axis=0, concat_axis=0, tiled=True)  5.22 us
    pallas_call x1, Pallas kernels, low_of(): pl.pallas_call(functools.partial(low_kernel, count), out_shape=(pltpu.HBM...  4.21 us
    ppermute x15, waiting for transfers between devices, trade(): return lax.ppermute(value, 'replica', [(i, i ^ mask) for i in range(count)])  4.17 us
    pallas_call x1, Pallas kernels, attend(): pl.pallas_call(attend_kernel, out_shape=jax.ShapeDtypeStruct((steps, head...  3.86 us
  transfers between devices with their start and end apart: 17, of which 6 were waited for; matrix products, arithmetic and copies ran while one was open for 6% of the time, Pallas kernels for 27%

profile of v8, /device:TPU:0, one launch (start us, length us, event | category | flops | bytes accessed | tf_op | source)
XLA Modules:
  0.0 58.4 jit_solution(2752793802029254470)
XLA Ops:
  0.0 0.5 collective-permute-start
  0.5 4.6 %collective-permute-start.11 = (bf16[3,2,5120]{2,1,0:T(2,128)(2,1)}, bf16[3,2,5120]{2,1,0:T(2,128)(2,1)S(1)}, u32[]{:S(2)}, u32[]{:S(2)}) collective-permute-start(bf16[3,2,5120]{2,1,0:T(2,128)(2,1)} %param.9), channel_id=1, source_target_pairs={{0,12},{1,13},{2,14},{3,15},{4,8},{5,9},{6,10},{7,11},{8,4},{9,5},... | collective-permute-start | bytes 184328 | tf_op jit(solution)/shard_map/ppermute | solution.py:233
  5.1 0.0 collective-permute-start.7
  5.1 0.8 %select_reduce_fusion = s32[2,64]{1,0:T(2,128)S(1)} fusion(s32[2,32]{1,0:T(2,128)} %param.16), kind=kLoop, calls=%fused_computation | loop fusion | flops 12160 | bytes 768 | tf_op jit(solution)/shard_map/reduce_max | solution.py:113
  5.8 0.7 %dynamic_slice.3 = s32[2]{0:T(128)S(1)} dynamic-slice(s32[32]{0:T(128)} %param.15, s32[]{:T(128)S(6)} %select_n.11), dynamic_slice_sizes={2} | dynamic-slice | bytes 20 | tf_op jit(solution)/shard_map/dynamic_slice | solution.py:674
  6.6 0.0 collective-permute-done
  6.6 0.7 %collective-permute-start.3 = (bf16[3,2,5120]{2,1,0:T(2,128)(2,1)}, bf16[3,2,5120]{2,1,0:T(2,128)(2,1)S(1)}, u32[]{:S(2)}, u32[]{:S(2)}) collective-permute-start(bf16[3,2,5120]{2,1,0:T(2,128)(2,1)} %param.9), channel_id=1, source_target_pairs={{0,4},{1,5},{2,6},{3,7},{4,0},{5,1},{6,2},{7,3},{8,12},{9,13},{10,... | collective-permute-start | bytes 184328 | tf_op jit(solution)/shard_map/ppermute | solution.py:233
  7.3 1.7 %collective-permute-start.1 = (bf16[3,2,5120]{2,1,0:T(2,128)(2,1)}, bf16[3,2,5120]{2,1,0:T(2,128)(2,1)S(1)}, u32[]{:S(2)}, u32[]{:S(2)}) collective-permute-start(bf16[3,2,5120]{2,1,0:T(2,128)(2,1)} %param.9), channel_id=1, source_target_pairs={{0,2},{1,3},{2,0},{3,1},{4,6},{5,7},{6,4},{7,5},{8,10},{9,11},{10,... | collective-permute-start | bytes 184328 | tf_op jit(solution)/shard_map/ppermute | solution.py:233
  8.9 0.8 %select_reduce_fusion.1.stored_ref = s32[32]{0:T(128)S(1)} fusion(s32[64]{0:T(128)} %param.13, s32[32]{0:T(128)} %param.14), kind=kLoop, calls=%fused_computation.2 | loop fusion | flops 6112 | bytes 512 | tf_op jit(solution)/shard_map/reduce_sum | solution.py:657
  9.8 0.0 collective-permute-done.11
  9.8 0.4 collective-permute-start.13
  10.2 0.0 collective-permute-start.12
  10.2 0.9 %collective-permute-done.7 = bf16[3,2,5120]{2,1,0:T(2,128)(2,1)S(1)} collective-permute-done((bf16[3,2,5120]{2,1,0:T(2,128)(2,1)}, bf16[3,2,5120]{2,1,0:T(2,128)(2,1)S(1)}, u32[]{:S(2)}, u32[]{:S(2)}) %collective-permute-start.7) | collective-permute-done | bytes 61472 | tf_op jit(solution)/shard_map/ppermute | solution.py:233
  11.2 1.5 %collective-permute-start.9 = (bf16[3,2,5120]{2,1,0:T(2,128)(2,1)S(1)}, bf16[3,2,5120]{2,1,0:T(2,128)(2,1)S(1)}, u32[]{:S(2)}, u32[]{:S(2)}) collective-permute-start(bf16[3,2,5120]{2,1,0:T(2,128)(2,1)S(1)} %collective-permute-done.7), channel_id=1, source_target_pairs={{0,2},{1,3},{2,0},{3,1},{4,6},{5,7},{6,4},{7,5},{8,10},{9,11},{10,... | collective-permute-start | bytes 184328 | tf_op jit(solution)/shard_map/ppermute | solution.py:233
  12.7 0.0 collective-permute-done.3
  12.7 0.0 collective-permute-start.8
  12.7 0.0 collective-permute-done.1
  12.7 1.0 %collective-permute-start.5 = (bf16[3,2,5120]{2,1,0:T(2,128)(2,1)S(1)}, bf16[3,2,5120]{2,1,0:T(2,128)(2,1)S(1)}, u32[]{:S(2)}, u32[]{:S(2)}) collective-permute-start(bf16[3,2,5120]{2,1,0:T(2,128)(2,1)S(1)} %collective-permute-done.3), channel_id=1, source_target_pairs={{0,2},{1,3},{2,0},{3,1},{4,6},{5,7},{6,4},{7,5},{8,10},{9,11},{10,... | collective-permute-start | bytes 184328 | tf_op jit(solution)/shard_map/ppermute | solution.py:233
  13.7 0.1 add.46
  13.8 0.1 sub.15
  13.9 0.1 reshape.96.slot_ref
  14.0 0.7 %collective-permute-done.13 = bf16[3,2,5120]{2,1,0:T(2,128)(2,1)S(1)} collective-permute-done((bf16[3,2,5120]{2,1,0:T(2,128)(2,1)S(1)}, bf16[3,2,5120]{2,1,0:T(2,128)(2,1)S(1)}, u32[]{:S(2)}, u32[]{:S(2)}) %collective-permute-start.13) | collective-permute-done | bytes 61472 | tf_op jit(solution)/shard_map/ppermute | solution.py:233
  14.7 0.0 collective-permute-start.4
  14.7 0.0 collective-permute-done.12
  14.7 0.5 collective-permute-start.2
  15.2 0.1 collective-permute-done.9
  15.4 0.0 collective-permute-start.14
  15.4 0.0 collective-permute-done.8
  15.4 0.5 collective-permute-start.10
  15.9 1.2 %collective-permute-done.5 = bf16[3,2,5120]{2,1,0:T(2,128)(2,1)S(1)} collective-permute-done((bf16[3,2,5120]{2,1,0:T(2,128)(2,1)S(1)}, bf16[3,2,5120]{2,1,0:T(2,128)(2,1)S(1)}, u32[]{:S(2)}, u32[]{:S(2)}) %collective-permute-start.5) | collective-permute-done | bytes 61472 | tf_op jit(solution)/shard_map/ppermute | solution.py:233
  17.1 0.0 collective-permute-start.6
  17.2 1.2 %collective-permute-done.6 = bf16[3,2,5120]{2,1,0:T(2,128)(2,1)S(1)} collective-permute-done((bf16[3,2,5120]{2,1,0:T(2,128)(2,1)S(1)}, bf16[3,2,5120]{2,1,0:T(2,128)(2,1)S(1)}, u32[]{:S(2)}, u32[]{:S(2)}) %collective-permute-start.6) | collective-permute-done | bytes 61472 | tf_op jit(solution)/shard_map/ppermute | solution.py:233
  18.3 4.2 %low_rows.1 = (bf16[40,48,2,128]{3,2,1,0:T(2,128)(2,1)}, bf16[16,48,128]{2,1,0:T(8,128)(2,1)}) custom-call(s32[1]{0:T(128)} %bitcast.me_ref, s32[1,96]{1,0:T(1,128)S(1)} %reshape.96.slot_ref, bf16[4,64,5120]{2,1,0:T(8,128)(2,1)} %down_ref.1, bf16[3,40,2,128]{3,2,1,0:T(2,128)(2,1)} %bitcast.73, bf16[3,40,2,128]{3,2,1,0:T(2,128)(2,1)S(1)} %bitcast.56, ...), custom_call_target="tpu_custom_call" | custom-call | flops 100000000 | bytes 4000000 | tf_op jit(solution)/shard_map/low_rows/pallas_call | solution.py:351
  22.6 5.2 %all-to-all-start = ((bf16[16,48,128]{2,1,0:T(8,128)(2,1)}), bf16[16,48,128]{2,1,0:T(8,128)(2,1)S(1)}, u32[]{:S(2)}, u32[]{:S(2)}) async-start(bf16[16,48,128]{2,1,0:T(8,128)(2,1)} %get-tuple-element.16), calls=%async_computation | async-start | bytes 393216 | tf_op jit(solution)/shard_map/all_to_all | solution.py:669
  27.8 0.1 fusion
  27.9 8.9 %project.1 = (bf16[16,9,3,2,128]{4,3,2,1,0:T(2,128)(2,1)}, f32[96,320]{1,0:T(8,128)}, bf16[2048,320]{1,0:T(8,128)(2,1)S(1)}) custom-call(s32[32]{0:T(128)S(1)} %select_reduce_fusion.1.stored_ref, bf16[40,48,2,128]{3,2,1,0:T(2,128)(2,1)} %get-tuple-element.17.x_ref, bf16[3,320,5120]{2,1,0:T(8,128)(2,1)} %bitcast.71, bf16[64,64,320]{2,1,0:T(8,128)(2,1)} %up_ref.1), custom_call_target="tpu_custom_call" | custom-call | flops 1000000000 | bytes 11000000 | tf_op jit(solution)/shard_map/project/pallas_call | solution.py:449
  36.9 2.2 %update_values.1 = bf16[16,9,3,2,128]{4,3,2,1,0:T(2,128)(2,1)} custom-call(bf16[16,48,128]{2,1,0:T(8,128)(2,1)S(1)} %all-to-all-done.low_ref, f32[96,320]{1,0:T(8,128)} %get-tuple-element.18.base_ref, bf16[2048,320]{1,0:T(8,128)(2,1)S(1)} %get-tuple-element.19.maps_ref, ...), custom_call_target="tpu_custom_call", output_to_operand_aliasing={{}: (3, {})} | custom-call | flops 300000000 | bytes 4000000 | tf_op jit(solution)/shard_map/update_values/pallas_call | solution.py:504
  39.0 6.0 %all-to-all-start.1 = ((bf16[16,9,3,2,128]{4,3,2,1,0:T(2,128)(2,1)}), bf16[16,9,3,2,128]{4,3,2,1,0:T(2,128)(2,1)S(1)}, u32[]{:S(2)}, u32[]{:S(2)}) async-start(bf16[16,9,3,2,128]{4,3,2,1,0:T(2,128)(2,1)} %update_values.1), calls=%async_computation.1 | async-start | bytes 442368 | tf_op jit(solution)/shard_map/all_to_all | solution.py:672
  45.1 0.1 and.12
  45.1 0.1 and.13
  45.3 0.1 add.50
  45.4 0.1 add.47
  45.5 0.1 add.48
  45.6 6.9 %cache_by_head.1 = (bf16[40,256,128]{2,1,0:T(8,128)(2,1)S(1)}, bf16[40,256,128]{2,1,0:T(8,128)(2,1)}) custom-call(bf16[256,40,2,128]{3,2,1,0:T(2,128)(2,1)} %bitcast.72), custom_call_target="tpu_custom_call" | custom-call | bytes 12000000 | tf_op jit(solution)/shard_map/cache_by_head/pallas_call | solution.py:288
  52.5 0.1 pad_maximum_fusion
  52.6 0.1 and_convert_fusion.live_ref
  52.6 1.8 %all-to-all-done.1.pieces_ref = bf16[16,9,3,2,128]{4,3,2,1,0:T(2,128)(2,1)S(1)} async-done(((bf16[16,9,3,2,128]{4,3,2,1,0:T(2,128)(2,1)}), bf16[16,9,3,2,128]{4,3,2,1,0:T(2,128)(2,1)S(1)}, u32[]{:S(2)}, u32[]{:S(2)}) %all-to-all-start.1) | async-done | bytes 221216 | tf_op jit(solution)/shard_map/all_to_all | solution.py:672
  54.4 3.9 %attention.1 = bf16[3,40,2,128]{3,2,1,0:T(2,128)(2,1)} custom-call(f32[8,128]{1,0:T(8,128)S(1)} %get-tuple-element.26.cos_ref, f32[8,128]{1,0:T(8,128)S(1)} %get-tuple-element.27.sin_ref, s32[2,256]{1,0:T(2,128)S(1)} %and_convert_fusion.live_ref, bf16[16,9,3,2,128]{4,3,2,1,0:T(2,128)(2,1)S(1)} %all-to-all-done.1.pieces_ref, ...), custom_call_target="tpu_custom_call" | custom-call | flops 1000000000 | bytes 6000000 | tf_op jit(solution)/shard_map/attention/pallas_call | solution.py:609
  (13 shorter events, 0.1 us)
Async XLA Ops:
  0.0 6.6 %collective-permute-start = (bf16[3,2,5120]{2,1,0:T(2,128)(2,1)}, bf16[3,2,5120]{2,1,0:T(2,128)(2,1)S(1)}, u32[]{:S(2)}, u32[]{:S(2)}) collective-permute-start(bf16[3,2,5120]{2,1,0:T(2,128)(2,1)} %param.9), channel_id=1, source_target_pairs={{0,1},{1,0},{2,3},{3,2},{4,5},{5,4},{6,7},{7,6},{8,9},{9,8},{10,11... | collective-permute-start | bytes 184328 | tf_op jit(solution)/shard_map/ppermute | solution.py:233
  0.5 9.3 %collective-permute-start.11 = (bf16[3,2,5120]{2,1,0:T(2,128)(2,1)}, bf16[3,2,5120]{2,1,0:T(2,128)(2,1)S(1)}, u32[]{:S(2)}, u32[]{:S(2)}) collective-permute-start(bf16[3,2,5120]{2,1,0:T(2,128)(2,1)} %param.9), channel_id=1, source_target_pairs={{0,12},{1,13},{2,14},{3,15},{4,8},{5,9},{6,10},{7,11},{8,4},{9,5},... | collective-permute-start | bytes 184328 | tf_op jit(solution)/shard_map/ppermute | solution.py:233
  5.1 6.1 %collective-permute-start.7 = (bf16[3,2,5120]{2,1,0:T(2,128)(2,1)}, bf16[3,2,5120]{2,1,0:T(2,128)(2,1)S(1)}, u32[]{:S(2)}, u32[]{:S(2)}) collective-permute-start(bf16[3,2,5120]{2,1,0:T(2,128)(2,1)} %param.9), channel_id=1, source_target_pairs={{0,8},{1,9},{2,10},{3,11},{4,12},{5,13},{6,14},{7,15},{8,0},{9,1},... | collective-permute-start | bytes 184328 | tf_op jit(solution)/shard_map/ppermute | solution.py:233
  6.6 6.1 %collective-permute-start.3 = (bf16[3,2,5120]{2,1,0:T(2,128)(2,1)}, bf16[3,2,5120]{2,1,0:T(2,128)(2,1)S(1)}, u32[]{:S(2)}, u32[]{:S(2)}) collective-permute-start(bf16[3,2,5120]{2,1,0:T(2,128)(2,1)} %param.9), channel_id=1, source_target_pairs={{0,4},{1,5},{2,6},{3,7},{4,0},{5,1},{6,2},{7,3},{8,12},{9,13},{10,... | collective-permute-start | bytes 184328 | tf_op jit(solution)/shard_map/ppermute | solution.py:233
  7.3 5.4 %collective-permute-start.1 = (bf16[3,2,5120]{2,1,0:T(2,128)(2,1)}, bf16[3,2,5120]{2,1,0:T(2,128)(2,1)S(1)}, u32[]{:S(2)}, u32[]{:S(2)}) collective-permute-start(bf16[3,2,5120]{2,1,0:T(2,128)(2,1)} %param.9), channel_id=1, source_target_pairs={{0,2},{1,3},{2,0},{3,1},{4,6},{5,7},{6,4},{7,5},{8,10},{9,11},{10,... | collective-permute-start | bytes 184328 | tf_op jit(solution)/shard_map/ppermute | solution.py:233
  9.8 4.9 %collective-permute-start.13 = (bf16[3,2,5120]{2,1,0:T(2,128)(2,1)S(1)}, bf16[3,2,5120]{2,1,0:T(2,128)(2,1)S(1)}, u32[]{:S(2)}, u32[]{:S(2)}) collective-permute-start(bf16[3,2,5120]{2,1,0:T(2,128)(2,1)S(1)} %collective-permute-done.11), channel_id=1, source_target_pairs={{0,2},{1,3},{2,0},{3,1},{4,6},{5,7},{6,4},{7,5},{8,10},{9,11},{10,... | collective-permute-start | bytes 184328 | tf_op jit(solution)/shard_map/ppermute | solution.py:233
  10.2 4.5 %collective-permute-start.12 = (bf16[3,2,5120]{2,1,0:T(2,128)(2,1)S(1)}, bf16[3,2,5120]{2,1,0:T(2,128)(2,1)S(1)}, u32[]{:S(2)}, u32[]{:S(2)}) collective-permute-start(bf16[3,2,5120]{2,1,0:T(2,128)(2,1)S(1)} %collective-permute-done.11), channel_id=1, source_target_pairs={{0,1},{1,0},{2,3},{3,2},{4,5},{5,4},{6,7},{7,6},{8,9},{9,8},{10,11... | collective-permute-start | bytes 184328 | tf_op jit(solution)/shard_map/ppermute | solution.py:233
  11.2 4.2 %collective-permute-start.9 = (bf16[3,2,5120]{2,1,0:T(2,128)(2,1)S(1)}, bf16[3,2,5120]{2,1,0:T(2,128)(2,1)S(1)}, u32[]{:S(2)}, u32[]{:S(2)}) collective-permute-start(bf16[3,2,5120]{2,1,0:T(2,128)(2,1)S(1)} %collective-permute-done.7), channel_id=1, source_target_pairs={{0,2},{1,3},{2,0},{3,1},{4,6},{5,7},{6,4},{7,5},{8,10},{9,11},{10,... | collective-permute-start | bytes 184328 | tf_op jit(solution)/shard_map/ppermute | solution.py:233
  12.7 2.7 %collective-permute-start.8 = (bf16[3,2,5120]{2,1,0:T(2,128)(2,1)S(1)}, bf16[3,2,5120]{2,1,0:T(2,128)(2,1)S(1)}, u32[]{:S(2)}, u32[]{:S(2)}) collective-permute-start(bf16[3,2,5120]{2,1,0:T(2,128)(2,1)S(1)} %collective-permute-done.7), channel_id=1, source_target_pairs={{0,1},{1,0},{2,3},{3,2},{4,5},{5,4},{6,7},{7,6},{8,9},{9,8},{10,11... | collective-permute-start | bytes 184328 | tf_op jit(solution)/shard_map/ppermute | solution.py:233
  12.7 4.4 %collective-permute-start.5 = (bf16[3,2,5120]{2,1,0:T(2,128)(2,1)S(1)}, bf16[3,2,5120]{2,1,0:T(2,128)(2,1)S(1)}, u32[]{:S(2)}, u32[]{:S(2)}) collective-permute-start(bf16[3,2,5120]{2,1,0:T(2,128)(2,1)S(1)} %collective-permute-done.3), channel_id=1, source_target_pairs={{0,2},{1,3},{2,0},{3,1},{4,6},{5,7},{6,4},{7,5},{8,10},{9,11},{10,... | collective-permute-start | bytes 184328 | tf_op jit(solution)/shard_map/ppermute | solution.py:233
  14.7 2.4 %collective-permute-start.4 = (bf16[3,2,5120]{2,1,0:T(2,128)(2,1)S(1)}, bf16[3,2,5120]{2,1,0:T(2,128)(2,1)S(1)}, u32[]{:S(2)}, u32[]{:S(2)}) collective-permute-start(bf16[3,2,5120]{2,1,0:T(2,128)(2,1)S(1)} %collective-permute-done.3), channel_id=1, source_target_pairs={{0,1},{1,0},{2,3},{3,2},{4,5},{5,4},{6,7},{7,6},{8,9},{9,8},{10,11... | collective-permute-start | bytes 184328 | tf_op jit(solution)/shard_map/ppermute | solution.py:233
  14.7 2.4 %collective-permute-start.2 = (bf16[3,2,5120]{2,1,0:T(2,128)(2,1)S(1)}, bf16[3,2,5120]{2,1,0:T(2,128)(2,1)S(1)}, u32[]{:S(2)}, u32[]{:S(2)}) collective-permute-start(bf16[3,2,5120]{2,1,0:T(2,128)(2,1)S(1)} %collective-permute-done.1), channel_id=1, source_target_pairs={{0,1},{1,0},{2,3},{3,2},{4,5},{5,4},{6,7},{7,6},{8,9},{9,8},{10,11... | collective-permute-start | bytes 184328 | tf_op jit(solution)/shard_map/ppermute | solution.py:233
  15.4 1.7 %collective-permute-start.14 = (bf16[3,2,5120]{2,1,0:T(2,128)(2,1)S(1)}, bf16[3,2,5120]{2,1,0:T(2,128)(2,1)S(1)}, u32[]{:S(2)}, u32[]{:S(2)}) collective-permute-start(bf16[3,2,5120]{2,1,0:T(2,128)(2,1)S(1)} %collective-permute-done.13), channel_id=1, source_target_pairs={{0,1},{1,0},{2,3},{3,2},{4,5},{5,4},{6,7},{7,6},{8,9},{9,8},{10,11... | collective-permute-start | bytes 184328 | tf_op jit(solution)/shard_map/ppermute | solution.py:233
  15.4 1.7 %collective-permute-start.10 = (bf16[3,2,5120]{2,1,0:T(2,128)(2,1)S(1)}, bf16[3,2,5120]{2,1,0:T(2,128)(2,1)S(1)}, u32[]{:S(2)}, u32[]{:S(2)}) collective-permute-start(bf16[3,2,5120]{2,1,0:T(2,128)(2,1)S(1)} %collective-permute-done.9), channel_id=1, source_target_pairs={{0,1},{1,0},{2,3},{3,2},{4,5},{5,4},{6,7},{7,6},{8,9},{9,8},{10,11... | collective-permute-start | bytes 184328 | tf_op jit(solution)/shard_map/ppermute | solution.py:233
  17.1 1.2 %collective-permute-start.6 = (bf16[3,2,5120]{2,1,0:T(2,128)(2,1)S(1)}, bf16[3,2,5120]{2,1,0:T(2,128)(2,1)S(1)}, u32[]{:S(2)}, u32[]{:S(2)}) collective-permute-start(bf16[3,2,5120]{2,1,0:T(2,128)(2,1)S(1)} %collective-permute-done.5), channel_id=1, source_target_pairs={{0,1},{1,0},{2,3},{3,2},{4,5},{5,4},{6,7},{7,6},{8,9},{9,8},{10,11... | collective-permute-start | bytes 184328 | tf_op jit(solution)/shard_map/ppermute | solution.py:233
  22.6 14.3 %all-to-all-start = ((bf16[16,48,128]{2,1,0:T(8,128)(2,1)}), bf16[16,48,128]{2,1,0:T(8,128)(2,1)S(1)}, u32[]{:S(2)}, u32[]{:S(2)}) async-start(bf16[16,48,128]{2,1,0:T(8,128)(2,1)} %get-tuple-element.16), calls=%async_computation | async-start | bytes 393216 | tf_op jit(solution)/shard_map/all_to_all | solution.py:669
  39.0 15.4 %all-to-all-start.1 = ((bf16[16,9,3,2,128]{4,3,2,1,0:T(2,128)(2,1)}), bf16[16,9,3,2,128]{4,3,2,1,0:T(2,128)(2,1)S(1)}, u32[]{:S(2)}, u32[]{:S(2)}) async-start(bf16[16,9,3,2,128]{4,3,2,1,0:T(2,128)(2,1)} %update_values.1), calls=%async_computation.1 | async-start | bytes 442368 | tf_op jit(solution)/shard_map/all_to_all | solution.py:672

commit v9 on v8

--- a/solution.py
+++ b/solution.py
@@ -309,27 +309,30 @@
     return jnp.concatenate([x[c] for c in range(x.shape[0])], axis=1)
 
 
+def step_rows(x, first, chunks):
+    steps, _, count = x.shape[:3]
+    flat = x.reshape(steps, x.shape[1], 2 * count, HD)
+    return jnp.concatenate(
+        [jnp.concatenate([flat[t, c] for c in range(first, first + chunks)], axis=1) for t in range(steps)], axis=0
+    )
+
+
 def low_kernel(count, me_ref, slot_ref, down_ref, *refs):
-    blocks, (x_ref, low_ref, x_buf, maps, made_ref, sem, low_sem, down_sem, own_sem) = refs[:count], refs[count:]
+    blocks, (x_ref, low_ref, x_buf, maps, made_ref, sem, down_sem, x_sem, low_sem) = refs[:count], refs[count:]
     me = me_ref[0]
-    steps = blocks[0].shape[0]
     holders, rank, width = down_ref.shape
-    fetches = start_all(
-        [pltpu.make_async_copy(down_ref.at[h], maps.at[h], down_sem.at[h]) for h in range(holders)]
-    )
-    copies = []
-    for k, block in enumerate(blocks):
-        for t in range(steps):
-            copies.append(
-                pltpu.make_async_copy(block.at[t], x_buf.at[:, (me ^ k) * steps + t], sem.at[k * steps + t])
-            )
-    wait_all(start_all(copies))
-    keep = pltpu.make_async_copy(x_buf, x_ref, own_sem)
+    fetch = pltpu.make_async_copy(down_ref, maps, down_sem)
+    fetch.start()
+    wait_all(
+        start_all(
+            [pltpu.make_async_copy(block, x_buf.at[:, :, me ^ k], sem.at[k]) for k, block in enumerate(blocks)]
+        )
+    )
+    keep = pltpu.make_async_copy(x_buf, x_ref, x_sem)
     keep.start()
-    chunks, pairs = x_buf.shape[:2]
-    rows = 2 * pairs
-    x = lanes_of(x_buf.reshape(chunks, rows, HD))
-    wait_all(fetches)
+    x = step_rows(x_buf, 0, x_buf.shape[1])
+    rows = x.shape[0]
+    fetch.wait()
     made = lax.dot_general(
         maps.reshape(holders * rank, width)[...], x, CONTRACT_LANES, preferred_element_type=jnp.float32
     )
@@ -338,8 +341,12 @@
     for h in range(holders):
         low = low + jnp.where(slot == h, made[h * rank : (h + 1) * rank], 0.0)
     low = low.T
-    made_ref[...] = jnp.concatenate([low[: rows // 2], low[rows // 2 :]], axis=1).astype(made_ref.dtype)
-    wait_all(start_all([pltpu.make_async_copy(made_ref, low_ref.at[k], low_sem.at[k]) for k in range(count)]))
+    low = jnp.concatenate([low[: rows // 2], low[rows // 2 :]], axis=1).astype(made_ref.dtype)
+    for k in range(count):
+        made_ref[k] = low
+    send = pltpu.make_async_copy(made_ref, low_ref, low_sem)
+    send.start()
+    send.wait()
     keep.wait()
 
 
@@ -351,18 +358,18 @@
     return pl.pallas_call(
         functools.partial(low_kernel, count),
         out_shape=(
-            pltpu.HBM((chunks, rows // 2, 2, HD), jnp.bfloat16),
+            pltpu.HBM((steps, chunks, count, 2, HD), jnp.bfloat16),
             pltpu.HBM((count, rows // 2, 2 * rank), jnp.bfloat16),
         ),
         in_specs=[SMEM, VMEM, HBM] + [ANY] * count,
         out_specs=(HBM, HBM),
         scratch_shapes=[
-            pltpu.VMEM((chunks, rows // 2, 2, HD), jnp.bfloat16),
+            pltpu.VMEM((steps, chunks, count, 2, HD), jnp.bfloat16),
             pltpu.VMEM(down.shape, jnp.bfloat16),
-            pltpu.VMEM((rows // 2, 2 * rank), jnp.bfloat16),
-            pltpu.SemaphoreType.DMA((count * steps,)),
+            pltpu.VMEM((count, rows // 2, 2 * rank), jnp.bfloat16),
             pltpu.SemaphoreType.DMA((count,)),
-            pltpu.SemaphoreType.DMA((down.shape[0],)),
+            pltpu.SemaphoreType.DMA,
+            pltpu.SemaphoreType.DMA,
             pltpu.SemaphoreType.DMA,
         ],
         compiler_params=pltpu.CompilerParams(vmem_limit_bytes=16 * 2**20),
@@ -372,36 +379,25 @@
 
 
 def put_chunks(buf, first, value):
+    steps, count = buf.shape[1:3]
+    flat = buf.reshape(buf.shape[0], steps, 2 * count, HD)
     wide = value.shape[1]
     for c in range(-(-wide // HD)):
         part = value[:, c * HD : min((c + 1) * HD, wide)]
         if part.shape[1] < HD:
             part = jnp.concatenate([part, jnp.zeros((part.shape[0], HD - part.shape[1]), part.dtype)], axis=1)
-        buf[first + c] = part.astype(buf.dtype)
-
-
-def send_blocks(buf, out_ref, first, sem):
-    count, _, steps = out_ref.shape[:3]
-    chunks = buf.shape[0]
-    return start_all(
-        [
-            pltpu.make_async_copy(
-                buf.at[:, k * steps : (k + 1) * steps], out_ref.at[k, first : first + chunks], sem.at[k]
-            )
-            for k in range(count)
-        ]
-    )
-
-
-PROJECT_CHUNK = 512
-PROJECT_AHEAD = 3
+        part = part.astype(buf.dtype)
+        for t in range(steps):
+            flat[first + c, t] = part[t * 2 * count : (t + 1) * 2 * count]
+
+
+PROJECT_CHUNK = 1024
+PROJECT_AHEAD = 2
 
 
 def project_kernel(
-    stored_ref, x_ref, w_ref, up_ref, send_ref, base_ref, maps_ref, x_buf, w_buf, total, buf, base, x_sem, w_sem, sem, base_sem, up_sem
+    stored_ref, x_ref, w_ref, up_ref, early_ref, base_ref, maps_ref, x_buf, w_buf, total, x_sem, w_sem, up_sem
 ):
-    chunks, pairs = x_buf.shape[:2]
-    rows = 2 * pairs
     columns, width = w_ref.shape[1:]
     parts = width // PROJECT_CHUNK
     per = PROJECT_CHUNK // HD
@@ -420,51 +416,41 @@
         ]
     )
     fetch_x.wait()
-    x_rows = x_buf.reshape(chunks, rows, HD)
     for p in range(parts):
         fetches[p].wait()
         start_all(fetches[p + PROJECT_AHEAD : p + PROJECT_AHEAD + 1])
-        x = jnp.concatenate([x_rows[c] for c in range(p * per, (p + 1) * per)], axis=1)
+        x = step_rows(x_buf, p * per, per)
         for i in range(3):
             made = lax.dot_general(w_buf[p, i], x, CONTRACT_LANES, preferred_element_type=jnp.float32)
             total[i] = made if p == 0 else total[i] + made
-    each = buf.shape[0] // 2
-    flat = buf.reshape(buf.shape[0], rows, HD)
+    each = early_ref.shape[0] // 2
     for i in range(2):
-        put_chunks(flat, i * each, total[i].T)
-    sent = send_blocks(buf, send_ref, 0, sem)
-    base[...] = total[2].T
-    keep = pltpu.make_async_copy(base, base_ref, base_sem)
-    keep.start()
-    wait_all(sent)
-    keep.wait()
+        put_chunks(early_ref, i * each, total[i].T)
+    base_ref[...] = total[2].T
     wait_all(maps)
 
 
-def project(stored, x, weight, up, count):
-    chunks, pairs = x.shape[:2]
+def project(stored, x, weight, up):
+    steps, _, count = x.shape[:3]
     columns, width = weight.shape[1:]
     each = -(-columns // HD)
+    rows = 2 * steps * count
     parts = width // PROJECT_CHUNK
     return pl.pallas_call(
         project_kernel,
         out_shape=(
-            pltpu.HBM((count, 3 * each, pairs // count, 2, HD), jnp.bfloat16),
-            pltpu.HBM((2 * pairs, columns), jnp.float32),
+            pltpu.VMEM((2 * each, steps, count, 2, HD), jnp.bfloat16),
+            pltpu.VMEM((rows, columns), jnp.float32),
             pltpu.VMEM((stored.shape[0] * up.shape[1], columns), up.dtype),
         ),
         in_specs=[SMEM, HBM, HBM, HBM],
-        out_specs=(HBM, HBM, VMEM),
+        out_specs=(VMEM, VMEM, VMEM),
         scratch_shapes=[
             pltpu.VMEM(x.shape, jnp.bfloat16),
             pltpu.VMEM((parts, 3, columns, PROJECT_CHUNK), jnp.bfloat16),
-            pltpu.VMEM((3, columns, 2 * pairs), jnp.float32),
-            pltpu.VMEM((2 * each, pairs, 2, HD), jnp.bfloat16),
-            pltpu.VMEM((2 * pairs, columns), jnp.float32),
+            pltpu.VMEM((3, columns, rows), jnp.float32),
             pltpu.SemaphoreType.DMA,
             pltpu.SemaphoreType.DMA((parts,)),
-            pltpu.SemaphoreType.DMA((count,)),
-            pltpu.SemaphoreType.DMA,
             pltpu.SemaphoreType.DMA((stored.shape[0],)),
         ],
         compiler_params=pltpu.CompilerParams(vmem_limit_bytes=24 * 2**20),
@@ -473,50 +459,48 @@
     )(stored, in_hbm(x), in_hbm(weight), in_hbm(up))
 
 
-def update_kernel(low_ref, base_ref, maps_ref, send_in, send_ref, base, buf, base_sem, sem):
+def update_kernel(low_ref, early_ref, base_ref, maps_ref, send_ref, buf, sem):
     count, half, packed = low_ref.shape
     rank = packed // 2
     rows = 2 * half
-    per = rows // count
-    fetch_base = pltpu.make_async_copy(base_ref, base, base_sem)
-    fetch_base.start()
     low = low_ref[0].astype(jnp.float32)
     for s in range(1, count):
         low = low + low_ref[s].astype(jnp.float32)
     low = jnp.concatenate([low[:, :rank], low[:, rank:]], axis=0)
     batch = 256 // rank
+    requests = maps_ref.shape[0] // rank
     spread = jnp.concatenate([low] * batch, axis=1)
     row = lax.broadcasted_iota(jnp.int32, (rows, batch * rank), 0)
     which = lax.broadcasted_iota(jnp.int32, (rows, batch * rank), 1) // rank
-    ahead = (row // per) * 2 + row % 2 - which
-    total = jnp.zeros(base.shape, jnp.float32)
-    for a in range(0, maps_ref.shape[0] // rank, batch):
+    ahead = row % requests - which
+    total = jnp.zeros(base_ref.shape, jnp.float32)
+    for a in range(0, requests, batch):
         wide = jnp.where(ahead == a, spread, 0.0).astype(jnp.bfloat16)
         total = total + jnp.dot(wide, maps_ref[a * rank : (a + batch) * rank], preferred_element_type=jnp.float32)
-    fetch_base.wait()
-    put_chunks(buf.reshape(buf.shape[0], rows, HD), 0, base[...] + adapter_scale * total)
-    wait_all(send_blocks(buf, send_ref, send_ref.shape[1] - buf.shape[0], sem))
-
-
-def update_values(lows, base, maps, send):
-    count, chunks = send.shape[:2]
-    rows, columns = base.shape
+    early = early_ref.shape[0]
+    buf[:early] = early_ref[...]
+    put_chunks(buf, early, base_ref[...] + adapter_scale * total)
+    wait_all(
+        start_all([pltpu.make_async_copy(buf.at[:, :, k], send_ref.at[k], sem.at[k]) for k in range(count)])
+    )
+
+
+def update_values(lows, early, base, maps):
+    chunks, steps, count = early.shape[:3]
+    chunks = chunks * 3 // 2
     return pl.pallas_call(
         update_kernel,
-        out_shape=pltpu.HBM(send.shape, send.dtype),
-        in_specs=[VMEM, HBM, VMEM, HBM],
+        out_shape=pltpu.HBM((count, chunks, steps, 2, HD), early.dtype),
+        in_specs=[VMEM, VMEM, VMEM, VMEM],
         out_specs=HBM,
         scratch_shapes=[
-            pltpu.VMEM(base.shape, jnp.float32),
-            pltpu.VMEM((chunks // 3, rows // 2, 2, HD), jnp.bfloat16),
-            pltpu.SemaphoreType.DMA,
+            pltpu.VMEM((chunks, steps, count, 2, HD), early.dtype),
             pltpu.SemaphoreType.DMA((count,)),
         ],
-        input_output_aliases={3: 0},
         compiler_params=pltpu.CompilerParams(vmem_limit_bytes=8 * 2**20),
         cost_estimate=pl.CostEstimate(flops=3 * 10**8, bytes_accessed=4 * 10**6, transcendentals=0),
         name="update_values",
-    )(lows, in_hbm(base), maps, in_hbm(send))
+    )(lows, early, base, maps)
 
 
 def attend_kernel(cos_ref, sin_ref, live_ref, pieces_ref, keys_ref, values_ref, out_ref, values_buf, kn_ref, vn_ref, sem):
@@ -662,13 +646,12 @@
         ),
         axis=1,
     )
-    slot = (stored - me * holder_count).reshape(count, 1, req_dev)
-    slot = jnp.broadcast_to(slot, (count, steps, req_dev)).reshape(1, -1)
+    slot = jnp.concatenate([stored - me * holder_count] * steps)[None, :]
 
     x, lows = low_of(me.astype(jnp.int32).reshape(1), blocks, slot, adapter_down_maps)
     lows = lax.all_to_all(lows, "replica", split_axis=0, concat_axis=0, tiled=True)
-    send, base, maps = project(stored, x, query_key_value_weight.transpose(0, 2, 1), adapter_up_maps, count)
-    send = update_values(lows, base, maps, send)
+    early, base, maps = project(stored, x, query_key_value_weight.transpose(0, 2, 1), adapter_up_maps)
+    send = update_values(lows, early, base, maps)
     pieces = lax.all_to_all(send, "replica", split_axis=0, concat_axis=0, tiled=True)
 
     my_lengths = lax.dynamic_slice_in_dim(lengths, me * req_dev, req_dev)

time: 58.9 us -> 56.7 us (0.963)
  Pallas kernels: 26 us -> 23.3 us
  waiting for transfers between devices: 5.97 us -> 7.75 us
  starting transfers between devices: 22.7 us -> 21.6 us
    pallas_call x2, Pallas kernels: 11.1 us -> 8.97 us  [the longest x1 7.54 us: project(): pl.pallas_call(project_kernel, out_shape=(pltpu.VMEM((2 * each, steps, co...]
    all_to_all x1, waiting for transfers between devices: 0.01 us -> 1.32 us  [chip_plan(): lax.all_to_all(lows, 'replica', split_axis=0, concat_axis=0, tiled=True)]
    all_to_all x1, starting transfers between devices: 6.03 us -> 4.71 us  [chip_plan(): lax.all_to_all(send, 'replica', split_axis=0, concat_axis=0, tiled=True)]
    pallas_call x1, Pallas kernels: 4.21 us -> 3.61 us  [low_of(): pl.pallas_call(functools.partial(low_kernel, count), out_shape=(pltpu.HBM...]
  transfers between devices with their start and end apart: 17 -> 17, of which waited for: 6 -> 8; matrix products, arithmetic and copies ran while one was open for 6% -> 6% of each run, Pallas kernels for 27% -> 26%
where the time goes in v9:
time: 56.7 us; the launch traced here: 56.3 us
  Pallas kernels  23.3 us (41%)
  starting transfers between devices  21.6 us (38%)
  waiting for transfers between devices  7.75 us (14%)
  other arithmetic  1.99 us (4%)
  local copies, waits for them, and re-layouts  1.31 us (2%)
    ppermute x15, starting transfers between devices, trade(): return lax.ppermute(value, 'replica', [(i, i ^ mask) for i in range(count)])  11.4 us
    pallas_call x1, Pallas kernels, project(): pl.pallas_call(project_kernel, out_shape=(pltpu.VMEM((2 * each, steps, co...  7.54 us
    pallas_call x1, Pallas kernels, cache_by_head(): pl.pallas_call(cache_kernel, out_shape=(jax.ShapeDtypeStruct((heads, toke...  6.9 us
    all_to_all x1, starting transfers between devices, chip_plan(): lax.all_to_all(lows, 'replica', split_axis=0, concat_axis=0, tiled=True)  5.49 us
    all_to_all x1, starting transfers between devices, chip_plan(): lax.all_to_all(send, 'replica', split_axis=0, concat_axis=0, tiled=True)  4.71 us
    ppermute x15, waiting for transfers between devices, trade(): return lax.ppermute(value, 'replica', [(i, i ^ mask) for i in range(count)])  4.64 us
    pallas_call x1, Pallas kernels, attend(): pl.pallas_call(attend_kernel, out_shape=jax.ShapeDtypeStruct((steps, head...  3.86 us
    pallas_call x1, Pallas kernels, low_of(): pl.pallas_call(functools.partial(low_kernel, count), out_shape=(pltpu.HBM...  3.61 us
  transfers between devices with their start and end apart: 17, of which 8 were waited for; matrix products, arithmetic and copies ran while one was open for 6% of the time, Pallas kernels for 26%

profile of v9, /device:TPU:0, one launch (start us, length us, event | category | flops | bytes accessed | tf_op | source)
XLA Modules:
  0.0 56.3 jit_solution(7573865019711790935)
XLA Ops:
  0.0 0.5 collective-permute-start
  0.5 4.6 %collective-permute-start.11 = (bf16[3,2,5120]{2,1,0:T(2,128)(2,1)}, bf16[3,2,5120]{2,1,0:T(2,128)(2,1)S(1)}, u32[]{:S(2)}, u32[]{:S(2)}) collective-permute-start(bf16[3,2,5120]{2,1,0:T(2,128)(2,1)} %param.9), channel_id=1, source_target_pairs={{0,12},{1,13},{2,14},{3,15},{4,8},{5,9},{6,10},{7,11},{8,4},{9,5},... | collective-permute-start | bytes 184328 | tf_op jit(solution)/shard_map/ppermute | solution.py:233
  5.1 0.0 collective-permute-start.7
  5.1 0.8 %select_reduce_fusion = s32[2,64]{1,0:T(2,128)S(1)} fusion(s32[2,32]{1,0:T(2,128)} %param.16), kind=kLoop, calls=%fused_computation | loop fusion | flops 12160 | bytes 768 | tf_op jit(solution)/shard_map/reduce_max | solution.py:113
  5.8 0.7 %dynamic_slice.3 = s32[2]{0:T(128)S(1)} dynamic-slice(s32[32]{0:T(128)} %param.15, s32[]{:T(128)S(6)} %select_n.11), dynamic_slice_sizes={2} | dynamic-slice | bytes 20 | tf_op jit(solution)/shard_map/dynamic_slice | solution.py:657
  6.6 0.8 %select_reduce_fusion.1.stored_ref = s32[32]{0:T(128)S(1)} fusion(s32[64]{0:T(128)} %param.13, s32[32]{0:T(128)} %param.14), kind=kLoop, calls=%fused_computation.2 | loop fusion | flops 6112 | bytes 512 | tf_op jit(solution)/shard_map/reduce_sum | solution.py:641
  7.4 0.0 collective-permute-done
  7.4 0.7 %collective-permute-start.3 = (bf16[3,2,5120]{2,1,0:T(2,128)(2,1)}, bf16[3,2,5120]{2,1,0:T(2,128)(2,1)S(1)}, u32[]{:S(2)}, u32[]{:S(2)}) collective-permute-start(bf16[3,2,5120]{2,1,0:T(2,128)(2,1)} %param.9), channel_id=1, source_target_pairs={{0,4},{1,5},{2,6},{3,7},{4,0},{5,1},{6,2},{7,3},{8,12},{9,13},{10,... | collective-permute-start | bytes 184328 | tf_op jit(solution)/shard_map/ppermute | solution.py:233
  8.1 1.7 %collective-permute-start.1 = (bf16[3,2,5120]{2,1,0:T(2,128)(2,1)}, bf16[3,2,5120]{2,1,0:T(2,128)(2,1)S(1)}, u32[]{:S(2)}, u32[]{:S(2)}) collective-permute-start(bf16[3,2,5120]{2,1,0:T(2,128)(2,1)} %param.9), channel_id=1, source_target_pairs={{0,2},{1,3},{2,0},{3,1},{4,6},{5,7},{6,4},{7,5},{8,10},{9,11},{10,... | collective-permute-start | bytes 184328 | tf_op jit(solution)/shard_map/ppermute | solution.py:233
  9.8 0.1 add.46
  9.9 0.0 collective-permute-done.11
  9.9 0.4 collective-permute-start.13
  10.2 0.0 collective-permute-start.12
  10.3 0.8 %collective-permute-done.7 = bf16[3,2,5120]{2,1,0:T(2,128)(2,1)S(1)} collective-permute-done((bf16[3,2,5120]{2,1,0:T(2,128)(2,1)}, bf16[3,2,5120]{2,1,0:T(2,128)(2,1)S(1)}, u32[]{:S(2)}, u32[]{:S(2)}) %collective-permute-start.7) | collective-permute-done | bytes 61472 | tf_op jit(solution)/shard_map/ppermute | solution.py:233
  11.1 1.5 %collective-permute-start.9 = (bf16[3,2,5120]{2,1,0:T(2,128)(2,1)S(1)}, bf16[3,2,5120]{2,1,0:T(2,128)(2,1)S(1)}, u32[]{:S(2)}, u32[]{:S(2)}) collective-permute-start(bf16[3,2,5120]{2,1,0:T(2,128)(2,1)S(1)} %collective-permute-done.7), channel_id=1, source_target_pairs={{0,2},{1,3},{2,0},{3,1},{4,6},{5,7},{6,4},{7,5},{8,10},{9,11},{10,... | collective-permute-start | bytes 184328 | tf_op jit(solution)/shard_map/ppermute | solution.py:233
  12.6 0.0 collective-permute-done.3
  12.6 0.0 collective-permute-start.8
  12.6 0.6 %collective-permute-done.1 = bf16[3,2,5120]{2,1,0:T(2,128)(2,1)S(1)} collective-permute-done((bf16[3,2,5120]{2,1,0:T(2,128)(2,1)}, bf16[3,2,5120]{2,1,0:T(2,128)(2,1)S(1)}, u32[]{:S(2)}, u32[]{:S(2)}) %collective-permute-start.1) | collective-permute-done | bytes 61472 | tf_op jit(solution)/shard_map/ppermute | solution.py:233
  13.2 1.1 %collective-permute-start.5 = (bf16[3,2,5120]{2,1,0:T(2,128)(2,1)S(1)}, bf16[3,2,5120]{2,1,0:T(2,128)(2,1)S(1)}, u32[]{:S(2)}, u32[]{:S(2)}) collective-permute-start(bf16[3,2,5120]{2,1,0:T(2,128)(2,1)S(1)} %collective-permute-done.3), channel_id=1, source_target_pairs={{0,2},{1,3},{2,0},{3,1},{4,6},{5,7},{6,4},{7,5},{8,10},{9,11},{10,... | collective-permute-start | bytes 184328 | tf_op jit(solution)/shard_map/ppermute | solution.py:233
  14.3 0.4 collective-permute-done.13
  14.7 0.0 collective-permute-start.4
  14.7 0.0 collective-permute-done.12
  14.7 0.5 collective-permute-start.2
  15.2 0.1 collective-permute-done.9
  15.4 0.0 collective-permute-start.14
  15.4 0.0 collective-permute-done.8
  15.4 0.5 collective-permute-start.10
  15.9 1.5 %collective-permute-done.5 = bf16[3,2,5120]{2,1,0:T(2,128)(2,1)S(1)} collective-permute-done((bf16[3,2,5120]{2,1,0:T(2,128)(2,1)S(1)}, bf16[3,2,5120]{2,1,0:T(2,128)(2,1)S(1)}, u32[]{:S(2)}, u32[]{:S(2)}) %collective-permute-start.5) | collective-permute-done | bytes 61472 | tf_op jit(solution)/shard_map/ppermute | solution.py:233
  17.4 0.0 collective-permute-start.6
  17.4 0.1 add_bitcast_fusion.slot_ref
  17.5 1.1 %collective-permute-done.6 = bf16[3,2,5120]{2,1,0:T(2,128)(2,1)S(1)} collective-permute-done((bf16[3,2,5120]{2,1,0:T(2,128)(2,1)S(1)}, bf16[3,2,5120]{2,1,0:T(2,128)(2,1)S(1)}, u32[]{:S(2)}, u32[]{:S(2)}) %collective-permute-start.6) | collective-permute-done | bytes 61472 | tf_op jit(solution)/shard_map/ppermute | solution.py:233
  18.7 3.6 %low_rows.1 = (bf16[3,40,16,2,128]{4,3,2,1,0:T(2,128)(2,1)}, bf16[16,48,128]{2,1,0:T(8,128)(2,1)}) custom-call(s32[1]{0:T(128)} %bitcast.me_ref, s32[1,96]{1,0:T(1,128)S(1)} %add_bitcast_fusion.slot_ref, bf16[4,64,5120]{2,1,0:T(8,128)(2,1)} %down_ref.1, bf16[3,40,2,128]{3,2,1,0:T(2,128)(2,1)} %bitcast.75, bf16[3,40,2,128]{3,2,1,0:T(2,128)(2,1)S(1)} %bitcast.58, ...), custom_call_target="tpu_custom_call" | custom-call | flops 100000000 | bytes 4000000 | tf_op jit(solution)/shard_map/low_rows/pallas_call | solution.py:358
  22.3 5.5 %all-to-all-start = ((bf16[16,48,128]{2,1,0:T(8,128)(2,1)}), bf16[16,48,128]{2,1,0:T(8,128)(2,1)S(1)}, u32[]{:S(2)}, u32[]{:S(2)}) async-start(bf16[16,48,128]{2,1,0:T(8,128)(2,1)} %get-tuple-element.16), calls=%async_computation | async-start | bytes 393216 | tf_op jit(solution)/shard_map/all_to_all | solution.py:652
  27.8 0.1 fusion
  27.9 7.5 %project.1 = (bf16[6,3,16,2,128]{4,3,2,1,0:T(2,128)(2,1)S(1)}, f32[96,320]{1,0:T(8,128)S(1)}, bf16[2048,320]{1,0:T(8,128)(2,1)S(1)}) custom-call(s32[32]{0:T(128)S(1)} %select_reduce_fusion.1.stored_ref, bf16[3,40,16,2,128]{4,3,2,1,0:T(2,128)(2,1)} %get-tuple-element.17.x_ref, bf16[3,320,5120]{2,1,0:T(8,128)(2,1)} %bitcast.73, bf16[64,64,320]{2,1,0:T(8,128)(2,1)} %up_ref.1), custom_call_target="tpu_custom_call" | custom-call | flops 1000000000 | bytes 11000000 | tf_op jit(solution)/shard_map/project/pallas_call | solution.py:439
  35.5 1.3 %all-to-all-done.low_ref = bf16[16,48,128]{2,1,0:T(8,128)(2,1)S(1)} async-done(((bf16[16,48,128]{2,1,0:T(8,128)(2,1)}), bf16[16,48,128]{2,1,0:T(8,128)(2,1)S(1)}, u32[]{:S(2)}, u32[]{:S(2)}) %all-to-all-start) | async-done | bytes 196640 | tf_op jit(solution)/shard_map/all_to_all | solution.py:652
  36.8 1.4 %update_values.1 = bf16[16,9,3,2,128]{4,3,2,1,0:T(2,128)(2,1)} custom-call(bf16[16,48,128]{2,1,0:T(8,128)(2,1)S(1)} %all-to-all-done.low_ref, bf16[6,3,16,2,128]{4,3,2,1,0:T(2,128)(2,1)S(1)} %get-tuple-element.18.early_ref, f32[96,320]{1,0:T(8,128)S(1)} %get-tuple-element.19.base_ref, bf16[2048,320]{1,0:T(8,128)(2,1)S(1)} %get-tuple-element.20.maps_ref), custom_call_target="tpu_custom_call" | custom-call | flops 300000000 | bytes 4000000 | tf_op jit(solution)/shard_map/update_values/pallas_call | solution.py:491
  38.2 4.7 %all-to-all-start.1 = ((bf16[16,9,3,2,128]{4,3,2,1,0:T(2,128)(2,1)}), bf16[16,9,3,2,128]{4,3,2,1,0:T(2,128)(2,1)S(1)}, u32[]{:S(2)}, u32[]{:S(2)}) async-start(bf16[16,9,3,2,128]{4,3,2,1,0:T(2,128)(2,1)} %update_values.1), calls=%async_computation.1 | async-start | bytes 442368 | tf_op jit(solution)/shard_map/all_to_all | solution.py:655
  42.9 0.1 and.12
  43.0 0.1 and.13
  43.2 0.1 add.50
  43.3 0.1 add.47
  43.3 0.1 add.48
  43.5 6.9 %cache_by_head.1 = (bf16[40,256,128]{2,1,0:T(8,128)(2,1)S(1)}, bf16[40,256,128]{2,1,0:T(8,128)(2,1)}) custom-call(bf16[256,40,2,128]{3,2,1,0:T(2,128)(2,1)} %bitcast.74), custom_call_target="tpu_custom_call" | custom-call | bytes 12000000 | tf_op jit(solution)/shard_map/cache_by_head/pallas_call | solution.py:288
  50.4 0.1 pad_maximum_fusion
  50.4 0.1 and_convert_fusion.live_ref
  50.5 1.8 %all-to-all-done.1.pieces_ref = bf16[16,9,3,2,128]{4,3,2,1,0:T(2,128)(2,1)S(1)} async-done(((bf16[16,9,3,2,128]{4,3,2,1,0:T(2,128)(2,1)}), bf16[16,9,3,2,128]{4,3,2,1,0:T(2,128)(2,1)S(1)}, u32[]{:S(2)}, u32[]{:S(2)}) %all-to-all-start.1) | async-done | bytes 221216 | tf_op jit(solution)/shard_map/all_to_all | solution.py:655
  52.3 3.9 %attention.1 = bf16[3,40,2,128]{3,2,1,0:T(2,128)(2,1)} custom-call(f32[8,128]{1,0:T(8,128)S(1)} %get-tuple-element.26.cos_ref, f32[8,128]{1,0:T(8,128)S(1)} %get-tuple-element.27.sin_ref, s32[2,256]{1,0:T(2,128)S(1)} %and_convert_fusion.live_ref, bf16[16,9,3,2,128]{4,3,2,1,0:T(2,128)(2,1)S(1)} %all-to-all-done.1.pieces_ref, ...), custom_call_target="tpu_custom_call" | custom-call | flops 1000000000 | bytes 6000000 | tf_op jit(solution)/shard_map/attention/pallas_call | solution.py:593
  (11 shorter events, 0.1 us)
Async XLA Ops:
  0.0 7.4 %collective-permute-start = (bf16[3,2,5120]{2,1,0:T(2,128)(2,1)}, bf16[3,2,5120]{2,1,0:T(2,128)(2,1)S(1)}, u32[]{:S(2)}, u32[]{:S(2)}) collective-permute-start(bf16[3,2,5120]{2,1,0:T(2,128)(2,1)} %param.9), channel_id=1, source_target_pairs={{0,1},{1,0},{2,3},{3,2},{4,5},{5,4},{6,7},{7,6},{8,9},{9,8},{10,11... | collective-permute-start | bytes 184328 | tf_op jit(solution)/shard_map/ppermute | solution.py:233
  0.5 9.4 %collective-permute-start.11 = (bf16[3,2,5120]{2,1,0:T(2,128)(2,1)}, bf16[3,2,5120]{2,1,0:T(2,128)(2,1)S(1)}, u32[]{:S(2)}, u32[]{:S(2)}) collective-permute-start(bf16[3,2,5120]{2,1,0:T(2,128)(2,1)} %param.9), channel_id=1, source_target_pairs={{0,12},{1,13},{2,14},{3,15},{4,8},{5,9},{6,10},{7,11},{8,4},{9,5},... | collective-permute-start | bytes 184328 | tf_op jit(solution)/shard_map/ppermute | solution.py:233
  5.1 6.0 %collective-permute-start.7 = (bf16[3,2,5120]{2,1,0:T(2,128)(2,1)}, bf16[3,2,5120]{2,1,0:T(2,128)(2,1)S(1)}, u32[]{:S(2)}, u32[]{:S(2)}) collective-permute-start(bf16[3,2,5120]{2,1,0:T(2,128)(2,1)} %param.9), channel_id=1, source_target_pairs={{0,8},{1,9},{2,10},{3,11},{4,12},{5,13},{6,14},{7,15},{8,0},{9,1},... | collective-permute-start | bytes 184328 | tf_op jit(solution)/shard_map/ppermute | solution.py:233
  7.4 5.2 %collective-permute-start.3 = (bf16[3,2,5120]{2,1,0:T(2,128)(2,1)}, bf16[3,2,5120]{2,1,0:T(2,128)(2,1)S(1)}, u32[]{:S(2)}, u32[]{:S(2)}) collective-permute-start(bf16[3,2,5120]{2,1,0:T(2,128)(2,1)} %param.9), channel_id=1, source_target_pairs={{0,4},{1,5},{2,6},{3,7},{4,0},{5,1},{6,2},{7,3},{8,12},{9,13},{10,... | collective-permute-start | bytes 184328 | tf_op jit(solution)/shard_map/ppermute | solution.py:233
  8.1 5.1 %collective-permute-start.1 = (bf16[3,2,5120]{2,1,0:T(2,128)(2,1)}, bf16[3,2,5120]{2,1,0:T(2,128)(2,1)S(1)}, u32[]{:S(2)}, u32[]{:S(2)}) collective-permute-start(bf16[3,2,5120]{2,1,0:T(2,128)(2,1)} %param.9), channel_id=1, source_target_pairs={{0,2},{1,3},{2,0},{3,1},{4,6},{5,7},{6,4},{7,5},{8,10},{9,11},{10,... | collective-permute-start | bytes 184328 | tf_op jit(solution)/shard_map/ppermute | solution.py:233
  9.9 4.8 %collective-permute-start.13 = (bf16[3,2,5120]{2,1,0:T(2,128)(2,1)S(1)}, bf16[3,2,5120]{2,1,0:T(2,128)(2,1)S(1)}, u32[]{:S(2)}, u32[]{:S(2)}) collective-permute-start(bf16[3,2,5120]{2,1,0:T(2,128)(2,1)S(1)} %collective-permute-done.11), channel_id=1, source_target_pairs={{0,2},{1,3},{2,0},{3,1},{4,6},{5,7},{6,4},{7,5},{8,10},{9,11},{10,... | collective-permute-start | bytes 184328 | tf_op jit(solution)/shard_map/ppermute | solution.py:233
  10.2 4.5 %collective-permute-start.12 = (bf16[3,2,5120]{2,1,0:T(2,128)(2,1)S(1)}, bf16[3,2,5120]{2,1,0:T(2,128)(2,1)S(1)}, u32[]{:S(2)}, u32[]{:S(2)}) collective-permute-start(bf16[3,2,5120]{2,1,0:T(2,128)(2,1)S(1)} %collective-permute-done.11), channel_id=1, source_target_pairs={{0,1},{1,0},{2,3},{3,2},{4,5},{5,4},{6,7},{7,6},{8,9},{9,8},{10,11... | collective-permute-start | bytes 184328 | tf_op jit(solution)/shard_map/ppermute | solution.py:233
  11.1 4.3 %collective-permute-start.9 = (bf16[3,2,5120]{2,1,0:T(2,128)(2,1)S(1)}, bf16[3,2,5120]{2,1,0:T(2,128)(2,1)S(1)}, u32[]{:S(2)}, u32[]{:S(2)}) collective-permute-start(bf16[3,2,5120]{2,1,0:T(2,128)(2,1)S(1)} %collective-permute-done.7), channel_id=1, source_target_pairs={{0,2},{1,3},{2,0},{3,1},{4,6},{5,7},{6,4},{7,5},{8,10},{9,11},{10,... | collective-permute-start | bytes 184328 | tf_op jit(solution)/shard_map/ppermute | solution.py:233
  12.6 2.8 %collective-permute-start.8 = (bf16[3,2,5120]{2,1,0:T(2,128)(2,1)S(1)}, bf16[3,2,5120]{2,1,0:T(2,128)(2,1)S(1)}, u32[]{:S(2)}, u32[]{:S(2)}) collective-permute-start(bf16[3,2,5120]{2,1,0:T(2,128)(2,1)S(1)} %collective-permute-done.7), channel_id=1, source_target_pairs={{0,1},{1,0},{2,3},{3,2},{4,5},{5,4},{6,7},{7,6},{8,9},{9,8},{10,11... | collective-permute-start | bytes 184328 | tf_op jit(solution)/shard_map/ppermute | solution.py:233
  13.2 4.2 %collective-permute-start.5 = (bf16[3,2,5120]{2,1,0:T(2,128)(2,1)S(1)}, bf16[3,2,5120]{2,1,0:T(2,128)(2,1)S(1)}, u32[]{:S(2)}, u32[]{:S(2)}) collective-permute-start(bf16[3,2,5120]{2,1,0:T(2,128)(2,1)S(1)} %collective-permute-done.3), channel_id=1, source_target_pairs={{0,2},{1,3},{2,0},{3,1},{4,6},{5,7},{6,4},{7,5},{8,10},{9,11},{10,... | collective-permute-start | bytes 184328 | tf_op jit(solution)/shard_map/ppermute | solution.py:233
  14.7 2.8 %collective-permute-start.4 = (bf16[3,2,5120]{2,1,0:T(2,128)(2,1)S(1)}, bf16[3,2,5120]{2,1,0:T(2,128)(2,1)S(1)}, u32[]{:S(2)}, u32[]{:S(2)}) collective-permute-start(bf16[3,2,5120]{2,1,0:T(2,128)(2,1)S(1)} %collective-permute-done.3), channel_id=1, source_target_pairs={{0,1},{1,0},{2,3},{3,2},{4,5},{5,4},{6,7},{7,6},{8,9},{9,8},{10,11... | collective-permute-start | bytes 184328 | tf_op jit(solution)/shard_map/ppermute | solution.py:233
  14.7 2.8 %collective-permute-start.2 = (bf16[3,2,5120]{2,1,0:T(2,128)(2,1)S(1)}, bf16[3,2,5120]{2,1,0:T(2,128)(2,1)S(1)}, u32[]{:S(2)}, u32[]{:S(2)}) collective-permute-start(bf16[3,2,5120]{2,1,0:T(2,128)(2,1)S(1)} %collective-permute-done.1), channel_id=1, source_target_pairs={{0,1},{1,0},{2,3},{3,2},{4,5},{5,4},{6,7},{7,6},{8,9},{9,8},{10,11... | collective-permute-start | bytes 184328 | tf_op jit(solution)/shard_map/ppermute | solution.py:233
  15.4 2.1 %collective-permute-start.14 = (bf16[3,2,5120]{2,1,0:T(2,128)(2,1)S(1)}, bf16[3,2,5120]{2,1,0:T(2,128)(2,1)S(1)}, u32[]{:S(2)}, u32[]{:S(2)}) collective-permute-start(bf16[3,2,5120]{2,1,0:T(2,128)(2,1)S(1)} %collective-permute-done.13), channel_id=1, source_target_pairs={{0,1},{1,0},{2,3},{3,2},{4,5},{5,4},{6,7},{7,6},{8,9},{9,8},{10,11... | collective-permute-start | bytes 184328 | tf_op jit(solution)/shard_map/ppermute | solution.py:233
  15.4 2.1 %collective-permute-start.10 = (bf16[3,2,5120]{2,1,0:T(2,128)(2,1)S(1)}, bf16[3,2,5120]{2,1,0:T(2,128)(2,1)S(1)}, u32[]{:S(2)}, u32[]{:S(2)}) collective-permute-start(bf16[3,2,5120]{2,1,0:T(2,128)(2,1)S(1)} %collective-permute-done.9), channel_id=1, source_target_pairs={{0,1},{1,0},{2,3},{3,2},{4,5},{5,4},{6,7},{7,6},{8,9},{9,8},{10,11... | collective-permute-start | bytes 184328 | tf_op jit(solution)/shard_map/ppermute | solution.py:233
  17.4 1.2 %collective-permute-start.6 = (bf16[3,2,5120]{2,1,0:T(2,128)(2,1)S(1)}, bf16[3,2,5120]{2,1,0:T(2,128)(2,1)S(1)}, u32[]{:S(2)}, u32[]{:S(2)}) collective-permute-start(bf16[3,2,5120]{2,1,0:T(2,128)(2,1)S(1)} %collective-permute-done.5), channel_id=1, source_target_pairs={{0,1},{1,0},{2,3},{3,2},{4,5},{5,4},{6,7},{7,6},{8,9},{9,8},{10,11... | collective-permute-start | bytes 184328 | tf_op jit(solution)/shard_map/ppermute | solution.py:233
  22.3 14.5 %all-to-all-start = ((bf16[16,48,128]{2,1,0:T(8,128)(2,1)}), bf16[16,48,128]{2,1,0:T(8,128)(2,1)S(1)}, u32[]{:S(2)}, u32[]{:S(2)}) async-start(bf16[16,48,128]{2,1,0:T(8,128)(2,1)} %get-tuple-element.16), calls=%async_computation | async-start | bytes 393216 | tf_op jit(solution)/shard_map/all_to_all | solution.py:652
  38.2 14.1 %all-to-all-start.1 = ((bf16[16,9,3,2,128]{4,3,2,1,0:T(2,128)(2,1)}), bf16[16,9,3,2,128]{4,3,2,1,0:T(2,128)(2,1)S(1)}, u32[]{:S(2)}, u32[]{:S(2)}) async-start(bf16[16,9,3,2,128]{4,3,2,1,0:T(2,128)(2,1)} %update_values.1), calls=%async_computation.1 | async-start | bytes 442368 | tf_op jit(solution)/shard_map/all_to_all | solution.py:655

commit v10 on v9

--- a/solution.py
+++ b/solution.py
@@ -317,37 +317,48 @@
     )
 
 
+def index_kernel(me_ref, stored_ref, slot_ref, column_ref):
+    requests = stored_ref.shape[1]
+    steps = slot_ref.shape[1] // requests
+    row = jnp.concatenate([stored_ref[...]] * steps, axis=1)
+    slot_ref[...] = row - me_ref[0]
+    wide = jnp.concatenate([row, jnp.zeros((1, HD - row.shape[1]), row.dtype)], axis=1)
+    column_ref[...] = jnp.broadcast_to(wide.astype(jnp.float32), (HD, HD)).T[: row.shape[1], :1].astype(jnp.int32)
+
+
+def index_work(first, stored, steps):
+    rows = stored.shape[0] * steps
+    return pl.pallas_call(
+        index_kernel,
+        out_shape=(jax.ShapeDtypeStruct((1, rows), jnp.int32), jax.ShapeDtypeStruct((rows, 1), jnp.int32)),
+        in_specs=[SMEM, VMEM],
+        out_specs=(VMEM, VMEM),
+        compiler_params=pltpu.CompilerParams(vmem_limit_bytes=2 * 2**20),
+        cost_estimate=pl.CostEstimate(flops=2 * 10**10, bytes_accessed=10**4, transcendentals=0),
+        name="index_work",
+    )(first, stored[None, :])
+
+
 def low_kernel(count, me_ref, slot_ref, down_ref, *refs):
-    blocks, (x_ref, low_ref, x_buf, maps, made_ref, sem, down_sem, x_sem, low_sem) = refs[:count], refs[count:]
+    blocks, (x_ref, low_ref, sem) = refs[:count], refs[count:]
     me = me_ref[0]
     holders, rank, width = down_ref.shape
-    fetch = pltpu.make_async_copy(down_ref, maps, down_sem)
-    fetch.start()
     wait_all(
         start_all(
-            [pltpu.make_async_copy(block, x_buf.at[:, :, me ^ k], sem.at[k]) for k, block in enumerate(blocks)]
+            [pltpu.make_async_copy(block, x_ref.at[:, :, me ^ k], sem.at[k]) for k, block in enumerate(blocks)]
         )
     )
-    keep = pltpu.make_async_copy(x_buf, x_ref, x_sem)
-    keep.start()
-    x = step_rows(x_buf, 0, x_buf.shape[1])
+    x = step_rows(x_ref, 0, x_ref.shape[1])
     rows = x.shape[0]
-    fetch.wait()
     made = lax.dot_general(
-        maps.reshape(holders * rank, width)[...], x, CONTRACT_LANES, preferred_element_type=jnp.float32
+        down_ref.reshape(holders * rank, width)[...], x, CONTRACT_LANES, preferred_element_type=jnp.float32
     )
     slot = slot_ref[...]
     low = jnp.zeros((rank, rows), jnp.float32)
     for h in range(holders):
         low = low + jnp.where(slot == h, made[h * rank : (h + 1) * rank], 0.0)
     low = low.T
-    low = jnp.concatenate([low[: rows // 2], low[rows // 2 :]], axis=1).astype(made_ref.dtype)
-    for k in range(count):
-        made_ref[k] = low
-    send = pltpu.make_async_copy(made_ref, low_ref, low_sem)
-    send.start()
-    send.wait()
-    keep.wait()
+    low_ref[...] = jnp.concatenate([low[: rows // 2], low[rows // 2 :]], axis=1).astype(low_ref.dtype)
 
 
 def low_of(me, blocks, slot, down):
@@ -358,24 +369,16 @@
     return pl.pallas_call(
         functools.partial(low_kernel, count),
         out_shape=(
-            pltpu.HBM((steps, chunks, count, 2, HD), jnp.bfloat16),
-            pltpu.HBM((count, rows // 2, 2 * rank), jnp.bfloat16),
+            jax.ShapeDtypeStruct((steps, chunks, count, 2, HD), jnp.bfloat16),
+            jax.ShapeDtypeStruct((rows // 2, 2 * rank), jnp.bfloat16),
         ),
-        in_specs=[SMEM, VMEM, HBM] + [ANY] * count,
-        out_specs=(HBM, HBM),
-        scratch_shapes=[
-            pltpu.VMEM((steps, chunks, count, 2, HD), jnp.bfloat16),
-            pltpu.VMEM(down.shape, jnp.bfloat16),
-            pltpu.VMEM((count, rows // 2, 2 * rank), jnp.bfloat16),
-            pltpu.SemaphoreType.DMA((count,)),
-            pltpu.SemaphoreType.DMA,
-            pltpu.SemaphoreType.DMA,
-            pltpu.SemaphoreType.DMA,
-        ],
-        compiler_params=pltpu.CompilerParams(vmem_limit_bytes=16 * 2**20),
+        in_specs=[SMEM, VMEM, VMEM] + [ANY] * count,
+        out_specs=(VMEM, VMEM),
+        scratch_shapes=[pltpu.SemaphoreType.DMA((count,))],
+        compiler_params=pltpu.CompilerParams(vmem_limit_bytes=12 * 2**20),
         cost_estimate=pl.CostEstimate(flops=10**8, bytes_accessed=4 * 10**6, transcendentals=0),
         name="low_rows",
-    )(me, slot, in_hbm(down), *blocks)
+    )(me, slot, down, *blocks)
 
 
 def put_chunks(buf, first, value):
@@ -391,116 +394,69 @@
             flat[first + c, t] = part[t * 2 * count : (t + 1) * 2 * count]
 
 
-PROJECT_CHUNK = 1024
-PROJECT_AHEAD = 2
-
-
-def project_kernel(
-    stored_ref, x_ref, w_ref, up_ref, early_ref, base_ref, maps_ref, x_buf, w_buf, total, x_sem, w_sem, up_sem
-):
-    columns, width = w_ref.shape[1:]
-    parts = width // PROJECT_CHUNK
-    per = PROJECT_CHUNK // HD
-    fetch_x = pltpu.make_async_copy(x_ref, x_buf, x_sem)
-    fetch_x.start()
-    fetches = [
-        pltpu.make_async_copy(w_ref.at[:, :, p * PROJECT_CHUNK : (p + 1) * PROJECT_CHUNK], w_buf.at[p], w_sem.at[p])
-        for p in range(parts)
-    ]
-    start_all(fetches[:PROJECT_AHEAD])
-    rank = up_ref.shape[1]
-    maps = start_all(
-        [
-            pltpu.make_async_copy(up_ref.at[stored_ref[q]], maps_ref.at[q * rank : (q + 1) * rank], up_sem.at[q])
-            for q in range(stored_ref.shape[0])
-        ]
-    )
-    fetch_x.wait()
-    for p in range(parts):
-        fetches[p].wait()
-        start_all(fetches[p + PROJECT_AHEAD : p + PROJECT_AHEAD + 1])
-        x = step_rows(x_buf, p * per, per)
-        for i in range(3):
-            made = lax.dot_general(w_buf[p, i], x, CONTRACT_LANES, preferred_element_type=jnp.float32)
-            total[i] = made if p == 0 else total[i] + made
-    each = early_ref.shape[0] // 2
-    for i in range(2):
-        put_chunks(early_ref, i * each, total[i].T)
-    base_ref[...] = total[2].T
-    wait_all(maps)
-
-
-def project(stored, x, weight, up):
+def project_kernel(which, x_ref, w_ref, out_ref):
+    x = step_rows(x_ref, 0, x_ref.shape[1])
+    made = lax.dot_general(w_ref[which], x, CONTRACT_LANES, preferred_element_type=jnp.float32).T
+    if which < 2:
+        put_chunks(out_ref, 0, made)
+    else:
+        out_ref[...] = made
+
+
+def project(which, x, weight):
     steps, _, count = x.shape[:3]
-    columns, width = weight.shape[1:]
-    each = -(-columns // HD)
-    rows = 2 * steps * count
-    parts = width // PROJECT_CHUNK
+    columns = weight.shape[1]
+    chunks = jax.ShapeDtypeStruct((-(-columns // HD), steps, count, 2, HD), jnp.bfloat16)
+    base = jax.ShapeDtypeStruct((2 * steps * count, columns), jnp.float32)
     return pl.pallas_call(
-        project_kernel,
-        out_shape=(
-            pltpu.VMEM((2 * each, steps, count, 2, HD), jnp.bfloat16),
-            pltpu.VMEM((rows, columns), jnp.float32),
-            pltpu.VMEM((stored.shape[0] * up.shape[1], columns), up.dtype),
-        ),
-        in_specs=[SMEM, HBM, HBM, HBM],
-        out_specs=(VMEM, VMEM, VMEM),
-        scratch_shapes=[
-            pltpu.VMEM(x.shape, jnp.bfloat16),
-            pltpu.VMEM((parts, 3, columns, PROJECT_CHUNK), jnp.bfloat16),
-            pltpu.VMEM((3, columns, rows), jnp.float32),
-            pltpu.SemaphoreType.DMA,
-            pltpu.SemaphoreType.DMA((parts,)),
-            pltpu.SemaphoreType.DMA((stored.shape[0],)),
-        ],
-        compiler_params=pltpu.CompilerParams(vmem_limit_bytes=24 * 2**20),
-        cost_estimate=pl.CostEstimate(flops=10**9, bytes_accessed=11 * 10**6, transcendentals=0),
+        functools.partial(project_kernel, which),
+        out_shape=chunks if which < 2 else base,
+        in_specs=[VMEM, VMEM],
+        out_specs=VMEM,
+        compiler_params=pltpu.CompilerParams(vmem_limit_bytes=16 * 2**20),
+        cost_estimate=pl.CostEstimate(flops=5 * 10**8, bytes_accessed=4 * 10**6, transcendentals=0),
         name="project",
-    )(stored, in_hbm(x), in_hbm(weight), in_hbm(up))
-
-
-def update_kernel(low_ref, early_ref, base_ref, maps_ref, send_ref, buf, sem):
-    count, half, packed = low_ref.shape
+    )(x, weight)
+
+
+def update_kernel(stored_ref, query_ref, key_ref, base_ref, up_ref, low_ref, more_ref, send_ref, buf, sem):
+    half, packed = low_ref.shape
     rank = packed // 2
     rows = 2 * half
-    low = low_ref[0].astype(jnp.float32)
-    for s in range(1, count):
-        low = low + low_ref[s].astype(jnp.float32)
+    count = send_ref.shape[0]
+    low = low_ref[...].astype(jnp.float32) + more_ref[...].astype(jnp.float32)
     low = jnp.concatenate([low[:, :rank], low[:, rank:]], axis=0)
     batch = 256 // rank
-    requests = maps_ref.shape[0] // rank
     spread = jnp.concatenate([low] * batch, axis=1)
-    row = lax.broadcasted_iota(jnp.int32, (rows, batch * rank), 0)
-    which = lax.broadcasted_iota(jnp.int32, (rows, batch * rank), 1) // rank
-    ahead = row % requests - which
+    ahead = stored_ref[...] - lax.broadcasted_iota(jnp.int32, (rows, batch * rank), 1) // rank
     total = jnp.zeros(base_ref.shape, jnp.float32)
-    for a in range(0, requests, batch):
+    for a in range(0, up_ref.shape[0] // rank, batch):
         wide = jnp.where(ahead == a, spread, 0.0).astype(jnp.bfloat16)
-        total = total + jnp.dot(wide, maps_ref[a * rank : (a + batch) * rank], preferred_element_type=jnp.float32)
-    early = early_ref.shape[0]
-    buf[:early] = early_ref[...]
-    put_chunks(buf, early, base_ref[...] + adapter_scale * total)
+        total = total + jnp.dot(wide, up_ref[a * rank : (a + batch) * rank], preferred_element_type=jnp.float32)
+    each = query_ref.shape[0]
+    buf[:each] = query_ref[...]
+    buf[each : 2 * each] = key_ref[...]
+    put_chunks(buf, 2 * each, base_ref[...] + adapter_scale * total)
     wait_all(
         start_all([pltpu.make_async_copy(buf.at[:, :, k], send_ref.at[k], sem.at[k]) for k in range(count)])
     )
 
 
-def update_values(lows, early, base, maps):
-    chunks, steps, count = early.shape[:3]
-    chunks = chunks * 3 // 2
+def update_values(stored, query, key, base, up, low, more):
+    chunks, steps, count = query.shape[:3]
     return pl.pallas_call(
         update_kernel,
-        out_shape=pltpu.HBM((count, chunks, steps, 2, HD), early.dtype),
-        in_specs=[VMEM, VMEM, VMEM, VMEM],
+        out_shape=pltpu.HBM((count, 3 * chunks, steps, 2, HD), query.dtype),
+        in_specs=[VMEM] * 7,
         out_specs=HBM,
         scratch_shapes=[
-            pltpu.VMEM((chunks, steps, count, 2, HD), early.dtype),
+            pltpu.VMEM((3 * chunks, steps, count, 2, HD), query.dtype),
             pltpu.SemaphoreType.DMA((count,)),
         ],
         compiler_params=pltpu.CompilerParams(vmem_limit_bytes=8 * 2**20),
         cost_estimate=pl.CostEstimate(flops=3 * 10**8, bytes_accessed=4 * 10**6, transcendentals=0),
         name="update_values",
-    )(lows, early, base, maps)
+    )(stored, query, key, base, up, low, more)
 
 
 def attend_kernel(cos_ref, sin_ref, live_ref, pieces_ref, keys_ref, values_ref, out_ref, values_buf, kn_ref, vn_ref, sem):
@@ -646,12 +602,43 @@
         ),
         axis=1,
     )
+    slot, column = index_work((me * holder_count).astype(jnp.int32).reshape(1), stored, steps)
+
+    held = {m: trade(hidden, m, count) for m in range(8, count, 4)}
+    held[1] = trade(hidden, 1, count)
+    held[0], held[1] = lax.optimization_barrier((hidden, held[1]))
+    held[4] = trade(held[0], 4, count)
+    held[2] = trade(held[0], 2, count)
+    held.update({m | 2: trade(held[m], 2, count) for m in range(4, count, 4)})
+    held.update({m | 1: trade(held[m], 1, count) for m in range(2, count, 2)})
+    blocks = [
+        held[k].reshape(steps, req_dev, heads, HD).transpose(0, 2, 1, 3) for k in range(count)
+    ]
+    blocks[0] = in_hbm(blocks[0])
+
+    stored = jnp.sum(
+        jnp.where(
+            request_adapter[:, None] == jnp.arange(adapter_count, dtype=jnp.int32)[None, :],
+            adapter_storage_row[None, :],
+            0,
+        ),
+        axis=1,
+    )
     slot = jnp.concatenate([stored - me * holder_count] * steps)[None, :]
 
-    x, lows = low_of(me.astype(jnp.int32).reshape(1), blocks, slot, adapter_down_maps)
-    lows = lax.all_to_all(lows, "replica", split_axis=0, concat_axis=0, tiled=True)
-    early, base, maps = project(stored, x, query_key_value_weight.transpose(0, 2, 1), adapter_up_maps)
-    send = update_values(lows, early, base, maps)
+    x, low = low_of(me.astype(jnp.int32).reshape(1), blocks, slot, adapter_down_maps)
+    weight = query_key_value_weight.transpose(0, 2, 1)
+    parts = []
+    hops = [1 << i for i in range(count.bit_length() - 1)]
+    for i, mask in enumerate(hops):
+        arrived = trade(low, mask, count)
+        if i < 3:
+            part = project(i, x, weight)
+            arrived, part = lax.optimization_barrier((arrived, part))
+            parts.append(part)
+        if mask != hops[-1]:
+            low = low + arrived
+    send = update_values(column, *parts, adapter_up_maps.reshape(adapter_count * rank, -1), low, arrived)
     pieces = lax.all_to_all(send, "replica", split_axis=0, concat_axis=0, tiled=True)
 
     my_lengths = lax.dynamic_slice_in_dim(lengths, me * req_dev, req_dev)

time: 56.7 us -> 55.2 us (0.974)
  Pallas kernels: 23.3 us -> 18.5 us
  waiting for transfers between devices: 7.75 us -> 10.7 us
  starting transfers between devices: 21.6 us -> 22.5 us
  other arithmetic: 1.99 us -> 1.33 us
    all_to_all x1 -> x0, starting transfers between devices: 5.49 us -> none  [chip_plan(): lax.all_to_all(lows, 'replica', split_axis=0, concat_axis=0, tiled=True)]
    ppermute x15 -> x19, starting transfers between devices: 11.4 us -> 16.9 us  [trade(): return lax.ppermute(value, 'replica', [(i, i ^ mask) for i in range(count)])]
    pallas_call x3 -> x6, Pallas kernels: 12.6 us -> 7.72 us  [the longest x3 3.36 us: project(): pl.pallas_call(functools.partial(project_kernel, which), out_shape=chunks...]
    ppermute x15 -> x19, waiting for transfers between devices: 4.64 us -> 8.95 us  [trade(): return lax.ppermute(value, 'replica', [(i, i ^ mask) for i in range(count)])]
    all_to_all x1 -> x0, waiting for transfers between devices: 1.32 us -> none  [chip_plan(): lax.all_to_all(lows, 'replica', split_axis=0, concat_axis=0, tiled=True)]
    all_to_all x1, starting transfers between devices: 4.71 us -> 5.62 us  [chip_plan(): lax.all_to_all(send, 'replica', split_axis=0, concat_axis=0, tiled=True)]
    reduce_max x1, other arithmetic: 0.77 us -> 0.09 us  [live_tokens(): jnp.max(jnp.where(request_page_table[:, :, None] == pages[None, None, :],...]
  transfers between devices with their start and end apart: 17 -> 20, of which waited for: 8 -> 10; matrix products, arithmetic and copies ran while one was open for 6% -> 5% of each run, Pallas kernels for 26% -> 20%
where the time goes in v10:
time: 55.2 us; the launch traced here: 54.9 us
  starting transfers between devices  22.5 us (41%)
  Pallas kernels  18.5 us (34%)
  waiting for transfers between devices  10.7 us (19%)
  local copies, waits for them, and re-layouts  1.49 us (3%)
  other arithmetic  1.33 us (2%)
    ppermute x19, starting transfers between devices, trade(): return lax.ppermute(value, 'replica', [(i, i ^ mask) for i in range(count)])  16.9 us
    ppermute x19, waiting for transfers between devices, trade(): return lax.ppermute(value, 'replica', [(i, i ^ mask) for i in range(count)])  8.95 us
    pallas_call x1, Pallas kernels, cache_by_head(): pl.pallas_call(cache_kernel, out_shape=(jax.ShapeDtypeStruct((heads, toke...  6.91 us
    all_to_all x1, starting transfers between devices, chip_plan(): lax.all_to_all(send, 'replica', split_axis=0, concat_axis=0, tiled=True)  5.62 us
    pallas_call x1, Pallas kernels, attend(): pl.pallas_call(attend_kernel, out_shape=jax.ShapeDtypeStruct((steps, head...  3.85 us
    pallas_call x3, Pallas kernels, project(): pl.pallas_call(functools.partial(project_kernel, which), out_shape=chunks...  3.36 us
    pallas_call x1, Pallas kernels, low_of(): pl.pallas_call(functools.partial(low_kernel, count), out_shape=(jax.Shape...  2.06 us
    all_to_all x1, waiting for transfers between devices, chip_plan(): lax.all_to_all(send, 'replica', split_axis=0, concat_axis=0, tiled=True)  1.78 us
  transfers between devices with their start and end apart: 20, of which 10 were waited for; matrix products, arithmetic and copies ran while one was open for 5% of the time, Pallas kernels for 20%

profile of v10, /device:TPU:0, one launch (start us, length us, event | category | flops | bytes accessed | tf_op | source)
XLA Modules:
  0.0 54.9 jit_solution(16509180460703476540)
XLA Ops:
  0.0 0.5 collective-permute-start
  0.5 4.6 %collective-permute-start.11 = (bf16[3,2,5120]{2,1,0:T(2,128)(2,1)}, bf16[3,2,5120]{2,1,0:T(2,128)(2,1)S(1)}, u32[]{:S(2)}, u32[]{:S(2)}) collective-permute-start(bf16[3,2,5120]{2,1,0:T(2,128)(2,1)} %param.9), channel_id=1, source_target_pairs={{0,12},{1,13},{2,14},{3,15},{4,8},{5,9},{6,10},{7,11},{8,4},{9,5},... | collective-permute-start | bytes 184328 | tf_op jit(solution)/shard_map/ppermute | solution.py:233
  5.1 0.7 %dynamic_slice.3 = s32[2]{0:T(128)S(1)} dynamic-slice(s32[32]{0:T(128)} %param.15, s32[]{:T(128)S(6)} %select_n.12), dynamic_slice_sizes={2} | dynamic-slice | bytes 20 | tf_op jit(solution)/shard_map/dynamic_slice | solution.py:644
  5.8 0.1 add.55
  5.9 0.9 %select_reduce_fusion.1 = s32[32]{0:T(128)S(1)} fusion(s32[64]{0:T(128)} %param.13, s32[32]{0:T(128)} %param.14), kind=kLoop, calls=%fused_computation.2 | loop fusion | flops 6112 | bytes 512 | tf_op jit(solution)/shard_map/reduce_sum | solution.py:597
  6.8 0.0 copy-start.3
  6.8 0.0 copy-start.1
  6.8 0.7 %index_work.1 = (s32[1,96]{1,0:T(1,128)}, s32[96,1]{1,0:T(8,128)S(1)}) custom-call(s32[1]{0:T(128)} %bitcast.me_ref, s32[1,32]{1,0:T(1,128)S(1)} %bitcast.82), custom_call_target="tpu_custom_call" | custom-call | flops 20000000000 | bytes 10000 | tf_op jit(solution)/shard_map/index_work/pallas_call | solution.py:331
  7.5 0.1 fusion
  7.6 0.1 copy-done.2
  7.7 0.6 %collective-permute-start.3 = (bf16[3,2,5120]{2,1,0:T(2,128)(2,1)S(1)}, bf16[3,2,5120]{2,1,0:T(2,128)(2,1)S(1)}, u32[]{:S(2)}, u32[]{:S(2)}) collective-permute-start(bf16[3,2,5120]{2,1,0:T(2,128)(2,1)S(1)} %copy-done.2), channel_id=1, source_target_pairs={{0,4},{1,5},{2,6},{3,7},{4,0},{5,1},{6,2},{7,3},{8,12},{9,13},{10,... | collective-permute-start | bytes 184328 | tf_op jit(solution)/shard_map/ppermute | solution.py:233
  8.4 1.7 %collective-permute-start.1 = (bf16[3,2,5120]{2,1,0:T(2,128)(2,1)S(1)}, bf16[3,2,5120]{2,1,0:T(2,128)(2,1)S(1)}, u32[]{:S(2)}, u32[]{:S(2)}) collective-permute-start(bf16[3,2,5120]{2,1,0:T(2,128)(2,1)S(1)} %copy-done.2), channel_id=1, source_target_pairs={{0,2},{1,3},{2,0},{3,1},{4,6},{5,7},{6,4},{7,5},{8,10},{9,11},{10,... | collective-permute-start | bytes 184328 | tf_op jit(solution)/shard_map/ppermute | solution.py:233
  10.1 0.4 collective-permute-start.13
  10.4 0.7 %collective-permute-done.7 = bf16[3,2,5120]{2,1,0:T(2,128)(2,1)S(1)} collective-permute-done((bf16[3,2,5120]{2,1,0:T(2,128)(2,1)}, bf16[3,2,5120]{2,1,0:T(2,128)(2,1)S(1)}, u32[]{:S(2)}, u32[]{:S(2)}) %collective-permute-start.7) | collective-permute-done | bytes 61472 | tf_op jit(solution)/shard_map/ppermute | solution.py:233
  11.1 1.5 %collective-permute-start.9 = (bf16[3,2,5120]{2,1,0:T(2,128)(2,1)S(1)}, bf16[3,2,5120]{2,1,0:T(2,128)(2,1)S(1)}, u32[]{:S(2)}, u32[]{:S(2)}) collective-permute-start(bf16[3,2,5120]{2,1,0:T(2,128)(2,1)S(1)} %collective-permute-done.7), channel_id=1, source_target_pairs={{0,2},{1,3},{2,0},{3,1},{4,6},{5,7},{6,4},{7,5},{8,10},{9,11},{10,... | collective-permute-start | bytes 184328 | tf_op jit(solution)/shard_map/ppermute | solution.py:233
  12.6 0.5 collective-permute-done.1
  13.1 1.2 %collective-permute-start.5 = (bf16[3,2,5120]{2,1,0:T(2,128)(2,1)S(1)}, bf16[3,2,5120]{2,1,0:T(2,128)(2,1)S(1)}, u32[]{:S(2)}, u32[]{:S(2)}) collective-permute-start(bf16[3,2,5120]{2,1,0:T(2,128)(2,1)S(1)} %collective-permute-done.3), channel_id=1, source_target_pairs={{0,2},{1,3},{2,0},{3,1},{4,6},{5,7},{6,4},{7,5},{8,10},{9,11},{10,... | collective-permute-start | bytes 184328 | tf_op jit(solution)/shard_map/ppermute | solution.py:233
  14.3 0.1 select_reduce_fusion
  14.4 0.4 collective-permute-done.13
  14.8 0.5 collective-permute-start.2
  15.3 0.1 collective-permute-done.9
  15.5 0.5 collective-permute-start.10
  16.0 1.3 %collective-permute-done.5 = bf16[3,2,5120]{2,1,0:T(2,128)(2,1)S(1)} collective-permute-done((bf16[3,2,5120]{2,1,0:T(2,128)(2,1)S(1)}, bf16[3,2,5120]{2,1,0:T(2,128)(2,1)S(1)}, u32[]{:S(2)}, u32[]{:S(2)}) %collective-permute-start.5) | collective-permute-done | bytes 61472 | tf_op jit(solution)/shard_map/ppermute | solution.py:233
  17.3 0.1 add_bitcast_fusion.slot_ref
  17.4 1.1 %collective-permute-done.6 = bf16[3,2,5120]{2,1,0:T(2,128)(2,1)S(1)} collective-permute-done((bf16[3,2,5120]{2,1,0:T(2,128)(2,1)S(1)}, bf16[3,2,5120]{2,1,0:T(2,128)(2,1)S(1)}, u32[]{:S(2)}, u32[]{:S(2)}) %collective-permute-start.6) | collective-permute-done | bytes 61472 | tf_op jit(solution)/shard_map/ppermute | solution.py:233
  18.6 2.1 %low_rows.1 = (bf16[3,40,16,2,128]{4,3,2,1,0:T(2,128)(2,1)S(1)}, bf16[48,128]{1,0:T(8,128)(2,1)S(1)}) custom-call(s32[1]{0:T(128)} %bitcast.2.me_ref, s32[1,96]{1,0:T(1,128)S(1)} %add_bitcast_fusion.slot_ref, bf16[4,64,5120]{2,1,0:T(8,128)(2,1)S(1)} %copy-done.1, bf16[3,40,2,128]{3,2,1,0:T(2,128)(2,1)} %bitcast.84, bf16[3,40,2,128]{3,2,1,0:T(2,128)(2,1)S(1)} %bitcast.67, ...), custom_call_target="tpu_custom_call" | custom-call | flops 100000000 | bytes 4000000 | tf_op jit(solution)/shard_map/low_rows/pallas_call | solution.py:369
  20.6 0.2 collective-permute-start.15
  20.9 1.1 %project.3.query_ref = bf16[3,3,16,2,128]{4,3,2,1,0:T(2,128)(2,1)S(1)} custom-call(bf16[3,40,16,2,128]{4,3,2,1,0:T(2,128)(2,1)S(1)} %get-tuple-element.22.x_ref, bf16[3,320,5120]{2,1,0:T(8,128)(2,1)S(1)} %bitcast.63), custom_call_target="tpu_custom_call" | custom-call | flops 500000000 | bytes 4000000 | tf_op jit(solution)/shard_map/project/pallas_call | solution.py:411
  22.0 1.3 %collective-permute-start.16 = (bf16[48,128]{1,0:T(8,128)(2,1)S(1)}, bf16[48,128]{1,0:T(8,128)(2,1)S(1)}, u32[]{:S(2)}, u32[]{:S(2)}) collective-permute-start(bf16[48,128]{1,0:T(8,128)(2,1)S(1)} %add.62), channel_id=1, source_target_pairs={{0,2},{1,3},{2,0},{3,1},{4,6},{5,7},{6,4},{7,5},{8,10},{9,11},{10,... | collective-permute-start | bytes 36872 | tf_op jit(solution)/shard_map/ppermute | solution.py:233
  23.3 1.1 %project.4.key_ref = bf16[3,3,16,2,128]{4,3,2,1,0:T(2,128)(2,1)S(1)} custom-call(bf16[3,40,16,2,128]{4,3,2,1,0:T(2,128)(2,1)S(1)} %get-tuple-element.22.x_ref, bf16[3,320,5120]{2,1,0:T(8,128)(2,1)S(1)} %bitcast.64), custom_call_target="tpu_custom_call" | custom-call | flops 500000000 | bytes 4000000 | tf_op jit(solution)/shard_map/project/pallas_call | solution.py:411
  24.5 1.3 %collective-permute-done.16 = bf16[48,128]{1,0:T(8,128)(2,1)S(1)} collective-permute-done((bf16[48,128]{1,0:T(8,128)(2,1)S(1)}, bf16[48,128]{1,0:T(8,128)(2,1)S(1)}, u32[]{:S(2)}, u32[]{:S(2)}) %collective-permute-start.16) | collective-permute-done | bytes 12320 | tf_op jit(solution)/shard_map/ppermute | solution.py:233
  25.8 1.4 %collective-permute-start.17 = (bf16[48,128]{1,0:T(8,128)(2,1)S(1)}, bf16[48,128]{1,0:T(8,128)(2,1)S(1)}, u32[]{:S(2)}, u32[]{:S(2)}) collective-permute-start(bf16[48,128]{1,0:T(8,128)(2,1)S(1)} %add.63), channel_id=1, source_target_pairs={{0,4},{1,5},{2,6},{3,7},{4,0},{5,1},{6,2},{7,3},{8,12},{9,13},{10,... | collective-permute-start | bytes 36872 | tf_op jit(solution)/shard_map/ppermute | solution.py:233
  27.2 1.1 %project.5.base_ref = f32[96,320]{1,0:T(8,128)S(1)} custom-call(bf16[3,40,16,2,128]{4,3,2,1,0:T(2,128)(2,1)S(1)} %get-tuple-element.22.x_ref, bf16[3,320,5120]{2,1,0:T(8,128)(2,1)S(1)} %bitcast.65), custom_call_target="tpu_custom_call" | custom-call | flops 500000000 | bytes 4000000 | tf_op jit(solution)/shard_map/project/pallas_call | solution.py:411
  28.3 1.3 %collective-permute-done.17 = bf16[48,128]{1,0:T(8,128)(2,1)S(1)} collective-permute-done((bf16[48,128]{1,0:T(8,128)(2,1)S(1)}, bf16[48,128]{1,0:T(8,128)(2,1)S(1)}, u32[]{:S(2)}, u32[]{:S(2)}) %collective-permute-start.17) | collective-permute-done | bytes 12320 | tf_op jit(solution)/shard_map/ppermute | solution.py:233
  29.6 2.5 %collective-permute-start.18 = (bf16[48,128]{1,0:T(8,128)(2,1)S(1)}, bf16[48,128]{1,0:T(8,128)(2,1)S(1)}, u32[]{:S(2)}, u32[]{:S(2)}) collective-permute-start(bf16[48,128]{1,0:T(8,128)(2,1)S(1)} %add.64.low_ref), channel_id=1, source_target_pairs={{0,8},{1,9},{2,10},{3,11},{4,12},{5,13},{6,14},{7,15},{8,0},{9,1},... | collective-permute-start | bytes 36872 | tf_op jit(solution)/shard_map/ppermute | solution.py:233
  32.0 2.2 %collective-permute-done.18.more_ref = bf16[48,128]{1,0:T(8,128)(2,1)S(1)} collective-permute-done((bf16[48,128]{1,0:T(8,128)(2,1)S(1)}, bf16[48,128]{1,0:T(8,128)(2,1)S(1)}, u32[]{:S(2)}, u32[]{:S(2)}) %collective-permute-start.18) | collective-permute-done | bytes 12320 | tf_op jit(solution)/shard_map/ppermute | solution.py:233
  34.2 1.6 %update_values.1 = bf16[16,9,3,2,128]{4,3,2,1,0:T(2,128)(2,1)} custom-call(s32[96,1]{1,0:T(8,128)S(1)} %get-tuple-element.18.stored_ref, bf16[3,3,16,2,128]{4,3,2,1,0:T(2,128)(2,1)S(1)} %project.3.query_ref, bf16[3,3,16,2,128]{4,3,2,1,0:T(2,128)(2,1)S(1)} %project.4.key_ref, f32[96,320]{1,0:T(8,128)S(1)} %project.5.base_ref, bf16[4096,320]{1,0:T(8,128)(2,1)S(1)} %bitcast.66, ...), custom_call_target="tpu_custom_call" | custom-call | flops 300000000 | bytes 4000000 | tf_op jit(solution)/shard_map/update_values/pallas_call | solution.py:447
  35.9 5.6 %all-to-all-start = ((bf16[16,9,3,2,128]{4,3,2,1,0:T(2,128)(2,1)}), bf16[16,9,3,2,128]{4,3,2,1,0:T(2,128)(2,1)S(1)}, u32[]{:S(2)}, u32[]{:S(2)}) async-start(bf16[16,9,3,2,128]{4,3,2,1,0:T(2,128)(2,1)} %update_values.1), calls=%async_computation | async-start | bytes 442368 | tf_op jit(solution)/shard_map/all_to_all | solution.py:642
  41.5 0.1 and.12
  41.6 0.1 and.13
  41.7 0.1 add.59
  41.8 0.1 add.56
  41.9 0.1 add.57
  42.0 6.9 %cache_by_head.1 = (bf16[40,256,128]{2,1,0:T(8,128)(2,1)S(1)}, bf16[40,256,128]{2,1,0:T(8,128)(2,1)}) custom-call(bf16[256,40,2,128]{3,2,1,0:T(2,128)(2,1)} %bitcast.83), custom_call_target="tpu_custom_call" | custom-call | bytes 12000000 | tf_op jit(solution)/shard_map/cache_by_head/pallas_call | solution.py:288
  49.0 0.1 pad_maximum_fusion
  49.0 0.1 and_convert_fusion.live_ref
  49.1 1.8 %all-to-all-done.pieces_ref = bf16[16,9,3,2,128]{4,3,2,1,0:T(2,128)(2,1)S(1)} async-done(((bf16[16,9,3,2,128]{4,3,2,1,0:T(2,128)(2,1)}), bf16[16,9,3,2,128]{4,3,2,1,0:T(2,128)(2,1)S(1)}, u32[]{:S(2)}, u32[]{:S(2)}) %all-to-all-start) | async-done | bytes 221216 | tf_op jit(solution)/shard_map/all_to_all | solution.py:642
  50.9 3.8 %attention.1 = bf16[3,40,2,128]{3,2,1,0:T(2,128)(2,1)} custom-call(f32[8,128]{1,0:T(8,128)S(1)} %get-tuple-element.34.cos_ref, f32[8,128]{1,0:T(8,128)S(1)} %get-tuple-element.35.sin_ref, s32[2,256]{1,0:T(2,128)S(1)} %and_convert_fusion.live_ref, bf16[16,9,3,2,128]{4,3,2,1,0:T(2,128)(2,1)S(1)} %all-to-all-done.pieces_ref, ...), custom_call_target="tpu_custom_call" | custom-call | flops 1000000000 | bytes 6000000 | tf_op jit(solution)/shard_map/attention/pallas_call | solution.py:549
  (38 shorter events, 0.1 us)
Async XLA Ops:
  0.0 7.6 %collective-permute-start = (bf16[3,2,5120]{2,1,0:T(2,128)(2,1)}, bf16[3,2,5120]{2,1,0:T(2,128)(2,1)S(1)}, u32[]{:S(2)}, u32[]{:S(2)}) collective-permute-start(bf16[3,2,5120]{2,1,0:T(2,128)(2,1)} %param.9), channel_id=1, source_target_pairs={{0,1},{1,0},{2,3},{3,2},{4,5},{5,4},{6,7},{7,6},{8,9},{9,8},{10,11... | collective-permute-start | bytes 184328 | tf_op jit(solution)/shard_map/ppermute | solution.py:233
  0.5 9.6 %collective-permute-start.11 = (bf16[3,2,5120]{2,1,0:T(2,128)(2,1)}, bf16[3,2,5120]{2,1,0:T(2,128)(2,1)S(1)}, u32[]{:S(2)}, u32[]{:S(2)}) collective-permute-start(bf16[3,2,5120]{2,1,0:T(2,128)(2,1)} %param.9), channel_id=1, source_target_pairs={{0,12},{1,13},{2,14},{3,15},{4,8},{5,9},{6,10},{7,11},{8,4},{9,5},... | collective-permute-start | bytes 184328 | tf_op jit(solution)/shard_map/ppermute | solution.py:233
  5.1 6.0 %collective-permute-start.7 = (bf16[3,2,5120]{2,1,0:T(2,128)(2,1)}, bf16[3,2,5120]{2,1,0:T(2,128)(2,1)S(1)}, u32[]{:S(2)}, u32[]{:S(2)}) collective-permute-start(bf16[3,2,5120]{2,1,0:T(2,128)(2,1)} %param.9), channel_id=1, source_target_pairs={{0,8},{1,9},{2,10},{3,11},{4,12},{5,13},{6,14},{7,15},{8,0},{9,1},... | collective-permute-start | bytes 184328 | tf_op jit(solution)/shard_map/ppermute | solution.py:233
  6.8 14.1 %slice-start = ((s8[9830400]{0:T(1024)(128)(4,1)}), s8[4194304]{0:T(1024)(128)(4,1)S(1)}, s32[]{:S(2)}) async-start(s8[9830400]{0:T(1024)(128)(4,1)} %bitcast.61), calls=%async_computation.1 | async-start | bytes 8388608
  6.8 1.0 %copy-start.2 = (bf16[3,2,5120]{2,1,0:T(2,128)(2,1)S(1)}, bf16[3,2,5120]{2,1,0:T(2,128)(2,1)}, u32[]{:S(2)}) copy-start(bf16[3,2,5120]{2,1,0:T(2,128)(2,1)} %param.9) | copy-start | bytes 184324
  6.8 7.6 %copy-start.3 = (s32[2,32]{1,0:T(2,128)S(1)}, s32[2,32]{1,0:T(2,128)}, u32[]{:S(2)}) copy-start(s32[2,32]{1,0:T(2,128)} %param.16) | copy-start | bytes 772
  6.8 11.8 %copy-start.1 = (bf16[4,64,5120]{2,1,0:T(8,128)(2,1)S(1)}, bf16[4,64,5120]{2,1,0:T(8,128)(2,1)}, u32[]{:S(2)}) copy-start(bf16[4,64,5120]{2,1,0:T(8,128)(2,1)} %down_ref.1) | copy-start | bytes 7864324
  6.8 14.1 %slice-start.1 = ((s8[9830400]{0:T(1024)(128)(4,1)}), s8[4194304]{0:T(1024)(128)(4,1)S(1)}, s32[]{:S(2)}) async-start(s8[9830400]{0:T(1024)(128)(4,1)} %bitcast.61), calls=%async_computation.2 | async-start | bytes 8388608
  6.8 14.1 %slice-start.2 = ((s8[9830400]{0:T(1024)(128)(4,1)}), s8[1441792]{0:T(1024)(128)(4,1)S(1)}, s32[]{:S(2)}) async-start(s8[9830400]{0:T(1024)(128)(4,1)} %bitcast.61), calls=%async_computation.3 | async-start | bytes 2883584
  7.7 4.9 %collective-permute-start.3 = (bf16[3,2,5120]{2,1,0:T(2,128)(2,1)S(1)}, bf16[3,2,5120]{2,1,0:T(2,128)(2,1)S(1)}, u32[]{:S(2)}, u32[]{:S(2)}) collective-permute-start(bf16[3,2,5120]{2,1,0:T(2,128)(2,1)S(1)} %copy-done.2), channel_id=1, source_target_pairs={{0,4},{1,5},{2,6},{3,7},{4,0},{5,1},{6,2},{7,3},{8,12},{9,13},{10,... | collective-permute-start | bytes 184328 | tf_op jit(solution)/shard_map/ppermute | solution.py:233
  8.4 4.7 %collective-permute-start.1 = (bf16[3,2,5120]{2,1,0:T(2,128)(2,1)S(1)}, bf16[3,2,5120]{2,1,0:T(2,128)(2,1)S(1)}, u32[]{:S(2)}, u32[]{:S(2)}) collective-permute-start(bf16[3,2,5120]{2,1,0:T(2,128)(2,1)S(1)} %copy-done.2), channel_id=1, source_target_pairs={{0,2},{1,3},{2,0},{3,1},{4,6},{5,7},{6,4},{7,5},{8,10},{9,11},{10,... | collective-permute-start | bytes 184328 | tf_op jit(solution)/shard_map/ppermute | solution.py:233
  10.1 4.8 %collective-permute-start.13 = (bf16[3,2,5120]{2,1,0:T(2,128)(2,1)S(1)}, bf16[3,2,5120]{2,1,0:T(2,128)(2,1)S(1)}, u32[]{:S(2)}, u32[]{:S(2)}) collective-permute-start(bf16[3,2,5120]{2,1,0:T(2,128)(2,1)S(1)} %collective-permute-done.11), channel_id=1, source_target_pairs={{0,2},{1,3},{2,0},{3,1},{4,6},{5,7},{6,4},{7,5},{8,10},{9,11},{10,... | collective-permute-start | bytes 184328 | tf_op jit(solution)/shard_map/ppermute | solution.py:233
  10.4 4.4 %collective-permute-start.12 = (bf16[3,2,5120]{2,1,0:T(2,128)(2,1)S(1)}, bf16[3,2,5120]{2,1,0:T(2,128)(2,1)S(1)}, u32[]{:S(2)}, u32[]{:S(2)}) collective-permute-start(bf16[3,2,5120]{2,1,0:T(2,128)(2,1)S(1)} %collective-permute-done.11), channel_id=1, source_target_pairs={{0,1},{1,0},{2,3},{3,2},{4,5},{5,4},{6,7},{7,6},{8,9},{9,8},{10,11... | collective-permute-start | bytes 184328 | tf_op jit(solution)/shard_map/ppermute | solution.py:233
  11.1 4.4 %collective-permute-start.9 = (bf16[3,2,5120]{2,1,0:T(2,128)(2,1)S(1)}, bf16[3,2,5120]{2,1,0:T(2,128)(2,1)S(1)}, u32[]{:S(2)}, u32[]{:S(2)}) collective-permute-start(bf16[3,2,5120]{2,1,0:T(2,128)(2,1)S(1)} %collective-permute-done.7), channel_id=1, source_target_pairs={{0,2},{1,3},{2,0},{3,1},{4,6},{5,7},{6,4},{7,5},{8,10},{9,11},{10,... | collective-permute-start | bytes 184328 | tf_op jit(solution)/shard_map/ppermute | solution.py:233
  12.6 2.9 %collective-permute-start.8 = (bf16[3,2,5120]{2,1,0:T(2,128)(2,1)S(1)}, bf16[3,2,5120]{2,1,0:T(2,128)(2,1)S(1)}, u32[]{:S(2)}, u32[]{:S(2)}) collective-permute-start(bf16[3,2,5120]{2,1,0:T(2,128)(2,1)S(1)} %collective-permute-done.7), channel_id=1, source_target_pairs={{0,1},{1,0},{2,3},{3,2},{4,5},{5,4},{6,7},{7,6},{8,9},{9,8},{10,11... | collective-permute-start | bytes 184328 | tf_op jit(solution)/shard_map/ppermute | solution.py:233
  13.1 4.2 %collective-permute-start.5 = (bf16[3,2,5120]{2,1,0:T(2,128)(2,1)S(1)}, bf16[3,2,5120]{2,1,0:T(2,128)(2,1)S(1)}, u32[]{:S(2)}, u32[]{:S(2)}) collective-permute-start(bf16[3,2,5120]{2,1,0:T(2,128)(2,1)S(1)} %collective-permute-done.3), channel_id=1, source_target_pairs={{0,2},{1,3},{2,0},{3,1},{4,6},{5,7},{6,4},{7,5},{8,10},{9,11},{10,... | collective-permute-start | bytes 184328 | tf_op jit(solution)/shard_map/ppermute | solution.py:233
  14.8 2.6 %collective-permute-start.4 = (bf16[3,2,5120]{2,1,0:T(2,128)(2,1)S(1)}, bf16[3,2,5120]{2,1,0:T(2,128)(2,1)S(1)}, u32[]{:S(2)}, u32[]{:S(2)}) collective-permute-start(bf16[3,2,5120]{2,1,0:T(2,128)(2,1)S(1)} %collective-permute-done.3), channel_id=1, source_target_pairs={{0,1},{1,0},{2,3},{3,2},{4,5},{5,4},{6,7},{7,6},{8,9},{9,8},{10,11... | collective-permute-start | bytes 184328 | tf_op jit(solution)/shard_map/ppermute | solution.py:233
  14.8 2.6 %collective-permute-start.2 = (bf16[3,2,5120]{2,1,0:T(2,128)(2,1)S(1)}, bf16[3,2,5120]{2,1,0:T(2,128)(2,1)S(1)}, u32[]{:S(2)}, u32[]{:S(2)}) collective-permute-start(bf16[3,2,5120]{2,1,0:T(2,128)(2,1)S(1)} %collective-permute-done.1), channel_id=1, source_target_pairs={{0,1},{1,0},{2,3},{3,2},{4,5},{5,4},{6,7},{7,6},{8,9},{9,8},{10,11... | collective-permute-start | bytes 184328 | tf_op jit(solution)/shard_map/ppermute | solution.py:233
  15.5 1.9 %collective-permute-start.14 = (bf16[3,2,5120]{2,1,0:T(2,128)(2,1)S(1)}, bf16[3,2,5120]{2,1,0:T(2,128)(2,1)S(1)}, u32[]{:S(2)}, u32[]{:S(2)}) collective-permute-start(bf16[3,2,5120]{2,1,0:T(2,128)(2,1)S(1)} %collective-permute-done.13), channel_id=1, source_target_pairs={{0,1},{1,0},{2,3},{3,2},{4,5},{5,4},{6,7},{7,6},{8,9},{9,8},{10,11... | collective-permute-start | bytes 184328 | tf_op jit(solution)/shard_map/ppermute | solution.py:233
  15.5 1.9 %collective-permute-start.10 = (bf16[3,2,5120]{2,1,0:T(2,128)(2,1)S(1)}, bf16[3,2,5120]{2,1,0:T(2,128)(2,1)S(1)}, u32[]{:S(2)}, u32[]{:S(2)}) collective-permute-start(bf16[3,2,5120]{2,1,0:T(2,128)(2,1)S(1)} %collective-permute-done.9), channel_id=1, source_target_pairs={{0,1},{1,0},{2,3},{3,2},{4,5},{5,4},{6,7},{7,6},{8,9},{9,8},{10,11... | collective-permute-start | bytes 184328 | tf_op jit(solution)/shard_map/ppermute | solution.py:233
  17.3 1.2 %collective-permute-start.6 = (bf16[3,2,5120]{2,1,0:T(2,128)(2,1)S(1)}, bf16[3,2,5120]{2,1,0:T(2,128)(2,1)S(1)}, u32[]{:S(2)}, u32[]{:S(2)}) collective-permute-start(bf16[3,2,5120]{2,1,0:T(2,128)(2,1)S(1)} %collective-permute-done.5), channel_id=1, source_target_pairs={{0,1},{1,0},{2,3},{3,2},{4,5},{5,4},{6,7},{7,6},{8,9},{9,8},{10,11... | collective-permute-start | bytes 184328 | tf_op jit(solution)/shard_map/ppermute | solution.py:233
  20.6 1.4 %collective-permute-start.15 = (bf16[48,128]{1,0:T(8,128)(2,1)S(1)}, bf16[48,128]{1,0:T(8,128)(2,1)S(1)}, u32[]{:S(2)}, u32[]{:S(2)}) collective-permute-start(bf16[48,128]{1,0:T(8,128)(2,1)S(1)} %get-tuple-element.21), channel_id=1, source_target_pairs={{0,1},{1,0},{2,3},{3,2},{4,5},{5,4},{6,7},{7,6},{8,9},{9,8},{10,11... | collective-permute-start | bytes 36872 | tf_op jit(solution)/shard_map/ppermute | solution.py:233
  22.0 3.8 %collective-permute-start.16 = (bf16[48,128]{1,0:T(8,128)(2,1)S(1)}, bf16[48,128]{1,0:T(8,128)(2,1)S(1)}, u32[]{:S(2)}, u32[]{:S(2)}) collective-permute-start(bf16[48,128]{1,0:T(8,128)(2,1)S(1)} %add.62), channel_id=1, source_target_pairs={{0,2},{1,3},{2,0},{3,1},{4,6},{5,7},{6,4},{7,5},{8,10},{9,11},{10,... | collective-permute-start | bytes 36872 | tf_op jit(solution)/shard_map/ppermute | solution.py:233
  25.8 8.4 %copy-start = (bf16[64,64,320]{2,1,0:T(8,128)(2,1)S(1)}, bf16[64,64,320]{2,1,0:T(8,128)(2,1)}, u32[]{:S(2)}) copy-start(bf16[64,64,320]{2,1,0:T(8,128)(2,1)} %param.12) | copy-start | bytes 7864324
  25.8 3.8 %collective-permute-start.17 = (bf16[48,128]{1,0:T(8,128)(2,1)S(1)}, bf16[48,128]{1,0:T(8,128)(2,1)S(1)}, u32[]{:S(2)}, u32[]{:S(2)}) collective-permute-start(bf16[48,128]{1,0:T(8,128)(2,1)S(1)} %add.63), channel_id=1, source_target_pairs={{0,4},{1,5},{2,6},{3,7},{4,0},{5,1},{6,2},{7,3},{8,12},{9,13},{10,... | collective-permute-start | bytes 36872 | tf_op jit(solution)/shard_map/ppermute | solution.py:233
  29.6 4.7 %collective-permute-start.18 = (bf16[48,128]{1,0:T(8,128)(2,1)S(1)}, bf16[48,128]{1,0:T(8,128)(2,1)S(1)}, u32[]{:S(2)}, u32[]{:S(2)}) collective-permute-start(bf16[48,128]{1,0:T(8,128)(2,1)S(1)} %add.64.low_ref), channel_id=1, source_target_pairs={{0,8},{1,9},{2,10},{3,11},{4,12},{5,13},{6,14},{7,15},{8,0},{9,1},... | collective-permute-start | bytes 36872 | tf_op jit(solution)/shard_map/ppermute | solution.py:233
  35.9 15.0 %all-to-all-start = ((bf16[16,9,3,2,128]{4,3,2,1,0:T(2,128)(2,1)}), bf16[16,9,3,2,128]{4,3,2,1,0:T(2,128)(2,1)S(1)}, u32[]{:S(2)}, u32[]{:S(2)}) async-start(bf16[16,9,3,2,128]{4,3,2,1,0:T(2,128)(2,1)} %update_values.1), calls=%async_computation | async-start | bytes 442368 | tf_op jit(solution)/shard_map/all_to_all | solution.py:642

commit v11 on v10

--- a/solution.py
+++ b/solution.py
@@ -257,12 +257,12 @@
         copy.wait()
 
 
-CACHE_PARTS = 4
-
-
-def cache_kernel(pool_ref, keys_ref, values_ref, raw, values, sem, out_sem):
+CACHE_PARTS = 2
+
+
+def cache_kernel(first, pool_ref, keys_ref, values_ref, raw, values, sem, out_sem):
     heads, tokens = raw.shape[:2]
-    copies = start_all([pltpu.make_async_copy(pool_ref.at[:, h], raw.at[h], sem.at[h]) for h in range(heads)])
+    copies = start_all([pltpu.make_async_copy(pool_ref.at[:, first + h], raw.at[h], sem.at[h]) for h in range(heads)])
     rows = raw.reshape(heads, 2 * tokens, HD)
     to = lax.broadcasted_iota(jnp.int32, (2 * tokens, 2 * tokens), 0)
     source = lax.broadcasted_iota(jnp.int32, (2 * tokens, 2 * tokens), 1)
@@ -283,10 +283,10 @@
     wait_all(sent)
 
 
-def cache_by_head(pool):
-    tokens, heads = pool.shape[:2]
+def cache_by_head(pool, first, heads):
+    tokens = pool.shape[0]
     return pl.pallas_call(
-        cache_kernel,
+        functools.partial(cache_kernel, first),
         out_shape=(
             jax.ShapeDtypeStruct((heads, tokens, HD), pool.dtype),
             pltpu.HBM((heads, tokens, HD), pool.dtype),
@@ -299,7 +299,7 @@
             pltpu.SemaphoreType.DMA((heads,)),
             pltpu.SemaphoreType.DMA((CACHE_PARTS,)),
         ],
-        compiler_params=pltpu.CompilerParams(vmem_limit_bytes=16 * 2**20),
+        compiler_params=pltpu.CompilerParams(vmem_limit_bytes=12 * 2**20),
         cost_estimate=pl.CostEstimate(flops=0, bytes_accessed=12 * 10**6, transcendentals=0),
         name="cache_by_head",
     )(in_hbm(pool))
@@ -419,12 +419,15 @@
     )(x, weight)
 
 
-def update_kernel(stored_ref, query_ref, key_ref, base_ref, up_ref, low_ref, more_ref, send_ref, buf, sem):
-    half, packed = low_ref.shape
+def update_kernel(stored_ref, query_ref, key_ref, base_ref, up_ref, *refs):
+    lows, (send_ref, buf, sem) = refs[:-3], refs[-3:]
+    half, packed = lows[0].shape
     rank = packed // 2
     rows = 2 * half
     count = send_ref.shape[0]
-    low = low_ref[...].astype(jnp.float32) + more_ref[...].astype(jnp.float32)
+    low = lows[0][...].astype(jnp.float32)
+    for more in lows[1:]:
+        low = low + more[...].astype(jnp.float32)
     low = jnp.concatenate([low[:, :rank], low[:, rank:]], axis=0)
     batch = 256 // rank
     spread = jnp.concatenate([low] * batch, axis=1)
@@ -442,12 +445,12 @@
     )
 
 
-def update_values(stored, query, key, base, up, low, more):
+def update_values(stored, query, key, base, up, lows):
     chunks, steps, count = query.shape[:3]
     return pl.pallas_call(
         update_kernel,
         out_shape=pltpu.HBM((count, 3 * chunks, steps, 2, HD), query.dtype),
-        in_specs=[VMEM] * 7,
+        in_specs=[VMEM] * (5 + len(lows)),
         out_specs=HBM,
         scratch_shapes=[
             pltpu.VMEM((3 * chunks, steps, count, 2, HD), query.dtype),
@@ -456,10 +459,11 @@
         compiler_params=pltpu.CompilerParams(vmem_limit_bytes=8 * 2**20),
         cost_estimate=pl.CostEstimate(flops=3 * 10**8, bytes_accessed=4 * 10**6, transcendentals=0),
         name="update_values",
-    )(stored, query, key, base, up, low, more)
-
-
-def attend_kernel(cos_ref, sin_ref, live_ref, pieces_ref, keys_ref, values_ref, out_ref, values_buf, kn_ref, vn_ref, sem):
+    )(stored, query, key, base, up, *lows)
+
+
+def attend_kernel(cos_ref, sin_ref, live_ref, pieces_ref, *refs):
+    keys_refs, values_refs, (out_ref, values_buf, kn_ref, vn_ref, sem) = refs[:2], refs[2:4], refs[4:]
     count, _, steps = pieces_ref.shape[:3]
     rows = 2 * steps
     each = pieces_ref.shape[1] // 3
@@ -467,10 +471,11 @@
     lanes = heads * HD
     group = rows * HEAD_BLOCK
     chips = range(count // 2)
+    places = [divmod(c, count // 4) for c in chips]
     fetches = start_all(
         [
-            pltpu.make_async_copy(values_ref.at[c * heads : (c + 1) * heads], values_buf.at[c], sem.at[c])
-            for c in chips
+            pltpu.make_async_copy(values_refs[half].at[at * heads : (at + 1) * heads], values_buf.at[c], sem.at[c])
+            for c, (half, at) in enumerate(places)
         ]
     )
     cosine = cos_ref[...][:rows]
@@ -514,7 +519,8 @@
         spreads.append(jnp.where(own_head, spread, 0.0).astype(jnp.bfloat16))
     scores, fresh = [], []
     for c in chips:
-        keys = jnp.concatenate([keys_ref[c * heads + h] for h in range(heads)], axis=1)
+        half, at = places[c]
+        keys = jnp.concatenate([keys_refs[half][at * heads + h] for h in range(heads)], axis=1)
         kn = kn_ref[c].astype(jnp.bfloat16)
         scores.append(lax.dot_general(spreads[c], keys, CONTRACT_LANES, preferred_element_type=jnp.float32))
         fresh.append(lax.dot_general(spreads[c], kn, CONTRACT_LANES, preferred_element_type=jnp.float32))
@@ -543,13 +549,13 @@
 
 def attend(cosine, sine, live, pieces, keys, values):
     count, _, steps = pieces.shape[:3]
-    heads, tokens = keys.shape[:2]
+    heads, tokens = 2 * keys[0].shape[0], keys[0].shape[1]
     chips = count // 2
     per = heads // chips
     return pl.pallas_call(
         attend_kernel,
         out_shape=jax.ShapeDtypeStruct((steps, heads, 2, HD), jnp.bfloat16),
-        in_specs=[VMEM] * 5 + [HBM],
+        in_specs=[VMEM] * 6 + [HBM] * 2,
         out_specs=VMEM,
         scratch_shapes=[pltpu.VMEM((chips, per, tokens, HD), jnp.bfloat16)]
         + [pltpu.VMEM((chips, 16, per * HD), jnp.float32)] * 2
@@ -557,7 +563,7 @@
         compiler_params=pltpu.CompilerParams(vmem_limit_bytes=16 * 2**20),
         cost_estimate=pl.CostEstimate(flops=10**9, bytes_accessed=6 * 10**6, transcendentals=0),
         name="attention",
-    )(cosine, sine, live, pieces, keys, in_hbm(values))
+    )(cosine, sine, live, pieces, *keys, *[in_hbm(x) for x in values])
 
 
 def chip_plan(
@@ -580,19 +586,7 @@
     adapter_count = adapter_storage_row.shape[0]
 
     tokens = pool_pages * page_len
-    keys, values = cache_by_head(key_value_pool.reshape(tokens, 2, heads, HD).transpose(0, 2, 1, 3))
-
-    held = {m: trade(hidden, m, count) for m in range(8, count, 4)}
-    held[1] = trade(hidden, 1, count)
-    held[0], held[1] = lax.optimization_barrier((hidden, held[1]))
-    held[4] = trade(held[0], 4, count)
-    held[2] = trade(held[0], 2, count)
-    held.update({m | 2: trade(held[m], 2, count) for m in range(4, count, 4)})
-    held.update({m | 1: trade(held[m], 1, count) for m in range(2, count, 2)})
-    blocks = [
-        held[k].reshape(steps, req_dev, heads, HD).transpose(0, 2, 1, 3) for k in range(count)
-    ]
-    blocks[0] = in_hbm(blocks[0])
+    pool = key_value_pool.reshape(tokens, 2, heads, HD).transpose(0, 2, 1, 3)
 
     stored = jnp.sum(
         jnp.where(
@@ -604,46 +598,36 @@
     )
     slot, column = index_work((me * holder_count).astype(jnp.int32).reshape(1), stored, steps)
 
-    held = {m: trade(hidden, m, count) for m in range(8, count, 4)}
-    held[1] = trade(hidden, 1, count)
-    held[0], held[1] = lax.optimization_barrier((hidden, held[1]))
-    held[4] = trade(held[0], 4, count)
-    held[2] = trade(held[0], 2, count)
+    held = {m: trade(hidden, m, count) for m in range(count - 4, 0, -4)}
+    own, slot, column = lax.optimization_barrier((hidden, slot, column))
+    held[2] = trade(own, 2, count)
+    own, held[4] = lax.optimization_barrier((hidden, held[4]))
+    held[1] = trade(own, 1, count)
+    held[0] = hidden
     held.update({m | 2: trade(held[m], 2, count) for m in range(4, count, 4)})
     held.update({m | 1: trade(held[m], 1, count) for m in range(2, count, 2)})
-    blocks = [
-        held[k].reshape(steps, req_dev, heads, HD).transpose(0, 2, 1, 3) for k in range(count)
-    ]
+    blocks = [held[k].reshape(steps, req_dev, heads, HD).transpose(0, 2, 1, 3) for k in range(count)]
     blocks[0] = in_hbm(blocks[0])
-
-    stored = jnp.sum(
-        jnp.where(
-            request_adapter[:, None] == jnp.arange(adapter_count, dtype=jnp.int32)[None, :],
-            adapter_storage_row[None, :],
-            0,
-        ),
-        axis=1,
-    )
-    slot = jnp.concatenate([stored - me * holder_count] * steps)[None, :]
 
     x, low = low_of(me.astype(jnp.int32).reshape(1), blocks, slot, adapter_down_maps)
     weight = query_key_value_weight.transpose(0, 2, 1)
-    parts = []
-    hops = [1 << i for i in range(count.bit_length() - 1)]
-    for i, mask in enumerate(hops):
-        arrived = trade(low, mask, count)
-        if i < 3:
-            part = project(i, x, weight)
-            arrived, part = lax.optimization_barrier((arrived, part))
-            parts.append(part)
-        if mask != hops[-1]:
-            low = low + arrived
-    send = update_values(column, *parts, adapter_up_maps.reshape(adapter_count * rank, -1), low, arrived)
+    arrived = [trade(low, m, count) for m in (1, 2, 3)]
+    query, key = project(0, x, weight), project(1, x, weight)
+    arrived, query, key, pool = lax.optimization_barrier((arrived, query, key, pool))
+    low = (low + arrived[0]) + (arrived[1] + arrived[2])
+    arrived = [trade(low, m, count) for m in range(4, count, 4)]
+    base = project(2, x, weight)
+    early_cache = cache_by_head(pool, 0, heads // 2)
+    arrived, base, early_cache = lax.optimization_barrier((arrived, base, early_cache))
+    send = update_values(column, query, key, base, adapter_up_maps.reshape(adapter_count * rank, -1), [low, *arrived])
+    send, pool = lax.optimization_barrier((send, pool))
+    late_cache = cache_by_head(pool, heads // 2, heads // 2)
     pieces = lax.all_to_all(send, "replica", split_axis=0, concat_axis=0, tiled=True)
 
     my_lengths = lax.dynamic_slice_in_dim(lengths, me * req_dev, req_dev)
     cosine, sine = rotation(my_lengths, steps)
     live = live_tokens(my_lengths, request_page_table, pool_pages, page_len).astype(jnp.int32)
+    keys, values = zip(early_cache, late_cache)
     out = attend(cosine, sine, live.reshape(req_dev, tokens), pieces, keys, values)
     return out.transpose(0, 2, 1, 3).reshape(steps, req_dev, width)
 

time: 55.2 us -> 61.4 us (1.11)
  local copies, waits for them, and re-layouts: 1.49 us -> 5.1 us
  Pallas kernels: 18.5 us -> 20.7 us
    unnamed x14 -> x12, local copies, waits for them, and re-layouts: 0.17 us -> 4.44 us
    pallas_call x1 -> x2, Pallas kernels: 6.91 us -> 9.45 us  [cache_by_head(): pl.pallas_call(functools.partial(cache_kernel, first), out_shape=(jax.Sha...]
    ppermute x19 -> x21, waiting for transfers between devices: 8.95 us -> 6.49 us  [trade(): return lax.ppermute(value, 'replica', [(i, i ^ mask) for i in range(count)])]
    all_to_all x1, waiting for transfers between devices: 1.78 us -> 4.05 us  [chip_plan(): lax.all_to_all(send, 'replica', split_axis=0, concat_axis=0, tiled=True)]
    ppermute x19 -> x21, starting transfers between devices: 16.9 us -> 18.2 us  [trade(): return lax.ppermute(value, 'replica', [(i, i ^ mask) for i in range(count)])]
    all_to_all x1, starting transfers between devices: 5.62 us -> 4.82 us  [chip_plan(): lax.all_to_all(send, 'replica', split_axis=0, concat_axis=0, tiled=True)]
    dynamic_slice x1, local copies, waits for them, and re-layouts: 0.73 us -> 0.08 us  [chip_plan(): my_lengths = lax.dynamic_slice_in_dim(lengths, me * req_dev, req_dev)]
  transfers between devices with their start and end apart: 20 -> 22, of which waited for: 10 -> 7; matrix products, arithmetic and copies ran while one was open for 5% -> 3% of each run, Pallas kernels for 20% -> 21%
where the time goes in v11:
time: 61.4 us; the launch traced here: 61 us
  starting transfers between devices  23 us (37%)
  Pallas kernels  20.7 us (34%)
  waiting for transfers between devices  10.5 us (17%)
  local copies, waits for them, and re-layouts  5.1 us (8%)
  other arithmetic  1.24 us (2%)
    ppermute x21, starting transfers between devices, trade(): return lax.ppermute(value, 'replica', [(i, i ^ mask) for i in range(count)])  18.2 us
    pallas_call x2, Pallas kernels, cache_by_head(): pl.pallas_call(functools.partial(cache_kernel, first), out_shape=(jax.Sha...  9.45 us
    ppermute x21, waiting for transfers between devices, trade(): return lax.ppermute(value, 'replica', [(i, i ^ mask) for i in range(count)])  6.49 us
    all_to_all x1, starting transfers between devices, chip_plan(): lax.all_to_all(send, 'replica', split_axis=0, concat_axis=0, tiled=True)  4.82 us
    unnamed x12, local copies, waits for them, and re-layouts  4.44 us
    all_to_all x1, waiting for transfers between devices, chip_plan(): lax.all_to_all(send, 'replica', split_axis=0, concat_axis=0, tiled=True)  4.05 us
    pallas_call x1, Pallas kernels, attend(): pl.pallas_call(attend_kernel, out_shape=jax.ShapeDtypeStruct((steps, head...  3.89 us
    pallas_call x3, Pallas kernels, project(): pl.pallas_call(functools.partial(project_kernel, which), out_shape=chunks...  3.42 us
  transfers between devices with their start and end apart: 22, of which 7 were waited for; matrix products, arithmetic and copies ran while one was open for 3% of the time, Pallas kernels for 21%

profile of v11, /device:TPU:0, one launch (start us, length us, event | category | flops | bytes accessed | tf_op | source)
XLA Modules:
  0.0 61.0 jit_solution(9559570646067514495)
XLA Ops:
  0.0 3.0 %collective-permute-start = (bf16[3,2,5120]{2,1,0:T(2,128)(2,1)}, bf16[3,2,5120]{2,1,0:T(2,128)(2,1)S(1)}, u32[]{:S(2)}, u32[]{:S(2)}) collective-permute-start(bf16[3,2,5120]{2,1,0:T(2,128)(2,1)} %param.9), channel_id=1, source_target_pairs={{0,4},{1,5},{2,6},{3,7},{4,0},{5,1},{6,2},{7,3},{8,12},{9,13},{10,... | collective-permute-start | bytes 184328 | tf_op jit(solution)/shard_map/ppermute | solution.py:233
  3.0 2.5 %collective-permute-start.11 = (bf16[3,2,5120]{2,1,0:T(2,128)(2,1)}, bf16[3,2,5120]{2,1,0:T(2,128)(2,1)S(1)}, u32[]{:S(2)}, u32[]{:S(2)}) collective-permute-start(bf16[3,2,5120]{2,1,0:T(2,128)(2,1)} %param.9), channel_id=1, source_target_pairs={{0,12},{1,13},{2,14},{3,15},{4,8},{5,9},{6,10},{7,11},{8,4},{9,5},... | collective-permute-start | bytes 184328 | tf_op jit(solution)/shard_map/ppermute | solution.py:233
  5.5 0.1 collective-permute-start.7
  5.6 0.8 %select_reduce_fusion.1 = s32[32]{0:T(128)S(1)} fusion(s32[64]{0:T(128)} %param.13, s32[32]{0:T(128)} %param.14), kind=kLoop, calls=%fused_computation.2 | loop fusion | flops 6112 | bytes 512 | tf_op jit(solution)/shard_map/reduce_sum | solution.py:591
  6.5 0.2 index_work.1
  6.7 0.6 %copy-done.3 = bf16[3,2,5120]{2,1,0:T(2,128)(2,1)S(1)} copy-done((bf16[3,2,5120]{2,1,0:T(2,128)(2,1)S(1)}, bf16[3,2,5120]{2,1,0:T(2,128)(2,1)}, u32[]{:S(2)}) %copy-start.3) | copy-done | bytes 61464
  7.3 1.5 %collective-permute-start.2 = (bf16[3,2,5120]{2,1,0:T(2,128)(2,1)S(1)}, bf16[3,2,5120]{2,1,0:T(2,128)(2,1)S(1)}, u32[]{:S(2)}, u32[]{:S(2)}) collective-permute-start(bf16[3,2,5120]{2,1,0:T(2,128)(2,1)S(1)} %copy-done.3), channel_id=1, source_target_pairs={{0,2},{1,3},{2,0},{3,1},{4,6},{5,7},{6,4},{7,5},{8,10},{9,11},{10,... | collective-permute-start | bytes 184328 | tf_op jit(solution)/shard_map/ppermute | solution.py:233
  8.8 0.1 dynamic_slice.3
  8.9 0.1 add.55
  9.0 2.5 %collective-permute-done.2 = bf16[3,2,5120]{2,1,0:T(2,128)(2,1)S(1)} collective-permute-done((bf16[3,2,5120]{2,1,0:T(2,128)(2,1)S(1)}, bf16[3,2,5120]{2,1,0:T(2,128)(2,1)S(1)}, u32[]{:S(2)}, u32[]{:S(2)}) %collective-permute-start.2) | collective-permute-done | bytes 61472 | tf_op jit(solution)/shard_map/ppermute | solution.py:233
  11.5 0.1 fusion
  11.6 1.6 %collective-permute-start.5 = (bf16[3,2,5120]{2,1,0:T(2,128)(2,1)S(1)}, bf16[3,2,5120]{2,1,0:T(2,128)(2,1)S(1)}, u32[]{:S(2)}, u32[]{:S(2)}) collective-permute-start(bf16[3,2,5120]{2,1,0:T(2,128)(2,1)S(1)} %collective-permute-done), channel_id=1, source_target_pairs={{0,2},{1,3},{2,0},{3,1},{4,6},{5,7},{6,4},{7,5},{8,10},{9,11},{10,... | collective-permute-start | bytes 184328 | tf_op jit(solution)/shard_map/ppermute | solution.py:233
  13.2 0.2 collective-permute-start.4
  13.5 0.3 collective-permute-start.1
  13.8 0.5 collective-permute-start.13
  14.3 1.5 %collective-permute-start.9 = (bf16[3,2,5120]{2,1,0:T(2,128)(2,1)S(1)}, bf16[3,2,5120]{2,1,0:T(2,128)(2,1)S(1)}, u32[]{:S(2)}, u32[]{:S(2)}) collective-permute-start(bf16[3,2,5120]{2,1,0:T(2,128)(2,1)S(1)} %collective-permute-done.7), channel_id=1, source_target_pairs={{0,2},{1,3},{2,0},{3,1},{4,6},{5,7},{6,4},{7,5},{8,10},{9,11},{10,... | collective-permute-start | bytes 184328 | tf_op jit(solution)/shard_map/ppermute | solution.py:233
  15.8 0.1 select_reduce_fusion
  16.0 0.2 collective-permute-done.5
  16.1 0.3 collective-permute-start.8
  16.5 0.2 collective-permute-start.6
  16.6 1.9 %collective-permute-done.13 = bf16[3,2,5120]{2,1,0:T(2,128)(2,1)S(1)} collective-permute-done((bf16[3,2,5120]{2,1,0:T(2,128)(2,1)S(1)}, bf16[3,2,5120]{2,1,0:T(2,128)(2,1)S(1)}, u32[]{:S(2)}, u32[]{:S(2)}) %collective-permute-start.13) | collective-permute-done | bytes 61472 | tf_op jit(solution)/shard_map/ppermute | solution.py:233
  18.6 0.7 %collective-permute-done.9 = bf16[3,2,5120]{2,1,0:T(2,128)(2,1)S(1)} collective-permute-done((bf16[3,2,5120]{2,1,0:T(2,128)(2,1)S(1)}, bf16[3,2,5120]{2,1,0:T(2,128)(2,1)S(1)}, u32[]{:S(2)}, u32[]{:S(2)}) %collective-permute-start.9) | collective-permute-done | bytes 61472 | tf_op jit(solution)/shard_map/ppermute | solution.py:233
  19.2 0.6 collective-permute-done.14
  19.8 0.7 %collective-permute-done.10 = bf16[3,2,5120]{2,1,0:T(2,128)(2,1)S(1)} collective-permute-done((bf16[3,2,5120]{2,1,0:T(2,128)(2,1)S(1)}, bf16[3,2,5120]{2,1,0:T(2,128)(2,1)S(1)}, u32[]{:S(2)}, u32[]{:S(2)}) %collective-permute-start.10) | collective-permute-done | bytes 61472 | tf_op jit(solution)/shard_map/ppermute | solution.py:233
  20.5 2.1 %low_rows.1 = (bf16[3,40,16,2,128]{4,3,2,1,0:T(2,128)(2,1)S(1)}, bf16[48,128]{1,0:T(8,128)(2,1)S(1)}) custom-call(s32[1]{0:T(128)} %bitcast.2.me_ref, s32[1,96]{1,0:T(1,128)S(1)} %get-tuple-element.35.slot_ref, bf16[4,64,5120]{2,1,0:T(8,128)(2,1)S(1)} %copy-done.2, bf16[3,40,2,128]{3,2,1,0:T(2,128)(2,1)} %bitcast.81, bf16[3,40,2,128]{3,2,1,0:T(2,128)(2,1)S(1)} %bitcast.70, ...), custom_call_target="tpu_custom_call" | custom-call | flops 100000000 | bytes 4000000 | tf_op jit(solution)/shard_map/low_rows/pallas_call | solution.py:369
  22.6 0.9 %collective-permute-start.17 = (bf16[48,128]{1,0:T(8,128)(2,1)S(1)}, bf16[48,128]{1,0:T(8,128)(2,1)S(1)}, u32[]{:S(2)}, u32[]{:S(2)}) collective-permute-start(bf16[48,128]{1,0:T(8,128)(2,1)S(1)} %get-tuple-element.39), channel_id=1, source_target_pairs={{0,3},{1,2},{2,1},{3,0},{4,7},{5,6},{6,5},{7,4},{8,11},{9,10},{10,... | collective-permute-start | bytes 36872 | tf_op jit(solution)/shard_map/ppermute | solution.py:233
  23.5 0.9 %collective-permute-start.16 = (bf16[48,128]{1,0:T(8,128)(2,1)S(1)}, bf16[48,128]{1,0:T(8,128)(2,1)S(1)}, u32[]{:S(2)}, u32[]{:S(2)}) collective-permute-start(bf16[48,128]{1,0:T(8,128)(2,1)S(1)} %get-tuple-element.39), channel_id=1, source_target_pairs={{0,2},{1,3},{2,0},{3,1},{4,6},{5,7},{6,4},{7,5},{8,10},{9,11},{10,... | collective-permute-start | bytes 36872 | tf_op jit(solution)/shard_map/ppermute | solution.py:233
  24.4 0.1 collective-permute-start.15
  24.5 3.8 %copy-done = bf16[3,5120,320]{1,2,0:T(8,128)(2,1)S(1)} copy-done((bf16[3,5120,320]{1,2,0:T(8,128)(2,1)S(1)}, bf16[3,5120,320]{1,2,0:T(8,128)(2,1)}, u32[]{:S(2)}) %copy-start) | copy-done | bytes 9830424
  28.3 1.1 %project.4.key_ref = bf16[3,3,16,2,128]{4,3,2,1,0:T(2,128)(2,1)S(1)} custom-call(bf16[3,40,16,2,128]{4,3,2,1,0:T(2,128)(2,1)S(1)} %get-tuple-element.40.x_ref, bf16[3,320,5120]{2,1,0:T(8,128)(2,1)S(1)} %bitcast.59), custom_call_target="tpu_custom_call" | custom-call | flops 500000000 | bytes 4000000 | tf_op jit(solution)/shard_map/project/pallas_call | solution.py:411
  29.5 1.1 %project.3.query_ref = bf16[3,3,16,2,128]{4,3,2,1,0:T(2,128)(2,1)S(1)} custom-call(bf16[3,40,16,2,128]{4,3,2,1,0:T(2,128)(2,1)S(1)} %get-tuple-element.40.x_ref, bf16[3,320,5120]{2,1,0:T(8,128)(2,1)S(1)} %bitcast.60), custom_call_target="tpu_custom_call" | custom-call | flops 500000000 | bytes 4000000 | tf_op jit(solution)/shard_map/project/pallas_call | solution.py:411
  30.7 3.0 %collective-permute-start.20 = (bf16[48,128]{1,0:T(8,128)(2,1)S(1)}, bf16[48,128]{1,0:T(8,128)(2,1)S(1)}, u32[]{:S(2)}, u32[]{:S(2)}) collective-permute-start(bf16[48,128]{1,0:T(8,128)(2,1)S(1)} %add_add_fusion.refs_0_), channel_id=1, source_target_pairs={{0,12},{1,13},{2,14},{3,15},{4,8},{5,9},{6,10},{7,11},{8,4},{9,5},... | collective-permute-start | bytes 36872 | tf_op jit(solution)/shard_map/ppermute | solution.py:233
  33.6 0.3 collective-permute-start.19
  34.0 1.1 %collective-permute-start.18 = (bf16[48,128]{1,0:T(8,128)(2,1)S(1)}, bf16[48,128]{1,0:T(8,128)(2,1)S(1)}, u32[]{:S(2)}, u32[]{:S(2)}) collective-permute-start(bf16[48,128]{1,0:T(8,128)(2,1)S(1)} %add_add_fusion.refs_0_), channel_id=1, source_target_pairs={{0,4},{1,5},{2,6},{3,7},{4,0},{5,1},{6,2},{7,3},{8,12},{9,13},{10,... | collective-permute-start | bytes 36872 | tf_op jit(solution)/shard_map/ppermute | solution.py:233
  35.1 1.1 %project.5.base_ref = f32[96,320]{1,0:T(8,128)S(1)} custom-call(bf16[3,40,16,2,128]{4,3,2,1,0:T(2,128)(2,1)S(1)} %get-tuple-element.40.x_ref, bf16[3,320,5120]{2,1,0:T(8,128)(2,1)S(1)} %bitcast.61), custom_call_target="tpu_custom_call" | custom-call | flops 500000000 | bytes 4000000 | tf_op jit(solution)/shard_map/project/pallas_call | solution.py:411
  36.2 4.8 %cache_by_head.2 = (bf16[20,256,128]{2,1,0:T(8,128)(2,1)S(1)}, bf16[20,256,128]{2,1,0:T(8,128)(2,1)}) custom-call(bf16[256,40,2,128]{3,2,1,0:T(2,128)(2,1)} %bitcast.79), custom_call_target="tpu_custom_call" | custom-call | bytes 12000000 | tf_op jit(solution)/shard_map/cache_by_head/pallas_call | solution.py:288
  41.1 1.6 %update_values.1 = bf16[16,9,3,2,128]{4,3,2,1,0:T(2,128)(2,1)} custom-call(s32[96,1]{1,0:T(8,128)S(1)} %get-tuple-element.34.stored_ref, bf16[3,3,16,2,128]{4,3,2,1,0:T(2,128)(2,1)S(1)} %project.3.query_ref, bf16[3,3,16,2,128]{4,3,2,1,0:T(2,128)(2,1)S(1)} %project.4.key_ref, f32[96,320]{1,0:T(8,128)S(1)} %project.5.base_ref, bf16[4096,320]{1,0:T(8,128)(2,1)S(1)} %bitcast.62, ...), custom_call_target="tpu_custom_call" | custom-call | flops 300000000 | bytes 4000000 | tf_op jit(solution)/shard_map/update_values/pallas_call | solution.py:450
  42.7 4.8 %all-to-all-start = ((bf16[16,9,3,2,128]{4,3,2,1,0:T(2,128)(2,1)}), bf16[16,9,3,2,128]{4,3,2,1,0:T(2,128)(2,1)S(1)}, u32[]{:S(2)}, u32[]{:S(2)}) async-start(bf16[16,9,3,2,128]{4,3,2,1,0:T(2,128)(2,1)} %update_values.1), calls=%async_computation | async-start | bytes 442368 | tf_op jit(solution)/shard_map/all_to_all | solution.py:625
  47.6 0.1 and.12
  47.7 0.1 and.13
  47.8 0.1 add.59
  47.9 0.1 add.56
  48.0 0.1 add.57
  48.1 0.1 pad_maximum_fusion
  48.2 0.1 and_convert_fusion.live_ref
  48.3 4.6 %cache_by_head.3 = (bf16[20,256,128]{2,1,0:T(8,128)(2,1)S(1)}, bf16[20,256,128]{2,1,0:T(8,128)(2,1)}) custom-call(bf16[256,40,2,128]{3,2,1,0:T(2,128)(2,1)} %bitcast.80), custom_call_target="tpu_custom_call" | custom-call | bytes 12000000 | tf_op jit(solution)/shard_map/cache_by_head/pallas_call | solution.py:288
  52.9 4.1 %all-to-all-done.pieces_ref = bf16[16,9,3,2,128]{4,3,2,1,0:T(2,128)(2,1)S(1)} async-done(((bf16[16,9,3,2,128]{4,3,2,1,0:T(2,128)(2,1)}), bf16[16,9,3,2,128]{4,3,2,1,0:T(2,128)(2,1)S(1)}, u32[]{:S(2)}, u32[]{:S(2)}) %all-to-all-start) | async-done | bytes 221216 | tf_op jit(solution)/shard_map/all_to_all | solution.py:625
  57.0 3.9 %attention.1 = bf16[3,40,2,128]{3,2,1,0:T(2,128)(2,1)} custom-call(f32[8,128]{1,0:T(8,128)S(1)} %get-tuple-element.62.cos_ref, f32[8,128]{1,0:T(8,128)S(1)} %get-tuple-element.63.sin_ref, s32[2,256]{1,0:T(2,128)S(1)} %and_convert_fusion.live_ref, bf16[16,9,3,2,128]{4,3,2,1,0:T(2,128)(2,1)S(1)} %all-to-all-done.pieces_ref, ...), custom_call_target="tpu_custom_call" | custom-call | flops 1000000000 | bytes 6000000 | tf_op jit(solution)/shard_map/attention/pallas_call | solution.py:555
  (36 shorter events, 0.2 us)
Async XLA Ops:
  0.0 11.6 %collective-permute-start = (bf16[3,2,5120]{2,1,0:T(2,128)(2,1)}, bf16[3,2,5120]{2,1,0:T(2,128)(2,1)S(1)}, u32[]{:S(2)}, u32[]{:S(2)}) collective-permute-start(bf16[3,2,5120]{2,1,0:T(2,128)(2,1)} %param.9), channel_id=1, source_target_pairs={{0,4},{1,5},{2,6},{3,7},{4,0},{5,1},{6,2},{7,3},{8,12},{9,13},{10,... | collective-permute-start | bytes 184328 | tf_op jit(solution)/shard_map/ppermute | solution.py:233
  3.0 10.4 %collective-permute-start.11 = (bf16[3,2,5120]{2,1,0:T(2,128)(2,1)}, bf16[3,2,5120]{2,1,0:T(2,128)(2,1)S(1)}, u32[]{:S(2)}, u32[]{:S(2)}) collective-permute-start(bf16[3,2,5120]{2,1,0:T(2,128)(2,1)} %param.9), channel_id=1, source_target_pairs={{0,12},{1,13},{2,14},{3,15},{4,8},{5,9},{6,10},{7,11},{8,4},{9,5},... | collective-permute-start | bytes 184328 | tf_op jit(solution)/shard_map/ppermute | solution.py:233
  5.5 8.3 %collective-permute-start.7 = (bf16[3,2,5120]{2,1,0:T(2,128)(2,1)}, bf16[3,2,5120]{2,1,0:T(2,128)(2,1)S(1)}, u32[]{:S(2)}, u32[]{:S(2)}) collective-permute-start(bf16[3,2,5120]{2,1,0:T(2,128)(2,1)} %param.9), channel_id=1, source_target_pairs={{0,8},{1,9},{2,10},{3,11},{4,12},{5,13},{6,14},{7,15},{8,0},{9,1},... | collective-permute-start | bytes 184328 | tf_op jit(solution)/shard_map/ppermute | solution.py:233
  6.5 0.8 %copy-start.3 = (bf16[3,2,5120]{2,1,0:T(2,128)(2,1)S(1)}, bf16[3,2,5120]{2,1,0:T(2,128)(2,1)}, u32[]{:S(2)}) copy-start(bf16[3,2,5120]{2,1,0:T(2,128)(2,1)} %param.9) | copy-start | bytes 184324
  6.5 2.4 %copy-start.5 = (s32[32]{0:T(128)S(1)}, s32[32]{0:T(128)}, u32[]{:S(2)}) copy-start(s32[32]{0:T(128)} %param.15) | copy-start | bytes 388
  6.5 9.3 %copy-start.4 = (s32[2,32]{1,0:T(2,128)S(1)}, s32[2,32]{1,0:T(2,128)}, u32[]{:S(2)}) copy-start(s32[2,32]{1,0:T(2,128)} %param.16) | copy-start | bytes 772
  6.5 14.0 %copy-start.2 = (bf16[4,64,5120]{2,1,0:T(8,128)(2,1)S(1)}, bf16[4,64,5120]{2,1,0:T(8,128)(2,1)}, u32[]{:S(2)}) copy-start(bf16[4,64,5120]{2,1,0:T(8,128)(2,1)} %down_ref.1) | copy-start | bytes 7864324
  7.3 4.2 %collective-permute-start.2 = (bf16[3,2,5120]{2,1,0:T(2,128)(2,1)S(1)}, bf16[3,2,5120]{2,1,0:T(2,128)(2,1)S(1)}, u32[]{:S(2)}, u32[]{:S(2)}) collective-permute-start(bf16[3,2,5120]{2,1,0:T(2,128)(2,1)S(1)} %copy-done.3), channel_id=1, source_target_pairs={{0,2},{1,3},{2,0},{3,1},{4,6},{5,7},{6,4},{7,5},{8,10},{9,11},{10,... | collective-permute-start | bytes 184328 | tf_op jit(solution)/shard_map/ppermute | solution.py:233
  11.5 2.7 %collective-permute-start.3 = (bf16[3,2,5120]{2,1,0:T(2,128)(2,1)S(1)}, bf16[3,2,5120]{2,1,0:T(2,128)(2,1)S(1)}, u32[]{:S(2)}, u32[]{:S(2)}) collective-permute-start(bf16[3,2,5120]{2,1,0:T(2,128)(2,1)S(1)} %collective-permute-done.2), channel_id=1, source_target_pairs={{0,1},{1,0},{2,3},{3,2},{4,5},{5,4},{6,7},{7,6},{8,9},{9,8},{10,11... | collective-permute-start | bytes 184328 | tf_op jit(solution)/shard_map/ppermute | solution.py:233
  11.6 4.5 %collective-permute-start.5 = (bf16[3,2,5120]{2,1,0:T(2,128)(2,1)S(1)}, bf16[3,2,5120]{2,1,0:T(2,128)(2,1)S(1)}, u32[]{:S(2)}, u32[]{:S(2)}) collective-permute-start(bf16[3,2,5120]{2,1,0:T(2,128)(2,1)S(1)} %collective-permute-done), channel_id=1, source_target_pairs={{0,2},{1,3},{2,0},{3,1},{4,6},{5,7},{6,4},{7,5},{8,10},{9,11},{10,... | collective-permute-start | bytes 184328 | tf_op jit(solution)/shard_map/ppermute | solution.py:233
  13.2 3.2 %collective-permute-start.4 = (bf16[3,2,5120]{2,1,0:T(2,128)(2,1)S(1)}, bf16[3,2,5120]{2,1,0:T(2,128)(2,1)S(1)}, u32[]{:S(2)}, u32[]{:S(2)}) collective-permute-start(bf16[3,2,5120]{2,1,0:T(2,128)(2,1)S(1)} %collective-permute-done), channel_id=1, source_target_pairs={{0,1},{1,0},{2,3},{3,2},{4,5},{5,4},{6,7},{7,6},{8,9},{9,8},{10,11... | collective-permute-start | bytes 184328 | tf_op jit(solution)/shard_map/ppermute | solution.py:233
  13.5 2.4 %collective-permute-start.1 = (bf16[3,2,5120]{2,1,0:T(2,128)(2,1)S(1)}, bf16[3,2,5120]{2,1,0:T(2,128)(2,1)S(1)}, u32[]{:S(2)}, u32[]{:S(2)}) collective-permute-start(bf16[3,2,5120]{2,1,0:T(2,128)(2,1)S(1)} %copy-done.3), channel_id=1, source_target_pairs={{0,1},{1,0},{2,3},{3,2},{4,5},{5,4},{6,7},{7,6},{8,9},{9,8},{10,11... | collective-permute-start | bytes 184328 | tf_op jit(solution)/shard_map/ppermute | solution.py:233
  13.8 4.8 %collective-permute-start.13 = (bf16[3,2,5120]{2,1,0:T(2,128)(2,1)S(1)}, bf16[3,2,5120]{2,1,0:T(2,128)(2,1)S(1)}, u32[]{:S(2)}, u32[]{:S(2)}) collective-permute-start(bf16[3,2,5120]{2,1,0:T(2,128)(2,1)S(1)} %collective-permute-done.11), channel_id=1, source_target_pairs={{0,2},{1,3},{2,0},{3,1},{4,6},{5,7},{6,4},{7,5},{8,10},{9,11},{10,... | collective-permute-start | bytes 184328 | tf_op jit(solution)/shard_map/ppermute | solution.py:233
  14.3 4.9 %collective-permute-start.9 = (bf16[3,2,5120]{2,1,0:T(2,128)(2,1)S(1)}, bf16[3,2,5120]{2,1,0:T(2,128)(2,1)S(1)}, u32[]{:S(2)}, u32[]{:S(2)}) collective-permute-start(bf16[3,2,5120]{2,1,0:T(2,128)(2,1)S(1)} %collective-permute-done.7), channel_id=1, source_target_pairs={{0,2},{1,3},{2,0},{3,1},{4,6},{5,7},{6,4},{7,5},{8,10},{9,11},{10,... | collective-permute-start | bytes 184328 | tf_op jit(solution)/shard_map/ppermute | solution.py:233
  15.9 3.3 %collective-permute-start.12 = (bf16[3,2,5120]{2,1,0:T(2,128)(2,1)S(1)}, bf16[3,2,5120]{2,1,0:T(2,128)(2,1)S(1)}, u32[]{:S(2)}, u32[]{:S(2)}) collective-permute-start(bf16[3,2,5120]{2,1,0:T(2,128)(2,1)S(1)} %collective-permute-done.11), channel_id=1, source_target_pairs={{0,1},{1,0},{2,3},{3,2},{4,5},{5,4},{6,7},{7,6},{8,9},{9,8},{10,11... | collective-permute-start | bytes 184328 | tf_op jit(solution)/shard_map/ppermute | solution.py:233
  16.1 3.1 %collective-permute-start.8 = (bf16[3,2,5120]{2,1,0:T(2,128)(2,1)S(1)}, bf16[3,2,5120]{2,1,0:T(2,128)(2,1)S(1)}, u32[]{:S(2)}, u32[]{:S(2)}) collective-permute-start(bf16[3,2,5120]{2,1,0:T(2,128)(2,1)S(1)} %collective-permute-done.7), channel_id=1, source_target_pairs={{0,1},{1,0},{2,3},{3,2},{4,5},{5,4},{6,7},{7,6},{8,9},{9,8},{10,11... | collective-permute-start | bytes 184328 | tf_op jit(solution)/shard_map/ppermute | solution.py:233
  16.5 2.8 %collective-permute-start.6 = (bf16[3,2,5120]{2,1,0:T(2,128)(2,1)S(1)}, bf16[3,2,5120]{2,1,0:T(2,128)(2,1)S(1)}, u32[]{:S(2)}, u32[]{:S(2)}) collective-permute-start(bf16[3,2,5120]{2,1,0:T(2,128)(2,1)S(1)} %collective-permute-done.5), channel_id=1, source_target_pairs={{0,1},{1,0},{2,3},{3,2},{4,5},{5,4},{6,7},{7,6},{8,9},{9,8},{10,11... | collective-permute-start | bytes 184328 | tf_op jit(solution)/shard_map/ppermute | solution.py:233
  18.5 1.2 %collective-permute-start.14 = (bf16[3,2,5120]{2,1,0:T(2,128)(2,1)S(1)}, bf16[3,2,5120]{2,1,0:T(2,128)(2,1)S(1)}, u32[]{:S(2)}, u32[]{:S(2)}) collective-permute-start(bf16[3,2,5120]{2,1,0:T(2,128)(2,1)S(1)} %collective-permute-done.13), channel_id=1, source_target_pairs={{0,1},{1,0},{2,3},{3,2},{4,5},{5,4},{6,7},{7,6},{8,9},{9,8},{10,11... | collective-permute-start | bytes 184328 | tf_op jit(solution)/shard_map/ppermute | solution.py:233
  19.2 1.2 %collective-permute-start.10 = (bf16[3,2,5120]{2,1,0:T(2,128)(2,1)S(1)}, bf16[3,2,5120]{2,1,0:T(2,128)(2,1)S(1)}, u32[]{:S(2)}, u32[]{:S(2)}) collective-permute-start(bf16[3,2,5120]{2,1,0:T(2,128)(2,1)S(1)} %collective-permute-done.9), channel_id=1, source_target_pairs={{0,1},{1,0},{2,3},{3,2},{4,5},{5,4},{6,7},{7,6},{8,9},{9,8},{10,11... | collective-permute-start | bytes 184328 | tf_op jit(solution)/shard_map/ppermute | solution.py:233
  22.6 8.0 %collective-permute-start.17 = (bf16[48,128]{1,0:T(8,128)(2,1)S(1)}, bf16[48,128]{1,0:T(8,128)(2,1)S(1)}, u32[]{:S(2)}, u32[]{:S(2)}) collective-permute-start(bf16[48,128]{1,0:T(8,128)(2,1)S(1)} %get-tuple-element.39), channel_id=1, source_target_pairs={{0,3},{1,2},{2,1},{3,0},{4,7},{5,6},{6,5},{7,4},{8,11},{9,10},{10,... | collective-permute-start | bytes 36872 | tf_op jit(solution)/shard_map/ppermute | solution.py:233
  23.5 7.1 %collective-permute-start.16 = (bf16[48,128]{1,0:T(8,128)(2,1)S(1)}, bf16[48,128]{1,0:T(8,128)(2,1)S(1)}, u32[]{:S(2)}, u32[]{:S(2)}) collective-permute-start(bf16[48,128]{1,0:T(8,128)(2,1)S(1)} %get-tuple-element.39), channel_id=1, source_target_pairs={{0,2},{1,3},{2,0},{3,1},{4,6},{5,7},{6,4},{7,5},{8,10},{9,11},{10,... | collective-permute-start | bytes 36872 | tf_op jit(solution)/shard_map/ppermute | solution.py:233
  24.4 6.2 %collective-permute-start.15 = (bf16[48,128]{1,0:T(8,128)(2,1)S(1)}, bf16[48,128]{1,0:T(8,128)(2,1)S(1)}, u32[]{:S(2)}, u32[]{:S(2)}) collective-permute-start(bf16[48,128]{1,0:T(8,128)(2,1)S(1)} %get-tuple-element.39), channel_id=1, source_target_pairs={{0,1},{1,0},{2,3},{3,2},{4,5},{5,4},{6,7},{7,6},{8,9},{9,8},{10,11... | collective-permute-start | bytes 36872 | tf_op jit(solution)/shard_map/ppermute | solution.py:233
  24.5 3.8 %copy-start = (bf16[3,5120,320]{1,2,0:T(8,128)(2,1)S(1)}, bf16[3,5120,320]{1,2,0:T(8,128)(2,1)}, u32[]{:S(2)}) copy-start(bf16[3,5120,320]{1,2,0:T(8,128)(2,1)} %param.10) | copy-start | bytes 29491204
  30.7 10.4 %collective-permute-start.20 = (bf16[48,128]{1,0:T(8,128)(2,1)S(1)}, bf16[48,128]{1,0:T(8,128)(2,1)S(1)}, u32[]{:S(2)}, u32[]{:S(2)}) collective-permute-start(bf16[48,128]{1,0:T(8,128)(2,1)S(1)} %add_add_fusion.refs_0_), channel_id=1, source_target_pairs={{0,12},{1,13},{2,14},{3,15},{4,8},{5,9},{6,10},{7,11},{8,4},{9,5},... | collective-permute-start | bytes 36872 | tf_op jit(solution)/shard_map/ppermute | solution.py:233
  33.6 7.5 %collective-permute-start.19 = (bf16[48,128]{1,0:T(8,128)(2,1)S(1)}, bf16[48,128]{1,0:T(8,128)(2,1)S(1)}, u32[]{:S(2)}, u32[]{:S(2)}) collective-permute-start(bf16[48,128]{1,0:T(8,128)(2,1)S(1)} %add_add_fusion.refs_0_), channel_id=1, source_target_pairs={{0,8},{1,9},{2,10},{3,11},{4,12},{5,13},{6,14},{7,15},{8,0},{9,1},... | collective-permute-start | bytes 36872 | tf_op jit(solution)/shard_map/ppermute | solution.py:233
  34.0 7.1 %collective-permute-start.18 = (bf16[48,128]{1,0:T(8,128)(2,1)S(1)}, bf16[48,128]{1,0:T(8,128)(2,1)S(1)}, u32[]{:S(2)}, u32[]{:S(2)}) collective-permute-start(bf16[48,128]{1,0:T(8,128)(2,1)S(1)} %add_add_fusion.refs_0_), channel_id=1, source_target_pairs={{0,4},{1,5},{2,6},{3,7},{4,0},{5,1},{6,2},{7,3},{8,12},{9,13},{10,... | collective-permute-start | bytes 36872 | tf_op jit(solution)/shard_map/ppermute | solution.py:233
  36.2 4.9 %copy-start.1 = (bf16[64,64,320]{2,1,0:T(8,128)(2,1)S(1)}, bf16[64,64,320]{2,1,0:T(8,128)(2,1)}, u32[]{:S(2)}) copy-start(bf16[64,64,320]{2,1,0:T(8,128)(2,1)} %param.12) | copy-start | bytes 7864324
  42.7 14.2 %all-to-all-start = ((bf16[16,9,3,2,128]{4,3,2,1,0:T(2,128)(2,1)}), bf16[16,9,3,2,128]{4,3,2,1,0:T(2,128)(2,1)S(1)}, u32[]{:S(2)}, u32[]{:S(2)}) async-start(bf16[16,9,3,2,128]{4,3,2,1,0:T(2,128)(2,1)} %update_values.1), calls=%async_computation | async-start | bytes 442368 | tf_op jit(solution)/shard_map/all_to_all | solution.py:625

commit v12 on v11

--- a/solution.py
+++ b/solution.py
@@ -229,6 +229,31 @@
     return out.reshape(steps, req_dev, width)
 
 
+def rotation_rows(lengths, first, req_dev, steps):
+    row = jnp.arange(ROWS, dtype=jnp.int32)
+    wanted = first + row % req_dev
+    chosen = jnp.where(wanted[:, None] == jnp.arange(lengths.shape[0], dtype=jnp.int32)[None, :], lengths[None, :], 0)
+    positions = jnp.sum(chosen, axis=1, keepdims=True) + (row // req_dev)[:, None]
+    lane = jnp.arange(HD, dtype=jnp.int32)
+    frequency = jnp.exp((lane % (HD // 2)).astype(jnp.float32) * (-2.0 * jnp.log(10000.0) / HD))
+    angles = positions.astype(jnp.float32) * frequency[None, :]
+    return jnp.cos(angles), jnp.where(lane < HD // 2, -1.0, 1.0)[None, :] * jnp.sin(angles)
+
+
+def live_lanes(lengths, first, request_page_table, tokens, page_len):
+    req_dev, max_pages = request_page_table.shape
+    wanted = first + jnp.arange(req_dev, dtype=jnp.int32)
+    chosen = jnp.where(wanted[:, None] == jnp.arange(lengths.shape[0], dtype=jnp.int32)[None, :], lengths[None, :], 0)
+    lane = jnp.arange(tokens, dtype=jnp.int32)
+    page = jnp.arange(max_pages, dtype=jnp.int32)
+    place = jnp.max(
+        jnp.where(request_page_table[:, :, None] == (lane // page_len)[None, None, :], page[None, :, None], -1),
+        axis=1,
+    )
+    token = place * page_len + (lane % page_len)[None, :]
+    return ((place >= 0) & (token < jnp.sum(chosen, axis=1, keepdims=True))).astype(jnp.int32)
+
+
 def trade(value, mask, count):
     return lax.ppermute(value, "replica", [(i, i ^ mask) for i in range(count)])
 
@@ -257,7 +282,7 @@
         copy.wait()
 
 
-CACHE_PARTS = 2
+CACHE_SECTION = 10
 
 
 def cache_kernel(first, pool_ref, keys_ref, values_ref, raw, values, sem, out_sem):
@@ -269,8 +294,8 @@
     wanted = jnp.where(to < tokens, 2 * to, 2 * (to - tokens) + 1)
     pick = jnp.where(source == wanted, 1.0, 0.0).astype(jnp.bfloat16)
     sent = []
-    part = heads // CACHE_PARTS
-    for p in range(CACHE_PARTS):
+    part = CACHE_SECTION
+    for p in range(heads // part):
         wait_all(copies[p * part : (p + 1) * part])
         for h in range(p * part, (p + 1) * part, 2):
             both = jnp.concatenate([rows[h], rows[h + 1]], axis=1)
@@ -297,7 +322,7 @@
             pltpu.VMEM((heads, tokens, 2, HD), pool.dtype),
             pltpu.VMEM((heads, tokens, HD), pool.dtype),
             pltpu.SemaphoreType.DMA((heads,)),
-            pltpu.SemaphoreType.DMA((CACHE_PARTS,)),
+            pltpu.SemaphoreType.DMA((heads // CACHE_SECTION,)),
         ],
         compiler_params=pltpu.CompilerParams(vmem_limit_bytes=12 * 2**20),
         cost_estimate=pl.CostEstimate(flops=0, bytes_accessed=12 * 10**6, transcendentals=0),
@@ -471,7 +496,8 @@
     lanes = heads * HD
     group = rows * HEAD_BLOCK
     chips = range(count // 2)
-    places = [divmod(c, count // 4) for c in chips]
+    early = keys_refs[0].shape[0] // heads
+    places = [(0, c) if c < early else (1, c - early) for c in chips]
     fetches = start_all(
         [
             pltpu.make_async_copy(values_refs[half].at[at * heads : (at + 1) * heads], values_buf.at[c], sem.at[c])
@@ -549,7 +575,7 @@
 
 def attend(cosine, sine, live, pieces, keys, values):
     count, _, steps = pieces.shape[:3]
-    heads, tokens = 2 * keys[0].shape[0], keys[0].shape[1]
+    heads, tokens = sum(x.shape[0] for x in keys), keys[0].shape[1]
     chips = count // 2
     per = heads // chips
     return pl.pallas_call(
@@ -596,16 +622,19 @@
         ),
         axis=1,
     )
+    cosine, sine = rotation_rows(lengths, me * req_dev, req_dev, steps)
+    live = live_lanes(lengths, me * req_dev, request_page_table, tokens, page_len)
     slot, column = index_work((me * holder_count).astype(jnp.int32).reshape(1), stored, steps)
 
     held = {m: trade(hidden, m, count) for m in range(count - 4, 0, -4)}
     own, slot, column = lax.optimization_barrier((hidden, slot, column))
     held[2] = trade(own, 2, count)
-    own, held[4] = lax.optimization_barrier((hidden, held[4]))
-    held[1] = trade(own, 1, count)
+    held.update({m | 2: trade(held[m], 2, count) for m in range(4, count, 4)})
     held[0] = hidden
-    held.update({m | 2: trade(held[m], 2, count) for m in range(4, count, 4)})
-    held.update({m | 1: trade(held[m], 1, count) for m in range(2, count, 2)})
+    ready = [0, 2, *range(4, count, 4)]
+    *waiting, held[count - 2] = lax.optimization_barrier([held[m] for m in ready] + [held[count - 2]])
+    held.update(zip(ready, waiting))
+    held.update({m | 1: trade(held[m], 1, count) for m in range(0, count, 2)})
     blocks = [held[k].reshape(steps, req_dev, heads, HD).transpose(0, 2, 1, 3) for k in range(count)]
     blocks[0] = in_hbm(blocks[0])
 
@@ -617,18 +646,16 @@
     low = (low + arrived[0]) + (arrived[1] + arrived[2])
     arrived = [trade(low, m, count) for m in range(4, count, 4)]
     base = project(2, x, weight)
-    early_cache = cache_by_head(pool, 0, heads // 2)
+    early_heads = heads // 4
+    early_cache = cache_by_head(pool, 0, early_heads)
     arrived, base, early_cache = lax.optimization_barrier((arrived, base, early_cache))
     send = update_values(column, query, key, base, adapter_up_maps.reshape(adapter_count * rank, -1), [low, *arrived])
     send, pool = lax.optimization_barrier((send, pool))
-    late_cache = cache_by_head(pool, heads // 2, heads // 2)
+    late_cache = cache_by_head(pool, early_heads, heads - early_heads)
     pieces = lax.all_to_all(send, "replica", split_axis=0, concat_axis=0, tiled=True)
 
-    my_lengths = lax.dynamic_slice_in_dim(lengths, me * req_dev, req_dev)
-    cosine, sine = rotation(my_lengths, steps)
-    live = live_tokens(my_lengths, request_page_table, pool_pages, page_len).astype(jnp.int32)
     keys, values = zip(early_cache, late_cache)
-    out = attend(cosine, sine, live.reshape(req_dev, tokens), pieces, keys, values)
+    out = attend(cosine, sine, live, pieces, keys, values)
     return out.transpose(0, 2, 1, 3).reshape(steps, req_dev, width)
 
 

time: 61.4 us -> 59.8 us (0.974)
  waiting for transfers between devices: 10.5 us -> 7.58 us
  starting transfers between devices: 23 us -> 24.9 us
  local copies, waits for them, and re-layouts: 5.1 us -> 4.44 us
    ppermute x21, waiting for transfers between devices: 6.49 us -> 4.06 us  [trade(): return lax.ppermute(value, 'replica', [(i, i ^ mask) for i in range(count)])]
    ppermute x21, starting transfers between devices: 18.2 us -> 19.5 us  [trade(): return lax.ppermute(value, 'replica', [(i, i ^ mask) for i in range(count)])]
    all_to_all x1, starting transfers between devices: 4.82 us -> 5.45 us  [chip_plan(): lax.all_to_all(send, 'replica', split_axis=0, concat_axis=0, tiled=True)]
  transfers between devices with their start and end apart: 22 -> 22, of which waited for: 7 -> 8; matrix products, arithmetic and copies ran while one was open for 3% -> 3% of each run, Pallas kernels for 21% -> 22%
where the time goes in v12:
time: 59.8 us; the launch traced here: 59.4 us
  starting transfers between devices  24.9 us (42%)
  Pallas kernels  20.6 us (34%)
  waiting for transfers between devices  7.58 us (13%)
  local copies, waits for them, and re-layouts  4.44 us (7%)
  other arithmetic  1.53 us (3%)
    ppermute x21, starting transfers between devices, trade(): return lax.ppermute(value, 'replica', [(i, i ^ mask) for i in range(count)])  19.5 us
    pallas_call x2, Pallas kernels, cache_by_head(): pl.pallas_call(functools.partial(cache_kernel, first), out_shape=(jax.Sha...  9.32 us
    all_to_all x1, starting transfers between devices, chip_plan(): lax.all_to_all(send, 'replica', split_axis=0, concat_axis=0, tiled=True)  5.45 us
    unnamed x12, local copies, waits for them, and re-layouts  4.44 us
    ppermute x21, waiting for transfers between devices, trade(): return lax.ppermute(value, 'replica', [(i, i ^ mask) for i in range(count)])  4.06 us
    pallas_call x1, Pallas kernels, attend(): pl.pallas_call(attend_kernel, out_shape=jax.ShapeDtypeStruct((steps, head...  3.84 us
    pallas_call x3, Pallas kernels, project(): pl.pallas_call(functools.partial(project_kernel, which), out_shape=chunks...  3.56 us
    all_to_all x1, waiting for transfers between devices, chip_plan(): lax.all_to_all(send, 'replica', split_axis=0, concat_axis=0, tiled=True)  3.53 us
  transfers between devices with their start and end apart: 22, of which 8 were waited for; matrix products, arithmetic and copies ran while one was open for 3% of the time, Pallas kernels for 22%

profile of v12, /device:TPU:0, one launch (start us, length us, event | category | flops | bytes accessed | tf_op | source)
XLA Modules:
  0.0 59.4 jit_solution(14825654185152583074)
XLA Ops:
  0.0 4.0 %collective-permute-start.2 = (bf16[3,2,5120]{2,1,0:T(2,128)(2,1)}, bf16[3,2,5120]{2,1,0:T(2,128)(2,1)S(1)}, u32[]{:S(2)}, u32[]{:S(2)}) collective-permute-start(bf16[3,2,5120]{2,1,0:T(2,128)(2,1)} %param.9), channel_id=1, source_target_pairs={{0,8},{1,9},{2,10},{3,11},{4,12},{5,13},{6,14},{7,15},{8,0},{9,1},... | collective-permute-start | bytes 184328 | tf_op jit(solution)/shard_map/ppermute | solution.py:258
  4.0 1.6 %collective-permute-start.1 = (bf16[3,2,5120]{2,1,0:T(2,128)(2,1)}, bf16[3,2,5120]{2,1,0:T(2,128)(2,1)S(1)}, u32[]{:S(2)}, u32[]{:S(2)}) collective-permute-start(bf16[3,2,5120]{2,1,0:T(2,128)(2,1)} %param.9), channel_id=1, source_target_pairs={{0,4},{1,5},{2,6},{3,7},{4,0},{5,1},{6,2},{7,3},{8,12},{9,13},{10,... | collective-permute-start | bytes 184328 | tf_op jit(solution)/shard_map/ppermute | solution.py:258
  5.6 0.8 %select_reduce_fusion.1 = s32[32]{0:T(128)S(1)} fusion(s32[64]{0:T(128)} %param.13, s32[32]{0:T(128)} %param.14), kind=kLoop, calls=%fused_computation.1 | loop fusion | flops 6112 | bytes 512 | tf_op jit(solution)/shard_map/reduce_sum | solution.py:617
  6.5 0.0 copy-start.5
  6.5 0.0 copy-start.4
  6.5 0.0 copy-start.2
  6.5 0.2 index_work.1
  6.7 0.6 %copy-done.3 = bf16[3,2,5120]{2,1,0:T(2,128)(2,1)S(1)} copy-done((bf16[3,2,5120]{2,1,0:T(2,128)(2,1)S(1)}, bf16[3,2,5120]{2,1,0:T(2,128)(2,1)}, u32[]{:S(2)}) %copy-start.3) | copy-done | bytes 61464
  7.3 1.7 %collective-permute-start = (bf16[3,2,5120]{2,1,0:T(2,128)(2,1)S(1)}, bf16[3,2,5120]{2,1,0:T(2,128)(2,1)S(1)}, u32[]{:S(2)}, u32[]{:S(2)}) collective-permute-start(bf16[3,2,5120]{2,1,0:T(2,128)(2,1)S(1)} %copy-done.3), channel_id=1, source_target_pairs={{0,2},{1,3},{2,0},{3,1},{4,6},{5,7},{6,4},{7,5},{8,10},{9,11},{10,... | collective-permute-start | bytes 184328 | tf_op jit(solution)/shard_map/ppermute | solution.py:258
  9.1 0.2 fusion.3
  9.2 0.1 select_reduce_fusion
  9.3 0.1 and_convert_fusion.live_ref
  9.4 0.0 collective-permute-done.2
  9.4 0.3 collective-permute-start.11
  9.7 1.7 %collective-permute-start.8 = (bf16[3,2,5120]{2,1,0:T(2,128)(2,1)S(1)}, bf16[3,2,5120]{2,1,0:T(2,128)(2,1)S(1)}, u32[]{:S(2)}, u32[]{:S(2)}) collective-permute-start(bf16[3,2,5120]{2,1,0:T(2,128)(2,1)S(1)} %collective-permute-done.1), channel_id=1, source_target_pairs={{0,2},{1,3},{2,0},{3,1},{4,6},{5,7},{6,4},{7,5},{8,10},{9,11},{10,... | collective-permute-start | bytes 184328 | tf_op jit(solution)/shard_map/ppermute | solution.py:258
  11.5 0.4 collective-permute-done.3
  11.8 1.5 %collective-permute-start.4 = (bf16[3,2,5120]{2,1,0:T(2,128)(2,1)S(1)}, bf16[3,2,5120]{2,1,0:T(2,128)(2,1)S(1)}, u32[]{:S(2)}, u32[]{:S(2)}) collective-permute-start(bf16[3,2,5120]{2,1,0:T(2,128)(2,1)S(1)} %collective-permute-done.3), channel_id=1, source_target_pairs={{0,2},{1,3},{2,0},{3,1},{4,6},{5,7},{6,4},{7,5},{8,10},{9,11},{10,... | collective-permute-start | bytes 184328 | tf_op jit(solution)/shard_map/ppermute | solution.py:258
  13.4 2.7 %collective-permute-done.4 = bf16[3,2,5120]{2,1,0:T(2,128)(2,1)S(1)} collective-permute-done((bf16[3,2,5120]{2,1,0:T(2,128)(2,1)S(1)}, bf16[3,2,5120]{2,1,0:T(2,128)(2,1)S(1)}, u32[]{:S(2)}, u32[]{:S(2)}) %collective-permute-start.4) | collective-permute-done | bytes 61472 | tf_op jit(solution)/shard_map/ppermute | solution.py:258
  16.1 0.5 collective-permute-start.12
  16.6 0.1 collective-permute-start.9
  16.7 0.2 select_reduce_fusion.2
  16.8 0.5 collective-permute-start.6
  17.3 0.1 collective-permute-start.7
  17.4 0.1 collective-permute-done.12
  17.5 0.4 collective-permute-start.10
  17.9 0.1 collective-permute-start.13
  18.0 0.4 collective-permute-start.14
  18.4 0.2 collective-permute-done.7
  18.6 0.2 collective-permute-done.10
  18.7 0.4 collective-permute-done.13
  19.1 0.2 collective-permute-done.14
  19.3 2.0 %low_rows.1 = (bf16[3,40,16,2,128]{4,3,2,1,0:T(2,128)(2,1)S(1)}, bf16[48,128]{1,0:T(8,128)(2,1)S(1)}) custom-call(s32[1]{0:T(128)} %bitcast.2.me_ref, s32[1,96]{1,0:T(1,128)S(1)} %get-tuple-element.39.slot_ref, bf16[4,64,5120]{2,1,0:T(8,128)(2,1)S(1)} %copy-done.2, bf16[3,40,2,128]{3,2,1,0:T(2,128)(2,1)} %bitcast.81, bf16[3,40,2,128]{3,2,1,0:T(2,128)(2,1)S(1)} %bitcast.70, ...), custom_call_target="tpu_custom_call" | custom-call | flops 100000000 | bytes 4000000 | tf_op jit(solution)/shard_map/low_rows/pallas_call | solution.py:394
  21.3 1.5 %collective-permute-start.17 = (bf16[48,128]{1,0:T(8,128)(2,1)S(1)}, bf16[48,128]{1,0:T(8,128)(2,1)S(1)}, u32[]{:S(2)}, u32[]{:S(2)}) collective-permute-start(bf16[48,128]{1,0:T(8,128)(2,1)S(1)} %get-tuple-element.47), channel_id=1, source_target_pairs={{0,3},{1,2},{2,1},{3,0},{4,7},{5,6},{6,5},{7,4},{8,11},{9,10},{10,... | collective-permute-start | bytes 36872 | tf_op jit(solution)/shard_map/ppermute | solution.py:258
  22.9 0.5 collective-permute-start.16
  23.4 3.8 %copy-done = bf16[3,5120,320]{1,2,0:T(8,128)(2,1)S(1)} copy-done((bf16[3,5120,320]{1,2,0:T(8,128)(2,1)S(1)}, bf16[3,5120,320]{1,2,0:T(8,128)(2,1)}, u32[]{:S(2)}) %copy-start) | copy-done | bytes 9830424
  27.2 1.2 %project.4.key_ref = bf16[3,3,16,2,128]{4,3,2,1,0:T(2,128)(2,1)S(1)} custom-call(bf16[3,40,16,2,128]{4,3,2,1,0:T(2,128)(2,1)S(1)} %get-tuple-element.48.x_ref, bf16[3,320,5120]{2,1,0:T(8,128)(2,1)S(1)} %bitcast.59), custom_call_target="tpu_custom_call" | custom-call | flops 500000000 | bytes 4000000 | tf_op jit(solution)/shard_map/project/pallas_call | solution.py:436
  28.4 1.2 %project.3.query_ref = bf16[3,3,16,2,128]{4,3,2,1,0:T(2,128)(2,1)S(1)} custom-call(bf16[3,40,16,2,128]{4,3,2,1,0:T(2,128)(2,1)S(1)} %get-tuple-element.48.x_ref, bf16[3,320,5120]{2,1,0:T(8,128)(2,1)S(1)} %bitcast.60), custom_call_target="tpu_custom_call" | custom-call | flops 500000000 | bytes 4000000 | tf_op jit(solution)/shard_map/project/pallas_call | solution.py:436
  29.6 3.3 %collective-permute-start.20 = (bf16[48,128]{1,0:T(8,128)(2,1)S(1)}, bf16[48,128]{1,0:T(8,128)(2,1)S(1)}, u32[]{:S(2)}, u32[]{:S(2)}) collective-permute-start(bf16[48,128]{1,0:T(8,128)(2,1)S(1)} %add_add_fusion.refs_0_), channel_id=1, source_target_pairs={{0,12},{1,13},{2,14},{3,15},{4,8},{5,9},{6,10},{7,11},{8,4},{9,5},... | collective-permute-start | bytes 36872 | tf_op jit(solution)/shard_map/ppermute | solution.py:258
  32.9 1.1 %collective-permute-start.18 = (bf16[48,128]{1,0:T(8,128)(2,1)S(1)}, bf16[48,128]{1,0:T(8,128)(2,1)S(1)}, u32[]{:S(2)}, u32[]{:S(2)}) collective-permute-start(bf16[48,128]{1,0:T(8,128)(2,1)S(1)} %add_add_fusion.refs_0_), channel_id=1, source_target_pairs={{0,4},{1,5},{2,6},{3,7},{4,0},{5,1},{6,2},{7,3},{8,12},{9,13},{10,... | collective-permute-start | bytes 36872 | tf_op jit(solution)/shard_map/ppermute | solution.py:258
  34.1 1.2 %project.5.base_ref = f32[96,320]{1,0:T(8,128)S(1)} custom-call(bf16[3,40,16,2,128]{4,3,2,1,0:T(2,128)(2,1)S(1)} %get-tuple-element.48.x_ref, bf16[3,320,5120]{2,1,0:T(8,128)(2,1)S(1)} %bitcast.61), custom_call_target="tpu_custom_call" | custom-call | flops 500000000 | bytes 4000000 | tf_op jit(solution)/shard_map/project/pallas_call | solution.py:436
  35.2 0.0 copy-start.1
  35.3 3.6 %cache_by_head.2 = (bf16[10,256,128]{2,1,0:T(8,128)(2,1)S(1)}, bf16[10,256,128]{2,1,0:T(8,128)(2,1)}) custom-call(bf16[256,40,2,128]{3,2,1,0:T(2,128)(2,1)} %bitcast.79), custom_call_target="tpu_custom_call" | custom-call | bytes 12000000 | tf_op jit(solution)/shard_map/cache_by_head/pallas_call | solution.py:313
  38.9 1.7 %update_values.1 = bf16[16,9,3,2,128]{4,3,2,1,0:T(2,128)(2,1)} custom-call(s32[96,1]{1,0:T(8,128)S(1)} %get-tuple-element.38.stored_ref, bf16[3,3,16,2,128]{4,3,2,1,0:T(2,128)(2,1)S(1)} %project.3.query_ref, bf16[3,3,16,2,128]{4,3,2,1,0:T(2,128)(2,1)S(1)} %project.4.key_ref, f32[96,320]{1,0:T(8,128)S(1)} %project.5.base_ref, bf16[4096,320]{1,0:T(8,128)(2,1)S(1)} %bitcast.62, ...), custom_call_target="tpu_custom_call" | custom-call | flops 300000000 | bytes 4000000 | tf_op jit(solution)/shard_map/update_values/pallas_call | solution.py:475
  40.6 5.5 %all-to-all-start = ((bf16[16,9,3,2,128]{4,3,2,1,0:T(2,128)(2,1)}), bf16[16,9,3,2,128]{4,3,2,1,0:T(2,128)(2,1)S(1)}, u32[]{:S(2)}, u32[]{:S(2)}) async-start(bf16[16,9,3,2,128]{4,3,2,1,0:T(2,128)(2,1)} %update_values.1), calls=%async_computation | async-start | bytes 442368 | tf_op jit(solution)/shard_map/all_to_all | solution.py:655
  46.0 0.1 fusion
  46.1 5.7 %cache_by_head.3 = (bf16[30,256,128]{2,1,0:T(8,128)(2,1)S(1)}, bf16[30,256,128]{2,1,0:T(8,128)(2,1)}) custom-call(bf16[256,40,2,128]{3,2,1,0:T(2,128)(2,1)} %bitcast.80), custom_call_target="tpu_custom_call" | custom-call | bytes 12000000 | tf_op jit(solution)/shard_map/cache_by_head/pallas_call | solution.py:313
  51.9 3.5 %all-to-all-done.pieces_ref = bf16[16,9,3,2,128]{4,3,2,1,0:T(2,128)(2,1)S(1)} async-done(((bf16[16,9,3,2,128]{4,3,2,1,0:T(2,128)(2,1)}), bf16[16,9,3,2,128]{4,3,2,1,0:T(2,128)(2,1)S(1)}, u32[]{:S(2)}, u32[]{:S(2)}) %all-to-all-start) | async-done | bytes 221216 | tf_op jit(solution)/shard_map/all_to_all | solution.py:655
  55.4 3.8 %attention.1 = bf16[3,40,2,128]{3,2,1,0:T(2,128)(2,1)} custom-call(f32[8,128]{1,0:T(8,128)S(1)} %get-tuple-element.68.cos_ref, f32[8,128]{1,0:T(8,128)S(1)} %get-tuple-element.67.sin_ref, s32[2,256]{1,0:T(2,128)S(1)} %and_convert_fusion.live_ref, bf16[16,9,3,2,128]{4,3,2,1,0:T(2,128)(2,1)S(1)} %all-to-all-done.pieces_ref, ...), custom_call_target="tpu_custom_call" | custom-call | flops 1000000000 | bytes 6000000 | tf_op jit(solution)/shard_map/attention/pallas_call | solution.py:581
  (30 shorter events, 0.1 us)
Async XLA Ops:
  0.0 9.4 %collective-permute-start.2 = (bf16[3,2,5120]{2,1,0:T(2,128)(2,1)}, bf16[3,2,5120]{2,1,0:T(2,128)(2,1)S(1)}, u32[]{:S(2)}, u32[]{:S(2)}) collective-permute-start(bf16[3,2,5120]{2,1,0:T(2,128)(2,1)} %param.9), channel_id=1, source_target_pairs={{0,8},{1,9},{2,10},{3,11},{4,12},{5,13},{6,14},{7,15},{8,0},{9,1},... | collective-permute-start | bytes 184328 | tf_op jit(solution)/shard_map/ppermute | solution.py:258
  4.0 5.7 %collective-permute-start.1 = (bf16[3,2,5120]{2,1,0:T(2,128)(2,1)}, bf16[3,2,5120]{2,1,0:T(2,128)(2,1)S(1)}, u32[]{:S(2)}, u32[]{:S(2)}) collective-permute-start(bf16[3,2,5120]{2,1,0:T(2,128)(2,1)} %param.9), channel_id=1, source_target_pairs={{0,4},{1,5},{2,6},{3,7},{4,0},{5,1},{6,2},{7,3},{8,12},{9,13},{10,... | collective-permute-start | bytes 184328 | tf_op jit(solution)/shard_map/ppermute | solution.py:258
  5.6 6.2 %collective-permute-start.3 = (bf16[3,2,5120]{2,1,0:T(2,128)(2,1)}, bf16[3,2,5120]{2,1,0:T(2,128)(2,1)S(1)}, u32[]{:S(2)}, u32[]{:S(2)}) collective-permute-start(bf16[3,2,5120]{2,1,0:T(2,128)(2,1)} %param.9), channel_id=1, source_target_pairs={{0,12},{1,13},{2,14},{3,15},{4,8},{5,9},{6,10},{7,11},{8,4},{9,5},... | collective-permute-start | bytes 184328 | tf_op jit(solution)/shard_map/ppermute | solution.py:258
  6.5 0.8 %copy-start.3 = (bf16[3,2,5120]{2,1,0:T(2,128)(2,1)S(1)}, bf16[3,2,5120]{2,1,0:T(2,128)(2,1)}, u32[]{:S(2)}) copy-start(bf16[3,2,5120]{2,1,0:T(2,128)(2,1)} %param.9) | copy-start | bytes 184324
  6.5 2.6 %copy-start.5 = (s32[32]{0:T(128)S(1)}, s32[32]{0:T(128)}, u32[]{:S(2)}) copy-start(s32[32]{0:T(128)} %param.15) | copy-start | bytes 388
  6.5 2.8 %copy-start.4 = (s32[2,32]{1,0:T(2,128)S(1)}, s32[2,32]{1,0:T(2,128)}, u32[]{:S(2)}) copy-start(s32[2,32]{1,0:T(2,128)} %param.16) | copy-start | bytes 772
  6.5 12.8 %copy-start.2 = (bf16[4,64,5120]{2,1,0:T(8,128)(2,1)S(1)}, bf16[4,64,5120]{2,1,0:T(8,128)(2,1)}, u32[]{:S(2)}) copy-start(bf16[4,64,5120]{2,1,0:T(8,128)(2,1)} %down_ref.1) | copy-start | bytes 7864324
  7.3 6.1 %collective-permute-start = (bf16[3,2,5120]{2,1,0:T(2,128)(2,1)S(1)}, bf16[3,2,5120]{2,1,0:T(2,128)(2,1)S(1)}, u32[]{:S(2)}, u32[]{:S(2)}) collective-permute-start(bf16[3,2,5120]{2,1,0:T(2,128)(2,1)S(1)} %copy-done.3), channel_id=1, source_target_pairs={{0,2},{1,3},{2,0},{3,1},{4,6},{5,7},{6,4},{7,5},{8,10},{9,11},{10,... | collective-permute-start | bytes 184328 | tf_op jit(solution)/shard_map/ppermute | solution.py:258
  9.4 6.7 %collective-permute-start.11 = (bf16[3,2,5120]{2,1,0:T(2,128)(2,1)S(1)}, bf16[3,2,5120]{2,1,0:T(2,128)(2,1)S(1)}, u32[]{:S(2)}, u32[]{:S(2)}) collective-permute-start(bf16[3,2,5120]{2,1,0:T(2,128)(2,1)S(1)} %collective-permute-done.2), channel_id=1, source_target_pairs={{0,2},{1,3},{2,0},{3,1},{4,6},{5,7},{6,4},{7,5},{8,10},{9,11},{10,... | collective-permute-start | bytes 184328 | tf_op jit(solution)/shard_map/ppermute | solution.py:258
  9.7 6.9 %collective-permute-start.8 = (bf16[3,2,5120]{2,1,0:T(2,128)(2,1)S(1)}, bf16[3,2,5120]{2,1,0:T(2,128)(2,1)S(1)}, u32[]{:S(2)}, u32[]{:S(2)}) collective-permute-start(bf16[3,2,5120]{2,1,0:T(2,128)(2,1)S(1)} %collective-permute-done.1), channel_id=1, source_target_pairs={{0,2},{1,3},{2,0},{3,1},{4,6},{5,7},{6,4},{7,5},{8,10},{9,11},{10,... | collective-permute-start | bytes 184328 | tf_op jit(solution)/shard_map/ppermute | solution.py:258
  11.8 4.2 %collective-permute-start.4 = (bf16[3,2,5120]{2,1,0:T(2,128)(2,1)S(1)}, bf16[3,2,5120]{2,1,0:T(2,128)(2,1)S(1)}, u32[]{:S(2)}, u32[]{:S(2)}) collective-permute-start(bf16[3,2,5120]{2,1,0:T(2,128)(2,1)S(1)} %collective-permute-done.3), channel_id=1, source_target_pairs={{0,2},{1,3},{2,0},{3,1},{4,6},{5,7},{6,4},{7,5},{8,10},{9,11},{10,... | collective-permute-start | bytes 184328 | tf_op jit(solution)/shard_map/ppermute | solution.py:258
  16.1 1.9 %collective-permute-start.5 = (bf16[3,2,5120]{2,1,0:T(2,128)(2,1)S(1)}, bf16[3,2,5120]{2,1,0:T(2,128)(2,1)S(1)}, u32[]{:S(2)}, u32[]{:S(2)}) collective-permute-start(bf16[3,2,5120]{2,1,0:T(2,128)(2,1)S(1)} %copy-done.3), channel_id=1, source_target_pairs={{0,1},{1,0},{2,3},{3,2},{4,5},{5,4},{6,7},{7,6},{8,9},{9,8},{10,11... | collective-permute-start | bytes 184328 | tf_op jit(solution)/shard_map/ppermute | solution.py:258
  16.1 1.4 %collective-permute-start.12 = (bf16[3,2,5120]{2,1,0:T(2,128)(2,1)S(1)}, bf16[3,2,5120]{2,1,0:T(2,128)(2,1)S(1)}, u32[]{:S(2)}, u32[]{:S(2)}) collective-permute-start(bf16[3,2,5120]{2,1,0:T(2,128)(2,1)S(1)} %collective-permute-done.11), channel_id=1, source_target_pairs={{0,1},{1,0},{2,3},{3,2},{4,5},{5,4},{6,7},{7,6},{8,9},{9,8},{10,11... | collective-permute-start | bytes 184328 | tf_op jit(solution)/shard_map/ppermute | solution.py:258
  16.6 1.3 %collective-permute-start.9 = (bf16[3,2,5120]{2,1,0:T(2,128)(2,1)S(1)}, bf16[3,2,5120]{2,1,0:T(2,128)(2,1)S(1)}, u32[]{:S(2)}, u32[]{:S(2)}) collective-permute-start(bf16[3,2,5120]{2,1,0:T(2,128)(2,1)S(1)} %collective-permute-done.8), channel_id=1, source_target_pairs={{0,1},{1,0},{2,3},{3,2},{4,5},{5,4},{6,7},{7,6},{8,9},{9,8},{10,11... | collective-permute-start | bytes 184328 | tf_op jit(solution)/shard_map/ppermute | solution.py:258
  16.8 1.5 %collective-permute-start.6 = (bf16[3,2,5120]{2,1,0:T(2,128)(2,1)S(1)}, bf16[3,2,5120]{2,1,0:T(2,128)(2,1)S(1)}, u32[]{:S(2)}, u32[]{:S(2)}) collective-permute-start(bf16[3,2,5120]{2,1,0:T(2,128)(2,1)S(1)} %collective-permute-done), channel_id=1, source_target_pairs={{0,1},{1,0},{2,3},{3,2},{4,5},{5,4},{6,7},{7,6},{8,9},{9,8},{10,11... | collective-permute-start | bytes 184328 | tf_op jit(solution)/shard_map/ppermute | solution.py:258
  17.3 1.2 %collective-permute-start.7 = (bf16[3,2,5120]{2,1,0:T(2,128)(2,1)S(1)}, bf16[3,2,5120]{2,1,0:T(2,128)(2,1)S(1)}, u32[]{:S(2)}, u32[]{:S(2)}) collective-permute-start(bf16[3,2,5120]{2,1,0:T(2,128)(2,1)S(1)} %collective-permute-done.1), channel_id=1, source_target_pairs={{0,1},{1,0},{2,3},{3,2},{4,5},{5,4},{6,7},{7,6},{8,9},{9,8},{10,11... | collective-permute-start | bytes 184328 | tf_op jit(solution)/shard_map/ppermute | solution.py:258
  17.5 1.3 %collective-permute-start.10 = (bf16[3,2,5120]{2,1,0:T(2,128)(2,1)S(1)}, bf16[3,2,5120]{2,1,0:T(2,128)(2,1)S(1)}, u32[]{:S(2)}, u32[]{:S(2)}) collective-permute-start(bf16[3,2,5120]{2,1,0:T(2,128)(2,1)S(1)} %collective-permute-done.2), channel_id=1, source_target_pairs={{0,1},{1,0},{2,3},{3,2},{4,5},{5,4},{6,7},{7,6},{8,9},{9,8},{10,11... | collective-permute-start | bytes 184328 | tf_op jit(solution)/shard_map/ppermute | solution.py:258
  17.9 1.2 %collective-permute-start.13 = (bf16[3,2,5120]{2,1,0:T(2,128)(2,1)S(1)}, bf16[3,2,5120]{2,1,0:T(2,128)(2,1)S(1)}, u32[]{:S(2)}, u32[]{:S(2)}) collective-permute-start(bf16[3,2,5120]{2,1,0:T(2,128)(2,1)S(1)} %collective-permute-done.3), channel_id=1, source_target_pairs={{0,1},{1,0},{2,3},{3,2},{4,5},{5,4},{6,7},{7,6},{8,9},{9,8},{10,11... | collective-permute-start | bytes 184328 | tf_op jit(solution)/shard_map/ppermute | solution.py:258
  18.0 1.3 %collective-permute-start.14 = (bf16[3,2,5120]{2,1,0:T(2,128)(2,1)S(1)}, bf16[3,2,5120]{2,1,0:T(2,128)(2,1)S(1)}, u32[]{:S(2)}, u32[]{:S(2)}) collective-permute-start(bf16[3,2,5120]{2,1,0:T(2,128)(2,1)S(1)} %collective-permute-done.4), channel_id=1, source_target_pairs={{0,1},{1,0},{2,3},{3,2},{4,5},{5,4},{6,7},{7,6},{8,9},{9,8},{10,11... | collective-permute-start | bytes 184328 | tf_op jit(solution)/shard_map/ppermute | solution.py:258
  21.3 8.2 %collective-permute-start.17 = (bf16[48,128]{1,0:T(8,128)(2,1)S(1)}, bf16[48,128]{1,0:T(8,128)(2,1)S(1)}, u32[]{:S(2)}, u32[]{:S(2)}) collective-permute-start(bf16[48,128]{1,0:T(8,128)(2,1)S(1)} %get-tuple-element.47), channel_id=1, source_target_pairs={{0,3},{1,2},{2,1},{3,0},{4,7},{5,6},{6,5},{7,4},{8,11},{9,10},{10,... | collective-permute-start | bytes 36872 | tf_op jit(solution)/shard_map/ppermute | solution.py:258
  22.9 6.7 %collective-permute-start.16 = (bf16[48,128]{1,0:T(8,128)(2,1)S(1)}, bf16[48,128]{1,0:T(8,128)(2,1)S(1)}, u32[]{:S(2)}, u32[]{:S(2)}) collective-permute-start(bf16[48,128]{1,0:T(8,128)(2,1)S(1)} %get-tuple-element.47), channel_id=1, source_target_pairs={{0,2},{1,3},{2,0},{3,1},{4,6},{5,7},{6,4},{7,5},{8,10},{9,11},{10,... | collective-permute-start | bytes 36872 | tf_op jit(solution)/shard_map/ppermute | solution.py:258
  23.4 6.2 %collective-permute-start.15 = (bf16[48,128]{1,0:T(8,128)(2,1)S(1)}, bf16[48,128]{1,0:T(8,128)(2,1)S(1)}, u32[]{:S(2)}, u32[]{:S(2)}) collective-permute-start(bf16[48,128]{1,0:T(8,128)(2,1)S(1)} %get-tuple-element.47), channel_id=1, source_target_pairs={{0,1},{1,0},{2,3},{3,2},{4,5},{5,4},{6,7},{7,6},{8,9},{9,8},{10,11... | collective-permute-start | bytes 36872 | tf_op jit(solution)/shard_map/ppermute | solution.py:258
  23.4 3.8 %copy-start = (bf16[3,5120,320]{1,2,0:T(8,128)(2,1)S(1)}, bf16[3,5120,320]{1,2,0:T(8,128)(2,1)}, u32[]{:S(2)}) copy-start(bf16[3,5120,320]{1,2,0:T(8,128)(2,1)} %param.10) | copy-start | bytes 29491204
  29.6 9.2 %collective-permute-start.20 = (bf16[48,128]{1,0:T(8,128)(2,1)S(1)}, bf16[48,128]{1,0:T(8,128)(2,1)S(1)}, u32[]{:S(2)}, u32[]{:S(2)}) collective-permute-start(bf16[48,128]{1,0:T(8,128)(2,1)S(1)} %add_add_fusion.refs_0_), channel_id=1, source_target_pairs={{0,12},{1,13},{2,14},{3,15},{4,8},{5,9},{6,10},{7,11},{8,4},{9,5},... | collective-permute-start | bytes 36872 | tf_op jit(solution)/shard_map/ppermute | solution.py:258
  32.9 5.9 %collective-permute-start.19 = (bf16[48,128]{1,0:T(8,128)(2,1)S(1)}, bf16[48,128]{1,0:T(8,128)(2,1)S(1)}, u32[]{:S(2)}, u32[]{:S(2)}) collective-permute-start(bf16[48,128]{1,0:T(8,128)(2,1)S(1)} %add_add_fusion.refs_0_), channel_id=1, source_target_pairs={{0,8},{1,9},{2,10},{3,11},{4,12},{5,13},{6,14},{7,15},{8,0},{9,1},... | collective-permute-start | bytes 36872 | tf_op jit(solution)/shard_map/ppermute | solution.py:258
  32.9 6.0 %collective-permute-start.18 = (bf16[48,128]{1,0:T(8,128)(2,1)S(1)}, bf16[48,128]{1,0:T(8,128)(2,1)S(1)}, u32[]{:S(2)}, u32[]{:S(2)}) collective-permute-start(bf16[48,128]{1,0:T(8,128)(2,1)S(1)} %add_add_fusion.refs_0_), channel_id=1, source_target_pairs={{0,4},{1,5},{2,6},{3,7},{4,0},{5,1},{6,2},{7,3},{8,12},{9,13},{10,... | collective-permute-start | bytes 36872 | tf_op jit(solution)/shard_map/ppermute | solution.py:258
  35.2 3.6 %copy-start.1 = (bf16[64,64,320]{2,1,0:T(8,128)(2,1)S(1)}, bf16[64,64,320]{2,1,0:T(8,128)(2,1)}, u32[]{:S(2)}) copy-start(bf16[64,64,320]{2,1,0:T(8,128)(2,1)} %param.12) | copy-start | bytes 7864324
  40.6 14.8 %all-to-all-start = ((bf16[16,9,3,2,128]{4,3,2,1,0:T(2,128)(2,1)}), bf16[16,9,3,2,128]{4,3,2,1,0:T(2,128)(2,1)S(1)}, u32[]{:S(2)}, u32[]{:S(2)}) async-start(bf16[16,9,3,2,128]{4,3,2,1,0:T(2,128)(2,1)} %update_values.1), calls=%async_computation | async-start | bytes 442368 | tf_op jit(solution)/shard_map/all_to_all | solution.py:655

commit v13 on v12

--- a/solution.py
+++ b/solution.py
@@ -342,6 +342,26 @@
     )
 
 
+def pack_kernel(*refs):
+    blocks, (out_ref, sem) = refs[:-2], refs[-2:]
+    wait_all(
+        start_all([pltpu.make_async_copy(block, out_ref.at[i], sem.at[i]) for i, block in enumerate(blocks)])
+    )
+
+
+def packed(blocks):
+    return pl.pallas_call(
+        pack_kernel,
+        out_shape=jax.ShapeDtypeStruct((len(blocks),) + blocks[0].shape, blocks[0].dtype),
+        in_specs=[ANY] * len(blocks),
+        out_specs=VMEM,
+        scratch_shapes=[pltpu.SemaphoreType.DMA((len(blocks),))],
+        compiler_params=pltpu.CompilerParams(vmem_limit_bytes=2 * 2**20),
+        cost_estimate=pl.CostEstimate(flops=0, bytes_accessed=10**6, transcendentals=0),
+        name="pack_blocks",
+    )(*blocks)
+
+
 def index_kernel(me_ref, stored_ref, slot_ref, column_ref):
     requests = stored_ref.shape[1]
     steps = slot_ref.shape[1] // requests
@@ -364,14 +384,13 @@
     )(first, stored[None, :])
 
 
-def low_kernel(count, me_ref, slot_ref, down_ref, *refs):
-    blocks, (x_ref, low_ref, sem) = refs[:count], refs[count:]
+def low_kernel(places, packs, me_ref, slot_ref, down_ref, pack_ref, *refs):
+    blocks, (x_ref, low_ref, sem) = refs[: len(places)], refs[len(places) :]
     me = me_ref[0]
     holders, rank, width = down_ref.shape
+    sources = list(zip(places, blocks)) + [(k, pack_ref.at[i]) for i, k in enumerate(packs)]
     wait_all(
-        start_all(
-            [pltpu.make_async_copy(block, x_ref.at[:, :, me ^ k], sem.at[k]) for k, block in enumerate(blocks)]
-        )
+        start_all([pltpu.make_async_copy(block, x_ref.at[:, :, me ^ k], sem.at[k]) for k, block in sources])
     )
     x = step_rows(x_ref, 0, x_ref.shape[1])
     rows = x.shape[0]
@@ -386,24 +405,24 @@
     low_ref[...] = jnp.concatenate([low[: rows // 2], low[rows // 2 :]], axis=1).astype(low_ref.dtype)
 
 
-def low_of(me, blocks, slot, down):
-    count = len(blocks)
+def low_of(me, blocks, packs, pack, slot, down):
+    count = len(blocks) + len(packs)
     steps, chunks = blocks[0].shape[:2]
     rows = count * steps * 2
     rank = down.shape[1]
     return pl.pallas_call(
-        functools.partial(low_kernel, count),
+        functools.partial(low_kernel, tuple(blocks), packs),
         out_shape=(
             jax.ShapeDtypeStruct((steps, chunks, count, 2, HD), jnp.bfloat16),
             jax.ShapeDtypeStruct((rows // 2, 2 * rank), jnp.bfloat16),
         ),
-        in_specs=[SMEM, VMEM, VMEM] + [ANY] * count,
+        in_specs=[SMEM, VMEM, VMEM, ANY] + [ANY] * len(blocks),
         out_specs=(VMEM, VMEM),
         scratch_shapes=[pltpu.SemaphoreType.DMA((count,))],
         compiler_params=pltpu.CompilerParams(vmem_limit_bytes=12 * 2**20),
         cost_estimate=pl.CostEstimate(flops=10**8, bytes_accessed=4 * 10**6, transcendentals=0),
         name="low_rows",
-    )(me, slot, down, *blocks)
+    )(me, slot, down, pack, *blocks.values())
 
 
 def put_chunks(buf, first, value):
@@ -488,7 +507,8 @@
 
 
 def attend_kernel(cos_ref, sin_ref, live_ref, pieces_ref, *refs):
-    keys_refs, values_refs, (out_ref, values_buf, kn_ref, vn_ref, sem) = refs[:2], refs[2:4], refs[4:]
+    *parts, out_ref, values_buf, kn_ref, vn_ref, sem = refs
+    keys_refs, values_refs = parts[: len(parts) // 2], parts[len(parts) // 2 :]
     count, _, steps = pieces_ref.shape[:3]
     rows = 2 * steps
     each = pieces_ref.shape[1] // 3
@@ -581,7 +601,7 @@
     return pl.pallas_call(
         attend_kernel,
         out_shape=jax.ShapeDtypeStruct((steps, heads, 2, HD), jnp.bfloat16),
-        in_specs=[VMEM] * 6 + [HBM] * 2,
+        in_specs=[VMEM] * (4 + len(keys)) + [HBM] * len(values),
         out_specs=VMEM,
         scratch_shapes=[pltpu.VMEM((chips, per, tokens, HD), jnp.bfloat16)]
         + [pltpu.VMEM((chips, 16, per * HD), jnp.float32)] * 2
@@ -622,23 +642,25 @@
         ),
         axis=1,
     )
-    cosine, sine = rotation_rows(lengths, me * req_dev, req_dev, steps)
-    live = live_lanes(lengths, me * req_dev, request_page_table, tokens, page_len)
-    slot, column = index_work((me * holder_count).astype(jnp.int32).reshape(1), stored, steps)
-
-    held = {m: trade(hidden, m, count) for m in range(count - 4, 0, -4)}
-    own, slot, column = lax.optimization_barrier((hidden, slot, column))
-    held[2] = trade(own, 2, count)
+    first, slots, here, stored = lax.optimization_barrier(
+        (me * req_dev, (me * holder_count).astype(jnp.int32).reshape(1), me.astype(jnp.int32).reshape(1), stored)
+    )
+    slot, column = index_work(slots, stored, steps)
+    cosine, sine = rotation_rows(lengths, first, req_dev, steps)
+    live = live_lanes(lengths, first, request_page_table, tokens, page_len)
+
+    whole = hidden.reshape(steps, req_dev, heads, HD).transpose(0, 2, 1, 3)
+    held = {m: trade(hidden, m, count) for m in range(4, count, 4)}
+    held[2] = trade(hidden, 2, count)
     held.update({m | 2: trade(held[m], 2, count) for m in range(4, count, 4)})
-    held[0] = hidden
-    ready = [0, 2, *range(4, count, 4)]
-    *waiting, held[count - 2] = lax.optimization_barrier([held[m] for m in ready] + [held[count - 2]])
-    held.update(zip(ready, waiting))
-    held.update({m | 1: trade(held[m], 1, count) for m in range(0, count, 2)})
-    blocks = [held[k].reshape(steps, req_dev, heads, HD).transpose(0, 2, 1, 3) for k in range(count)]
-    blocks[0] = in_hbm(blocks[0])
-
-    x, low = low_of(me.astype(jnp.int32).reshape(1), blocks, slot, adapter_down_maps)
+    held = {k: v.reshape(steps, req_dev, heads, HD).transpose(0, 2, 1, 3) for k, v in held.items()}
+    held[0] = in_hbm(whole)
+    line = tuple(range(0, count, 4))
+    near = count // 2 + 2
+    *share, held[near] = lax.optimization_barrier([whole] + [held[m] for m in line[1:]] + [held[near]])
+    pack = trade(packed(share), 1, count)
+    held.update({m | 1: trade(held[m], 1, count) for m in range(2, count, 4)})
+    x, low = low_of(here, held, tuple(m | 1 for m in line), pack, slot, adapter_down_maps)
     weight = query_key_value_weight.transpose(0, 2, 1)
     arrived = [trade(low, m, count) for m in (1, 2, 3)]
     query, key = project(0, x, weight), project(1, x, weight)
@@ -646,16 +668,13 @@
     low = (low + arrived[0]) + (arrived[1] + arrived[2])
     arrived = [trade(low, m, count) for m in range(4, count, 4)]
     base = project(2, x, weight)
-    early_heads = heads // 4
-    early_cache = cache_by_head(pool, 0, early_heads)
-    arrived, base, early_cache = lax.optimization_barrier((arrived, base, early_cache))
+    arrived, base = lax.optimization_barrier((arrived, base))
     send = update_values(column, query, key, base, adapter_up_maps.reshape(adapter_count * rank, -1), [low, *arrived])
     send, pool = lax.optimization_barrier((send, pool))
-    late_cache = cache_by_head(pool, early_heads, heads - early_heads)
+    keys, values = cache_by_head(pool, 0, heads)
     pieces = lax.all_to_all(send, "replica", split_axis=0, concat_axis=0, tiled=True)
 
-    keys, values = zip(early_cache, late_cache)
-    out = attend(cosine, sine, live, pieces, keys, values)
+    out = attend(cosine, sine, live, pieces, [keys], [values])
     return out.transpose(0, 2, 1, 3).reshape(steps, req_dev, width)
 
 

time: 59.8 us -> 56.2 us (0.940)
  waiting for transfers between devices: 7.58 us -> 13 us
  local copies, waits for them, and re-layouts: 4.44 us -> 0.04 us
  starting transfers between devices: 24.9 us -> 21 us
  Pallas kernels: 20.6 us -> 18.5 us
  other arithmetic: 1.53 us -> 2.86 us
    ppermute x21 -> x18, waiting for transfers between devices: 4.06 us -> 10.7 us  [trade(): return lax.ppermute(value, 'replica', [(i, i ^ mask) for i in range(count)])]
    unnamed x12 -> x14, local copies, waits for them, and re-layouts: 4.44 us -> 0.04 us
    ppermute x21 -> x18, starting transfers between devices: 19.5 us -> 16.8 us  [trade(): return lax.ppermute(value, 'replica', [(i, i ^ mask) for i in range(count)])]
    pallas_call x2 -> x1, Pallas kernels: 9.32 us -> 6.87 us  [cache_by_head(): pl.pallas_call(functools.partial(cache_kernel, first), out_shape=(jax.Sha...]
    all_to_all x1, starting transfers between devices: 5.45 us -> 4.18 us  [chip_plan(): lax.all_to_all(send, 'replica', split_axis=0, concat_axis=0, tiled=True)]
    all_to_all x1, waiting for transfers between devices: 3.53 us -> 2.38 us  [chip_plan(): lax.all_to_all(send, 'replica', split_axis=0, concat_axis=0, tiled=True)]
    reduce_max x1, other arithmetic: 0.09 us -> 0.77 us  [live_lanes(): jnp.max(jnp.where(request_page_table[:, :, None] == (lane // page_len)[No...]
    reduce_sum x1, other arithmetic: 0.18 us -> 0.84 us  [live_lanes(): jnp.sum(chosen, axis=1, keepdims=True)]
  transfers between devices with their start and end apart: 22 -> 19, of which waited for: 8 -> 10; matrix products, arithmetic and copies ran while one was open for 3% -> 5% of each run, Pallas kernels for 22% -> 19%
where the time goes in v13:
time: 56.2 us; the launch traced here: 55.9 us
  starting transfers between devices  21 us (37%)
  Pallas kernels  18.5 us (33%)
  waiting for transfers between devices  13 us (23%)
  other arithmetic  2.86 us (5%)
    ppermute x18, starting transfers between devices, trade(): return lax.ppermute(value, 'replica', [(i, i ^ mask) for i in range(count)])  16.8 us
    ppermute x18, waiting for transfers between devices, trade(): return lax.ppermute(value, 'replica', [(i, i ^ mask) for i in range(count)])  10.7 us
    pallas_call x1, Pallas kernels, cache_by_head(): pl.pallas_call(functools.partial(cache_kernel, first), out_shape=(jax.Sha...  6.87 us
    all_to_all x1, starting transfers between devices, chip_plan(): lax.all_to_all(send, 'replica', split_axis=0, concat_axis=0, tiled=True)  4.18 us
    pallas_call x1, Pallas kernels, attend(): pl.pallas_call(attend_kernel, out_shape=jax.ShapeDtypeStruct((steps, head...  3.85 us
    pallas_call x3, Pallas kernels, project(): pl.pallas_call(functools.partial(project_kernel, which), out_shape=chunks...  3.36 us
    all_to_all x1, waiting for transfers between devices, chip_plan(): lax.all_to_all(send, 'replica', split_axis=0, concat_axis=0, tiled=True)  2.38 us
    pallas_call x1, Pallas kernels, low_of(): pl.pallas_call(functools.partial(low_kernel, tuple(blocks), packs), out_s...  2.31 us
  transfers between devices with their start and end apart: 19, of which 10 were waited for; matrix products, arithmetic and copies ran while one was open for 5% of the time, Pallas kernels for 19%

profile of v13, /device:TPU:0, one launch (start us, length us, event | category | flops | bytes accessed | tf_op | source)
XLA Modules:
  0.0 55.9 jit_solution(16492578726313047234)
XLA Ops:
  0.0 4.0 %collective-permute-start.1 = (bf16[3,2,5120]{2,1,0:T(2,128)(2,1)}, bf16[3,2,5120]{2,1,0:T(2,128)(2,1)S(1)}, u32[]{:S(2)}, u32[]{:S(2)}) collective-permute-start(bf16[3,2,5120]{2,1,0:T(2,128)(2,1)} %param.9), channel_id=1, source_target_pairs={{0,8},{1,9},{2,10},{3,11},{4,12},{5,13},{6,14},{7,15},{8,0},{9,1},... | collective-permute-start | bytes 184328 | tf_op jit(solution)/shard_map/ppermute | solution.py:258
  4.0 1.6 %collective-permute-start = (bf16[3,2,5120]{2,1,0:T(2,128)(2,1)}, bf16[3,2,5120]{2,1,0:T(2,128)(2,1)S(1)}, u32[]{:S(2)}, u32[]{:S(2)}) collective-permute-start(bf16[3,2,5120]{2,1,0:T(2,128)(2,1)} %param.9), channel_id=1, source_target_pairs={{0,4},{1,5},{2,6},{3,7},{4,0},{5,1},{6,2},{7,3},{8,12},{9,13},{10,... | collective-permute-start | bytes 184328 | tf_op jit(solution)/shard_map/ppermute | solution.py:258
  5.6 1.5 %collective-permute-start.5 = (bf16[3,2,5120]{2,1,0:T(2,128)(2,1)}, bf16[3,2,5120]{2,1,0:T(2,128)(2,1)S(1)}, u32[]{:S(2)}, u32[]{:S(2)}) collective-permute-start(bf16[3,2,5120]{2,1,0:T(2,128)(2,1)} %param.9), channel_id=1, source_target_pairs={{0,2},{1,3},{2,0},{3,1},{4,6},{5,7},{6,4},{7,5},{8,10},{9,11},{10,... | collective-permute-start | bytes 184328 | tf_op jit(solution)/shard_map/ppermute | solution.py:258
  7.1 0.2 collective-permute-start.2
  7.4 0.8 %select_reduce_fusion.1 = s32[32]{0:T(128)S(1)} fusion(s32[64]{0:T(128)} %param.13, s32[32]{0:T(128)} %param.14), kind=kLoop, calls=%fused_computation.1 | loop fusion | flops 6112 | bytes 512 | tf_op jit(solution)/shard_map/reduce_sum | solution.py:637
  8.2 0.8 %fusion.3 = s32[2]{0:T(128)S(1)} fusion(s32[32]{0:T(128)} %param.15, s32[2]{0:T(128)S(1)} %iota_add_fusion), kind=kLoop, calls=%fused_computation.22 | loop fusion | flops 190 | bytes 144 | tf_op jit(solution)/shard_map/reduce_sum | solution.py:254
  9.1 0.8 %select_reduce_fusion = s32[2,256]{1,0:T(2,128)S(1)} fusion(s32[256]{0:T(256)S(1)} %and_select_fusion.1, s32[2,32]{1,0:T(2,128)} %param.16), kind=kLoop, calls=%fused_computation | loop fusion | flops 48640 | bytes 3328 | tf_op jit(solution)/shard_map/reduce_max | solution.py:249
  9.8 0.0 slice-start
  9.8 0.0 copy-start.2
  9.9 0.0 copy-start.3
  9.9 0.0 copy-start.1
  9.9 0.0 slice-start.1
  9.9 0.2 index_work.1
  10.1 0.0 collective-permute-done.1
  10.1 0.4 collective-permute-start.3
  10.4 0.1 and_convert_fusion.live_ref
  10.5 2.8 %collective-permute-done.2 = bf16[3,2,5120]{2,1,0:T(2,128)(2,1)S(1)} collective-permute-done((bf16[3,2,5120]{2,1,0:T(2,128)(2,1)}, bf16[3,2,5120]{2,1,0:T(2,128)(2,1)S(1)}, u32[]{:S(2)}, u32[]{:S(2)}) %collective-permute-start.2) | collective-permute-done | bytes 61472 | tf_op jit(solution)/shard_map/ppermute | solution.py:258
  13.4 1.0 %collective-permute-done.3 = bf16[3,2,5120]{2,1,0:T(2,128)(2,1)S(1)} collective-permute-done((bf16[3,2,5120]{2,1,0:T(2,128)(2,1)S(1)}, bf16[3,2,5120]{2,1,0:T(2,128)(2,1)S(1)}, u32[]{:S(2)}, u32[]{:S(2)}) %collective-permute-start.3) | collective-permute-done | bytes 61472 | tf_op jit(solution)/shard_map/ppermute | solution.py:258
  14.4 0.3 pack_blocks.1
  14.7 0.1 collective-permute-start.4
  14.8 0.4 collective-permute-start.6
  15.2 1.7 %collective-permute-start.7 = (bf16[3,2,5120]{2,1,0:T(2,128)(2,1)S(1)}, bf16[3,2,5120]{2,1,0:T(2,128)(2,1)S(1)}, u32[]{:S(2)}, u32[]{:S(2)}) collective-permute-start(bf16[3,2,5120]{2,1,0:T(2,128)(2,1)S(1)} %collective-permute-done.2), channel_id=1, source_target_pairs={{0,2},{1,3},{2,0},{3,1},{4,6},{5,7},{6,4},{7,5},{8,10},{9,11},{10,... | collective-permute-start | bytes 184328 | tf_op jit(solution)/shard_map/ppermute | solution.py:258
  16.9 0.2 select_reduce_fusion.2
  17.1 0.1 collective-permute-start.8
  17.2 2.5 %collective-permute-done.6 = bf16[3,2,5120]{2,1,0:T(2,128)(2,1)S(1)} collective-permute-done((bf16[3,2,5120]{2,1,0:T(2,128)(2,1)S(1)}, bf16[3,2,5120]{2,1,0:T(2,128)(2,1)S(1)}, u32[]{:S(2)}, u32[]{:S(2)}) %collective-permute-start.6) | collective-permute-done | bytes 61472 | tf_op jit(solution)/shard_map/ppermute | solution.py:258
  19.7 0.5 collective-permute-start.10
  20.2 0.3 collective-permute-done.7
  20.6 0.4 collective-permute-done.9.refs_9_
  20.9 0.2 collective-permute-done.10.refs_10_
  21.1 0.7 %collective-permute-done.11.refs_11_ = bf16[3,40,2,128]{3,2,1,0:T(2,128)(2,1)S(1)} collective-permute-done((bf16[3,40,2,128]{3,2,1,0:T(2,128)(2,1)S(1)}, bf16[3,40,2,128]{3,2,1,0:T(2,128)(2,1)S(1)}, u32[]{:S(2)}, u32[]{:S(2)}) %collective-permute-start.11) | collective-permute-done | bytes 61472 | tf_op jit(solution)/shard_map/ppermute | solution.py:258
  21.8 2.3 %low_rows.1 = (bf16[3,40,16,2,128]{4,3,2,1,0:T(2,128)(2,1)S(1)}, bf16[48,128]{1,0:T(8,128)(2,1)S(1)}) custom-call(s32[1]{0:T(128)} %bitcast.1.me_ref, s32[1,96]{1,0:T(1,128)S(1)} %get-tuple-element.37.slot_ref, bf16[4,64,5120]{2,1,0:T(8,128)(2,1)S(1)} %copy-done.1, bf16[4,3,40,2,128]{4,3,2,1,0:T(2,128)(2,1)S(1)} %collective-permute-done.4.pack_ref, ...), custom_call_target="tpu_custom_call" | custom-call | flops 100000000 | bytes 4000000 | tf_op jit(solution)/shard_map/low_rows/pallas_call | solution.py:413
  24.1 0.4 collective-permute-start.14
  24.5 1.4 %collective-permute-start.13 = (bf16[48,128]{1,0:T(8,128)(2,1)S(1)}, bf16[48,128]{1,0:T(8,128)(2,1)S(1)}, u32[]{:S(2)}, u32[]{:S(2)}) collective-permute-start(bf16[48,128]{1,0:T(8,128)(2,1)S(1)} %get-tuple-element.43), channel_id=1, source_target_pairs={{0,2},{1,3},{2,0},{3,1},{4,6},{5,7},{6,4},{7,5},{8,10},{9,11},{10,... | collective-permute-start | bytes 36872 | tf_op jit(solution)/shard_map/ppermute | solution.py:258
  26.0 0.1 collective-permute-start.12
  26.1 1.1 %project.4.key_ref = bf16[3,3,16,2,128]{4,3,2,1,0:T(2,128)(2,1)S(1)} custom-call(bf16[3,40,16,2,128]{4,3,2,1,0:T(2,128)(2,1)S(1)} %get-tuple-element.44.x_ref, bf16[3,320,5120]{2,1,0:T(8,128)(2,1)S(1)} %bitcast.37), custom_call_target="tpu_custom_call" | custom-call | flops 500000000 | bytes 4000000 | tf_op jit(solution)/shard_map/project/pallas_call | solution.py:455
  27.2 1.1 %project.3.query_ref = bf16[3,3,16,2,128]{4,3,2,1,0:T(2,128)(2,1)S(1)} custom-call(bf16[3,40,16,2,128]{4,3,2,1,0:T(2,128)(2,1)S(1)} %get-tuple-element.44.x_ref, bf16[3,320,5120]{2,1,0:T(8,128)(2,1)S(1)} %bitcast.38), custom_call_target="tpu_custom_call" | custom-call | flops 500000000 | bytes 4000000 | tf_op jit(solution)/shard_map/project/pallas_call | solution.py:455
  28.4 0.0 copy-start
  28.4 3.7 %collective-permute-start.17 = (bf16[48,128]{1,0:T(8,128)(2,1)S(1)}, bf16[48,128]{1,0:T(8,128)(2,1)S(1)}, u32[]{:S(2)}, u32[]{:S(2)}) collective-permute-start(bf16[48,128]{1,0:T(8,128)(2,1)S(1)} %add_add_fusion.refs_0_), channel_id=1, source_target_pairs={{0,12},{1,13},{2,14},{3,15},{4,8},{5,9},{6,10},{7,11},{8,4},{9,5},... | collective-permute-start | bytes 36872 | tf_op jit(solution)/shard_map/ppermute | solution.py:258
  32.1 0.8 %collective-permute-start.15 = (bf16[48,128]{1,0:T(8,128)(2,1)S(1)}, bf16[48,128]{1,0:T(8,128)(2,1)S(1)}, u32[]{:S(2)}, u32[]{:S(2)}) collective-permute-start(bf16[48,128]{1,0:T(8,128)(2,1)S(1)} %add_add_fusion.refs_0_), channel_id=1, source_target_pairs={{0,4},{1,5},{2,6},{3,7},{4,0},{5,1},{6,2},{7,3},{8,12},{9,13},{10,... | collective-permute-start | bytes 36872 | tf_op jit(solution)/shard_map/ppermute | solution.py:258
  32.8 1.1 %project.5.base_ref = f32[96,320]{1,0:T(8,128)S(1)} custom-call(bf16[3,40,16,2,128]{4,3,2,1,0:T(2,128)(2,1)S(1)} %get-tuple-element.44.x_ref, bf16[3,320,5120]{2,1,0:T(8,128)(2,1)S(1)} %bitcast.39), custom_call_target="tpu_custom_call" | custom-call | flops 500000000 | bytes 4000000 | tf_op jit(solution)/shard_map/project/pallas_call | solution.py:455
  33.9 0.1 collective-permute-done.17.refs_3_
  34.1 2.6 %collective-permute-done.16.refs_2_ = bf16[48,128]{1,0:T(8,128)(2,1)S(1)} collective-permute-done((bf16[48,128]{1,0:T(8,128)(2,1)S(1)}, bf16[48,128]{1,0:T(8,128)(2,1)S(1)}, u32[]{:S(2)}, u32[]{:S(2)}) %collective-permute-start.16) | collective-permute-done | bytes 12320 | tf_op jit(solution)/shard_map/ppermute | solution.py:258
  36.7 1.6 %update_values.1 = bf16[16,9,3,2,128]{4,3,2,1,0:T(2,128)(2,1)} custom-call(s32[96,1]{1,0:T(8,128)S(1)} %get-tuple-element.35.stored_ref, bf16[3,3,16,2,128]{4,3,2,1,0:T(2,128)(2,1)S(1)} %project.3.query_ref, bf16[3,3,16,2,128]{4,3,2,1,0:T(2,128)(2,1)S(1)} %project.4.key_ref, f32[96,320]{1,0:T(8,128)S(1)} %project.5.base_ref, bf16[4096,320]{1,0:T(8,128)(2,1)S(1)} %bitcast.40, ...), custom_call_target="tpu_custom_call" | custom-call | flops 300000000 | bytes 4000000 | tf_op jit(solution)/shard_map/update_values/pallas_call | solution.py:494
  38.3 4.2 %all-to-all-start = ((bf16[16,9,3,2,128]{4,3,2,1,0:T(2,128)(2,1)}), bf16[16,9,3,2,128]{4,3,2,1,0:T(2,128)(2,1)S(1)}, u32[]{:S(2)}, u32[]{:S(2)}) async-start(bf16[16,9,3,2,128]{4,3,2,1,0:T(2,128)(2,1)} %update_values.1), calls=%async_computation | async-start | bytes 442368 | tf_op jit(solution)/shard_map/all_to_all | solution.py:675
  42.5 0.1 fusion
  42.6 6.9 %cache_by_head.1 = (bf16[40,256,128]{2,1,0:T(8,128)(2,1)S(1)}, bf16[40,256,128]{2,1,0:T(8,128)(2,1)}) custom-call(bf16[256,40,2,128]{3,2,1,0:T(2,128)(2,1)} %bitcast.58), custom_call_target="tpu_custom_call" | custom-call | bytes 12000000 | tf_op jit(solution)/shard_map/cache_by_head/pallas_call | solution.py:313
  49.5 2.4 %all-to-all-done.pieces_ref = bf16[16,9,3,2,128]{4,3,2,1,0:T(2,128)(2,1)S(1)} async-done(((bf16[16,9,3,2,128]{4,3,2,1,0:T(2,128)(2,1)}), bf16[16,9,3,2,128]{4,3,2,1,0:T(2,128)(2,1)S(1)}, u32[]{:S(2)}, u32[]{:S(2)}) %all-to-all-start) | async-done | bytes 221216 | tf_op jit(solution)/shard_map/all_to_all | solution.py:675
  51.9 3.9 %attention.1 = bf16[3,40,2,128]{3,2,1,0:T(2,128)(2,1)} custom-call(f32[8,128]{1,0:T(8,128)S(1)} %get-tuple-element.60.cos_ref, f32[8,128]{1,0:T(8,128)S(1)} %get-tuple-element.59.sin_ref, s32[2,256]{1,0:T(2,128)S(1)} %and_convert_fusion.live_ref, bf16[16,9,3,2,128]{4,3,2,1,0:T(2,128)(2,1)S(1)} %all-to-all-done.pieces_ref, ...), custom_call_target="tpu_custom_call" | custom-call | flops 1000000000 | bytes 6000000 | tf_op jit(solution)/shard_map/attention/pallas_call | solution.py:601
  (27 shorter events, 0.1 us)
Async XLA Ops:
  0.0 10.1 %collective-permute-start.1 = (bf16[3,2,5120]{2,1,0:T(2,128)(2,1)}, bf16[3,2,5120]{2,1,0:T(2,128)(2,1)S(1)}, u32[]{:S(2)}, u32[]{:S(2)}) collective-permute-start(bf16[3,2,5120]{2,1,0:T(2,128)(2,1)} %param.9), channel_id=1, source_target_pairs={{0,8},{1,9},{2,10},{3,11},{4,12},{5,13},{6,14},{7,15},{8,0},{9,1},... | collective-permute-start | bytes 184328 | tf_op jit(solution)/shard_map/ppermute | solution.py:258
  4.0 6.5 %collective-permute-start = (bf16[3,2,5120]{2,1,0:T(2,128)(2,1)}, bf16[3,2,5120]{2,1,0:T(2,128)(2,1)S(1)}, u32[]{:S(2)}, u32[]{:S(2)}) collective-permute-start(bf16[3,2,5120]{2,1,0:T(2,128)(2,1)} %param.9), channel_id=1, source_target_pairs={{0,4},{1,5},{2,6},{3,7},{4,0},{5,1},{6,2},{7,3},{8,12},{9,13},{10,... | collective-permute-start | bytes 184328 | tf_op jit(solution)/shard_map/ppermute | solution.py:258
  5.6 11.5 %collective-permute-start.5 = (bf16[3,2,5120]{2,1,0:T(2,128)(2,1)}, bf16[3,2,5120]{2,1,0:T(2,128)(2,1)S(1)}, u32[]{:S(2)}, u32[]{:S(2)}) collective-permute-start(bf16[3,2,5120]{2,1,0:T(2,128)(2,1)} %param.9), channel_id=1, source_target_pairs={{0,2},{1,3},{2,0},{3,1},{4,6},{5,7},{6,4},{7,5},{8,10},{9,11},{10,... | collective-permute-start | bytes 184328 | tf_op jit(solution)/shard_map/ppermute | solution.py:258
  7.1 6.2 %collective-permute-start.2 = (bf16[3,2,5120]{2,1,0:T(2,128)(2,1)}, bf16[3,2,5120]{2,1,0:T(2,128)(2,1)S(1)}, u32[]{:S(2)}, u32[]{:S(2)}) collective-permute-start(bf16[3,2,5120]{2,1,0:T(2,128)(2,1)} %param.9), channel_id=1, source_target_pairs={{0,12},{1,13},{2,14},{3,15},{4,8},{5,9},{6,10},{7,11},{8,4},{9,5},... | collective-permute-start | bytes 184328 | tf_op jit(solution)/shard_map/ppermute | solution.py:258
  9.8 16.2 %slice-start = ((s8[9830400]{0:T(1024)(128)(4,1)}), s8[4194304]{0:T(1024)(128)(4,1)S(1)}, s32[]{:S(2)}) async-start(s8[9830400]{0:T(1024)(128)(4,1)} %bitcast.35), calls=%async_computation.1 | async-start | bytes 8388608
  9.8 4.5 %copy-start.2 = (bf16[3,2,5120]{2,1,0:T(2,128)(2,1)S(1)}, bf16[3,2,5120]{2,1,0:T(2,128)(2,1)}, u32[]{:S(2)}) copy-start(bf16[3,2,5120]{2,1,0:T(2,128)(2,1)} %param.9) | copy-start | bytes 184324
  9.9 7.1 %copy-start.3 = (s32[32]{0:T(128)S(1)}, s32[32]{0:T(128)}, u32[]{:S(2)}) copy-start(s32[32]{0:T(128)} %param.15) | copy-start | bytes 388
  9.9 11.9 %copy-start.1 = (bf16[4,64,5120]{2,1,0:T(8,128)(2,1)S(1)}, bf16[4,64,5120]{2,1,0:T(8,128)(2,1)}, u32[]{:S(2)}) copy-start(bf16[4,64,5120]{2,1,0:T(8,128)(2,1)} %down_ref.1) | copy-start | bytes 7864324
  9.9 16.2 %slice-start.1 = ((s8[9830400]{0:T(1024)(128)(4,1)}), s8[4194304]{0:T(1024)(128)(4,1)S(1)}, s32[]{:S(2)}) async-start(s8[9830400]{0:T(1024)(128)(4,1)} %bitcast.35), calls=%async_computation.2 | async-start | bytes 8388608
  9.9 16.2 %slice-start.2 = ((s8[9830400]{0:T(1024)(128)(4,1)}), s8[1441792]{0:T(1024)(128)(4,1)S(1)}, s32[]{:S(2)}) async-start(s8[9830400]{0:T(1024)(128)(4,1)} %bitcast.35), calls=%async_computation.3 | async-start | bytes 2883584
  10.1 4.3 %collective-permute-start.3 = (bf16[3,2,5120]{2,1,0:T(2,128)(2,1)S(1)}, bf16[3,2,5120]{2,1,0:T(2,128)(2,1)S(1)}, u32[]{:S(2)}, u32[]{:S(2)}) collective-permute-start(bf16[3,2,5120]{2,1,0:T(2,128)(2,1)S(1)} %collective-permute-done.1), channel_id=1, source_target_pairs={{0,2},{1,3},{2,0},{3,1},{4,6},{5,7},{6,4},{7,5},{8,10},{9,11},{10,... | collective-permute-start | bytes 184328 | tf_op jit(solution)/shard_map/ppermute | solution.py:258
  14.7 7.1 %collective-permute-start.4 = (bf16[4,3,40,2,128]{4,3,2,1,0:T(2,128)(2,1)S(1)}, bf16[4,3,40,2,128]{4,3,2,1,0:T(2,128)(2,1)S(1)}, u32[]{:S(2)}, u32[]{:S(2)}) collective-permute-start(bf16[4,3,40,2,128]{4,3,2,1,0:T(2,128)(2,1)S(1)} %pack_blocks.1), channel_id=1, source_target_pairs={{0,1},{1,0},{2,3},{3,2},{4,5},{5,4},{6,7},{7,6},{8,9},{9,8},{10,11... | collective-permute-start | bytes 737288 | tf_op jit(solution)/shard_map/ppermute | solution.py:258
  14.8 4.9 %collective-permute-start.6 = (bf16[3,2,5120]{2,1,0:T(2,128)(2,1)S(1)}, bf16[3,2,5120]{2,1,0:T(2,128)(2,1)S(1)}, u32[]{:S(2)}, u32[]{:S(2)}) collective-permute-start(bf16[3,2,5120]{2,1,0:T(2,128)(2,1)S(1)} %collective-permute-done), channel_id=1, source_target_pairs={{0,2},{1,3},{2,0},{3,1},{4,6},{5,7},{6,4},{7,5},{8,10},{9,11},{10,... | collective-permute-start | bytes 184328 | tf_op jit(solution)/shard_map/ppermute | solution.py:258
  15.2 5.4 %collective-permute-start.7 = (bf16[3,2,5120]{2,1,0:T(2,128)(2,1)S(1)}, bf16[3,2,5120]{2,1,0:T(2,128)(2,1)S(1)}, u32[]{:S(2)}, u32[]{:S(2)}) collective-permute-start(bf16[3,2,5120]{2,1,0:T(2,128)(2,1)S(1)} %collective-permute-done.2), channel_id=1, source_target_pairs={{0,2},{1,3},{2,0},{3,1},{4,6},{5,7},{6,4},{7,5},{8,10},{9,11},{10,... | collective-permute-start | bytes 184328 | tf_op jit(solution)/shard_map/ppermute | solution.py:258
  17.1 3.5 %collective-permute-start.8 = (bf16[3,40,2,128]{3,2,1,0:T(2,128)(2,1)S(1)}, bf16[3,40,2,128]{3,2,1,0:T(2,128)(2,1)S(1)}, u32[]{:S(2)}, u32[]{:S(2)}) collective-permute-start(bf16[3,40,2,128]{3,2,1,0:T(2,128)(2,1)S(1)} %bitcast.49), channel_id=1, source_target_pairs={{0,1},{1,0},{2,3},{3,2},{4,5},{5,4},{6,7},{7,6},{8,9},{9,8},{10,11... | collective-permute-start | bytes 184328 | tf_op jit(solution)/shard_map/ppermute | solution.py:258
  19.7 1.2 %collective-permute-start.9 = (bf16[3,40,2,128]{3,2,1,0:T(2,128)(2,1)S(1)}, bf16[3,40,2,128]{3,2,1,0:T(2,128)(2,1)S(1)}, u32[]{:S(2)}, u32[]{:S(2)}) collective-permute-start(bf16[3,40,2,128]{3,2,1,0:T(2,128)(2,1)S(1)} %bitcast.53), channel_id=1, source_target_pairs={{0,1},{1,0},{2,3},{3,2},{4,5},{5,4},{6,7},{7,6},{8,9},{9,8},{10,11... | collective-permute-start | bytes 184328 | tf_op jit(solution)/shard_map/ppermute | solution.py:258
  19.7 1.4 %collective-permute-start.10 = (bf16[3,40,2,128]{3,2,1,0:T(2,128)(2,1)S(1)}, bf16[3,40,2,128]{3,2,1,0:T(2,128)(2,1)S(1)}, u32[]{:S(2)}, u32[]{:S(2)}) collective-permute-start(bf16[3,40,2,128]{3,2,1,0:T(2,128)(2,1)S(1)} %bitcast.51), channel_id=1, source_target_pairs={{0,1},{1,0},{2,3},{3,2},{4,5},{5,4},{6,7},{7,6},{8,9},{9,8},{10,11... | collective-permute-start | bytes 184328 | tf_op jit(solution)/shard_map/ppermute | solution.py:258
  20.5 1.2 %collective-permute-start.11 = (bf16[3,40,2,128]{3,2,1,0:T(2,128)(2,1)S(1)}, bf16[3,40,2,128]{3,2,1,0:T(2,128)(2,1)S(1)}, u32[]{:S(2)}, u32[]{:S(2)}) collective-permute-start(bf16[3,40,2,128]{3,2,1,0:T(2,128)(2,1)S(1)} %bitcast.55), channel_id=1, source_target_pairs={{0,1},{1,0},{2,3},{3,2},{4,5},{5,4},{6,7},{7,6},{8,9},{9,8},{10,11... | collective-permute-start | bytes 184328 | tf_op jit(solution)/shard_map/ppermute | solution.py:258
  24.1 4.2 %collective-permute-start.14 = (bf16[48,128]{1,0:T(8,128)(2,1)S(1)}, bf16[48,128]{1,0:T(8,128)(2,1)S(1)}, u32[]{:S(2)}, u32[]{:S(2)}) collective-permute-start(bf16[48,128]{1,0:T(8,128)(2,1)S(1)} %get-tuple-element.43), channel_id=1, source_target_pairs={{0,3},{1,2},{2,1},{3,0},{4,7},{5,6},{6,5},{7,4},{8,11},{9,10},{10,... | collective-permute-start | bytes 36872 | tf_op jit(solution)/shard_map/ppermute | solution.py:258
  24.5 3.8 %collective-permute-start.13 = (bf16[48,128]{1,0:T(8,128)(2,1)S(1)}, bf16[48,128]{1,0:T(8,128)(2,1)S(1)}, u32[]{:S(2)}, u32[]{:S(2)}) collective-permute-start(bf16[48,128]{1,0:T(8,128)(2,1)S(1)} %get-tuple-element.43), channel_id=1, source_target_pairs={{0,2},{1,3},{2,0},{3,1},{4,6},{5,7},{6,4},{7,5},{8,10},{9,11},{10,... | collective-permute-start | bytes 36872 | tf_op jit(solution)/shard_map/ppermute | solution.py:258
  26.0 2.4 %collective-permute-start.12 = (bf16[48,128]{1,0:T(8,128)(2,1)S(1)}, bf16[48,128]{1,0:T(8,128)(2,1)S(1)}, u32[]{:S(2)}, u32[]{:S(2)}) collective-permute-start(bf16[48,128]{1,0:T(8,128)(2,1)S(1)} %get-tuple-element.43), channel_id=1, source_target_pairs={{0,1},{1,0},{2,3},{3,2},{4,5},{5,4},{6,7},{7,6},{8,9},{9,8},{10,11... | collective-permute-start | bytes 36872 | tf_op jit(solution)/shard_map/ppermute | solution.py:258
  28.4 8.3 %copy-start = (bf16[64,64,320]{2,1,0:T(8,128)(2,1)S(1)}, bf16[64,64,320]{2,1,0:T(8,128)(2,1)}, u32[]{:S(2)}) copy-start(bf16[64,64,320]{2,1,0:T(8,128)(2,1)} %param.12) | copy-start | bytes 7864324
  28.4 5.7 %collective-permute-start.17 = (bf16[48,128]{1,0:T(8,128)(2,1)S(1)}, bf16[48,128]{1,0:T(8,128)(2,1)S(1)}, u32[]{:S(2)}, u32[]{:S(2)}) collective-permute-start(bf16[48,128]{1,0:T(8,128)(2,1)S(1)} %add_add_fusion.refs_0_), channel_id=1, source_target_pairs={{0,12},{1,13},{2,14},{3,15},{4,8},{5,9},{6,10},{7,11},{8,4},{9,5},... | collective-permute-start | bytes 36872 | tf_op jit(solution)/shard_map/ppermute | solution.py:258
  32.1 4.6 %collective-permute-start.16 = (bf16[48,128]{1,0:T(8,128)(2,1)S(1)}, bf16[48,128]{1,0:T(8,128)(2,1)S(1)}, u32[]{:S(2)}, u32[]{:S(2)}) collective-permute-start(bf16[48,128]{1,0:T(8,128)(2,1)S(1)} %add_add_fusion.refs_0_), channel_id=1, source_target_pairs={{0,8},{1,9},{2,10},{3,11},{4,12},{5,13},{6,14},{7,15},{8,0},{9,1},... | collective-permute-start | bytes 36872 | tf_op jit(solution)/shard_map/ppermute | solution.py:258
  32.1 4.6 %collective-permute-start.15 = (bf16[48,128]{1,0:T(8,128)(2,1)S(1)}, bf16[48,128]{1,0:T(8,128)(2,1)S(1)}, u32[]{:S(2)}, u32[]{:S(2)}) collective-permute-start(bf16[48,128]{1,0:T(8,128)(2,1)S(1)} %add_add_fusion.refs_0_), channel_id=1, source_target_pairs={{0,4},{1,5},{2,6},{3,7},{4,0},{5,1},{6,2},{7,3},{8,12},{9,13},{10,... | collective-permute-start | bytes 36872 | tf_op jit(solution)/shard_map/ppermute | solution.py:258
  38.3 13.6 %all-to-all-start = ((bf16[16,9,3,2,128]{4,3,2,1,0:T(2,128)(2,1)}), bf16[16,9,3,2,128]{4,3,2,1,0:T(2,128)(2,1)S(1)}, u32[]{:S(2)}, u32[]{:S(2)}) async-start(bf16[16,9,3,2,128]{4,3,2,1,0:T(2,128)(2,1)} %update_values.1), calls=%async_computation | async-start | bytes 442368 | tf_op jit(solution)/shard_map/all_to_all | solution.py:675

commit v14 on v12

--- a/solution.py
+++ b/solution.py
@@ -488,7 +488,8 @@
 
 
 def attend_kernel(cos_ref, sin_ref, live_ref, pieces_ref, *refs):
-    keys_refs, values_refs, (out_ref, values_buf, kn_ref, vn_ref, sem) = refs[:2], refs[2:4], refs[4:]
+    *parts, out_ref, values_buf, kn_ref, vn_ref, sem = refs
+    keys_refs, values_refs = parts[: len(parts) // 2], parts[len(parts) // 2 :]
     count, _, steps = pieces_ref.shape[:3]
     rows = 2 * steps
     each = pieces_ref.shape[1] // 3
@@ -581,7 +582,7 @@
     return pl.pallas_call(
         attend_kernel,
         out_shape=jax.ShapeDtypeStruct((steps, heads, 2, HD), jnp.bfloat16),
-        in_specs=[VMEM] * 6 + [HBM] * 2,
+        in_specs=[VMEM] * (4 + len(keys)) + [HBM] * len(values),
         out_specs=VMEM,
         scratch_shapes=[pltpu.VMEM((chips, per, tokens, HD), jnp.bfloat16)]
         + [pltpu.VMEM((chips, 16, per * HD), jnp.float32)] * 2
@@ -622,23 +623,21 @@
         ),
         axis=1,
     )
-    cosine, sine = rotation_rows(lengths, me * req_dev, req_dev, steps)
-    live = live_lanes(lengths, me * req_dev, request_page_table, tokens, page_len)
-    slot, column = index_work((me * holder_count).astype(jnp.int32).reshape(1), stored, steps)
-
-    held = {m: trade(hidden, m, count) for m in range(count - 4, 0, -4)}
-    own, slot, column = lax.optimization_barrier((hidden, slot, column))
-    held[2] = trade(own, 2, count)
-    held.update({m | 2: trade(held[m], 2, count) for m in range(4, count, 4)})
-    held[0] = hidden
-    ready = [0, 2, *range(4, count, 4)]
-    *waiting, held[count - 2] = lax.optimization_barrier([held[m] for m in ready] + [held[count - 2]])
-    held.update(zip(ready, waiting))
-    held.update({m | 1: trade(held[m], 1, count) for m in range(0, count, 2)})
+    first, slots, here, stored = lax.optimization_barrier(
+        (me * req_dev, (me * holder_count).astype(jnp.int32).reshape(1), me.astype(jnp.int32).reshape(1), stored)
+    )
+    slot, column = index_work(slots, stored, steps)
+
+    held = {0: hidden}
+    held.update({m: trade(hidden, m, count) for m in range(4, count, 4)})
+    _, lengths, request_page_table = lax.optimization_barrier((held[4], lengths, request_page_table))
+    cosine, sine = rotation_rows(lengths, first, req_dev, steps)
+    live = live_lanes(lengths, first, request_page_table, tokens, page_len)
+    for mask in (2, 1):
+        held.update({k ^ mask: trade(v, mask, count) for k, v in list(held.items())})
     blocks = [held[k].reshape(steps, req_dev, heads, HD).transpose(0, 2, 1, 3) for k in range(count)]
     blocks[0] = in_hbm(blocks[0])
-
-    x, low = low_of(me.astype(jnp.int32).reshape(1), blocks, slot, adapter_down_maps)
+    x, low = low_of(here, blocks, slot, adapter_down_maps)
     weight = query_key_value_weight.transpose(0, 2, 1)
     arrived = [trade(low, m, count) for m in (1, 2, 3)]
     query, key = project(0, x, weight), project(1, x, weight)
@@ -646,16 +645,13 @@
     low = (low + arrived[0]) + (arrived[1] + arrived[2])
     arrived = [trade(low, m, count) for m in range(4, count, 4)]
     base = project(2, x, weight)
-    early_heads = heads // 4
-    early_cache = cache_by_head(pool, 0, early_heads)
-    arrived, base, early_cache = lax.optimization_barrier((arrived, base, early_cache))
+    arrived, base = lax.optimization_barrier((arrived, base))
     send = update_values(column, query, key, base, adapter_up_maps.reshape(adapter_count * rank, -1), [low, *arrived])
     send, pool = lax.optimization_barrier((send, pool))
-    late_cache = cache_by_head(pool, early_heads, heads - early_heads)
+    keys, values = cache_by_head(pool, 0, heads)
     pieces = lax.all_to_all(send, "replica", split_axis=0, concat_axis=0, tiled=True)
 
-    keys, values = zip(early_cache, late_cache)
-    out = attend(cosine, sine, live, pieces, keys, values)
+    out = attend(cosine, sine, live, pieces, [keys], [values])
     return out.transpose(0, 2, 1, 3).reshape(steps, req_dev, width)
 
 

time: 59.8 us -> 52.4 us (0.88)
  starting transfers between devices: 24.9 us -> 20.6 us
  local copies, waits for them, and re-layouts: 4.44 us -> 0.62 us
  waiting for transfers between devices: 7.58 us -> 11 us
  Pallas kernels: 20.6 us -> 18 us
    ppermute x21, waiting for transfers between devices: 4.06 us -> 8.66 us  [trade(): return lax.ppermute(value, 'replica', [(i, i ^ mask) for i in range(count)])]
    unnamed x12 -> x14, local copies, waits for them, and re-layouts: 4.44 us -> 0.62 us
    ppermute x21, starting transfers between devices: 19.5 us -> 16.4 us  [trade(): return lax.ppermute(value, 'replica', [(i, i ^ mask) for i in range(count)])]
    pallas_call x2 -> x1, Pallas kernels: 9.32 us -> 6.89 us  [cache_by_head(): pl.pallas_call(functools.partial(cache_kernel, first), out_shape=(jax.Sha...]
    all_to_all x1, starting transfers between devices: 5.45 us -> 4.18 us  [chip_plan(): lax.all_to_all(send, 'replica', split_axis=0, concat_axis=0, tiled=True)]
    all_to_all x1, waiting for transfers between devices: 3.53 us -> 2.36 us  [chip_plan(): lax.all_to_all(send, 'replica', split_axis=0, concat_axis=0, tiled=True)]
  transfers between devices with their start and end apart: 22 -> 22, of which waited for: 8 -> 8; matrix products, arithmetic and copies ran while one was open for 3% -> 3% of each run, Pallas kernels for 22% -> 20%
where the time goes in v14:
time: 52.4 us; the launch traced here: 52.1 us
  starting transfers between devices  20.6 us (39%)
  Pallas kernels  18 us (34%)
  waiting for transfers between devices  11 us (21%)
  other arithmetic  1.53 us (3%)
  local copies, waits for them, and re-layouts  0.62 us (1%)
    ppermute x21, starting transfers between devices, trade(): return lax.ppermute(value, 'replica', [(i, i ^ mask) for i in range(count)])  16.4 us
    ppermute x21, waiting for transfers between devices, trade(): return lax.ppermute(value, 'replica', [(i, i ^ mask) for i in range(count)])  8.66 us
    pallas_call x1, Pallas kernels, cache_by_head(): pl.pallas_call(functools.partial(cache_kernel, first), out_shape=(jax.Sha...  6.89 us
    all_to_all x1, starting transfers between devices, chip_plan(): lax.all_to_all(send, 'replica', split_axis=0, concat_axis=0, tiled=True)  4.18 us
    pallas_call x1, Pallas kernels, attend(): pl.pallas_call(attend_kernel, out_shape=jax.ShapeDtypeStruct((steps, head...  3.85 us
    pallas_call x3, Pallas kernels, project(): pl.pallas_call(functools.partial(project_kernel, which), out_shape=chunks...  3.37 us
    all_to_all x1, waiting for transfers between devices, chip_plan(): lax.all_to_all(send, 'replica', split_axis=0, concat_axis=0, tiled=True)  2.36 us
    pallas_call x1, Pallas kernels, low_of(): pl.pallas_call(functools.partial(low_kernel, count), out_shape=(jax.Shape...  2.06 us
  transfers between devices with their start and end apart: 22, of which 8 were waited for; matrix products, arithmetic and copies ran while one was open for 3% of the time, Pallas kernels for 20%

profile of v14, /device:TPU:0, one launch (start us, length us, event | category | flops | bytes accessed | tf_op | source)
XLA Modules:
  0.0 52.1 jit_solution(17396606298267391915)
XLA Ops:
  0.0 3.0 %collective-permute-start.2 = (bf16[3,2,5120]{2,1,0:T(2,128)(2,1)}, bf16[3,2,5120]{2,1,0:T(2,128)(2,1)S(1)}, u32[]{:S(2)}, u32[]{:S(2)}) collective-permute-start(bf16[3,2,5120]{2,1,0:T(2,128)(2,1)} %param.9), channel_id=1, source_target_pairs={{0,2},{1,3},{2,0},{3,1},{4,6},{5,7},{6,4},{7,5},{8,10},{9,11},{10,... | collective-permute-start | bytes 184328 | tf_op jit(solution)/shard_map/ppermute | solution.py:258
  3.0 0.0 collective-permute-start.1
  3.0 1.6 %collective-permute-start = (bf16[3,2,5120]{2,1,0:T(2,128)(2,1)}, bf16[3,2,5120]{2,1,0:T(2,128)(2,1)S(1)}, u32[]{:S(2)}, u32[]{:S(2)}) collective-permute-start(bf16[3,2,5120]{2,1,0:T(2,128)(2,1)} %param.9), channel_id=1, source_target_pairs={{0,4},{1,5},{2,6},{3,7},{4,0},{5,1},{6,2},{7,3},{8,12},{9,13},{10,... | collective-permute-start | bytes 184328 | tf_op jit(solution)/shard_map/ppermute | solution.py:258
  4.5 2.5 %collective-permute-start.11 = (bf16[3,2,5120]{2,1,0:T(2,128)(2,1)}, bf16[3,2,5120]{2,1,0:T(2,128)(2,1)S(1)}, u32[]{:S(2)}, u32[]{:S(2)}) collective-permute-start(bf16[3,2,5120]{2,1,0:T(2,128)(2,1)} %param.9), channel_id=1, source_target_pairs={{0,12},{1,13},{2,14},{3,15},{4,8},{5,9},{6,10},{7,11},{8,4},{9,5},... | collective-permute-start | bytes 184328 | tf_op jit(solution)/shard_map/ppermute | solution.py:258
  7.0 0.1 collective-permute-start.7
  7.2 0.9 %select_reduce_fusion.1 = s32[32]{0:T(128)S(1)} fusion(s32[64]{0:T(128)} %param.13, s32[32]{0:T(128)} %param.14), kind=kLoop, calls=%fused_computation.1 | loop fusion | flops 6112 | bytes 512 | tf_op jit(solution)/shard_map/reduce_sum | solution.py:618
  8.0 0.0 slice-start
  8.0 0.0 copy-start.2
  8.0 0.0 copy-start.3
  8.1 0.0 copy-start.1
  8.1 0.0 slice-start.2
  8.1 0.2 index_work.1
  8.3 0.6 %copy-done.2 = s32[2,32]{1,0:T(2,128)S(1)} copy-done((s32[2,32]{1,0:T(2,128)S(1)}, s32[2,32]{1,0:T(2,128)}, u32[]{:S(2)}) %copy-start.2) | copy-done | bytes 280
  8.9 0.1 select_reduce_fusion
  9.0 0.6 %collective-permute-start.5 = (bf16[3,2,5120]{2,1,0:T(2,128)(2,1)S(1)}, bf16[3,2,5120]{2,1,0:T(2,128)(2,1)S(1)}, u32[]{:S(2)}, u32[]{:S(2)}) collective-permute-start(bf16[3,2,5120]{2,1,0:T(2,128)(2,1)S(1)} %collective-permute-done), channel_id=1, source_target_pairs={{0,2},{1,3},{2,0},{3,1},{4,6},{5,7},{6,4},{7,5},{8,10},{9,11},{10,... | collective-permute-start | bytes 184328 | tf_op jit(solution)/shard_map/ppermute | solution.py:258
  9.5 0.2 fusion.3
  9.7 0.1 collective-permute-start.4
  9.8 0.5 collective-permute-start.3
  10.3 0.9 %collective-permute-done.11 = bf16[3,2,5120]{2,1,0:T(2,128)(2,1)S(1)} collective-permute-done((bf16[3,2,5120]{2,1,0:T(2,128)(2,1)}, bf16[3,2,5120]{2,1,0:T(2,128)(2,1)S(1)}, u32[]{:S(2)}, u32[]{:S(2)}) %collective-permute-start.11) | collective-permute-done | bytes 61472 | tf_op jit(solution)/shard_map/ppermute | solution.py:258
  11.2 0.6 %collective-permute-start.13 = (bf16[3,2,5120]{2,1,0:T(2,128)(2,1)S(1)}, bf16[3,2,5120]{2,1,0:T(2,128)(2,1)S(1)}, u32[]{:S(2)}, u32[]{:S(2)}) collective-permute-start(bf16[3,2,5120]{2,1,0:T(2,128)(2,1)S(1)} %collective-permute-done.11), channel_id=1, source_target_pairs={{0,2},{1,3},{2,0},{3,1},{4,6},{5,7},{6,4},{7,5},{8,10},{9,11},{10,... | collective-permute-start | bytes 184328 | tf_op jit(solution)/shard_map/ppermute | solution.py:258
  11.8 1.9 %collective-permute-done.7 = bf16[3,2,5120]{2,1,0:T(2,128)(2,1)S(1)} collective-permute-done((bf16[3,2,5120]{2,1,0:T(2,128)(2,1)}, bf16[3,2,5120]{2,1,0:T(2,128)(2,1)S(1)}, u32[]{:S(2)}, u32[]{:S(2)}) %collective-permute-start.7) | collective-permute-done | bytes 61472 | tf_op jit(solution)/shard_map/ppermute | solution.py:258
  13.7 0.5 collective-permute-start.9
  14.2 0.1 and_convert_fusion.live_ref
  14.3 0.0 collective-permute-start.12
  14.3 0.5 collective-permute-start.8
  14.8 0.1 collective-permute-start.6
  14.9 0.5 collective-permute-done.13
  15.4 2.5 %collective-permute-done.9 = bf16[3,2,5120]{2,1,0:T(2,128)(2,1)S(1)} collective-permute-done((bf16[3,2,5120]{2,1,0:T(2,128)(2,1)S(1)}, bf16[3,2,5120]{2,1,0:T(2,128)(2,1)S(1)}, u32[]{:S(2)}, u32[]{:S(2)}) %collective-permute-start.9) | collective-permute-done | bytes 61472 | tf_op jit(solution)/shard_map/ppermute | solution.py:258
  17.9 0.2 select_reduce_fusion.2
  18.2 1.0 %collective-permute-done.10 = bf16[3,2,5120]{2,1,0:T(2,128)(2,1)S(1)} collective-permute-done((bf16[3,2,5120]{2,1,0:T(2,128)(2,1)S(1)}, bf16[3,2,5120]{2,1,0:T(2,128)(2,1)S(1)}, u32[]{:S(2)}, u32[]{:S(2)}) %collective-permute-start.10) | collective-permute-done | bytes 61472 | tf_op jit(solution)/shard_map/ppermute | solution.py:258
  19.2 2.1 %low_rows.1 = (bf16[3,40,16,2,128]{4,3,2,1,0:T(2,128)(2,1)S(1)}, bf16[48,128]{1,0:T(8,128)(2,1)S(1)}) custom-call(s32[1]{0:T(128)} %bitcast.1.me_ref, s32[1,96]{1,0:T(1,128)S(1)} %get-tuple-element.36.slot_ref, bf16[4,64,5120]{2,1,0:T(8,128)(2,1)S(1)} %copy-done.1, bf16[3,40,2,128]{3,2,1,0:T(2,128)(2,1)} %bitcast.82, bf16[3,40,2,128]{3,2,1,0:T(2,128)(2,1)S(1)} %bitcast.66, ...), custom_call_target="tpu_custom_call" | custom-call | flops 100000000 | bytes 4000000 | tf_op jit(solution)/shard_map/low_rows/pallas_call | solution.py:394
  21.3 0.3 collective-permute-start.17
  21.6 1.5 %collective-permute-start.16 = (bf16[48,128]{1,0:T(8,128)(2,1)S(1)}, bf16[48,128]{1,0:T(8,128)(2,1)S(1)}, u32[]{:S(2)}, u32[]{:S(2)}) collective-permute-start(bf16[48,128]{1,0:T(8,128)(2,1)S(1)} %get-tuple-element.37), channel_id=1, source_target_pairs={{0,2},{1,3},{2,0},{3,1},{4,6},{5,7},{6,4},{7,5},{8,10},{9,11},{10,... | collective-permute-start | bytes 36872 | tf_op jit(solution)/shard_map/ppermute | solution.py:258
  23.1 0.1 collective-permute-start.15
  23.2 1.1 %project.4.key_ref = bf16[3,3,16,2,128]{4,3,2,1,0:T(2,128)(2,1)S(1)} custom-call(bf16[3,40,16,2,128]{4,3,2,1,0:T(2,128)(2,1)S(1)} %get-tuple-element.38.x_ref, bf16[3,320,5120]{2,1,0:T(8,128)(2,1)S(1)} %bitcast.61), custom_call_target="tpu_custom_call" | custom-call | flops 500000000 | bytes 4000000 | tf_op jit(solution)/shard_map/project/pallas_call | solution.py:436
  24.3 1.1 %project.3.query_ref = bf16[3,3,16,2,128]{4,3,2,1,0:T(2,128)(2,1)S(1)} custom-call(bf16[3,40,16,2,128]{4,3,2,1,0:T(2,128)(2,1)S(1)} %get-tuple-element.38.x_ref, bf16[3,320,5120]{2,1,0:T(8,128)(2,1)S(1)} %bitcast.62), custom_call_target="tpu_custom_call" | custom-call | flops 500000000 | bytes 4000000 | tf_op jit(solution)/shard_map/project/pallas_call | solution.py:436
  25.5 0.0 copy-start
  25.5 2.8 %collective-permute-start.20 = (bf16[48,128]{1,0:T(8,128)(2,1)S(1)}, bf16[48,128]{1,0:T(8,128)(2,1)S(1)}, u32[]{:S(2)}, u32[]{:S(2)}) collective-permute-start(bf16[48,128]{1,0:T(8,128)(2,1)S(1)} %add_add_fusion.refs_0_), channel_id=1, source_target_pairs={{0,12},{1,13},{2,14},{3,15},{4,8},{5,9},{6,10},{7,11},{8,4},{9,5},... | collective-permute-start | bytes 36872 | tf_op jit(solution)/shard_map/ppermute | solution.py:258
  28.3 1.7 %collective-permute-start.18 = (bf16[48,128]{1,0:T(8,128)(2,1)S(1)}, bf16[48,128]{1,0:T(8,128)(2,1)S(1)}, u32[]{:S(2)}, u32[]{:S(2)}) collective-permute-start(bf16[48,128]{1,0:T(8,128)(2,1)S(1)} %add_add_fusion.refs_0_), channel_id=1, source_target_pairs={{0,4},{1,5},{2,6},{3,7},{4,0},{5,1},{6,2},{7,3},{8,12},{9,13},{10,... | collective-permute-start | bytes 36872 | tf_op jit(solution)/shard_map/ppermute | solution.py:258
  30.0 1.1 %project.5.base_ref = f32[96,320]{1,0:T(8,128)S(1)} custom-call(bf16[3,40,16,2,128]{4,3,2,1,0:T(2,128)(2,1)S(1)} %get-tuple-element.38.x_ref, bf16[3,320,5120]{2,1,0:T(8,128)(2,1)S(1)} %bitcast.63), custom_call_target="tpu_custom_call" | custom-call | flops 500000000 | bytes 4000000 | tf_op jit(solution)/shard_map/project/pallas_call | solution.py:436
  31.1 0.2 collective-permute-done.20.refs_3_
  31.3 1.6 %collective-permute-done.19.refs_2_ = bf16[48,128]{1,0:T(8,128)(2,1)S(1)} collective-permute-done((bf16[48,128]{1,0:T(8,128)(2,1)S(1)}, bf16[48,128]{1,0:T(8,128)(2,1)S(1)}, u32[]{:S(2)}, u32[]{:S(2)}) %collective-permute-start.19) | collective-permute-done | bytes 12320 | tf_op jit(solution)/shard_map/ppermute | solution.py:258
  32.9 1.6 %update_values.1 = bf16[16,9,3,2,128]{4,3,2,1,0:T(2,128)(2,1)} custom-call(s32[96,1]{1,0:T(8,128)S(1)} %get-tuple-element.34.stored_ref, bf16[3,3,16,2,128]{4,3,2,1,0:T(2,128)(2,1)S(1)} %project.3.query_ref, bf16[3,3,16,2,128]{4,3,2,1,0:T(2,128)(2,1)S(1)} %project.4.key_ref, f32[96,320]{1,0:T(8,128)S(1)} %project.5.base_ref, bf16[4096,320]{1,0:T(8,128)(2,1)S(1)} %bitcast.64, ...), custom_call_target="tpu_custom_call" | custom-call | flops 300000000 | bytes 4000000 | tf_op jit(solution)/shard_map/update_values/pallas_call | solution.py:475
  34.5 4.2 %all-to-all-start = ((bf16[16,9,3,2,128]{4,3,2,1,0:T(2,128)(2,1)}), bf16[16,9,3,2,128]{4,3,2,1,0:T(2,128)(2,1)S(1)}, u32[]{:S(2)}, u32[]{:S(2)}) async-start(bf16[16,9,3,2,128]{4,3,2,1,0:T(2,128)(2,1)} %update_values.1), calls=%async_computation | async-start | bytes 442368 | tf_op jit(solution)/shard_map/all_to_all | solution.py:652
  38.7 0.1 fusion
  38.8 6.9 %cache_by_head.1 = (bf16[40,256,128]{2,1,0:T(8,128)(2,1)S(1)}, bf16[40,256,128]{2,1,0:T(8,128)(2,1)}) custom-call(bf16[256,40,2,128]{3,2,1,0:T(2,128)(2,1)} %bitcast.81), custom_call_target="tpu_custom_call" | custom-call | bytes 12000000 | tf_op jit(solution)/shard_map/cache_by_head/pallas_call | solution.py:313
  45.7 2.4 %all-to-all-done.pieces_ref = bf16[16,9,3,2,128]{4,3,2,1,0:T(2,128)(2,1)S(1)} async-done(((bf16[16,9,3,2,128]{4,3,2,1,0:T(2,128)(2,1)}), bf16[16,9,3,2,128]{4,3,2,1,0:T(2,128)(2,1)S(1)}, u32[]{:S(2)}, u32[]{:S(2)}) %all-to-all-start) | async-done | bytes 221216 | tf_op jit(solution)/shard_map/all_to_all | solution.py:652
  48.1 3.8 %attention.1 = bf16[3,40,2,128]{3,2,1,0:T(2,128)(2,1)} custom-call(f32[8,128]{1,0:T(8,128)S(1)} %get-tuple-element.54.cos_ref, f32[8,128]{1,0:T(8,128)S(1)} %get-tuple-element.53.sin_ref, s32[2,256]{1,0:T(2,128)S(1)} %and_convert_fusion.live_ref, bf16[16,9,3,2,128]{4,3,2,1,0:T(2,128)(2,1)S(1)} %all-to-all-done.pieces_ref, ...), custom_call_target="tpu_custom_call" | custom-call | flops 1000000000 | bytes 6000000 | tf_op jit(solution)/shard_map/attention/pallas_call | solution.py:582
  (32 shorter events, 0.1 us)
Async XLA Ops:
  0.0 9.7 %collective-permute-start.2 = (bf16[3,2,5120]{2,1,0:T(2,128)(2,1)}, bf16[3,2,5120]{2,1,0:T(2,128)(2,1)S(1)}, u32[]{:S(2)}, u32[]{:S(2)}) collective-permute-start(bf16[3,2,5120]{2,1,0:T(2,128)(2,1)} %param.9), channel_id=1, source_target_pairs={{0,2},{1,3},{2,0},{3,1},{4,6},{5,7},{6,4},{7,5},{8,10},{9,11},{10,... | collective-permute-start | bytes 184328 | tf_op jit(solution)/shard_map/ppermute | solution.py:258
  3.0 6.8 %collective-permute-start.1 = (bf16[3,2,5120]{2,1,0:T(2,128)(2,1)}, bf16[3,2,5120]{2,1,0:T(2,128)(2,1)S(1)}, u32[]{:S(2)}, u32[]{:S(2)}) collective-permute-start(bf16[3,2,5120]{2,1,0:T(2,128)(2,1)} %param.9), channel_id=1, source_target_pairs={{0,1},{1,0},{2,3},{3,2},{4,5},{5,4},{6,7},{7,6},{8,9},{9,8},{10,11... | collective-permute-start | bytes 184328 | tf_op jit(solution)/shard_map/ppermute | solution.py:258
  3.0 5.3 %collective-permute-start = (bf16[3,2,5120]{2,1,0:T(2,128)(2,1)}, bf16[3,2,5120]{2,1,0:T(2,128)(2,1)S(1)}, u32[]{:S(2)}, u32[]{:S(2)}) collective-permute-start(bf16[3,2,5120]{2,1,0:T(2,128)(2,1)} %param.9), channel_id=1, source_target_pairs={{0,4},{1,5},{2,6},{3,7},{4,0},{5,1},{6,2},{7,3},{8,12},{9,13},{10,... | collective-permute-start | bytes 184328 | tf_op jit(solution)/shard_map/ppermute | solution.py:258
  4.5 6.6 %collective-permute-start.11 = (bf16[3,2,5120]{2,1,0:T(2,128)(2,1)}, bf16[3,2,5120]{2,1,0:T(2,128)(2,1)S(1)}, u32[]{:S(2)}, u32[]{:S(2)}) collective-permute-start(bf16[3,2,5120]{2,1,0:T(2,128)(2,1)} %param.9), channel_id=1, source_target_pairs={{0,12},{1,13},{2,14},{3,15},{4,8},{5,9},{6,10},{7,11},{8,4},{9,5},... | collective-permute-start | bytes 184328 | tf_op jit(solution)/shard_map/ppermute | solution.py:258
  7.0 6.7 %collective-permute-start.7 = (bf16[3,2,5120]{2,1,0:T(2,128)(2,1)}, bf16[3,2,5120]{2,1,0:T(2,128)(2,1)S(1)}, u32[]{:S(2)}, u32[]{:S(2)}) collective-permute-start(bf16[3,2,5120]{2,1,0:T(2,128)(2,1)} %param.9), channel_id=1, source_target_pairs={{0,8},{1,9},{2,10},{3,11},{4,12},{5,13},{6,14},{7,15},{8,0},{9,1},... | collective-permute-start | bytes 184328 | tf_op jit(solution)/shard_map/ppermute | solution.py:258
  8.0 15.2 %slice-start = ((s8[9830400]{0:T(1024)(128)(4,1)}), s8[4194304]{0:T(1024)(128)(4,1)S(1)}, s32[]{:S(2)}) async-start(s8[9830400]{0:T(1024)(128)(4,1)} %bitcast.59), calls=%async_computation.1 | async-start | bytes 8388608
  8.0 0.8 %copy-start.2 = (s32[2,32]{1,0:T(2,128)S(1)}, s32[2,32]{1,0:T(2,128)}, u32[]{:S(2)}) copy-start(s32[2,32]{1,0:T(2,128)} %param.16) | copy-start | bytes 772
  8.0 1.5 %copy-start.3 = (s32[32]{0:T(128)S(1)}, s32[32]{0:T(128)}, u32[]{:S(2)}) copy-start(s32[32]{0:T(128)} %param.15) | copy-start | bytes 388
  8.1 11.1 %copy-start.1 = (bf16[4,64,5120]{2,1,0:T(8,128)(2,1)S(1)}, bf16[4,64,5120]{2,1,0:T(8,128)(2,1)}, u32[]{:S(2)}) copy-start(bf16[4,64,5120]{2,1,0:T(8,128)(2,1)} %down_ref.1) | copy-start | bytes 7864324
  8.1 15.1 %slice-start.1 = ((s8[9830400]{0:T(1024)(128)(4,1)}), s8[4194304]{0:T(1024)(128)(4,1)S(1)}, s32[]{:S(2)}) async-start(s8[9830400]{0:T(1024)(128)(4,1)} %bitcast.59), calls=%async_computation.2 | async-start | bytes 8388608
  8.1 15.1 %slice-start.2 = ((s8[9830400]{0:T(1024)(128)(4,1)}), s8[1441792]{0:T(1024)(128)(4,1)S(1)}, s32[]{:S(2)}) async-start(s8[9830400]{0:T(1024)(128)(4,1)} %bitcast.59), calls=%async_computation.3 | async-start | bytes 2883584
  9.0 5.4 %collective-permute-start.5 = (bf16[3,2,5120]{2,1,0:T(2,128)(2,1)S(1)}, bf16[3,2,5120]{2,1,0:T(2,128)(2,1)S(1)}, u32[]{:S(2)}, u32[]{:S(2)}) collective-permute-start(bf16[3,2,5120]{2,1,0:T(2,128)(2,1)S(1)} %collective-permute-done), channel_id=1, source_target_pairs={{0,2},{1,3},{2,0},{3,1},{4,6},{5,7},{6,4},{7,5},{8,10},{9,11},{10,... | collective-permute-start | bytes 184328 | tf_op jit(solution)/shard_map/ppermute | solution.py:258
  9.7 5.1 %collective-permute-start.4 = (bf16[3,2,5120]{2,1,0:T(2,128)(2,1)S(1)}, bf16[3,2,5120]{2,1,0:T(2,128)(2,1)S(1)}, u32[]{:S(2)}, u32[]{:S(2)}) collective-permute-start(bf16[3,2,5120]{2,1,0:T(2,128)(2,1)S(1)} %collective-permute-done), channel_id=1, source_target_pairs={{0,1},{1,0},{2,3},{3,2},{4,5},{5,4},{6,7},{7,6},{8,9},{9,8},{10,11... | collective-permute-start | bytes 184328 | tf_op jit(solution)/shard_map/ppermute | solution.py:258
  9.8 4.5 %collective-permute-start.3 = (bf16[3,2,5120]{2,1,0:T(2,128)(2,1)S(1)}, bf16[3,2,5120]{2,1,0:T(2,128)(2,1)S(1)}, u32[]{:S(2)}, u32[]{:S(2)}) collective-permute-start(bf16[3,2,5120]{2,1,0:T(2,128)(2,1)S(1)} %collective-permute-done.2), channel_id=1, source_target_pairs={{0,1},{1,0},{2,3},{3,2},{4,5},{5,4},{6,7},{7,6},{8,9},{9,8},{10,11... | collective-permute-start | bytes 184328 | tf_op jit(solution)/shard_map/ppermute | solution.py:258
  11.2 4.2 %collective-permute-start.13 = (bf16[3,2,5120]{2,1,0:T(2,128)(2,1)S(1)}, bf16[3,2,5120]{2,1,0:T(2,128)(2,1)S(1)}, u32[]{:S(2)}, u32[]{:S(2)}) collective-permute-start(bf16[3,2,5120]{2,1,0:T(2,128)(2,1)S(1)} %collective-permute-done.11), channel_id=1, source_target_pairs={{0,2},{1,3},{2,0},{3,1},{4,6},{5,7},{6,4},{7,5},{8,10},{9,11},{10,... | collective-permute-start | bytes 184328 | tf_op jit(solution)/shard_map/ppermute | solution.py:258
  13.7 4.2 %collective-permute-start.9 = (bf16[3,2,5120]{2,1,0:T(2,128)(2,1)S(1)}, bf16[3,2,5120]{2,1,0:T(2,128)(2,1)S(1)}, u32[]{:S(2)}, u32[]{:S(2)}) collective-permute-start(bf16[3,2,5120]{2,1,0:T(2,128)(2,1)S(1)} %collective-permute-done.7), channel_id=1, source_target_pairs={{0,2},{1,3},{2,0},{3,1},{4,6},{5,7},{6,4},{7,5},{8,10},{9,11},{10,... | collective-permute-start | bytes 184328 | tf_op jit(solution)/shard_map/ppermute | solution.py:258
  14.3 3.8 %collective-permute-start.12 = (bf16[3,2,5120]{2,1,0:T(2,128)(2,1)S(1)}, bf16[3,2,5120]{2,1,0:T(2,128)(2,1)S(1)}, u32[]{:S(2)}, u32[]{:S(2)}) collective-permute-start(bf16[3,2,5120]{2,1,0:T(2,128)(2,1)S(1)} %collective-permute-done.11), channel_id=1, source_target_pairs={{0,1},{1,0},{2,3},{3,2},{4,5},{5,4},{6,7},{7,6},{8,9},{9,8},{10,11... | collective-permute-start | bytes 184328 | tf_op jit(solution)/shard_map/ppermute | solution.py:258
  14.3 3.8 %collective-permute-start.8 = (bf16[3,2,5120]{2,1,0:T(2,128)(2,1)S(1)}, bf16[3,2,5120]{2,1,0:T(2,128)(2,1)S(1)}, u32[]{:S(2)}, u32[]{:S(2)}) collective-permute-start(bf16[3,2,5120]{2,1,0:T(2,128)(2,1)S(1)} %collective-permute-done.7), channel_id=1, source_target_pairs={{0,1},{1,0},{2,3},{3,2},{4,5},{5,4},{6,7},{7,6},{8,9},{9,8},{10,11... | collective-permute-start | bytes 184328 | tf_op jit(solution)/shard_map/ppermute | solution.py:258
  14.8 3.3 %collective-permute-start.6 = (bf16[3,2,5120]{2,1,0:T(2,128)(2,1)S(1)}, bf16[3,2,5120]{2,1,0:T(2,128)(2,1)S(1)}, u32[]{:S(2)}, u32[]{:S(2)}) collective-permute-start(bf16[3,2,5120]{2,1,0:T(2,128)(2,1)S(1)} %collective-permute-done.5), channel_id=1, source_target_pairs={{0,1},{1,0},{2,3},{3,2},{4,5},{5,4},{6,7},{7,6},{8,9},{9,8},{10,11... | collective-permute-start | bytes 184328 | tf_op jit(solution)/shard_map/ppermute | solution.py:258
  15.4 2.7 %collective-permute-start.14 = (bf16[3,2,5120]{2,1,0:T(2,128)(2,1)S(1)}, bf16[3,2,5120]{2,1,0:T(2,128)(2,1)S(1)}, u32[]{:S(2)}, u32[]{:S(2)}) collective-permute-start(bf16[3,2,5120]{2,1,0:T(2,128)(2,1)S(1)} %collective-permute-done.13), channel_id=1, source_target_pairs={{0,1},{1,0},{2,3},{3,2},{4,5},{5,4},{6,7},{7,6},{8,9},{9,8},{10,11... | collective-permute-start | bytes 184328 | tf_op jit(solution)/shard_map/ppermute | solution.py:258
  17.9 1.2 %collective-permute-start.10 = (bf16[3,2,5120]{2,1,0:T(2,128)(2,1)S(1)}, bf16[3,2,5120]{2,1,0:T(2,128)(2,1)S(1)}, u32[]{:S(2)}, u32[]{:S(2)}) collective-permute-start(bf16[3,2,5120]{2,1,0:T(2,128)(2,1)S(1)} %collective-permute-done.9), channel_id=1, source_target_pairs={{0,1},{1,0},{2,3},{3,2},{4,5},{5,4},{6,7},{7,6},{8,9},{9,8},{10,11... | collective-permute-start | bytes 184328 | tf_op jit(solution)/shard_map/ppermute | solution.py:258
  21.3 4.2 %collective-permute-start.17 = (bf16[48,128]{1,0:T(8,128)(2,1)S(1)}, bf16[48,128]{1,0:T(8,128)(2,1)S(1)}, u32[]{:S(2)}, u32[]{:S(2)}) collective-permute-start(bf16[48,128]{1,0:T(8,128)(2,1)S(1)} %get-tuple-element.37), channel_id=1, source_target_pairs={{0,3},{1,2},{2,1},{3,0},{4,7},{5,6},{6,5},{7,4},{8,11},{9,10},{10,... | collective-permute-start | bytes 36872 | tf_op jit(solution)/shard_map/ppermute | solution.py:258
  21.6 3.9 %collective-permute-start.16 = (bf16[48,128]{1,0:T(8,128)(2,1)S(1)}, bf16[48,128]{1,0:T(8,128)(2,1)S(1)}, u32[]{:S(2)}, u32[]{:S(2)}) collective-permute-start(bf16[48,128]{1,0:T(8,128)(2,1)S(1)} %get-tuple-element.37), channel_id=1, source_target_pairs={{0,2},{1,3},{2,0},{3,1},{4,6},{5,7},{6,4},{7,5},{8,10},{9,11},{10,... | collective-permute-start | bytes 36872 | tf_op jit(solution)/shard_map/ppermute | solution.py:258
  23.1 2.4 %collective-permute-start.15 = (bf16[48,128]{1,0:T(8,128)(2,1)S(1)}, bf16[48,128]{1,0:T(8,128)(2,1)S(1)}, u32[]{:S(2)}, u32[]{:S(2)}) collective-permute-start(bf16[48,128]{1,0:T(8,128)(2,1)S(1)} %get-tuple-element.37), channel_id=1, source_target_pairs={{0,1},{1,0},{2,3},{3,2},{4,5},{5,4},{6,7},{7,6},{8,9},{9,8},{10,11... | collective-permute-start | bytes 36872 | tf_op jit(solution)/shard_map/ppermute | solution.py:258
  25.5 7.4 %copy-start = (bf16[64,64,320]{2,1,0:T(8,128)(2,1)S(1)}, bf16[64,64,320]{2,1,0:T(8,128)(2,1)}, u32[]{:S(2)}) copy-start(bf16[64,64,320]{2,1,0:T(8,128)(2,1)} %param.12) | copy-start | bytes 7864324
  25.5 5.7 %collective-permute-start.20 = (bf16[48,128]{1,0:T(8,128)(2,1)S(1)}, bf16[48,128]{1,0:T(8,128)(2,1)S(1)}, u32[]{:S(2)}, u32[]{:S(2)}) collective-permute-start(bf16[48,128]{1,0:T(8,128)(2,1)S(1)} %add_add_fusion.refs_0_), channel_id=1, source_target_pairs={{0,12},{1,13},{2,14},{3,15},{4,8},{5,9},{6,10},{7,11},{8,4},{9,5},... | collective-permute-start | bytes 36872 | tf_op jit(solution)/shard_map/ppermute | solution.py:258
  28.3 4.6 %collective-permute-start.19 = (bf16[48,128]{1,0:T(8,128)(2,1)S(1)}, bf16[48,128]{1,0:T(8,128)(2,1)S(1)}, u32[]{:S(2)}, u32[]{:S(2)}) collective-permute-start(bf16[48,128]{1,0:T(8,128)(2,1)S(1)} %add_add_fusion.refs_0_), channel_id=1, source_target_pairs={{0,8},{1,9},{2,10},{3,11},{4,12},{5,13},{6,14},{7,15},{8,0},{9,1},... | collective-permute-start | bytes 36872 | tf_op jit(solution)/shard_map/ppermute | solution.py:258
  28.3 4.6 %collective-permute-start.18 = (bf16[48,128]{1,0:T(8,128)(2,1)S(1)}, bf16[48,128]{1,0:T(8,128)(2,1)S(1)}, u32[]{:S(2)}, u32[]{:S(2)}) collective-permute-start(bf16[48,128]{1,0:T(8,128)(2,1)S(1)} %add_add_fusion.refs_0_), channel_id=1, source_target_pairs={{0,4},{1,5},{2,6},{3,7},{4,0},{5,1},{6,2},{7,3},{8,12},{9,13},{10,... | collective-permute-start | bytes 36872 | tf_op jit(solution)/shard_map/ppermute | solution.py:258
  34.5 13.6 %all-to-all-start = ((bf16[16,9,3,2,128]{4,3,2,1,0:T(2,128)(2,1)}), bf16[16,9,3,2,128]{4,3,2,1,0:T(2,128)(2,1)S(1)}, u32[]{:S(2)}, u32[]{:S(2)}) async-start(bf16[16,9,3,2,128]{4,3,2,1,0:T(2,128)(2,1)} %update_values.1), calls=%async_computation | async-start | bytes 442368 | tf_op jit(solution)/shard_map/all_to_all | solution.py:652

commit v15 on v14

--- a/solution.py
+++ b/solution.py
@@ -283,11 +283,13 @@
 
 
 CACHE_SECTION = 10
+CACHE_AHEAD = 2
 
 
 def cache_kernel(first, pool_ref, keys_ref, values_ref, raw, values, sem, out_sem):
     heads, tokens = raw.shape[:2]
-    copies = start_all([pltpu.make_async_copy(pool_ref.at[:, first + h], raw.at[h], sem.at[h]) for h in range(heads)])
+    copies = [pltpu.make_async_copy(pool_ref.at[:, first + h], raw.at[h], sem.at[h]) for h in range(heads)]
+    start_all(copies[: CACHE_AHEAD * CACHE_SECTION])
     rows = raw.reshape(heads, 2 * tokens, HD)
     to = lax.broadcasted_iota(jnp.int32, (2 * tokens, 2 * tokens), 0)
     source = lax.broadcasted_iota(jnp.int32, (2 * tokens, 2 * tokens), 1)
@@ -297,6 +299,7 @@
     part = CACHE_SECTION
     for p in range(heads // part):
         wait_all(copies[p * part : (p + 1) * part])
+        start_all(copies[(p + CACHE_AHEAD) * part : (p + CACHE_AHEAD + 1) * part])
         for h in range(p * part, (p + 1) * part, 2):
             both = jnp.concatenate([rows[h], rows[h + 1]], axis=1)
             made = jnp.dot(pick, both, preferred_element_type=jnp.float32).astype(jnp.bfloat16)
@@ -633,8 +636,10 @@
     _, lengths, request_page_table = lax.optimization_barrier((held[4], lengths, request_page_table))
     cosine, sine = rotation_rows(lengths, first, req_dev, steps)
     live = live_lanes(lengths, first, request_page_table, tokens, page_len)
-    for mask in (2, 1):
-        held.update({k ^ mask: trade(v, mask, count) for k, v in list(held.items())})
+    held.update({k | 2: trade(v, 2, count) for k, v in list(held.items())})
+    ready = [0, 2, 4, 6]
+    held.update(zip(ready, lax.optimization_barrier([held[k] for k in ready])))
+    held.update({k | 1: trade(v, 1, count) for k, v in list(held.items())})
     blocks = [held[k].reshape(steps, req_dev, heads, HD).transpose(0, 2, 1, 3) for k in range(count)]
     blocks[0] = in_hbm(blocks[0])
     x, low = low_of(here, blocks, slot, adapter_down_maps)

time: 52.4 us -> 52 us (level)
  local copies, waits for them, and re-layouts: 0.62 us -> 0.05 us
    unnamed x14 -> x16, local copies, waits for them, and re-layouts: 0.62 us -> 0.05 us
  transfers between devices with their start and end apart: 22 -> 22, of which waited for: 8 -> 9; matrix products, arithmetic and copies ran while one was open for 3% -> 3% of each run, Pallas kernels for 20% -> 20%
where the time goes in v15:
time: 52 us; the launch traced here: 51.7 us
  starting transfers between devices  20.9 us (40%)
  Pallas kernels  18 us (35%)
  waiting for transfers between devices  10.8 us (21%)
  other arithmetic  1.53 us (3%)
    ppermute x21, starting transfers between devices, trade(): return lax.ppermute(value, 'replica', [(i, i ^ mask) for i in range(count)])  16.8 us
    ppermute x21, waiting for transfers between devices, trade(): return lax.ppermute(value, 'replica', [(i, i ^ mask) for i in range(count)])  8.49 us
    pallas_call x1, Pallas kernels, cache_by_head(): pl.pallas_call(functools.partial(cache_kernel, first), out_shape=(jax.Sha...  6.9 us
    all_to_all x1, starting transfers between devices, chip_plan(): lax.all_to_all(send, 'replica', split_axis=0, concat_axis=0, tiled=True)  4.18 us
    pallas_call x1, Pallas kernels, attend(): pl.pallas_call(attend_kernel, out_shape=jax.ShapeDtypeStruct((steps, head...  3.85 us
    pallas_call x3, Pallas kernels, project(): pl.pallas_call(functools.partial(project_kernel, which), out_shape=chunks...  3.35 us
    all_to_all x1, waiting for transfers between devices, chip_plan(): lax.all_to_all(send, 'replica', split_axis=0, concat_axis=0, tiled=True)  2.35 us
    pallas_call x1, Pallas kernels, low_of(): pl.pallas_call(functools.partial(low_kernel, count), out_shape=(jax.Shape...  2.06 us
  transfers between devices with their start and end apart: 22, of which 9 were waited for; matrix products, arithmetic and copies ran while one was open for 3% of the time, Pallas kernels for 20%

profile of v15, /device:TPU:0, one launch (start us, length us, event | category | flops | bytes accessed | tf_op | source)
XLA Modules:
  0.0 51.7 jit_solution(12670242054522172080)
XLA Ops:
  0.0 3.0 %collective-permute-start.1 = (bf16[3,2,5120]{2,1,0:T(2,128)(2,1)}, bf16[3,2,5120]{2,1,0:T(2,128)(2,1)S(1)}, u32[]{:S(2)}, u32[]{:S(2)}) collective-permute-start(bf16[3,2,5120]{2,1,0:T(2,128)(2,1)} %param.9), channel_id=1, source_target_pairs={{0,2},{1,3},{2,0},{3,1},{4,6},{5,7},{6,4},{7,5},{8,10},{9,11},{10,... | collective-permute-start | bytes 184328 | tf_op jit(solution)/shard_map/ppermute | solution.py:258
  3.0 1.6 %collective-permute-start = (bf16[3,2,5120]{2,1,0:T(2,128)(2,1)}, bf16[3,2,5120]{2,1,0:T(2,128)(2,1)S(1)}, u32[]{:S(2)}, u32[]{:S(2)}) collective-permute-start(bf16[3,2,5120]{2,1,0:T(2,128)(2,1)} %param.9), channel_id=1, source_target_pairs={{0,4},{1,5},{2,6},{3,7},{4,0},{5,1},{6,2},{7,3},{8,12},{9,13},{10,... | collective-permute-start | bytes 184328 | tf_op jit(solution)/shard_map/ppermute | solution.py:258
  4.5 2.5 %collective-permute-start.11 = (bf16[3,2,5120]{2,1,0:T(2,128)(2,1)}, bf16[3,2,5120]{2,1,0:T(2,128)(2,1)S(1)}, u32[]{:S(2)}, u32[]{:S(2)}) collective-permute-start(bf16[3,2,5120]{2,1,0:T(2,128)(2,1)} %param.9), channel_id=1, source_target_pairs={{0,12},{1,13},{2,14},{3,15},{4,8},{5,9},{6,10},{7,11},{8,4},{9,5},... | collective-permute-start | bytes 184328 | tf_op jit(solution)/shard_map/ppermute | solution.py:258
  7.0 0.1 collective-permute-start.7
  7.2 0.9 %select_reduce_fusion.1 = s32[32]{0:T(128)S(1)} fusion(s32[64]{0:T(128)} %param.13, s32[32]{0:T(128)} %param.14), kind=kLoop, calls=%fused_computation.1 | loop fusion | flops 6112 | bytes 512 | tf_op jit(solution)/shard_map/reduce_sum | solution.py:621
  8.0 0.0 slice-start
  8.0 0.0 copy-start.3
  8.0 0.0 copy-start.4
  8.1 0.0 copy-start.2
  8.1 0.0 copy-start.1
  8.1 0.2 index_work.1
  8.3 0.6 %collective-permute-start.2 = (bf16[3,2,5120]{2,1,0:T(2,128)(2,1)S(1)}, bf16[3,2,5120]{2,1,0:T(2,128)(2,1)S(1)}, u32[]{:S(2)}, u32[]{:S(2)}) collective-permute-start(bf16[3,2,5120]{2,1,0:T(2,128)(2,1)S(1)} %collective-permute-done), channel_id=1, source_target_pairs={{0,2},{1,3},{2,0},{3,1},{4,6},{5,7},{6,4},{7,5},{8,10},{9,11},{10,... | collective-permute-start | bytes 184328 | tf_op jit(solution)/shard_map/ppermute | solution.py:258
  8.9 2.4 %collective-permute-done.11 = bf16[3,2,5120]{2,1,0:T(2,128)(2,1)S(1)} collective-permute-done((bf16[3,2,5120]{2,1,0:T(2,128)(2,1)}, bf16[3,2,5120]{2,1,0:T(2,128)(2,1)S(1)}, u32[]{:S(2)}, u32[]{:S(2)}) %collective-permute-start.11) | collective-permute-done | bytes 61472 | tf_op jit(solution)/shard_map/ppermute | solution.py:258
  11.3 0.5 collective-permute-start.13
  11.8 0.1 select_reduce_fusion
  11.9 1.3 %collective-permute-done.7 = bf16[3,2,5120]{2,1,0:T(2,128)(2,1)S(1)} collective-permute-done((bf16[3,2,5120]{2,1,0:T(2,128)(2,1)}, bf16[3,2,5120]{2,1,0:T(2,128)(2,1)S(1)}, u32[]{:S(2)}, u32[]{:S(2)}) %collective-permute-start.7) | collective-permute-done | bytes 61472 | tf_op jit(solution)/shard_map/ppermute | solution.py:258
  13.2 0.5 collective-permute-start.9
  13.7 0.2 fusion.3
  13.8 0.1 collective-permute-start.8
  13.9 0.5 collective-permute-start.3
  14.4 0.1 and_convert_fusion.live_ref
  14.5 1.4 %collective-permute-done.13 = bf16[3,2,5120]{2,1,0:T(2,128)(2,1)S(1)} collective-permute-done((bf16[3,2,5120]{2,1,0:T(2,128)(2,1)S(1)}, bf16[3,2,5120]{2,1,0:T(2,128)(2,1)S(1)}, u32[]{:S(2)}, u32[]{:S(2)}) %collective-permute-start.13) | collective-permute-done | bytes 61472 | tf_op jit(solution)/shard_map/ppermute | solution.py:258
  15.9 0.5 collective-permute-start.5
  16.4 0.9 %collective-permute-done.9 = bf16[3,2,5120]{2,1,0:T(2,128)(2,1)S(1)} collective-permute-done((bf16[3,2,5120]{2,1,0:T(2,128)(2,1)S(1)}, bf16[3,2,5120]{2,1,0:T(2,128)(2,1)S(1)}, u32[]{:S(2)}, u32[]{:S(2)}) %collective-permute-start.9) | collective-permute-done | bytes 61472 | tf_op jit(solution)/shard_map/ppermute | solution.py:258
  17.4 0.5 collective-permute-start.14
  17.9 0.1 collective-permute-start.10
  18.0 0.2 select_reduce_fusion.2
  18.2 0.5 collective-permute-done.6
  18.6 0.2 collective-permute-done.14
  18.8 0.4 collective-permute-done.10
  19.1 2.1 %low_rows.1 = (bf16[3,40,16,2,128]{4,3,2,1,0:T(2,128)(2,1)S(1)}, bf16[48,128]{1,0:T(8,128)(2,1)S(1)}) custom-call(s32[1]{0:T(128)} %bitcast.1.me_ref, s32[1,96]{1,0:T(1,128)S(1)} %get-tuple-element.40.slot_ref, bf16[4,64,5120]{2,1,0:T(8,128)(2,1)S(1)} %copy-done.1, bf16[3,40,2,128]{3,2,1,0:T(2,128)(2,1)} %bitcast.82, bf16[3,40,2,128]{3,2,1,0:T(2,128)(2,1)S(1)} %bitcast.74, ...), custom_call_target="tpu_custom_call" | custom-call | flops 100000000 | bytes 4000000 | tf_op jit(solution)/shard_map/low_rows/pallas_call | solution.py:397
  21.2 0.3 collective-permute-start.17
  21.5 1.5 %collective-permute-start.16 = (bf16[48,128]{1,0:T(8,128)(2,1)S(1)}, bf16[48,128]{1,0:T(8,128)(2,1)S(1)}, u32[]{:S(2)}, u32[]{:S(2)}) collective-permute-start(bf16[48,128]{1,0:T(8,128)(2,1)S(1)} %get-tuple-element.45), channel_id=1, source_target_pairs={{0,2},{1,3},{2,0},{3,1},{4,6},{5,7},{6,4},{7,5},{8,10},{9,11},{10,... | collective-permute-start | bytes 36872 | tf_op jit(solution)/shard_map/ppermute | solution.py:258
  23.1 0.1 collective-permute-start.15
  23.2 1.1 %project.4.key_ref = bf16[3,3,16,2,128]{4,3,2,1,0:T(2,128)(2,1)S(1)} custom-call(bf16[3,40,16,2,128]{4,3,2,1,0:T(2,128)(2,1)S(1)} %get-tuple-element.46.x_ref, bf16[3,320,5120]{2,1,0:T(8,128)(2,1)S(1)} %bitcast.61), custom_call_target="tpu_custom_call" | custom-call | flops 500000000 | bytes 4000000 | tf_op jit(solution)/shard_map/project/pallas_call | solution.py:439
  24.3 1.1 %project.3.query_ref = bf16[3,3,16,2,128]{4,3,2,1,0:T(2,128)(2,1)S(1)} custom-call(bf16[3,40,16,2,128]{4,3,2,1,0:T(2,128)(2,1)S(1)} %get-tuple-element.46.x_ref, bf16[3,320,5120]{2,1,0:T(8,128)(2,1)S(1)} %bitcast.62), custom_call_target="tpu_custom_call" | custom-call | flops 500000000 | bytes 4000000 | tf_op jit(solution)/shard_map/project/pallas_call | solution.py:439
  25.4 0.0 copy-start
  25.5 2.4 %collective-permute-start.20 = (bf16[48,128]{1,0:T(8,128)(2,1)S(1)}, bf16[48,128]{1,0:T(8,128)(2,1)S(1)}, u32[]{:S(2)}, u32[]{:S(2)}) collective-permute-start(bf16[48,128]{1,0:T(8,128)(2,1)S(1)} %add_add_fusion.refs_0_), channel_id=1, source_target_pairs={{0,12},{1,13},{2,14},{3,15},{4,8},{5,9},{6,10},{7,11},{8,4},{9,5},... | collective-permute-start | bytes 36872 | tf_op jit(solution)/shard_map/ppermute | solution.py:258
  27.9 0.2 collective-permute-start.19
  28.1 1.8 %collective-permute-start.18 = (bf16[48,128]{1,0:T(8,128)(2,1)S(1)}, bf16[48,128]{1,0:T(8,128)(2,1)S(1)}, u32[]{:S(2)}, u32[]{:S(2)}) collective-permute-start(bf16[48,128]{1,0:T(8,128)(2,1)S(1)} %add_add_fusion.refs_0_), channel_id=1, source_target_pairs={{0,4},{1,5},{2,6},{3,7},{4,0},{5,1},{6,2},{7,3},{8,12},{9,13},{10,... | collective-permute-start | bytes 36872 | tf_op jit(solution)/shard_map/ppermute | solution.py:258
  29.9 1.1 %project.5.base_ref = f32[96,320]{1,0:T(8,128)S(1)} custom-call(bf16[3,40,16,2,128]{4,3,2,1,0:T(2,128)(2,1)S(1)} %get-tuple-element.46.x_ref, bf16[3,320,5120]{2,1,0:T(8,128)(2,1)S(1)} %bitcast.63), custom_call_target="tpu_custom_call" | custom-call | flops 500000000 | bytes 4000000 | tf_op jit(solution)/shard_map/project/pallas_call | solution.py:439
  31.0 1.4 %collective-permute-done.19.refs_2_ = bf16[48,128]{1,0:T(8,128)(2,1)S(1)} collective-permute-done((bf16[48,128]{1,0:T(8,128)(2,1)S(1)}, bf16[48,128]{1,0:T(8,128)(2,1)S(1)}, u32[]{:S(2)}, u32[]{:S(2)}) %collective-permute-start.19) | collective-permute-done | bytes 12320 | tf_op jit(solution)/shard_map/ppermute | solution.py:258
  32.5 1.6 %update_values.1 = bf16[16,9,3,2,128]{4,3,2,1,0:T(2,128)(2,1)} custom-call(s32[96,1]{1,0:T(8,128)S(1)} %get-tuple-element.38.stored_ref, bf16[3,3,16,2,128]{4,3,2,1,0:T(2,128)(2,1)S(1)} %project.3.query_ref, bf16[3,3,16,2,128]{4,3,2,1,0:T(2,128)(2,1)S(1)} %project.4.key_ref, f32[96,320]{1,0:T(8,128)S(1)} %project.5.base_ref, bf16[4096,320]{1,0:T(8,128)(2,1)S(1)} %bitcast.64, ...), custom_call_target="tpu_custom_call" | custom-call | flops 300000000 | bytes 4000000 | tf_op jit(solution)/shard_map/update_values/pallas_call | solution.py:478
  34.1 4.2 %all-to-all-start = ((bf16[16,9,3,2,128]{4,3,2,1,0:T(2,128)(2,1)}), bf16[16,9,3,2,128]{4,3,2,1,0:T(2,128)(2,1)S(1)}, u32[]{:S(2)}, u32[]{:S(2)}) async-start(bf16[16,9,3,2,128]{4,3,2,1,0:T(2,128)(2,1)} %update_values.1), calls=%async_computation | async-start | bytes 442368 | tf_op jit(solution)/shard_map/all_to_all | solution.py:657
  38.3 0.1 fusion
  38.4 6.9 %cache_by_head.1 = (bf16[40,256,128]{2,1,0:T(8,128)(2,1)S(1)}, bf16[40,256,128]{2,1,0:T(8,128)(2,1)}) custom-call(bf16[256,40,2,128]{3,2,1,0:T(2,128)(2,1)} %bitcast.81), custom_call_target="tpu_custom_call" | custom-call | bytes 12000000 | tf_op jit(solution)/shard_map/cache_by_head/pallas_call | solution.py:316
  45.4 2.4 %all-to-all-done.pieces_ref = bf16[16,9,3,2,128]{4,3,2,1,0:T(2,128)(2,1)S(1)} async-done(((bf16[16,9,3,2,128]{4,3,2,1,0:T(2,128)(2,1)}), bf16[16,9,3,2,128]{4,3,2,1,0:T(2,128)(2,1)S(1)}, u32[]{:S(2)}, u32[]{:S(2)}) %all-to-all-start) | async-done | bytes 221216 | tf_op jit(solution)/shard_map/all_to_all | solution.py:657
  47.7 3.8 %attention.1 = bf16[3,40,2,128]{3,2,1,0:T(2,128)(2,1)} custom-call(f32[8,128]{1,0:T(8,128)S(1)} %get-tuple-element.62.cos_ref, f32[8,128]{1,0:T(8,128)S(1)} %get-tuple-element.61.sin_ref, s32[2,256]{1,0:T(2,128)S(1)} %and_convert_fusion.live_ref, bf16[16,9,3,2,128]{4,3,2,1,0:T(2,128)(2,1)S(1)} %all-to-all-done.pieces_ref, ...), custom_call_target="tpu_custom_call" | custom-call | flops 1000000000 | bytes 6000000 | tf_op jit(solution)/shard_map/attention/pallas_call | solution.py:585
  (34 shorter events, 0.1 us)
Async XLA Ops:
  0.0 13.8 %collective-permute-start.1 = (bf16[3,2,5120]{2,1,0:T(2,128)(2,1)}, bf16[3,2,5120]{2,1,0:T(2,128)(2,1)S(1)}, u32[]{:S(2)}, u32[]{:S(2)}) collective-permute-start(bf16[3,2,5120]{2,1,0:T(2,128)(2,1)} %param.9), channel_id=1, source_target_pairs={{0,2},{1,3},{2,0},{3,1},{4,6},{5,7},{6,4},{7,5},{8,10},{9,11},{10,... | collective-permute-start | bytes 184328 | tf_op jit(solution)/shard_map/ppermute | solution.py:258
  3.0 5.3 %collective-permute-start = (bf16[3,2,5120]{2,1,0:T(2,128)(2,1)}, bf16[3,2,5120]{2,1,0:T(2,128)(2,1)S(1)}, u32[]{:S(2)}, u32[]{:S(2)}) collective-permute-start(bf16[3,2,5120]{2,1,0:T(2,128)(2,1)} %param.9), channel_id=1, source_target_pairs={{0,4},{1,5},{2,6},{3,7},{4,0},{5,1},{6,2},{7,3},{8,12},{9,13},{10,... | collective-permute-start | bytes 184328 | tf_op jit(solution)/shard_map/ppermute | solution.py:258
  4.5 6.7 %collective-permute-start.11 = (bf16[3,2,5120]{2,1,0:T(2,128)(2,1)}, bf16[3,2,5120]{2,1,0:T(2,128)(2,1)S(1)}, u32[]{:S(2)}, u32[]{:S(2)}) collective-permute-start(bf16[3,2,5120]{2,1,0:T(2,128)(2,1)} %param.9), channel_id=1, source_target_pairs={{0,12},{1,13},{2,14},{3,15},{4,8},{5,9},{6,10},{7,11},{8,4},{9,5},... | collective-permute-start | bytes 184328 | tf_op jit(solution)/shard_map/ppermute | solution.py:258
  7.0 6.1 %collective-permute-start.7 = (bf16[3,2,5120]{2,1,0:T(2,128)(2,1)}, bf16[3,2,5120]{2,1,0:T(2,128)(2,1)S(1)}, u32[]{:S(2)}, u32[]{:S(2)}) collective-permute-start(bf16[3,2,5120]{2,1,0:T(2,128)(2,1)} %param.9), channel_id=1, source_target_pairs={{0,8},{1,9},{2,10},{3,11},{4,12},{5,13},{6,14},{7,15},{8,0},{9,1},... | collective-permute-start | bytes 184328 | tf_op jit(solution)/shard_map/ppermute | solution.py:258
  8.0 15.1 %slice-start = ((s8[9830400]{0:T(1024)(128)(4,1)}), s8[4194304]{0:T(1024)(128)(4,1)S(1)}, s32[]{:S(2)}) async-start(s8[9830400]{0:T(1024)(128)(4,1)} %bitcast.59), calls=%async_computation.1 | async-start | bytes 8388608
  8.0 3.7 %copy-start.3 = (s32[2,32]{1,0:T(2,128)S(1)}, s32[2,32]{1,0:T(2,128)}, u32[]{:S(2)}) copy-start(s32[2,32]{1,0:T(2,128)} %param.16) | copy-start | bytes 772
  8.0 5.6 %copy-start.4 = (s32[32]{0:T(128)S(1)}, s32[32]{0:T(128)}, u32[]{:S(2)}) copy-start(s32[32]{0:T(128)} %param.15) | copy-start | bytes 388
  8.1 5.9 %copy-start.2 = (bf16[3,2,5120]{2,1,0:T(2,128)(2,1)S(1)}, bf16[3,2,5120]{2,1,0:T(2,128)(2,1)}, u32[]{:S(2)}) copy-start(bf16[3,2,5120]{2,1,0:T(2,128)(2,1)} %param.9) | copy-start | bytes 184324
  8.1 11.1 %copy-start.1 = (bf16[4,64,5120]{2,1,0:T(8,128)(2,1)S(1)}, bf16[4,64,5120]{2,1,0:T(8,128)(2,1)}, u32[]{:S(2)}) copy-start(bf16[4,64,5120]{2,1,0:T(8,128)(2,1)} %down_ref.1) | copy-start | bytes 7864324
  8.1 15.1 %slice-start.1 = ((s8[9830400]{0:T(1024)(128)(4,1)}), s8[4194304]{0:T(1024)(128)(4,1)S(1)}, s32[]{:S(2)}) async-start(s8[9830400]{0:T(1024)(128)(4,1)} %bitcast.59), calls=%async_computation.2 | async-start | bytes 8388608
  8.1 15.1 %slice-start.2 = ((s8[9830400]{0:T(1024)(128)(4,1)}), s8[1441792]{0:T(1024)(128)(4,1)S(1)}, s32[]{:S(2)}) async-start(s8[9830400]{0:T(1024)(128)(4,1)} %bitcast.59), calls=%async_computation.3 | async-start | bytes 2883584
  8.3 5.6 %collective-permute-start.2 = (bf16[3,2,5120]{2,1,0:T(2,128)(2,1)S(1)}, bf16[3,2,5120]{2,1,0:T(2,128)(2,1)S(1)}, u32[]{:S(2)}, u32[]{:S(2)}) collective-permute-start(bf16[3,2,5120]{2,1,0:T(2,128)(2,1)S(1)} %collective-permute-done), channel_id=1, source_target_pairs={{0,2},{1,3},{2,0},{3,1},{4,6},{5,7},{6,4},{7,5},{8,10},{9,11},{10,... | collective-permute-start | bytes 184328 | tf_op jit(solution)/shard_map/ppermute | solution.py:258
  11.3 4.7 %collective-permute-start.13 = (bf16[3,2,5120]{2,1,0:T(2,128)(2,1)S(1)}, bf16[3,2,5120]{2,1,0:T(2,128)(2,1)S(1)}, u32[]{:S(2)}, u32[]{:S(2)}) collective-permute-start(bf16[3,2,5120]{2,1,0:T(2,128)(2,1)S(1)} %collective-permute-done.11), channel_id=1, source_target_pairs={{0,2},{1,3},{2,0},{3,1},{4,6},{5,7},{6,4},{7,5},{8,10},{9,11},{10,... | collective-permute-start | bytes 184328 | tf_op jit(solution)/shard_map/ppermute | solution.py:258
  11.8 4.2 %collective-permute-start.12 = (bf16[3,2,5120]{2,1,0:T(2,128)(2,1)S(1)}, bf16[3,2,5120]{2,1,0:T(2,128)(2,1)S(1)}, u32[]{:S(2)}, u32[]{:S(2)}) collective-permute-start(bf16[3,2,5120]{2,1,0:T(2,128)(2,1)S(1)} %collective-permute-done.11), channel_id=1, source_target_pairs={{0,1},{1,0},{2,3},{3,2},{4,5},{5,4},{6,7},{7,6},{8,9},{9,8},{10,11... | collective-permute-start | bytes 184328 | tf_op jit(solution)/shard_map/ppermute | solution.py:258
  13.2 4.2 %collective-permute-start.9 = (bf16[3,2,5120]{2,1,0:T(2,128)(2,1)S(1)}, bf16[3,2,5120]{2,1,0:T(2,128)(2,1)S(1)}, u32[]{:S(2)}, u32[]{:S(2)}) collective-permute-start(bf16[3,2,5120]{2,1,0:T(2,128)(2,1)S(1)} %collective-permute-done.7), channel_id=1, source_target_pairs={{0,2},{1,3},{2,0},{3,1},{4,6},{5,7},{6,4},{7,5},{8,10},{9,11},{10,... | collective-permute-start | bytes 184328 | tf_op jit(solution)/shard_map/ppermute | solution.py:258
  13.8 3.5 %collective-permute-start.8 = (bf16[3,2,5120]{2,1,0:T(2,128)(2,1)S(1)}, bf16[3,2,5120]{2,1,0:T(2,128)(2,1)S(1)}, u32[]{:S(2)}, u32[]{:S(2)}) collective-permute-start(bf16[3,2,5120]{2,1,0:T(2,128)(2,1)S(1)} %collective-permute-done.7), channel_id=1, source_target_pairs={{0,1},{1,0},{2,3},{3,2},{4,5},{5,4},{6,7},{7,6},{8,9},{9,8},{10,11... | collective-permute-start | bytes 184328 | tf_op jit(solution)/shard_map/ppermute | solution.py:258
  13.9 3.9 %collective-permute-start.3 = (bf16[3,2,5120]{2,1,0:T(2,128)(2,1)S(1)}, bf16[3,2,5120]{2,1,0:T(2,128)(2,1)S(1)}, u32[]{:S(2)}, u32[]{:S(2)}) collective-permute-start(bf16[3,2,5120]{2,1,0:T(2,128)(2,1)S(1)} %copy-done.2), channel_id=1, source_target_pairs={{0,1},{1,0},{2,3},{3,2},{4,5},{5,4},{6,7},{7,6},{8,9},{9,8},{10,11... | collective-permute-start | bytes 184328 | tf_op jit(solution)/shard_map/ppermute | solution.py:258
  15.9 2.2 %collective-permute-start.4 = (bf16[3,2,5120]{2,1,0:T(2,128)(2,1)S(1)}, bf16[3,2,5120]{2,1,0:T(2,128)(2,1)S(1)}, u32[]{:S(2)}, u32[]{:S(2)}) collective-permute-start(bf16[3,2,5120]{2,1,0:T(2,128)(2,1)S(1)} %collective-permute-done.1), channel_id=1, source_target_pairs={{0,1},{1,0},{2,3},{3,2},{4,5},{5,4},{6,7},{7,6},{8,9},{9,8},{10,11... | collective-permute-start | bytes 184328 | tf_op jit(solution)/shard_map/ppermute | solution.py:258
  15.9 2.2 %collective-permute-start.5 = (bf16[3,2,5120]{2,1,0:T(2,128)(2,1)S(1)}, bf16[3,2,5120]{2,1,0:T(2,128)(2,1)S(1)}, u32[]{:S(2)}, u32[]{:S(2)}) collective-permute-start(bf16[3,2,5120]{2,1,0:T(2,128)(2,1)S(1)} %collective-permute-done), channel_id=1, source_target_pairs={{0,1},{1,0},{2,3},{3,2},{4,5},{5,4},{6,7},{7,6},{8,9},{9,8},{10,11... | collective-permute-start | bytes 184328 | tf_op jit(solution)/shard_map/ppermute | solution.py:258
  17.4 1.2 %collective-permute-start.6 = (bf16[3,2,5120]{2,1,0:T(2,128)(2,1)S(1)}, bf16[3,2,5120]{2,1,0:T(2,128)(2,1)S(1)}, u32[]{:S(2)}, u32[]{:S(2)}) collective-permute-start(bf16[3,2,5120]{2,1,0:T(2,128)(2,1)S(1)} %collective-permute-done.2), channel_id=1, source_target_pairs={{0,1},{1,0},{2,3},{3,2},{4,5},{5,4},{6,7},{7,6},{8,9},{9,8},{10,11... | collective-permute-start | bytes 184328 | tf_op jit(solution)/shard_map/ppermute | solution.py:258
  17.4 1.4 %collective-permute-start.14 = (bf16[3,2,5120]{2,1,0:T(2,128)(2,1)S(1)}, bf16[3,2,5120]{2,1,0:T(2,128)(2,1)S(1)}, u32[]{:S(2)}, u32[]{:S(2)}) collective-permute-start(bf16[3,2,5120]{2,1,0:T(2,128)(2,1)S(1)} %collective-permute-done.13), channel_id=1, source_target_pairs={{0,1},{1,0},{2,3},{3,2},{4,5},{5,4},{6,7},{7,6},{8,9},{9,8},{10,11... | collective-permute-start | bytes 184328 | tf_op jit(solution)/shard_map/ppermute | solution.py:258
  17.9 1.2 %collective-permute-start.10 = (bf16[3,2,5120]{2,1,0:T(2,128)(2,1)S(1)}, bf16[3,2,5120]{2,1,0:T(2,128)(2,1)S(1)}, u32[]{:S(2)}, u32[]{:S(2)}) collective-permute-start(bf16[3,2,5120]{2,1,0:T(2,128)(2,1)S(1)} %collective-permute-done.9), channel_id=1, source_target_pairs={{0,1},{1,0},{2,3},{3,2},{4,5},{5,4},{6,7},{7,6},{8,9},{9,8},{10,11... | collective-permute-start | bytes 184328 | tf_op jit(solution)/shard_map/ppermute | solution.py:258
  21.2 4.2 %collective-permute-start.17 = (bf16[48,128]{1,0:T(8,128)(2,1)S(1)}, bf16[48,128]{1,0:T(8,128)(2,1)S(1)}, u32[]{:S(2)}, u32[]{:S(2)}) collective-permute-start(bf16[48,128]{1,0:T(8,128)(2,1)S(1)} %get-tuple-element.45), channel_id=1, source_target_pairs={{0,3},{1,2},{2,1},{3,0},{4,7},{5,6},{6,5},{7,4},{8,11},{9,10},{10,... | collective-permute-start | bytes 36872 | tf_op jit(solution)/shard_map/ppermute | solution.py:258
  21.5 3.9 %collective-permute-start.16 = (bf16[48,128]{1,0:T(8,128)(2,1)S(1)}, bf16[48,128]{1,0:T(8,128)(2,1)S(1)}, u32[]{:S(2)}, u32[]{:S(2)}) collective-permute-start(bf16[48,128]{1,0:T(8,128)(2,1)S(1)} %get-tuple-element.45), channel_id=1, source_target_pairs={{0,2},{1,3},{2,0},{3,1},{4,6},{5,7},{6,4},{7,5},{8,10},{9,11},{10,... | collective-permute-start | bytes 36872 | tf_op jit(solution)/shard_map/ppermute | solution.py:258
  23.1 2.4 %collective-permute-start.15 = (bf16[48,128]{1,0:T(8,128)(2,1)S(1)}, bf16[48,128]{1,0:T(8,128)(2,1)S(1)}, u32[]{:S(2)}, u32[]{:S(2)}) collective-permute-start(bf16[48,128]{1,0:T(8,128)(2,1)S(1)} %get-tuple-element.45), channel_id=1, source_target_pairs={{0,1},{1,0},{2,3},{3,2},{4,5},{5,4},{6,7},{7,6},{8,9},{9,8},{10,11... | collective-permute-start | bytes 36872 | tf_op jit(solution)/shard_map/ppermute | solution.py:258
  25.4 7.0 %copy-start = (bf16[64,64,320]{2,1,0:T(8,128)(2,1)S(1)}, bf16[64,64,320]{2,1,0:T(8,128)(2,1)}, u32[]{:S(2)}) copy-start(bf16[64,64,320]{2,1,0:T(8,128)(2,1)} %param.12) | copy-start | bytes 7864324
  25.5 5.6 %collective-permute-start.20 = (bf16[48,128]{1,0:T(8,128)(2,1)S(1)}, bf16[48,128]{1,0:T(8,128)(2,1)S(1)}, u32[]{:S(2)}, u32[]{:S(2)}) collective-permute-start(bf16[48,128]{1,0:T(8,128)(2,1)S(1)} %add_add_fusion.refs_0_), channel_id=1, source_target_pairs={{0,12},{1,13},{2,14},{3,15},{4,8},{5,9},{6,10},{7,11},{8,4},{9,5},... | collective-permute-start | bytes 36872 | tf_op jit(solution)/shard_map/ppermute | solution.py:258
  27.9 4.6 %collective-permute-start.19 = (bf16[48,128]{1,0:T(8,128)(2,1)S(1)}, bf16[48,128]{1,0:T(8,128)(2,1)S(1)}, u32[]{:S(2)}, u32[]{:S(2)}) collective-permute-start(bf16[48,128]{1,0:T(8,128)(2,1)S(1)} %add_add_fusion.refs_0_), channel_id=1, source_target_pairs={{0,8},{1,9},{2,10},{3,11},{4,12},{5,13},{6,14},{7,15},{8,0},{9,1},... | collective-permute-start | bytes 36872 | tf_op jit(solution)/shard_map/ppermute | solution.py:258
  28.1 4.4 %collective-permute-start.18 = (bf16[48,128]{1,0:T(8,128)(2,1)S(1)}, bf16[48,128]{1,0:T(8,128)(2,1)S(1)}, u32[]{:S(2)}, u32[]{:S(2)}) collective-permute-start(bf16[48,128]{1,0:T(8,128)(2,1)S(1)} %add_add_fusion.refs_0_), channel_id=1, source_target_pairs={{0,4},{1,5},{2,6},{3,7},{4,0},{5,1},{6,2},{7,3},{8,12},{9,13},{10,... | collective-permute-start | bytes 36872 | tf_op jit(solution)/shard_map/ppermute | solution.py:258
  34.1 13.6 %all-to-all-start = ((bf16[16,9,3,2,128]{4,3,2,1,0:T(2,128)(2,1)}), bf16[16,9,3,2,128]{4,3,2,1,0:T(2,128)(2,1)S(1)}, u32[]{:S(2)}, u32[]{:S(2)}) async-start(bf16[16,9,3,2,128]{4,3,2,1,0:T(2,128)(2,1)} %update_values.1), calls=%async_computation | async-start | bytes 442368 | tf_op jit(solution)/shard_map/all_to_all | solution.py:657

commit v16 on v15

--- a/solution.py
+++ b/solution.py
@@ -283,7 +283,8 @@
 
 
 CACHE_SECTION = 10
-CACHE_AHEAD = 2
+CACHE_AHEAD = 4
+CACHE_TOKENS = 128
 
 
 def cache_kernel(first, pool_ref, keys_ref, values_ref, raw, values, sem, out_sem):
@@ -291,9 +292,10 @@
     copies = [pltpu.make_async_copy(pool_ref.at[:, first + h], raw.at[h], sem.at[h]) for h in range(heads)]
     start_all(copies[: CACHE_AHEAD * CACHE_SECTION])
     rows = raw.reshape(heads, 2 * tokens, HD)
-    to = lax.broadcasted_iota(jnp.int32, (2 * tokens, 2 * tokens), 0)
-    source = lax.broadcasted_iota(jnp.int32, (2 * tokens, 2 * tokens), 1)
-    wanted = jnp.where(to < tokens, 2 * to, 2 * (to - tokens) + 1)
+    block = min(tokens, CACHE_TOKENS)
+    to = lax.broadcasted_iota(jnp.int32, (2 * block, 2 * block), 0)
+    source = lax.broadcasted_iota(jnp.int32, (2 * block, 2 * block), 1)
+    wanted = jnp.where(to < block, 2 * to, 2 * (to - block) + 1)
     pick = jnp.where(source == wanted, 1.0, 0.0).astype(jnp.bfloat16)
     sent = []
     part = CACHE_SECTION
@@ -301,11 +303,14 @@
         wait_all(copies[p * part : (p + 1) * part])
         start_all(copies[(p + CACHE_AHEAD) * part : (p + CACHE_AHEAD + 1) * part])
         for h in range(p * part, (p + 1) * part, 2):
-            both = jnp.concatenate([rows[h], rows[h + 1]], axis=1)
-            made = jnp.dot(pick, both, preferred_element_type=jnp.float32).astype(jnp.bfloat16)
-            for i in range(2):
-                keys_ref[h + i] = made[:tokens, i * HD : (i + 1) * HD]
-                values[h + i] = made[tokens:, i * HD : (i + 1) * HD]
+            for first_token in range(0, tokens, block):
+                raw_rows = slice(2 * first_token, 2 * (first_token + block))
+                both = jnp.concatenate([rows[h, raw_rows], rows[h + 1, raw_rows]], axis=1)
+                made = jnp.dot(pick, both, preferred_element_type=jnp.float32).astype(jnp.bfloat16)
+                span = slice(first_token, first_token + block)
+                for i in range(2):
+                    keys_ref[h + i, span] = made[:block, i * HD : (i + 1) * HD]
+                    values[h + i, span] = made[block:, i * HD : (i + 1) * HD]
         span = slice(p * part, (p + 1) * part)
         sent += start_all([pltpu.make_async_copy(values.at[span], values_ref.at[span], out_sem.at[p])])
     wait_all(sent)
@@ -426,7 +431,8 @@
     x = step_rows(x_ref, 0, x_ref.shape[1])
     made = lax.dot_general(w_ref[which], x, CONTRACT_LANES, preferred_element_type=jnp.float32).T
     if which < 2:
-        put_chunks(out_ref, 0, made)
+        pad = jnp.zeros((made.shape[0], HD // 2), made.dtype)
+        put_chunks(out_ref, 0, jnp.concatenate([made, pad] if which == 0 else [pad, made], axis=1))
     else:
         out_ref[...] = made
 
@@ -465,9 +471,10 @@
         wide = jnp.where(ahead == a, spread, 0.0).astype(jnp.bfloat16)
         total = total + jnp.dot(wide, up_ref[a * rank : (a + batch) * rank], preferred_element_type=jnp.float32)
     each = query_ref.shape[0]
-    buf[:each] = query_ref[...]
-    buf[each : 2 * each] = key_ref[...]
-    put_chunks(buf, 2 * each, base_ref[...] + adapter_scale * total)
+    buf[: each - 1] = query_ref[: each - 1]
+    buf[each - 1] = query_ref[each - 1] + key_ref[0]
+    buf[each : 2 * each - 1] = key_ref[1:]
+    put_chunks(buf, 2 * each - 1, base_ref[...] + adapter_scale * total)
     wait_all(
         start_all([pltpu.make_async_copy(buf.at[:, :, k], send_ref.at[k], sem.at[k]) for k in range(count)])
     )
@@ -477,11 +484,11 @@
     chunks, steps, count = query.shape[:3]
     return pl.pallas_call(
         update_kernel,
-        out_shape=pltpu.HBM((count, 3 * chunks, steps, 2, HD), query.dtype),
+        out_shape=pltpu.HBM((count, 3 * chunks - 1, steps, 2, HD), query.dtype),
         in_specs=[VMEM] * (5 + len(lows)),
         out_specs=HBM,
         scratch_shapes=[
-            pltpu.VMEM((3 * chunks, steps, count, 2, HD), query.dtype),
+            pltpu.VMEM((3 * chunks - 1, steps, count, 2, HD), query.dtype),
             pltpu.SemaphoreType.DMA((count,)),
         ],
         compiler_params=pltpu.CompilerParams(vmem_limit_bytes=8 * 2**20),
@@ -495,7 +502,7 @@
     keys_refs, values_refs = parts[: len(parts) // 2], parts[len(parts) // 2 :]
     count, _, steps = pieces_ref.shape[:3]
     rows = 2 * steps
-    each = pieces_ref.shape[1] // 3
+    each = (pieces_ref.shape[1] + 1) // 3
     heads = 2 * out_ref.shape[1] // count
     lanes = heads * HD
     group = rows * HEAD_BLOCK
@@ -512,12 +519,27 @@
     sine = sin_ref[...][:rows]
     left = lax.broadcasted_iota(jnp.int32, (rows, HD), 1) < HD // 2
 
+    def halves(chip, at):
+        return [
+            [pieces_ref[2 * chip + core, at + c].reshape(rows, HD).astype(jnp.float32) for c in range(each)]
+            for core in range(2)
+        ]
+
+    def swapped(parts):
+        return [pltpu.roll(x, HD // 2, 1) for x in parts]
+
+    def joined(parts):
+        return [jnp.where(left, a, b) for a, b in zip(parts[:-1], parts[1:])]
+
     def chip_columns(chip, at):
-        low = [pieces_ref[2 * chip, at + c].reshape(rows, HD).astype(jnp.float32) for c in range(each)]
-        high = [pieces_ref[2 * chip + 1, at + c].reshape(rows, HD).astype(jnp.float32) for c in range(each)]
-        high = [pltpu.roll(x, HD // 2, 1) for x in high]
-        whole = low[:-1] + [jnp.where(left, low[-1], high[0])]
-        return whole + [jnp.where(left, a, b) for a, b in zip(high[:-1], high[1:])]
+        low, high = halves(chip, at)
+        high = swapped(high)
+        return low[:-1] + [jnp.where(left, low[-1], high[0])] + joined(high)
+
+    def chip_keys(chip):
+        low, high = halves(chip, each - 1)
+        low = swapped(low)
+        return joined(low) + [jnp.where(left, low[-1], high[0])] + high[1:]
 
     def rotated(parts):
         return [x * cosine + pltpu.roll(x, HD // 2, 1) * sine for x in parts]
@@ -541,8 +563,8 @@
     spreads = []
     for c in chips:
         query = jnp.concatenate(rotated(chip_columns(c, 0)), axis=1)
-        kn_ref[c, 0:rows] = jnp.concatenate(rotated(chip_columns(c, each)), axis=1)
-        vn_ref[c, 0:rows] = jnp.concatenate(chip_columns(c, 2 * each), axis=1)
+        kn_ref[c, 0:rows] = jnp.concatenate(rotated(chip_keys(c)), axis=1)
+        vn_ref[c, 0:rows] = jnp.concatenate(chip_columns(c, 2 * each - 1), axis=1)
         spread = jnp.concatenate(
             [jnp.broadcast_to(query[j : j + 1], (HEAD_BLOCK, lanes)) for j in range(rows)], axis=0
         )

time: 52 us -> 51.6 us (level)
  no operation moved by 1% of the time
where the time goes in v16:
time: 51.6 us; the launch traced here: 51.3 us
  starting transfers between devices  20.9 us (41%)
  Pallas kernels  17.5 us (34%)
  waiting for transfers between devices  10.9 us (21%)
  other arithmetic  1.53 us (3%)
    ppermute x21, starting transfers between devices, trade(): return lax.ppermute(value, 'replica', [(i, i ^ mask) for i in range(count)])  16.8 us
    ppermute x21, waiting for transfers between devices, trade(): return lax.ppermute(value, 'replica', [(i, i ^ mask) for i in range(count)])  8.49 us
    pallas_call x1, Pallas kernels, cache_by_head(): pl.pallas_call(functools.partial(cache_kernel, first), out_shape=(jax.Sha...  6.4 us
    all_to_all x1, starting transfers between devices, chip_plan(): lax.all_to_all(send, 'replica', split_axis=0, concat_axis=0, tiled=True)  4.1 us
    pallas_call x1, Pallas kernels, attend(): pl.pallas_call(attend_kernel, out_shape=jax.ShapeDtypeStruct((steps, head...  3.83 us
    pallas_call x3, Pallas kernels, project(): pl.pallas_call(functools.partial(project_kernel, which), out_shape=chunks...  3.44 us
    all_to_all x1, waiting for transfers between devices, chip_plan(): lax.all_to_all(send, 'replica', split_axis=0, concat_axis=0, tiled=True)  2.45 us
    pallas_call x1, Pallas kernels, low_of(): pl.pallas_call(functools.partial(low_kernel, count), out_shape=(jax.Shape...  2.06 us
  transfers between devices with their start and end apart: 22, of which 9 were waited for; matrix products, arithmetic and copies ran while one was open for 3% of the time, Pallas kernels for 20%

profile of v16, /device:TPU:0, one launch (start us, length us, event | category | flops | bytes accessed | tf_op | source)
XLA Modules:
  0.0 51.3 jit_solution(876228786488597987)
XLA Ops:
  0.0 3.0 %collective-permute-start.1 = (bf16[3,2,5120]{2,1,0:T(2,128)(2,1)}, bf16[3,2,5120]{2,1,0:T(2,128)(2,1)S(1)}, u32[]{:S(2)}, u32[]{:S(2)}) collective-permute-start(bf16[3,2,5120]{2,1,0:T(2,128)(2,1)} %param.9), channel_id=1, source_target_pairs={{0,2},{1,3},{2,0},{3,1},{4,6},{5,7},{6,4},{7,5},{8,10},{9,11},{10,... | collective-permute-start | bytes 184328 | tf_op jit(solution)/shard_map/ppermute | solution.py:258
  3.0 1.6 %collective-permute-start = (bf16[3,2,5120]{2,1,0:T(2,128)(2,1)}, bf16[3,2,5120]{2,1,0:T(2,128)(2,1)S(1)}, u32[]{:S(2)}, u32[]{:S(2)}) collective-permute-start(bf16[3,2,5120]{2,1,0:T(2,128)(2,1)} %param.9), channel_id=1, source_target_pairs={{0,4},{1,5},{2,6},{3,7},{4,0},{5,1},{6,2},{7,3},{8,12},{9,13},{10,... | collective-permute-start | bytes 184328 | tf_op jit(solution)/shard_map/ppermute | solution.py:258
  4.5 2.5 %collective-permute-start.11 = (bf16[3,2,5120]{2,1,0:T(2,128)(2,1)}, bf16[3,2,5120]{2,1,0:T(2,128)(2,1)S(1)}, u32[]{:S(2)}, u32[]{:S(2)}) collective-permute-start(bf16[3,2,5120]{2,1,0:T(2,128)(2,1)} %param.9), channel_id=1, source_target_pairs={{0,12},{1,13},{2,14},{3,15},{4,8},{5,9},{6,10},{7,11},{8,4},{9,5},... | collective-permute-start | bytes 184328 | tf_op jit(solution)/shard_map/ppermute | solution.py:258
  7.0 0.1 collective-permute-start.7
  7.2 0.9 %select_reduce_fusion.1 = s32[32]{0:T(128)S(1)} fusion(s32[64]{0:T(128)} %param.13, s32[32]{0:T(128)} %param.14), kind=kLoop, calls=%fused_computation.1 | loop fusion | flops 6112 | bytes 512 | tf_op jit(solution)/shard_map/reduce_sum | solution.py:643
  8.0 0.0 slice-start
  8.0 0.0 copy-start.3
  8.0 0.0 copy-start.4
  8.1 0.0 copy-start.2
  8.1 0.0 copy-start.1
  8.1 0.2 index_work.1
  8.3 0.6 %collective-permute-start.2 = (bf16[3,2,5120]{2,1,0:T(2,128)(2,1)S(1)}, bf16[3,2,5120]{2,1,0:T(2,128)(2,1)S(1)}, u32[]{:S(2)}, u32[]{:S(2)}) collective-permute-start(bf16[3,2,5120]{2,1,0:T(2,128)(2,1)S(1)} %collective-permute-done), channel_id=1, source_target_pairs={{0,2},{1,3},{2,0},{3,1},{4,6},{5,7},{6,4},{7,5},{8,10},{9,11},{10,... | collective-permute-start | bytes 184328 | tf_op jit(solution)/shard_map/ppermute | solution.py:258
  8.9 2.4 %collective-permute-done.11 = bf16[3,2,5120]{2,1,0:T(2,128)(2,1)S(1)} collective-permute-done((bf16[3,2,5120]{2,1,0:T(2,128)(2,1)}, bf16[3,2,5120]{2,1,0:T(2,128)(2,1)S(1)}, u32[]{:S(2)}, u32[]{:S(2)}) %collective-permute-start.11) | collective-permute-done | bytes 61472 | tf_op jit(solution)/shard_map/ppermute | solution.py:258
  11.3 0.5 collective-permute-start.13
  11.8 0.1 select_reduce_fusion
  11.9 1.3 %collective-permute-done.7 = bf16[3,2,5120]{2,1,0:T(2,128)(2,1)S(1)} collective-permute-done((bf16[3,2,5120]{2,1,0:T(2,128)(2,1)}, bf16[3,2,5120]{2,1,0:T(2,128)(2,1)S(1)}, u32[]{:S(2)}, u32[]{:S(2)}) %collective-permute-start.7) | collective-permute-done | bytes 61472 | tf_op jit(solution)/shard_map/ppermute | solution.py:258
  13.2 0.5 collective-permute-start.9
  13.7 0.2 fusion.3
  13.8 0.1 collective-permute-start.8
  13.9 0.5 collective-permute-start.3
  14.4 0.1 and_convert_fusion.live_ref
  14.5 1.4 %collective-permute-done.13 = bf16[3,2,5120]{2,1,0:T(2,128)(2,1)S(1)} collective-permute-done((bf16[3,2,5120]{2,1,0:T(2,128)(2,1)S(1)}, bf16[3,2,5120]{2,1,0:T(2,128)(2,1)S(1)}, u32[]{:S(2)}, u32[]{:S(2)}) %collective-permute-start.13) | collective-permute-done | bytes 61472 | tf_op jit(solution)/shard_map/ppermute | solution.py:258
  15.9 0.5 collective-permute-start.5
  16.4 0.9 %collective-permute-done.9 = bf16[3,2,5120]{2,1,0:T(2,128)(2,1)S(1)} collective-permute-done((bf16[3,2,5120]{2,1,0:T(2,128)(2,1)S(1)}, bf16[3,2,5120]{2,1,0:T(2,128)(2,1)S(1)}, u32[]{:S(2)}, u32[]{:S(2)}) %collective-permute-start.9) | collective-permute-done | bytes 61472 | tf_op jit(solution)/shard_map/ppermute | solution.py:258
  17.4 0.5 collective-permute-start.14
  17.9 0.1 collective-permute-start.10
  18.0 0.2 select_reduce_fusion.2
  18.2 0.5 collective-permute-done.6
  18.6 0.2 collective-permute-done.14
  18.8 0.4 collective-permute-done.10
  19.1 2.1 %low_rows.1 = (bf16[3,40,16,2,128]{4,3,2,1,0:T(2,128)(2,1)S(1)}, bf16[48,128]{1,0:T(8,128)(2,1)S(1)}) custom-call(s32[1]{0:T(128)} %bitcast.1.me_ref, s32[1,96]{1,0:T(1,128)S(1)} %get-tuple-element.40.slot_ref, bf16[4,64,5120]{2,1,0:T(8,128)(2,1)S(1)} %copy-done.1, bf16[3,40,2,128]{3,2,1,0:T(2,128)(2,1)} %bitcast.82, bf16[3,40,2,128]{3,2,1,0:T(2,128)(2,1)S(1)} %bitcast.74, ...), custom_call_target="tpu_custom_call" | custom-call | flops 100000000 | bytes 4000000 | tf_op jit(solution)/shard_map/low_rows/pallas_call | solution.py:402
  21.2 0.3 collective-permute-start.17
  21.5 1.5 %collective-permute-start.16 = (bf16[48,128]{1,0:T(8,128)(2,1)S(1)}, bf16[48,128]{1,0:T(8,128)(2,1)S(1)}, u32[]{:S(2)}, u32[]{:S(2)}) collective-permute-start(bf16[48,128]{1,0:T(8,128)(2,1)S(1)} %get-tuple-element.45), channel_id=1, source_target_pairs={{0,2},{1,3},{2,0},{3,1},{4,6},{5,7},{6,4},{7,5},{8,10},{9,11},{10,... | collective-permute-start | bytes 36872 | tf_op jit(solution)/shard_map/ppermute | solution.py:258
  23.1 0.1 collective-permute-start.15
  23.2 1.2 %project.4.key_ref = bf16[3,3,16,2,128]{4,3,2,1,0:T(2,128)(2,1)S(1)} custom-call(bf16[3,40,16,2,128]{4,3,2,1,0:T(2,128)(2,1)S(1)} %get-tuple-element.46.x_ref, bf16[3,320,5120]{2,1,0:T(8,128)(2,1)S(1)} %bitcast.61), custom_call_target="tpu_custom_call" | custom-call | flops 500000000 | bytes 4000000 | tf_op jit(solution)/shard_map/project/pallas_call | solution.py:445
  24.4 1.1 %project.3.query_ref = bf16[3,3,16,2,128]{4,3,2,1,0:T(2,128)(2,1)S(1)} custom-call(bf16[3,40,16,2,128]{4,3,2,1,0:T(2,128)(2,1)S(1)} %get-tuple-element.46.x_ref, bf16[3,320,5120]{2,1,0:T(8,128)(2,1)S(1)} %bitcast.62), custom_call_target="tpu_custom_call" | custom-call | flops 500000000 | bytes 4000000 | tf_op jit(solution)/shard_map/project/pallas_call | solution.py:445
  25.5 0.0 copy-start
  25.6 2.4 %collective-permute-start.20 = (bf16[48,128]{1,0:T(8,128)(2,1)S(1)}, bf16[48,128]{1,0:T(8,128)(2,1)S(1)}, u32[]{:S(2)}, u32[]{:S(2)}) collective-permute-start(bf16[48,128]{1,0:T(8,128)(2,1)S(1)} %add_add_fusion.refs_0_), channel_id=1, source_target_pairs={{0,12},{1,13},{2,14},{3,15},{4,8},{5,9},{6,10},{7,11},{8,4},{9,5},... | collective-permute-start | bytes 36872 | tf_op jit(solution)/shard_map/ppermute | solution.py:258
  28.0 0.1 collective-permute-start.19
  28.1 1.9 %collective-permute-start.18 = (bf16[48,128]{1,0:T(8,128)(2,1)S(1)}, bf16[48,128]{1,0:T(8,128)(2,1)S(1)}, u32[]{:S(2)}, u32[]{:S(2)}) collective-permute-start(bf16[48,128]{1,0:T(8,128)(2,1)S(1)} %add_add_fusion.refs_0_), channel_id=1, source_target_pairs={{0,4},{1,5},{2,6},{3,7},{4,0},{5,1},{6,2},{7,3},{8,12},{9,13},{10,... | collective-permute-start | bytes 36872 | tf_op jit(solution)/shard_map/ppermute | solution.py:258
  30.0 1.1 %project.5.base_ref = f32[96,320]{1,0:T(8,128)S(1)} custom-call(bf16[3,40,16,2,128]{4,3,2,1,0:T(2,128)(2,1)S(1)} %get-tuple-element.46.x_ref, bf16[3,320,5120]{2,1,0:T(8,128)(2,1)S(1)} %bitcast.63), custom_call_target="tpu_custom_call" | custom-call | flops 500000000 | bytes 4000000 | tf_op jit(solution)/shard_map/project/pallas_call | solution.py:445
  31.1 1.4 %collective-permute-done.19.refs_2_ = bf16[48,128]{1,0:T(8,128)(2,1)S(1)} collective-permute-done((bf16[48,128]{1,0:T(8,128)(2,1)S(1)}, bf16[48,128]{1,0:T(8,128)(2,1)S(1)}, u32[]{:S(2)}, u32[]{:S(2)}) %collective-permute-start.19) | collective-permute-done | bytes 12320 | tf_op jit(solution)/shard_map/ppermute | solution.py:258
  32.6 1.6 %update_values.1 = bf16[16,8,3,2,128]{4,3,2,1,0:T(2,128)(2,1)} custom-call(s32[96,1]{1,0:T(8,128)S(1)} %get-tuple-element.38.stored_ref, bf16[3,3,16,2,128]{4,3,2,1,0:T(2,128)(2,1)S(1)} %project.3.query_ref, bf16[3,3,16,2,128]{4,3,2,1,0:T(2,128)(2,1)S(1)} %project.4.key_ref, f32[96,320]{1,0:T(8,128)S(1)} %project.5.base_ref, bf16[4096,320]{1,0:T(8,128)(2,1)S(1)} %bitcast.64, ...), custom_call_target="tpu_custom_call" | custom-call | flops 300000000 | bytes 4000000 | tf_op jit(solution)/shard_map/update_values/pallas_call | solution.py:485
  34.2 4.1 %all-to-all-start = ((bf16[16,8,3,2,128]{4,3,2,1,0:T(2,128)(2,1)}), bf16[16,8,3,2,128]{4,3,2,1,0:T(2,128)(2,1)S(1)}, u32[]{:S(2)}, u32[]{:S(2)}) async-start(bf16[16,8,3,2,128]{4,3,2,1,0:T(2,128)(2,1)} %update_values.1), calls=%async_computation | async-start | bytes 393216 | tf_op jit(solution)/shard_map/all_to_all | solution.py:679
  38.3 0.1 fusion
  38.5 6.4 %cache_by_head.1 = (bf16[40,256,128]{2,1,0:T(8,128)(2,1)S(1)}, bf16[40,256,128]{2,1,0:T(8,128)(2,1)}) custom-call(bf16[256,40,2,128]{3,2,1,0:T(2,128)(2,1)} %bitcast.81), custom_call_target="tpu_custom_call" | custom-call | bytes 12000000 | tf_op jit(solution)/shard_map/cache_by_head/pallas_call | solution.py:321
  44.9 2.5 %all-to-all-done.pieces_ref = bf16[16,8,3,2,128]{4,3,2,1,0:T(2,128)(2,1)S(1)} async-done(((bf16[16,8,3,2,128]{4,3,2,1,0:T(2,128)(2,1)}), bf16[16,8,3,2,128]{4,3,2,1,0:T(2,128)(2,1)S(1)}, u32[]{:S(2)}, u32[]{:S(2)}) %all-to-all-start) | async-done | bytes 196640 | tf_op jit(solution)/shard_map/all_to_all | solution.py:679
  47.3 3.8 %attention.1 = bf16[3,40,2,128]{3,2,1,0:T(2,128)(2,1)} custom-call(f32[8,128]{1,0:T(8,128)S(1)} %get-tuple-element.62.cos_ref, f32[8,128]{1,0:T(8,128)S(1)} %get-tuple-element.61.sin_ref, s32[2,256]{1,0:T(2,128)S(1)} %and_convert_fusion.live_ref, bf16[16,8,3,2,128]{4,3,2,1,0:T(2,128)(2,1)S(1)} %all-to-all-done.pieces_ref, ...), custom_call_target="tpu_custom_call" | custom-call | flops 1000000000 | bytes 6000000 | tf_op jit(solution)/shard_map/attention/pallas_call | solution.py:607
  (34 shorter events, 0.1 us)
Async XLA Ops:
  0.0 13.8 %collective-permute-start.1 = (bf16[3,2,5120]{2,1,0:T(2,128)(2,1)}, bf16[3,2,5120]{2,1,0:T(2,128)(2,1)S(1)}, u32[]{:S(2)}, u32[]{:S(2)}) collective-permute-start(bf16[3,2,5120]{2,1,0:T(2,128)(2,1)} %param.9), channel_id=1, source_target_pairs={{0,2},{1,3},{2,0},{3,1},{4,6},{5,7},{6,4},{7,5},{8,10},{9,11},{10,... | collective-permute-start | bytes 184328 | tf_op jit(solution)/shard_map/ppermute | solution.py:258
  3.0 5.3 %collective-permute-start = (bf16[3,2,5120]{2,1,0:T(2,128)(2,1)}, bf16[3,2,5120]{2,1,0:T(2,128)(2,1)S(1)}, u32[]{:S(2)}, u32[]{:S(2)}) collective-permute-start(bf16[3,2,5120]{2,1,0:T(2,128)(2,1)} %param.9), channel_id=1, source_target_pairs={{0,4},{1,5},{2,6},{3,7},{4,0},{5,1},{6,2},{7,3},{8,12},{9,13},{10,... | collective-permute-start | bytes 184328 | tf_op jit(solution)/shard_map/ppermute | solution.py:258
  4.5 6.7 %collective-permute-start.11 = (bf16[3,2,5120]{2,1,0:T(2,128)(2,1)}, bf16[3,2,5120]{2,1,0:T(2,128)(2,1)S(1)}, u32[]{:S(2)}, u32[]{:S(2)}) collective-permute-start(bf16[3,2,5120]{2,1,0:T(2,128)(2,1)} %param.9), channel_id=1, source_target_pairs={{0,12},{1,13},{2,14},{3,15},{4,8},{5,9},{6,10},{7,11},{8,4},{9,5},... | collective-permute-start | bytes 184328 | tf_op jit(solution)/shard_map/ppermute | solution.py:258
  7.0 6.1 %collective-permute-start.7 = (bf16[3,2,5120]{2,1,0:T(2,128)(2,1)}, bf16[3,2,5120]{2,1,0:T(2,128)(2,1)S(1)}, u32[]{:S(2)}, u32[]{:S(2)}) collective-permute-start(bf16[3,2,5120]{2,1,0:T(2,128)(2,1)} %param.9), channel_id=1, source_target_pairs={{0,8},{1,9},{2,10},{3,11},{4,12},{5,13},{6,14},{7,15},{8,0},{9,1},... | collective-permute-start | bytes 184328 | tf_op jit(solution)/shard_map/ppermute | solution.py:258
  8.0 15.1 %slice-start = ((s8[9830400]{0:T(1024)(128)(4,1)}), s8[4194304]{0:T(1024)(128)(4,1)S(1)}, s32[]{:S(2)}) async-start(s8[9830400]{0:T(1024)(128)(4,1)} %bitcast.59), calls=%async_computation.1 | async-start | bytes 8388608
  8.0 3.7 %copy-start.3 = (s32[2,32]{1,0:T(2,128)S(1)}, s32[2,32]{1,0:T(2,128)}, u32[]{:S(2)}) copy-start(s32[2,32]{1,0:T(2,128)} %param.16) | copy-start | bytes 772
  8.0 5.6 %copy-start.4 = (s32[32]{0:T(128)S(1)}, s32[32]{0:T(128)}, u32[]{:S(2)}) copy-start(s32[32]{0:T(128)} %param.15) | copy-start | bytes 388
  8.1 5.9 %copy-start.2 = (bf16[3,2,5120]{2,1,0:T(2,128)(2,1)S(1)}, bf16[3,2,5120]{2,1,0:T(2,128)(2,1)}, u32[]{:S(2)}) copy-start(bf16[3,2,5120]{2,1,0:T(2,128)(2,1)} %param.9) | copy-start | bytes 184324
  8.1 11.1 %copy-start.1 = (bf16[4,64,5120]{2,1,0:T(8,128)(2,1)S(1)}, bf16[4,64,5120]{2,1,0:T(8,128)(2,1)}, u32[]{:S(2)}) copy-start(bf16[4,64,5120]{2,1,0:T(8,128)(2,1)} %down_ref.1) | copy-start | bytes 7864324
  8.1 15.1 %slice-start.1 = ((s8[9830400]{0:T(1024)(128)(4,1)}), s8[4194304]{0:T(1024)(128)(4,1)S(1)}, s32[]{:S(2)}) async-start(s8[9830400]{0:T(1024)(128)(4,1)} %bitcast.59), calls=%async_computation.2 | async-start | bytes 8388608
  8.1 15.1 %slice-start.2 = ((s8[9830400]{0:T(1024)(128)(4,1)}), s8[1441792]{0:T(1024)(128)(4,1)S(1)}, s32[]{:S(2)}) async-start(s8[9830400]{0:T(1024)(128)(4,1)} %bitcast.59), calls=%async_computation.3 | async-start | bytes 2883584
  8.3 5.6 %collective-permute-start.2 = (bf16[3,2,5120]{2,1,0:T(2,128)(2,1)S(1)}, bf16[3,2,5120]{2,1,0:T(2,128)(2,1)S(1)}, u32[]{:S(2)}, u32[]{:S(2)}) collective-permute-start(bf16[3,2,5120]{2,1,0:T(2,128)(2,1)S(1)} %collective-permute-done), channel_id=1, source_target_pairs={{0,2},{1,3},{2,0},{3,1},{4,6},{5,7},{6,4},{7,5},{8,10},{9,11},{10,... | collective-permute-start | bytes 184328 | tf_op jit(solution)/shard_map/ppermute | solution.py:258
  11.3 4.7 %collective-permute-start.13 = (bf16[3,2,5120]{2,1,0:T(2,128)(2,1)S(1)}, bf16[3,2,5120]{2,1,0:T(2,128)(2,1)S(1)}, u32[]{:S(2)}, u32[]{:S(2)}) collective-permute-start(bf16[3,2,5120]{2,1,0:T(2,128)(2,1)S(1)} %collective-permute-done.11), channel_id=1, source_target_pairs={{0,2},{1,3},{2,0},{3,1},{4,6},{5,7},{6,4},{7,5},{8,10},{9,11},{10,... | collective-permute-start | bytes 184328 | tf_op jit(solution)/shard_map/ppermute | solution.py:258
  11.8 4.2 %collective-permute-start.12 = (bf16[3,2,5120]{2,1,0:T(2,128)(2,1)S(1)}, bf16[3,2,5120]{2,1,0:T(2,128)(2,1)S(1)}, u32[]{:S(2)}, u32[]{:S(2)}) collective-permute-start(bf16[3,2,5120]{2,1,0:T(2,128)(2,1)S(1)} %collective-permute-done.11), channel_id=1, source_target_pairs={{0,1},{1,0},{2,3},{3,2},{4,5},{5,4},{6,7},{7,6},{8,9},{9,8},{10,11... | collective-permute-start | bytes 184328 | tf_op jit(solution)/shard_map/ppermute | solution.py:258
  13.2 4.2 %collective-permute-start.9 = (bf16[3,2,5120]{2,1,0:T(2,128)(2,1)S(1)}, bf16[3,2,5120]{2,1,0:T(2,128)(2,1)S(1)}, u32[]{:S(2)}, u32[]{:S(2)}) collective-permute-start(bf16[3,2,5120]{2,1,0:T(2,128)(2,1)S(1)} %collective-permute-done.7), channel_id=1, source_target_pairs={{0,2},{1,3},{2,0},{3,1},{4,6},{5,7},{6,4},{7,5},{8,10},{9,11},{10,... | collective-permute-start | bytes 184328 | tf_op jit(solution)/shard_map/ppermute | solution.py:258
  13.8 3.5 %collective-permute-start.8 = (bf16[3,2,5120]{2,1,0:T(2,128)(2,1)S(1)}, bf16[3,2,5120]{2,1,0:T(2,128)(2,1)S(1)}, u32[]{:S(2)}, u32[]{:S(2)}) collective-permute-start(bf16[3,2,5120]{2,1,0:T(2,128)(2,1)S(1)} %collective-permute-done.7), channel_id=1, source_target_pairs={{0,1},{1,0},{2,3},{3,2},{4,5},{5,4},{6,7},{7,6},{8,9},{9,8},{10,11... | collective-permute-start | bytes 184328 | tf_op jit(solution)/shard_map/ppermute | solution.py:258
  13.9 3.9 %collective-permute-start.3 = (bf16[3,2,5120]{2,1,0:T(2,128)(2,1)S(1)}, bf16[3,2,5120]{2,1,0:T(2,128)(2,1)S(1)}, u32[]{:S(2)}, u32[]{:S(2)}) collective-permute-start(bf16[3,2,5120]{2,1,0:T(2,128)(2,1)S(1)} %copy-done.2), channel_id=1, source_target_pairs={{0,1},{1,0},{2,3},{3,2},{4,5},{5,4},{6,7},{7,6},{8,9},{9,8},{10,11... | collective-permute-start | bytes 184328 | tf_op jit(solution)/shard_map/ppermute | solution.py:258
  15.9 2.2 %collective-permute-start.4 = (bf16[3,2,5120]{2,1,0:T(2,128)(2,1)S(1)}, bf16[3,2,5120]{2,1,0:T(2,128)(2,1)S(1)}, u32[]{:S(2)}, u32[]{:S(2)}) collective-permute-start(bf16[3,2,5120]{2,1,0:T(2,128)(2,1)S(1)} %collective-permute-done.1), channel_id=1, source_target_pairs={{0,1},{1,0},{2,3},{3,2},{4,5},{5,4},{6,7},{7,6},{8,9},{9,8},{10,11... | collective-permute-start | bytes 184328 | tf_op jit(solution)/shard_map/ppermute | solution.py:258
  15.9 2.2 %collective-permute-start.5 = (bf16[3,2,5120]{2,1,0:T(2,128)(2,1)S(1)}, bf16[3,2,5120]{2,1,0:T(2,128)(2,1)S(1)}, u32[]{:S(2)}, u32[]{:S(2)}) collective-permute-start(bf16[3,2,5120]{2,1,0:T(2,128)(2,1)S(1)} %collective-permute-done), channel_id=1, source_target_pairs={{0,1},{1,0},{2,3},{3,2},{4,5},{5,4},{6,7},{7,6},{8,9},{9,8},{10,11... | collective-permute-start | bytes 184328 | tf_op jit(solution)/shard_map/ppermute | solution.py:258
  17.4 1.2 %collective-permute-start.6 = (bf16[3,2,5120]{2,1,0:T(2,128)(2,1)S(1)}, bf16[3,2,5120]{2,1,0:T(2,128)(2,1)S(1)}, u32[]{:S(2)}, u32[]{:S(2)}) collective-permute-start(bf16[3,2,5120]{2,1,0:T(2,128)(2,1)S(1)} %collective-permute-done.2), channel_id=1, source_target_pairs={{0,1},{1,0},{2,3},{3,2},{4,5},{5,4},{6,7},{7,6},{8,9},{9,8},{10,11... | collective-permute-start | bytes 184328 | tf_op jit(solution)/shard_map/ppermute | solution.py:258
  17.4 1.4 %collective-permute-start.14 = (bf16[3,2,5120]{2,1,0:T(2,128)(2,1)S(1)}, bf16[3,2,5120]{2,1,0:T(2,128)(2,1)S(1)}, u32[]{:S(2)}, u32[]{:S(2)}) collective-permute-start(bf16[3,2,5120]{2,1,0:T(2,128)(2,1)S(1)} %collective-permute-done.13), channel_id=1, source_target_pairs={{0,1},{1,0},{2,3},{3,2},{4,5},{5,4},{6,7},{7,6},{8,9},{9,8},{10,11... | collective-permute-start | bytes 184328 | tf_op jit(solution)/shard_map/ppermute | solution.py:258
  17.9 1.2 %collective-permute-start.10 = (bf16[3,2,5120]{2,1,0:T(2,128)(2,1)S(1)}, bf16[3,2,5120]{2,1,0:T(2,128)(2,1)S(1)}, u32[]{:S(2)}, u32[]{:S(2)}) collective-permute-start(bf16[3,2,5120]{2,1,0:T(2,128)(2,1)S(1)} %collective-permute-done.9), channel_id=1, source_target_pairs={{0,1},{1,0},{2,3},{3,2},{4,5},{5,4},{6,7},{7,6},{8,9},{9,8},{10,11... | collective-permute-start | bytes 184328 | tf_op jit(solution)/shard_map/ppermute | solution.py:258
  21.2 4.3 %collective-permute-start.17 = (bf16[48,128]{1,0:T(8,128)(2,1)S(1)}, bf16[48,128]{1,0:T(8,128)(2,1)S(1)}, u32[]{:S(2)}, u32[]{:S(2)}) collective-permute-start(bf16[48,128]{1,0:T(8,128)(2,1)S(1)} %get-tuple-element.45), channel_id=1, source_target_pairs={{0,3},{1,2},{2,1},{3,0},{4,7},{5,6},{6,5},{7,4},{8,11},{9,10},{10,... | collective-permute-start | bytes 36872 | tf_op jit(solution)/shard_map/ppermute | solution.py:258
  21.5 4.0 %collective-permute-start.16 = (bf16[48,128]{1,0:T(8,128)(2,1)S(1)}, bf16[48,128]{1,0:T(8,128)(2,1)S(1)}, u32[]{:S(2)}, u32[]{:S(2)}) collective-permute-start(bf16[48,128]{1,0:T(8,128)(2,1)S(1)} %get-tuple-element.45), channel_id=1, source_target_pairs={{0,2},{1,3},{2,0},{3,1},{4,6},{5,7},{6,4},{7,5},{8,10},{9,11},{10,... | collective-permute-start | bytes 36872 | tf_op jit(solution)/shard_map/ppermute | solution.py:258
  23.1 2.5 %collective-permute-start.15 = (bf16[48,128]{1,0:T(8,128)(2,1)S(1)}, bf16[48,128]{1,0:T(8,128)(2,1)S(1)}, u32[]{:S(2)}, u32[]{:S(2)}) collective-permute-start(bf16[48,128]{1,0:T(8,128)(2,1)S(1)} %get-tuple-element.45), channel_id=1, source_target_pairs={{0,1},{1,0},{2,3},{3,2},{4,5},{5,4},{6,7},{7,6},{8,9},{9,8},{10,11... | collective-permute-start | bytes 36872 | tf_op jit(solution)/shard_map/ppermute | solution.py:258
  25.5 7.0 %copy-start = (bf16[64,64,320]{2,1,0:T(8,128)(2,1)S(1)}, bf16[64,64,320]{2,1,0:T(8,128)(2,1)}, u32[]{:S(2)}) copy-start(bf16[64,64,320]{2,1,0:T(8,128)(2,1)} %param.12) | copy-start | bytes 7864324
  25.6 5.6 %collective-permute-start.20 = (bf16[48,128]{1,0:T(8,128)(2,1)S(1)}, bf16[48,128]{1,0:T(8,128)(2,1)S(1)}, u32[]{:S(2)}, u32[]{:S(2)}) collective-permute-start(bf16[48,128]{1,0:T(8,128)(2,1)S(1)} %add_add_fusion.refs_0_), channel_id=1, source_target_pairs={{0,12},{1,13},{2,14},{3,15},{4,8},{5,9},{6,10},{7,11},{8,4},{9,5},... | collective-permute-start | bytes 36872 | tf_op jit(solution)/shard_map/ppermute | solution.py:258
  28.0 4.6 %collective-permute-start.19 = (bf16[48,128]{1,0:T(8,128)(2,1)S(1)}, bf16[48,128]{1,0:T(8,128)(2,1)S(1)}, u32[]{:S(2)}, u32[]{:S(2)}) collective-permute-start(bf16[48,128]{1,0:T(8,128)(2,1)S(1)} %add_add_fusion.refs_0_), channel_id=1, source_target_pairs={{0,8},{1,9},{2,10},{3,11},{4,12},{5,13},{6,14},{7,15},{8,0},{9,1},... | collective-permute-start | bytes 36872 | tf_op jit(solution)/shard_map/ppermute | solution.py:258
  28.1 4.5 %collective-permute-start.18 = (bf16[48,128]{1,0:T(8,128)(2,1)S(1)}, bf16[48,128]{1,0:T(8,128)(2,1)S(1)}, u32[]{:S(2)}, u32[]{:S(2)}) collective-permute-start(bf16[48,128]{1,0:T(8,128)(2,1)S(1)} %add_add_fusion.refs_0_), channel_id=1, source_target_pairs={{0,4},{1,5},{2,6},{3,7},{4,0},{5,1},{6,2},{7,3},{8,12},{9,13},{10,... | collective-permute-start | bytes 36872 | tf_op jit(solution)/shard_map/ppermute | solution.py:258
  34.2 13.1 %all-to-all-start = ((bf16[16,8,3,2,128]{4,3,2,1,0:T(2,128)(2,1)}), bf16[16,8,3,2,128]{4,3,2,1,0:T(2,128)(2,1)S(1)}, u32[]{:S(2)}, u32[]{:S(2)}) async-start(bf16[16,8,3,2,128]{4,3,2,1,0:T(2,128)(2,1)} %update_values.1), calls=%async_computation | async-start | bytes 393216 | tf_op jit(solution)/shard_map/all_to_all | solution.py:679

commit v17 on v16

--- a/solution.py
+++ b/solution.py
@@ -519,9 +519,11 @@
     sine = sin_ref[...][:rows]
     left = lax.broadcasted_iota(jnp.int32, (rows, HD), 1) < HD // 2
 
+    flat = pieces_ref.reshape(count, pieces_ref.shape[1], rows, HD)
+
     def halves(chip, at):
         return [
-            [pieces_ref[2 * chip + core, at + c].reshape(rows, HD).astype(jnp.float32) for c in range(each)]
+            [flat[2 * chip + core, at + c].astype(jnp.float32) for c in range(each)]
             for core in range(2)
         ]
 
@@ -581,8 +583,8 @@
         old = jnp.where(live, scores[c] * (HD**-0.5), masked_score)
         new = jnp.where(new_live, fresh[c] * (HD**-0.5), masked_score)
         top = jnp.maximum(jnp.max(old, axis=1, keepdims=True), jnp.max(new, axis=1, keepdims=True))
-        old = jnp.where(live, jnp.exp(old - top), 0.0)
-        new = jnp.where(new_live, jnp.exp(new - top), 0.0)
+        old = jnp.exp(old - top)
+        new = jnp.exp(new - top)
         totals.append(jnp.sum(old, axis=1, keepdims=True) + jnp.sum(new, axis=1, keepdims=True))
         weights.append(old.astype(jnp.bfloat16))
         fresh_weights.append(new.astype(jnp.bfloat16))
@@ -592,8 +594,9 @@
         vn = vn_ref[c].astype(jnp.bfloat16)
         mixed = jnp.dot(weights[c], values, preferred_element_type=jnp.float32)
         mixed = mixed + jnp.dot(fresh_weights[c], vn, preferred_element_type=jnp.float32)
-        mixed = jnp.where(own_head, mixed / totals[c], 0.0)
-        out = jnp.sum(mixed.reshape(rows, HEAD_BLOCK, lanes), axis=1).astype(out_ref.dtype)
+        mixed = jnp.sum(jnp.where(own_head, mixed, 0.0).reshape(rows, HEAD_BLOCK, lanes), axis=1)
+        total = jnp.sum(jnp.where(own_head, totals[c], 0.0).reshape(rows, HEAD_BLOCK, lanes), axis=1)
+        out = (mixed / total).astype(out_ref.dtype)
         for t in range(steps):
             for h in range(heads):
                 out_ref[t, c * heads + h] = out[2 * t : 2 * t + 2, h * HD : (h + 1) * HD]

time: 51.6 us -> 51.7 us (level)
  transfers between devices with their start and end apart: 22 -> 22, of which waited for: 9 -> 9; matrix products, arithmetic and copies ran while one was open for 3% -> 3% of each run, Pallas kernels for 20% -> 19%
where the time goes in v17:
time: 51.7 us; the launch traced here: 51.5 us
  starting transfers between devices  20.9 us (40%)
  Pallas kernels  17.7 us (34%)
  waiting for transfers between devices  10.9 us (21%)
  other arithmetic  1.53 us (3%)
    ppermute x21, starting transfers between devices, trade(): return lax.ppermute(value, 'replica', [(i, i ^ mask) for i in range(count)])  16.8 us
    ppermute x21, waiting for transfers between devices, trade(): return lax.ppermute(value, 'replica', [(i, i ^ mask) for i in range(count)])  8.49 us
    pallas_call x1, Pallas kernels, cache_by_head(): pl.pallas_call(functools.partial(cache_kernel, first), out_shape=(jax.Sha...  6.4 us
    all_to_all x1, starting transfers between devices, chip_plan(): lax.all_to_all(send, 'replica', split_axis=0, concat_axis=0, tiled=True)  4.1 us
    pallas_call x1, Pallas kernels, attend(): pl.pallas_call(attend_kernel, out_shape=jax.ShapeDtypeStruct((steps, head...  3.98 us
    pallas_call x3, Pallas kernels, project(): pl.pallas_call(functools.partial(project_kernel, which), out_shape=chunks...  3.44 us
    all_to_all x1, waiting for transfers between devices, chip_plan(): lax.all_to_all(send, 'replica', split_axis=0, concat_axis=0, tiled=True)  2.45 us
    pallas_call x1, Pallas kernels, low_of(): pl.pallas_call(functools.partial(low_kernel, count), out_shape=(jax.Shape...  2.06 us
  transfers between devices with their start and end apart: 22, of which 9 were waited for; matrix products, arithmetic and copies ran while one was open for 3% of the time, Pallas kernels for 19%

profile of v17, /device:TPU:0, one launch (start us, length us, event | category | flops | bytes accessed | tf_op | source)
XLA Modules:
  0.0 51.5 jit_solution(17531641747963403194)
XLA Ops:
  0.0 3.0 %collective-permute-start.1 = (bf16[3,2,5120]{2,1,0:T(2,128)(2,1)}, bf16[3,2,5120]{2,1,0:T(2,128)(2,1)S(1)}, u32[]{:S(2)}, u32[]{:S(2)}) collective-permute-start(bf16[3,2,5120]{2,1,0:T(2,128)(2,1)} %param.9), channel_id=1, source_target_pairs={{0,2},{1,3},{2,0},{3,1},{4,6},{5,7},{6,4},{7,5},{8,10},{9,11},{10,... | collective-permute-start | bytes 184328 | tf_op jit(solution)/shard_map/ppermute | solution.py:258
  3.0 1.6 %collective-permute-start = (bf16[3,2,5120]{2,1,0:T(2,128)(2,1)}, bf16[3,2,5120]{2,1,0:T(2,128)(2,1)S(1)}, u32[]{:S(2)}, u32[]{:S(2)}) collective-permute-start(bf16[3,2,5120]{2,1,0:T(2,128)(2,1)} %param.9), channel_id=1, source_target_pairs={{0,4},{1,5},{2,6},{3,7},{4,0},{5,1},{6,2},{7,3},{8,12},{9,13},{10,... | collective-permute-start | bytes 184328 | tf_op jit(solution)/shard_map/ppermute | solution.py:258
  4.5 2.5 %collective-permute-start.11 = (bf16[3,2,5120]{2,1,0:T(2,128)(2,1)}, bf16[3,2,5120]{2,1,0:T(2,128)(2,1)S(1)}, u32[]{:S(2)}, u32[]{:S(2)}) collective-permute-start(bf16[3,2,5120]{2,1,0:T(2,128)(2,1)} %param.9), channel_id=1, source_target_pairs={{0,12},{1,13},{2,14},{3,15},{4,8},{5,9},{6,10},{7,11},{8,4},{9,5},... | collective-permute-start | bytes 184328 | tf_op jit(solution)/shard_map/ppermute | solution.py:258
  7.0 0.1 collective-permute-start.7
  7.2 0.9 %select_reduce_fusion.1 = s32[32]{0:T(128)S(1)} fusion(s32[64]{0:T(128)} %param.13, s32[32]{0:T(128)} %param.14), kind=kLoop, calls=%fused_computation.1 | loop fusion | flops 6112 | bytes 512 | tf_op jit(solution)/shard_map/reduce_sum | solution.py:646
  8.0 0.0 slice-start
  8.0 0.0 copy-start.3
  8.0 0.0 copy-start.4
  8.1 0.0 copy-start.2
  8.1 0.0 copy-start.1
  8.1 0.2 index_work.1
  8.3 0.6 %collective-permute-start.2 = (bf16[3,2,5120]{2,1,0:T(2,128)(2,1)S(1)}, bf16[3,2,5120]{2,1,0:T(2,128)(2,1)S(1)}, u32[]{:S(2)}, u32[]{:S(2)}) collective-permute-start(bf16[3,2,5120]{2,1,0:T(2,128)(2,1)S(1)} %collective-permute-done), channel_id=1, source_target_pairs={{0,2},{1,3},{2,0},{3,1},{4,6},{5,7},{6,4},{7,5},{8,10},{9,11},{10,... | collective-permute-start | bytes 184328 | tf_op jit(solution)/shard_map/ppermute | solution.py:258
  8.9 2.4 %collective-permute-done.11 = bf16[3,2,5120]{2,1,0:T(2,128)(2,1)S(1)} collective-permute-done((bf16[3,2,5120]{2,1,0:T(2,128)(2,1)}, bf16[3,2,5120]{2,1,0:T(2,128)(2,1)S(1)}, u32[]{:S(2)}, u32[]{:S(2)}) %collective-permute-start.11) | collective-permute-done | bytes 61472 | tf_op jit(solution)/shard_map/ppermute | solution.py:258
  11.3 0.5 collective-permute-start.13
  11.8 0.1 select_reduce_fusion
  11.9 1.3 %collective-permute-done.7 = bf16[3,2,5120]{2,1,0:T(2,128)(2,1)S(1)} collective-permute-done((bf16[3,2,5120]{2,1,0:T(2,128)(2,1)}, bf16[3,2,5120]{2,1,0:T(2,128)(2,1)S(1)}, u32[]{:S(2)}, u32[]{:S(2)}) %collective-permute-start.7) | collective-permute-done | bytes 61472 | tf_op jit(solution)/shard_map/ppermute | solution.py:258
  13.2 0.5 collective-permute-start.9
  13.7 0.2 fusion.3
  13.8 0.1 collective-permute-start.8
  13.9 0.5 collective-permute-start.3
  14.4 0.1 and_convert_fusion.live_ref
  14.5 1.4 %collective-permute-done.13 = bf16[3,2,5120]{2,1,0:T(2,128)(2,1)S(1)} collective-permute-done((bf16[3,2,5120]{2,1,0:T(2,128)(2,1)S(1)}, bf16[3,2,5120]{2,1,0:T(2,128)(2,1)S(1)}, u32[]{:S(2)}, u32[]{:S(2)}) %collective-permute-start.13) | collective-permute-done | bytes 61472 | tf_op jit(solution)/shard_map/ppermute | solution.py:258
  15.9 0.5 collective-permute-start.5
  16.4 0.9 %collective-permute-done.9 = bf16[3,2,5120]{2,1,0:T(2,128)(2,1)S(1)} collective-permute-done((bf16[3,2,5120]{2,1,0:T(2,128)(2,1)S(1)}, bf16[3,2,5120]{2,1,0:T(2,128)(2,1)S(1)}, u32[]{:S(2)}, u32[]{:S(2)}) %collective-permute-start.9) | collective-permute-done | bytes 61472 | tf_op jit(solution)/shard_map/ppermute | solution.py:258
  17.4 0.5 collective-permute-start.14
  17.9 0.1 collective-permute-start.10
  18.0 0.2 select_reduce_fusion.2
  18.2 0.5 collective-permute-done.6
  18.6 0.2 collective-permute-done.14
  18.8 0.4 collective-permute-done.10
  19.1 2.1 %low_rows.1 = (bf16[3,40,16,2,128]{4,3,2,1,0:T(2,128)(2,1)S(1)}, bf16[48,128]{1,0:T(8,128)(2,1)S(1)}) custom-call(s32[1]{0:T(128)} %bitcast.1.me_ref, s32[1,96]{1,0:T(1,128)S(1)} %get-tuple-element.40.slot_ref, bf16[4,64,5120]{2,1,0:T(8,128)(2,1)S(1)} %copy-done.1, bf16[3,40,2,128]{3,2,1,0:T(2,128)(2,1)} %bitcast.82, bf16[3,40,2,128]{3,2,1,0:T(2,128)(2,1)S(1)} %bitcast.74, ...), custom_call_target="tpu_custom_call" | custom-call | flops 100000000 | bytes 4000000 | tf_op jit(solution)/shard_map/low_rows/pallas_call | solution.py:402
  21.2 0.3 collective-permute-start.17
  21.5 1.5 %collective-permute-start.16 = (bf16[48,128]{1,0:T(8,128)(2,1)S(1)}, bf16[48,128]{1,0:T(8,128)(2,1)S(1)}, u32[]{:S(2)}, u32[]{:S(2)}) collective-permute-start(bf16[48,128]{1,0:T(8,128)(2,1)S(1)} %get-tuple-element.45), channel_id=1, source_target_pairs={{0,2},{1,3},{2,0},{3,1},{4,6},{5,7},{6,4},{7,5},{8,10},{9,11},{10,... | collective-permute-start | bytes 36872 | tf_op jit(solution)/shard_map/ppermute | solution.py:258
  23.1 0.1 collective-permute-start.15
  23.2 1.2 %project.4.key_ref = bf16[3,3,16,2,128]{4,3,2,1,0:T(2,128)(2,1)S(1)} custom-call(bf16[3,40,16,2,128]{4,3,2,1,0:T(2,128)(2,1)S(1)} %get-tuple-element.46.x_ref, bf16[3,320,5120]{2,1,0:T(8,128)(2,1)S(1)} %bitcast.61), custom_call_target="tpu_custom_call" | custom-call | flops 500000000 | bytes 4000000 | tf_op jit(solution)/shard_map/project/pallas_call | solution.py:445
  24.4 1.1 %project.3.query_ref = bf16[3,3,16,2,128]{4,3,2,1,0:T(2,128)(2,1)S(1)} custom-call(bf16[3,40,16,2,128]{4,3,2,1,0:T(2,128)(2,1)S(1)} %get-tuple-element.46.x_ref, bf16[3,320,5120]{2,1,0:T(8,128)(2,1)S(1)} %bitcast.62), custom_call_target="tpu_custom_call" | custom-call | flops 500000000 | bytes 4000000 | tf_op jit(solution)/shard_map/project/pallas_call | solution.py:445
  25.5 0.0 copy-start
  25.6 2.4 %collective-permute-start.20 = (bf16[48,128]{1,0:T(8,128)(2,1)S(1)}, bf16[48,128]{1,0:T(8,128)(2,1)S(1)}, u32[]{:S(2)}, u32[]{:S(2)}) collective-permute-start(bf16[48,128]{1,0:T(8,128)(2,1)S(1)} %add_add_fusion.refs_0_), channel_id=1, source_target_pairs={{0,12},{1,13},{2,14},{3,15},{4,8},{5,9},{6,10},{7,11},{8,4},{9,5},... | collective-permute-start | bytes 36872 | tf_op jit(solution)/shard_map/ppermute | solution.py:258
  28.0 0.1 collective-permute-start.19
  28.1 1.9 %collective-permute-start.18 = (bf16[48,128]{1,0:T(8,128)(2,1)S(1)}, bf16[48,128]{1,0:T(8,128)(2,1)S(1)}, u32[]{:S(2)}, u32[]{:S(2)}) collective-permute-start(bf16[48,128]{1,0:T(8,128)(2,1)S(1)} %add_add_fusion.refs_0_), channel_id=1, source_target_pairs={{0,4},{1,5},{2,6},{3,7},{4,0},{5,1},{6,2},{7,3},{8,12},{9,13},{10,... | collective-permute-start | bytes 36872 | tf_op jit(solution)/shard_map/ppermute | solution.py:258
  30.0 1.1 %project.5.base_ref = f32[96,320]{1,0:T(8,128)S(1)} custom-call(bf16[3,40,16,2,128]{4,3,2,1,0:T(2,128)(2,1)S(1)} %get-tuple-element.46.x_ref, bf16[3,320,5120]{2,1,0:T(8,128)(2,1)S(1)} %bitcast.63), custom_call_target="tpu_custom_call" | custom-call | flops 500000000 | bytes 4000000 | tf_op jit(solution)/shard_map/project/pallas_call | solution.py:445
  31.1 1.4 %collective-permute-done.19.refs_2_ = bf16[48,128]{1,0:T(8,128)(2,1)S(1)} collective-permute-done((bf16[48,128]{1,0:T(8,128)(2,1)S(1)}, bf16[48,128]{1,0:T(8,128)(2,1)S(1)}, u32[]{:S(2)}, u32[]{:S(2)}) %collective-permute-start.19) | collective-permute-done | bytes 12320 | tf_op jit(solution)/shard_map/ppermute | solution.py:258
  32.6 1.6 %update_values.1 = bf16[16,8,3,2,128]{4,3,2,1,0:T(2,128)(2,1)} custom-call(s32[96,1]{1,0:T(8,128)S(1)} %get-tuple-element.38.stored_ref, bf16[3,3,16,2,128]{4,3,2,1,0:T(2,128)(2,1)S(1)} %project.3.query_ref, bf16[3,3,16,2,128]{4,3,2,1,0:T(2,128)(2,1)S(1)} %project.4.key_ref, f32[96,320]{1,0:T(8,128)S(1)} %project.5.base_ref, bf16[4096,320]{1,0:T(8,128)(2,1)S(1)} %bitcast.64, ...), custom_call_target="tpu_custom_call" | custom-call | flops 300000000 | bytes 4000000 | tf_op jit(solution)/shard_map/update_values/pallas_call | solution.py:485
  34.2 4.1 %all-to-all-start = ((bf16[16,8,3,2,128]{4,3,2,1,0:T(2,128)(2,1)}), bf16[16,8,3,2,128]{4,3,2,1,0:T(2,128)(2,1)S(1)}, u32[]{:S(2)}, u32[]{:S(2)}) async-start(bf16[16,8,3,2,128]{4,3,2,1,0:T(2,128)(2,1)} %update_values.1), calls=%async_computation | async-start | bytes 393216 | tf_op jit(solution)/shard_map/all_to_all | solution.py:682
  38.3 0.1 fusion
  38.5 6.4 %cache_by_head.1 = (bf16[40,256,128]{2,1,0:T(8,128)(2,1)S(1)}, bf16[40,256,128]{2,1,0:T(8,128)(2,1)}) custom-call(bf16[256,40,2,128]{3,2,1,0:T(2,128)(2,1)} %bitcast.81), custom_call_target="tpu_custom_call" | custom-call | bytes 12000000 | tf_op jit(solution)/shard_map/cache_by_head/pallas_call | solution.py:321
  44.9 2.5 %all-to-all-done.pieces_ref = bf16[16,8,3,2,128]{4,3,2,1,0:T(2,128)(2,1)S(1)} async-done(((bf16[16,8,3,2,128]{4,3,2,1,0:T(2,128)(2,1)}), bf16[16,8,3,2,128]{4,3,2,1,0:T(2,128)(2,1)S(1)}, u32[]{:S(2)}, u32[]{:S(2)}) %all-to-all-start) | async-done | bytes 196640 | tf_op jit(solution)/shard_map/all_to_all | solution.py:682
  47.3 4.0 %attention.1 = bf16[3,40,2,128]{3,2,1,0:T(2,128)(2,1)} custom-call(f32[8,128]{1,0:T(8,128)S(1)} %get-tuple-element.62.cos_ref, f32[8,128]{1,0:T(8,128)S(1)} %get-tuple-element.61.sin_ref, s32[2,256]{1,0:T(2,128)S(1)} %and_convert_fusion.live_ref, bf16[16,8,3,2,128]{4,3,2,1,0:T(2,128)(2,1)S(1)} %all-to-all-done.pieces_ref, ...), custom_call_target="tpu_custom_call" | custom-call | flops 1000000000 | bytes 6000000 | tf_op jit(solution)/shard_map/attention/pallas_call | solution.py:610
  (34 shorter events, 0.1 us)
Async XLA Ops:
  0.0 13.8 %collective-permute-start.1 = (bf16[3,2,5120]{2,1,0:T(2,128)(2,1)}, bf16[3,2,5120]{2,1,0:T(2,128)(2,1)S(1)}, u32[]{:S(2)}, u32[]{:S(2)}) collective-permute-start(bf16[3,2,5120]{2,1,0:T(2,128)(2,1)} %param.9), channel_id=1, source_target_pairs={{0,2},{1,3},{2,0},{3,1},{4,6},{5,7},{6,4},{7,5},{8,10},{9,11},{10,... | collective-permute-start | bytes 184328 | tf_op jit(solution)/shard_map/ppermute | solution.py:258
  3.0 5.3 %collective-permute-start = (bf16[3,2,5120]{2,1,0:T(2,128)(2,1)}, bf16[3,2,5120]{2,1,0:T(2,128)(2,1)S(1)}, u32[]{:S(2)}, u32[]{:S(2)}) collective-permute-start(bf16[3,2,5120]{2,1,0:T(2,128)(2,1)} %param.9), channel_id=1, source_target_pairs={{0,4},{1,5},{2,6},{3,7},{4,0},{5,1},{6,2},{7,3},{8,12},{9,13},{10,... | collective-permute-start | bytes 184328 | tf_op jit(solution)/shard_map/ppermute | solution.py:258
  4.5 6.7 %collective-permute-start.11 = (bf16[3,2,5120]{2,1,0:T(2,128)(2,1)}, bf16[3,2,5120]{2,1,0:T(2,128)(2,1)S(1)}, u32[]{:S(2)}, u32[]{:S(2)}) collective-permute-start(bf16[3,2,5120]{2,1,0:T(2,128)(2,1)} %param.9), channel_id=1, source_target_pairs={{0,12},{1,13},{2,14},{3,15},{4,8},{5,9},{6,10},{7,11},{8,4},{9,5},... | collective-permute-start | bytes 184328 | tf_op jit(solution)/shard_map/ppermute | solution.py:258
  7.0 6.1 %collective-permute-start.7 = (bf16[3,2,5120]{2,1,0:T(2,128)(2,1)}, bf16[3,2,5120]{2,1,0:T(2,128)(2,1)S(1)}, u32[]{:S(2)}, u32[]{:S(2)}) collective-permute-start(bf16[3,2,5120]{2,1,0:T(2,128)(2,1)} %param.9), channel_id=1, source_target_pairs={{0,8},{1,9},{2,10},{3,11},{4,12},{5,13},{6,14},{7,15},{8,0},{9,1},... | collective-permute-start | bytes 184328 | tf_op jit(solution)/shard_map/ppermute | solution.py:258
  8.0 15.1 %slice-start = ((s8[9830400]{0:T(1024)(128)(4,1)}), s8[4194304]{0:T(1024)(128)(4,1)S(1)}, s32[]{:S(2)}) async-start(s8[9830400]{0:T(1024)(128)(4,1)} %bitcast.59), calls=%async_computation.1 | async-start | bytes 8388608
  8.0 3.7 %copy-start.3 = (s32[2,32]{1,0:T(2,128)S(1)}, s32[2,32]{1,0:T(2,128)}, u32[]{:S(2)}) copy-start(s32[2,32]{1,0:T(2,128)} %param.16) | copy-start | bytes 772
  8.0 5.6 %copy-start.4 = (s32[32]{0:T(128)S(1)}, s32[32]{0:T(128)}, u32[]{:S(2)}) copy-start(s32[32]{0:T(128)} %param.15) | copy-start | bytes 388
  8.1 5.9 %copy-start.2 = (bf16[3,2,5120]{2,1,0:T(2,128)(2,1)S(1)}, bf16[3,2,5120]{2,1,0:T(2,128)(2,1)}, u32[]{:S(2)}) copy-start(bf16[3,2,5120]{2,1,0:T(2,128)(2,1)} %param.9) | copy-start | bytes 184324
  8.1 11.1 %copy-start.1 = (bf16[4,64,5120]{2,1,0:T(8,128)(2,1)S(1)}, bf16[4,64,5120]{2,1,0:T(8,128)(2,1)}, u32[]{:S(2)}) copy-start(bf16[4,64,5120]{2,1,0:T(8,128)(2,1)} %down_ref.1) | copy-start | bytes 7864324
  8.1 15.1 %slice-start.1 = ((s8[9830400]{0:T(1024)(128)(4,1)}), s8[4194304]{0:T(1024)(128)(4,1)S(1)}, s32[]{:S(2)}) async-start(s8[9830400]{0:T(1024)(128)(4,1)} %bitcast.59), calls=%async_computation.2 | async-start | bytes 8388608
  8.1 15.1 %slice-start.2 = ((s8[9830400]{0:T(1024)(128)(4,1)}), s8[1441792]{0:T(1024)(128)(4,1)S(1)}, s32[]{:S(2)}) async-start(s8[9830400]{0:T(1024)(128)(4,1)} %bitcast.59), calls=%async_computation.3 | async-start | bytes 2883584
  8.3 5.6 %collective-permute-start.2 = (bf16[3,2,5120]{2,1,0:T(2,128)(2,1)S(1)}, bf16[3,2,5120]{2,1,0:T(2,128)(2,1)S(1)}, u32[]{:S(2)}, u32[]{:S(2)}) collective-permute-start(bf16[3,2,5120]{2,1,0:T(2,128)(2,1)S(1)} %collective-permute-done), channel_id=1, source_target_pairs={{0,2},{1,3},{2,0},{3,1},{4,6},{5,7},{6,4},{7,5},{8,10},{9,11},{10,... | collective-permute-start | bytes 184328 | tf_op jit(solution)/shard_map/ppermute | solution.py:258
  11.3 4.7 %collective-permute-start.13 = (bf16[3,2,5120]{2,1,0:T(2,128)(2,1)S(1)}, bf16[3,2,5120]{2,1,0:T(2,128)(2,1)S(1)}, u32[]{:S(2)}, u32[]{:S(2)}) collective-permute-start(bf16[3,2,5120]{2,1,0:T(2,128)(2,1)S(1)} %collective-permute-done.11), channel_id=1, source_target_pairs={{0,2},{1,3},{2,0},{3,1},{4,6},{5,7},{6,4},{7,5},{8,10},{9,11},{10,... | collective-permute-start | bytes 184328 | tf_op jit(solution)/shard_map/ppermute | solution.py:258
  11.8 4.2 %collective-permute-start.12 = (bf16[3,2,5120]{2,1,0:T(2,128)(2,1)S(1)}, bf16[3,2,5120]{2,1,0:T(2,128)(2,1)S(1)}, u32[]{:S(2)}, u32[]{:S(2)}) collective-permute-start(bf16[3,2,5120]{2,1,0:T(2,128)(2,1)S(1)} %collective-permute-done.11), channel_id=1, source_target_pairs={{0,1},{1,0},{2,3},{3,2},{4,5},{5,4},{6,7},{7,6},{8,9},{9,8},{10,11... | collective-permute-start | bytes 184328 | tf_op jit(solution)/shard_map/ppermute | solution.py:258
  13.2 4.2 %collective-permute-start.9 = (bf16[3,2,5120]{2,1,0:T(2,128)(2,1)S(1)}, bf16[3,2,5120]{2,1,0:T(2,128)(2,1)S(1)}, u32[]{:S(2)}, u32[]{:S(2)}) collective-permute-start(bf16[3,2,5120]{2,1,0:T(2,128)(2,1)S(1)} %collective-permute-done.7), channel_id=1, source_target_pairs={{0,2},{1,3},{2,0},{3,1},{4,6},{5,7},{6,4},{7,5},{8,10},{9,11},{10,... | collective-permute-start | bytes 184328 | tf_op jit(solution)/shard_map/ppermute | solution.py:258
  13.8 3.5 %collective-permute-start.8 = (bf16[3,2,5120]{2,1,0:T(2,128)(2,1)S(1)}, bf16[3,2,5120]{2,1,0:T(2,128)(2,1)S(1)}, u32[]{:S(2)}, u32[]{:S(2)}) collective-permute-start(bf16[3,2,5120]{2,1,0:T(2,128)(2,1)S(1)} %collective-permute-done.7), channel_id=1, source_target_pairs={{0,1},{1,0},{2,3},{3,2},{4,5},{5,4},{6,7},{7,6},{8,9},{9,8},{10,11... | collective-permute-start | bytes 184328 | tf_op jit(solution)/shard_map/ppermute | solution.py:258
  13.9 3.9 %collective-permute-start.3 = (bf16[3,2,5120]{2,1,0:T(2,128)(2,1)S(1)}, bf16[3,2,5120]{2,1,0:T(2,128)(2,1)S(1)}, u32[]{:S(2)}, u32[]{:S(2)}) collective-permute-start(bf16[3,2,5120]{2,1,0:T(2,128)(2,1)S(1)} %copy-done.2), channel_id=1, source_target_pairs={{0,1},{1,0},{2,3},{3,2},{4,5},{5,4},{6,7},{7,6},{8,9},{9,8},{10,11... | collective-permute-start | bytes 184328 | tf_op jit(solution)/shard_map/ppermute | solution.py:258
  15.9 2.2 %collective-permute-start.4 = (bf16[3,2,5120]{2,1,0:T(2,128)(2,1)S(1)}, bf16[3,2,5120]{2,1,0:T(2,128)(2,1)S(1)}, u32[]{:S(2)}, u32[]{:S(2)}) collective-permute-start(bf16[3,2,5120]{2,1,0:T(2,128)(2,1)S(1)} %collective-permute-done.1), channel_id=1, source_target_pairs={{0,1},{1,0},{2,3},{3,2},{4,5},{5,4},{6,7},{7,6},{8,9},{9,8},{10,11... | collective-permute-start | bytes 184328 | tf_op jit(solution)/shard_map/ppermute | solution.py:258
  15.9 2.2 %collective-permute-start.5 = (bf16[3,2,5120]{2,1,0:T(2,128)(2,1)S(1)}, bf16[3,2,5120]{2,1,0:T(2,128)(2,1)S(1)}, u32[]{:S(2)}, u32[]{:S(2)}) collective-permute-start(bf16[3,2,5120]{2,1,0:T(2,128)(2,1)S(1)} %collective-permute-done), channel_id=1, source_target_pairs={{0,1},{1,0},{2,3},{3,2},{4,5},{5,4},{6,7},{7,6},{8,9},{9,8},{10,11... | collective-permute-start | bytes 184328 | tf_op jit(solution)/shard_map/ppermute | solution.py:258
  17.4 1.2 %collective-permute-start.6 = (bf16[3,2,5120]{2,1,0:T(2,128)(2,1)S(1)}, bf16[3,2,5120]{2,1,0:T(2,128)(2,1)S(1)}, u32[]{:S(2)}, u32[]{:S(2)}) collective-permute-start(bf16[3,2,5120]{2,1,0:T(2,128)(2,1)S(1)} %collective-permute-done.2), channel_id=1, source_target_pairs={{0,1},{1,0},{2,3},{3,2},{4,5},{5,4},{6,7},{7,6},{8,9},{9,8},{10,11... | collective-permute-start | bytes 184328 | tf_op jit(solution)/shard_map/ppermute | solution.py:258
  17.4 1.4 %collective-permute-start.14 = (bf16[3,2,5120]{2,1,0:T(2,128)(2,1)S(1)}, bf16[3,2,5120]{2,1,0:T(2,128)(2,1)S(1)}, u32[]{:S(2)}, u32[]{:S(2)}) collective-permute-start(bf16[3,2,5120]{2,1,0:T(2,128)(2,1)S(1)} %collective-permute-done.13), channel_id=1, source_target_pairs={{0,1},{1,0},{2,3},{3,2},{4,5},{5,4},{6,7},{7,6},{8,9},{9,8},{10,11... | collective-permute-start | bytes 184328 | tf_op jit(solution)/shard_map/ppermute | solution.py:258
  17.9 1.2 %collective-permute-start.10 = (bf16[3,2,5120]{2,1,0:T(2,128)(2,1)S(1)}, bf16[3,2,5120]{2,1,0:T(2,128)(2,1)S(1)}, u32[]{:S(2)}, u32[]{:S(2)}) collective-permute-start(bf16[3,2,5120]{2,1,0:T(2,128)(2,1)S(1)} %collective-permute-done.9), channel_id=1, source_target_pairs={{0,1},{1,0},{2,3},{3,2},{4,5},{5,4},{6,7},{7,6},{8,9},{9,8},{10,11... | collective-permute-start | bytes 184328 | tf_op jit(solution)/shard_map/ppermute | solution.py:258
  21.2 4.3 %collective-permute-start.17 = (bf16[48,128]{1,0:T(8,128)(2,1)S(1)}, bf16[48,128]{1,0:T(8,128)(2,1)S(1)}, u32[]{:S(2)}, u32[]{:S(2)}) collective-permute-start(bf16[48,128]{1,0:T(8,128)(2,1)S(1)} %get-tuple-element.45), channel_id=1, source_target_pairs={{0,3},{1,2},{2,1},{3,0},{4,7},{5,6},{6,5},{7,4},{8,11},{9,10},{10,... | collective-permute-start | bytes 36872 | tf_op jit(solution)/shard_map/ppermute | solution.py:258
  21.5 4.0 %collective-permute-start.16 = (bf16[48,128]{1,0:T(8,128)(2,1)S(1)}, bf16[48,128]{1,0:T(8,128)(2,1)S(1)}, u32[]{:S(2)}, u32[]{:S(2)}) collective-permute-start(bf16[48,128]{1,0:T(8,128)(2,1)S(1)} %get-tuple-element.45), channel_id=1, source_target_pairs={{0,2},{1,3},{2,0},{3,1},{4,6},{5,7},{6,4},{7,5},{8,10},{9,11},{10,... | collective-permute-start | bytes 36872 | tf_op jit(solution)/shard_map/ppermute | solution.py:258
  23.1 2.5 %collective-permute-start.15 = (bf16[48,128]{1,0:T(8,128)(2,1)S(1)}, bf16[48,128]{1,0:T(8,128)(2,1)S(1)}, u32[]{:S(2)}, u32[]{:S(2)}) collective-permute-start(bf16[48,128]{1,0:T(8,128)(2,1)S(1)} %get-tuple-element.45), channel_id=1, source_target_pairs={{0,1},{1,0},{2,3},{3,2},{4,5},{5,4},{6,7},{7,6},{8,9},{9,8},{10,11... | collective-permute-start | bytes 36872 | tf_op jit(solution)/shard_map/ppermute | solution.py:258
  25.5 7.0 %copy-start = (bf16[64,64,320]{2,1,0:T(8,128)(2,1)S(1)}, bf16[64,64,320]{2,1,0:T(8,128)(2,1)}, u32[]{:S(2)}) copy-start(bf16[64,64,320]{2,1,0:T(8,128)(2,1)} %param.12) | copy-start | bytes 7864324
  25.6 5.6 %collective-permute-start.20 = (bf16[48,128]{1,0:T(8,128)(2,1)S(1)}, bf16[48,128]{1,0:T(8,128)(2,1)S(1)}, u32[]{:S(2)}, u32[]{:S(2)}) collective-permute-start(bf16[48,128]{1,0:T(8,128)(2,1)S(1)} %add_add_fusion.refs_0_), channel_id=1, source_target_pairs={{0,12},{1,13},{2,14},{3,15},{4,8},{5,9},{6,10},{7,11},{8,4},{9,5},... | collective-permute-start | bytes 36872 | tf_op jit(solution)/shard_map/ppermute | solution.py:258
  28.0 4.6 %collective-permute-start.19 = (bf16[48,128]{1,0:T(8,128)(2,1)S(1)}, bf16[48,128]{1,0:T(8,128)(2,1)S(1)}, u32[]{:S(2)}, u32[]{:S(2)}) collective-permute-start(bf16[48,128]{1,0:T(8,128)(2,1)S(1)} %add_add_fusion.refs_0_), channel_id=1, source_target_pairs={{0,8},{1,9},{2,10},{3,11},{4,12},{5,13},{6,14},{7,15},{8,0},{9,1},... | collective-permute-start | bytes 36872 | tf_op jit(solution)/shard_map/ppermute | solution.py:258
  28.1 4.5 %collective-permute-start.18 = (bf16[48,128]{1,0:T(8,128)(2,1)S(1)}, bf16[48,128]{1,0:T(8,128)(2,1)S(1)}, u32[]{:S(2)}, u32[]{:S(2)}) collective-permute-start(bf16[48,128]{1,0:T(8,128)(2,1)S(1)} %add_add_fusion.refs_0_), channel_id=1, source_target_pairs={{0,4},{1,5},{2,6},{3,7},{4,0},{5,1},{6,2},{7,3},{8,12},{9,13},{10,... | collective-permute-start | bytes 36872 | tf_op jit(solution)/shard_map/ppermute | solution.py:258
  34.2 13.1 %all-to-all-start = ((bf16[16,8,3,2,128]{4,3,2,1,0:T(2,128)(2,1)}), bf16[16,8,3,2,128]{4,3,2,1,0:T(2,128)(2,1)S(1)}, u32[]{:S(2)}, u32[]{:S(2)}) async-start(bf16[16,8,3,2,128]{4,3,2,1,0:T(2,128)(2,1)} %update_values.1), calls=%async_computation | async-start | bytes 393216 | tf_op jit(solution)/shard_map/all_to_all | solution.py:682

commit v18 on v16

--- a/solution.py
+++ b/solution.py
@@ -350,68 +350,99 @@
     )
 
 
-def index_kernel(me_ref, stored_ref, slot_ref, column_ref):
+def index_kernel(holders, me_ref, stored_ref, slot_ref, column_ref):
+    me = me_ref[0]
     requests = stored_ref.shape[1]
+    half = requests // 2
     steps = slot_ref.shape[1] // requests
-    row = jnp.concatenate([stored_ref[...]] * steps, axis=1)
-    slot_ref[...] = row - me_ref[0]
+    wide = jnp.concatenate([stored_ref[...], jnp.zeros((1, HD - requests), jnp.int32)], axis=1)
+    by_row = jnp.broadcast_to(wide.astype(jnp.float32), (HD, HD)).T[:requests]
+    lane = lax.broadcasted_iota(jnp.int32, (requests, HD), 1)
+    core = (me % 2) ^ (lane // half)
+    wanted = ((lane % half) // 2 * 2 + core) * 2 + lane % 2
+    place = lax.broadcasted_iota(jnp.int32, (requests, HD), 0)
+    chosen = jnp.sum(jnp.where(place == wanted, by_row, 0.0), axis=0, keepdims=True)
+    row = jnp.concatenate([chosen[:, :half]] * steps + [chosen[:, half:requests]] * steps, axis=1)
+    slot_ref[...] = row.astype(jnp.int32) - me * holders
     wide = jnp.concatenate([row, jnp.zeros((1, HD - row.shape[1]), row.dtype)], axis=1)
-    column_ref[...] = jnp.broadcast_to(wide.astype(jnp.float32), (HD, HD)).T[: row.shape[1], :1].astype(jnp.int32)
-
-
-def index_work(first, stored, steps):
+    column_ref[...] = jnp.broadcast_to(wide, (HD, HD)).T[: row.shape[1], :1].astype(jnp.int32)
+
+
+def index_work(me, holders, stored, steps):
     rows = stored.shape[0] * steps
     return pl.pallas_call(
-        index_kernel,
+        functools.partial(index_kernel, holders),
         out_shape=(jax.ShapeDtypeStruct((1, rows), jnp.int32), jax.ShapeDtypeStruct((rows, 1), jnp.int32)),
         in_specs=[SMEM, VMEM],
         out_specs=(VMEM, VMEM),
         compiler_params=pltpu.CompilerParams(vmem_limit_bytes=2 * 2**20),
         cost_estimate=pl.CostEstimate(flops=2 * 10**10, bytes_accessed=10**4, transcendentals=0),
         name="index_work",
-    )(first, stored[None, :])
-
-
-def low_kernel(count, me_ref, slot_ref, down_ref, *refs):
-    blocks, (x_ref, low_ref, sem) = refs[:count], refs[count:]
+    )(me, stored[None, :])
+
+
+def line_copies(me, blocks, x_ref, sem):
+    return [
+        pltpu.make_async_copy(block, x_ref.at[:, :, (me // 2) ^ i], sem.at[i]) for i, block in enumerate(blocks)
+    ]
+
+
+def line_kernel(chips, me_ref, *refs):
+    blocks, (x_ref, sem) = refs[:chips], refs[chips:]
+    wait_all(start_all(line_copies(me_ref[0], blocks, x_ref, sem)))
+
+
+def line_rows(me, blocks):
+    chips = len(blocks)
+    steps, chunks = blocks[0].shape[:2]
+    return pl.pallas_call(
+        functools.partial(line_kernel, chips),
+        out_shape=jax.ShapeDtypeStruct((steps, chunks, chips, 2, HD), jnp.bfloat16),
+        in_specs=[SMEM] + [ANY] * chips,
+        out_specs=VMEM,
+        scratch_shapes=[pltpu.SemaphoreType.DMA((chips,))],
+        compiler_params=pltpu.CompilerParams(vmem_limit_bytes=4 * 2**20),
+        cost_estimate=pl.CostEstimate(flops=0, bytes_accessed=10**6, transcendentals=0),
+        name="line_rows",
+    )(me, *blocks)
+
+
+def low_kernel(chips, me_ref, slot_ref, down_ref, other_ref, *refs):
+    blocks, (x_ref, near_ref, far_ref, sem) = refs[:chips], refs[chips:]
     me = me_ref[0]
     holders, rank, width = down_ref.shape
-    wait_all(
-        start_all(
-            [pltpu.make_async_copy(block, x_ref.at[:, :, me ^ k], sem.at[k]) for k, block in enumerate(blocks)]
-        )
-    )
+    wait_all(start_all(line_copies(me, blocks, x_ref, sem)))
     x = step_rows(x_ref, 0, x_ref.shape[1])
     rows = x.shape[0]
-    made = lax.dot_general(
-        down_ref.reshape(holders * rank, width)[...], x, CONTRACT_LANES, preferred_element_type=jnp.float32
-    )
-    slot = slot_ref[...]
+    slot = slot_ref[...][:, :rows]
     low = jnp.zeros((rank, rows), jnp.float32)
-    for h in range(holders):
-        low = low + jnp.where(slot == h, made[h * rank : (h + 1) * rank], 0.0)
-    low = low.T
-    low_ref[...] = jnp.concatenate([low[: rows // 2], low[rows // 2 :]], axis=1).astype(low_ref.dtype)
-
-
-def low_of(me, blocks, slot, down):
-    count = len(blocks)
+    for maps_ref, first in ((down_ref, 0), (other_ref, holders * (1 - 2 * (me % 2)))):
+        made = lax.dot_general(
+            maps_ref.reshape(holders * rank, width)[...], x, CONTRACT_LANES, preferred_element_type=jnp.float32
+        )
+        for h in range(holders):
+            low = low + jnp.where(slot == first + h, made[h * rank : (h + 1) * rank], 0.0)
+    low = low.T.astype(near_ref.dtype)
+    none = jnp.zeros((rows, HD - rank), near_ref.dtype)
+    near_ref[...] = jnp.concatenate([low, none], axis=1)
+    far_ref[...] = jnp.concatenate([none, low], axis=1)
+
+
+def low_of(me, blocks, slot, down, other):
+    chips = len(blocks)
     steps, chunks = blocks[0].shape[:2]
-    rows = count * steps * 2
-    rank = down.shape[1]
+    rows = chips * steps * 2
+    low = jax.ShapeDtypeStruct((rows, HD), jnp.bfloat16)
     return pl.pallas_call(
-        functools.partial(low_kernel, count),
-        out_shape=(
-            jax.ShapeDtypeStruct((steps, chunks, count, 2, HD), jnp.bfloat16),
-            jax.ShapeDtypeStruct((rows // 2, 2 * rank), jnp.bfloat16),
-        ),
-        in_specs=[SMEM, VMEM, VMEM] + [ANY] * count,
-        out_specs=(VMEM, VMEM),
-        scratch_shapes=[pltpu.SemaphoreType.DMA((count,))],
+        functools.partial(low_kernel, chips),
+        out_shape=(jax.ShapeDtypeStruct((steps, chunks, chips, 2, HD), jnp.bfloat16), low, low),
+        in_specs=[SMEM, VMEM, VMEM, VMEM] + [ANY] * chips,
+        out_specs=(VMEM, VMEM, VMEM),
+        scratch_shapes=[pltpu.SemaphoreType.DMA((chips,))],
         compiler_params=pltpu.CompilerParams(vmem_limit_bytes=12 * 2**20),
         cost_estimate=pl.CostEstimate(flops=10**8, bytes_accessed=4 * 10**6, transcendentals=0),
         name="low_rows",
-    )(me, slot, down, *blocks)
+    )(me, slot, down, other, *blocks)
 
 
 def put_chunks(buf, first, value):
@@ -427,8 +458,8 @@
             flat[first + c, t] = part[t * 2 * count : (t + 1) * 2 * count]
 
 
-def project_kernel(which, x_ref, w_ref, out_ref):
-    x = step_rows(x_ref, 0, x_ref.shape[1])
+def project_kernel(which, own_ref, other_ref, w_ref, out_ref):
+    x = jnp.concatenate([step_rows(x_ref, 0, x_ref.shape[1]) for x_ref in (own_ref, other_ref)], axis=0)
     made = lax.dot_general(w_ref[which], x, CONTRACT_LANES, preferred_element_type=jnp.float32).T
     if which < 2:
         pad = jnp.zeros((made.shape[0], HD // 2), made.dtype)
@@ -437,23 +468,23 @@
         out_ref[...] = made
 
 
-def project(which, x, weight):
-    steps, _, count = x.shape[:3]
+def project(which, own, other, weight):
+    steps, _, chips = own.shape[:3]
     columns = weight.shape[1]
-    chunks = jax.ShapeDtypeStruct((-(-columns // HD), steps, count, 2, HD), jnp.bfloat16)
-    base = jax.ShapeDtypeStruct((2 * steps * count, columns), jnp.float32)
+    chunks = jax.ShapeDtypeStruct((-(-columns // HD), 2 * steps, chips, 2, HD), jnp.bfloat16)
+    base = jax.ShapeDtypeStruct((4 * steps * chips, columns), jnp.float32)
     return pl.pallas_call(
         functools.partial(project_kernel, which),
         out_shape=chunks if which < 2 else base,
-        in_specs=[VMEM, VMEM],
+        in_specs=[VMEM, VMEM, VMEM],
         out_specs=VMEM,
         compiler_params=pltpu.CompilerParams(vmem_limit_bytes=16 * 2**20),
         cost_estimate=pl.CostEstimate(flops=5 * 10**8, bytes_accessed=4 * 10**6, transcendentals=0),
         name="project",
-    )(x, weight)
-
-
-def update_kernel(stored_ref, query_ref, key_ref, base_ref, up_ref, *refs):
+    )(own, other, weight)
+
+
+def update_kernel(me_ref, stored_ref, query_ref, key_ref, base_ref, up_ref, *refs):
     lows, (send_ref, buf, sem) = refs[:-3], refs[-3:]
     half, packed = lows[0].shape
     rank = packed // 2
@@ -475,26 +506,31 @@
     buf[each - 1] = query_ref[each - 1] + key_ref[0]
     buf[each : 2 * each - 1] = key_ref[1:]
     put_chunks(buf, 2 * each - 1, base_ref[...] + adapter_scale * total)
-    wait_all(
-        start_all([pltpu.make_async_copy(buf.at[:, :, k], send_ref.at[k], sem.at[k]) for k in range(count)])
-    )
-
-
-def update_values(stored, query, key, base, up, lows):
-    chunks, steps, count = query.shape[:3]
+    core = me_ref[0] % 2
+    steps = send_ref.shape[2]
+    copies = []
+    for half in range(2):
+        for chip in range(count // 2):
+            part = buf.at[:, half * steps : (half + 1) * steps, chip]
+            copies.append(pltpu.make_async_copy(part, send_ref.at[2 * chip + (core ^ half)], sem.at[half, chip]))
+    wait_all(start_all(copies))
+
+
+def update_values(me, stored, query, key, base, up, lows):
+    chunks, halves, chips = query.shape[:3]
     return pl.pallas_call(
         update_kernel,
-        out_shape=pltpu.HBM((count, 3 * chunks - 1, steps, 2, HD), query.dtype),
-        in_specs=[VMEM] * (5 + len(lows)),
+        out_shape=pltpu.HBM((2 * chips, 3 * chunks - 1, halves // 2, 2, HD), query.dtype),
+        in_specs=[SMEM] + [VMEM] * (5 + len(lows)),
         out_specs=HBM,
         scratch_shapes=[
-            pltpu.VMEM((3 * chunks - 1, steps, count, 2, HD), query.dtype),
-            pltpu.SemaphoreType.DMA((count,)),
+            pltpu.VMEM((3 * chunks - 1, halves, chips, 2, HD), query.dtype),
+            pltpu.SemaphoreType.DMA((2, chips)),
         ],
         compiler_params=pltpu.CompilerParams(vmem_limit_bytes=8 * 2**20),
         cost_estimate=pl.CostEstimate(flops=3 * 10**8, bytes_accessed=4 * 10**6, transcendentals=0),
         name="update_values",
-    )(stored, query, key, base, up, *lows)
+    )(me, stored, query, key, base, up, *lows)
 
 
 def attend_kernel(cos_ref, sin_ref, live_ref, pieces_ref, *refs):
@@ -648,32 +684,33 @@
         ),
         axis=1,
     )
-    first, slots, here, stored = lax.optimization_barrier(
-        (me * req_dev, (me * holder_count).astype(jnp.int32).reshape(1), me.astype(jnp.int32).reshape(1), stored)
-    )
-    slot, column = index_work(slots, stored, steps)
-
+    first, here, stored = lax.optimization_barrier((me * req_dev, me.astype(jnp.int32).reshape(1), stored))
+    slot, column = index_work(here, holder_count, stored, steps)
+
+    other_maps = trade(adapter_down_maps, 1, count)
     held = {0: hidden}
     held.update({m: trade(hidden, m, count) for m in range(4, count, 4)})
     _, lengths, request_page_table = lax.optimization_barrier((held[4], lengths, request_page_table))
     cosine, sine = rotation_rows(lengths, first, req_dev, steps)
     live = live_lanes(lengths, first, request_page_table, tokens, page_len)
     held.update({k | 2: trade(v, 2, count) for k, v in list(held.items())})
-    ready = [0, 2, 4, 6]
+    ready = [0, 2, 4, 6, *range(8, count, 4)]
     held.update(zip(ready, lax.optimization_barrier([held[k] for k in ready])))
     held.update({k | 1: trade(v, 1, count) for k, v in list(held.items())})
     blocks = [held[k].reshape(steps, req_dev, heads, HD).transpose(0, 2, 1, 3) for k in range(count)]
     blocks[0] = in_hbm(blocks[0])
-    x, low = low_of(here, blocks, slot, adapter_down_maps)
+    own, near, far = low_of(here, blocks[0::2], slot, adapter_down_maps, other_maps)
+    *late, near = lax.optimization_barrier(blocks[1::2] + [near])
+    other = line_rows(here, late)
     weight = query_key_value_weight.transpose(0, 2, 1)
-    arrived = [trade(low, m, count) for m in (1, 2, 3)]
-    query, key = project(0, x, weight), project(1, x, weight)
+    arrived = [trade(far, 1, count), trade(near, 2, count), trade(far, 3, count)]
+    query, key = project(0, own, other, weight), project(1, own, other, weight)
     arrived, query, key, pool = lax.optimization_barrier((arrived, query, key, pool))
-    low = (low + arrived[0]) + (arrived[1] + arrived[2])
+    low = (near + arrived[0]) + (arrived[1] + arrived[2])
     arrived = [trade(low, m, count) for m in range(4, count, 4)]
-    base = project(2, x, weight)
+    base = project(2, own, other, weight)
     arrived, base = lax.optimization_barrier((arrived, base))
-    send = update_values(column, query, key, base, adapter_up_maps.reshape(adapter_count * rank, -1), [low, *arrived])
+    send = update_values(here, column, query, key, base, adapter_up_maps.reshape(adapter_count * rank, -1), [low, *arrived])
     send, pool = lax.optimization_barrier((send, pool))
     keys, values = cache_by_head(pool, 0, heads)
     pieces = lax.all_to_all(send, "replica", split_axis=0, concat_axis=0, tiled=True)

time: 51.6 us -> 52 us (level)
  waiting for transfers between devices: 10.9 us -> 9.08 us
  Pallas kernels: 17.5 us -> 18.7 us
  starting transfers between devices: 20.9 us -> 22 us
    ppermute x21 -> x22, waiting for transfers between devices: 8.49 us -> 6.65 us  [trade(): return lax.ppermute(value, 'replica', [(i, i ^ mask) for i in range(count)])]
    ppermute x21 -> x22, starting transfers between devices: 16.8 us -> 18.2 us  [trade(): return lax.ppermute(value, 'replica', [(i, i ^ mask) for i in range(count)])]
    pallas_call x3 -> x4, Pallas kernels: 3.86 us -> 5.01 us  [the longest x1 2.6 us: low_of(): pl.pallas_call(functools.partial(low_kernel, chips), out_shape=(jax.Shape...]
  transfers between devices with their start and end apart: 22 -> 23, of which waited for: 9 -> 7; matrix products, arithmetic and copies ran while one was open for 3% -> 3% of each run, Pallas kernels for 20% -> 25%
where the time goes in v18:
time: 52 us; the launch traced here: 51.7 us
  starting transfers between devices  22 us (42%)
  Pallas kernels  18.7 us (36%)
  waiting for transfers between devices  9.08 us (17%)
  other arithmetic  1.53 us (3%)
    ppermute x22, starting transfers between devices, trade(): return lax.ppermute(value, 'replica', [(i, i ^ mask) for i in range(count)])  18.2 us
    ppermute x22, waiting for transfers between devices, trade(): return lax.ppermute(value, 'replica', [(i, i ^ mask) for i in range(count)])  6.65 us
    pallas_call x1, Pallas kernels, cache_by_head(): pl.pallas_call(functools.partial(cache_kernel, first), out_shape=(jax.Sha...  6.38 us
    pallas_call x1, Pallas kernels, attend(): pl.pallas_call(attend_kernel, out_shape=jax.ShapeDtypeStruct((steps, head...  3.85 us
    all_to_all x1, starting transfers between devices, chip_plan(): lax.all_to_all(send, 'replica', split_axis=0, concat_axis=0, tiled=True)  3.75 us
    pallas_call x3, Pallas kernels, project(): pl.pallas_call(functools.partial(project_kernel, which), out_shape=chunks...  3.5 us
    pallas_call x1, Pallas kernels, low_of(): pl.pallas_call(functools.partial(low_kernel, chips), out_shape=(jax.Shape...  2.6 us
    all_to_all x1, waiting for transfers between devices, chip_plan(): lax.all_to_all(send, 'replica', split_axis=0, concat_axis=0, tiled=True)  2.42 us
  transfers between devices with their start and end apart: 23, of which 7 were waited for; matrix products, arithmetic and copies ran while one was open for 3% of the time, Pallas kernels for 25%

profile of v18, /device:TPU:0, one launch (start us, length us, event | category | flops | bytes accessed | tf_op | source)
XLA Modules:
  0.0 51.7 jit_solution(5363244534308757578)
XLA Ops:
  0.0 4.0 %collective-permute-start.4 = (bf16[3,2,5120]{2,1,0:T(2,128)(2,1)}, bf16[3,2,5120]{2,1,0:T(2,128)(2,1)S(1)}, u32[]{:S(2)}, u32[]{:S(2)}) collective-permute-start(bf16[3,2,5120]{2,1,0:T(2,128)(2,1)} %param.9), channel_id=1, source_target_pairs={{0,8},{1,9},{2,10},{3,11},{4,12},{5,13},{6,14},{7,15},{8,0},{9,1},... | collective-permute-start | bytes 184328 | tf_op jit(solution)/shard_map/ppermute | solution.py:258
  4.0 1.5 %collective-permute-start.2 = (bf16[3,2,5120]{2,1,0:T(2,128)(2,1)}, bf16[3,2,5120]{2,1,0:T(2,128)(2,1)S(1)}, u32[]{:S(2)}, u32[]{:S(2)}) collective-permute-start(bf16[3,2,5120]{2,1,0:T(2,128)(2,1)} %param.9), channel_id=1, source_target_pairs={{0,2},{1,3},{2,0},{3,1},{4,6},{5,7},{6,4},{7,5},{8,10},{9,11},{10,... | collective-permute-start | bytes 184328 | tf_op jit(solution)/shard_map/ppermute | solution.py:258
  5.6 1.6 %collective-permute-start = (bf16[3,2,5120]{2,1,0:T(2,128)(2,1)}, bf16[3,2,5120]{2,1,0:T(2,128)(2,1)S(1)}, u32[]{:S(2)}, u32[]{:S(2)}) collective-permute-start(bf16[3,2,5120]{2,1,0:T(2,128)(2,1)} %param.9), channel_id=1, source_target_pairs={{0,4},{1,5},{2,6},{3,7},{4,0},{5,1},{6,2},{7,3},{8,12},{9,13},{10,... | collective-permute-start | bytes 184328 | tf_op jit(solution)/shard_map/ppermute | solution.py:258
  7.1 0.2 collective-permute-start.5
  7.4 0.0 collective-permute-start.1
  7.4 0.9 %select_reduce_fusion.1 = s32[32]{0:T(128)S(1)} fusion(s32[64]{0:T(128)} %param.13, s32[32]{0:T(128)} %param.14), kind=kLoop, calls=%fused_computation.1 | loop fusion | flops 6112 | bytes 512 | tf_op jit(solution)/shard_map/reduce_sum | solution.py:679
  8.2 0.0 copy-start.4
  8.3 0.0 copy-start.5
  8.3 0.0 copy-start.3
  8.3 0.0 copy-start.2
  8.3 0.0 copy-start
  8.3 0.3 index_work.1
  8.6 1.4 %collective-permute-done = bf16[3,2,5120]{2,1,0:T(2,128)(2,1)S(1)} collective-permute-done((bf16[3,2,5120]{2,1,0:T(2,128)(2,1)}, bf16[3,2,5120]{2,1,0:T(2,128)(2,1)S(1)}, u32[]{:S(2)}, u32[]{:S(2)}) %collective-permute-start) | collective-permute-done | bytes 61472 | tf_op jit(solution)/shard_map/ppermute | solution.py:258
  10.0 0.5 collective-permute-start.3
  10.5 0.0 collective-permute-done.4
  10.5 1.5 %collective-permute-start.6 = (bf16[3,2,5120]{2,1,0:T(2,128)(2,1)S(1)}, bf16[3,2,5120]{2,1,0:T(2,128)(2,1)S(1)}, u32[]{:S(2)}, u32[]{:S(2)}) collective-permute-start(bf16[3,2,5120]{2,1,0:T(2,128)(2,1)S(1)} %collective-permute-done.4), channel_id=1, source_target_pairs={{0,2},{1,3},{2,0},{3,1},{4,6},{5,7},{6,4},{7,5},{8,10},{9,11},{10,... | collective-permute-start | bytes 184328 | tf_op jit(solution)/shard_map/ppermute | solution.py:258
  12.0 1.3 %collective-permute-done.5 = bf16[3,2,5120]{2,1,0:T(2,128)(2,1)S(1)} collective-permute-done((bf16[3,2,5120]{2,1,0:T(2,128)(2,1)}, bf16[3,2,5120]{2,1,0:T(2,128)(2,1)S(1)}, u32[]{:S(2)}, u32[]{:S(2)}) %collective-permute-start.5) | collective-permute-done | bytes 61472 | tf_op jit(solution)/shard_map/ppermute | solution.py:258
  13.4 0.5 collective-permute-start.7
  13.9 0.1 select_reduce_fusion
  14.0 0.2 fusion.3
  14.2 0.4 collective-permute-done.3
  14.6 0.5 collective-permute-start.10
  15.1 0.5 collective-permute-done.6
  15.5 0.1 and_convert_fusion.live_ref
  15.6 2.0 %collective-permute-done.7 = bf16[3,2,5120]{2,1,0:T(2,128)(2,1)S(1)} collective-permute-done((bf16[3,2,5120]{2,1,0:T(2,128)(2,1)S(1)}, bf16[3,2,5120]{2,1,0:T(2,128)(2,1)S(1)}, u32[]{:S(2)}, u32[]{:S(2)}) %collective-permute-start.7) | collective-permute-done | bytes 61472 | tf_op jit(solution)/shard_map/ppermute | solution.py:258
  17.6 0.5 collective-permute-start.12
  18.1 0.1 collective-permute-start.13
  18.2 0.4 collective-permute-start.15
  18.6 0.1 collective-permute-start.16
  18.7 0.2 select_reduce_fusion.2
  18.9 2.6 %low_rows.1 = (bf16[3,40,8,2,128]{4,3,2,1,0:T(2,128)(2,1)S(1)}, bf16[48,128]{1,0:T(8,128)(2,1)S(1)}, bf16[48,128]{1,0:T(8,128)(2,1)S(1)}) custom-call(s32[1]{0:T(128)} %bitcast.me_ref, s32[1,96]{1,0:T(1,128)S(1)} %get-tuple-element.50.slot_ref, bf16[4,64,5120]{2,1,0:T(8,128)(2,1)S(1)} %copy-done.2, ...), custom_call_target="tpu_custom_call" | custom-call | flops 100000000 | bytes 4000000 | tf_op jit(solution)/shard_map/low_rows/pallas_call | solution.py:436
  21.5 0.6 %collective-permute-start.18 = (bf16[48,128]{1,0:T(8,128)(2,1)S(1)}, bf16[48,128]{1,0:T(8,128)(2,1)S(1)}, u32[]{:S(2)}, u32[]{:S(2)}) collective-permute-start(bf16[48,128]{1,0:T(8,128)(2,1)S(1)} %get-tuple-element.57), channel_id=1, source_target_pairs={{0,3},{1,2},{2,1},{3,0},{4,7},{5,6},{6,5},{7,4},{8,11},{9,10},{10,... | collective-permute-start | bytes 36872 | tf_op jit(solution)/shard_map/ppermute | solution.py:258
  22.1 0.1 collective-permute-start.8
  22.2 1.6 %collective-permute-start.17 = (bf16[48,128]{1,0:T(8,128)(2,1)S(1)}, bf16[48,128]{1,0:T(8,128)(2,1)S(1)}, u32[]{:S(2)}, u32[]{:S(2)}) collective-permute-start(bf16[48,128]{1,0:T(8,128)(2,1)S(1)} %get-tuple-element.59), channel_id=1, source_target_pairs={{0,2},{1,3},{2,0},{3,1},{4,6},{5,7},{6,4},{7,5},{8,10},{9,11},{10,... | collective-permute-start | bytes 36872 | tf_op jit(solution)/shard_map/ppermute | solution.py:258
  23.8 0.4 line_rows.1.other_ref
  24.2 1.2 %project.4.key_ref = bf16[3,6,8,2,128]{4,3,2,1,0:T(2,128)(2,1)S(1)} custom-call(bf16[3,40,8,2,128]{4,3,2,1,0:T(2,128)(2,1)S(1)} %get-tuple-element.60.own_ref, bf16[3,40,8,2,128]{4,3,2,1,0:T(2,128)(2,1)S(1)} %line_rows.1.other_ref, bf16[3,320,5120]{2,1,0:T(8,128)(2,1)S(1)} %bitcast.58), custom_call_target="tpu_custom_call" | custom-call | flops 500000000 | bytes 4000000 | tf_op jit(solution)/shard_map/project/pallas_call | solution.py:476
  25.5 1.1 %project.3.query_ref = bf16[3,6,8,2,128]{4,3,2,1,0:T(2,128)(2,1)S(1)} custom-call(bf16[3,40,8,2,128]{4,3,2,1,0:T(2,128)(2,1)S(1)} %get-tuple-element.60.own_ref, bf16[3,40,8,2,128]{4,3,2,1,0:T(2,128)(2,1)S(1)} %line_rows.1.other_ref, bf16[3,320,5120]{2,1,0:T(8,128)(2,1)S(1)} %bitcast.59), custom_call_target="tpu_custom_call" | custom-call | flops 500000000 | bytes 4000000 | tf_op jit(solution)/shard_map/project/pallas_call | solution.py:476
  26.7 0.0 copy-start.1
  26.7 2.0 %collective-permute-start.21 = (bf16[48,128]{1,0:T(8,128)(2,1)S(1)}, bf16[48,128]{1,0:T(8,128)(2,1)S(1)}, u32[]{:S(2)}, u32[]{:S(2)}) collective-permute-start(bf16[48,128]{1,0:T(8,128)(2,1)S(1)} %add_add_fusion.refs_0_), channel_id=1, source_target_pairs={{0,12},{1,13},{2,14},{3,15},{4,8},{5,9},{6,10},{7,11},{8,4},{9,5},... | collective-permute-start | bytes 36872 | tf_op jit(solution)/shard_map/ppermute | solution.py:258
  28.7 2.4 %collective-permute-start.19 = (bf16[48,128]{1,0:T(8,128)(2,1)S(1)}, bf16[48,128]{1,0:T(8,128)(2,1)S(1)}, u32[]{:S(2)}, u32[]{:S(2)}) collective-permute-start(bf16[48,128]{1,0:T(8,128)(2,1)S(1)} %add_add_fusion.refs_0_), channel_id=1, source_target_pairs={{0,4},{1,5},{2,6},{3,7},{4,0},{5,1},{6,2},{7,3},{8,12},{9,13},{10,... | collective-permute-start | bytes 36872 | tf_op jit(solution)/shard_map/ppermute | solution.py:258
  31.1 1.1 %project.5.base_ref = f32[96,320]{1,0:T(8,128)S(1)} custom-call(bf16[3,40,8,2,128]{4,3,2,1,0:T(2,128)(2,1)S(1)} %get-tuple-element.60.own_ref, bf16[3,40,8,2,128]{4,3,2,1,0:T(2,128)(2,1)S(1)} %line_rows.1.other_ref, bf16[3,320,5120]{2,1,0:T(8,128)(2,1)S(1)} %bitcast.60), custom_call_target="tpu_custom_call" | custom-call | flops 500000000 | bytes 4000000 | tf_op jit(solution)/shard_map/project/pallas_call | solution.py:476
  32.3 1.0 %collective-permute-done.20.refs_2_ = bf16[48,128]{1,0:T(8,128)(2,1)S(1)} collective-permute-done((bf16[48,128]{1,0:T(8,128)(2,1)S(1)}, bf16[48,128]{1,0:T(8,128)(2,1)S(1)}, u32[]{:S(2)}, u32[]{:S(2)}) %collective-permute-start.20) | collective-permute-done | bytes 12320 | tf_op jit(solution)/shard_map/ppermute | solution.py:258
  33.3 1.7 %update_values.1 = bf16[16,8,3,2,128]{4,3,2,1,0:T(2,128)(2,1)} custom-call(s32[1]{0:T(128)} %bitcast.me_ref, s32[96,1]{1,0:T(8,128)S(1)} %get-tuple-element.49.stored_ref, bf16[3,6,8,2,128]{4,3,2,1,0:T(2,128)(2,1)S(1)} %project.3.query_ref, bf16[3,6,8,2,128]{4,3,2,1,0:T(2,128)(2,1)S(1)} %project.4.key_ref, f32[96,320]{1,0:T(8,128)S(1)} %project.5.base_ref, ...), custom_call_target="tpu_custom_call" | custom-call | flops 300000000 | bytes 4000000 | tf_op jit(solution)/shard_map/update_values/pallas_call | solution.py:521
  35.0 3.7 %all-to-all-start = ((bf16[16,8,3,2,128]{4,3,2,1,0:T(2,128)(2,1)}), bf16[16,8,3,2,128]{4,3,2,1,0:T(2,128)(2,1)S(1)}, u32[]{:S(2)}, u32[]{:S(2)}) async-start(bf16[16,8,3,2,128]{4,3,2,1,0:T(2,128)(2,1)} %update_values.1), calls=%async_computation | async-start | bytes 393216 | tf_op jit(solution)/shard_map/all_to_all | solution.py:716
  38.8 0.1 fusion
  38.9 6.4 %cache_by_head.1 = (bf16[40,256,128]{2,1,0:T(8,128)(2,1)S(1)}, bf16[40,256,128]{2,1,0:T(8,128)(2,1)}) custom-call(bf16[256,40,2,128]{3,2,1,0:T(2,128)(2,1)} %bitcast.78), custom_call_target="tpu_custom_call" | custom-call | bytes 12000000 | tf_op jit(solution)/shard_map/cache_by_head/pallas_call | solution.py:321
  45.3 2.4 %all-to-all-done.pieces_ref = bf16[16,8,3,2,128]{4,3,2,1,0:T(2,128)(2,1)S(1)} async-done(((bf16[16,8,3,2,128]{4,3,2,1,0:T(2,128)(2,1)}), bf16[16,8,3,2,128]{4,3,2,1,0:T(2,128)(2,1)S(1)}, u32[]{:S(2)}, u32[]{:S(2)}) %all-to-all-start) | async-done | bytes 196640 | tf_op jit(solution)/shard_map/all_to_all | solution.py:716
  47.7 3.8 %attention.1 = bf16[3,40,2,128]{3,2,1,0:T(2,128)(2,1)} custom-call(f32[8,128]{1,0:T(8,128)S(1)} %get-tuple-element.84.cos_ref, f32[8,128]{1,0:T(8,128)S(1)} %get-tuple-element.83.sin_ref, s32[2,256]{1,0:T(2,128)S(1)} %and_convert_fusion.live_ref, bf16[16,8,3,2,128]{4,3,2,1,0:T(2,128)(2,1)S(1)} %all-to-all-done.pieces_ref, ...), custom_call_target="tpu_custom_call" | custom-call | flops 1000000000 | bytes 6000000 | tf_op jit(solution)/shard_map/attention/pallas_call | solution.py:643
  (32 shorter events, 0.1 us)
Async XLA Ops:
  0.0 10.5 %collective-permute-start.4 = (bf16[3,2,5120]{2,1,0:T(2,128)(2,1)}, bf16[3,2,5120]{2,1,0:T(2,128)(2,1)S(1)}, u32[]{:S(2)}, u32[]{:S(2)}) collective-permute-start(bf16[3,2,5120]{2,1,0:T(2,128)(2,1)} %param.9), channel_id=1, source_target_pairs={{0,8},{1,9},{2,10},{3,11},{4,12},{5,13},{6,14},{7,15},{8,0},{9,1},... | collective-permute-start | bytes 184328 | tf_op jit(solution)/shard_map/ppermute | solution.py:258
  4.0 10.1 %collective-permute-start.2 = (bf16[3,2,5120]{2,1,0:T(2,128)(2,1)}, bf16[3,2,5120]{2,1,0:T(2,128)(2,1)S(1)}, u32[]{:S(2)}, u32[]{:S(2)}) collective-permute-start(bf16[3,2,5120]{2,1,0:T(2,128)(2,1)} %param.9), channel_id=1, source_target_pairs={{0,2},{1,3},{2,0},{3,1},{4,6},{5,7},{6,4},{7,5},{8,10},{9,11},{10,... | collective-permute-start | bytes 184328 | tf_op jit(solution)/shard_map/ppermute | solution.py:258
  5.6 4.4 %collective-permute-start = (bf16[3,2,5120]{2,1,0:T(2,128)(2,1)}, bf16[3,2,5120]{2,1,0:T(2,128)(2,1)S(1)}, u32[]{:S(2)}, u32[]{:S(2)}) collective-permute-start(bf16[3,2,5120]{2,1,0:T(2,128)(2,1)} %param.9), channel_id=1, source_target_pairs={{0,4},{1,5},{2,6},{3,7},{4,0},{5,1},{6,2},{7,3},{8,12},{9,13},{10,... | collective-permute-start | bytes 184328 | tf_op jit(solution)/shard_map/ppermute | solution.py:258
  7.1 6.2 %collective-permute-start.5 = (bf16[3,2,5120]{2,1,0:T(2,128)(2,1)}, bf16[3,2,5120]{2,1,0:T(2,128)(2,1)S(1)}, u32[]{:S(2)}, u32[]{:S(2)}) collective-permute-start(bf16[3,2,5120]{2,1,0:T(2,128)(2,1)} %param.9), channel_id=1, source_target_pairs={{0,12},{1,13},{2,14},{3,15},{4,8},{5,9},{6,10},{7,11},{8,4},{9,5},... | collective-permute-start | bytes 184328 | tf_op jit(solution)/shard_map/ppermute | solution.py:258
  7.4 11.3 %collective-permute-start.1 = (bf16[4,64,5120]{2,1,0:T(8,128)(2,1)}, bf16[4,64,5120]{2,1,0:T(8,128)(2,1)S(1)}, u32[]{:S(2)}, u32[]{:S(2)}) collective-permute-start(bf16[4,64,5120]{2,1,0:T(8,128)(2,1)} %down_ref.1), channel_id=1, source_target_pairs={{0,1},{1,0},{2,3},{3,2},{4,5},{5,4},{6,7},{7,6},{8,9},{9,8},{10,11... | collective-permute-start | bytes 7864328 | tf_op jit(solution)/shard_map/ppermute | solution.py:258
  8.2 5.6 %copy-start.4 = (s32[2,32]{1,0:T(2,128)S(1)}, s32[2,32]{1,0:T(2,128)}, u32[]{:S(2)}) copy-start(s32[2,32]{1,0:T(2,128)} %param.16) | copy-start | bytes 772
  8.3 5.7 %copy-start.5 = (s32[32]{0:T(128)S(1)}, s32[32]{0:T(128)}, u32[]{:S(2)}) copy-start(s32[32]{0:T(128)} %param.15) | copy-start | bytes 388
  8.3 6.3 %copy-start.3 = (bf16[3,2,5120]{2,1,0:T(2,128)(2,1)S(1)}, bf16[3,2,5120]{2,1,0:T(2,128)(2,1)}, u32[]{:S(2)}) copy-start(bf16[3,2,5120]{2,1,0:T(2,128)(2,1)} %param.9) | copy-start | bytes 184324
  8.3 10.6 %copy-start.2 = (bf16[4,64,5120]{2,1,0:T(8,128)(2,1)S(1)}, bf16[4,64,5120]{2,1,0:T(8,128)(2,1)}, u32[]{:S(2)}) copy-start(bf16[4,64,5120]{2,1,0:T(8,128)(2,1)} %down_ref.1) | copy-start | bytes 7864324
  8.3 15.9 %copy-start = (bf16[3,5120,320]{1,2,0:T(8,128)(2,1)S(1)}, bf16[3,5120,320]{1,2,0:T(8,128)(2,1)}, u32[]{:S(2)}) copy-start(bf16[3,5120,320]{1,2,0:T(8,128)(2,1)} %param.10) | copy-start | bytes 29491204
  10.0 4.6 %collective-permute-start.3 = (bf16[3,2,5120]{2,1,0:T(2,128)(2,1)S(1)}, bf16[3,2,5120]{2,1,0:T(2,128)(2,1)S(1)}, u32[]{:S(2)}, u32[]{:S(2)}) collective-permute-start(bf16[3,2,5120]{2,1,0:T(2,128)(2,1)S(1)} %collective-permute-done), channel_id=1, source_target_pairs={{0,2},{1,3},{2,0},{3,1},{4,6},{5,7},{6,4},{7,5},{8,10},{9,11},{10,... | collective-permute-start | bytes 184328 | tf_op jit(solution)/shard_map/ppermute | solution.py:258
  10.5 5.0 %collective-permute-start.6 = (bf16[3,2,5120]{2,1,0:T(2,128)(2,1)S(1)}, bf16[3,2,5120]{2,1,0:T(2,128)(2,1)S(1)}, u32[]{:S(2)}, u32[]{:S(2)}) collective-permute-start(bf16[3,2,5120]{2,1,0:T(2,128)(2,1)S(1)} %collective-permute-done.4), channel_id=1, source_target_pairs={{0,2},{1,3},{2,0},{3,1},{4,6},{5,7},{6,4},{7,5},{8,10},{9,11},{10,... | collective-permute-start | bytes 184328 | tf_op jit(solution)/shard_map/ppermute | solution.py:258
  13.4 4.2 %collective-permute-start.7 = (bf16[3,2,5120]{2,1,0:T(2,128)(2,1)S(1)}, bf16[3,2,5120]{2,1,0:T(2,128)(2,1)S(1)}, u32[]{:S(2)}, u32[]{:S(2)}) collective-permute-start(bf16[3,2,5120]{2,1,0:T(2,128)(2,1)S(1)} %collective-permute-done.5), channel_id=1, source_target_pairs={{0,2},{1,3},{2,0},{3,1},{4,6},{5,7},{6,4},{7,5},{8,10},{9,11},{10,... | collective-permute-start | bytes 184328 | tf_op jit(solution)/shard_map/ppermute | solution.py:258
  14.6 3.5 %collective-permute-start.9 = (bf16[3,2,5120]{2,1,0:T(2,128)(2,1)S(1)}, bf16[3,2,5120]{2,1,0:T(2,128)(2,1)S(1)}, u32[]{:S(2)}, u32[]{:S(2)}) collective-permute-start(bf16[3,2,5120]{2,1,0:T(2,128)(2,1)S(1)} %copy-done.3), channel_id=1, source_target_pairs={{0,1},{1,0},{2,3},{3,2},{4,5},{5,4},{6,7},{7,6},{8,9},{9,8},{10,11... | collective-permute-start | bytes 184328 | tf_op jit(solution)/shard_map/ppermute | solution.py:258
  14.6 3.6 %collective-permute-start.10 = (bf16[3,2,5120]{2,1,0:T(2,128)(2,1)S(1)}, bf16[3,2,5120]{2,1,0:T(2,128)(2,1)S(1)}, u32[]{:S(2)}, u32[]{:S(2)}) collective-permute-start(bf16[3,2,5120]{2,1,0:T(2,128)(2,1)S(1)} %collective-permute-done.2), channel_id=1, source_target_pairs={{0,1},{1,0},{2,3},{3,2},{4,5},{5,4},{6,7},{7,6},{8,9},{9,8},{10,11... | collective-permute-start | bytes 184328 | tf_op jit(solution)/shard_map/ppermute | solution.py:258
  15.5 2.1 %collective-permute-start.14 = (bf16[3,2,5120]{2,1,0:T(2,128)(2,1)S(1)}, bf16[3,2,5120]{2,1,0:T(2,128)(2,1)S(1)}, u32[]{:S(2)}, u32[]{:S(2)}) collective-permute-start(bf16[3,2,5120]{2,1,0:T(2,128)(2,1)S(1)} %collective-permute-done.6), channel_id=1, source_target_pairs={{0,1},{1,0},{2,3},{3,2},{4,5},{5,4},{6,7},{7,6},{8,9},{9,8},{10,11... | collective-permute-start | bytes 184328 | tf_op jit(solution)/shard_map/ppermute | solution.py:258
  17.6 3.9 %collective-permute-start.11 = (bf16[3,2,5120]{2,1,0:T(2,128)(2,1)S(1)}, bf16[3,2,5120]{2,1,0:T(2,128)(2,1)S(1)}, u32[]{:S(2)}, u32[]{:S(2)}) collective-permute-start(bf16[3,2,5120]{2,1,0:T(2,128)(2,1)S(1)} %collective-permute-done), channel_id=1, source_target_pairs={{0,1},{1,0},{2,3},{3,2},{4,5},{5,4},{6,7},{7,6},{8,9},{9,8},{10,11... | collective-permute-start | bytes 184328 | tf_op jit(solution)/shard_map/ppermute | solution.py:258
  17.6 4.5 %collective-permute-start.12 = (bf16[3,2,5120]{2,1,0:T(2,128)(2,1)S(1)}, bf16[3,2,5120]{2,1,0:T(2,128)(2,1)S(1)}, u32[]{:S(2)}, u32[]{:S(2)}) collective-permute-start(bf16[3,2,5120]{2,1,0:T(2,128)(2,1)S(1)} %collective-permute-done.3), channel_id=1, source_target_pairs={{0,1},{1,0},{2,3},{3,2},{4,5},{5,4},{6,7},{7,6},{8,9},{9,8},{10,11... | collective-permute-start | bytes 184328 | tf_op jit(solution)/shard_map/ppermute | solution.py:258
  18.1 4.1 %collective-permute-start.13 = (bf16[3,2,5120]{2,1,0:T(2,128)(2,1)S(1)}, bf16[3,2,5120]{2,1,0:T(2,128)(2,1)S(1)}, u32[]{:S(2)}, u32[]{:S(2)}) collective-permute-start(bf16[3,2,5120]{2,1,0:T(2,128)(2,1)S(1)} %collective-permute-done.4), channel_id=1, source_target_pairs={{0,1},{1,0},{2,3},{3,2},{4,5},{5,4},{6,7},{7,6},{8,9},{9,8},{10,11... | collective-permute-start | bytes 184328 | tf_op jit(solution)/shard_map/ppermute | solution.py:258
  18.2 4.0 %collective-permute-start.15 = (bf16[3,2,5120]{2,1,0:T(2,128)(2,1)S(1)}, bf16[3,2,5120]{2,1,0:T(2,128)(2,1)S(1)}, u32[]{:S(2)}, u32[]{:S(2)}) collective-permute-start(bf16[3,2,5120]{2,1,0:T(2,128)(2,1)S(1)} %collective-permute-done.5), channel_id=1, source_target_pairs={{0,1},{1,0},{2,3},{3,2},{4,5},{5,4},{6,7},{7,6},{8,9},{9,8},{10,11... | collective-permute-start | bytes 184328 | tf_op jit(solution)/shard_map/ppermute | solution.py:258
  18.6 3.6 %collective-permute-start.16 = (bf16[3,2,5120]{2,1,0:T(2,128)(2,1)S(1)}, bf16[3,2,5120]{2,1,0:T(2,128)(2,1)S(1)}, u32[]{:S(2)}, u32[]{:S(2)}) collective-permute-start(bf16[3,2,5120]{2,1,0:T(2,128)(2,1)S(1)} %collective-permute-done.7), channel_id=1, source_target_pairs={{0,1},{1,0},{2,3},{3,2},{4,5},{5,4},{6,7},{7,6},{8,9},{9,8},{10,11... | collective-permute-start | bytes 184328 | tf_op jit(solution)/shard_map/ppermute | solution.py:258
  21.5 5.1 %collective-permute-start.18 = (bf16[48,128]{1,0:T(8,128)(2,1)S(1)}, bf16[48,128]{1,0:T(8,128)(2,1)S(1)}, u32[]{:S(2)}, u32[]{:S(2)}) collective-permute-start(bf16[48,128]{1,0:T(8,128)(2,1)S(1)} %get-tuple-element.57), channel_id=1, source_target_pairs={{0,3},{1,2},{2,1},{3,0},{4,7},{5,6},{6,5},{7,4},{8,11},{9,10},{10,... | collective-permute-start | bytes 36872 | tf_op jit(solution)/shard_map/ppermute | solution.py:258
  22.1 4.5 %collective-permute-start.8 = (bf16[48,128]{1,0:T(8,128)(2,1)S(1)}, bf16[48,128]{1,0:T(8,128)(2,1)S(1)}, u32[]{:S(2)}, u32[]{:S(2)}) collective-permute-start(bf16[48,128]{1,0:T(8,128)(2,1)S(1)} %get-tuple-element.57), channel_id=1, source_target_pairs={{0,1},{1,0},{2,3},{3,2},{4,5},{5,4},{6,7},{7,6},{8,9},{9,8},{10,11... | collective-permute-start | bytes 36872 | tf_op jit(solution)/shard_map/ppermute | solution.py:258
  22.2 4.4 %collective-permute-start.17 = (bf16[48,128]{1,0:T(8,128)(2,1)S(1)}, bf16[48,128]{1,0:T(8,128)(2,1)S(1)}, u32[]{:S(2)}, u32[]{:S(2)}) collective-permute-start(bf16[48,128]{1,0:T(8,128)(2,1)S(1)} %get-tuple-element.59), channel_id=1, source_target_pairs={{0,2},{1,3},{2,0},{3,1},{4,6},{5,7},{6,4},{7,5},{8,10},{9,11},{10,... | collective-permute-start | bytes 36872 | tf_op jit(solution)/shard_map/ppermute | solution.py:258
  26.7 6.6 %copy-start.1 = (bf16[64,64,320]{2,1,0:T(8,128)(2,1)S(1)}, bf16[64,64,320]{2,1,0:T(8,128)(2,1)}, u32[]{:S(2)}) copy-start(bf16[64,64,320]{2,1,0:T(8,128)(2,1)} %param.12) | copy-start | bytes 7864324
  26.7 5.6 %collective-permute-start.21 = (bf16[48,128]{1,0:T(8,128)(2,1)S(1)}, bf16[48,128]{1,0:T(8,128)(2,1)S(1)}, u32[]{:S(2)}, u32[]{:S(2)}) collective-permute-start(bf16[48,128]{1,0:T(8,128)(2,1)S(1)} %add_add_fusion.refs_0_), channel_id=1, source_target_pairs={{0,12},{1,13},{2,14},{3,15},{4,8},{5,9},{6,10},{7,11},{8,4},{9,5},... | collective-permute-start | bytes 36872 | tf_op jit(solution)/shard_map/ppermute | solution.py:258
  28.7 4.6 %collective-permute-start.20 = (bf16[48,128]{1,0:T(8,128)(2,1)S(1)}, bf16[48,128]{1,0:T(8,128)(2,1)S(1)}, u32[]{:S(2)}, u32[]{:S(2)}) collective-permute-start(bf16[48,128]{1,0:T(8,128)(2,1)S(1)} %add_add_fusion.refs_0_), channel_id=1, source_target_pairs={{0,8},{1,9},{2,10},{3,11},{4,12},{5,13},{6,14},{7,15},{8,0},{9,1},... | collective-permute-start | bytes 36872 | tf_op jit(solution)/shard_map/ppermute | solution.py:258
  28.7 4.6 %collective-permute-start.19 = (bf16[48,128]{1,0:T(8,128)(2,1)S(1)}, bf16[48,128]{1,0:T(8,128)(2,1)S(1)}, u32[]{:S(2)}, u32[]{:S(2)}) collective-permute-start(bf16[48,128]{1,0:T(8,128)(2,1)S(1)} %add_add_fusion.refs_0_), channel_id=1, source_target_pairs={{0,4},{1,5},{2,6},{3,7},{4,0},{5,1},{6,2},{7,3},{8,12},{9,13},{10,... | collective-permute-start | bytes 36872 | tf_op jit(solution)/shard_map/ppermute | solution.py:258
  35.0 12.7 %all-to-all-start = ((bf16[16,8,3,2,128]{4,3,2,1,0:T(2,128)(2,1)}), bf16[16,8,3,2,128]{4,3,2,1,0:T(2,128)(2,1)S(1)}, u32[]{:S(2)}, u32[]{:S(2)}) async-start(bf16[16,8,3,2,128]{4,3,2,1,0:T(2,128)(2,1)} %update_values.1), calls=%async_computation | async-start | bytes 393216 | tf_op jit(solution)/shard_map/all_to_all | solution.py:716

commit v19 on v16

--- a/solution.py
+++ b/solution.py
@@ -350,6 +350,26 @@
     )
 
 
+def pack_kernel(*refs):
+    blocks, (out_ref, sem) = refs[:-2], refs[-2:]
+    wait_all(
+        start_all([pltpu.make_async_copy(block, out_ref.at[i], sem.at[i]) for i, block in enumerate(blocks)])
+    )
+
+
+def packed(blocks):
+    return pl.pallas_call(
+        pack_kernel,
+        out_shape=jax.ShapeDtypeStruct((len(blocks),) + blocks[0].shape, blocks[0].dtype),
+        in_specs=[ANY] * len(blocks),
+        out_specs=VMEM,
+        scratch_shapes=[pltpu.SemaphoreType.DMA((len(blocks),))],
+        compiler_params=pltpu.CompilerParams(vmem_limit_bytes=2 * 2**20),
+        cost_estimate=pl.CostEstimate(flops=0, bytes_accessed=10**6, transcendentals=0),
+        name="pack_blocks",
+    )(*blocks)
+
+
 def index_kernel(me_ref, stored_ref, slot_ref, column_ref):
     requests = stored_ref.shape[1]
     steps = slot_ref.shape[1] // requests
@@ -372,14 +392,13 @@
     )(first, stored[None, :])
 
 
-def low_kernel(count, me_ref, slot_ref, down_ref, *refs):
-    blocks, (x_ref, low_ref, sem) = refs[:count], refs[count:]
+def low_kernel(places, packs, me_ref, slot_ref, down_ref, pack_ref, *refs):
+    blocks, (x_ref, low_ref, sem) = refs[: len(places)], refs[len(places) :]
     me = me_ref[0]
     holders, rank, width = down_ref.shape
+    sources = list(zip(places, blocks)) + [(k, pack_ref.at[i]) for i, k in enumerate(packs)]
     wait_all(
-        start_all(
-            [pltpu.make_async_copy(block, x_ref.at[:, :, me ^ k], sem.at[k]) for k, block in enumerate(blocks)]
-        )
+        start_all([pltpu.make_async_copy(block, x_ref.at[:, :, me ^ k], sem.at[k]) for k, block in sources])
     )
     x = step_rows(x_ref, 0, x_ref.shape[1])
     rows = x.shape[0]
@@ -394,24 +413,24 @@
     low_ref[...] = jnp.concatenate([low[: rows // 2], low[rows // 2 :]], axis=1).astype(low_ref.dtype)
 
 
-def low_of(me, blocks, slot, down):
-    count = len(blocks)
+def low_of(me, blocks, packs, pack, slot, down):
+    count = len(blocks) + len(packs)
     steps, chunks = blocks[0].shape[:2]
     rows = count * steps * 2
     rank = down.shape[1]
     return pl.pallas_call(
-        functools.partial(low_kernel, count),
+        functools.partial(low_kernel, tuple(blocks), packs),
         out_shape=(
             jax.ShapeDtypeStruct((steps, chunks, count, 2, HD), jnp.bfloat16),
             jax.ShapeDtypeStruct((rows // 2, 2 * rank), jnp.bfloat16),
         ),
-        in_specs=[SMEM, VMEM, VMEM] + [ANY] * count,
+        in_specs=[SMEM, VMEM, VMEM, ANY] + [ANY] * len(blocks),
         out_specs=(VMEM, VMEM),
         scratch_shapes=[pltpu.SemaphoreType.DMA((count,))],
         compiler_params=pltpu.CompilerParams(vmem_limit_bytes=12 * 2**20),
         cost_estimate=pl.CostEstimate(flops=10**8, bytes_accessed=4 * 10**6, transcendentals=0),
         name="low_rows",
-    )(me, slot, down, *blocks)
+    )(me, slot, down, pack, *blocks.values())
 
 
 def put_chunks(buf, first, value):
@@ -586,8 +605,8 @@
         totals.append(jnp.sum(old, axis=1, keepdims=True) + jnp.sum(new, axis=1, keepdims=True))
         weights.append(old.astype(jnp.bfloat16))
         fresh_weights.append(new.astype(jnp.bfloat16))
-    wait_all(fetches)
     for c in chips:
+        fetches[c].wait()
         values = lanes_of(values_buf[c])
         vn = vn_ref[c].astype(jnp.bfloat16)
         mixed = jnp.dot(weights[c], values, preferred_element_type=jnp.float32)
@@ -659,12 +678,13 @@
     cosine, sine = rotation_rows(lengths, first, req_dev, steps)
     live = live_lanes(lengths, first, request_page_table, tokens, page_len)
     held.update({k | 2: trade(v, 2, count) for k, v in list(held.items())})
-    ready = [0, 2, 4, 6]
-    held.update(zip(ready, lax.optimization_barrier([held[k] for k in ready])))
-    held.update({k | 1: trade(v, 1, count) for k, v in list(held.items())})
-    blocks = [held[k].reshape(steps, req_dev, heads, HD).transpose(0, 2, 1, 3) for k in range(count)]
-    blocks[0] = in_hbm(blocks[0])
-    x, low = low_of(here, blocks, slot, adapter_down_maps)
+    held = {k: v.reshape(steps, req_dev, heads, HD).transpose(0, 2, 1, 3) for k, v in held.items()}
+    line = tuple(range(0, count, 4))
+    *share, held[2], held[6] = lax.optimization_barrier([held[k] for k in line] + [held[2], held[6]])
+    pack = trade(packed(share), 1, count)
+    held.update({k | 1: trade(held[k], 1, count) for k in range(2, count, 4)})
+    held[0] = in_hbm(held[0])
+    x, low = low_of(here, held, tuple(k | 1 for k in line), pack, slot, adapter_down_maps)
     weight = query_key_value_weight.transpose(0, 2, 1)
     arrived = [trade(low, m, count) for m in (1, 2, 3)]
     query, key = project(0, x, weight), project(1, x, weight)

time: 51.6 us -> 51.2 us (level)
  waiting for transfers between devices: 10.9 us -> 8.71 us
  starting transfers between devices: 20.9 us -> 21.9 us
  Pallas kernels: 17.5 us -> 18.4 us
    ppermute x21 -> x18, waiting for transfers between devices: 8.49 us -> 6.25 us  [trade(): return lax.ppermute(value, 'replica', [(i, i ^ mask) for i in range(count)])]
    ppermute x21 -> x18, starting transfers between devices: 16.8 us -> 17.4 us  [trade(): return lax.ppermute(value, 'replica', [(i, i ^ mask) for i in range(count)])]
    pallas_call x1 -> x2, Pallas kernels: 2.06 us -> 2.45 us  [the longest x1 2.09 us: low_of(): pl.pallas_call(functools.partial(low_kernel, tuple(blocks), packs), out_s...]
  transfers between devices with their start and end apart: 22 -> 19, of which waited for: 9 -> 6; matrix products, arithmetic and copies ran while one was open for 3% -> 3% of each run, Pallas kernels for 20% -> 20%
where the time goes in v19:
time: 51.2 us; the launch traced here: 51 us
  starting transfers between devices  21.9 us (43%)
  Pallas kernels  18.4 us (36%)
  waiting for transfers between devices  8.71 us (17%)
  other arithmetic  1.53 us (3%)
    ppermute x18, starting transfers between devices, trade(): return lax.ppermute(value, 'replica', [(i, i ^ mask) for i in range(count)])  17.4 us
    pallas_call x1, Pallas kernels, cache_by_head(): pl.pallas_call(functools.partial(cache_kernel, first), out_shape=(jax.Sha...  6.4 us
    ppermute x18, waiting for transfers between devices, trade(): return lax.ppermute(value, 'replica', [(i, i ^ mask) for i in range(count)])  6.25 us
    all_to_all x1, starting transfers between devices, chip_plan(): lax.all_to_all(send, 'replica', split_axis=0, concat_axis=0, tiled=True)  4.44 us
    pallas_call x1, Pallas kernels, attend(): pl.pallas_call(attend_kernel, out_shape=jax.ShapeDtypeStruct((steps, head...  4.28 us
    pallas_call x3, Pallas kernels, project(): pl.pallas_call(functools.partial(project_kernel, which), out_shape=chunks...  3.44 us
    all_to_all x1, waiting for transfers between devices, chip_plan(): lax.all_to_all(send, 'replica', split_axis=0, concat_axis=0, tiled=True)  2.46 us
    pallas_call x1, Pallas kernels, low_of(): pl.pallas_call(functools.partial(low_kernel, tuple(blocks), packs), out_s...  2.09 us
  transfers between devices with their start and end apart: 19, of which 6 were waited for; matrix products, arithmetic and copies ran while one was open for 3% of the time, Pallas kernels for 20%

profile of v19, /device:TPU:0, one launch (start us, length us, event | category | flops | bytes accessed | tf_op | source)
XLA Modules:
  0.0 51.0 jit_solution(10660110170921228270)
XLA Ops:
  0.0 4.0 %collective-permute-start.1 = (bf16[3,2,5120]{2,1,0:T(2,128)(2,1)}, bf16[3,2,5120]{2,1,0:T(2,128)(2,1)S(1)}, u32[]{:S(2)}, u32[]{:S(2)}) collective-permute-start(bf16[3,2,5120]{2,1,0:T(2,128)(2,1)} %param.9), channel_id=1, source_target_pairs={{0,8},{1,9},{2,10},{3,11},{4,12},{5,13},{6,14},{7,15},{8,0},{9,1},... | collective-permute-start | bytes 184328 | tf_op jit(solution)/shard_map/ppermute | solution.py:258
  4.0 1.6 %collective-permute-start = (bf16[3,2,5120]{2,1,0:T(2,128)(2,1)}, bf16[3,2,5120]{2,1,0:T(2,128)(2,1)S(1)}, u32[]{:S(2)}, u32[]{:S(2)}) collective-permute-start(bf16[3,2,5120]{2,1,0:T(2,128)(2,1)} %param.9), channel_id=1, source_target_pairs={{0,4},{1,5},{2,6},{3,7},{4,0},{5,1},{6,2},{7,3},{8,12},{9,13},{10,... | collective-permute-start | bytes 184328 | tf_op jit(solution)/shard_map/ppermute | solution.py:258
  5.6 1.5 %collective-permute-start.3 = (bf16[3,2,5120]{2,1,0:T(2,128)(2,1)}, bf16[3,2,5120]{2,1,0:T(2,128)(2,1)S(1)}, u32[]{:S(2)}, u32[]{:S(2)}) collective-permute-start(bf16[3,2,5120]{2,1,0:T(2,128)(2,1)} %param.9), channel_id=1, source_target_pairs={{0,2},{1,3},{2,0},{3,1},{4,6},{5,7},{6,4},{7,5},{8,10},{9,11},{10,... | collective-permute-start | bytes 184328 | tf_op jit(solution)/shard_map/ppermute | solution.py:258
  7.1 0.2 collective-permute-start.2
  7.4 0.9 %select_reduce_fusion.1 = s32[32]{0:T(128)S(1)} fusion(s32[64]{0:T(128)} %param.13, s32[32]{0:T(128)} %param.14), kind=kLoop, calls=%fused_computation.1 | loop fusion | flops 6112 | bytes 512 | tf_op jit(solution)/shard_map/reduce_sum | solution.py:662
  8.2 0.0 slice-start
  8.3 0.0 copy-start.3
  8.3 0.0 copy-start.4
  8.3 0.0 copy-start.2
  8.3 0.0 copy-start.1
  8.3 0.0 slice-start.1
  8.3 0.0 slice-start.2
  8.3 0.2 index_work.1
  8.5 1.5 %collective-permute-start.4 = (bf16[3,2,5120]{2,1,0:T(2,128)(2,1)S(1)}, bf16[3,2,5120]{2,1,0:T(2,128)(2,1)S(1)}, u32[]{:S(2)}, u32[]{:S(2)}) collective-permute-start(bf16[3,2,5120]{2,1,0:T(2,128)(2,1)S(1)} %collective-permute-done), channel_id=1, source_target_pairs={{0,2},{1,3},{2,0},{3,1},{4,6},{5,7},{6,4},{7,5},{8,10},{9,11},{10,... | collective-permute-start | bytes 184328 | tf_op jit(solution)/shard_map/ppermute | solution.py:258
  10.0 0.6 %collective-permute-start.6 = (bf16[3,2,5120]{2,1,0:T(2,128)(2,1)S(1)}, bf16[3,2,5120]{2,1,0:T(2,128)(2,1)S(1)}, u32[]{:S(2)}, u32[]{:S(2)}) collective-permute-start(bf16[3,2,5120]{2,1,0:T(2,128)(2,1)S(1)} %collective-permute-done.1), channel_id=1, source_target_pairs={{0,2},{1,3},{2,0},{3,1},{4,6},{5,7},{6,4},{7,5},{8,10},{9,11},{10,... | collective-permute-start | bytes 184328 | tf_op jit(solution)/shard_map/ppermute | solution.py:258
  10.6 0.1 select_reduce_fusion
  10.7 2.7 %collective-permute-done.2 = bf16[3,2,5120]{2,1,0:T(2,128)(2,1)S(1)} collective-permute-done((bf16[3,2,5120]{2,1,0:T(2,128)(2,1)}, bf16[3,2,5120]{2,1,0:T(2,128)(2,1)S(1)}, u32[]{:S(2)}, u32[]{:S(2)}) %collective-permute-start.2) | collective-permute-done | bytes 61472 | tf_op jit(solution)/shard_map/ppermute | solution.py:258
  13.4 0.5 collective-permute-start.7
  13.9 0.2 fusion.3
  14.1 0.0 collective-permute-done.4
  14.1 0.4 pack_blocks.1
  14.4 0.1 collective-permute-start.5
  14.5 0.1 and_convert_fusion.live_ref
  14.6 0.5 collective-permute-start.10
  15.1 0.1 collective-permute-start.8
  15.2 0.4 collective-permute-start.9
  15.6 2.0 %collective-permute-done.7 = bf16[3,2,5120]{2,1,0:T(2,128)(2,1)S(1)} collective-permute-done((bf16[3,2,5120]{2,1,0:T(2,128)(2,1)S(1)}, bf16[3,2,5120]{2,1,0:T(2,128)(2,1)S(1)}, u32[]{:S(2)}, u32[]{:S(2)}) %collective-permute-start.7) | collective-permute-done | bytes 61472 | tf_op jit(solution)/shard_map/ppermute | solution.py:258
  17.6 0.2 select_reduce_fusion.2
  17.8 1.0 %collective-permute-done.11.refs_11_ = bf16[3,40,2,128]{3,2,1,0:T(2,128)(2,1)S(1)} collective-permute-done((bf16[3,40,2,128]{3,2,1,0:T(2,128)(2,1)S(1)}, bf16[3,40,2,128]{3,2,1,0:T(2,128)(2,1)S(1)}, u32[]{:S(2)}, u32[]{:S(2)}) %collective-permute-start.11) | collective-permute-done | bytes 61472 | tf_op jit(solution)/shard_map/ppermute | solution.py:258
  18.8 2.1 %low_rows.1 = (bf16[3,40,16,2,128]{4,3,2,1,0:T(2,128)(2,1)S(1)}, bf16[48,128]{1,0:T(8,128)(2,1)S(1)}) custom-call(s32[1]{0:T(128)} %bitcast.1.me_ref, s32[1,96]{1,0:T(1,128)S(1)} %get-tuple-element.42.slot_ref, bf16[4,64,5120]{2,1,0:T(8,128)(2,1)S(1)} %copy-done.1, bf16[4,3,40,2,128]{4,3,2,1,0:T(2,128)(2,1)S(1)} %collective-permute-done.5.pack_ref, ...), custom_call_target="tpu_custom_call" | custom-call | flops 100000000 | bytes 4000000 | tf_op jit(solution)/shard_map/low_rows/pallas_call | solution.py:421
  20.9 0.3 collective-permute-start.14
  21.3 1.5 %collective-permute-start.13 = (bf16[48,128]{1,0:T(8,128)(2,1)S(1)}, bf16[48,128]{1,0:T(8,128)(2,1)S(1)}, u32[]{:S(2)}, u32[]{:S(2)}) collective-permute-start(bf16[48,128]{1,0:T(8,128)(2,1)S(1)} %get-tuple-element.49), channel_id=1, source_target_pairs={{0,2},{1,3},{2,0},{3,1},{4,6},{5,7},{6,4},{7,5},{8,10},{9,11},{10,... | collective-permute-start | bytes 36872 | tf_op jit(solution)/shard_map/ppermute | solution.py:258
  22.8 0.1 collective-permute-start.12
  22.9 1.2 %project.4.key_ref = bf16[3,3,16,2,128]{4,3,2,1,0:T(2,128)(2,1)S(1)} custom-call(bf16[3,40,16,2,128]{4,3,2,1,0:T(2,128)(2,1)S(1)} %get-tuple-element.50.x_ref, bf16[3,320,5120]{2,1,0:T(8,128)(2,1)S(1)} %bitcast.37), custom_call_target="tpu_custom_call" | custom-call | flops 500000000 | bytes 4000000 | tf_op jit(solution)/shard_map/project/pallas_call | solution.py:464
  24.1 1.1 %project.3.query_ref = bf16[3,3,16,2,128]{4,3,2,1,0:T(2,128)(2,1)S(1)} custom-call(bf16[3,40,16,2,128]{4,3,2,1,0:T(2,128)(2,1)S(1)} %get-tuple-element.50.x_ref, bf16[3,320,5120]{2,1,0:T(8,128)(2,1)S(1)} %bitcast.38), custom_call_target="tpu_custom_call" | custom-call | flops 500000000 | bytes 4000000 | tf_op jit(solution)/shard_map/project/pallas_call | solution.py:464
  25.3 0.0 copy-start
  25.3 1.3 %collective-permute-start.17 = (bf16[48,128]{1,0:T(8,128)(2,1)S(1)}, bf16[48,128]{1,0:T(8,128)(2,1)S(1)}, u32[]{:S(2)}, u32[]{:S(2)}) collective-permute-start(bf16[48,128]{1,0:T(8,128)(2,1)S(1)} %add_add_fusion.refs_0_), channel_id=1, source_target_pairs={{0,12},{1,13},{2,14},{3,15},{4,8},{5,9},{6,10},{7,11},{8,4},{9,5},... | collective-permute-start | bytes 36872 | tf_op jit(solution)/shard_map/ppermute | solution.py:258
  26.6 0.2 collective-permute-start.16
  26.8 2.9 %collective-permute-start.15 = (bf16[48,128]{1,0:T(8,128)(2,1)S(1)}, bf16[48,128]{1,0:T(8,128)(2,1)S(1)}, u32[]{:S(2)}, u32[]{:S(2)}) collective-permute-start(bf16[48,128]{1,0:T(8,128)(2,1)S(1)} %add_add_fusion.refs_0_), channel_id=1, source_target_pairs={{0,4},{1,5},{2,6},{3,7},{4,0},{5,1},{6,2},{7,3},{8,12},{9,13},{10,... | collective-permute-start | bytes 36872 | tf_op jit(solution)/shard_map/ppermute | solution.py:258
  29.7 1.1 %project.5.base_ref = f32[96,320]{1,0:T(8,128)S(1)} custom-call(bf16[3,40,16,2,128]{4,3,2,1,0:T(2,128)(2,1)S(1)} %get-tuple-element.50.x_ref, bf16[3,320,5120]{2,1,0:T(8,128)(2,1)S(1)} %bitcast.39), custom_call_target="tpu_custom_call" | custom-call | flops 500000000 | bytes 4000000 | tf_op jit(solution)/shard_map/project/pallas_call | solution.py:464
  30.9 0.3 collective-permute-done.16.refs_2_
  31.2 0.2 collective-permute-done.15.refs_1_
  31.4 1.7 %update_values.1 = bf16[16,8,3,2,128]{4,3,2,1,0:T(2,128)(2,1)} custom-call(s32[96,1]{1,0:T(8,128)S(1)} %get-tuple-element.40.stored_ref, bf16[3,3,16,2,128]{4,3,2,1,0:T(2,128)(2,1)S(1)} %project.3.query_ref, bf16[3,3,16,2,128]{4,3,2,1,0:T(2,128)(2,1)S(1)} %project.4.key_ref, f32[96,320]{1,0:T(8,128)S(1)} %project.5.base_ref, bf16[4096,320]{1,0:T(8,128)(2,1)S(1)} %bitcast.40, ...), custom_call_target="tpu_custom_call" | custom-call | flops 300000000 | bytes 4000000 | tf_op jit(solution)/shard_map/update_values/pallas_call | solution.py:504
  33.1 4.4 %all-to-all-start = ((bf16[16,8,3,2,128]{4,3,2,1,0:T(2,128)(2,1)}), bf16[16,8,3,2,128]{4,3,2,1,0:T(2,128)(2,1)S(1)}, u32[]{:S(2)}, u32[]{:S(2)}) async-start(bf16[16,8,3,2,128]{4,3,2,1,0:T(2,128)(2,1)} %update_values.1), calls=%async_computation | async-start | bytes 393216 | tf_op jit(solution)/shard_map/all_to_all | solution.py:699
  37.5 0.1 fusion
  37.6 6.4 %cache_by_head.1 = (bf16[40,256,128]{2,1,0:T(8,128)(2,1)S(1)}, bf16[40,256,128]{2,1,0:T(8,128)(2,1)}) custom-call(bf16[256,40,2,128]{3,2,1,0:T(2,128)(2,1)} %bitcast.58), custom_call_target="tpu_custom_call" | custom-call | bytes 12000000 | tf_op jit(solution)/shard_map/cache_by_head/pallas_call | solution.py:321
  44.1 2.5 %all-to-all-done.pieces_ref = bf16[16,8,3,2,128]{4,3,2,1,0:T(2,128)(2,1)S(1)} async-done(((bf16[16,8,3,2,128]{4,3,2,1,0:T(2,128)(2,1)}), bf16[16,8,3,2,128]{4,3,2,1,0:T(2,128)(2,1)S(1)}, u32[]{:S(2)}, u32[]{:S(2)}) %all-to-all-start) | async-done | bytes 196640 | tf_op jit(solution)/shard_map/all_to_all | solution.py:699
  46.5 4.3 %attention.1 = bf16[3,40,2,128]{3,2,1,0:T(2,128)(2,1)} custom-call(f32[8,128]{1,0:T(8,128)S(1)} %get-tuple-element.66.cos_ref, f32[8,128]{1,0:T(8,128)S(1)} %get-tuple-element.65.sin_ref, s32[2,256]{1,0:T(2,128)S(1)} %and_convert_fusion.live_ref, bf16[16,8,3,2,128]{4,3,2,1,0:T(2,128)(2,1)S(1)} %all-to-all-done.pieces_ref, ...), custom_call_target="tpu_custom_call" | custom-call | flops 1000000000 | bytes 6000000 | tf_op jit(solution)/shard_map/attention/pallas_call | solution.py:626
  (29 shorter events, 0.1 us)
Async XLA Ops:
  0.0 10.0 %collective-permute-start.1 = (bf16[3,2,5120]{2,1,0:T(2,128)(2,1)}, bf16[3,2,5120]{2,1,0:T(2,128)(2,1)S(1)}, u32[]{:S(2)}, u32[]{:S(2)}) collective-permute-start(bf16[3,2,5120]{2,1,0:T(2,128)(2,1)} %param.9), channel_id=1, source_target_pairs={{0,8},{1,9},{2,10},{3,11},{4,12},{5,13},{6,14},{7,15},{8,0},{9,1},... | collective-permute-start | bytes 184328 | tf_op jit(solution)/shard_map/ppermute | solution.py:258
  4.0 4.5 %collective-permute-start = (bf16[3,2,5120]{2,1,0:T(2,128)(2,1)}, bf16[3,2,5120]{2,1,0:T(2,128)(2,1)S(1)}, u32[]{:S(2)}, u32[]{:S(2)}) collective-permute-start(bf16[3,2,5120]{2,1,0:T(2,128)(2,1)} %param.9), channel_id=1, source_target_pairs={{0,4},{1,5},{2,6},{3,7},{4,0},{5,1},{6,2},{7,3},{8,12},{9,13},{10,... | collective-permute-start | bytes 184328 | tf_op jit(solution)/shard_map/ppermute | solution.py:258
  5.6 8.4 %collective-permute-start.3 = (bf16[3,2,5120]{2,1,0:T(2,128)(2,1)}, bf16[3,2,5120]{2,1,0:T(2,128)(2,1)S(1)}, u32[]{:S(2)}, u32[]{:S(2)}) collective-permute-start(bf16[3,2,5120]{2,1,0:T(2,128)(2,1)} %param.9), channel_id=1, source_target_pairs={{0,2},{1,3},{2,0},{3,1},{4,6},{5,7},{6,4},{7,5},{8,10},{9,11},{10,... | collective-permute-start | bytes 184328 | tf_op jit(solution)/shard_map/ppermute | solution.py:258
  7.1 6.2 %collective-permute-start.2 = (bf16[3,2,5120]{2,1,0:T(2,128)(2,1)}, bf16[3,2,5120]{2,1,0:T(2,128)(2,1)S(1)}, u32[]{:S(2)}, u32[]{:S(2)}) collective-permute-start(bf16[3,2,5120]{2,1,0:T(2,128)(2,1)} %param.9), channel_id=1, source_target_pairs={{0,12},{1,13},{2,14},{3,15},{4,8},{5,9},{6,10},{7,11},{8,4},{9,5},... | collective-permute-start | bytes 184328 | tf_op jit(solution)/shard_map/ppermute | solution.py:258
  8.2 14.6 %slice-start = ((s8[9830400]{0:T(1024)(128)(4,1)}), s8[4194304]{0:T(1024)(128)(4,1)S(1)}, s32[]{:S(2)}) async-start(s8[9830400]{0:T(1024)(128)(4,1)} %bitcast.35), calls=%async_computation.1 | async-start | bytes 8388608
  8.3 2.4 %copy-start.3 = (s32[2,32]{1,0:T(2,128)S(1)}, s32[2,32]{1,0:T(2,128)}, u32[]{:S(2)}) copy-start(s32[2,32]{1,0:T(2,128)} %param.16) | copy-start | bytes 772
  8.3 5.6 %copy-start.4 = (s32[32]{0:T(128)S(1)}, s32[32]{0:T(128)}, u32[]{:S(2)}) copy-start(s32[32]{0:T(128)} %param.15) | copy-start | bytes 388
  8.3 5.8 %copy-start.2 = (bf16[3,2,5120]{2,1,0:T(2,128)(2,1)S(1)}, bf16[3,2,5120]{2,1,0:T(2,128)(2,1)}, u32[]{:S(2)}) copy-start(bf16[3,2,5120]{2,1,0:T(2,128)(2,1)} %param.9) | copy-start | bytes 184324
  8.3 10.6 %copy-start.1 = (bf16[4,64,5120]{2,1,0:T(8,128)(2,1)S(1)}, bf16[4,64,5120]{2,1,0:T(8,128)(2,1)}, u32[]{:S(2)}) copy-start(bf16[4,64,5120]{2,1,0:T(8,128)(2,1)} %down_ref.1) | copy-start | bytes 7864324
  8.3 14.6 %slice-start.1 = ((s8[9830400]{0:T(1024)(128)(4,1)}), s8[4194304]{0:T(1024)(128)(4,1)S(1)}, s32[]{:S(2)}) async-start(s8[9830400]{0:T(1024)(128)(4,1)} %bitcast.35), calls=%async_computation.2 | async-start | bytes 8388608
  8.3 14.6 %slice-start.2 = ((s8[9830400]{0:T(1024)(128)(4,1)}), s8[1441792]{0:T(1024)(128)(4,1)S(1)}, s32[]{:S(2)}) async-start(s8[9830400]{0:T(1024)(128)(4,1)} %bitcast.35), calls=%async_computation.3 | async-start | bytes 2883584
  8.5 5.5 %collective-permute-start.4 = (bf16[3,2,5120]{2,1,0:T(2,128)(2,1)S(1)}, bf16[3,2,5120]{2,1,0:T(2,128)(2,1)S(1)}, u32[]{:S(2)}, u32[]{:S(2)}) collective-permute-start(bf16[3,2,5120]{2,1,0:T(2,128)(2,1)S(1)} %collective-permute-done), channel_id=1, source_target_pairs={{0,2},{1,3},{2,0},{3,1},{4,6},{5,7},{6,4},{7,5},{8,10},{9,11},{10,... | collective-permute-start | bytes 184328 | tf_op jit(solution)/shard_map/ppermute | solution.py:258
  10.0 4.6 %collective-permute-start.6 = (bf16[3,2,5120]{2,1,0:T(2,128)(2,1)S(1)}, bf16[3,2,5120]{2,1,0:T(2,128)(2,1)S(1)}, u32[]{:S(2)}, u32[]{:S(2)}) collective-permute-start(bf16[3,2,5120]{2,1,0:T(2,128)(2,1)S(1)} %collective-permute-done.1), channel_id=1, source_target_pairs={{0,2},{1,3},{2,0},{3,1},{4,6},{5,7},{6,4},{7,5},{8,10},{9,11},{10,... | collective-permute-start | bytes 184328 | tf_op jit(solution)/shard_map/ppermute | solution.py:258
  13.4 4.2 %collective-permute-start.7 = (bf16[3,2,5120]{2,1,0:T(2,128)(2,1)S(1)}, bf16[3,2,5120]{2,1,0:T(2,128)(2,1)S(1)}, u32[]{:S(2)}, u32[]{:S(2)}) collective-permute-start(bf16[3,2,5120]{2,1,0:T(2,128)(2,1)S(1)} %collective-permute-done.2), channel_id=1, source_target_pairs={{0,2},{1,3},{2,0},{3,1},{4,6},{5,7},{6,4},{7,5},{8,10},{9,11},{10,... | collective-permute-start | bytes 184328 | tf_op jit(solution)/shard_map/ppermute | solution.py:258
  14.4 4.4 %collective-permute-start.5 = (bf16[4,3,40,2,128]{4,3,2,1,0:T(2,128)(2,1)S(1)}, bf16[4,3,40,2,128]{4,3,2,1,0:T(2,128)(2,1)S(1)}, u32[]{:S(2)}, u32[]{:S(2)}) collective-permute-start(bf16[4,3,40,2,128]{4,3,2,1,0:T(2,128)(2,1)S(1)} %pack_blocks.1), channel_id=1, source_target_pairs={{0,1},{1,0},{2,3},{3,2},{4,5},{5,4},{6,7},{7,6},{8,9},{9,8},{10,11... | collective-permute-start | bytes 737288 | tf_op jit(solution)/shard_map/ppermute | solution.py:258
  14.6 3.2 %collective-permute-start.10 = (bf16[3,40,2,128]{3,2,1,0:T(2,128)(2,1)S(1)}, bf16[3,40,2,128]{3,2,1,0:T(2,128)(2,1)S(1)}, u32[]{:S(2)}, u32[]{:S(2)}) collective-permute-start(bf16[3,40,2,128]{3,2,1,0:T(2,128)(2,1)S(1)} %bitcast.53), channel_id=1, source_target_pairs={{0,1},{1,0},{2,3},{3,2},{4,5},{5,4},{6,7},{7,6},{8,9},{9,8},{10,11... | collective-permute-start | bytes 184328 | tf_op jit(solution)/shard_map/ppermute | solution.py:258
  15.1 2.7 %collective-permute-start.8 = (bf16[3,40,2,128]{3,2,1,0:T(2,128)(2,1)S(1)}, bf16[3,40,2,128]{3,2,1,0:T(2,128)(2,1)S(1)}, u32[]{:S(2)}, u32[]{:S(2)}) collective-permute-start(bf16[3,40,2,128]{3,2,1,0:T(2,128)(2,1)S(1)} %bitcast.49), channel_id=1, source_target_pairs={{0,1},{1,0},{2,3},{3,2},{4,5},{5,4},{6,7},{7,6},{8,9},{9,8},{10,11... | collective-permute-start | bytes 184328 | tf_op jit(solution)/shard_map/ppermute | solution.py:258
  15.2 2.6 %collective-permute-start.9 = (bf16[3,40,2,128]{3,2,1,0:T(2,128)(2,1)S(1)}, bf16[3,40,2,128]{3,2,1,0:T(2,128)(2,1)S(1)}, u32[]{:S(2)}, u32[]{:S(2)}) collective-permute-start(bf16[3,40,2,128]{3,2,1,0:T(2,128)(2,1)S(1)} %bitcast.51), channel_id=1, source_target_pairs={{0,1},{1,0},{2,3},{3,2},{4,5},{5,4},{6,7},{7,6},{8,9},{9,8},{10,11... | collective-permute-start | bytes 184328 | tf_op jit(solution)/shard_map/ppermute | solution.py:258
  17.6 1.2 %collective-permute-start.11 = (bf16[3,40,2,128]{3,2,1,0:T(2,128)(2,1)S(1)}, bf16[3,40,2,128]{3,2,1,0:T(2,128)(2,1)S(1)}, u32[]{:S(2)}, u32[]{:S(2)}) collective-permute-start(bf16[3,40,2,128]{3,2,1,0:T(2,128)(2,1)S(1)} %bitcast.55), channel_id=1, source_target_pairs={{0,1},{1,0},{2,3},{3,2},{4,5},{5,4},{6,7},{7,6},{8,9},{9,8},{10,11... | collective-permute-start | bytes 184328 | tf_op jit(solution)/shard_map/ppermute | solution.py:258
  20.9 4.3 %collective-permute-start.14 = (bf16[48,128]{1,0:T(8,128)(2,1)S(1)}, bf16[48,128]{1,0:T(8,128)(2,1)S(1)}, u32[]{:S(2)}, u32[]{:S(2)}) collective-permute-start(bf16[48,128]{1,0:T(8,128)(2,1)S(1)} %get-tuple-element.49), channel_id=1, source_target_pairs={{0,3},{1,2},{2,1},{3,0},{4,7},{5,6},{6,5},{7,4},{8,11},{9,10},{10,... | collective-permute-start | bytes 36872 | tf_op jit(solution)/shard_map/ppermute | solution.py:258
  21.3 4.0 %collective-permute-start.13 = (bf16[48,128]{1,0:T(8,128)(2,1)S(1)}, bf16[48,128]{1,0:T(8,128)(2,1)S(1)}, u32[]{:S(2)}, u32[]{:S(2)}) collective-permute-start(bf16[48,128]{1,0:T(8,128)(2,1)S(1)} %get-tuple-element.49), channel_id=1, source_target_pairs={{0,2},{1,3},{2,0},{3,1},{4,6},{5,7},{6,4},{7,5},{8,10},{9,11},{10,... | collective-permute-start | bytes 36872 | tf_op jit(solution)/shard_map/ppermute | solution.py:258
  22.8 2.4 %collective-permute-start.12 = (bf16[48,128]{1,0:T(8,128)(2,1)S(1)}, bf16[48,128]{1,0:T(8,128)(2,1)S(1)}, u32[]{:S(2)}, u32[]{:S(2)}) collective-permute-start(bf16[48,128]{1,0:T(8,128)(2,1)S(1)} %get-tuple-element.49), channel_id=1, source_target_pairs={{0,1},{1,0},{2,3},{3,2},{4,5},{5,4},{6,7},{7,6},{8,9},{9,8},{10,11... | collective-permute-start | bytes 36872 | tf_op jit(solution)/shard_map/ppermute | solution.py:258
  25.3 6.1 %copy-start = (bf16[64,64,320]{2,1,0:T(8,128)(2,1)S(1)}, bf16[64,64,320]{2,1,0:T(8,128)(2,1)}, u32[]{:S(2)}) copy-start(bf16[64,64,320]{2,1,0:T(8,128)(2,1)} %param.12) | copy-start | bytes 7864324
  25.3 5.6 %collective-permute-start.17 = (bf16[48,128]{1,0:T(8,128)(2,1)S(1)}, bf16[48,128]{1,0:T(8,128)(2,1)S(1)}, u32[]{:S(2)}, u32[]{:S(2)}) collective-permute-start(bf16[48,128]{1,0:T(8,128)(2,1)S(1)} %add_add_fusion.refs_0_), channel_id=1, source_target_pairs={{0,12},{1,13},{2,14},{3,15},{4,8},{5,9},{6,10},{7,11},{8,4},{9,5},... | collective-permute-start | bytes 36872 | tf_op jit(solution)/shard_map/ppermute | solution.py:258
  26.6 4.6 %collective-permute-start.16 = (bf16[48,128]{1,0:T(8,128)(2,1)S(1)}, bf16[48,128]{1,0:T(8,128)(2,1)S(1)}, u32[]{:S(2)}, u32[]{:S(2)}) collective-permute-start(bf16[48,128]{1,0:T(8,128)(2,1)S(1)} %add_add_fusion.refs_0_), channel_id=1, source_target_pairs={{0,8},{1,9},{2,10},{3,11},{4,12},{5,13},{6,14},{7,15},{8,0},{9,1},... | collective-permute-start | bytes 36872 | tf_op jit(solution)/shard_map/ppermute | solution.py:258
  26.8 4.6 %collective-permute-start.15 = (bf16[48,128]{1,0:T(8,128)(2,1)S(1)}, bf16[48,128]{1,0:T(8,128)(2,1)S(1)}, u32[]{:S(2)}, u32[]{:S(2)}) collective-permute-start(bf16[48,128]{1,0:T(8,128)(2,1)S(1)} %add_add_fusion.refs_0_), channel_id=1, source_target_pairs={{0,4},{1,5},{2,6},{3,7},{4,0},{5,1},{6,2},{7,3},{8,12},{9,13},{10,... | collective-permute-start | bytes 36872 | tf_op jit(solution)/shard_map/ppermute | solution.py:258
  33.1 13.4 %all-to-all-start = ((bf16[16,8,3,2,128]{4,3,2,1,0:T(2,128)(2,1)}), bf16[16,8,3,2,128]{4,3,2,1,0:T(2,128)(2,1)S(1)}, u32[]{:S(2)}, u32[]{:S(2)}) async-start(bf16[16,8,3,2,128]{4,3,2,1,0:T(2,128)(2,1)} %update_values.1), calls=%async_computation | async-start | bytes 393216 | tf_op jit(solution)/shard_map/all_to_all | solution.py:699

commit v20 on v19

--- a/solution.py
+++ b/solution.py
@@ -605,8 +605,8 @@
         totals.append(jnp.sum(old, axis=1, keepdims=True) + jnp.sum(new, axis=1, keepdims=True))
         weights.append(old.astype(jnp.bfloat16))
         fresh_weights.append(new.astype(jnp.bfloat16))
+    wait_all(fetches)
     for c in chips:
-        fetches[c].wait()
         values = lanes_of(values_buf[c])
         vn = vn_ref[c].astype(jnp.bfloat16)
         mixed = jnp.dot(weights[c], values, preferred_element_type=jnp.float32)

time: 51.2 us -> 50.8 us (level)
  transfers between devices with their start and end apart: 19 -> 19, of which waited for: 6 -> 6; matrix products, arithmetic and copies ran while one was open for 3% -> 3% of each run, Pallas kernels for 20% -> 21%
where the time goes in v20:
time: 50.8 us; the launch traced here: 50.5 us
  starting transfers between devices  21.9 us (43%)
  Pallas kernels  17.9 us (35%)
  waiting for transfers between devices  8.71 us (17%)
  other arithmetic  1.53 us (3%)
    ppermute x18, starting transfers between devices, trade(): return lax.ppermute(value, 'replica', [(i, i ^ mask) for i in range(count)])  17.4 us
    pallas_call x1, Pallas kernels, cache_by_head(): pl.pallas_call(functools.partial(cache_kernel, first), out_shape=(jax.Sha...  6.4 us
    ppermute x18, waiting for transfers between devices, trade(): return lax.ppermute(value, 'replica', [(i, i ^ mask) for i in range(count)])  6.25 us
    all_to_all x1, starting transfers between devices, chip_plan(): lax.all_to_all(send, 'replica', split_axis=0, concat_axis=0, tiled=True)  4.44 us
    pallas_call x1, Pallas kernels, attend(): pl.pallas_call(attend_kernel, out_shape=jax.ShapeDtypeStruct((steps, head...  3.83 us
    pallas_call x3, Pallas kernels, project(): pl.pallas_call(functools.partial(project_kernel, which), out_shape=chunks...  3.44 us
    all_to_all x1, waiting for transfers between devices, chip_plan(): lax.all_to_all(send, 'replica', split_axis=0, concat_axis=0, tiled=True)  2.46 us
    pallas_call x1, Pallas kernels, low_of(): pl.pallas_call(functools.partial(low_kernel, tuple(blocks), packs), out_s...  2.09 us
  transfers between devices with their start and end apart: 19, of which 6 were waited for; matrix products, arithmetic and copies ran while one was open for 3% of the time, Pallas kernels for 21%

profile of v20, /device:TPU:0, one launch (start us, length us, event | category | flops | bytes accessed | tf_op | source)
XLA Modules:
  0.0 50.5 jit_solution(4514084168229976570)
XLA Ops:
  0.0 4.0 %collective-permute-start.1 = (bf16[3,2,5120]{2,1,0:T(2,128)(2,1)}, bf16[3,2,5120]{2,1,0:T(2,128)(2,1)S(1)}, u32[]{:S(2)}, u32[]{:S(2)}) collective-permute-start(bf16[3,2,5120]{2,1,0:T(2,128)(2,1)} %param.9), channel_id=1, source_target_pairs={{0,8},{1,9},{2,10},{3,11},{4,12},{5,13},{6,14},{7,15},{8,0},{9,1},... | collective-permute-start | bytes 184328 | tf_op jit(solution)/shard_map/ppermute | solution.py:258
  4.0 1.6 %collective-permute-start = (bf16[3,2,5120]{2,1,0:T(2,128)(2,1)}, bf16[3,2,5120]{2,1,0:T(2,128)(2,1)S(1)}, u32[]{:S(2)}, u32[]{:S(2)}) collective-permute-start(bf16[3,2,5120]{2,1,0:T(2,128)(2,1)} %param.9), channel_id=1, source_target_pairs={{0,4},{1,5},{2,6},{3,7},{4,0},{5,1},{6,2},{7,3},{8,12},{9,13},{10,... | collective-permute-start | bytes 184328 | tf_op jit(solution)/shard_map/ppermute | solution.py:258
  5.6 1.5 %collective-permute-start.3 = (bf16[3,2,5120]{2,1,0:T(2,128)(2,1)}, bf16[3,2,5120]{2,1,0:T(2,128)(2,1)S(1)}, u32[]{:S(2)}, u32[]{:S(2)}) collective-permute-start(bf16[3,2,5120]{2,1,0:T(2,128)(2,1)} %param.9), channel_id=1, source_target_pairs={{0,2},{1,3},{2,0},{3,1},{4,6},{5,7},{6,4},{7,5},{8,10},{9,11},{10,... | collective-permute-start | bytes 184328 | tf_op jit(solution)/shard_map/ppermute | solution.py:258
  7.1 0.2 collective-permute-start.2
  7.4 0.9 %select_reduce_fusion.1 = s32[32]{0:T(128)S(1)} fusion(s32[64]{0:T(128)} %param.13, s32[32]{0:T(128)} %param.14), kind=kLoop, calls=%fused_computation.1 | loop fusion | flops 6112 | bytes 512 | tf_op jit(solution)/shard_map/reduce_sum | solution.py:662
  8.2 0.0 slice-start
  8.3 0.0 copy-start.3
  8.3 0.0 copy-start.4
  8.3 0.0 copy-start.2
  8.3 0.0 copy-start.1
  8.3 0.0 slice-start.1
  8.3 0.2 index_work.1
  8.5 1.5 %collective-permute-start.4 = (bf16[3,2,5120]{2,1,0:T(2,128)(2,1)S(1)}, bf16[3,2,5120]{2,1,0:T(2,128)(2,1)S(1)}, u32[]{:S(2)}, u32[]{:S(2)}) collective-permute-start(bf16[3,2,5120]{2,1,0:T(2,128)(2,1)S(1)} %collective-permute-done), channel_id=1, source_target_pairs={{0,2},{1,3},{2,0},{3,1},{4,6},{5,7},{6,4},{7,5},{8,10},{9,11},{10,... | collective-permute-start | bytes 184328 | tf_op jit(solution)/shard_map/ppermute | solution.py:258
  10.0 0.0 collective-permute-done.1
  10.0 0.6 %collective-permute-start.6 = (bf16[3,2,5120]{2,1,0:T(2,128)(2,1)S(1)}, bf16[3,2,5120]{2,1,0:T(2,128)(2,1)S(1)}, u32[]{:S(2)}, u32[]{:S(2)}) collective-permute-start(bf16[3,2,5120]{2,1,0:T(2,128)(2,1)S(1)} %collective-permute-done.1), channel_id=1, source_target_pairs={{0,2},{1,3},{2,0},{3,1},{4,6},{5,7},{6,4},{7,5},{8,10},{9,11},{10,... | collective-permute-start | bytes 184328 | tf_op jit(solution)/shard_map/ppermute | solution.py:258
  10.6 0.1 select_reduce_fusion
  10.7 2.7 %collective-permute-done.2 = bf16[3,2,5120]{2,1,0:T(2,128)(2,1)S(1)} collective-permute-done((bf16[3,2,5120]{2,1,0:T(2,128)(2,1)}, bf16[3,2,5120]{2,1,0:T(2,128)(2,1)S(1)}, u32[]{:S(2)}, u32[]{:S(2)}) %collective-permute-start.2) | collective-permute-done | bytes 61472 | tf_op jit(solution)/shard_map/ppermute | solution.py:258
  13.4 0.5 %collective-permute-start.7 = (bf16[3,2,5120]{2,1,0:T(2,128)(2,1)S(1)}, bf16[3,2,5120]{2,1,0:T(2,128)(2,1)S(1)}, u32[]{:S(2)}, u32[]{:S(2)}) collective-permute-start(bf16[3,2,5120]{2,1,0:T(2,128)(2,1)S(1)} %collective-permute-done.2), channel_id=1, source_target_pairs={{0,2},{1,3},{2,0},{3,1},{4,6},{5,7},{6,4},{7,5},{8,10},{9,11},{10,... | collective-permute-start | bytes 184328 | tf_op jit(solution)/shard_map/ppermute | solution.py:258
  13.9 0.2 fusion.3
  14.1 0.4 pack_blocks.1
  14.4 0.1 collective-permute-start.5
  14.5 0.1 and_convert_fusion.live_ref
  14.6 0.5 collective-permute-start.10
  15.1 0.1 collective-permute-start.8
  15.2 0.4 collective-permute-start.9
  15.6 2.0 %collective-permute-done.7 = bf16[3,2,5120]{2,1,0:T(2,128)(2,1)S(1)} collective-permute-done((bf16[3,2,5120]{2,1,0:T(2,128)(2,1)S(1)}, bf16[3,2,5120]{2,1,0:T(2,128)(2,1)S(1)}, u32[]{:S(2)}, u32[]{:S(2)}) %collective-permute-start.7) | collective-permute-done | bytes 61472 | tf_op jit(solution)/shard_map/ppermute | solution.py:258
  17.6 0.0 collective-permute-start.11
  17.6 0.2 select_reduce_fusion.2
  17.8 1.0 %collective-permute-done.11.refs_11_ = bf16[3,40,2,128]{3,2,1,0:T(2,128)(2,1)S(1)} collective-permute-done((bf16[3,40,2,128]{3,2,1,0:T(2,128)(2,1)S(1)}, bf16[3,40,2,128]{3,2,1,0:T(2,128)(2,1)S(1)}, u32[]{:S(2)}, u32[]{:S(2)}) %collective-permute-start.11) | collective-permute-done | bytes 61472 | tf_op jit(solution)/shard_map/ppermute | solution.py:258
  18.8 2.1 %low_rows.1 = (bf16[3,40,16,2,128]{4,3,2,1,0:T(2,128)(2,1)S(1)}, bf16[48,128]{1,0:T(8,128)(2,1)S(1)}) custom-call(s32[1]{0:T(128)} %bitcast.1.me_ref, s32[1,96]{1,0:T(1,128)S(1)} %get-tuple-element.42.slot_ref, bf16[4,64,5120]{2,1,0:T(8,128)(2,1)S(1)} %copy-done.1, bf16[4,3,40,2,128]{4,3,2,1,0:T(2,128)(2,1)S(1)} %collective-permute-done.5.pack_ref, ...), custom_call_target="tpu_custom_call" | custom-call | flops 100000000 | bytes 4000000 | tf_op jit(solution)/shard_map/low_rows/pallas_call | solution.py:421
  20.9 0.3 collective-permute-start.14
  21.3 1.5 %collective-permute-start.13 = (bf16[48,128]{1,0:T(8,128)(2,1)S(1)}, bf16[48,128]{1,0:T(8,128)(2,1)S(1)}, u32[]{:S(2)}, u32[]{:S(2)}) collective-permute-start(bf16[48,128]{1,0:T(8,128)(2,1)S(1)} %get-tuple-element.49), channel_id=1, source_target_pairs={{0,2},{1,3},{2,0},{3,1},{4,6},{5,7},{6,4},{7,5},{8,10},{9,11},{10,... | collective-permute-start | bytes 36872 | tf_op jit(solution)/shard_map/ppermute | solution.py:258
  22.8 0.1 collective-permute-start.12
  22.9 1.2 %project.4.key_ref = bf16[3,3,16,2,128]{4,3,2,1,0:T(2,128)(2,1)S(1)} custom-call(bf16[3,40,16,2,128]{4,3,2,1,0:T(2,128)(2,1)S(1)} %get-tuple-element.50.x_ref, bf16[3,320,5120]{2,1,0:T(8,128)(2,1)S(1)} %bitcast.37), custom_call_target="tpu_custom_call" | custom-call | flops 500000000 | bytes 4000000 | tf_op jit(solution)/shard_map/project/pallas_call | solution.py:464
  24.1 1.1 %project.3.query_ref = bf16[3,3,16,2,128]{4,3,2,1,0:T(2,128)(2,1)S(1)} custom-call(bf16[3,40,16,2,128]{4,3,2,1,0:T(2,128)(2,1)S(1)} %get-tuple-element.50.x_ref, bf16[3,320,5120]{2,1,0:T(8,128)(2,1)S(1)} %bitcast.38), custom_call_target="tpu_custom_call" | custom-call | flops 500000000 | bytes 4000000 | tf_op jit(solution)/shard_map/project/pallas_call | solution.py:464
  25.3 0.0 copy-start
  25.3 1.3 %collective-permute-start.17 = (bf16[48,128]{1,0:T(8,128)(2,1)S(1)}, bf16[48,128]{1,0:T(8,128)(2,1)S(1)}, u32[]{:S(2)}, u32[]{:S(2)}) collective-permute-start(bf16[48,128]{1,0:T(8,128)(2,1)S(1)} %add_add_fusion.refs_0_), channel_id=1, source_target_pairs={{0,12},{1,13},{2,14},{3,15},{4,8},{5,9},{6,10},{7,11},{8,4},{9,5},... | collective-permute-start | bytes 36872 | tf_op jit(solution)/shard_map/ppermute | solution.py:258
  26.6 0.2 collective-permute-start.16
  26.8 2.9 %collective-permute-start.15 = (bf16[48,128]{1,0:T(8,128)(2,1)S(1)}, bf16[48,128]{1,0:T(8,128)(2,1)S(1)}, u32[]{:S(2)}, u32[]{:S(2)}) collective-permute-start(bf16[48,128]{1,0:T(8,128)(2,1)S(1)} %add_add_fusion.refs_0_), channel_id=1, source_target_pairs={{0,4},{1,5},{2,6},{3,7},{4,0},{5,1},{6,2},{7,3},{8,12},{9,13},{10,... | collective-permute-start | bytes 36872 | tf_op jit(solution)/shard_map/ppermute | solution.py:258
  29.7 1.1 %project.5.base_ref = f32[96,320]{1,0:T(8,128)S(1)} custom-call(bf16[3,40,16,2,128]{4,3,2,1,0:T(2,128)(2,1)S(1)} %get-tuple-element.50.x_ref, bf16[3,320,5120]{2,1,0:T(8,128)(2,1)S(1)} %bitcast.39), custom_call_target="tpu_custom_call" | custom-call | flops 500000000 | bytes 4000000 | tf_op jit(solution)/shard_map/project/pallas_call | solution.py:464
  30.9 0.3 collective-permute-done.16.refs_2_
  31.2 0.2 collective-permute-done.15.refs_1_
  31.4 1.7 %update_values.1 = bf16[16,8,3,2,128]{4,3,2,1,0:T(2,128)(2,1)} custom-call(s32[96,1]{1,0:T(8,128)S(1)} %get-tuple-element.40.stored_ref, bf16[3,3,16,2,128]{4,3,2,1,0:T(2,128)(2,1)S(1)} %project.3.query_ref, bf16[3,3,16,2,128]{4,3,2,1,0:T(2,128)(2,1)S(1)} %project.4.key_ref, f32[96,320]{1,0:T(8,128)S(1)} %project.5.base_ref, bf16[4096,320]{1,0:T(8,128)(2,1)S(1)} %bitcast.40, ...), custom_call_target="tpu_custom_call" | custom-call | flops 300000000 | bytes 4000000 | tf_op jit(solution)/shard_map/update_values/pallas_call | solution.py:504
  33.1 4.4 %all-to-all-start = ((bf16[16,8,3,2,128]{4,3,2,1,0:T(2,128)(2,1)}), bf16[16,8,3,2,128]{4,3,2,1,0:T(2,128)(2,1)S(1)}, u32[]{:S(2)}, u32[]{:S(2)}) async-start(bf16[16,8,3,2,128]{4,3,2,1,0:T(2,128)(2,1)} %update_values.1), calls=%async_computation | async-start | bytes 393216 | tf_op jit(solution)/shard_map/all_to_all | solution.py:699
  37.5 0.1 fusion
  37.6 6.4 %cache_by_head.1 = (bf16[40,256,128]{2,1,0:T(8,128)(2,1)S(1)}, bf16[40,256,128]{2,1,0:T(8,128)(2,1)}) custom-call(bf16[256,40,2,128]{3,2,1,0:T(2,128)(2,1)} %bitcast.58), custom_call_target="tpu_custom_call" | custom-call | bytes 12000000 | tf_op jit(solution)/shard_map/cache_by_head/pallas_call | solution.py:321
  44.1 2.5 %all-to-all-done.pieces_ref = bf16[16,8,3,2,128]{4,3,2,1,0:T(2,128)(2,1)S(1)} async-done(((bf16[16,8,3,2,128]{4,3,2,1,0:T(2,128)(2,1)}), bf16[16,8,3,2,128]{4,3,2,1,0:T(2,128)(2,1)S(1)}, u32[]{:S(2)}, u32[]{:S(2)}) %all-to-all-start) | async-done | bytes 196640 | tf_op jit(solution)/shard_map/all_to_all | solution.py:699
  46.5 3.8 %attention.1 = bf16[3,40,2,128]{3,2,1,0:T(2,128)(2,1)} custom-call(f32[8,128]{1,0:T(8,128)S(1)} %get-tuple-element.66.cos_ref, f32[8,128]{1,0:T(8,128)S(1)} %get-tuple-element.65.sin_ref, s32[2,256]{1,0:T(2,128)S(1)} %and_convert_fusion.live_ref, bf16[16,8,3,2,128]{4,3,2,1,0:T(2,128)(2,1)S(1)} %all-to-all-done.pieces_ref, ...), custom_call_target="tpu_custom_call" | custom-call | flops 1000000000 | bytes 6000000 | tf_op jit(solution)/shard_map/attention/pallas_call | solution.py:626
  (29 shorter events, 0.1 us)
Async XLA Ops:
  0.0 10.0 %collective-permute-start.1 = (bf16[3,2,5120]{2,1,0:T(2,128)(2,1)}, bf16[3,2,5120]{2,1,0:T(2,128)(2,1)S(1)}, u32[]{:S(2)}, u32[]{:S(2)}) collective-permute-start(bf16[3,2,5120]{2,1,0:T(2,128)(2,1)} %param.9), channel_id=1, source_target_pairs={{0,8},{1,9},{2,10},{3,11},{4,12},{5,13},{6,14},{7,15},{8,0},{9,1},... | collective-permute-start | bytes 184328 | tf_op jit(solution)/shard_map/ppermute | solution.py:258
  4.0 4.5 %collective-permute-start = (bf16[3,2,5120]{2,1,0:T(2,128)(2,1)}, bf16[3,2,5120]{2,1,0:T(2,128)(2,1)S(1)}, u32[]{:S(2)}, u32[]{:S(2)}) collective-permute-start(bf16[3,2,5120]{2,1,0:T(2,128)(2,1)} %param.9), channel_id=1, source_target_pairs={{0,4},{1,5},{2,6},{3,7},{4,0},{5,1},{6,2},{7,3},{8,12},{9,13},{10,... | collective-permute-start | bytes 184328 | tf_op jit(solution)/shard_map/ppermute | solution.py:258
  5.6 8.4 %collective-permute-start.3 = (bf16[3,2,5120]{2,1,0:T(2,128)(2,1)}, bf16[3,2,5120]{2,1,0:T(2,128)(2,1)S(1)}, u32[]{:S(2)}, u32[]{:S(2)}) collective-permute-start(bf16[3,2,5120]{2,1,0:T(2,128)(2,1)} %param.9), channel_id=1, source_target_pairs={{0,2},{1,3},{2,0},{3,1},{4,6},{5,7},{6,4},{7,5},{8,10},{9,11},{10,... | collective-permute-start | bytes 184328 | tf_op jit(solution)/shard_map/ppermute | solution.py:258
  7.1 6.2 %collective-permute-start.2 = (bf16[3,2,5120]{2,1,0:T(2,128)(2,1)}, bf16[3,2,5120]{2,1,0:T(2,128)(2,1)S(1)}, u32[]{:S(2)}, u32[]{:S(2)}) collective-permute-start(bf16[3,2,5120]{2,1,0:T(2,128)(2,1)} %param.9), channel_id=1, source_target_pairs={{0,12},{1,13},{2,14},{3,15},{4,8},{5,9},{6,10},{7,11},{8,4},{9,5},... | collective-permute-start | bytes 184328 | tf_op jit(solution)/shard_map/ppermute | solution.py:258
  8.2 14.6 %slice-start = ((s8[9830400]{0:T(1024)(128)(4,1)}), s8[4194304]{0:T(1024)(128)(4,1)S(1)}, s32[]{:S(2)}) async-start(s8[9830400]{0:T(1024)(128)(4,1)} %bitcast.35), calls=%async_computation.1 | async-start | bytes 8388608
  8.3 2.4 %copy-start.3 = (s32[2,32]{1,0:T(2,128)S(1)}, s32[2,32]{1,0:T(2,128)}, u32[]{:S(2)}) copy-start(s32[2,32]{1,0:T(2,128)} %param.16) | copy-start | bytes 772
  8.3 5.6 %copy-start.4 = (s32[32]{0:T(128)S(1)}, s32[32]{0:T(128)}, u32[]{:S(2)}) copy-start(s32[32]{0:T(128)} %param.15) | copy-start | bytes 388
  8.3 5.8 %copy-start.2 = (bf16[3,2,5120]{2,1,0:T(2,128)(2,1)S(1)}, bf16[3,2,5120]{2,1,0:T(2,128)(2,1)}, u32[]{:S(2)}) copy-start(bf16[3,2,5120]{2,1,0:T(2,128)(2,1)} %param.9) | copy-start | bytes 184324
  8.3 10.6 %copy-start.1 = (bf16[4,64,5120]{2,1,0:T(8,128)(2,1)S(1)}, bf16[4,64,5120]{2,1,0:T(8,128)(2,1)}, u32[]{:S(2)}) copy-start(bf16[4,64,5120]{2,1,0:T(8,128)(2,1)} %down_ref.1) | copy-start | bytes 7864324
  8.3 14.6 %slice-start.1 = ((s8[9830400]{0:T(1024)(128)(4,1)}), s8[4194304]{0:T(1024)(128)(4,1)S(1)}, s32[]{:S(2)}) async-start(s8[9830400]{0:T(1024)(128)(4,1)} %bitcast.35), calls=%async_computation.2 | async-start | bytes 8388608
  8.3 14.6 %slice-start.2 = ((s8[9830400]{0:T(1024)(128)(4,1)}), s8[1441792]{0:T(1024)(128)(4,1)S(1)}, s32[]{:S(2)}) async-start(s8[9830400]{0:T(1024)(128)(4,1)} %bitcast.35), calls=%async_computation.3 | async-start | bytes 2883584
  8.5 5.5 %collective-permute-start.4 = (bf16[3,2,5120]{2,1,0:T(2,128)(2,1)S(1)}, bf16[3,2,5120]{2,1,0:T(2,128)(2,1)S(1)}, u32[]{:S(2)}, u32[]{:S(2)}) collective-permute-start(bf16[3,2,5120]{2,1,0:T(2,128)(2,1)S(1)} %collective-permute-done), channel_id=1, source_target_pairs={{0,2},{1,3},{2,0},{3,1},{4,6},{5,7},{6,4},{7,5},{8,10},{9,11},{10,... | collective-permute-start | bytes 184328 | tf_op jit(solution)/shard_map/ppermute | solution.py:258
  10.0 4.6 %collective-permute-start.6 = (bf16[3,2,5120]{2,1,0:T(2,128)(2,1)S(1)}, bf16[3,2,5120]{2,1,0:T(2,128)(2,1)S(1)}, u32[]{:S(2)}, u32[]{:S(2)}) collective-permute-start(bf16[3,2,5120]{2,1,0:T(2,128)(2,1)S(1)} %collective-permute-done.1), channel_id=1, source_target_pairs={{0,2},{1,3},{2,0},{3,1},{4,6},{5,7},{6,4},{7,5},{8,10},{9,11},{10,... | collective-permute-start | bytes 184328 | tf_op jit(solution)/shard_map/ppermute | solution.py:258
  13.4 4.2 %collective-permute-start.7 = (bf16[3,2,5120]{2,1,0:T(2,128)(2,1)S(1)}, bf16[3,2,5120]{2,1,0:T(2,128)(2,1)S(1)}, u32[]{:S(2)}, u32[]{:S(2)}) collective-permute-start(bf16[3,2,5120]{2,1,0:T(2,128)(2,1)S(1)} %collective-permute-done.2), channel_id=1, source_target_pairs={{0,2},{1,3},{2,0},{3,1},{4,6},{5,7},{6,4},{7,5},{8,10},{9,11},{10,... | collective-permute-start | bytes 184328 | tf_op jit(solution)/shard_map/ppermute | solution.py:258
  14.4 4.4 %collective-permute-start.5 = (bf16[4,3,40,2,128]{4,3,2,1,0:T(2,128)(2,1)S(1)}, bf16[4,3,40,2,128]{4,3,2,1,0:T(2,128)(2,1)S(1)}, u32[]{:S(2)}, u32[]{:S(2)}) collective-permute-start(bf16[4,3,40,2,128]{4,3,2,1,0:T(2,128)(2,1)S(1)} %pack_blocks.1), channel_id=1, source_target_pairs={{0,1},{1,0},{2,3},{3,2},{4,5},{5,4},{6,7},{7,6},{8,9},{9,8},{10,11... | collective-permute-start | bytes 737288 | tf_op jit(solution)/shard_map/ppermute | solution.py:258
  14.6 3.2 %collective-permute-start.10 = (bf16[3,40,2,128]{3,2,1,0:T(2,128)(2,1)S(1)}, bf16[3,40,2,128]{3,2,1,0:T(2,128)(2,1)S(1)}, u32[]{:S(2)}, u32[]{:S(2)}) collective-permute-start(bf16[3,40,2,128]{3,2,1,0:T(2,128)(2,1)S(1)} %bitcast.53), channel_id=1, source_target_pairs={{0,1},{1,0},{2,3},{3,2},{4,5},{5,4},{6,7},{7,6},{8,9},{9,8},{10,11... | collective-permute-start | bytes 184328 | tf_op jit(solution)/shard_map/ppermute | solution.py:258
  15.1 2.7 %collective-permute-start.8 = (bf16[3,40,2,128]{3,2,1,0:T(2,128)(2,1)S(1)}, bf16[3,40,2,128]{3,2,1,0:T(2,128)(2,1)S(1)}, u32[]{:S(2)}, u32[]{:S(2)}) collective-permute-start(bf16[3,40,2,128]{3,2,1,0:T(2,128)(2,1)S(1)} %bitcast.49), channel_id=1, source_target_pairs={{0,1},{1,0},{2,3},{3,2},{4,5},{5,4},{6,7},{7,6},{8,9},{9,8},{10,11... | collective-permute-start | bytes 184328 | tf_op jit(solution)/shard_map/ppermute | solution.py:258
  15.2 2.6 %collective-permute-start.9 = (bf16[3,40,2,128]{3,2,1,0:T(2,128)(2,1)S(1)}, bf16[3,40,2,128]{3,2,1,0:T(2,128)(2,1)S(1)}, u32[]{:S(2)}, u32[]{:S(2)}) collective-permute-start(bf16[3,40,2,128]{3,2,1,0:T(2,128)(2,1)S(1)} %bitcast.51), channel_id=1, source_target_pairs={{0,1},{1,0},{2,3},{3,2},{4,5},{5,4},{6,7},{7,6},{8,9},{9,8},{10,11... | collective-permute-start | bytes 184328 | tf_op jit(solution)/shard_map/ppermute | solution.py:258
  17.6 1.2 %collective-permute-start.11 = (bf16[3,40,2,128]{3,2,1,0:T(2,128)(2,1)S(1)}, bf16[3,40,2,128]{3,2,1,0:T(2,128)(2,1)S(1)}, u32[]{:S(2)}, u32[]{:S(2)}) collective-permute-start(bf16[3,40,2,128]{3,2,1,0:T(2,128)(2,1)S(1)} %bitcast.55), channel_id=1, source_target_pairs={{0,1},{1,0},{2,3},{3,2},{4,5},{5,4},{6,7},{7,6},{8,9},{9,8},{10,11... | collective-permute-start | bytes 184328 | tf_op jit(solution)/shard_map/ppermute | solution.py:258
  20.9 4.3 %collective-permute-start.14 = (bf16[48,128]{1,0:T(8,128)(2,1)S(1)}, bf16[48,128]{1,0:T(8,128)(2,1)S(1)}, u32[]{:S(2)}, u32[]{:S(2)}) collective-permute-start(bf16[48,128]{1,0:T(8,128)(2,1)S(1)} %get-tuple-element.49), channel_id=1, source_target_pairs={{0,3},{1,2},{2,1},{3,0},{4,7},{5,6},{6,5},{7,4},{8,11},{9,10},{10,... | collective-permute-start | bytes 36872 | tf_op jit(solution)/shard_map/ppermute | solution.py:258
  21.3 4.0 %collective-permute-start.13 = (bf16[48,128]{1,0:T(8,128)(2,1)S(1)}, bf16[48,128]{1,0:T(8,128)(2,1)S(1)}, u32[]{:S(2)}, u32[]{:S(2)}) collective-permute-start(bf16[48,128]{1,0:T(8,128)(2,1)S(1)} %get-tuple-element.49), channel_id=1, source_target_pairs={{0,2},{1,3},{2,0},{3,1},{4,6},{5,7},{6,4},{7,5},{8,10},{9,11},{10,... | collective-permute-start | bytes 36872 | tf_op jit(solution)/shard_map/ppermute | solution.py:258
  22.8 2.4 %collective-permute-start.12 = (bf16[48,128]{1,0:T(8,128)(2,1)S(1)}, bf16[48,128]{1,0:T(8,128)(2,1)S(1)}, u32[]{:S(2)}, u32[]{:S(2)}) collective-permute-start(bf16[48,128]{1,0:T(8,128)(2,1)S(1)} %get-tuple-element.49), channel_id=1, source_target_pairs={{0,1},{1,0},{2,3},{3,2},{4,5},{5,4},{6,7},{7,6},{8,9},{9,8},{10,11... | collective-permute-start | bytes 36872 | tf_op jit(solution)/shard_map/ppermute | solution.py:258
  25.3 6.1 %copy-start = (bf16[64,64,320]{2,1,0:T(8,128)(2,1)S(1)}, bf16[64,64,320]{2,1,0:T(8,128)(2,1)}, u32[]{:S(2)}) copy-start(bf16[64,64,320]{2,1,0:T(8,128)(2,1)} %param.12) | copy-start | bytes 7864324
  25.3 5.6 %collective-permute-start.17 = (bf16[48,128]{1,0:T(8,128)(2,1)S(1)}, bf16[48,128]{1,0:T(8,128)(2,1)S(1)}, u32[]{:S(2)}, u32[]{:S(2)}) collective-permute-start(bf16[48,128]{1,0:T(8,128)(2,1)S(1)} %add_add_fusion.refs_0_), channel_id=1, source_target_pairs={{0,12},{1,13},{2,14},{3,15},{4,8},{5,9},{6,10},{7,11},{8,4},{9,5},... | collective-permute-start | bytes 36872 | tf_op jit(solution)/shard_map/ppermute | solution.py:258
  26.6 4.6 %collective-permute-start.16 = (bf16[48,128]{1,0:T(8,128)(2,1)S(1)}, bf16[48,128]{1,0:T(8,128)(2,1)S(1)}, u32[]{:S(2)}, u32[]{:S(2)}) collective-permute-start(bf16[48,128]{1,0:T(8,128)(2,1)S(1)} %add_add_fusion.refs_0_), channel_id=1, source_target_pairs={{0,8},{1,9},{2,10},{3,11},{4,12},{5,13},{6,14},{7,15},{8,0},{9,1},... | collective-permute-start | bytes 36872 | tf_op jit(solution)/shard_map/ppermute | solution.py:258
  26.8 4.6 %collective-permute-start.15 = (bf16[48,128]{1,0:T(8,128)(2,1)S(1)}, bf16[48,128]{1,0:T(8,128)(2,1)S(1)}, u32[]{:S(2)}, u32[]{:S(2)}) collective-permute-start(bf16[48,128]{1,0:T(8,128)(2,1)S(1)} %add_add_fusion.refs_0_), channel_id=1, source_target_pairs={{0,4},{1,5},{2,6},{3,7},{4,0},{5,1},{6,2},{7,3},{8,12},{9,13},{10,... | collective-permute-start | bytes 36872 | tf_op jit(solution)/shard_map/ppermute | solution.py:258
  33.1 13.4 %all-to-all-start = ((bf16[16,8,3,2,128]{4,3,2,1,0:T(2,128)(2,1)}), bf16[16,8,3,2,128]{4,3,2,1,0:T(2,128)(2,1)S(1)}, u32[]{:S(2)}, u32[]{:S(2)}) async-start(bf16[16,8,3,2,128]{4,3,2,1,0:T(2,128)(2,1)} %update_values.1), calls=%async_computation | async-start | bytes 393216 | tf_op jit(solution)/shard_map/all_to_all | solution.py:699

commit v21 on v20

--- a/solution.py
+++ b/solution.py
@@ -677,6 +677,8 @@
     _, lengths, request_page_table = lax.optimization_barrier((held[4], lengths, request_page_table))
     cosine, sine = rotation_rows(lengths, first, req_dev, steps)
     live = live_lanes(lengths, first, request_page_table, tokens, page_len)
+    far = count - 4
+    held[4], held[far] = lax.optimization_barrier((held[4], held[far]))
     held.update({k | 2: trade(v, 2, count) for k, v in list(held.items())})
     held = {k: v.reshape(steps, req_dev, heads, HD).transpose(0, 2, 1, 3) for k, v in held.items()}
     line = tuple(range(0, count, 4))

time: 50.8 us -> 50.1 us (0.986)
  waiting for transfers between devices: 8.71 us -> 7.87 us
    ppermute x18, starting transfers between devices: 17.4 us -> 18.3 us  [trade(): return lax.ppermute(value, 'replica', [(i, i ^ mask) for i in range(count)])]
    ppermute x18, waiting for transfers between devices: 6.25 us -> 5.51 us  [trade(): return lax.ppermute(value, 'replica', [(i, i ^ mask) for i in range(count)])]
    all_to_all x1, starting transfers between devices: 4.44 us -> 3.74 us  [chip_plan(): lax.all_to_all(send, 'replica', split_axis=0, concat_axis=0, tiled=True)]
  transfers between devices with their start and end apart: 19 -> 19, of which waited for: 6 -> 12; matrix products, arithmetic and copies ran while one was open for 3% -> 3% of each run, Pallas kernels for 21% -> 21%
where the time goes in v21:
time: 50.1 us; the launch traced here: 49.8 us
  starting transfers between devices  22.1 us (44%)
  Pallas kernels  17.9 us (36%)
  waiting for transfers between devices  7.87 us (16%)
  other arithmetic  1.53 us (3%)
    ppermute x18, starting transfers between devices, trade(): return lax.ppermute(value, 'replica', [(i, i ^ mask) for i in range(count)])  18.3 us
    pallas_call x1, Pallas kernels, cache_by_head(): pl.pallas_call(functools.partial(cache_kernel, first), out_shape=(jax.Sha...  6.4 us
    ppermute x18, waiting for transfers between devices, trade(): return lax.ppermute(value, 'replica', [(i, i ^ mask) for i in range(count)])  5.51 us
    pallas_call x1, Pallas kernels, attend(): pl.pallas_call(attend_kernel, out_shape=jax.ShapeDtypeStruct((steps, head...  3.83 us
    all_to_all x1, starting transfers between devices, chip_plan(): lax.all_to_all(send, 'replica', split_axis=0, concat_axis=0, tiled=True)  3.74 us
    pallas_call x3, Pallas kernels, project(): pl.pallas_call(functools.partial(project_kernel, which), out_shape=chunks...  3.45 us
    all_to_all x1, waiting for transfers between devices, chip_plan(): lax.all_to_all(send, 'replica', split_axis=0, concat_axis=0, tiled=True)  2.36 us
    pallas_call x1, Pallas kernels, low_of(): pl.pallas_call(functools.partial(low_kernel, tuple(blocks), packs), out_s...  2.09 us
  transfers between devices with their start and end apart: 19, of which 12 were waited for; matrix products, arithmetic and copies ran while one was open for 3% of the time, Pallas kernels for 21%

profile of v21, /device:TPU:0, one launch (start us, length us, event | category | flops | bytes accessed | tf_op | source)
XLA Modules:
  0.0 49.8 jit_solution(2189856487420672226)
XLA Ops:
  0.0 5.0 %collective-permute-start.1 = (bf16[3,2,5120]{2,1,0:T(2,128)(2,1)}, bf16[3,2,5120]{2,1,0:T(2,128)(2,1)S(1)}, u32[]{:S(2)}, u32[]{:S(2)}) collective-permute-start(bf16[3,2,5120]{2,1,0:T(2,128)(2,1)} %param.9), channel_id=1, source_target_pairs={{0,12},{1,13},{2,14},{3,15},{4,8},{5,9},{6,10},{7,11},{8,4},{9,5},... | collective-permute-start | bytes 184328 | tf_op jit(solution)/shard_map/ppermute | solution.py:258
  5.1 1.5 %collective-permute-start.3 = (bf16[3,2,5120]{2,1,0:T(2,128)(2,1)}, bf16[3,2,5120]{2,1,0:T(2,128)(2,1)S(1)}, u32[]{:S(2)}, u32[]{:S(2)}) collective-permute-start(bf16[3,2,5120]{2,1,0:T(2,128)(2,1)} %param.9), channel_id=1, source_target_pairs={{0,2},{1,3},{2,0},{3,1},{4,6},{5,7},{6,4},{7,5},{8,10},{9,11},{10,... | collective-permute-start | bytes 184328 | tf_op jit(solution)/shard_map/ppermute | solution.py:258
  6.6 0.8 %collective-permute-start.2 = (bf16[3,2,5120]{2,1,0:T(2,128)(2,1)}, bf16[3,2,5120]{2,1,0:T(2,128)(2,1)S(1)}, u32[]{:S(2)}, u32[]{:S(2)}) collective-permute-start(bf16[3,2,5120]{2,1,0:T(2,128)(2,1)} %param.9), channel_id=1, source_target_pairs={{0,8},{1,9},{2,10},{3,11},{4,12},{5,13},{6,14},{7,15},{8,0},{9,1},... | collective-permute-start | bytes 184328 | tf_op jit(solution)/shard_map/ppermute | solution.py:258
  7.4 0.9 %select_reduce_fusion.1 = s32[32]{0:T(128)S(1)} fusion(s32[64]{0:T(128)} %param.13, s32[32]{0:T(128)} %param.14), kind=kLoop, calls=%fused_computation.1 | loop fusion | flops 6112 | bytes 512 | tf_op jit(solution)/shard_map/reduce_sum | solution.py:662
  8.2 0.0 slice-start
  8.3 0.0 copy-start.3
  8.3 0.0 copy-start.2
  8.3 0.0 copy-start.1
  8.3 0.2 index_work.1
  8.5 1.0 %collective-permute-done = bf16[3,2,5120]{2,1,0:T(2,128)(2,1)S(1)} collective-permute-done((bf16[3,2,5120]{2,1,0:T(2,128)(2,1)}, bf16[3,2,5120]{2,1,0:T(2,128)(2,1)S(1)}, u32[]{:S(2)}, u32[]{:S(2)}) %collective-permute-start) | collective-permute-done | bytes 61472 | tf_op jit(solution)/shard_map/ppermute | solution.py:258
  9.5 1.9 %collective-permute-start.4 = (bf16[3,2,5120]{2,1,0:T(2,128)(2,1)S(1)}, bf16[3,2,5120]{2,1,0:T(2,128)(2,1)S(1)}, u32[]{:S(2)}, u32[]{:S(2)}) collective-permute-start(bf16[3,2,5120]{2,1,0:T(2,128)(2,1)S(1)} %collective-permute-done), channel_id=1, source_target_pairs={{0,2},{1,3},{2,0},{3,1},{4,6},{5,7},{6,4},{7,5},{8,10},{9,11},{10,... | collective-permute-start | bytes 184328 | tf_op jit(solution)/shard_map/ppermute | solution.py:258
  11.4 0.1 collective-permute-start.7
  11.5 0.1 select_reduce_fusion
  11.6 0.4 collective-permute-done.2
  12.0 1.5 %collective-permute-start.6 = (bf16[3,2,5120]{2,1,0:T(2,128)(2,1)S(1)}, bf16[3,2,5120]{2,1,0:T(2,128)(2,1)S(1)}, u32[]{:S(2)}, u32[]{:S(2)}) collective-permute-start(bf16[3,2,5120]{2,1,0:T(2,128)(2,1)S(1)} %collective-permute-done.2), channel_id=1, source_target_pairs={{0,2},{1,3},{2,0},{3,1},{4,6},{5,7},{6,4},{7,5},{8,10},{9,11},{10,... | collective-permute-start | bytes 184328 | tf_op jit(solution)/shard_map/ppermute | solution.py:258
  13.6 0.2 fusion.3
  13.8 0.4 collective-permute-done.4
  14.2 0.3 pack_blocks.1
  14.5 0.1 collective-permute-start.5
  14.6 0.1 and_convert_fusion.live_ref
  14.7 0.9 %collective-permute-done.7 = bf16[3,2,5120]{2,1,0:T(2,128)(2,1)S(1)} collective-permute-done((bf16[3,2,5120]{2,1,0:T(2,128)(2,1)S(1)}, bf16[3,2,5120]{2,1,0:T(2,128)(2,1)S(1)}, u32[]{:S(2)}, u32[]{:S(2)}) %collective-permute-start.7) | collective-permute-done | bytes 61472 | tf_op jit(solution)/shard_map/ppermute | solution.py:258
  15.6 0.5 %collective-permute-start.8 = (bf16[3,40,2,128]{3,2,1,0:T(2,128)(2,1)S(1)}, bf16[3,40,2,128]{3,2,1,0:T(2,128)(2,1)S(1)}, u32[]{:S(2)}, u32[]{:S(2)}) collective-permute-start(bf16[3,40,2,128]{3,2,1,0:T(2,128)(2,1)S(1)} %bitcast.49), channel_id=1, source_target_pairs={{0,1},{1,0},{2,3},{3,2},{4,5},{5,4},{6,7},{7,6},{8,9},{9,8},{10,11... | collective-permute-start | bytes 184328 | tf_op jit(solution)/shard_map/ppermute | solution.py:258
  16.1 0.2 collective-permute-done.6
  16.3 0.4 collective-permute-start.10
  16.6 0.2 select_reduce_fusion.2
  16.8 0.0 collective-permute-done.11.refs_11_
  16.8 0.2 collective-permute-done.8.refs_8_
  17.0 0.4 collective-permute-done.9.refs_9_
  17.4 0.2 collective-permute-done.10.refs_10_
  17.5 2.1 %low_rows.1 = (bf16[3,40,16,2,128]{4,3,2,1,0:T(2,128)(2,1)S(1)}, bf16[48,128]{1,0:T(8,128)(2,1)S(1)}) custom-call(s32[1]{0:T(128)} %bitcast.1.me_ref, s32[1,96]{1,0:T(1,128)S(1)} %get-tuple-element.44.slot_ref, bf16[4,64,5120]{2,1,0:T(8,128)(2,1)S(1)} %copy-done.1, bf16[4,3,40,2,128]{4,3,2,1,0:T(2,128)(2,1)S(1)} %collective-permute-done.5.pack_ref, ...), custom_call_target="tpu_custom_call" | custom-call | flops 100000000 | bytes 4000000 | tf_op jit(solution)/shard_map/low_rows/pallas_call | solution.py:421
  19.6 1.3 %collective-permute-start.14 = (bf16[48,128]{1,0:T(8,128)(2,1)S(1)}, bf16[48,128]{1,0:T(8,128)(2,1)S(1)}, u32[]{:S(2)}, u32[]{:S(2)}) collective-permute-start(bf16[48,128]{1,0:T(8,128)(2,1)S(1)} %get-tuple-element.53), channel_id=1, source_target_pairs={{0,3},{1,2},{2,1},{3,0},{4,7},{5,6},{6,5},{7,4},{8,11},{9,10},{10,... | collective-permute-start | bytes 36872 | tf_op jit(solution)/shard_map/ppermute | solution.py:258
  21.0 0.7 %collective-permute-start.13 = (bf16[48,128]{1,0:T(8,128)(2,1)S(1)}, bf16[48,128]{1,0:T(8,128)(2,1)S(1)}, u32[]{:S(2)}, u32[]{:S(2)}) collective-permute-start(bf16[48,128]{1,0:T(8,128)(2,1)S(1)} %get-tuple-element.53), channel_id=1, source_target_pairs={{0,2},{1,3},{2,0},{3,1},{4,6},{5,7},{6,4},{7,5},{8,10},{9,11},{10,... | collective-permute-start | bytes 36872 | tf_op jit(solution)/shard_map/ppermute | solution.py:258
  21.7 1.2 %project.4.key_ref = bf16[3,3,16,2,128]{4,3,2,1,0:T(2,128)(2,1)S(1)} custom-call(bf16[3,40,16,2,128]{4,3,2,1,0:T(2,128)(2,1)S(1)} %get-tuple-element.54.x_ref, bf16[3,320,5120]{2,1,0:T(8,128)(2,1)S(1)} %bitcast.37), custom_call_target="tpu_custom_call" | custom-call | flops 500000000 | bytes 4000000 | tf_op jit(solution)/shard_map/project/pallas_call | solution.py:464
  22.9 1.1 %project.3.query_ref = bf16[3,3,16,2,128]{4,3,2,1,0:T(2,128)(2,1)S(1)} custom-call(bf16[3,40,16,2,128]{4,3,2,1,0:T(2,128)(2,1)S(1)} %get-tuple-element.54.x_ref, bf16[3,320,5120]{2,1,0:T(8,128)(2,1)S(1)} %bitcast.38), custom_call_target="tpu_custom_call" | custom-call | flops 500000000 | bytes 4000000 | tf_op jit(solution)/shard_map/project/pallas_call | solution.py:464
  24.1 0.6 %collective-permute-done.13 = bf16[48,128]{1,0:T(8,128)(2,1)S(1)} collective-permute-done((bf16[48,128]{1,0:T(8,128)(2,1)S(1)}, bf16[48,128]{1,0:T(8,128)(2,1)S(1)}, u32[]{:S(2)}, u32[]{:S(2)}) %collective-permute-start.13) | collective-permute-done | bytes 12320 | tf_op jit(solution)/shard_map/ppermute | solution.py:258
  24.7 0.0 copy-start
  24.7 2.2 %collective-permute-start.17 = (bf16[48,128]{1,0:T(8,128)(2,1)S(1)}, bf16[48,128]{1,0:T(8,128)(2,1)S(1)}, u32[]{:S(2)}, u32[]{:S(2)}) collective-permute-start(bf16[48,128]{1,0:T(8,128)(2,1)S(1)} %add_add_fusion.refs_0_), channel_id=1, source_target_pairs={{0,12},{1,13},{2,14},{3,15},{4,8},{5,9},{6,10},{7,11},{8,4},{9,5},... | collective-permute-start | bytes 36872 | tf_op jit(solution)/shard_map/ppermute | solution.py:258
  26.9 0.4 collective-permute-start.16
  27.4 1.8 %collective-permute-start.15 = (bf16[48,128]{1,0:T(8,128)(2,1)S(1)}, bf16[48,128]{1,0:T(8,128)(2,1)S(1)}, u32[]{:S(2)}, u32[]{:S(2)}) collective-permute-start(bf16[48,128]{1,0:T(8,128)(2,1)S(1)} %add_add_fusion.refs_0_), channel_id=1, source_target_pairs={{0,4},{1,5},{2,6},{3,7},{4,0},{5,1},{6,2},{7,3},{8,12},{9,13},{10,... | collective-permute-start | bytes 36872 | tf_op jit(solution)/shard_map/ppermute | solution.py:258
  29.1 1.1 %project.5.base_ref = f32[96,320]{1,0:T(8,128)S(1)} custom-call(bf16[3,40,16,2,128]{4,3,2,1,0:T(2,128)(2,1)S(1)} %get-tuple-element.54.x_ref, bf16[3,320,5120]{2,1,0:T(8,128)(2,1)S(1)} %bitcast.39), custom_call_target="tpu_custom_call" | custom-call | flops 500000000 | bytes 4000000 | tf_op jit(solution)/shard_map/project/pallas_call | solution.py:464
  30.3 0.1 collective-permute-done.17.refs_3_
  30.3 1.2 %collective-permute-done.16.refs_2_ = bf16[48,128]{1,0:T(8,128)(2,1)S(1)} collective-permute-done((bf16[48,128]{1,0:T(8,128)(2,1)S(1)}, bf16[48,128]{1,0:T(8,128)(2,1)S(1)}, u32[]{:S(2)}, u32[]{:S(2)}) %collective-permute-start.16) | collective-permute-done | bytes 12320 | tf_op jit(solution)/shard_map/ppermute | solution.py:258
  31.5 1.7 %update_values.1 = bf16[16,8,3,2,128]{4,3,2,1,0:T(2,128)(2,1)} custom-call(s32[96,1]{1,0:T(8,128)S(1)} %get-tuple-element.42.stored_ref, bf16[3,3,16,2,128]{4,3,2,1,0:T(2,128)(2,1)S(1)} %project.3.query_ref, bf16[3,3,16,2,128]{4,3,2,1,0:T(2,128)(2,1)S(1)} %project.4.key_ref, f32[96,320]{1,0:T(8,128)S(1)} %project.5.base_ref, bf16[4096,320]{1,0:T(8,128)(2,1)S(1)} %bitcast.40, ...), custom_call_target="tpu_custom_call" | custom-call | flops 300000000 | bytes 4000000 | tf_op jit(solution)/shard_map/update_values/pallas_call | solution.py:504
  33.2 3.7 %all-to-all-start = ((bf16[16,8,3,2,128]{4,3,2,1,0:T(2,128)(2,1)}), bf16[16,8,3,2,128]{4,3,2,1,0:T(2,128)(2,1)S(1)}, u32[]{:S(2)}, u32[]{:S(2)}) async-start(bf16[16,8,3,2,128]{4,3,2,1,0:T(2,128)(2,1)} %update_values.1), calls=%async_computation | async-start | bytes 393216 | tf_op jit(solution)/shard_map/all_to_all | solution.py:701
  37.0 0.1 fusion
  37.1 6.4 %cache_by_head.1 = (bf16[40,256,128]{2,1,0:T(8,128)(2,1)S(1)}, bf16[40,256,128]{2,1,0:T(8,128)(2,1)}) custom-call(bf16[256,40,2,128]{3,2,1,0:T(2,128)(2,1)} %bitcast.58), custom_call_target="tpu_custom_call" | custom-call | bytes 12000000 | tf_op jit(solution)/shard_map/cache_by_head/pallas_call | solution.py:321
  43.5 2.4 %all-to-all-done.pieces_ref = bf16[16,8,3,2,128]{4,3,2,1,0:T(2,128)(2,1)S(1)} async-done(((bf16[16,8,3,2,128]{4,3,2,1,0:T(2,128)(2,1)}), bf16[16,8,3,2,128]{4,3,2,1,0:T(2,128)(2,1)S(1)}, u32[]{:S(2)}, u32[]{:S(2)}) %all-to-all-start) | async-done | bytes 196640 | tf_op jit(solution)/shard_map/all_to_all | solution.py:701
  45.8 3.8 %attention.1 = bf16[3,40,2,128]{3,2,1,0:T(2,128)(2,1)} custom-call(f32[8,128]{1,0:T(8,128)S(1)} %get-tuple-element.70.cos_ref, f32[8,128]{1,0:T(8,128)S(1)} %get-tuple-element.69.sin_ref, s32[2,256]{1,0:T(2,128)S(1)} %and_convert_fusion.live_ref, bf16[16,8,3,2,128]{4,3,2,1,0:T(2,128)(2,1)S(1)} %all-to-all-done.pieces_ref, ...), custom_call_target="tpu_custom_call" | custom-call | flops 1000000000 | bytes 6000000 | tf_op jit(solution)/shard_map/attention/pallas_call | solution.py:626
  (29 shorter events, 0.1 us)
Async XLA Ops:
  0.0 8.5 %collective-permute-start.1 = (bf16[3,2,5120]{2,1,0:T(2,128)(2,1)}, bf16[3,2,5120]{2,1,0:T(2,128)(2,1)S(1)}, u32[]{:S(2)}, u32[]{:S(2)}) collective-permute-start(bf16[3,2,5120]{2,1,0:T(2,128)(2,1)} %param.9), channel_id=1, source_target_pairs={{0,12},{1,13},{2,14},{3,15},{4,8},{5,9},{6,10},{7,11},{8,4},{9,5},... | collective-permute-start | bytes 184328 | tf_op jit(solution)/shard_map/ppermute | solution.py:258
  5.0 4.4 %collective-permute-start = (bf16[3,2,5120]{2,1,0:T(2,128)(2,1)}, bf16[3,2,5120]{2,1,0:T(2,128)(2,1)S(1)}, u32[]{:S(2)}, u32[]{:S(2)}) collective-permute-start(bf16[3,2,5120]{2,1,0:T(2,128)(2,1)} %param.9), channel_id=1, source_target_pairs={{0,4},{1,5},{2,6},{3,7},{4,0},{5,1},{6,2},{7,3},{8,12},{9,13},{10,... | collective-permute-start | bytes 184328 | tf_op jit(solution)/shard_map/ppermute | solution.py:258
  5.1 8.7 %collective-permute-start.3 = (bf16[3,2,5120]{2,1,0:T(2,128)(2,1)}, bf16[3,2,5120]{2,1,0:T(2,128)(2,1)S(1)}, u32[]{:S(2)}, u32[]{:S(2)}) collective-permute-start(bf16[3,2,5120]{2,1,0:T(2,128)(2,1)} %param.9), channel_id=1, source_target_pairs={{0,2},{1,3},{2,0},{3,1},{4,6},{5,7},{6,4},{7,5},{8,10},{9,11},{10,... | collective-permute-start | bytes 184328 | tf_op jit(solution)/shard_map/ppermute | solution.py:258
  6.6 5.5 %collective-permute-start.2 = (bf16[3,2,5120]{2,1,0:T(2,128)(2,1)}, bf16[3,2,5120]{2,1,0:T(2,128)(2,1)S(1)}, u32[]{:S(2)}, u32[]{:S(2)}) collective-permute-start(bf16[3,2,5120]{2,1,0:T(2,128)(2,1)} %param.9), channel_id=1, source_target_pairs={{0,8},{1,9},{2,10},{3,11},{4,12},{5,13},{6,14},{7,15},{8,0},{9,1},... | collective-permute-start | bytes 184328 | tf_op jit(solution)/shard_map/ppermute | solution.py:258
  8.2 13.4 %slice-start = ((s8[9830400]{0:T(1024)(128)(4,1)}), s8[4194304]{0:T(1024)(128)(4,1)S(1)}, s32[]{:S(2)}) async-start(s8[9830400]{0:T(1024)(128)(4,1)} %bitcast.35), calls=%async_computation.1 | async-start | bytes 8388608
  8.3 3.3 %copy-start.3 = (s32[2,32]{1,0:T(2,128)S(1)}, s32[2,32]{1,0:T(2,128)}, u32[]{:S(2)}) copy-start(s32[2,32]{1,0:T(2,128)} %param.16) | copy-start | bytes 772
  8.3 5.3 %copy-start.4 = (s32[32]{0:T(128)S(1)}, s32[32]{0:T(128)}, u32[]{:S(2)}) copy-start(s32[32]{0:T(128)} %param.15) | copy-start | bytes 388
  8.3 5.9 %copy-start.2 = (bf16[3,2,5120]{2,1,0:T(2,128)(2,1)S(1)}, bf16[3,2,5120]{2,1,0:T(2,128)(2,1)}, u32[]{:S(2)}) copy-start(bf16[3,2,5120]{2,1,0:T(2,128)(2,1)} %param.9) | copy-start | bytes 184324
  8.3 9.2 %copy-start.1 = (bf16[4,64,5120]{2,1,0:T(8,128)(2,1)S(1)}, bf16[4,64,5120]{2,1,0:T(8,128)(2,1)}, u32[]{:S(2)}) copy-start(bf16[4,64,5120]{2,1,0:T(8,128)(2,1)} %down_ref.1) | copy-start | bytes 7864324
  8.3 13.4 %slice-start.1 = ((s8[9830400]{0:T(1024)(128)(4,1)}), s8[4194304]{0:T(1024)(128)(4,1)S(1)}, s32[]{:S(2)}) async-start(s8[9830400]{0:T(1024)(128)(4,1)} %bitcast.35), calls=%async_computation.2 | async-start | bytes 8388608
  8.3 13.4 %slice-start.2 = ((s8[9830400]{0:T(1024)(128)(4,1)}), s8[1441792]{0:T(1024)(128)(4,1)S(1)}, s32[]{:S(2)}) async-start(s8[9830400]{0:T(1024)(128)(4,1)} %bitcast.35), calls=%async_computation.3 | async-start | bytes 2883584
  9.5 4.7 %collective-permute-start.4 = (bf16[3,2,5120]{2,1,0:T(2,128)(2,1)S(1)}, bf16[3,2,5120]{2,1,0:T(2,128)(2,1)S(1)}, u32[]{:S(2)}, u32[]{:S(2)}) collective-permute-start(bf16[3,2,5120]{2,1,0:T(2,128)(2,1)S(1)} %collective-permute-done), channel_id=1, source_target_pairs={{0,2},{1,3},{2,0},{3,1},{4,6},{5,7},{6,4},{7,5},{8,10},{9,11},{10,... | collective-permute-start | bytes 184328 | tf_op jit(solution)/shard_map/ppermute | solution.py:258
  11.4 4.2 %collective-permute-start.7 = (bf16[3,2,5120]{2,1,0:T(2,128)(2,1)S(1)}, bf16[3,2,5120]{2,1,0:T(2,128)(2,1)S(1)}, u32[]{:S(2)}, u32[]{:S(2)}) collective-permute-start(bf16[3,2,5120]{2,1,0:T(2,128)(2,1)S(1)} %collective-permute-done.1), channel_id=1, source_target_pairs={{0,2},{1,3},{2,0},{3,1},{4,6},{5,7},{6,4},{7,5},{8,10},{9,11},{10,... | collective-permute-start | bytes 184328 | tf_op jit(solution)/shard_map/ppermute | solution.py:258
  12.0 4.2 %collective-permute-start.6 = (bf16[3,2,5120]{2,1,0:T(2,128)(2,1)S(1)}, bf16[3,2,5120]{2,1,0:T(2,128)(2,1)S(1)}, u32[]{:S(2)}, u32[]{:S(2)}) collective-permute-start(bf16[3,2,5120]{2,1,0:T(2,128)(2,1)S(1)} %collective-permute-done.2), channel_id=1, source_target_pairs={{0,2},{1,3},{2,0},{3,1},{4,6},{5,7},{6,4},{7,5},{8,10},{9,11},{10,... | collective-permute-start | bytes 184328 | tf_op jit(solution)/shard_map/ppermute | solution.py:258
  14.5 3.0 %collective-permute-start.5 = (bf16[4,3,40,2,128]{4,3,2,1,0:T(2,128)(2,1)S(1)}, bf16[4,3,40,2,128]{4,3,2,1,0:T(2,128)(2,1)S(1)}, u32[]{:S(2)}, u32[]{:S(2)}) collective-permute-start(bf16[4,3,40,2,128]{4,3,2,1,0:T(2,128)(2,1)S(1)} %pack_blocks.1), channel_id=1, source_target_pairs={{0,1},{1,0},{2,3},{3,2},{4,5},{5,4},{6,7},{7,6},{8,9},{9,8},{10,11... | collective-permute-start | bytes 737288 | tf_op jit(solution)/shard_map/ppermute | solution.py:258
  15.6 1.2 %collective-permute-start.11 = (bf16[3,40,2,128]{3,2,1,0:T(2,128)(2,1)S(1)}, bf16[3,40,2,128]{3,2,1,0:T(2,128)(2,1)S(1)}, u32[]{:S(2)}, u32[]{:S(2)}) collective-permute-start(bf16[3,40,2,128]{3,2,1,0:T(2,128)(2,1)S(1)} %bitcast.53), channel_id=1, source_target_pairs={{0,1},{1,0},{2,3},{3,2},{4,5},{5,4},{6,7},{7,6},{8,9},{9,8},{10,11... | collective-permute-start | bytes 184328 | tf_op jit(solution)/shard_map/ppermute | solution.py:258
  15.6 1.4 %collective-permute-start.8 = (bf16[3,40,2,128]{3,2,1,0:T(2,128)(2,1)S(1)}, bf16[3,40,2,128]{3,2,1,0:T(2,128)(2,1)S(1)}, u32[]{:S(2)}, u32[]{:S(2)}) collective-permute-start(bf16[3,40,2,128]{3,2,1,0:T(2,128)(2,1)S(1)} %bitcast.49), channel_id=1, source_target_pairs={{0,1},{1,0},{2,3},{3,2},{4,5},{5,4},{6,7},{7,6},{8,9},{9,8},{10,11... | collective-permute-start | bytes 184328 | tf_op jit(solution)/shard_map/ppermute | solution.py:258
  16.1 1.2 %collective-permute-start.9 = (bf16[3,40,2,128]{3,2,1,0:T(2,128)(2,1)S(1)}, bf16[3,40,2,128]{3,2,1,0:T(2,128)(2,1)S(1)}, u32[]{:S(2)}, u32[]{:S(2)}) collective-permute-start(bf16[3,40,2,128]{3,2,1,0:T(2,128)(2,1)S(1)} %bitcast.51), channel_id=1, source_target_pairs={{0,1},{1,0},{2,3},{3,2},{4,5},{5,4},{6,7},{7,6},{8,9},{9,8},{10,11... | collective-permute-start | bytes 184328 | tf_op jit(solution)/shard_map/ppermute | solution.py:258
  16.3 1.2 %collective-permute-start.10 = (bf16[3,40,2,128]{3,2,1,0:T(2,128)(2,1)S(1)}, bf16[3,40,2,128]{3,2,1,0:T(2,128)(2,1)S(1)}, u32[]{:S(2)}, u32[]{:S(2)}) collective-permute-start(bf16[3,40,2,128]{3,2,1,0:T(2,128)(2,1)S(1)} %bitcast.55), channel_id=1, source_target_pairs={{0,1},{1,0},{2,3},{3,2},{4,5},{5,4},{6,7},{7,6},{8,9},{9,8},{10,11... | collective-permute-start | bytes 184328 | tf_op jit(solution)/shard_map/ppermute | solution.py:258
  19.6 4.4 %collective-permute-start.14 = (bf16[48,128]{1,0:T(8,128)(2,1)S(1)}, bf16[48,128]{1,0:T(8,128)(2,1)S(1)}, u32[]{:S(2)}, u32[]{:S(2)}) collective-permute-start(bf16[48,128]{1,0:T(8,128)(2,1)S(1)} %get-tuple-element.53), channel_id=1, source_target_pairs={{0,3},{1,2},{2,1},{3,0},{4,7},{5,6},{6,5},{7,4},{8,11},{9,10},{10,... | collective-permute-start | bytes 36872 | tf_op jit(solution)/shard_map/ppermute | solution.py:258
  21.0 3.7 %collective-permute-start.13 = (bf16[48,128]{1,0:T(8,128)(2,1)S(1)}, bf16[48,128]{1,0:T(8,128)(2,1)S(1)}, u32[]{:S(2)}, u32[]{:S(2)}) collective-permute-start(bf16[48,128]{1,0:T(8,128)(2,1)S(1)} %get-tuple-element.53), channel_id=1, source_target_pairs={{0,2},{1,3},{2,0},{3,1},{4,6},{5,7},{6,4},{7,5},{8,10},{9,11},{10,... | collective-permute-start | bytes 36872 | tf_op jit(solution)/shard_map/ppermute | solution.py:258
  21.7 3.0 %collective-permute-start.12 = (bf16[48,128]{1,0:T(8,128)(2,1)S(1)}, bf16[48,128]{1,0:T(8,128)(2,1)S(1)}, u32[]{:S(2)}, u32[]{:S(2)}) collective-permute-start(bf16[48,128]{1,0:T(8,128)(2,1)S(1)} %get-tuple-element.53), channel_id=1, source_target_pairs={{0,1},{1,0},{2,3},{3,2},{4,5},{5,4},{6,7},{7,6},{8,9},{9,8},{10,11... | collective-permute-start | bytes 36872 | tf_op jit(solution)/shard_map/ppermute | solution.py:258
  24.7 6.9 %copy-start = (bf16[64,64,320]{2,1,0:T(8,128)(2,1)S(1)}, bf16[64,64,320]{2,1,0:T(8,128)(2,1)}, u32[]{:S(2)}) copy-start(bf16[64,64,320]{2,1,0:T(8,128)(2,1)} %param.12) | copy-start | bytes 7864324
  24.7 5.6 %collective-permute-start.17 = (bf16[48,128]{1,0:T(8,128)(2,1)S(1)}, bf16[48,128]{1,0:T(8,128)(2,1)S(1)}, u32[]{:S(2)}, u32[]{:S(2)}) collective-permute-start(bf16[48,128]{1,0:T(8,128)(2,1)S(1)} %add_add_fusion.refs_0_), channel_id=1, source_target_pairs={{0,12},{1,13},{2,14},{3,15},{4,8},{5,9},{6,10},{7,11},{8,4},{9,5},... | collective-permute-start | bytes 36872 | tf_op jit(solution)/shard_map/ppermute | solution.py:258
  26.9 4.6 %collective-permute-start.16 = (bf16[48,128]{1,0:T(8,128)(2,1)S(1)}, bf16[48,128]{1,0:T(8,128)(2,1)S(1)}, u32[]{:S(2)}, u32[]{:S(2)}) collective-permute-start(bf16[48,128]{1,0:T(8,128)(2,1)S(1)} %add_add_fusion.refs_0_), channel_id=1, source_target_pairs={{0,8},{1,9},{2,10},{3,11},{4,12},{5,13},{6,14},{7,15},{8,0},{9,1},... | collective-permute-start | bytes 36872 | tf_op jit(solution)/shard_map/ppermute | solution.py:258
  27.4 4.2 %collective-permute-start.15 = (bf16[48,128]{1,0:T(8,128)(2,1)S(1)}, bf16[48,128]{1,0:T(8,128)(2,1)S(1)}, u32[]{:S(2)}, u32[]{:S(2)}) collective-permute-start(bf16[48,128]{1,0:T(8,128)(2,1)S(1)} %add_add_fusion.refs_0_), channel_id=1, source_target_pairs={{0,4},{1,5},{2,6},{3,7},{4,0},{5,1},{6,2},{7,3},{8,12},{9,13},{10,... | collective-permute-start | bytes 36872 | tf_op jit(solution)/shard_map/ppermute | solution.py:258
  33.2 12.6 %all-to-all-start = ((bf16[16,8,3,2,128]{4,3,2,1,0:T(2,128)(2,1)}), bf16[16,8,3,2,128]{4,3,2,1,0:T(2,128)(2,1)S(1)}, u32[]{:S(2)}, u32[]{:S(2)}) async-start(bf16[16,8,3,2,128]{4,3,2,1,0:T(2,128)(2,1)} %update_values.1), calls=%async_computation | async-start | bytes 393216 | tf_op jit(solution)/shard_map/all_to_all | solution.py:701

commit v22 on v21

--- a/solution.py
+++ b/solution.py
@@ -522,10 +522,11 @@
     count, _, steps = pieces_ref.shape[:3]
     rows = 2 * steps
     each = (pieces_ref.shape[1] + 1) // 3
-    heads = 2 * out_ref.shape[1] // count
+    heads = 4 * out_ref.shape[1] // count
+    block = -(-heads // 8) * 8
     lanes = heads * HD
-    group = rows * HEAD_BLOCK
-    chips = range(count // 2)
+    group = rows * block
+    chips = range(count // 4)
     early = keys_refs[0].shape[0] // heads
     places = [(0, c) if c < early else (1, c - early) for c in chips]
     fetches = start_all(
@@ -563,15 +564,15 @@
     def rotated(parts):
         return [x * cosine + pltpu.roll(x, HD // 2, 1) * sine for x in parts]
 
-    row_head = lax.broadcasted_iota(jnp.int32, (group, lanes), 0) % HEAD_BLOCK
+    row_head = lax.broadcasted_iota(jnp.int32, (group, lanes), 0) % block
     lane_head = lax.broadcasted_iota(jnp.int32, (group, lanes), 1) // HD
     own_head = row_head == lane_head
-    row_j = lax.broadcasted_iota(jnp.int32, (group, 16), 0) // HEAD_BLOCK
+    row_j = lax.broadcasted_iota(jnp.int32, (group, 16), 0) // block
     new_j = lax.broadcasted_iota(jnp.int32, (group, 16), 1)
     new_live = (new_j < rows) & (new_j % 2 == row_j % 2) & (new_j // 2 <= row_j // 2)
     live = jnp.concatenate(
         [
-            jnp.broadcast_to(live_ref[j % 2 : j % 2 + 1, :], (HEAD_BLOCK, live_ref.shape[1]))
+            jnp.broadcast_to(live_ref[j % 2 : j % 2 + 1, :], (block, live_ref.shape[1]))
             for j in range(rows)
         ],
         axis=0,
@@ -581,11 +582,12 @@
     vn_ref[...] = jnp.zeros_like(vn_ref)
     spreads = []
     for c in chips:
-        query = jnp.concatenate(rotated(chip_columns(c, 0)), axis=1)
-        kn_ref[c, 0:rows] = jnp.concatenate(rotated(chip_keys(c)), axis=1)
-        vn_ref[c, 0:rows] = jnp.concatenate(chip_columns(c, 2 * each - 1), axis=1)
+        query = jnp.concatenate(rotated(chip_columns(2 * c, 0) + chip_columns(2 * c + 1, 0)), axis=1)
+        kn_ref[c, 0:rows] = jnp.concatenate(rotated(chip_keys(2 * c) + chip_keys(2 * c + 1)), axis=1)
+        fresh_columns = chip_columns(2 * c, 2 * each - 1) + chip_columns(2 * c + 1, 2 * each - 1)
+        vn_ref[c, 0:rows] = jnp.concatenate(fresh_columns, axis=1)
         spread = jnp.concatenate(
-            [jnp.broadcast_to(query[j : j + 1], (HEAD_BLOCK, lanes)) for j in range(rows)], axis=0
+            [jnp.broadcast_to(query[j : j + 1], (block, lanes)) for j in range(rows)], axis=0
         )
         spreads.append(jnp.where(own_head, spread, 0.0).astype(jnp.bfloat16))
     scores, fresh = [], []
@@ -611,8 +613,9 @@
         vn = vn_ref[c].astype(jnp.bfloat16)
         mixed = jnp.dot(weights[c], values, preferred_element_type=jnp.float32)
         mixed = mixed + jnp.dot(fresh_weights[c], vn, preferred_element_type=jnp.float32)
-        mixed = jnp.where(own_head, mixed / totals[c], 0.0)
-        out = jnp.sum(mixed.reshape(rows, HEAD_BLOCK, lanes), axis=1).astype(out_ref.dtype)
+        mixed = jnp.sum(jnp.where(own_head, mixed, 0.0).reshape(rows, block, lanes), axis=1)
+        total = jnp.sum(jnp.where(own_head, totals[c], 0.0).reshape(rows, block, lanes), axis=1)
+        out = (mixed / total).astype(out_ref.dtype)
         for t in range(steps):
             for h in range(heads):
                 out_ref[t, c * heads + h] = out[2 * t : 2 * t + 2, h * HD : (h + 1) * HD]
@@ -621,7 +624,7 @@
 def attend(cosine, sine, live, pieces, keys, values):
     count, _, steps = pieces.shape[:3]
     heads, tokens = sum(x.shape[0] for x in keys), keys[0].shape[1]
-    chips = count // 2
+    chips = count // 4
     per = heads // chips
     return pl.pallas_call(
         attend_kernel,

time: 50.1 us -> 50.2 us (level)
  no operation moved by 1% of the time
where the time goes in v22:
time: 50.2 us; the launch traced here: 50 us
  starting transfers between devices  22.1 us (44%)
  Pallas kernels  18 us (36%)
  waiting for transfers between devices  7.87 us (16%)
  other arithmetic  1.53 us (3%)
    ppermute x18, starting transfers between devices, trade(): return lax.ppermute(value, 'replica', [(i, i ^ mask) for i in range(count)])  18.3 us
    pallas_call x1, Pallas kernels, cache_by_head(): pl.pallas_call(functools.partial(cache_kernel, first), out_shape=(jax.Sha...  6.4 us
    ppermute x18, waiting for transfers between devices, trade(): return lax.ppermute(value, 'replica', [(i, i ^ mask) for i in range(count)])  5.51 us
    pallas_call x1, Pallas kernels, attend(): pl.pallas_call(attend_kernel, out_shape=jax.ShapeDtypeStruct((steps, head...  3.96 us
    all_to_all x1, starting transfers between devices, chip_plan(): lax.all_to_all(send, 'replica', split_axis=0, concat_axis=0, tiled=True)  3.74 us
    pallas_call x3, Pallas kernels, project(): pl.pallas_call(functools.partial(project_kernel, which), out_shape=chunks...  3.45 us
    all_to_all x1, waiting for transfers between devices, chip_plan(): lax.all_to_all(send, 'replica', split_axis=0, concat_axis=0, tiled=True)  2.36 us
    pallas_call x1, Pallas kernels, low_of(): pl.pallas_call(functools.partial(low_kernel, tuple(blocks), packs), out_s...  2.09 us
  transfers between devices with their start and end apart: 19, of which 12 were waited for; matrix products, arithmetic and copies ran while one was open for 3% of the time, Pallas kernels for 21%

profile of v22, /device:TPU:0, one launch (start us, length us, event | category | flops | bytes accessed | tf_op | source)
XLA Modules:
  0.0 50.0 jit_solution(4213535824246964280)
XLA Ops:
  0.0 5.0 %collective-permute-start.1 = (bf16[3,2,5120]{2,1,0:T(2,128)(2,1)}, bf16[3,2,5120]{2,1,0:T(2,128)(2,1)S(1)}, u32[]{:S(2)}, u32[]{:S(2)}) collective-permute-start(bf16[3,2,5120]{2,1,0:T(2,128)(2,1)} %param.9), channel_id=1, source_target_pairs={{0,12},{1,13},{2,14},{3,15},{4,8},{5,9},{6,10},{7,11},{8,4},{9,5},... | collective-permute-start | bytes 184328 | tf_op jit(solution)/shard_map/ppermute | solution.py:258
  5.1 1.5 %collective-permute-start.3 = (bf16[3,2,5120]{2,1,0:T(2,128)(2,1)}, bf16[3,2,5120]{2,1,0:T(2,128)(2,1)S(1)}, u32[]{:S(2)}, u32[]{:S(2)}) collective-permute-start(bf16[3,2,5120]{2,1,0:T(2,128)(2,1)} %param.9), channel_id=1, source_target_pairs={{0,2},{1,3},{2,0},{3,1},{4,6},{5,7},{6,4},{7,5},{8,10},{9,11},{10,... | collective-permute-start | bytes 184328 | tf_op jit(solution)/shard_map/ppermute | solution.py:258
  6.6 0.8 %collective-permute-start.2 = (bf16[3,2,5120]{2,1,0:T(2,128)(2,1)}, bf16[3,2,5120]{2,1,0:T(2,128)(2,1)S(1)}, u32[]{:S(2)}, u32[]{:S(2)}) collective-permute-start(bf16[3,2,5120]{2,1,0:T(2,128)(2,1)} %param.9), channel_id=1, source_target_pairs={{0,8},{1,9},{2,10},{3,11},{4,12},{5,13},{6,14},{7,15},{8,0},{9,1},... | collective-permute-start | bytes 184328 | tf_op jit(solution)/shard_map/ppermute | solution.py:258
  7.4 0.9 %select_reduce_fusion.1 = s32[32]{0:T(128)S(1)} fusion(s32[64]{0:T(128)} %param.13, s32[32]{0:T(128)} %param.14), kind=kLoop, calls=%fused_computation.1 | loop fusion | flops 6112 | bytes 512 | tf_op jit(solution)/shard_map/reduce_sum | solution.py:665
  8.2 0.0 slice-start
  8.3 0.0 copy-start.3
  8.3 0.0 copy-start.4
  8.3 0.0 copy-start.2
  8.3 0.2 index_work.1
  8.5 1.0 %collective-permute-done = bf16[3,2,5120]{2,1,0:T(2,128)(2,1)S(1)} collective-permute-done((bf16[3,2,5120]{2,1,0:T(2,128)(2,1)}, bf16[3,2,5120]{2,1,0:T(2,128)(2,1)S(1)}, u32[]{:S(2)}, u32[]{:S(2)}) %collective-permute-start) | collective-permute-done | bytes 61472 | tf_op jit(solution)/shard_map/ppermute | solution.py:258
  9.5 1.9 %collective-permute-start.4 = (bf16[3,2,5120]{2,1,0:T(2,128)(2,1)S(1)}, bf16[3,2,5120]{2,1,0:T(2,128)(2,1)S(1)}, u32[]{:S(2)}, u32[]{:S(2)}) collective-permute-start(bf16[3,2,5120]{2,1,0:T(2,128)(2,1)S(1)} %collective-permute-done), channel_id=1, source_target_pairs={{0,2},{1,3},{2,0},{3,1},{4,6},{5,7},{6,4},{7,5},{8,10},{9,11},{10,... | collective-permute-start | bytes 184328 | tf_op jit(solution)/shard_map/ppermute | solution.py:258
  11.4 0.1 collective-permute-start.7
  11.5 0.1 select_reduce_fusion
  11.6 0.4 collective-permute-done.2
  12.0 1.5 %collective-permute-start.6 = (bf16[3,2,5120]{2,1,0:T(2,128)(2,1)S(1)}, bf16[3,2,5120]{2,1,0:T(2,128)(2,1)S(1)}, u32[]{:S(2)}, u32[]{:S(2)}) collective-permute-start(bf16[3,2,5120]{2,1,0:T(2,128)(2,1)S(1)} %collective-permute-done.2), channel_id=1, source_target_pairs={{0,2},{1,3},{2,0},{3,1},{4,6},{5,7},{6,4},{7,5},{8,10},{9,11},{10,... | collective-permute-start | bytes 184328 | tf_op jit(solution)/shard_map/ppermute | solution.py:258
  13.6 0.2 fusion.3
  13.8 0.4 collective-permute-done.4
  14.2 0.3 pack_blocks.1
  14.5 0.1 collective-permute-start.5
  14.6 0.1 and_convert_fusion.live_ref
  14.7 0.9 %collective-permute-done.7 = bf16[3,2,5120]{2,1,0:T(2,128)(2,1)S(1)} collective-permute-done((bf16[3,2,5120]{2,1,0:T(2,128)(2,1)S(1)}, bf16[3,2,5120]{2,1,0:T(2,128)(2,1)S(1)}, u32[]{:S(2)}, u32[]{:S(2)}) %collective-permute-start.7) | collective-permute-done | bytes 61472 | tf_op jit(solution)/shard_map/ppermute | solution.py:258
  15.6 0.5 %collective-permute-start.8 = (bf16[3,40,2,128]{3,2,1,0:T(2,128)(2,1)S(1)}, bf16[3,40,2,128]{3,2,1,0:T(2,128)(2,1)S(1)}, u32[]{:S(2)}, u32[]{:S(2)}) collective-permute-start(bf16[3,40,2,128]{3,2,1,0:T(2,128)(2,1)S(1)} %bitcast.49), channel_id=1, source_target_pairs={{0,1},{1,0},{2,3},{3,2},{4,5},{5,4},{6,7},{7,6},{8,9},{9,8},{10,11... | collective-permute-start | bytes 184328 | tf_op jit(solution)/shard_map/ppermute | solution.py:258
  16.1 0.2 collective-permute-done.6
  16.3 0.4 collective-permute-start.10
  16.6 0.2 select_reduce_fusion.2
  16.8 0.0 collective-permute-done.11.refs_11_
  16.8 0.2 collective-permute-done.8.refs_8_
  17.0 0.4 collective-permute-done.9.refs_9_
  17.4 0.2 collective-permute-done.10.refs_10_
  17.5 2.1 %low_rows.1 = (bf16[3,40,16,2,128]{4,3,2,1,0:T(2,128)(2,1)S(1)}, bf16[48,128]{1,0:T(8,128)(2,1)S(1)}) custom-call(s32[1]{0:T(128)} %bitcast.1.me_ref, s32[1,96]{1,0:T(1,128)S(1)} %get-tuple-element.44.slot_ref, bf16[4,64,5120]{2,1,0:T(8,128)(2,1)S(1)} %copy-done.1, bf16[4,3,40,2,128]{4,3,2,1,0:T(2,128)(2,1)S(1)} %collective-permute-done.5.pack_ref, ...), custom_call_target="tpu_custom_call" | custom-call | flops 100000000 | bytes 4000000 | tf_op jit(solution)/shard_map/low_rows/pallas_call | solution.py:421
  19.6 1.3 %collective-permute-start.14 = (bf16[48,128]{1,0:T(8,128)(2,1)S(1)}, bf16[48,128]{1,0:T(8,128)(2,1)S(1)}, u32[]{:S(2)}, u32[]{:S(2)}) collective-permute-start(bf16[48,128]{1,0:T(8,128)(2,1)S(1)} %get-tuple-element.53), channel_id=1, source_target_pairs={{0,3},{1,2},{2,1},{3,0},{4,7},{5,6},{6,5},{7,4},{8,11},{9,10},{10,... | collective-permute-start | bytes 36872 | tf_op jit(solution)/shard_map/ppermute | solution.py:258
  21.0 0.7 %collective-permute-start.13 = (bf16[48,128]{1,0:T(8,128)(2,1)S(1)}, bf16[48,128]{1,0:T(8,128)(2,1)S(1)}, u32[]{:S(2)}, u32[]{:S(2)}) collective-permute-start(bf16[48,128]{1,0:T(8,128)(2,1)S(1)} %get-tuple-element.53), channel_id=1, source_target_pairs={{0,2},{1,3},{2,0},{3,1},{4,6},{5,7},{6,4},{7,5},{8,10},{9,11},{10,... | collective-permute-start | bytes 36872 | tf_op jit(solution)/shard_map/ppermute | solution.py:258
  21.7 1.2 %project.4.key_ref = bf16[3,3,16,2,128]{4,3,2,1,0:T(2,128)(2,1)S(1)} custom-call(bf16[3,40,16,2,128]{4,3,2,1,0:T(2,128)(2,1)S(1)} %get-tuple-element.54.x_ref, bf16[3,320,5120]{2,1,0:T(8,128)(2,1)S(1)} %bitcast.37), custom_call_target="tpu_custom_call" | custom-call | flops 500000000 | bytes 4000000 | tf_op jit(solution)/shard_map/project/pallas_call | solution.py:464
  22.9 1.1 %project.3.query_ref = bf16[3,3,16,2,128]{4,3,2,1,0:T(2,128)(2,1)S(1)} custom-call(bf16[3,40,16,2,128]{4,3,2,1,0:T(2,128)(2,1)S(1)} %get-tuple-element.54.x_ref, bf16[3,320,5120]{2,1,0:T(8,128)(2,1)S(1)} %bitcast.38), custom_call_target="tpu_custom_call" | custom-call | flops 500000000 | bytes 4000000 | tf_op jit(solution)/shard_map/project/pallas_call | solution.py:464
  24.1 0.6 %collective-permute-done.13 = bf16[48,128]{1,0:T(8,128)(2,1)S(1)} collective-permute-done((bf16[48,128]{1,0:T(8,128)(2,1)S(1)}, bf16[48,128]{1,0:T(8,128)(2,1)S(1)}, u32[]{:S(2)}, u32[]{:S(2)}) %collective-permute-start.13) | collective-permute-done | bytes 12320 | tf_op jit(solution)/shard_map/ppermute | solution.py:258
  24.7 0.0 copy-start
  24.7 2.2 %collective-permute-start.17 = (bf16[48,128]{1,0:T(8,128)(2,1)S(1)}, bf16[48,128]{1,0:T(8,128)(2,1)S(1)}, u32[]{:S(2)}, u32[]{:S(2)}) collective-permute-start(bf16[48,128]{1,0:T(8,128)(2,1)S(1)} %add_add_fusion.refs_0_), channel_id=1, source_target_pairs={{0,12},{1,13},{2,14},{3,15},{4,8},{5,9},{6,10},{7,11},{8,4},{9,5},... | collective-permute-start | bytes 36872 | tf_op jit(solution)/shard_map/ppermute | solution.py:258
  26.9 0.4 collective-permute-start.16
  27.4 1.8 %collective-permute-start.15 = (bf16[48,128]{1,0:T(8,128)(2,1)S(1)}, bf16[48,128]{1,0:T(8,128)(2,1)S(1)}, u32[]{:S(2)}, u32[]{:S(2)}) collective-permute-start(bf16[48,128]{1,0:T(8,128)(2,1)S(1)} %add_add_fusion.refs_0_), channel_id=1, source_target_pairs={{0,4},{1,5},{2,6},{3,7},{4,0},{5,1},{6,2},{7,3},{8,12},{9,13},{10,... | collective-permute-start | bytes 36872 | tf_op jit(solution)/shard_map/ppermute | solution.py:258
  29.1 1.1 %project.5.base_ref = f32[96,320]{1,0:T(8,128)S(1)} custom-call(bf16[3,40,16,2,128]{4,3,2,1,0:T(2,128)(2,1)S(1)} %get-tuple-element.54.x_ref, bf16[3,320,5120]{2,1,0:T(8,128)(2,1)S(1)} %bitcast.39), custom_call_target="tpu_custom_call" | custom-call | flops 500000000 | bytes 4000000 | tf_op jit(solution)/shard_map/project/pallas_call | solution.py:464
  30.3 0.1 collective-permute-done.17.refs_3_
  30.3 1.2 %collective-permute-done.16.refs_2_ = bf16[48,128]{1,0:T(8,128)(2,1)S(1)} collective-permute-done((bf16[48,128]{1,0:T(8,128)(2,1)S(1)}, bf16[48,128]{1,0:T(8,128)(2,1)S(1)}, u32[]{:S(2)}, u32[]{:S(2)}) %collective-permute-start.16) | collective-permute-done | bytes 12320 | tf_op jit(solution)/shard_map/ppermute | solution.py:258
  31.5 1.7 %update_values.1 = bf16[16,8,3,2,128]{4,3,2,1,0:T(2,128)(2,1)} custom-call(s32[96,1]{1,0:T(8,128)S(1)} %get-tuple-element.42.stored_ref, bf16[3,3,16,2,128]{4,3,2,1,0:T(2,128)(2,1)S(1)} %project.3.query_ref, bf16[3,3,16,2,128]{4,3,2,1,0:T(2,128)(2,1)S(1)} %project.4.key_ref, f32[96,320]{1,0:T(8,128)S(1)} %project.5.base_ref, bf16[4096,320]{1,0:T(8,128)(2,1)S(1)} %bitcast.40, ...), custom_call_target="tpu_custom_call" | custom-call | flops 300000000 | bytes 4000000 | tf_op jit(solution)/shard_map/update_values/pallas_call | solution.py:504
  33.2 3.7 %all-to-all-start = ((bf16[16,8,3,2,128]{4,3,2,1,0:T(2,128)(2,1)}), bf16[16,8,3,2,128]{4,3,2,1,0:T(2,128)(2,1)S(1)}, u32[]{:S(2)}, u32[]{:S(2)}) async-start(bf16[16,8,3,2,128]{4,3,2,1,0:T(2,128)(2,1)} %update_values.1), calls=%async_computation | async-start | bytes 393216 | tf_op jit(solution)/shard_map/all_to_all | solution.py:704
  37.0 0.1 fusion
  37.1 6.4 %cache_by_head.1 = (bf16[40,256,128]{2,1,0:T(8,128)(2,1)S(1)}, bf16[40,256,128]{2,1,0:T(8,128)(2,1)}) custom-call(bf16[256,40,2,128]{3,2,1,0:T(2,128)(2,1)} %bitcast.58), custom_call_target="tpu_custom_call" | custom-call | bytes 12000000 | tf_op jit(solution)/shard_map/cache_by_head/pallas_call | solution.py:321
  43.5 2.4 %all-to-all-done.pieces_ref = bf16[16,8,3,2,128]{4,3,2,1,0:T(2,128)(2,1)S(1)} async-done(((bf16[16,8,3,2,128]{4,3,2,1,0:T(2,128)(2,1)}), bf16[16,8,3,2,128]{4,3,2,1,0:T(2,128)(2,1)S(1)}, u32[]{:S(2)}, u32[]{:S(2)}) %all-to-all-start) | async-done | bytes 196640 | tf_op jit(solution)/shard_map/all_to_all | solution.py:704
  45.8 4.0 %attention.1 = bf16[3,40,2,128]{3,2,1,0:T(2,128)(2,1)} custom-call(f32[8,128]{1,0:T(8,128)S(1)} %get-tuple-element.70.cos_ref, f32[8,128]{1,0:T(8,128)S(1)} %get-tuple-element.69.sin_ref, s32[2,256]{1,0:T(2,128)S(1)} %and_convert_fusion.live_ref, bf16[16,8,3,2,128]{4,3,2,1,0:T(2,128)(2,1)S(1)} %all-to-all-done.pieces_ref, ...), custom_call_target="tpu_custom_call" | custom-call | flops 1000000000 | bytes 6000000 | tf_op jit(solution)/shard_map/attention/pallas_call | solution.py:629
  (29 shorter events, 0.1 us)
Async XLA Ops:
  0.0 8.5 %collective-permute-start.1 = (bf16[3,2,5120]{2,1,0:T(2,128)(2,1)}, bf16[3,2,5120]{2,1,0:T(2,128)(2,1)S(1)}, u32[]{:S(2)}, u32[]{:S(2)}) collective-permute-start(bf16[3,2,5120]{2,1,0:T(2,128)(2,1)} %param.9), channel_id=1, source_target_pairs={{0,12},{1,13},{2,14},{3,15},{4,8},{5,9},{6,10},{7,11},{8,4},{9,5},... | collective-permute-start | bytes 184328 | tf_op jit(solution)/shard_map/ppermute | solution.py:258
  5.0 4.4 %collective-permute-start = (bf16[3,2,5120]{2,1,0:T(2,128)(2,1)}, bf16[3,2,5120]{2,1,0:T(2,128)(2,1)S(1)}, u32[]{:S(2)}, u32[]{:S(2)}) collective-permute-start(bf16[3,2,5120]{2,1,0:T(2,128)(2,1)} %param.9), channel_id=1, source_target_pairs={{0,4},{1,5},{2,6},{3,7},{4,0},{5,1},{6,2},{7,3},{8,12},{9,13},{10,... | collective-permute-start | bytes 184328 | tf_op jit(solution)/shard_map/ppermute | solution.py:258
  5.1 8.7 %collective-permute-start.3 = (bf16[3,2,5120]{2,1,0:T(2,128)(2,1)}, bf16[3,2,5120]{2,1,0:T(2,128)(2,1)S(1)}, u32[]{:S(2)}, u32[]{:S(2)}) collective-permute-start(bf16[3,2,5120]{2,1,0:T(2,128)(2,1)} %param.9), channel_id=1, source_target_pairs={{0,2},{1,3},{2,0},{3,1},{4,6},{5,7},{6,4},{7,5},{8,10},{9,11},{10,... | collective-permute-start | bytes 184328 | tf_op jit(solution)/shard_map/ppermute | solution.py:258
  6.6 5.5 %collective-permute-start.2 = (bf16[3,2,5120]{2,1,0:T(2,128)(2,1)}, bf16[3,2,5120]{2,1,0:T(2,128)(2,1)S(1)}, u32[]{:S(2)}, u32[]{:S(2)}) collective-permute-start(bf16[3,2,5120]{2,1,0:T(2,128)(2,1)} %param.9), channel_id=1, source_target_pairs={{0,8},{1,9},{2,10},{3,11},{4,12},{5,13},{6,14},{7,15},{8,0},{9,1},... | collective-permute-start | bytes 184328 | tf_op jit(solution)/shard_map/ppermute | solution.py:258
  8.2 13.4 %slice-start = ((s8[9830400]{0:T(1024)(128)(4,1)}), s8[4194304]{0:T(1024)(128)(4,1)S(1)}, s32[]{:S(2)}) async-start(s8[9830400]{0:T(1024)(128)(4,1)} %bitcast.35), calls=%async_computation.1 | async-start | bytes 8388608
  8.3 3.3 %copy-start.3 = (s32[2,32]{1,0:T(2,128)S(1)}, s32[2,32]{1,0:T(2,128)}, u32[]{:S(2)}) copy-start(s32[2,32]{1,0:T(2,128)} %param.16) | copy-start | bytes 772
  8.3 5.3 %copy-start.4 = (s32[32]{0:T(128)S(1)}, s32[32]{0:T(128)}, u32[]{:S(2)}) copy-start(s32[32]{0:T(128)} %param.15) | copy-start | bytes 388
  8.3 5.9 %copy-start.2 = (bf16[3,2,5120]{2,1,0:T(2,128)(2,1)S(1)}, bf16[3,2,5120]{2,1,0:T(2,128)(2,1)}, u32[]{:S(2)}) copy-start(bf16[3,2,5120]{2,1,0:T(2,128)(2,1)} %param.9) | copy-start | bytes 184324
  8.3 9.2 %copy-start.1 = (bf16[4,64,5120]{2,1,0:T(8,128)(2,1)S(1)}, bf16[4,64,5120]{2,1,0:T(8,128)(2,1)}, u32[]{:S(2)}) copy-start(bf16[4,64,5120]{2,1,0:T(8,128)(2,1)} %down_ref.1) | copy-start | bytes 7864324
  8.3 13.4 %slice-start.1 = ((s8[9830400]{0:T(1024)(128)(4,1)}), s8[4194304]{0:T(1024)(128)(4,1)S(1)}, s32[]{:S(2)}) async-start(s8[9830400]{0:T(1024)(128)(4,1)} %bitcast.35), calls=%async_computation.2 | async-start | bytes 8388608
  8.3 13.4 %slice-start.2 = ((s8[9830400]{0:T(1024)(128)(4,1)}), s8[1441792]{0:T(1024)(128)(4,1)S(1)}, s32[]{:S(2)}) async-start(s8[9830400]{0:T(1024)(128)(4,1)} %bitcast.35), calls=%async_computation.3 | async-start | bytes 2883584
  9.5 4.7 %collective-permute-start.4 = (bf16[3,2,5120]{2,1,0:T(2,128)(2,1)S(1)}, bf16[3,2,5120]{2,1,0:T(2,128)(2,1)S(1)}, u32[]{:S(2)}, u32[]{:S(2)}) collective-permute-start(bf16[3,2,5120]{2,1,0:T(2,128)(2,1)S(1)} %collective-permute-done), channel_id=1, source_target_pairs={{0,2},{1,3},{2,0},{3,1},{4,6},{5,7},{6,4},{7,5},{8,10},{9,11},{10,... | collective-permute-start | bytes 184328 | tf_op jit(solution)/shard_map/ppermute | solution.py:258
  11.4 4.2 %collective-permute-start.7 = (bf16[3,2,5120]{2,1,0:T(2,128)(2,1)S(1)}, bf16[3,2,5120]{2,1,0:T(2,128)(2,1)S(1)}, u32[]{:S(2)}, u32[]{:S(2)}) collective-permute-start(bf16[3,2,5120]{2,1,0:T(2,128)(2,1)S(1)} %collective-permute-done.1), channel_id=1, source_target_pairs={{0,2},{1,3},{2,0},{3,1},{4,6},{5,7},{6,4},{7,5},{8,10},{9,11},{10,... | collective-permute-start | bytes 184328 | tf_op jit(solution)/shard_map/ppermute | solution.py:258
  12.0 4.2 %collective-permute-start.6 = (bf16[3,2,5120]{2,1,0:T(2,128)(2,1)S(1)}, bf16[3,2,5120]{2,1,0:T(2,128)(2,1)S(1)}, u32[]{:S(2)}, u32[]{:S(2)}) collective-permute-start(bf16[3,2,5120]{2,1,0:T(2,128)(2,1)S(1)} %collective-permute-done.2), channel_id=1, source_target_pairs={{0,2},{1,3},{2,0},{3,1},{4,6},{5,7},{6,4},{7,5},{8,10},{9,11},{10,... | collective-permute-start | bytes 184328 | tf_op jit(solution)/shard_map/ppermute | solution.py:258
  14.5 3.0 %collective-permute-start.5 = (bf16[4,3,40,2,128]{4,3,2,1,0:T(2,128)(2,1)S(1)}, bf16[4,3,40,2,128]{4,3,2,1,0:T(2,128)(2,1)S(1)}, u32[]{:S(2)}, u32[]{:S(2)}) collective-permute-start(bf16[4,3,40,2,128]{4,3,2,1,0:T(2,128)(2,1)S(1)} %pack_blocks.1), channel_id=1, source_target_pairs={{0,1},{1,0},{2,3},{3,2},{4,5},{5,4},{6,7},{7,6},{8,9},{9,8},{10,11... | collective-permute-start | bytes 737288 | tf_op jit(solution)/shard_map/ppermute | solution.py:258
  15.6 1.2 %collective-permute-start.11 = (bf16[3,40,2,128]{3,2,1,0:T(2,128)(2,1)S(1)}, bf16[3,40,2,128]{3,2,1,0:T(2,128)(2,1)S(1)}, u32[]{:S(2)}, u32[]{:S(2)}) collective-permute-start(bf16[3,40,2,128]{3,2,1,0:T(2,128)(2,1)S(1)} %bitcast.53), channel_id=1, source_target_pairs={{0,1},{1,0},{2,3},{3,2},{4,5},{5,4},{6,7},{7,6},{8,9},{9,8},{10,11... | collective-permute-start | bytes 184328 | tf_op jit(solution)/shard_map/ppermute | solution.py:258
  15.6 1.4 %collective-permute-start.8 = (bf16[3,40,2,128]{3,2,1,0:T(2,128)(2,1)S(1)}, bf16[3,40,2,128]{3,2,1,0:T(2,128)(2,1)S(1)}, u32[]{:S(2)}, u32[]{:S(2)}) collective-permute-start(bf16[3,40,2,128]{3,2,1,0:T(2,128)(2,1)S(1)} %bitcast.49), channel_id=1, source_target_pairs={{0,1},{1,0},{2,3},{3,2},{4,5},{5,4},{6,7},{7,6},{8,9},{9,8},{10,11... | collective-permute-start | bytes 184328 | tf_op jit(solution)/shard_map/ppermute | solution.py:258
  16.1 1.2 %collective-permute-start.9 = (bf16[3,40,2,128]{3,2,1,0:T(2,128)(2,1)S(1)}, bf16[3,40,2,128]{3,2,1,0:T(2,128)(2,1)S(1)}, u32[]{:S(2)}, u32[]{:S(2)}) collective-permute-start(bf16[3,40,2,128]{3,2,1,0:T(2,128)(2,1)S(1)} %bitcast.51), channel_id=1, source_target_pairs={{0,1},{1,0},{2,3},{3,2},{4,5},{5,4},{6,7},{7,6},{8,9},{9,8},{10,11... | collective-permute-start | bytes 184328 | tf_op jit(solution)/shard_map/ppermute | solution.py:258
  16.3 1.2 %collective-permute-start.10 = (bf16[3,40,2,128]{3,2,1,0:T(2,128)(2,1)S(1)}, bf16[3,40,2,128]{3,2,1,0:T(2,128)(2,1)S(1)}, u32[]{:S(2)}, u32[]{:S(2)}) collective-permute-start(bf16[3,40,2,128]{3,2,1,0:T(2,128)(2,1)S(1)} %bitcast.55), channel_id=1, source_target_pairs={{0,1},{1,0},{2,3},{3,2},{4,5},{5,4},{6,7},{7,6},{8,9},{9,8},{10,11... | collective-permute-start | bytes 184328 | tf_op jit(solution)/shard_map/ppermute | solution.py:258
  19.6 4.4 %collective-permute-start.14 = (bf16[48,128]{1,0:T(8,128)(2,1)S(1)}, bf16[48,128]{1,0:T(8,128)(2,1)S(1)}, u32[]{:S(2)}, u32[]{:S(2)}) collective-permute-start(bf16[48,128]{1,0:T(8,128)(2,1)S(1)} %get-tuple-element.53), channel_id=1, source_target_pairs={{0,3},{1,2},{2,1},{3,0},{4,7},{5,6},{6,5},{7,4},{8,11},{9,10},{10,... | collective-permute-start | bytes 36872 | tf_op jit(solution)/shard_map/ppermute | solution.py:258
  21.0 3.7 %collective-permute-start.13 = (bf16[48,128]{1,0:T(8,128)(2,1)S(1)}, bf16[48,128]{1,0:T(8,128)(2,1)S(1)}, u32[]{:S(2)}, u32[]{:S(2)}) collective-permute-start(bf16[48,128]{1,0:T(8,128)(2,1)S(1)} %get-tuple-element.53), channel_id=1, source_target_pairs={{0,2},{1,3},{2,0},{3,1},{4,6},{5,7},{6,4},{7,5},{8,10},{9,11},{10,... | collective-permute-start | bytes 36872 | tf_op jit(solution)/shard_map/ppermute | solution.py:258
  21.7 3.0 %collective-permute-start.12 = (bf16[48,128]{1,0:T(8,128)(2,1)S(1)}, bf16[48,128]{1,0:T(8,128)(2,1)S(1)}, u32[]{:S(2)}, u32[]{:S(2)}) collective-permute-start(bf16[48,128]{1,0:T(8,128)(2,1)S(1)} %get-tuple-element.53), channel_id=1, source_target_pairs={{0,1},{1,0},{2,3},{3,2},{4,5},{5,4},{6,7},{7,6},{8,9},{9,8},{10,11... | collective-permute-start | bytes 36872 | tf_op jit(solution)/shard_map/ppermute | solution.py:258
  24.7 6.9 %copy-start = (bf16[64,64,320]{2,1,0:T(8,128)(2,1)S(1)}, bf16[64,64,320]{2,1,0:T(8,128)(2,1)}, u32[]{:S(2)}) copy-start(bf16[64,64,320]{2,1,0:T(8,128)(2,1)} %param.12) | copy-start | bytes 7864324
  24.7 5.6 %collective-permute-start.17 = (bf16[48,128]{1,0:T(8,128)(2,1)S(1)}, bf16[48,128]{1,0:T(8,128)(2,1)S(1)}, u32[]{:S(2)}, u32[]{:S(2)}) collective-permute-start(bf16[48,128]{1,0:T(8,128)(2,1)S(1)} %add_add_fusion.refs_0_), channel_id=1, source_target_pairs={{0,12},{1,13},{2,14},{3,15},{4,8},{5,9},{6,10},{7,11},{8,4},{9,5},... | collective-permute-start | bytes 36872 | tf_op jit(solution)/shard_map/ppermute | solution.py:258
  26.9 4.6 %collective-permute-start.16 = (bf16[48,128]{1,0:T(8,128)(2,1)S(1)}, bf16[48,128]{1,0:T(8,128)(2,1)S(1)}, u32[]{:S(2)}, u32[]{:S(2)}) collective-permute-start(bf16[48,128]{1,0:T(8,128)(2,1)S(1)} %add_add_fusion.refs_0_), channel_id=1, source_target_pairs={{0,8},{1,9},{2,10},{3,11},{4,12},{5,13},{6,14},{7,15},{8,0},{9,1},... | collective-permute-start | bytes 36872 | tf_op jit(solution)/shard_map/ppermute | solution.py:258
  27.4 4.2 %collective-permute-start.15 = (bf16[48,128]{1,0:T(8,128)(2,1)S(1)}, bf16[48,128]{1,0:T(8,128)(2,1)S(1)}, u32[]{:S(2)}, u32[]{:S(2)}) collective-permute-start(bf16[48,128]{1,0:T(8,128)(2,1)S(1)} %add_add_fusion.refs_0_), channel_id=1, source_target_pairs={{0,4},{1,5},{2,6},{3,7},{4,0},{5,1},{6,2},{7,3},{8,12},{9,13},{10,... | collective-permute-start | bytes 36872 | tf_op jit(solution)/shard_map/ppermute | solution.py:258
  33.2 12.6 %all-to-all-start = ((bf16[16,8,3,2,128]{4,3,2,1,0:T(2,128)(2,1)}), bf16[16,8,3,2,128]{4,3,2,1,0:T(2,128)(2,1)S(1)}, u32[]{:S(2)}, u32[]{:S(2)}) async-start(bf16[16,8,3,2,128]{4,3,2,1,0:T(2,128)(2,1)} %update_values.1), calls=%async_computation | async-start | bytes 393216 | tf_op jit(solution)/shard_map/all_to_all | solution.py:704

commit v23 on v20

--- a/solution.py
+++ b/solution.py
@@ -674,7 +674,7 @@
 
     held = {0: hidden}
     held.update({m: trade(hidden, m, count) for m in range(4, count, 4)})
-    _, lengths, request_page_table = lax.optimization_barrier((held[4], lengths, request_page_table))
+    _, lengths, request_page_table = lax.optimization_barrier((held[count - 4], lengths, request_page_table))
     cosine, sine = rotation_rows(lengths, first, req_dev, steps)
     live = live_lanes(lengths, first, request_page_table, tokens, page_len)
     held.update({k | 2: trade(v, 2, count) for k, v in list(held.items())})

time: 50.8 us -> 51.4 us (1.012)
  waiting for transfers between devices: 8.71 us -> 9.52 us
    ppermute x18, waiting for transfers between devices: 6.25 us -> 7.07 us  [trade(): return lax.ppermute(value, 'replica', [(i, i ^ mask) for i in range(count)])]
  transfers between devices with their start and end apart: 19 -> 19, of which waited for: 6 -> 10; matrix products, arithmetic and copies ran while one was open for 3% -> 3% of each run, Pallas kernels for 21% -> 20%
where the time goes in v23:
time: 51.4 us; the launch traced here: 51.1 us
  starting transfers between devices  21.7 us (42%)
  Pallas kernels  17.9 us (35%)
  waiting for transfers between devices  9.52 us (19%)
  other arithmetic  1.53 us (3%)
    ppermute x18, starting transfers between devices, trade(): return lax.ppermute(value, 'replica', [(i, i ^ mask) for i in range(count)])  17.2 us
    ppermute x18, waiting for transfers between devices, trade(): return lax.ppermute(value, 'replica', [(i, i ^ mask) for i in range(count)])  7.07 us
    pallas_call x1, Pallas kernels, cache_by_head(): pl.pallas_call(functools.partial(cache_kernel, first), out_shape=(jax.Sha...  6.4 us
    all_to_all x1, starting transfers between devices, chip_plan(): lax.all_to_all(send, 'replica', split_axis=0, concat_axis=0, tiled=True)  4.49 us
    pallas_call x1, Pallas kernels, attend(): pl.pallas_call(attend_kernel, out_shape=jax.ShapeDtypeStruct((steps, head...  3.83 us
    pallas_call x3, Pallas kernels, project(): pl.pallas_call(functools.partial(project_kernel, which), out_shape=chunks...  3.44 us
    all_to_all x1, waiting for transfers between devices, chip_plan(): lax.all_to_all(send, 'replica', split_axis=0, concat_axis=0, tiled=True)  2.46 us
    pallas_call x1, Pallas kernels, low_of(): pl.pallas_call(functools.partial(low_kernel, tuple(blocks), packs), out_s...  2.09 us
  transfers between devices with their start and end apart: 19, of which 10 were waited for; matrix products, arithmetic and copies ran while one was open for 3% of the time, Pallas kernels for 20%

profile of v23, /device:TPU:0, one launch (start us, length us, event | category | flops | bytes accessed | tf_op | source)
XLA Modules:
  0.0 51.1 jit_solution(15358040251998268456)
XLA Ops:
  0.0 3.0 %collective-permute-start.1 = (bf16[3,2,5120]{2,1,0:T(2,128)(2,1)}, bf16[3,2,5120]{2,1,0:T(2,128)(2,1)S(1)}, u32[]{:S(2)}, u32[]{:S(2)}) collective-permute-start(bf16[3,2,5120]{2,1,0:T(2,128)(2,1)} %param.9), channel_id=1, source_target_pairs={{0,4},{1,5},{2,6},{3,7},{4,0},{5,1},{6,2},{7,3},{8,12},{9,13},{10,... | collective-permute-start | bytes 184328 | tf_op jit(solution)/shard_map/ppermute | solution.py:258
  3.0 2.5 %collective-permute-start = (bf16[3,2,5120]{2,1,0:T(2,128)(2,1)}, bf16[3,2,5120]{2,1,0:T(2,128)(2,1)S(1)}, u32[]{:S(2)}, u32[]{:S(2)}) collective-permute-start(bf16[3,2,5120]{2,1,0:T(2,128)(2,1)} %param.9), channel_id=1, source_target_pairs={{0,12},{1,13},{2,14},{3,15},{4,8},{5,9},{6,10},{7,11},{8,4},{9,5},... | collective-permute-start | bytes 184328 | tf_op jit(solution)/shard_map/ppermute | solution.py:258
  5.5 1.5 %collective-permute-start.3 = (bf16[3,2,5120]{2,1,0:T(2,128)(2,1)}, bf16[3,2,5120]{2,1,0:T(2,128)(2,1)S(1)}, u32[]{:S(2)}, u32[]{:S(2)}) collective-permute-start(bf16[3,2,5120]{2,1,0:T(2,128)(2,1)} %param.9), channel_id=1, source_target_pairs={{0,2},{1,3},{2,0},{3,1},{4,6},{5,7},{6,4},{7,5},{8,10},{9,11},{10,... | collective-permute-start | bytes 184328 | tf_op jit(solution)/shard_map/ppermute | solution.py:258
  7.0 0.1 collective-permute-start.2
  7.2 0.9 %select_reduce_fusion.1 = s32[32]{0:T(128)S(1)} fusion(s32[64]{0:T(128)} %param.13, s32[32]{0:T(128)} %param.14), kind=kLoop, calls=%fused_computation.1 | loop fusion | flops 6112 | bytes 512 | tf_op jit(solution)/shard_map/reduce_sum | solution.py:662
  8.0 0.0 slice-start
  8.0 0.0 copy-start.3
  8.0 0.0 copy-start.4
  8.1 0.0 copy-start.2
  8.1 0.2 index_work.1
  8.3 1.0 %collective-permute-done = bf16[3,2,5120]{2,1,0:T(2,128)(2,1)S(1)} collective-permute-done((bf16[3,2,5120]{2,1,0:T(2,128)(2,1)}, bf16[3,2,5120]{2,1,0:T(2,128)(2,1)S(1)}, u32[]{:S(2)}, u32[]{:S(2)}) %collective-permute-start) | collective-permute-done | bytes 61472 | tf_op jit(solution)/shard_map/ppermute | solution.py:258
  9.3 2.1 %collective-permute-start.7 = (bf16[3,2,5120]{2,1,0:T(2,128)(2,1)S(1)}, bf16[3,2,5120]{2,1,0:T(2,128)(2,1)S(1)}, u32[]{:S(2)}, u32[]{:S(2)}) collective-permute-start(bf16[3,2,5120]{2,1,0:T(2,128)(2,1)S(1)} %collective-permute-done), channel_id=1, source_target_pairs={{0,2},{1,3},{2,0},{3,1},{4,6},{5,7},{6,4},{7,5},{8,10},{9,11},{10,... | collective-permute-start | bytes 184328 | tf_op jit(solution)/shard_map/ppermute | solution.py:258
  11.3 0.0 collective-permute-start.4
  11.3 0.1 select_reduce_fusion
  11.4 1.6 %collective-permute-done.2 = bf16[3,2,5120]{2,1,0:T(2,128)(2,1)S(1)} collective-permute-done((bf16[3,2,5120]{2,1,0:T(2,128)(2,1)}, bf16[3,2,5120]{2,1,0:T(2,128)(2,1)S(1)}, u32[]{:S(2)}, u32[]{:S(2)}) %collective-permute-start.2) | collective-permute-done | bytes 61472 | tf_op jit(solution)/shard_map/ppermute | solution.py:258
  13.0 0.5 collective-permute-start.6
  13.5 0.2 fusion.3
  13.7 1.8 %collective-permute-done.4 = bf16[3,2,5120]{2,1,0:T(2,128)(2,1)S(1)} collective-permute-done((bf16[3,2,5120]{2,1,0:T(2,128)(2,1)S(1)}, bf16[3,2,5120]{2,1,0:T(2,128)(2,1)S(1)}, u32[]{:S(2)}, u32[]{:S(2)}) %collective-permute-start.4) | collective-permute-done | bytes 61472 | tf_op jit(solution)/shard_map/ppermute | solution.py:258
  15.5 0.3 pack_blocks.1
  15.9 0.1 collective-permute-start.5
  16.0 0.1 and_convert_fusion.live_ref
  16.0 0.5 collective-permute-start.11
  16.5 0.1 collective-permute-start.8
  16.6 0.4 collective-permute-start.9
  17.0 0.2 collective-permute-done.6
  17.2 0.2 select_reduce_fusion.2
  17.4 0.1 collective-permute-done.11.refs_11_
  17.5 0.2 collective-permute-done.8.refs_8_
  17.8 0.2 collective-permute-done.9.refs_9_
  17.9 0.5 %collective-permute-done.10.refs_10_ = bf16[3,40,2,128]{3,2,1,0:T(2,128)(2,1)S(1)} collective-permute-done((bf16[3,40,2,128]{3,2,1,0:T(2,128)(2,1)S(1)}, bf16[3,40,2,128]{3,2,1,0:T(2,128)(2,1)S(1)}, u32[]{:S(2)}, u32[]{:S(2)}) %collective-permute-start.10) | collective-permute-done | bytes 61472 | tf_op jit(solution)/shard_map/ppermute | solution.py:258
  18.5 2.1 %low_rows.1 = (bf16[3,40,16,2,128]{4,3,2,1,0:T(2,128)(2,1)S(1)}, bf16[48,128]{1,0:T(8,128)(2,1)S(1)}) custom-call(s32[1]{0:T(128)} %bitcast.1.me_ref, s32[1,96]{1,0:T(1,128)S(1)} %get-tuple-element.42.slot_ref, bf16[4,64,5120]{2,1,0:T(8,128)(2,1)S(1)} %copy-done.1, bf16[4,3,40,2,128]{4,3,2,1,0:T(2,128)(2,1)S(1)} %collective-permute-done.5.pack_ref, ...), custom_call_target="tpu_custom_call" | custom-call | flops 100000000 | bytes 4000000 | tf_op jit(solution)/shard_map/low_rows/pallas_call | solution.py:421
  20.6 0.6 %collective-permute-start.14 = (bf16[48,128]{1,0:T(8,128)(2,1)S(1)}, bf16[48,128]{1,0:T(8,128)(2,1)S(1)}, u32[]{:S(2)}, u32[]{:S(2)}) collective-permute-start(bf16[48,128]{1,0:T(8,128)(2,1)S(1)} %get-tuple-element.49), channel_id=1, source_target_pairs={{0,3},{1,2},{2,1},{3,0},{4,7},{5,6},{6,5},{7,4},{8,11},{9,10},{10,... | collective-permute-start | bytes 36872 | tf_op jit(solution)/shard_map/ppermute | solution.py:258
  21.2 1.3 %collective-permute-start.13 = (bf16[48,128]{1,0:T(8,128)(2,1)S(1)}, bf16[48,128]{1,0:T(8,128)(2,1)S(1)}, u32[]{:S(2)}, u32[]{:S(2)}) collective-permute-start(bf16[48,128]{1,0:T(8,128)(2,1)S(1)} %get-tuple-element.49), channel_id=1, source_target_pairs={{0,2},{1,3},{2,0},{3,1},{4,6},{5,7},{6,4},{7,5},{8,10},{9,11},{10,... | collective-permute-start | bytes 36872 | tf_op jit(solution)/shard_map/ppermute | solution.py:258
  22.4 0.1 collective-permute-start.12
  22.5 1.2 %project.4.key_ref = bf16[3,3,16,2,128]{4,3,2,1,0:T(2,128)(2,1)S(1)} custom-call(bf16[3,40,16,2,128]{4,3,2,1,0:T(2,128)(2,1)S(1)} %get-tuple-element.50.x_ref, bf16[3,320,5120]{2,1,0:T(8,128)(2,1)S(1)} %bitcast.37), custom_call_target="tpu_custom_call" | custom-call | flops 500000000 | bytes 4000000 | tf_op jit(solution)/shard_map/project/pallas_call | solution.py:464
  23.7 1.1 %project.3.query_ref = bf16[3,3,16,2,128]{4,3,2,1,0:T(2,128)(2,1)S(1)} custom-call(bf16[3,40,16,2,128]{4,3,2,1,0:T(2,128)(2,1)S(1)} %get-tuple-element.50.x_ref, bf16[3,320,5120]{2,1,0:T(8,128)(2,1)S(1)} %bitcast.38), custom_call_target="tpu_custom_call" | custom-call | flops 500000000 | bytes 4000000 | tf_op jit(solution)/shard_map/project/pallas_call | solution.py:464
  24.9 0.0 copy-start
  24.9 2.4 %collective-permute-start.17 = (bf16[48,128]{1,0:T(8,128)(2,1)S(1)}, bf16[48,128]{1,0:T(8,128)(2,1)S(1)}, u32[]{:S(2)}, u32[]{:S(2)}) collective-permute-start(bf16[48,128]{1,0:T(8,128)(2,1)S(1)} %add_add_fusion.refs_0_), channel_id=1, source_target_pairs={{0,12},{1,13},{2,14},{3,15},{4,8},{5,9},{6,10},{7,11},{8,4},{9,5},... | collective-permute-start | bytes 36872 | tf_op jit(solution)/shard_map/ppermute | solution.py:258
  27.3 0.5 collective-permute-start.16
  27.8 1.6 %collective-permute-start.15 = (bf16[48,128]{1,0:T(8,128)(2,1)S(1)}, bf16[48,128]{1,0:T(8,128)(2,1)S(1)}, u32[]{:S(2)}, u32[]{:S(2)}) collective-permute-start(bf16[48,128]{1,0:T(8,128)(2,1)S(1)} %add_add_fusion.refs_0_), channel_id=1, source_target_pairs={{0,4},{1,5},{2,6},{3,7},{4,0},{5,1},{6,2},{7,3},{8,12},{9,13},{10,... | collective-permute-start | bytes 36872 | tf_op jit(solution)/shard_map/ppermute | solution.py:258
  29.4 1.1 %project.5.base_ref = f32[96,320]{1,0:T(8,128)S(1)} custom-call(bf16[3,40,16,2,128]{4,3,2,1,0:T(2,128)(2,1)S(1)} %get-tuple-element.50.x_ref, bf16[3,320,5120]{2,1,0:T(8,128)(2,1)S(1)} %bitcast.39), custom_call_target="tpu_custom_call" | custom-call | flops 500000000 | bytes 4000000 | tf_op jit(solution)/shard_map/project/pallas_call | solution.py:464
  30.5 1.4 %collective-permute-done.16.refs_2_ = bf16[48,128]{1,0:T(8,128)(2,1)S(1)} collective-permute-done((bf16[48,128]{1,0:T(8,128)(2,1)S(1)}, bf16[48,128]{1,0:T(8,128)(2,1)S(1)}, u32[]{:S(2)}, u32[]{:S(2)}) %collective-permute-start.16) | collective-permute-done | bytes 12320 | tf_op jit(solution)/shard_map/ppermute | solution.py:258
  31.9 1.7 %update_values.1 = bf16[16,8,3,2,128]{4,3,2,1,0:T(2,128)(2,1)} custom-call(s32[96,1]{1,0:T(8,128)S(1)} %get-tuple-element.40.stored_ref, bf16[3,3,16,2,128]{4,3,2,1,0:T(2,128)(2,1)S(1)} %project.3.query_ref, bf16[3,3,16,2,128]{4,3,2,1,0:T(2,128)(2,1)S(1)} %project.4.key_ref, f32[96,320]{1,0:T(8,128)S(1)} %project.5.base_ref, bf16[4096,320]{1,0:T(8,128)(2,1)S(1)} %bitcast.40, ...), custom_call_target="tpu_custom_call" | custom-call | flops 300000000 | bytes 4000000 | tf_op jit(solution)/shard_map/update_values/pallas_call | solution.py:504
  33.6 4.5 %all-to-all-start = ((bf16[16,8,3,2,128]{4,3,2,1,0:T(2,128)(2,1)}), bf16[16,8,3,2,128]{4,3,2,1,0:T(2,128)(2,1)S(1)}, u32[]{:S(2)}, u32[]{:S(2)}) async-start(bf16[16,8,3,2,128]{4,3,2,1,0:T(2,128)(2,1)} %update_values.1), calls=%async_computation | async-start | bytes 393216 | tf_op jit(solution)/shard_map/all_to_all | solution.py:699
  38.1 0.1 fusion
  38.2 6.4 %cache_by_head.1 = (bf16[40,256,128]{2,1,0:T(8,128)(2,1)S(1)}, bf16[40,256,128]{2,1,0:T(8,128)(2,1)}) custom-call(bf16[256,40,2,128]{3,2,1,0:T(2,128)(2,1)} %bitcast.58), custom_call_target="tpu_custom_call" | custom-call | bytes 12000000 | tf_op jit(solution)/shard_map/cache_by_head/pallas_call | solution.py:321
  44.6 2.5 %all-to-all-done.pieces_ref = bf16[16,8,3,2,128]{4,3,2,1,0:T(2,128)(2,1)S(1)} async-done(((bf16[16,8,3,2,128]{4,3,2,1,0:T(2,128)(2,1)}), bf16[16,8,3,2,128]{4,3,2,1,0:T(2,128)(2,1)S(1)}, u32[]{:S(2)}, u32[]{:S(2)}) %all-to-all-start) | async-done | bytes 196640 | tf_op jit(solution)/shard_map/all_to_all | solution.py:699
  47.1 3.8 %attention.1 = bf16[3,40,2,128]{3,2,1,0:T(2,128)(2,1)} custom-call(f32[8,128]{1,0:T(8,128)S(1)} %get-tuple-element.66.cos_ref, f32[8,128]{1,0:T(8,128)S(1)} %get-tuple-element.65.sin_ref, s32[2,256]{1,0:T(2,128)S(1)} %and_convert_fusion.live_ref, bf16[16,8,3,2,128]{4,3,2,1,0:T(2,128)(2,1)S(1)} %all-to-all-done.pieces_ref, ...), custom_call_target="tpu_custom_call" | custom-call | flops 1000000000 | bytes 6000000 | tf_op jit(solution)/shard_map/attention/pallas_call | solution.py:626
  (29 shorter events, 0.1 us)
Async XLA Ops:
  0.0 11.3 %collective-permute-start.1 = (bf16[3,2,5120]{2,1,0:T(2,128)(2,1)}, bf16[3,2,5120]{2,1,0:T(2,128)(2,1)S(1)}, u32[]{:S(2)}, u32[]{:S(2)}) collective-permute-start(bf16[3,2,5120]{2,1,0:T(2,128)(2,1)} %param.9), channel_id=1, source_target_pairs={{0,4},{1,5},{2,6},{3,7},{4,0},{5,1},{6,2},{7,3},{8,12},{9,13},{10,... | collective-permute-start | bytes 184328 | tf_op jit(solution)/shard_map/ppermute | solution.py:258
  3.0 6.2 %collective-permute-start = (bf16[3,2,5120]{2,1,0:T(2,128)(2,1)}, bf16[3,2,5120]{2,1,0:T(2,128)(2,1)S(1)}, u32[]{:S(2)}, u32[]{:S(2)}) collective-permute-start(bf16[3,2,5120]{2,1,0:T(2,128)(2,1)} %param.9), channel_id=1, source_target_pairs={{0,12},{1,13},{2,14},{3,15},{4,8},{5,9},{6,10},{7,11},{8,4},{9,5},... | collective-permute-start | bytes 184328 | tf_op jit(solution)/shard_map/ppermute | solution.py:258
  5.5 8.2 %collective-permute-start.3 = (bf16[3,2,5120]{2,1,0:T(2,128)(2,1)}, bf16[3,2,5120]{2,1,0:T(2,128)(2,1)S(1)}, u32[]{:S(2)}, u32[]{:S(2)}) collective-permute-start(bf16[3,2,5120]{2,1,0:T(2,128)(2,1)} %param.9), channel_id=1, source_target_pairs={{0,2},{1,3},{2,0},{3,1},{4,6},{5,7},{6,4},{7,5},{8,10},{9,11},{10,... | collective-permute-start | bytes 184328 | tf_op jit(solution)/shard_map/ppermute | solution.py:258
  7.0 6.0 %collective-permute-start.2 = (bf16[3,2,5120]{2,1,0:T(2,128)(2,1)}, bf16[3,2,5120]{2,1,0:T(2,128)(2,1)S(1)}, u32[]{:S(2)}, u32[]{:S(2)}) collective-permute-start(bf16[3,2,5120]{2,1,0:T(2,128)(2,1)} %param.9), channel_id=1, source_target_pairs={{0,8},{1,9},{2,10},{3,11},{4,12},{5,13},{6,14},{7,15},{8,0},{9,1},... | collective-permute-start | bytes 184328 | tf_op jit(solution)/shard_map/ppermute | solution.py:258
  8.0 14.5 %slice-start = ((s8[9830400]{0:T(1024)(128)(4,1)}), s8[4194304]{0:T(1024)(128)(4,1)S(1)}, s32[]{:S(2)}) async-start(s8[9830400]{0:T(1024)(128)(4,1)} %bitcast.35), calls=%async_computation.1 | async-start | bytes 8388608
  8.0 3.3 %copy-start.3 = (s32[2,32]{1,0:T(2,128)S(1)}, s32[2,32]{1,0:T(2,128)}, u32[]{:S(2)}) copy-start(s32[2,32]{1,0:T(2,128)} %param.16) | copy-start | bytes 772
  8.0 5.5 %copy-start.4 = (s32[32]{0:T(128)S(1)}, s32[32]{0:T(128)}, u32[]{:S(2)}) copy-start(s32[32]{0:T(128)} %param.15) | copy-start | bytes 388
  8.1 7.5 %copy-start.2 = (bf16[3,2,5120]{2,1,0:T(2,128)(2,1)S(1)}, bf16[3,2,5120]{2,1,0:T(2,128)(2,1)}, u32[]{:S(2)}) copy-start(bf16[3,2,5120]{2,1,0:T(2,128)(2,1)} %param.9) | copy-start | bytes 184324
  8.1 10.4 %copy-start.1 = (bf16[4,64,5120]{2,1,0:T(8,128)(2,1)S(1)}, bf16[4,64,5120]{2,1,0:T(8,128)(2,1)}, u32[]{:S(2)}) copy-start(bf16[4,64,5120]{2,1,0:T(8,128)(2,1)} %down_ref.1) | copy-start | bytes 7864324
  8.1 14.4 %slice-start.1 = ((s8[9830400]{0:T(1024)(128)(4,1)}), s8[4194304]{0:T(1024)(128)(4,1)S(1)}, s32[]{:S(2)}) async-start(s8[9830400]{0:T(1024)(128)(4,1)} %bitcast.35), calls=%async_computation.2 | async-start | bytes 8388608
  8.1 14.4 %slice-start.2 = ((s8[9830400]{0:T(1024)(128)(4,1)}), s8[1441792]{0:T(1024)(128)(4,1)S(1)}, s32[]{:S(2)}) async-start(s8[9830400]{0:T(1024)(128)(4,1)} %bitcast.35), calls=%async_computation.3 | async-start | bytes 2883584
  9.3 6.8 %collective-permute-start.7 = (bf16[3,2,5120]{2,1,0:T(2,128)(2,1)S(1)}, bf16[3,2,5120]{2,1,0:T(2,128)(2,1)S(1)}, u32[]{:S(2)}, u32[]{:S(2)}) collective-permute-start(bf16[3,2,5120]{2,1,0:T(2,128)(2,1)S(1)} %collective-permute-done), channel_id=1, source_target_pairs={{0,2},{1,3},{2,0},{3,1},{4,6},{5,7},{6,4},{7,5},{8,10},{9,11},{10,... | collective-permute-start | bytes 184328 | tf_op jit(solution)/shard_map/ppermute | solution.py:258
  11.3 4.2 %collective-permute-start.4 = (bf16[3,2,5120]{2,1,0:T(2,128)(2,1)S(1)}, bf16[3,2,5120]{2,1,0:T(2,128)(2,1)S(1)}, u32[]{:S(2)}, u32[]{:S(2)}) collective-permute-start(bf16[3,2,5120]{2,1,0:T(2,128)(2,1)S(1)} %collective-permute-done.1), channel_id=1, source_target_pairs={{0,2},{1,3},{2,0},{3,1},{4,6},{5,7},{6,4},{7,5},{8,10},{9,11},{10,... | collective-permute-start | bytes 184328 | tf_op jit(solution)/shard_map/ppermute | solution.py:258
  13.0 4.2 %collective-permute-start.6 = (bf16[3,2,5120]{2,1,0:T(2,128)(2,1)S(1)}, bf16[3,2,5120]{2,1,0:T(2,128)(2,1)S(1)}, u32[]{:S(2)}, u32[]{:S(2)}) collective-permute-start(bf16[3,2,5120]{2,1,0:T(2,128)(2,1)S(1)} %collective-permute-done.2), channel_id=1, source_target_pairs={{0,2},{1,3},{2,0},{3,1},{4,6},{5,7},{6,4},{7,5},{8,10},{9,11},{10,... | collective-permute-start | bytes 184328 | tf_op jit(solution)/shard_map/ppermute | solution.py:258
  15.9 2.6 %collective-permute-start.5 = (bf16[4,3,40,2,128]{4,3,2,1,0:T(2,128)(2,1)S(1)}, bf16[4,3,40,2,128]{4,3,2,1,0:T(2,128)(2,1)S(1)}, u32[]{:S(2)}, u32[]{:S(2)}) collective-permute-start(bf16[4,3,40,2,128]{4,3,2,1,0:T(2,128)(2,1)S(1)} %pack_blocks.1), channel_id=1, source_target_pairs={{0,1},{1,0},{2,3},{3,2},{4,5},{5,4},{6,7},{7,6},{8,9},{9,8},{10,11... | collective-permute-start | bytes 737288 | tf_op jit(solution)/shard_map/ppermute | solution.py:258
  16.0 1.5 %collective-permute-start.11 = (bf16[3,40,2,128]{3,2,1,0:T(2,128)(2,1)S(1)}, bf16[3,40,2,128]{3,2,1,0:T(2,128)(2,1)S(1)}, u32[]{:S(2)}, u32[]{:S(2)}) collective-permute-start(bf16[3,40,2,128]{3,2,1,0:T(2,128)(2,1)S(1)} %bitcast.51), channel_id=1, source_target_pairs={{0,1},{1,0},{2,3},{3,2},{4,5},{5,4},{6,7},{7,6},{8,9},{9,8},{10,11... | collective-permute-start | bytes 184328 | tf_op jit(solution)/shard_map/ppermute | solution.py:258
  16.5 1.2 %collective-permute-start.8 = (bf16[3,40,2,128]{3,2,1,0:T(2,128)(2,1)S(1)}, bf16[3,40,2,128]{3,2,1,0:T(2,128)(2,1)S(1)}, u32[]{:S(2)}, u32[]{:S(2)}) collective-permute-start(bf16[3,40,2,128]{3,2,1,0:T(2,128)(2,1)S(1)} %bitcast.49), channel_id=1, source_target_pairs={{0,1},{1,0},{2,3},{3,2},{4,5},{5,4},{6,7},{7,6},{8,9},{9,8},{10,11... | collective-permute-start | bytes 184328 | tf_op jit(solution)/shard_map/ppermute | solution.py:258
  16.6 1.3 %collective-permute-start.9 = (bf16[3,40,2,128]{3,2,1,0:T(2,128)(2,1)S(1)}, bf16[3,40,2,128]{3,2,1,0:T(2,128)(2,1)S(1)}, u32[]{:S(2)}, u32[]{:S(2)}) collective-permute-start(bf16[3,40,2,128]{3,2,1,0:T(2,128)(2,1)S(1)} %bitcast.53), channel_id=1, source_target_pairs={{0,1},{1,0},{2,3},{3,2},{4,5},{5,4},{6,7},{7,6},{8,9},{9,8},{10,11... | collective-permute-start | bytes 184328 | tf_op jit(solution)/shard_map/ppermute | solution.py:258
  17.2 1.2 %collective-permute-start.10 = (bf16[3,40,2,128]{3,2,1,0:T(2,128)(2,1)S(1)}, bf16[3,40,2,128]{3,2,1,0:T(2,128)(2,1)S(1)}, u32[]{:S(2)}, u32[]{:S(2)}) collective-permute-start(bf16[3,40,2,128]{3,2,1,0:T(2,128)(2,1)S(1)} %bitcast.55), channel_id=1, source_target_pairs={{0,1},{1,0},{2,3},{3,2},{4,5},{5,4},{6,7},{7,6},{8,9},{9,8},{10,11... | collective-permute-start | bytes 184328 | tf_op jit(solution)/shard_map/ppermute | solution.py:258
  20.6 4.3 %collective-permute-start.14 = (bf16[48,128]{1,0:T(8,128)(2,1)S(1)}, bf16[48,128]{1,0:T(8,128)(2,1)S(1)}, u32[]{:S(2)}, u32[]{:S(2)}) collective-permute-start(bf16[48,128]{1,0:T(8,128)(2,1)S(1)} %get-tuple-element.49), channel_id=1, source_target_pairs={{0,3},{1,2},{2,1},{3,0},{4,7},{5,6},{6,5},{7,4},{8,11},{9,10},{10,... | collective-permute-start | bytes 36872 | tf_op jit(solution)/shard_map/ppermute | solution.py:258
  21.2 3.7 %collective-permute-start.13 = (bf16[48,128]{1,0:T(8,128)(2,1)S(1)}, bf16[48,128]{1,0:T(8,128)(2,1)S(1)}, u32[]{:S(2)}, u32[]{:S(2)}) collective-permute-start(bf16[48,128]{1,0:T(8,128)(2,1)S(1)} %get-tuple-element.49), channel_id=1, source_target_pairs={{0,2},{1,3},{2,0},{3,1},{4,6},{5,7},{6,4},{7,5},{8,10},{9,11},{10,... | collective-permute-start | bytes 36872 | tf_op jit(solution)/shard_map/ppermute | solution.py:258
  22.4 2.4 %collective-permute-start.12 = (bf16[48,128]{1,0:T(8,128)(2,1)S(1)}, bf16[48,128]{1,0:T(8,128)(2,1)S(1)}, u32[]{:S(2)}, u32[]{:S(2)}) collective-permute-start(bf16[48,128]{1,0:T(8,128)(2,1)S(1)} %get-tuple-element.49), channel_id=1, source_target_pairs={{0,1},{1,0},{2,3},{3,2},{4,5},{5,4},{6,7},{7,6},{8,9},{9,8},{10,11... | collective-permute-start | bytes 36872 | tf_op jit(solution)/shard_map/ppermute | solution.py:258
  24.9 7.0 %copy-start = (bf16[64,64,320]{2,1,0:T(8,128)(2,1)S(1)}, bf16[64,64,320]{2,1,0:T(8,128)(2,1)}, u32[]{:S(2)}) copy-start(bf16[64,64,320]{2,1,0:T(8,128)(2,1)} %param.12) | copy-start | bytes 7864324
  24.9 5.6 %collective-permute-start.17 = (bf16[48,128]{1,0:T(8,128)(2,1)S(1)}, bf16[48,128]{1,0:T(8,128)(2,1)S(1)}, u32[]{:S(2)}, u32[]{:S(2)}) collective-permute-start(bf16[48,128]{1,0:T(8,128)(2,1)S(1)} %add_add_fusion.refs_0_), channel_id=1, source_target_pairs={{0,12},{1,13},{2,14},{3,15},{4,8},{5,9},{6,10},{7,11},{8,4},{9,5},... | collective-permute-start | bytes 36872 | tf_op jit(solution)/shard_map/ppermute | solution.py:258
  27.3 4.6 %collective-permute-start.16 = (bf16[48,128]{1,0:T(8,128)(2,1)S(1)}, bf16[48,128]{1,0:T(8,128)(2,1)S(1)}, u32[]{:S(2)}, u32[]{:S(2)}) collective-permute-start(bf16[48,128]{1,0:T(8,128)(2,1)S(1)} %add_add_fusion.refs_0_), channel_id=1, source_target_pairs={{0,8},{1,9},{2,10},{3,11},{4,12},{5,13},{6,14},{7,15},{8,0},{9,1},... | collective-permute-start | bytes 36872 | tf_op jit(solution)/shard_map/ppermute | solution.py:258
  27.8 4.1 %collective-permute-start.15 = (bf16[48,128]{1,0:T(8,128)(2,1)S(1)}, bf16[48,128]{1,0:T(8,128)(2,1)S(1)}, u32[]{:S(2)}, u32[]{:S(2)}) collective-permute-start(bf16[48,128]{1,0:T(8,128)(2,1)S(1)} %add_add_fusion.refs_0_), channel_id=1, source_target_pairs={{0,4},{1,5},{2,6},{3,7},{4,0},{5,1},{6,2},{7,3},{8,12},{9,13},{10,... | collective-permute-start | bytes 36872 | tf_op jit(solution)/shard_map/ppermute | solution.py:258
  33.6 13.5 %all-to-all-start = ((bf16[16,8,3,2,128]{4,3,2,1,0:T(2,128)(2,1)}), bf16[16,8,3,2,128]{4,3,2,1,0:T(2,128)(2,1)S(1)}, u32[]{:S(2)}, u32[]{:S(2)}) async-start(bf16[16,8,3,2,128]{4,3,2,1,0:T(2,128)(2,1)} %update_values.1), calls=%async_computation | async-start | bytes 393216 | tf_op jit(solution)/shard_map/all_to_all | solution.py:699
